TPU v7x, 32 devices: a whole 2x2x4 slice. The times are simulated.
32 devices in a mesh: node: 8 (over y, x, core), chan: 4 (over z).
Axes of the slice: x: 2, y: 2, z: 4, core: 2. Of those that a mesh axis runs over, the one named last changes fastest.
Arguments:
- features: bfloat16 [14336, 1024], P('node', 'chan'), may hold values from -0.0625 to 0.0625
- weight: bfloat16 [1024, 1024], P('node', 'chan'), may hold values from -0.25 to 0.25
- pre_clean: bfloat16 [14336, 1024], P('node', 'chan'), may hold values from -6 to 6
- pre_corrupt: bfloat16 [14336, 1024], P('node', 'chan'), may hold values from -6 to 6
- grad_clean: bfloat16 [14336, 1024], P('node', 'chan'), may hold values from -6 to 6
- grad_corrupt: bfloat16 [14336, 1024], P('node', 'chan'), may hold values from -6 to 6
- slopes: float32 [1024], P('chan'), may hold values from 0.05 to 0.5
- adj_vals: bfloat16 [112, 5, 128, 128], P('node'), may hold values from 0 to 0.07861328
- adj_cols: int32 [112, 5], P('node'), may hold values from 0 to 111, as said below
- adj_count: int32 [112], P('node'), may hold values from 1 to 5, as said below
- shuffle_from: int32 [112], replicated, may hold values from 0 to 111, as said below
Outputs:
- grad_weight: float32 [1024, 1024], P('node', 'chan')
- grad_features: bfloat16 [14336, 1024], P('node', 'chan')
Inputs may be any that keep to these rules, and one draw needn't show every extreme that they name: `adj_cols`: entry [b, k] is a block within 2 of b, and entry [b, 0] is b itself. Slots k < adj_count[b] of row block b hold edge tiles; the other slots are padding and are not read. `shuffle_from`: A permutation of the blocks. The 14 blocks of one index of node take their rows from exactly 7 distinct indices of node, 2 blocks from each; among these are the index just after it and the index 4 away, counted round.
All inputs are finite; a program needn't handle non-finite values.
Results may differ from a plain program's by a relative error of at most 0.023.
Values may be sent and summed in bfloat16 or wider, within the bound.
No kernel may reach another device: no remote copies, remote signals or barrier semaphores. Data moves between devices by JAX's collectives and lax.ppermute only.
A program may use at most 128 MiB of HBM per device.

v0:
```python
import jax
import jax.numpy as jnp
from jax import lax
from jax.sharding import PartitionSpec as P


def shifted(value, axis, by):
    size = lax.axis_size(axis)
    pairs = [(i, i + by) for i in range(size) if 0 <= i + by < size]
    return lax.ppermute(value, axis, pairs)


def local_grad(grad_part, pre_part, slopes):
    factor = jnp.where(pre_part > 0, 1.0, slopes[None, :])
    return (grad_part.astype(jnp.float32) * factor).astype(jnp.bfloat16)


def local(
    features,
    weight,
    pre_clean,
    pre_corrupt,
    grad_clean,
    grad_corrupt,
    slopes,
    adj_vals,
    adj_cols,
    adj_count,
    shuffle_from,
):
    row_count, chan_width = features.shape
    blocks = adj_vals.shape[0]
    tile_slots = adj_vals.shape[1]
    tile_rows = adj_vals.shape[2]
    band_reach = (tile_slots - 1) // 2
    my_index = lax.axis_index("node")
    dev_count = lax.axis_size("node")
    d_clean = local_grad(grad_clean, pre_clean, slopes)
    d_corrupt = local_grad(grad_corrupt, pre_corrupt, slopes)
    stacked = jnp.concatenate([d_clean, d_corrupt], axis=1).reshape(
        blocks, tile_rows, 2 * chan_width
    )
    contrib = jnp.einsum("bkpq,bpc->bkqc", adj_vals, stacked, preferred_element_type=jnp.float32)
    span_blocks = blocks + 2 * band_reach
    targets = adj_cols - (my_index * blocks - band_reach)
    live_mask = jnp.arange(tile_slots)[None, :] < adj_count[:, None]
    chooser = (
        (targets.reshape(-1)[None, :] == jnp.arange(span_blocks)[:, None])
        & live_mask.reshape(-1)[None, :]
    ).astype(jnp.float32)
    summed = jnp.dot(
        chooser, contrib.reshape(blocks * tile_slots, -1), precision=lax.Precision.HIGHEST
    )
    summed = summed.reshape(span_blocks, tile_rows, 2 * chan_width)
    from_prev = shifted(summed[band_reach + blocks :].astype(jnp.bfloat16), "node", 1).astype(
        jnp.float32
    )
    from_next = shifted(summed[:band_reach].astype(jnp.bfloat16), "node", -1).astype(jnp.float32)
    remaining = blocks - band_reach
    middle = summed[band_reach : band_reach + blocks]
    middle = (
        middle
        + jnp.pad(from_prev, ((0, remaining), (0, 0), (0, 0)))
        + jnp.pad(from_next, ((remaining, 0), (0, 0), (0, 0)))
    )
    backprop = middle.astype(jnp.bfloat16).reshape(row_count, 2 * chan_width)
    back_clean = backprop[:, :chan_width]
    back_corrupt = backprop[:, chan_width:]
    my_blocks = my_index * blocks + jnp.arange(blocks)
    all_blocks = jnp.arange(shuffle_from.shape[0])
    one_hot = (shuffle_from[None, :] == my_blocks[:, None]).astype(jnp.int32)
    source_block = jnp.sum(one_hot * all_blocks[None, :], axis=1)
    wanted = (source_block[:, None] * tile_rows + jnp.arange(tile_rows)[None, :]).reshape(-1)
    portion = lax.all_gather(back_corrupt, "node", axis=0, tiled=True)
    inside = (wanted >= 0) & (wanted < portion.shape[0])
    fetched = jnp.take(portion, jnp.clip(wanted, 0, portion.shape[0] - 1), axis=0)
    unshuffled = jnp.where(inside[:, None], fetched, jnp.zeros_like(back_corrupt))
    combined = jnp.concatenate([back_clean, unshuffled], axis=1)
    product = lax.dot_general(
        lax.all_gather(features, "chan", axis=1, tiled=True),
        combined,
        (((0,), (0,)), ((), ())),
        preferred_element_type=jnp.float32,
    )
    partial_w = product[:, :chan_width] + product[:, chan_width:]
    share_rows = partial_w.shape[0] // dev_count
    summed_w = lax.psum(partial_w.astype(jnp.bfloat16), "node").astype(jnp.float32)
    grad_weight = lax.dynamic_slice_in_dim(summed_w, my_index * share_rows, share_rows, 0)
    portion = lax.all_gather(weight, "node", axis=0, tiled=True)
    doubled = jnp.concatenate([portion, portion], axis=1)
    partial_x = lax.dot_general(
        combined, doubled, (((1,), (1,)), ((), ())), preferred_element_type=jnp.float32
    )
    grad_features = lax.psum_scatter(
        partial_x.astype(jnp.bfloat16), "chan", scatter_dimension=1, tiled=True
    )
    return (grad_weight, grad_features)


def solution(mesh):
    placed = (
        P("node", "chan"),
        P("node", "chan"),
        P("node", "chan"),
        P("node", "chan"),
        P("node", "chan"),
        P("node", "chan"),
        P("chan"),
        P("node", None, None, None),
        P("node", None),
        P("node"),
        P(),
    )
    return jax.shard_map(
        local,
        mesh=mesh,
        in_specs=placed,
        out_specs=(P("node", "chan"), P("node", "chan")),
        check_vma=False,
    )
```

profile of v0, /device:TPU:0, one launch (start us, length us, event | category | flops | bytes accessed | tf_op | source)
XLA Modules:
  0.0 351.9 jit_solution(2223217565511406758)
XLA Ops:
  7.2 0.0 copy-start
  7.2 0.0 all-gather.3.cloned.1.call-start
  7.2 2.9 multiply_convert_fusion.1
  10.1 0.1 pad_maximum_fusion
  10.3 0.0 copy-done
  10.3 7.7 %convolution_bitcast_fusion = f32[14,5,128,512]{2,3,1,0:T(8,128)} fusion(bf16[14,128,512,1]{2,1,3,0:T(8,128)(2,1)S(1)} %bitcast.51, bf16[14,5,128,128]{3,2,1,0:T(8,128)(2,1)S(1)} %copy-done), kind=kOutput, calls=%fused_computation.1 | convolution fusion | flops 1174405120 | bytes 22478848 | tf_op jit(solution)/shard_map/bkpq,bpc->bkqc/dot_general | solution.py:43
  18.0 19.2 %copy.21 = f32[14,5,128,512]{3,2,1,0:T(8,128)} copy(f32[14,5,128,512]{2,3,1,0:T(8,128)} %convolution_bitcast_fusion) | data formatting | bytes 36700160 | tf_op jit(solution)/shard_map/bkpq,bpc->bkqc/dot_general | solution.py:43
  37.2 8.1 %pad.25 = f32[72,128,512]{2,1,0:T(8,128)S(1)} pad(f32[70,128,512]{2,1,0:T(8,128)} %bitcast.49, f32[]{:T(128)} %constant.57), padding=0_2x0_0x0_0 | pad | bytes 37224452
  45.3 0.0 copy-start.3
  45.3 0.0 copy-start.4
  45.3 21.7 %copy.26 = f32[9,8,128,512]{3,1,2,0:T(8,128)} copy(f32[9,8,128,512]{3,2,1,0:T(8,128)S(1)} %bitcast.47) | data formatting | bytes 37748736
  67.0 0.0 copy-done.3
  67.0 0.1 copy.19
  67.1 0.1 eq.28
  67.2 0.0 copy-done.4
  67.2 0.1 iota_compare_fusion.1
  67.3 0.1 lt.58
  67.4 10.2 %fusion.25 = (bf16[18,65536]{1,0:T(8,128)(2,1)S(1)}, f32[18,65536]{1,0:T(8,128)S(1)}) fusion(f32[70,65536]{1,0:T(8,128)} %bitcast.48, s32[70]{0:T(128)S(1)} %eq.28, pred[70]{0:T(512)(128)(4,1)S(1)} %lt.58), kind=kOutput, calls=%fused_computation.48 | convolution fusion | flops 992086528 | bytes 25428318 | tf_op jit(solution)/shard_map/dot_general | solution.py:51
  77.6 0.3 fusion.23
  77.9 2.4 collective-permute-start
  80.3 1.5 collective-permute-start.1
  81.8 0.3 slice.38
  82.1 2.4 copy.27
  84.6 0.0 collective-permute-done
  84.6 1.2 collective-permute-done.1
  85.8 0.4 fusion.1
  86.2 0.0 copy-start.5
  86.2 0.0 copy-start.2
  86.2 1.0 fusion.24
  87.2 0.0 all-gather.3.cloned.1.call-update
  87.3 0.0 all-gather.5.cloned.1.call-start
  87.3 0.7 all-gather.5.cloned.1.call-update
  88.0 0.0 all-reduce.4.cloned.1.call-start
  88.1 0.0 copy-done.5
  88.1 0.2 select_reduce_fusion
  88.3 0.1 fusion.12
  88.4 0.0 copy-done.2
  88.4 15.3 %all_gather.11 = bf16[1024,256]{1,0:T(8,128)(2,1)} all-gather(bf16[128,256]{1,0:T(8,128)(2,1)S(1)} %copy-done.2), channel_id=1, replica_groups=mesh['node'=8,'chan'=4] {'node'}, dimensions={0}, use_global_device_ids=true | all-gather | bytes 589824 | tf_op jit(solution)/shard_map/all_gather | solution.py:89
  103.8 0.1 fusion.15
  103.8 0.1 fusion.17
  103.9 39.1 %all-gather.3.cloned.1.call-done = bf16[14336,256]{1,0:T(8,128)(2,1)} async-done(((bf16[1792,256]{1,0:T(8,128)(2,1)}), bf16[14336,256]{1,0:T(8,128)(2,1)}) %all-gather.3.cloned.1.call-update) | async-done | bytes 7340048 | tf_op jit(solution)/shard_map/all_gather | solution.py:74
  143.0 8.2 %gather_fusion = bf16[1792,256]{1,0:T(8,128)(2,1)S(1)} fusion(bf16[14336,256]{1,0:T(8,128)(2,1)} %all-gather.3.cloned.1.call-done, s32[2048]{0:T(1024)S(1)} %pad_clamp_fusion), kind=kCustom, calls=%fused_computation | custom fusion | bytes 1842176 | tf_op jit(solution)/shard_map/jit(_take)/gather | solution.py:76
  151.2 2.0 select_select_fusion
  153.2 63.4 %all-gather.5.cloned.1.call-done = bf16[1792,1024]{1,0:T(8,128)(2,1)} async-done(((bf16[1792,256]{1,0:T(8,128)(2,1)}), bf16[1792,1024]{1,0:T(8,128)(2,1)}) %all-gather.5.cloned.1.call-update) | async-done | bytes 3670032 | tf_op jit(solution)/shard_map/all_gather | solution.py:80
  216.6 4.4 %convolution_bitcast_fusion.1 = f32[1024,512]{0,1:T(8,128)S(1)} fusion(bf16[1792,1024]{1,0:T(8,128)(2,1)} %all-gather.5.cloned.1.call-done, bf16[1792,256]{1,0:T(8,128)(2,1)} %select_select_fusion, bf16[1792,256]{1,0:T(8,128)(2,1)S(1)} %get-tuple-element.10), kind=kOutput, calls=%fused_computation.10 | convolution fusion | flops 1882718208 | bytes 7602176 | tf_op jit(solution)/shard_map/dot_general | solution.py:79
  221.0 0.9 fusion.2
  221.9 0.0 all-reduce.4.cloned.1.call-update
  221.9 0.0 reduce-scatter.2.cloned.1.call-start
  222.0 0.0 copy-start.1
  222.0 5.5 %convolution_convert_fusion = bf16[1792,1024]{1,0:T(8,128)(2,1)} fusion(bf16[1792,256]{1,0:T(8,128)(2,1)} %select_select_fusion, bf16[1792,256]{1,0:T(8,128)(2,1)S(1)} %get-tuple-element.10, bf16[1024,256]{1,0:T(8,128)(2,1)} %all_gather.11), kind=kOutput, calls=%fused_computation.2 | convolution fusion | flops 1886650368 | bytes 6029312 | tf_op jit(solution)/shard_map/dot_general | solution.py:91
  227.5 0.0 reduce-scatter.2.cloned.1.call-update
  227.5 47.3 %all-reduce.4.cloned.1.call-done = bf16[1024,256]{0,1:T(8,128)(2,1)} async-done(((bf16[1024,256]{0,1:T(8,128)(2,1)}), bf16[1024,256]{0,1:T(8,128)(2,1)}) %all-reduce.4.cloned.1.call-update) | async-done | bytes 524304 | tf_op jit(solution)/shard_map/psum | solution.py:87
  274.8 0.8 dynamic-slice_convert_fusion
  275.7 0.8 copy.22
  276.4 69.0 %reduce-scatter.2.cloned.1.call-done = bf16[1792,256]{1,0:T(8,128)(2,1)} async-done(((bf16[1792,1024]{1,0:T(8,128)(2,1)}), bf16[1792,256]{1,0:T(8,128)(2,1)}) %reduce-scatter.2.cloned.1.call-update) | async-done | bytes 917520 | tf_op jit(solution)/shard_map/reduce_scatter | solution.py:94
  345.4 0.0 copy-done.1
  (7 shorter events, 0.1 us)
Async XLA Ops:
  7.2 3.1 copy-start
  7.2 135.8 %all-gather.3.cloned.1.call-start = ((), (), s32[]{:S(2)}) async-start(), calls=%async_computation.1 | async-start | bytes 8257536 | tf_op jit(solution)/shard_map/all_gather | solution.py:74
  45.3 21.7 %copy-start.3 = (s32[14,5]{0,1:T(8,128)S(1)}, s32[14,5]{0,1:T(8,128)}, u32[]{:S(2)}) copy-start(s32[14,5]{0,1:T(8,128)} %param.19) | copy-start | bytes 844
  45.3 21.9 %copy-start.4 = (s32[14]{0:T(128)S(1)}, s32[14]{0:T(128)}, u32[]{:S(2)}) copy-start(s32[14]{0:T(128)} %param.20) | copy-start | bytes 172
  77.9 6.7 %collective-permute-start = (bf16[2,128,512]{2,1,0:T(8,128)(2,1)S(1)}, bf16[2,128,512]{2,1,0:T(8,128)(2,1)S(1)}, u32[]{:S(2)}, u32[]{:S(2)}) collective-permute-start(bf16[2,128,512]{2,1,0:T(8,128)(2,1)S(1)} %bitcast.56), channel_id=1, source_target_pairs={{0,4},{4,8},{8,12},{12,16},{16,20},{20,24},{24,28},{1,5},{5,9},{9,... | collective-permute-start | bytes 786440 | tf_op jit(solution)/shard_map/ppermute | solution.py:10
  80.3 5.5 %collective-permute-start.1 = (bf16[2,128,512]{2,1,0:T(8,128)(2,1)S(1)}, bf16[2,128,512]{2,1,0:T(8,128)(2,1)S(1)}, u32[]{:S(2)}, u32[]{:S(2)}) collective-permute-start(bf16[2,128,512]{2,1,0:T(8,128)(2,1)S(1)} %bitcast.57), channel_id=1, source_target_pairs={{4,0},{8,4},{12,8},{16,12},{20,16},{24,20},{28,24},{5,1},{9,5},{13... | collective-permute-start | bytes 786440 | tf_op jit(solution)/shard_map/ppermute | solution.py:10
  86.2 1.9 copy-start.5
  86.2 2.2 copy-start.2
  87.3 129.3 %all-gather.5.cloned.1.call-start = ((), (), s32[]{:S(2)}) async-start(), calls=%async_computation.2 | async-start | bytes 4587520 | tf_op jit(solution)/shard_map/all_gather | solution.py:80
  88.0 186.8 %all-reduce.4.cloned.1.call-start = ((), (), s32[]{:S(2)}) async-start(), calls=%async_computation.3 | async-start | bytes 1048576 | tf_op jit(solution)/shard_map/psum | solution.py:87
  221.9 123.5 %reduce-scatter.2.cloned.1.call-start = ((), (), s32[]{:S(2)}) async-start(), calls=%async_computation.4 | async-start | bytes 4587520 | tf_op jit(solution)/shard_map/reduce_scatter | solution.py:94
  222.0 123.4 %copy-start.1 = (bf16[14,5,128,128]{3,2,1,0:T(8,128)(2,1)S(1)}, bf16[14,5,128,128]{3,2,1,0:T(8,128)(2,1)}, u32[]{:S(2)}) copy-start(bf16[14,5,128,128]{3,2,1,0:T(8,128)(2,1)} %param.18) | copy-start | bytes 6881284
Sparse Core Ops, SparseCore 0:
  87.4 55.5 all-gather.2
  144.5 71.9 all-gather.4
  222.0 52.7 all-reduce.3
  277.7 67.7 reduce-scatter.1
where the time goes:
time: 353 us; the launch traced here: 352 us
  waiting for transfers between devices  221 us (63%)
  local copies, waits for them, and re-layouts  62.4 us (18%)
  matrix products  27.8 us (8%)
  blocking collectives  15.3 us (4%)
  between operations  14 us (4%)
  other arithmetic  7.68 us (2%)
  starting transfers between devices  4 us (1%)
    reduce_scatter x1, waiting for transfers between devices, local(): lax.psum_scatter(partial_x.astype(jnp.bfloat16), 'chan', scatter_dimensio...  69 us
    all_gather x1, waiting for transfers between devices, local(): lax.all_gather(features, 'chan', axis=1, tiled=True)  63.4 us
    psum x1, waiting for transfers between devices, local(): lax.psum(partial_w.astype(jnp.bfloat16), 'node').astype(jnp.float32)  47.3 us
    all_gather x1, waiting for transfers between devices, local(): portion = lax.all_gather(back_corrupt, 'node', axis=0, tiled=True)  39.1 us
    unnamed x18, local copies, waits for them, and re-layouts  33 us
    dot_general x1, local copies, waits for them, and re-layouts, local(): jnp.einsum('bkpq,bpc->bkqc', adj_vals, stacked, preferred_element_type=jn...  19.2 us
    all_gather x1, blocking collectives, local(): portion = lax.all_gather(weight, 'node', axis=0, tiled=True)  15.3 us
    dot_general x1, matrix products, local(): jnp.dot(chooser, contrib.reshape(blocks * tile_slots, -1), precision=lax....  10.2 us
  transfers between devices with their start and end apart: 6, of which 5 were waited for; matrix products, arithmetic and copies ran while one was open for 6% of the time, Pallas kernels for 0%

commit v1 on v0

v1 whole, which is shorter than its diff:
```python
import functools

import jax
import jax.numpy as jnp
from jax import lax
from jax.experimental import pallas as pl
from jax.experimental.pallas import tpu as pltpu
from jax.sharding import PartitionSpec as P

VMEM_LIMIT = 48 * 1024 * 1024


def params():
    return pltpu.CompilerParams(vmem_limit_bytes=VMEM_LIMIT)


def shifted(value, axis, by):
    size = lax.axis_size(axis)
    pairs = [(i, i + by) for i in range(size) if 0 <= i + by < size]
    return lax.ppermute(value, axis, pairs)


def swapped(value, axis, bit):
    size = lax.axis_size(axis)
    return lax.ppermute(value, axis, [(i, i ^ bit) for i in range(size)])


def exchanged(value, axis):
    return lax.all_to_all(value, axis, split_axis=0, concat_axis=0, tiled=True)


def masked_grad(grad_ref, pre_ref, slope):
    factor = jnp.where(pre_ref[...].astype(jnp.float32) > 0, 1.0, slope)
    return (grad_ref[...].astype(jnp.float32) * factor).astype(jnp.bfloat16)


def both_grads(gc, pc, gx, px, slopes):
    slope = slopes[...]
    return jnp.concatenate([masked_grad(gc, pc, slope), masked_grad(gx, px, slope)], axis=1)


def tile_product(tile, rhs):
    return lax.dot_general(
        tile, rhs, (((0,), (0,)), ((), ())), preferred_element_type=jnp.float32
    )


def border_kernel(reach, blocks, slots, width, targets, gc, pc, gx, px, slopes, adj, down, up, acc):
    step = pl.program_id(0)
    row = jnp.where(step < reach, step, step + blocks - 2 * reach)

    @pl.when(step == 0)
    def _():
        acc[...] = jnp.zeros_like(acc)

    rhs = both_grads(gc, pc, gx, px, slopes)
    for k in range(slots):
        target = targets[row, k]

        @pl.when((target >= 0) & ((target < reach) | (target >= reach + blocks)))
        def _():
            place = jnp.where(target < reach, target, target - blocks)
            acc[place] += tile_product(adj[0, k], rhs)

    @pl.when(step == 2 * reach - 1)
    def _():
        for which in range(2):
            part = acc[:, :, which * width : (which + 1) * width].astype(jnp.bfloat16)
            down[which] = part[:reach]
            up[which] = part[reach:]


def border(targets, gc, pc, gx, px, slopes, adj, reach):
    blocks, slots, rows, _ = adj.shape
    width = gc.shape[1]

    def row_of(i):
        return jnp.where(i < reach, i, i + blocks - 2 * reach)

    data = pl.BlockSpec((rows, width), lambda i, *_: (row_of(i), 0))
    halo = pl.BlockSpec((2, reach, rows, width), lambda i, *_: (0, 0, 0, 0))
    halo_shape = jax.ShapeDtypeStruct((2, reach, rows, width), jnp.bfloat16)
    return pl.pallas_call(
        functools.partial(border_kernel, reach, blocks, slots, width),
        grid_spec=pltpu.PrefetchScalarGridSpec(
            num_scalar_prefetch=1,
            grid=(2 * reach,),
            in_specs=[
                data,
                data,
                data,
                data,
                pl.BlockSpec((1, width), lambda i, *_: (0, 0)),
                pl.BlockSpec((1, slots, rows, rows), lambda i, *_: (row_of(i), 0, 0, 0)),
            ],
            out_specs=[halo, halo],
            scratch_shapes=[pltpu.VMEM((2 * reach, rows, 2 * width), jnp.float32)],
        ),
        out_shape=[halo_shape, halo_shape],
        compiler_params=params(),
        name="border",
    )(targets, gc, pc, gx, px, slopes, adj)


def inner_kernel(
    reach, blocks, slots, width, targets, places, gc, pc, gx, px, slopes, adj, clean, outgoing, acc
):
    step = pl.program_id(0)

    @pl.when(step == 0)
    def _():
        acc[...] = jnp.zeros_like(acc)

    rhs = both_grads(gc, pc, gx, px, slopes)
    for k in range(slots):
        target = targets[step, k] - reach

        @pl.when((target >= 0) & (target < blocks))
        def _():
            acc[target] += tile_product(adj[0, k], rhs)

    def finish(block):
        clean[block] = acc[block, :, :width].astype(jnp.bfloat16)
        outgoing[places[block]] = acc[block, :, width:].astype(jnp.bfloat16)

    @pl.when(step >= reach)
    def _():
        finish(step - reach)

    @pl.when(step == blocks - 1)
    def _():
        for j in range(reach):
            finish(blocks - reach + j)


def inner(targets, places, gc, pc, gx, px, slopes, adj, reach, sent):
    blocks, slots, rows, _ = adj.shape
    width = gc.shape[1]
    data = pl.BlockSpec((rows, width), lambda i, *_: (i, 0))
    return pl.pallas_call(
        functools.partial(inner_kernel, reach, blocks, slots, width),
        grid_spec=pltpu.PrefetchScalarGridSpec(
            num_scalar_prefetch=2,
            grid=(blocks,),
            in_specs=[
                data,
                data,
                data,
                data,
                pl.BlockSpec((1, width), lambda i, *_: (0, 0)),
                pl.BlockSpec((1, slots, rows, rows), lambda i, *_: (i, 0, 0, 0)),
            ],
            out_specs=[
                pl.BlockSpec((blocks, rows, width), lambda i, *_: (0, 0, 0)),
                pl.BlockSpec((sent, rows, width), lambda i, *_: (0, 0, 0)),
            ],
            scratch_shapes=[pltpu.VMEM((blocks, rows, 2 * width), jnp.float32)],
        ),
        out_shape=[
            jax.ShapeDtypeStruct((blocks, rows, width), jnp.bfloat16),
            jax.ShapeDtypeStruct((sent, rows, width), jnp.bfloat16),
        ],
        compiler_params=params(),
        cost_estimate=pl.CostEstimate(
            flops=4 * blocks * slots * rows * rows * width,
            bytes_accessed=12 * blocks * rows * width + 2 * blocks * slots * rows * rows,
            transcendentals=0,
        ),
        name="inner",
    )(targets, places, gc, pc, gx, px, slopes, adj)


def patch_kernel(reach, places, block, low, high, out):
    step = pl.program_id(0)

    @pl.when(step < reach)
    def _():
        out[...] = (block[...].astype(jnp.float32) + low[0].astype(jnp.float32)).astype(jnp.bfloat16)

    @pl.when(step >= reach)
    def _():
        out[...] = (block[...].astype(jnp.float32) + high[0].astype(jnp.float32)).astype(jnp.bfloat16)


def patch(places, outgoing, low, high, blocks):
    sent, rows, width = outgoing.shape
    reach = low.shape[1]

    def place_of(i, places):
        return places[jnp.where(i < reach, i, i + blocks - 2 * reach)]

    spot = pl.BlockSpec((1, rows, width), lambda i, places: (place_of(i, places), 0, 0))
    return pl.pallas_call(
        functools.partial(patch_kernel, reach),
        grid_spec=pltpu.PrefetchScalarGridSpec(
            num_scalar_prefetch=1,
            grid=(2 * reach,),
            in_specs=[
                spot,
                pl.BlockSpec(
                    (1, 1, rows, width), lambda i, _: (1, jnp.minimum(i, reach - 1), 0, 0)
                ),
                pl.BlockSpec(
                    (1, 1, rows, width), lambda i, _: (1, jnp.maximum(i - reach, 0), 0, 0)
                ),
            ],
            out_specs=spot,
        ),
        out_shape=jax.ShapeDtypeStruct(outgoing.shape, jnp.bfloat16),
        input_output_aliases={1: 0},
        compiler_params=params(),
        name="patch",
    )(places, outgoing, low, high)


def merge_kernel(reach, blocks, sources, clean, low, high, incoming, out):
    step = pl.program_id(0)
    total = clean[0].astype(jnp.float32) + incoming[0].astype(jnp.float32)
    out[...] = total.astype(jnp.bfloat16)

    @pl.when(step < reach)
    def _():
        out[...] = (total + low[0, 0].astype(jnp.float32)).astype(jnp.bfloat16)

    @pl.when(step >= blocks - reach)
    def _():
        out[...] = (total + high[0, 0].astype(jnp.float32)).astype(jnp.bfloat16)


def merge(sources, clean, low, high, incoming):
    blocks, rows, width = clean.shape
    reach = low.shape[1]
    return pl.pallas_call(
        functools.partial(merge_kernel, reach, blocks),
        grid_spec=pltpu.PrefetchScalarGridSpec(
            num_scalar_prefetch=1,
            grid=(blocks,),
            in_specs=[
                pl.BlockSpec((1, rows, width), lambda i, _: (i, 0, 0)),
                pl.BlockSpec(
                    (1, 1, rows, width), lambda i, _: (0, jnp.minimum(i, reach - 1), 0, 0)
                ),
                pl.BlockSpec(
                    (1, 1, rows, width),
                    lambda i, _: (0, jnp.maximum(i - (blocks - reach), 0), 0, 0),
                ),
                pl.BlockSpec((1, rows, width), lambda i, sources: (sources[i], 0, 0)),
            ],
            out_specs=pl.BlockSpec((rows, width), lambda i, _: (i, 0)),
        ),
        out_shape=jax.ShapeDtypeStruct((blocks * rows, width), jnp.bfloat16),
        compiler_params=params(),
        name="merge",
    )(sources, clean, low, high, incoming)


def weight_kernel(groups, shares, bits, me, feats, summed, keep, send):
    step = pl.program_id(0)
    height = keep.shape[2]
    for group in range(groups):
        product = lax.dot_general(
            feats[0], summed[group], (((0,), (0,)), ((), ())), preferred_element_type=jnp.float32
        ).astype(jnp.bfloat16)
        for share in range(shares):
            relative = (step * shares + share) ^ me[0]
            place = jnp.int32(0)
            for j in range(1, bits):
                place += ((relative >> j) & 1) << (bits - 1 - j)
            part = product[share * height : (share + 1) * height]

            @pl.when((relative & 1) == 0)
            def _():
                keep[place, group] = part

            @pl.when((relative & 1) == 1)
            def _():
                send[place, group] = part


def weight_partial(me, feats, summed, devs):
    groups, rows, width = feats.shape
    shares = devs // groups
    height = groups * width // devs
    bits = devs.bit_length() - 1
    half = (devs // 2, groups, height, width)
    out = pl.BlockSpec(half, lambda i, _: (0, 0, 0, 0))
    return pl.pallas_call(
        functools.partial(weight_kernel, groups, shares, bits),
        grid_spec=pltpu.PrefetchScalarGridSpec(
            num_scalar_prefetch=1,
            grid=(groups,),
            in_specs=[
                pl.BlockSpec((1, rows, width), lambda i, _: (i, 0, 0)),
                pl.BlockSpec((groups, rows, width), lambda i, _: (0, 0, 0)),
            ],
            out_specs=[out, out],
        ),
        out_shape=[jax.ShapeDtypeStruct(half, jnp.bfloat16)] * 2,
        compiler_params=params(),
        cost_estimate=pl.CostEstimate(
            flops=2 * rows * (groups * width) ** 2,
            bytes_accessed=2 * (groups * width) ** 2 + 4 * groups * rows * width,
            transcendentals=0,
        ),
        name="weight_partial",
    )(me, feats, summed)


def feature_kernel(groups, shares, summed, weight, out):
    total = None
    for group in range(groups):
        tile = jnp.concatenate([weight[share, group] for share in range(shares)], axis=0)
        product = lax.dot_general(
            summed[group], tile, (((1,), (1,)), ((), ())), preferred_element_type=jnp.float32
        )
        total = product if total is None else total + product
    out[0] = total.astype(jnp.bfloat16)


def feature_rows(summed, weight):
    groups, rows, width = summed.shape
    devs, _, height, _ = weight.shape
    shares = devs // groups
    return pl.pallas_call(
        functools.partial(feature_kernel, groups, shares),
        grid=(groups,),
        in_specs=[
            pl.BlockSpec((groups, rows, width), lambda i: (0, 0, 0)),
            pl.BlockSpec((shares, groups, height, width), lambda i: (i, 0, 0, 0)),
        ],
        out_specs=pl.BlockSpec((1, rows, width), lambda i: (i, 0, 0)),
        out_shape=jax.ShapeDtypeStruct((groups, rows, width), jnp.bfloat16),
        compiler_params=params(),
        cost_estimate=pl.CostEstimate(
            flops=2 * rows * (groups * width) ** 2,
            bytes_accessed=2 * (groups * width) ** 2 + 4 * groups * rows * width,
            transcendentals=0,
        ),
        name="feature_rows",
    )(summed, weight)


def routes(shuffle_from, my_index, blocks, devs, slots):
    owner = (shuffle_from // blocks).reshape(devs, blocks)
    earlier = jnp.arange(blocks)[None, :] < jnp.arange(blocks)[:, None]
    slot = jnp.sum(((owner[:, None, :] == owner[:, :, None]) & earlier[None]).astype(jnp.int32), axis=2)
    sender = jnp.arange(devs, dtype=jnp.int32)[:, None]
    places = lax.dynamic_slice_in_dim(owner * slots + slot, my_index, 1, 0)[0]
    landing = (sender * slots + slot).reshape(-1)
    mine = my_index * blocks + jnp.arange(blocks, dtype=jnp.int32)
    found = shuffle_from[None, :] == mine[:, None]
    sources = jnp.sum(jnp.where(found, landing[None, :], 0), axis=1)
    return places, sources


def local(
    features,
    weight,
    pre_clean,
    pre_corrupt,
    grad_clean,
    grad_corrupt,
    slopes,
    adj_vals,
    adj_cols,
    adj_count,
    shuffle_from,
):
    row_count, width = features.shape
    blocks, tile_slots, tile_rows, _ = adj_vals.shape
    reach = (tile_slots - 1) // 2
    my_index = lax.axis_index("node")
    devs = lax.axis_size("node")
    groups = lax.axis_size("chan")
    slots = -(-blocks // devs)

    live = jnp.arange(tile_slots)[None, :] < adj_count[:, None]
    targets = jnp.where(live, adj_cols - (my_index * blocks - reach), -1)
    slopes = slopes[None, :]
    down, up = border(
        targets, grad_clean, pre_clean, grad_corrupt, pre_corrupt, slopes, adj_vals, reach
    )
    from_prev = shifted(up, "node", 1)
    from_next = shifted(down, "node", -1)
    feature_cols = exchanged(features.reshape(groups, -1, width), "chan")
    whole_weight = lax.all_gather(weight, ("node", "chan"), axis=0)
    whole_weight = whole_weight.reshape(devs, groups, *weight.shape)

    places, sources = routes(shuffle_from, my_index, blocks, devs, slots)
    clean, outgoing = inner(
        targets,
        places,
        grad_clean,
        pre_clean,
        grad_corrupt,
        pre_corrupt,
        slopes,
        adj_vals,
        reach,
        devs * slots,
    )
    outgoing = patch(places, outgoing, from_prev, from_next, blocks)
    incoming = exchanged(outgoing, "node")
    summed = merge(sources, clean, from_prev, from_next, incoming)
    summed = exchanged(summed.reshape(groups, -1, width), "chan")

    keep, send = weight_partial(my_index[None], feature_cols, summed, devs)
    rows_out = feature_rows(summed, whole_weight)
    grad_features = exchanged(rows_out, "chan").reshape(row_count, width)

    bit = 1
    while True:
        total = keep.astype(jnp.float32) + swapped(send, "node", bit).astype(jnp.float32)
        bit *= 2
        if bit == devs:
            break
        half = total.shape[0] // 2
        keep, send = total[:half], total[half:].astype(jnp.bfloat16)
    parts = exchanged(total[0].astype(jnp.bfloat16), "chan")
    grad_weight = jnp.sum(parts.astype(jnp.float32), axis=0)
    return (grad_weight, grad_features)


def solution(mesh):
    placed = (
        P("node", "chan"),
        P("node", "chan"),
        P("node", "chan"),
        P("node", "chan"),
        P("node", "chan"),
        P("node", "chan"),
        P("chan"),
        P("node", None, None, None),
        P("node", None),
        P("node"),
        P(),
    )
    return jax.shard_map(
        local,
        mesh=mesh,
        in_specs=placed,
        out_specs=(P("node", "chan"), P("node", "chan")),
        check_vma=False,
    )
```

time: 353 us -> 200 us (0.57)
  waiting for transfers between devices: 221 us -> 89.8 us
  local copies, waits for them, and re-layouts: 62.4 us -> 13.3 us
  Pallas kernels: 0 us -> 29.5 us
  matrix products: 27.8 us -> 0 us
  starting transfers between devices: 4 us -> 22.8 us
  blocking collectives: 15.3 us -> 23.6 us
    all_gather x2 -> x1, waiting for transfers between devices: 102 us -> 2.42 us  [local(): whole_weight = lax.all_gather(weight, ('node', 'chan'), axis=0)]
    reduce_scatter x1 -> x0, waiting for transfers between devices: 69 us -> none  [local(): lax.psum_scatter(partial_x.astype(jnp.bfloat16), 'chan', scatter_dimensio...]
    all_to_all x0 -> x4, waiting for transfers between devices: none -> 61.1 us  [exchanged(): return lax.all_to_all(value, axis, split_axis=0, concat_axis=0, tiled=True)]
    psum x1 -> x0, waiting for transfers between devices: 47.3 us -> none  [local(): lax.psum(partial_w.astype(jnp.bfloat16), 'node').astype(jnp.float32)]
    pallas_call x0 -> x6, Pallas kernels: none -> 29.5 us  [the longest x1 11.5 us: inner(): pl.pallas_call(functools.partial(inner_kernel, reach, blocks, slots, widt...]
    dot_general x4 -> x0, matrix products: 27.8 us -> none  [the longest x1 10.2 us: local(): jnp.dot(chooser, contrib.reshape(blocks * tile_slots, -1), precision=lax....]
    ppermute x0 -> x3, waiting for transfers between devices: none -> 25.6 us  [swapped(): return lax.ppermute(value, axis, [(i, i ^ bit) for i in range(size)])]
    all_to_all x0 -> x1, blocking collectives: none -> 23.6 us  [exchanged(): return lax.all_to_all(value, axis, split_axis=0, concat_axis=0, tiled=True)]
  transfers between devices with their start and end apart: 6 -> 10, of which waited for: 5 -> 8; matrix products, arithmetic and copies ran while one was open for 6% -> 3% of each run, Pallas kernels for 0% -> 12%
where the time goes in v1:
time: 200 us; the launch traced here: 199 us
  waiting for transfers between devices  89.8 us (45%)
  Pallas kernels  29.5 us (15%)
  blocking collectives  23.6 us (12%)
  starting transfers between devices  22.8 us (11%)
  between operations  14.3 us (7%)
  local copies, waits for them, and re-layouts  13.3 us (7%)
  other arithmetic  5.9 us (3%)
    all_to_all x4, waiting for transfers between devices, exchanged(): return lax.all_to_all(value, axis, split_axis=0, concat_axis=0, tiled=True)  61.1 us
    ppermute x3, waiting for transfers between devices, swapped(): return lax.ppermute(value, axis, [(i, i ^ bit) for i in range(size)])  25.6 us
    all_to_all x1, blocking collectives, exchanged(): return lax.all_to_all(value, axis, split_axis=0, concat_axis=0, tiled=True)  23.6 us
    all_to_all x4, starting transfers between devices, exchanged(): return lax.all_to_all(value, axis, split_axis=0, concat_axis=0, tiled=True)  16.5 us
    unnamed x36, local copies, waits for them, and re-layouts  11.7 us
    pallas_call x1, Pallas kernels, inner(): pl.pallas_call(functools.partial(inner_kernel, reach, blocks, slots, widt...  11.5 us
    pallas_call x1, Pallas kernels, weight_partial(): pl.pallas_call(functools.partial(weight_kernel, groups, shares, bits), gr...  5.28 us
    pallas_call x1, Pallas kernels, merge(): pl.pallas_call(functools.partial(merge_kernel, reach, blocks), grid_spec=...  5.18 us
  transfers between devices with their start and end apart: 10, of which 8 were waited for; matrix products, arithmetic and copies ran while one was open for 3% of the time, Pallas kernels for 12%

profile of v1, /device:TPU:0, one launch (start us, length us, event | category | flops | bytes accessed | tf_op | source)
XLA Modules:
  0.0 199.1 jit_solution(5024455762029315725)
XLA Ops:
  7.2 0.8 copy.25
  7.9 0.7 subtract_select_fusion.targets
  8.7 1.2 copy-done
  9.9 1.2 copy-done.2
  11.0 1.2 copy-done.4
  12.2 1.2 copy-done.6
  13.4 0.7 copy-done.11
  14.1 0.0 copy-start.12
  14.1 4.1 %border.1 = (bf16[2,2,128,256]{3,2,1,0:T(8,128)(2,1)S(1)}, bf16[2,2,128,256]{3,2,1,0:T(8,128)(2,1)}) custom-call(s32[14,5]{1,0:T(8,128)S(1)} %subtract_select_fusion.targets, bf16[1792,256]{1,0:T(8,128)(2,1)S(1)} %copy-done, bf16[1792,256]{1,0:T(8,128)(2,1)S(1)} %copy-done.2, bf16[1792,256]{1,0:T(8,128)(2,1)S(1)} %copy-done.4, ...), custom_call_target="tpu_custom_call" | custom-call | tf_op jit(solution)/shard_map/border/pallas_call | solution.py:83
  18.2 2.5 %collective-permute-start = (bf16[2,2,128,256]{3,2,1,0:T(8,128)(2,1)}, bf16[2,2,128,256]{3,2,1,0:T(8,128)(2,1)S(1)}, u32[]{:S(2)}, u32[]{:S(2)}) collective-permute-start(bf16[2,2,128,256]{3,2,1,0:T(8,128)(2,1)} %get-tuple-element.9), channel_id=1, source_target_pairs={{0,4},{4,8},{8,12},{12,16},{16,20},{20,24},{24,28},{1,5},{5,9},{9,... | collective-permute-start | bytes 786440 | tf_op jit(solution)/shard_map/ppermute | solution.py:20
  20.7 1.3 collective-permute-start.1
  22.0 0.0 copy-done.15
  22.1 0.5 and_select_fusion
  22.6 0.6 iota_compare_fusion.1
  23.2 0.7 eq.31
  23.9 0.7 copy.23
  24.6 1.1 convert_reduce_fusion.1
  25.7 0.0 copy-start.13
  25.7 0.6 copy-done.13
  26.3 0.9 fusion.2.places
  27.1 0.0 copy-done.1
  27.2 0.0 copy-start.7
  27.2 1.2 copy-done.7
  28.4 11.5 %inner.1 = (bf16[14,128,256]{2,1,0:T(8,128)(2,1)S(1)}, bf16[16,128,256]{2,1,0:T(8,128)(2,1)S(1)}) custom-call(s32[14,5]{1,0:T(8,128)S(1)} %subtract_select_fusion.targets, s32[14]{0:T(128)S(1)} %fusion.2.places, bf16[1792,256]{1,0:T(8,128)(2,1)S(1)} %copy-done.1, bf16[1792,256]{1,0:T(8,128)(2,1)S(1)} %copy-done.3, bf16[1792,256]{1,0:T(8,128)(2,1)S(1)} %copy-done.5, ...), custom_call_target="tpu_custom_call" | custom-call | flops 1174405120 | bytes 7798784 | tf_op jit(solution)/shard_map/inner/pallas_call | solution.py:140
  39.9 0.0 copy-start.9
  39.9 0.0 collective-permute-done.low
  39.9 0.0 collective-permute-done.1.high
  39.9 0.7 patch.1
  40.7 0.0 copy-start.16
  40.7 23.6 %all_to_all.25.incoming = bf16[16,128,256]{2,1,0:T(8,128)(2,1)S(1)} all-to-all(bf16[16,128,256]{2,1,0:T(8,128)(2,1)S(1)} %patch.1), channel_id=1, replica_groups=mesh['node'=8,'chan'=4] {'node'}, dimensions={0} | all-to-all | bytes 2097152 | tf_op jit(solution)/shard_map/all_to_all | solution.py:29
  64.2 4.9 %all-to-all-start = ((bf16[4,448,256]{2,1,0:T(8,128)(2,1)}), bf16[4,448,256]{2,1,0:T(8,128)(2,1)S(1)}, u32[]{:S(2)}, u32[]{:S(2)}) async-start(bf16[4,448,256]{2,1,0:T(8,128)(2,1)} %bitcast.12), calls=%async_computation | async-start | bytes 1835008 | tf_op jit(solution)/shard_map/all_to_all | solution.py:29
  69.1 0.0 copy-done.14
  69.1 0.1 copy.24
  69.2 0.1 broadcast_add_fusion
  69.3 0.1 add.46
  69.4 0.0 copy-done.16
  69.4 0.2 select_reduce_fusion.sources
  69.6 1.2 copy-done.10
  70.7 5.2 %merge.1 = bf16[1792,256]{1,0:T(8,128)(2,1)} custom-call(s32[14]{0:T(128)S(1)} %select_reduce_fusion.sources, bf16[14,128,256]{2,1,0:T(8,128)(2,1)S(1)} %copy-done.10, bf16[2,2,128,256]{3,2,1,0:T(8,128)(2,1)S(1)} %collective-permute-done.low, bf16[2,2,128,256]{3,2,1,0:T(8,128)(2,1)S(1)} %collective-permute-done.1.high, ...), custom_call_target="tpu_custom_call" | custom-call | tf_op jit(solution)/shard_map/merge/pallas_call | solution.py:233
  75.9 15.5 %all-to-all-done.feats = bf16[4,448,256]{2,1,0:T(8,128)(2,1)S(1)} async-done(((bf16[4,448,256]{2,1,0:T(8,128)(2,1)}), bf16[4,448,256]{2,1,0:T(8,128)(2,1)S(1)}, u32[]{:S(2)}, u32[]{:S(2)}) %all-to-all-start) | async-done | bytes 917536 | tf_op jit(solution)/shard_map/all_to_all | solution.py:29
  91.4 3.5 %all-to-all-start.2 = ((bf16[4,448,256]{2,1,0:T(8,128)(2,1)}), bf16[4,448,256]{2,1,0:T(8,128)(2,1)S(1)}, u32[]{:S(2)}, u32[]{:S(2)}) async-start(bf16[4,448,256]{2,1,0:T(8,128)(2,1)} %bitcast.3), calls=%async_computation.2 | async-start | bytes 1835008 | tf_op jit(solution)/shard_map/all_to_all | solution.py:29
  94.9 0.0 all-gather.3.cloned.1.call-start
  94.9 0.7 all-gather.3.cloned.1.call-update
  95.6 22.7 %all-to-all-done.2.summed = bf16[4,448,256]{2,1,0:T(8,128)(2,1)S(1)} async-done(((bf16[4,448,256]{2,1,0:T(8,128)(2,1)}), bf16[4,448,256]{2,1,0:T(8,128)(2,1)S(1)}, u32[]{:S(2)}, u32[]{:S(2)}) %all-to-all-start.2) | async-done | bytes 917536 | tf_op jit(solution)/shard_map/all_to_all | solution.py:29
  118.3 5.3 %weight_partial.1 = (bf16[4,4,128,256]{3,2,1,0:T(8,128)(2,1)S(1)}, bf16[4,4,128,256]{3,2,1,0:T(8,128)(2,1)S(1)}) custom-call(s32[1]{0:T(128)} %bitcast.me, bf16[4,448,256]{2,1,0:T(8,128)(2,1)S(1)} %all-to-all-done.feats, bf16[4,448,256]{2,1,0:T(8,128)(2,1)S(1)} %all-to-all-done.2.summed), custom_call_target="tpu_custom_call" | custom-call | flops 939524096 | bytes 3932160 | tf_op jit(solution)/shard_map/weight_partial/pallas_call | solution.py:287
  123.6 0.1 collective-permute-start.2
  123.7 2.6 %collective-permute-done.2 = bf16[4,4,128,256]{3,2,1,0:T(8,128)(2,1)S(1)} collective-permute-done((bf16[4,4,128,256]{3,2,1,0:T(8,128)(2,1)S(1)}, bf16[4,4,128,256]{3,2,1,0:T(8,128)(2,1)S(1)}, u32[]{:S(2)}, u32[]{:S(2)}) %collective-permute-start.2) | collective-permute-done | bytes 1048608 | tf_op jit(solution)/shard_map/ppermute | solution.py:25
  126.3 0.3 convert_add_fusion
  126.6 0.1 slice.30
  126.7 1.4 collective-permute-start.3
  128.1 12.7 %collective-permute-done.3 = bf16[2,4,128,256]{3,2,1,0:T(8,128)(2,1)S(1)} collective-permute-done((bf16[2,4,128,256]{3,2,1,0:T(8,128)(2,1)S(1)}, bf16[2,4,128,256]{3,2,1,0:T(8,128)(2,1)S(1)}, u32[]{:S(2)}, u32[]{:S(2)}) %collective-permute-start.3) | collective-permute-done | bytes 524320 | tf_op jit(solution)/shard_map/ppermute | solution.py:25
  140.7 0.1 slice_add_fusion
  140.9 1.0 collective-permute-start.4
  141.9 10.3 %collective-permute-done.4 = bf16[1,4,128,256]{3,2,1,0:T(8,128)(2,1)S(1)} collective-permute-done((bf16[1,4,128,256]{3,2,1,0:T(8,128)(2,1)S(1)}, bf16[1,4,128,256]{3,2,1,0:T(8,128)(2,1)S(1)}, u32[]{:S(2)}, u32[]{:S(2)}) %collective-permute-start.4) | collective-permute-done | bytes 262176 | tf_op jit(solution)/shard_map/ppermute | solution.py:25
  152.2 0.8 fusion.1
  152.9 4.6 %all-to-all-start.3 = ((bf16[4,128,256]{2,1,0:T(8,128)(2,1)}), bf16[4,128,256]{2,1,0:T(8,128)(2,1)S(1)}, u32[]{:S(2)}, u32[]{:S(2)}) async-start(bf16[4,128,256]{2,1,0:T(8,128)(2,1)} %fusion.1), calls=%async_computation.3 | async-start | bytes 524288 | tf_op jit(solution)/shard_map/all_to_all | solution.py:29
  157.5 2.4 %all-gather.3.cloned.1.call-done = bf16[4096,256]{1,0:T(8,128)(2,1)} async-done(((bf16[128,256]{1,0:T(8,128)(2,1)}), bf16[4096,256]{1,0:T(8,128)(2,1)}) %all-gather.3.cloned.1.call-update) | async-done | bytes 2097168 | tf_op jit(solution)/shard_map/all_gather | solution.py:386
  160.0 1.6 copy-done.8
  161.6 2.7 %feature_rows.1 = bf16[4,448,256]{2,1,0:T(8,128)(2,1)} custom-call(bf16[4,448,256]{2,1,0:T(8,128)(2,1)S(1)} %all-to-all-done.2.summed, bf16[8,4,128,256]{3,2,1,0:T(8,128)(2,1)S(1)} %bitcast.8), custom_call_target="tpu_custom_call" | custom-call | flops 939524096 | bytes 3932160 | tf_op jit(solution)/shard_map/feature_rows/pallas_call | solution.py:324
  164.3 0.1 all-to-all-done.3
  164.4 3.5 %all-to-all-start.4 = ((bf16[4,448,256]{2,1,0:T(8,128)(2,1)}), bf16[4,448,256]{2,1,0:T(8,128)(2,1)S(1)}, u32[]{:S(2)}, u32[]{:S(2)}) async-start(bf16[4,448,256]{2,1,0:T(8,128)(2,1)} %feature_rows.1), calls=%async_computation.4 | async-start | bytes 1835008 | tf_op jit(solution)/shard_map/all_to_all | solution.py:29
  167.9 0.7 convert_reduce_fusion
  168.6 22.8 %all-to-all-done.4 = bf16[4,448,256]{2,1,0:T(8,128)(2,1)S(1)} async-done(((bf16[4,448,256]{2,1,0:T(8,128)(2,1)}), bf16[4,448,256]{2,1,0:T(8,128)(2,1)S(1)}, u32[]{:S(2)}, u32[]{:S(2)}) %all-to-all-start.4) | async-done | bytes 917536 | tf_op jit(solution)/shard_map/all_to_all | solution.py:29
  191.4 0.9 copy.29
  (19 shorter events, 0.1 us)
Async XLA Ops:
  8.7 1.2 copy-start
  9.9 1.2 copy-start.2
  11.0 1.2 copy-start.4
  12.2 1.2 copy-start.6
  13.4 0.7 copy-start.11
  14.1 8.0 %copy-start.15 = (s32[112]{0:T(128)S(1)}, s32[112]{0:T(128)}, u32[]{:S(2)}) copy-start(s32[112]{0:T(128)} %param.21) | copy-start | bytes 1348
  14.1 13.1 %copy-start.1 = (bf16[1792,256]{1,0:T(8,128)(2,1)S(1)}, bf16[1792,256]{1,0:T(8,128)(2,1)}, u32[]{:S(2)}) copy-start(bf16[1792,256]{1,0:T(8,128)(2,1)} %gc.3) | copy-start | bytes 2752516
  14.1 13.1 %copy-start.3 = (bf16[1792,256]{1,0:T(8,128)(2,1)S(1)}, bf16[1792,256]{1,0:T(8,128)(2,1)}, u32[]{:S(2)}) copy-start(bf16[1792,256]{1,0:T(8,128)(2,1)} %pc.3) | copy-start | bytes 2752516
  14.1 13.1 %copy-start.5 = (bf16[1792,256]{1,0:T(8,128)(2,1)S(1)}, bf16[1792,256]{1,0:T(8,128)(2,1)}, u32[]{:S(2)}) copy-start(bf16[1792,256]{1,0:T(8,128)(2,1)} %gx.3) | copy-start | bytes 2752516
  14.1 13.1 %copy-start.12 = (f32[256]{0:T(256)S(1)}, f32[256]{0:T(256)}, u32[]{:S(2)}) copy-start(f32[256]{0:T(256)} %param.17) | copy-start | bytes 3076
  18.2 21.7 %collective-permute-start = (bf16[2,2,128,256]{3,2,1,0:T(8,128)(2,1)}, bf16[2,2,128,256]{3,2,1,0:T(8,128)(2,1)S(1)}, u32[]{:S(2)}, u32[]{:S(2)}) collective-permute-start(bf16[2,2,128,256]{3,2,1,0:T(8,128)(2,1)} %get-tuple-element.9), channel_id=1, source_target_pairs={{0,4},{4,8},{8,12},{12,16},{16,20},{20,24},{24,28},{1,5},{5,9},{9,... | collective-permute-start | bytes 786440 | tf_op jit(solution)/shard_map/ppermute | solution.py:20
  20.7 19.2 %collective-permute-start.1 = (bf16[2,2,128,256]{3,2,1,0:T(8,128)(2,1)S(1)}, bf16[2,2,128,256]{3,2,1,0:T(8,128)(2,1)S(1)}, u32[]{:S(2)}, u32[]{:S(2)}) collective-permute-start(bf16[2,2,128,256]{3,2,1,0:T(8,128)(2,1)S(1)} %get-tuple-element.10), channel_id=1, source_target_pairs={{4,0},{8,4},{12,8},{16,12},{20,16},{24,20},{28,24},{5,1},{9,5},{13... | collective-permute-start | bytes 786440 | tf_op jit(solution)/shard_map/ppermute | solution.py:20
  25.7 0.6 copy-start.13
  27.2 1.2 copy-start.7
  39.9 24.3 %copy-start.9 = (bf16[14,128,256]{2,1,0:T(8,128)(2,1)}, bf16[14,128,256]{2,1,0:T(8,128)(2,1)S(1)}, u32[]{:S(2)}) copy-start(bf16[14,128,256]{2,1,0:T(8,128)(2,1)S(1)} %get-tuple-element.8.clean) | copy-start | bytes 2752516
  40.7 28.5 %copy-start.14 = (s32[8,14]{0,1:T(8,128)S(1)}, s32[8,14]{0,1:T(8,128)}, u32[]{:S(2)}) copy-start(s32[8,14]{0,1:T(8,128)} %copy-done.13) | copy-start | bytes 1348
  40.7 28.7 %copy-start.16 = (s32[112]{0:T(128)S(1)}, s32[112]{0:T(128)}, u32[]{:S(2)}) copy-start(s32[112]{0:T(128)} %param.21) | copy-start | bytes 1348
  64.2 27.1 %all-to-all-start = ((bf16[4,448,256]{2,1,0:T(8,128)(2,1)}), bf16[4,448,256]{2,1,0:T(8,128)(2,1)S(1)}, u32[]{:S(2)}, u32[]{:S(2)}) async-start(bf16[4,448,256]{2,1,0:T(8,128)(2,1)} %bitcast.12), calls=%async_computation | async-start | bytes 1835008 | tf_op jit(solution)/shard_map/all_to_all | solution.py:29
  69.6 1.2 copy-start.10
  91.4 27.0 %all-to-all-start.2 = ((bf16[4,448,256]{2,1,0:T(8,128)(2,1)}), bf16[4,448,256]{2,1,0:T(8,128)(2,1)S(1)}, u32[]{:S(2)}, u32[]{:S(2)}) async-start(bf16[4,448,256]{2,1,0:T(8,128)(2,1)} %bitcast.3), calls=%async_computation.2 | async-start | bytes 1835008 | tf_op jit(solution)/shard_map/all_to_all | solution.py:29
  94.9 65.1 %all-gather.3.cloned.1.call-start = ((), (), s32[]{:S(2)}) async-start(), calls=%async_computation.5 | async-start | bytes 2162688 | tf_op jit(solution)/shard_map/all_gather | solution.py:386
  123.6 2.7 %collective-permute-start.2 = (bf16[4,4,128,256]{3,2,1,0:T(8,128)(2,1)S(1)}, bf16[4,4,128,256]{3,2,1,0:T(8,128)(2,1)S(1)}, u32[]{:S(2)}, u32[]{:S(2)}) collective-permute-start(bf16[4,4,128,256]{3,2,1,0:T(8,128)(2,1)S(1)} %get-tuple-element.13), channel_id=1, source_target_pairs={{0,4},{4,0},{8,12},{12,8},{16,20},{20,16},{24,28},{28,24},{1,5},{5... | collective-permute-start | bytes 3145736 | tf_op jit(solution)/shard_map/ppermute | solution.py:25
  126.7 14.0 %collective-permute-start.3 = (bf16[2,4,128,256]{3,2,1,0:T(8,128)(2,1)S(1)}, bf16[2,4,128,256]{3,2,1,0:T(8,128)(2,1)S(1)}, u32[]{:S(2)}, u32[]{:S(2)}) collective-permute-start(bf16[2,4,128,256]{3,2,1,0:T(8,128)(2,1)S(1)} %slice.30), channel_id=1, source_target_pairs={{0,8},{4,12},{8,0},{12,4},{16,24},{20,28},{24,16},{28,20},{1,9},{5... | collective-permute-start | bytes 1572872 | tf_op jit(solution)/shard_map/ppermute | solution.py:25
  140.9 11.3 %collective-permute-start.4 = (bf16[1,4,128,256]{3,2,1,0:T(8,128)(2,1)S(1)}, bf16[1,4,128,256]{3,2,1,0:T(8,128)(2,1)S(1)}, u32[]{:S(2)}, u32[]{:S(2)}) collective-permute-start(bf16[1,4,128,256]{3,2,1,0:T(8,128)(2,1)S(1)} %slice.31), channel_id=1, source_target_pairs={{0,16},{4,20},{8,24},{12,28},{16,0},{20,4},{24,8},{28,12},{1,17},{... | collective-permute-start | bytes 786440 | tf_op jit(solution)/shard_map/ppermute | solution.py:25
  152.9 11.5 %all-to-all-start.3 = ((bf16[4,128,256]{2,1,0:T(8,128)(2,1)}), bf16[4,128,256]{2,1,0:T(8,128)(2,1)S(1)}, u32[]{:S(2)}, u32[]{:S(2)}) async-start(bf16[4,128,256]{2,1,0:T(8,128)(2,1)} %fusion.1), calls=%async_computation.3 | async-start | bytes 524288 | tf_op jit(solution)/shard_map/all_to_all | solution.py:29
  160.0 1.6 copy-start.8
  164.4 27.0 %all-to-all-start.4 = ((bf16[4,448,256]{2,1,0:T(8,128)(2,1)}), bf16[4,448,256]{2,1,0:T(8,128)(2,1)S(1)}, u32[]{:S(2)}, u32[]{:S(2)}) async-start(bf16[4,448,256]{2,1,0:T(8,128)(2,1)} %feature_rows.1), calls=%async_computation.4 | async-start | bytes 1835008 | tf_op jit(solution)/shard_map/all_to_all | solution.py:29
Sparse Core Ops, SparseCore 0:
  98.7 61.2 all-gather.2

commit v2 on v0

v2 whole, which is shorter than its diff:
```python
import functools
import math

import jax
import jax.numpy as jnp
from jax import lax
from jax.experimental import pallas as pl
from jax.experimental.pallas import tpu as pltpu
from jax.sharding import PartitionSpec as P

VMEM_LIMIT = 32 * 1024 * 1024
VMEM_ALL = 61 * 1024 * 1024
IN_VMEM = pl.BlockSpec(memory_space=pltpu.VMEM)
IN_SMEM = pl.BlockSpec(memory_space=pltpu.SMEM)
IN_HBM = pl.BlockSpec(memory_space=pltpu.HBM)


def params(limit=VMEM_LIMIT):
    return pltpu.CompilerParams(vmem_limit_bytes=limit)


def bf16(*shape):
    return jax.ShapeDtypeStruct(shape, jnp.bfloat16)


def wide(value):
    return value.astype(jnp.float32)


def shifted(value, axis, by):
    size = lax.axis_size(axis)
    pairs = [(i, i + by) for i in range(size) if 0 <= i + by < size]
    return lax.ppermute(value, axis, pairs)


def swapped(value, axis, by):
    size = lax.axis_size(axis)
    return lax.ppermute(value, axis, [(i, i ^ by) for i in range(size)])


def masked_grad(grad, pre, slope):
    return (wide(grad) * jnp.where(wide(pre) > 0, 1.0, slope)).astype(jnp.bfloat16)


def add_products(block, slot, slots, place, data, tiles, slopes, acc):
    gc, pc, gx, px = (data[i, slot] for i in range(4))
    slope = slopes[...]
    rhs = jnp.concatenate([masked_grad(gc, pc, slope), masked_grad(gx, px, slope)], axis=1)
    rows = tiles.shape[2]
    lhs = jnp.concatenate([tiles[slot, k].T for k in range(slots)], axis=0)
    product = jnp.dot(lhs, rhs, preferred_element_type=jnp.float32)
    for k in range(slots):
        acc[place(block, k)] += product[k * rows : (k + 1) * rows]


def block_copies(block, slot, rows, inputs, adj, data, tiles, sems):
    span = pl.ds(pl.multiple_of(block * rows, rows), rows)
    copies = [
        pltpu.make_async_copy(ref.at[span], data.at[i, slot], sems.at[i, slot])
        for i, ref in enumerate(inputs)
    ]
    return copies + [pltpu.make_async_copy(adj.at[block], tiles.at[slot], sems.at[4, slot])]


def border_kernel(
    reach, me, cols, count, gc, pc, gx, px, slopes, adj, down, up, data, tiles, acc, sems
):
    blocks, slots, rows, _ = adj.shape
    width = gc.shape[1]
    border = [*range(reach), *range(blocks - reach, blocks)]

    def copies(i):
        return block_copies(border[i], i, rows, (gc, pc, gx, px), adj, data, tiles, sems)

    for i in range(2 * reach):
        for copy in copies(i):
            copy.start()
    acc[...] = jnp.zeros_like(acc)

    def place(block, k):
        target = cols[k, block] - me[0] * blocks
        live = k < count[block]
        below = live & (target < 0)
        above = live & (target >= blocks)
        return jnp.where(below, target + reach, jnp.where(above, target - blocks + reach, 2 * reach))

    for i in range(2 * reach):
        for copy in copies(i):
            copy.wait()
        add_products(border[i], i, slots, place, data, tiles, slopes, acc)
    for which in range(2):
        part = acc[: 2 * reach, :, which * width : (which + 1) * width].astype(jnp.bfloat16)
        down[which] = part[:reach]
        up[which] = part[reach:]


def border(me, cols, count, gc, pc, gx, px, slopes, adj, reach):
    _, slots, rows, _ = adj.shape
    width = gc.shape[1]
    return pl.pallas_call(
        functools.partial(border_kernel, reach),
        in_specs=[IN_SMEM] * 3 + [IN_HBM] * 4 + [IN_VMEM, IN_HBM],
        out_specs=[IN_VMEM] * 2,
        out_shape=[bf16(2, reach, rows, width)] * 2,
        scratch_shapes=[
            pltpu.VMEM((4, 2 * reach, rows, width), jnp.bfloat16),
            pltpu.VMEM((2 * reach, slots, rows, rows), jnp.bfloat16),
            pltpu.VMEM((2 * reach + 1, rows, 2 * width), jnp.float32),
            pltpu.SemaphoreType.DMA((5, 2 * reach)),
        ],
        compiler_params=params(VMEM_ALL),
        cost_estimate=pl.CostEstimate(
            flops=8 * reach * slots * rows * rows * width,
            bytes_accessed=16 * reach * rows * width + 4 * reach * slots * rows * rows,
            transcendentals=0,
        ),
        name="border",
    )(me, cols, count, gc, pc, gx, px, slopes, adj)


def inner_kernel(me, cols, count, gc, pc, gx, px, slopes, adj, clean, corrupt, data, tiles, acc, sems):
    blocks, slots, rows, _ = adj.shape
    width = gc.shape[1]

    def copies(block):
        return block_copies(block, block, rows, (gc, pc, gx, px), adj, data, tiles, sems)

    for block in range(blocks):
        for copy in copies(block):
            copy.start()
    acc[...] = jnp.zeros_like(acc)

    def place(block, k):
        target = cols[k, block] - me[0] * blocks
        inside = (k < count[block]) & (target >= 0) & (target < blocks)
        return jnp.where(inside, target, blocks)

    per_step = 2 - blocks % 2

    @pl.loop(0, blocks // per_step)
    def _(step):
        for i in range(per_step):
            for copy in copies(step * per_step + i):
                copy.wait()
        for i in range(per_step):
            block = step * per_step + i
            add_products(block, block, slots, place, data, tiles, slopes, acc)

    @pl.loop(0, blocks)
    def _(block):
        clean[block] = acc[block, :, :width].astype(jnp.bfloat16)
        corrupt[block] = acc[block, :, width:].astype(jnp.bfloat16)


def inner(me, cols, count, gc, pc, gx, px, slopes, adj):
    blocks, slots, rows, _ = adj.shape
    width = gc.shape[1]
    return pl.pallas_call(
        inner_kernel,
        in_specs=[IN_SMEM] * 3 + [IN_HBM] * 4 + [IN_VMEM, IN_HBM],
        out_specs=[IN_VMEM] * 2,
        out_shape=[bf16(blocks, rows, width)] * 2,
        scratch_shapes=[
            pltpu.VMEM((4, blocks, rows, width), jnp.bfloat16),
            pltpu.VMEM((blocks, slots, rows, rows), jnp.bfloat16),
            pltpu.VMEM((blocks + 1, rows, 2 * width), jnp.float32),
            pltpu.SemaphoreType.DMA((5, blocks)),
        ],
        compiler_params=params(),
        cost_estimate=pl.CostEstimate(
            flops=4 * blocks * slots * rows * rows * width,
            bytes_accessed=12 * blocks * rows * width + 2 * blocks * slots * rows * rows,
            transcendentals=0,
        ),
        name="inner",
    )(me, cols, count, gc, pc, gx, px, slopes, adj)


def route_kernel(reach, slots, me, shuffle, clean, corrupt, low, high, whole, outgoing, used):
    blocks = clean.shape[0]
    for i in range(outgoing.shape[0] // slots):
        used[i] = 0
    for block in range(blocks):
        owner = shuffle[me[0] * blocks + block] // blocks
        slot = used[owner]
        used[owner] = slot + 1
        mine, theirs = clean[block], corrupt[block]
        if block < reach:
            mine = (wide(mine) + wide(low[0, block])).astype(jnp.bfloat16)
            theirs = (wide(theirs) + wide(low[1, block])).astype(jnp.bfloat16)
        elif block >= blocks - reach:
            at = block - (blocks - reach)
            mine = (wide(mine) + wide(high[0, at])).astype(jnp.bfloat16)
            theirs = (wide(theirs) + wide(high[1, at])).astype(jnp.bfloat16)
        whole[block] = mine
        outgoing[owner * slots + slot] = theirs


def route(me, shuffle, clean, corrupt, low, high, devs, slots):
    blocks, rows, width = clean.shape
    return pl.pallas_call(
        functools.partial(route_kernel, low.shape[1], slots),
        in_specs=[IN_SMEM] * 2 + [IN_VMEM] * 4,
        out_specs=[IN_VMEM] * 2,
        out_shape=[bf16(blocks, rows, width), bf16(devs * slots, rows, width)],
        scratch_shapes=[pltpu.SMEM((devs,), jnp.int32)],
        compiler_params=params(),
        name="route",
    )(me, shuffle, clean, corrupt, low, high)


def merge_kernel(quarter, index, landing, clean, incoming, out):
    _, rows, _ = clean.shape
    group = index[1]
    piece = math.gcd(rows, quarter)
    for place in range(incoming.shape[0]):
        block = landing[place]

        @pl.when(block >= 0)
        def _():
            total = (wide(clean[block]) + wide(incoming[place])).astype(jnp.bfloat16)
            for part in range(rows // piece):
                at = block * (rows // piece) + part
                owner = at // (quarter // piece)
                offset = (at - owner * (quarter // piece)) * piece
                out[owner ^ group, pl.ds(pl.multiple_of(offset, piece), piece)] = total[
                    part * piece : (part + 1) * piece
                ]


def merge(index, landing, clean, incoming, groups):
    blocks, rows, width = clean.shape
    quarter = blocks * rows // groups
    return pl.pallas_call(
        functools.partial(merge_kernel, quarter),
        in_specs=[IN_SMEM] * 2 + [IN_VMEM] * 2,
        out_specs=IN_VMEM,
        out_shape=bf16(groups, quarter, width),
        compiler_params=params(),
        name="merge",
    )(index, landing, clean, incoming)


def halving_orders(devs):
    bits = list(range(1, devs.bit_length() - 1))
    return bits, bits[::-1]


def weight_kernel(devs, index, *refs):
    groups = (len(refs) - 2) // 2
    feats, summed, (keep, send) = refs[:groups], refs[groups : 2 * groups], refs[2 * groups :]
    me, group = index[0], index[1]
    shares = devs // groups
    height, width = keep.shape[3:]
    rhs = jnp.concatenate([piece[...] for piece in summed], axis=1)
    for relative in range(groups):
        product = lax.dot_general(
            feats[relative][...],
            rhs,
            (((0,), (0,)), ((), ())),
            preferred_element_type=jnp.float32,
        ).astype(jnp.bfloat16)
        for share in range(shares):
            node = ((group ^ relative) * shares + share) ^ me
            for half, order in enumerate(halving_orders(devs)):
                place = jnp.int32(0)
                for bit in order:
                    place = place * 2 + ((node >> bit) & 1)
                for i in range(groups // 2):
                    column = (half * (groups // 2) + i) * width
                    part = product[share * height : (share + 1) * height, column : column + width]

                    @pl.when((node & 1) == 0)
                    def _():
                        keep[half, place, i] = part

                    @pl.when((node & 1) == 1)
                    def _():
                        send[half, place, i] = part


def weight_partial(index, feats, summed, devs):
    groups = len(feats)
    rows, width = feats[0].shape
    height = groups * width // devs
    return pl.pallas_call(
        functools.partial(weight_kernel, devs),
        in_specs=[IN_SMEM] + [IN_VMEM] * (2 * groups),
        out_specs=[IN_VMEM] * 2,
        out_shape=[bf16(2, devs // 2, groups // 2, height, width)] * 2,
        compiler_params=params(),
        cost_estimate=pl.CostEstimate(
            flops=2 * rows * (groups * width) ** 2,
            bytes_accessed=2 * (groups * width) ** 2 + 4 * groups * rows * width,
            transcendentals=0,
        ),
        name="weight_partial",
    )(index, *feats, *summed)


def feature_kernel(index, *refs):
    *summed, low, high, out = refs
    groups = len(summed)
    devs = low.shape[0]
    me, group = index[0], index[1]
    shares = devs // groups
    lhs = jnp.concatenate([piece[...] for piece in summed], axis=1)
    for relative in range(groups):
        rows = []
        for share in range(shares):
            node = ((group ^ relative) * shares + share) ^ me
            parts = []
            for half, order in zip((low, high), halving_orders(devs)):
                place = jnp.int32(0)
                for j, bit in enumerate([*order, 0]):
                    place += ((node >> bit) & 1) << j
                parts += [half[place, i] for i in range(groups // 2)]
            rows.append(jnp.concatenate(parts, axis=1))
        out[relative] = lax.dot_general(
            lhs,
            jnp.concatenate(rows, axis=0),
            (((1,), (1,)), ((), ())),
            preferred_element_type=jnp.float32,
        ).astype(jnp.bfloat16)


def feature_rows(index, summed, halves):
    groups = len(summed)
    rows, width = summed[0].shape
    return pl.pallas_call(
        feature_kernel,
        in_specs=[IN_SMEM] + [IN_VMEM] * (groups + 2),
        out_specs=IN_VMEM,
        out_shape=bf16(groups, rows, width),
        compiler_params=params(),
        cost_estimate=pl.CostEstimate(
            flops=2 * rows * (groups * width) ** 2,
            bytes_accessed=2 * (groups * width) ** 2 + 4 * groups * rows * width,
            transcendentals=0,
        ),
        name="feature_rows",
    )(index, *summed, *halves)


def gather_kernel(index, *refs):
    *pieces, out, sems = refs
    rows = pieces[0].shape[0]
    copies = [
        pltpu.make_async_copy(
            piece, out.at[pl.ds(pl.multiple_of((index[1] ^ i) * rows, rows), rows)], sems.at[i]
        )
        for i, piece in enumerate(pieces)
    ]
    for copy in copies:
        copy.start()
    for copy in copies:
        copy.wait()


def laid_out(index, pieces):
    rows, width = pieces[0].shape
    return pl.pallas_call(
        gather_kernel,
        in_specs=[IN_SMEM] + [IN_VMEM] * len(pieces),
        out_specs=IN_HBM,
        out_shape=bf16(len(pieces) * rows, width),
        scratch_shapes=[pltpu.SemaphoreType.DMA((len(pieces),))],
        compiler_params=params(),
        name="laid_out",
    )(index, *pieces)


def landing_blocks(shuffle_from, me, blocks, devs, slots):
    owner = (shuffle_from // blocks).reshape(devs, blocks)
    within = (shuffle_from % blocks).reshape(devs, blocks)
    for_me = owner == me
    earlier = jnp.arange(blocks)[None, :] < jnp.arange(blocks)[:, None]
    rank = jnp.sum((for_me[:, None, :] & earlier[None]).astype(jnp.int32), axis=2)
    picked = for_me[:, None, :] & (rank[:, None, :] == jnp.arange(slots)[None, :, None])
    return (jnp.sum(jnp.where(picked, within[:, None, :] + 1, 0), axis=2) - 1).reshape(-1)


def exchange_order(groups):
    return sorted(range(1, groups), reverse=True)


def local(
    features,
    weight,
    pre_clean,
    pre_corrupt,
    grad_clean,
    grad_corrupt,
    slopes,
    adj_vals,
    adj_cols,
    adj_count,
    shuffle_from,
):
    row_count, width = features.shape
    blocks, tile_slots, tile_rows, _ = adj_vals.shape
    reach = (tile_slots - 1) // 2
    me = lax.axis_index("node")
    group = lax.axis_index("chan")
    devs = lax.axis_size("node")
    groups = lax.axis_size("chan")
    slots = -(-blocks // devs)
    quarter = row_count // groups
    index = jnp.stack([me, group])

    args = (index, adj_cols.T, adj_count, grad_clean, pre_clean, grad_corrupt, pre_corrupt)
    args += (slopes[None, :], adj_vals)
    down, up = border(*args, reach)
    from_prev = shifted(up, "node", 1)
    from_next = shifted(down, "node", -1)

    tiles = [weight] + [swapped(weight, "chan", i) for i in range(1, groups)]
    clean, corrupt = inner(*args)
    clean, corrupt, tiles = lax.optimization_barrier((clean, corrupt, tiles))
    clean, outgoing = route(
        index, shuffle_from, clean, corrupt, from_prev, from_next, devs, slots
    )

    feats = [None] * groups
    by_quarter = features.reshape(groups, quarter, width)
    for i in [0, *exchange_order(groups)]:
        piece = lax.dynamic_index_in_dim(by_quarter, group ^ i, 0, keepdims=False)
        feats[i] = swapped(piece, "chan", i) if i else piece
    shuffle_from, outgoing = lax.optimization_barrier((shuffle_from, outgoing))
    landing = landing_blocks(shuffle_from, me, blocks, devs, slots)
    incoming = lax.all_to_all(outgoing, "node", split_axis=0, concat_axis=0, tiled=True)
    orders = halving_orders(devs)
    halves = [jnp.stack(part)[None] for part in (tiles[: groups // 2], tiles[groups // 2 :])]

    def gather_hop(halves, hop):
        return [
            jnp.concatenate([part, swapped(part, "node", 1 << order[hop])], axis=0)
            for part, order in zip(halves, orders)
        ]

    halves = gather_hop(halves, 0)
    incoming, feats, halves = lax.optimization_barrier((incoming, feats, halves))
    merged = merge(index, landing, clean, incoming, groups)
    summed = [merged[0]] + [None] * (groups - 1)
    for i in exchange_order(groups):
        summed[i] = swapped(merged[i], "chan", i)
    for hop in range(1, len(orders[0])):
        halves = gather_hop(halves, hop)
    summed, halves = lax.optimization_barrier((summed, halves))
    halves = [jnp.concatenate([part, swapped(part, "node", 1)], axis=0) for part in halves]

    rows_out = feature_rows(index, summed, halves)
    pieces = [rows_out[0]] + [None] * (groups - 1)
    for i in exchange_order(groups):
        pieces[i] = swapped(rows_out[i], "chan", i)

    keep, send = weight_partial(index, feats, summed, devs)
    total = wide(keep) + wide(swapped(send, "node", 1))
    shares = []
    for part, order in zip((total[0], total[1]), halving_orders(devs)):
        for bit in order:
            size = part.shape[0] // 2
            arrived = swapped(part[size:].astype(jnp.bfloat16), "node", 1 << bit)
            part = part[:size] + wide(arrived)
        shares.append(part[0])
    shares = jnp.concatenate(shares, axis=0)
    grad_weight = shares[0]
    for i in range(1, groups):
        grad_weight = grad_weight + wide(swapped(shares[i].astype(jnp.bfloat16), "chan", i))

    grad_features = laid_out(index, pieces)
    return (grad_weight, grad_features)


def solution(mesh):
    placed = (
        P("node", "chan"),
        P("node", "chan"),
        P("node", "chan"),
        P("node", "chan"),
        P("node", "chan"),
        P("node", "chan"),
        P("chan"),
        P("node", None, None, None),
        P("node", None),
        P("node"),
        P(),
    )
    return jax.shard_map(
        local,
        mesh=mesh,
        in_specs=placed,
        out_specs=(P("node", "chan"), P("node", "chan")),
        check_vma=False,
    )
```

time: 353 us -> 133 us (0.38)
  waiting for transfers between devices: 221 us -> 53.4 us
  local copies, waits for them, and re-layouts: 62.4 us -> 5.3 us
  starting transfers between devices: 4 us -> 39.5 us
  matrix products: 27.8 us -> 0 us
  Pallas kernels: 0 us -> 26.5 us
  blocking collectives: 15.3 us -> 0 us
  between operations: 14 us -> 1.05 us
    all_gather x2 -> x0, waiting for transfers between devices: 102 us -> none  [the longest x1 63.4 us: local(): lax.all_gather(features, 'chan', axis=1, tiled=True)]
    reduce_scatter x1 -> x0, waiting for transfers between devices: 69 us -> none  [local(): lax.psum_scatter(partial_x.astype(jnp.bfloat16), 'chan', scatter_dimensio...]
    psum x1 -> x0, waiting for transfers between devices: 47.3 us -> none  [local(): lax.psum(partial_w.astype(jnp.bfloat16), 'node').astype(jnp.float32)]
    ppermute x0 -> x26, waiting for transfers between devices: none -> 42.4 us  [swapped(): return lax.ppermute(value, axis, [(i, i ^ by) for i in range(size)])]
    ppermute x0 -> x26, starting transfers between devices: none -> 33.4 us  [swapped(): return lax.ppermute(value, axis, [(i, i ^ by) for i in range(size)])]
    unnamed x18 -> x26, local copies, waits for them, and re-layouts: 33 us -> 2.4 us
    dot_general x4 -> x0, matrix products: 27.8 us -> none  [the longest x1 10.2 us: local(): jnp.dot(chooser, contrib.reshape(blocks * tile_slots, -1), precision=lax....]
    pallas_call x0 -> x7, Pallas kernels: none -> 26.5 us  [the longest x1 13.5 us: inner(): pl.pallas_call(inner_kernel, in_specs=[IN_SMEM] * 3 + [IN_HBM] * 4 + [IN_...]
  transfers between devices with their start and end apart: 6 -> 29, of which waited for: 5 -> 9; matrix products, arithmetic and copies ran while one was open for 6% -> 7% of each run, Pallas kernels for 0% -> 18%
where the time goes in v2:
time: 133 us
  waiting for transfers between devices  53.4 us (40%)
  starting transfers between devices  39.5 us (30%)
  Pallas kernels  26.5 us (20%)
  other arithmetic  7.22 us (5%)
  local copies, waits for them, and re-layouts  5.3 us (4%)
    ppermute x26, waiting for transfers between devices, swapped(): return lax.ppermute(value, axis, [(i, i ^ by) for i in range(size)])  42.4 us
    ppermute x26, starting transfers between devices, swapped(): return lax.ppermute(value, axis, [(i, i ^ by) for i in range(size)])  33.4 us
    pallas_call x1, Pallas kernels, inner(): pl.pallas_call(inner_kernel, in_specs=[IN_SMEM] * 3 + [IN_HBM] * 4 + [IN_...  13.5 us
    all_to_all x1, waiting for transfers between devices, local(): lax.all_to_all(outgoing, 'node', split_axis=0, concat_axis=0, tiled=True)  11 us
    pallas_call x1, Pallas kernels, border(): pl.pallas_call(functools.partial(border_kernel, reach), in_specs=[IN_SMEM...  4.37 us
    all_to_all x1, starting transfers between devices, local(): lax.all_to_all(outgoing, 'node', split_axis=0, concat_axis=0, tiled=True)  3.56 us
    concatenate x4, other arithmetic, gather_hop(): jnp.concatenate([part, swapped(part, 'node', 1 << order[hop])], axis=0)  2.97 us
    pallas_call x1, Pallas kernels, weight_partial(): pl.pallas_call(functools.partial(weight_kernel, devs), in_specs=[IN_SMEM]...  2.8 us
  transfers between devices with their start and end apart: 29, of which 9 were waited for; matrix products, arithmetic and copies ran while one was open for 7% of the time, Pallas kernels for 18%

profile of v2, /device:TPU:0, one launch (start us, length us, event | category | flops | bytes accessed | tf_op | source)
XLA Modules:
  0.0 133.0 jit_solution(9376383897584664332)
XLA Ops:
  0.6 4.1 %collective-permute-start.1 = (bf16[128,256]{1,0:T(8,128)(2,1)}, bf16[128,256]{1,0:T(8,128)(2,1)S(1)}, u32[]{:S(2)}, u32[]{:S(2)}) collective-permute-start(bf16[128,256]{1,0:T(8,128)(2,1)} %param.12), channel_id=1, source_target_pairs={{0,2},{1,3},{2,0},{3,1},{4,6},{5,7},{6,4},{7,5},{8,10},{9,11},{10,... | collective-permute-start | bytes 196616 | tf_op jit(solution)/shard_map/ppermute | solution.py:38
  4.7 1.6 %collective-permute-start = (bf16[128,256]{1,0:T(8,128)(2,1)}, bf16[128,256]{1,0:T(8,128)(2,1)S(1)}, u32[]{:S(2)}, u32[]{:S(2)}) collective-permute-start(bf16[128,256]{1,0:T(8,128)(2,1)} %param.12), channel_id=1, source_target_pairs={{0,1},{1,0},{2,3},{3,2},{4,5},{5,4},{6,7},{7,6},{8,9},{9,8},{10,11... | collective-permute-start | bytes 196616 | tf_op jit(solution)/shard_map/ppermute | solution.py:38
  6.3 0.6 pad_add_fusion.me.index
  6.9 4.4 %border.1 = (bf16[2,2,128,256]{3,2,1,0:T(8,128)(2,1)}, bf16[2,2,128,256]{3,2,1,0:T(8,128)(2,1)}) custom-call(s32[2]{0:T(128)} %pad_add_fusion.me.index, s32[5,14]{1,0:T(8,128)} %bitcast.63, s32[14]{0:T(128)} %count.3, bf16[1792,256]{1,0:T(8,128)(2,1)} %gc.3, bf16[1792,256]{1,0:T(8,128)(2,1)} %pc.3, bf16[1792,256]{1,0:T(8,128)(2,1)} %gx.3, ...), custom_call_target="tpu_custom_call" | custom-call | flops 335544320 | bytes 1703936 | tf_op jit(solution)/shard_map/border/pallas_call | solution.py:100
  11.3 1.3 collective-permute-start.3
  12.6 1.3 collective-permute-start.4
  14.0 2.3 %dynamic-slice_bitcast_fusion = (bf16[448,256]{1,0:T(8,128)(2,1)}, bf16[448,256]{1,0:T(8,128)(2,1)}, bf16[448,256]{1,0:T(8,128)(2,1)}, bf16[448,256]{1,0:T(8,128)(2,1)S(1)}) fusion(bf16[4,448,256]{2,1,0:T(8,128)(2,1)} %bitcast.67, s32[]{:T(128)S(6)} %select_n.32, s32[]{:T(128)S(6)} %select_n.31, s32[]{:T(128)S(6)} %select_n.30, s32[]{:T(128)S(6)} %select_n.29), kind=kLoop, calls=%fused_computation.26 | loop fusion | bytes 1835024 | tf_op jit(solution)/shard_map/jit(dynamic_index_in_dim)/squeeze | solution.py:427
  16.3 1.2 copy-done.3
  17.5 1.2 copy-done.4
  18.7 13.5 %inner.1 = (bf16[14,128,256]{2,1,0:T(8,128)(2,1)S(1)}, bf16[14,128,256]{2,1,0:T(8,128)(2,1)S(1)}) custom-call(s32[2]{0:T(128)S(1)} %copy-done.5, s32[5,14]{1,0:T(8,128)S(1)} %bitcast.64, s32[14]{0:T(128)S(1)} %copy-done.8, bf16[1792,256]{1,0:T(8,128)(2,1)S(1)} %copy-done.1, bf16[1792,256]{1,0:T(8,128)(2,1)S(1)} %copy-done.2, ...), custom_call_target="tpu_custom_call" | custom-call | flops 1174405120 | bytes 7798784 | tf_op jit(solution)/shard_map/inner/pallas_call | solution.py:158
  32.2 3.9 %collective-permute-start.7 = (bf16[448,256]{1,0:T(8,128)(2,1)}, bf16[448,256]{1,0:T(8,128)(2,1)S(1)}, u32[]{:S(2)}, u32[]{:S(2)}) collective-permute-start(bf16[448,256]{1,0:T(8,128)(2,1)} %get-tuple-element.74), channel_id=1, source_target_pairs={{0,3},{1,2},{2,1},{3,0},{4,7},{5,6},{6,5},{7,4},{8,11},{9,10},{10,... | collective-permute-start | bytes 688136 | tf_op jit(solution)/shard_map/ppermute | solution.py:38
  36.1 0.9 maximum_bitcast_fusion.1
  36.9 5.4 %collective-permute-start.9 = (bf16[1,2,128,256]{3,2,1,0:T(8,128)(2,1)S(1)}, bf16[1,2,128,256]{3,2,1,0:T(8,128)(2,1)}, u32[]{:S(2)}, u32[]{:S(2)}) collective-permute-start(bf16[1,2,128,256]{3,2,1,0:T(8,128)(2,1)S(1)} %maximum_bitcast_fusion.1), channel_id=1, source_target_pairs={{0,16},{4,20},{8,24},{12,28},{16,0},{20,4},{24,8},{28,12},{1,17},{... | collective-permute-start | bytes 393224 | tf_op jit(solution)/shard_map/ppermute | solution.py:38
  42.4 0.9 maximum_bitcast_fusion
  43.3 0.8 collective-permute-start.5
  44.1 0.6 collective-permute-start.8
  44.7 1.7 %route.1 = (bf16[14,128,256]{2,1,0:T(8,128)(2,1)S(1)}, bf16[16,128,256]{2,1,0:T(8,128)(2,1)}) custom-call(s32[2]{0:T(128)S(1)} %copy-done.5, s32[112]{0:T(128)S(1)} %copy-done.9, bf16[14,128,256]{2,1,0:T(8,128)(2,1)S(1)} %get-tuple-element.33.clean, bf16[14,128,256]{2,1,0:T(8,128)(2,1)S(1)} %get-tuple-element.34.corrupt, ...), custom_call_target="tpu_custom_call" | custom-call | tf_op jit(solution)/shard_map/route/pallas_call | solution.py:201
  46.4 3.6 %all-to-all-start = ((bf16[16,128,256]{2,1,0:T(8,128)(2,1)}), bf16[16,128,256]{2,1,0:T(8,128)(2,1)S(1)}, u32[]{:S(2)}, u32[]{:S(2)}) async-start(bf16[16,128,256]{2,1,0:T(8,128)(2,1)} %get-tuple-element.38), calls=%async_computation | async-start | bytes 2097152 | tf_op jit(solution)/shard_map/all_to_all | solution.py:431
  50.0 0.9 pad_maximum_fusion.5
  51.0 1.0 pad_maximum_fusion.4
  52.0 0.1 eq.30
  52.1 0.1 add.65
  52.2 0.3 convert_reduce_fusion
  52.5 0.1 copy.13
  52.6 0.1 select_reduce_fusion
  52.7 1.6 %collective-permute-done.6.refs_2_ = bf16[448,256]{1,0:T(8,128)(2,1)S(1)} collective-permute-done((bf16[448,256]{1,0:T(8,128)(2,1)}, bf16[448,256]{1,0:T(8,128)(2,1)S(1)}, u32[]{:S(2)}, u32[]{:S(2)}) %collective-permute-start.6) | collective-permute-done | bytes 229408 | tf_op jit(solution)/shard_map/ppermute | solution.py:38
  54.4 11.0 %all-to-all-done.incoming = bf16[16,128,256]{2,1,0:T(8,128)(2,1)S(1)} async-done(((bf16[16,128,256]{2,1,0:T(8,128)(2,1)}), bf16[16,128,256]{2,1,0:T(8,128)(2,1)S(1)}, u32[]{:S(2)}, u32[]{:S(2)}) %all-to-all-start) | async-done | bytes 1048608 | tf_op jit(solution)/shard_map/all_to_all | solution.py:431
  65.4 0.5 collective-permute-start.13
  65.9 0.1 copy.14
  65.9 0.1 sub.13.landing
  66.0 0.6 collective-permute-start.14
  66.6 0.9 merge.1
  67.6 0.1 slice_bitcast_fusion.8
  67.6 3.7 %collective-permute-start.12 = (bf16[448,256]{1,0:T(8,128)(2,1)S(1)}, bf16[448,256]{1,0:T(8,128)(2,1)S(1)}, u32[]{:S(2)}, u32[]{:S(2)}) collective-permute-start(bf16[448,256]{1,0:T(8,128)(2,1)S(1)} %get-tuple-element.70), channel_id=1, source_target_pairs={{0,3},{1,2},{2,1},{3,0},{4,7},{5,6},{6,5},{7,4},{8,11},{9,10},{10,... | collective-permute-start | bytes 688136 | tf_op jit(solution)/shard_map/ppermute | solution.py:38
  71.3 0.8 collective-permute-start.10
  72.1 1.0 pad_maximum_fusion.2
  73.1 5.0 %collective-permute-done.12.refs_7_.refs_3_ = bf16[448,256]{1,0:T(8,128)(2,1)S(1)} collective-permute-done((bf16[448,256]{1,0:T(8,128)(2,1)S(1)}, bf16[448,256]{1,0:T(8,128)(2,1)S(1)}, u32[]{:S(2)}, u32[]{:S(2)}) %collective-permute-start.12) | collective-permute-done | bytes 229408 | tf_op jit(solution)/shard_map/ppermute | solution.py:38
  78.1 11.7 %collective-permute-done.11.refs_6_.refs_2_ = bf16[448,256]{1,0:T(8,128)(2,1)S(1)} collective-permute-done((bf16[448,256]{1,0:T(8,128)(2,1)S(1)}, bf16[448,256]{1,0:T(8,128)(2,1)S(1)}, u32[]{:S(2)}, u32[]{:S(2)}) %collective-permute-start.11) | collective-permute-done | bytes 229408 | tf_op jit(solution)/shard_map/ppermute | solution.py:38
  89.9 2.8 %weight_partial.1 = (bf16[2,4,2,128,256]{4,3,2,1,0:T(8,128)(2,1)S(1)}, bf16[2,4,2,128,256]{4,3,2,1,0:T(8,128)(2,1)S(1)}) custom-call(s32[2]{0:T(128)S(1)} %copy-done.5, bf16[448,256]{1,0:T(8,128)(2,1)S(1)} %get-tuple-element.43.refs_0_, bf16[448,256]{1,0:T(8,128)(2,1)S(1)} %collective-permute-done.5.refs_1_, ...), custom_call_target="tpu_custom_call" | custom-call | flops 939524096 | bytes 3932160 | tf_op jit(solution)/shard_map/weight_partial/pallas_call | solution.py:286
  92.7 0.1 collective-permute-start.15
  92.7 0.5 collective-permute-start.23
  93.2 0.1 collective-permute-start.24
  93.3 2.1 %collective-permute-done.15 = bf16[2,4,2,128,256]{4,3,2,1,0:T(8,128)(2,1)S(1)} collective-permute-done((bf16[2,4,2,128,256]{4,3,2,1,0:T(8,128)(2,1)S(1)}, bf16[2,4,2,128,256]{4,3,2,1,0:T(8,128)(2,1)S(1)}, u32[]{:S(2)}, u32[]{:S(2)}) %collective-permute-start.15) | collective-permute-done | bytes 1048608 | tf_op jit(solution)/shard_map/ppermute | solution.py:38
  95.4 0.3 fusion.10
  95.8 1.8 %collective-permute-start.19 = (bf16[2,2,128,256]{3,2,1,0:T(8,128)(2,1)S(1)}, bf16[2,2,128,256]{3,2,1,0:T(8,128)(2,1)S(1)}, u32[]{:S(2)}, u32[]{:S(2)}) collective-permute-start(bf16[2,2,128,256]{3,2,1,0:T(8,128)(2,1)S(1)} %get-tuple-element.64), channel_id=1, source_target_pairs={{0,16},{4,20},{8,24},{12,28},{16,0},{20,4},{24,8},{28,12},{1,17},{... | collective-permute-start | bytes 786440 | tf_op jit(solution)/shard_map/ppermute | solution.py:38
  97.5 0.3 collective-permute-start.16
  97.8 0.1 pad_maximum_fusion.refs_4_
  97.9 0.1 pad_maximum_fusion.1.refs_5_
  98.0 1.7 %feature_rows.1 = bf16[4,448,256]{2,1,0:T(8,128)(2,1)S(1)} custom-call(s32[2]{0:T(128)S(1)} %copy-done.5, bf16[448,256]{1,0:T(8,128)(2,1)S(1)} %get-tuple-element.52.refs_4_.refs_0_, bf16[448,256]{1,0:T(8,128)(2,1)S(1)} %collective-permute-done.10.refs_5_.refs_1_, bf16[448,256]{1,0:T(8,128)(2,1)S(1)} %collective-permute-done.11.refs_6_.refs_2_, ...), custom_call_target="tpu_custom_call" | custom-call | flops 939524096 | bytes 3932160 | tf_op jit(solution)/shard_map/feature_rows/pallas_call | solution.py:330
  99.7 4.5 %collective-permute-done.19 = bf16[2,2,128,256]{3,2,1,0:T(8,128)(2,1)S(1)} collective-permute-done((bf16[2,2,128,256]{3,2,1,0:T(8,128)(2,1)S(1)}, bf16[2,2,128,256]{3,2,1,0:T(8,128)(2,1)S(1)}, u32[]{:S(2)}, u32[]{:S(2)}) %collective-permute-start.19) | collective-permute-done | bytes 262176 | tf_op jit(solution)/shard_map/ppermute | solution.py:38
  104.2 1.4 %collective-permute-done.16 = bf16[2,2,128,256]{3,2,1,0:T(8,128)(2,1)S(1)} collective-permute-done((bf16[2,2,128,256]{3,2,1,0:T(8,128)(2,1)S(1)}, bf16[2,2,128,256]{3,2,1,0:T(8,128)(2,1)S(1)}, u32[]{:S(2)}, u32[]{:S(2)}) %collective-permute-start.16) | collective-permute-done | bytes 262176 | tf_op jit(solution)/shard_map/ppermute | solution.py:38
  105.6 0.1 fusion
  105.8 0.4 collective-permute-start.17
  106.2 0.1 slice_bitcast_fusion.4
  106.2 2.5 %collective-permute-start.27 = (bf16[448,256]{1,0:T(8,128)(2,1)S(1)}, bf16[448,256]{1,0:T(8,128)(2,1)S(1)}, u32[]{:S(2)}, u32[]{:S(2)}) collective-permute-start(bf16[448,256]{1,0:T(8,128)(2,1)S(1)} %get-tuple-element.66), channel_id=1, source_target_pairs={{0,3},{1,2},{2,1},{3,0},{4,7},{5,6},{6,5},{7,4},{8,11},{9,10},{10,... | collective-permute-start | bytes 688136 | tf_op jit(solution)/shard_map/ppermute | solution.py:38
  108.7 2.0 %collective-permute-start.25 = (bf16[448,256]{1,0:T(8,128)(2,1)S(1)}, bf16[448,256]{1,0:T(8,128)(2,1)S(1)}, u32[]{:S(2)}, u32[]{:S(2)}) collective-permute-start(bf16[448,256]{1,0:T(8,128)(2,1)S(1)} %get-tuple-element.68), channel_id=1, source_target_pairs={{0,1},{1,0},{2,3},{3,2},{4,5},{5,4},{6,7},{7,6},{8,9},{9,8},{10,11... | collective-permute-start | bytes 688136 | tf_op jit(solution)/shard_map/ppermute | solution.py:38
  110.7 0.4 collective-permute-start.20
  111.1 0.1 collective-permute-start.18
  111.2 4.5 %collective-permute-done.20 = bf16[1,2,128,256]{3,2,1,0:T(8,128)(2,1)S(1)} collective-permute-done((bf16[1,2,128,256]{3,2,1,0:T(8,128)(2,1)S(1)}, bf16[1,2,128,256]{3,2,1,0:T(8,128)(2,1)S(1)}, u32[]{:S(2)}, u32[]{:S(2)}) %collective-permute-start.20) | collective-permute-done | bytes 131104 | tf_op jit(solution)/shard_map/ppermute | solution.py:38
  115.8 1.0 collective-permute-start.21
  116.8 2.3 %collective-permute-start.22 = (bf16[128,256]{1,0:T(8,128)(2,1)S(1)}, bf16[128,256]{1,0:T(8,128)(2,1)S(1)}, u32[]{:S(2)}, u32[]{:S(2)}) collective-permute-start(bf16[128,256]{1,0:T(8,128)(2,1)S(1)} %get-tuple-element.79), channel_id=1, source_target_pairs={{0,3},{1,2},{2,1},{3,0},{4,7},{5,6},{6,5},{7,4},{8,11},{9,10},{10,... | collective-permute-start | bytes 196616 | tf_op jit(solution)/shard_map/ppermute | solution.py:38
  119.2 11.6 %collective-permute-done.26.refs_2_ = bf16[448,256]{1,0:T(8,128)(2,1)S(1)} collective-permute-done((bf16[448,256]{1,0:T(8,128)(2,1)S(1)}, bf16[448,256]{1,0:T(8,128)(2,1)S(1)}, u32[]{:S(2)}, u32[]{:S(2)}) %collective-permute-start.26) | collective-permute-done | bytes 229408 | tf_op jit(solution)/shard_map/ppermute | solution.py:38
  130.8 1.5 %laid_out.1 = bf16[1792,256]{1,0:T(8,128)(2,1)} custom-call(s32[2]{0:T(128)S(1)} %copy-done.5, bf16[448,256]{1,0:T(8,128)(2,1)S(1)} %get-tuple-element.69.refs_0_, bf16[448,256]{1,0:T(8,128)(2,1)S(1)} %collective-permute-done.25.refs_1_, bf16[448,256]{1,0:T(8,128)(2,1)S(1)} %collective-permute-done.26.refs_2_, ...), custom_call_target="tpu_custom_call" | custom-call | tf_op jit(solution)/shard_map/laid_out/pallas_call | solution.py:362
  132.3 0.7 fusion.5
  (60 shorter events, 0.4 us)
Async XLA Ops:
  0.6 31.5 %collective-permute-start.1 = (bf16[128,256]{1,0:T(8,128)(2,1)}, bf16[128,256]{1,0:T(8,128)(2,1)S(1)}, u32[]{:S(2)}, u32[]{:S(2)}) collective-permute-start(bf16[128,256]{1,0:T(8,128)(2,1)} %param.12), channel_id=1, source_target_pairs={{0,2},{1,3},{2,0},{3,1},{4,6},{5,7},{6,4},{7,5},{8,10},{9,11},{10,... | collective-permute-start | bytes 196616 | tf_op jit(solution)/shard_map/ppermute | solution.py:38
  4.7 31.3 %collective-permute-start = (bf16[128,256]{1,0:T(8,128)(2,1)}, bf16[128,256]{1,0:T(8,128)(2,1)S(1)}, u32[]{:S(2)}, u32[]{:S(2)}) collective-permute-start(bf16[128,256]{1,0:T(8,128)(2,1)} %param.12), channel_id=1, source_target_pairs={{0,1},{1,0},{2,3},{3,2},{4,5},{5,4},{6,7},{7,6},{8,9},{9,8},{10,11... | collective-permute-start | bytes 196616 | tf_op jit(solution)/shard_map/ppermute | solution.py:38
  6.3 29.7 %collective-permute-start.2 = (bf16[128,256]{1,0:T(8,128)(2,1)}, bf16[128,256]{1,0:T(8,128)(2,1)}, u32[]{:S(2)}, u32[]{:S(2)}) collective-permute-start(bf16[128,256]{1,0:T(8,128)(2,1)} %param.12), channel_id=1, source_target_pairs={{0,3},{1,2},{2,1},{3,0},{4,7},{5,6},{6,5},{7,4},{8,11},{9,10},{10,... | collective-permute-start | bytes 196616 | tf_op jit(solution)/shard_map/ppermute | solution.py:38
  6.9 9.3 %copy-start = (bf16[14,5,128,128]{3,2,1,0:T(8,128)(2,1)S(1)}, bf16[14,5,128,128]{3,2,1,0:T(8,128)(2,1)}, u32[]{:S(2)}) copy-start(bf16[14,5,128,128]{3,2,1,0:T(8,128)(2,1)} %adj.3) | copy-start | bytes 6881284
  6.9 9.3 %copy-start.5 = (s32[2]{0:T(128)S(1)}, s32[2]{0:T(128)}, u32[]{:S(2)}) copy-start(s32[2]{0:T(128)} %pad_add_fusion.me.index) | copy-start | bytes 28
  6.9 9.3 %copy-start.6 = (s32[14,5]{0,1:T(8,128)S(1)}, s32[14,5]{0,1:T(8,128)}, u32[]{:S(2)}) copy-start(s32[14,5]{0,1:T(8,128)} %param.19) | copy-start | bytes 844
  6.9 9.3 %copy-start.7 = (f32[256]{0:T(256)S(1)}, f32[256]{0:T(256)}, u32[]{:S(2)}) copy-start(f32[256]{0:T(256)} %param.17) | copy-start | bytes 3076
  6.9 9.3 %copy-start.8 = (s32[14]{0:T(128)S(1)}, s32[14]{0:T(128)}, u32[]{:S(2)}) copy-start(s32[14]{0:T(128)} %count.3) | copy-start | bytes 172
  11.3 31.9 %collective-permute-start.3 = (bf16[2,2,128,256]{3,2,1,0:T(8,128)(2,1)}, bf16[2,2,128,256]{3,2,1,0:T(8,128)(2,1)S(1)}, u32[]{:S(2)}, u32[]{:S(2)}) collective-permute-start(bf16[2,2,128,256]{3,2,1,0:T(8,128)(2,1)} %get-tuple-element.35), channel_id=1, source_target_pairs={{0,4},{4,8},{8,12},{12,16},{16,20},{20,24},{24,28},{1,5},{5,9},{9,... | collective-permute-start | bytes 786440 | tf_op jit(solution)/shard_map/ppermute | solution.py:33
  12.6 31.5 %collective-permute-start.4 = (bf16[2,2,128,256]{3,2,1,0:T(8,128)(2,1)}, bf16[2,2,128,256]{3,2,1,0:T(8,128)(2,1)S(1)}, u32[]{:S(2)}, u32[]{:S(2)}) collective-permute-start(bf16[2,2,128,256]{3,2,1,0:T(8,128)(2,1)} %get-tuple-element.36), channel_id=1, source_target_pairs={{4,0},{8,4},{12,8},{16,12},{20,16},{24,20},{28,24},{5,1},{9,5},{13... | collective-permute-start | bytes 786440 | tf_op jit(solution)/shard_map/ppermute | solution.py:33
  13.9 2.3 %copy-start.1 = (bf16[1792,256]{1,0:T(8,128)(2,1)S(1)}, bf16[1792,256]{1,0:T(8,128)(2,1)}, u32[]{:S(2)}) copy-start(bf16[1792,256]{1,0:T(8,128)(2,1)} %gc.3) | copy-start | bytes 2752516
  14.0 2.3 %copy-start.2 = (bf16[1792,256]{1,0:T(8,128)(2,1)S(1)}, bf16[1792,256]{1,0:T(8,128)(2,1)}, u32[]{:S(2)}) copy-start(bf16[1792,256]{1,0:T(8,128)(2,1)} %pc.3) | copy-start | bytes 2752516
  16.3 1.2 copy-start.3
  17.5 1.2 copy-start.4
  18.7 23.7 %copy-start.11 = (bf16[128,256]{1,0:T(8,128)(2,1)S(1)}, bf16[128,256]{1,0:T(8,128)(2,1)}, u32[]{:S(2)}) copy-start(bf16[128,256]{1,0:T(8,128)(2,1)} %param.12) | copy-start | bytes 196612
  18.7 26.0 %copy-start.9 = (s32[112]{0:T(128)S(1)}, s32[112]{0:T(128)}, u32[]{:S(2)}) copy-start(s32[112]{0:T(128)} %shuffle.1) | copy-start | bytes 1348
  32.2 20.6 %collective-permute-start.7 = (bf16[448,256]{1,0:T(8,128)(2,1)}, bf16[448,256]{1,0:T(8,128)(2,1)S(1)}, u32[]{:S(2)}, u32[]{:S(2)}) collective-permute-start(bf16[448,256]{1,0:T(8,128)(2,1)} %get-tuple-element.74), channel_id=1, source_target_pairs={{0,3},{1,2},{2,1},{3,0},{4,7},{5,6},{6,5},{7,4},{8,11},{9,10},{10,... | collective-permute-start | bytes 688136 | tf_op jit(solution)/shard_map/ppermute | solution.py:38
  36.0 6.4 %copy-start.12 = (bf16[128,256]{1,0:T(8,128)(2,1)}, bf16[128,256]{1,0:T(8,128)(2,1)S(1)}, u32[]{:S(2)}) copy-start(bf16[128,256]{1,0:T(8,128)(2,1)S(1)} %collective-permute-done) | copy-start | bytes 196612
  36.0 18.3 %collective-permute-start.6 = (bf16[448,256]{1,0:T(8,128)(2,1)}, bf16[448,256]{1,0:T(8,128)(2,1)S(1)}, u32[]{:S(2)}, u32[]{:S(2)}) collective-permute-start(bf16[448,256]{1,0:T(8,128)(2,1)} %get-tuple-element.75), channel_id=1, source_target_pairs={{0,2},{1,3},{2,0},{3,1},{4,6},{5,7},{6,4},{7,5},{8,10},{9,11},{10,... | collective-permute-start | bytes 688136 | tf_op jit(solution)/shard_map/ppermute | solution.py:38
  36.9 13.0 %collective-permute-start.9 = (bf16[1,2,128,256]{3,2,1,0:T(8,128)(2,1)S(1)}, bf16[1,2,128,256]{3,2,1,0:T(8,128)(2,1)}, u32[]{:S(2)}, u32[]{:S(2)}) collective-permute-start(bf16[1,2,128,256]{3,2,1,0:T(8,128)(2,1)S(1)} %maximum_bitcast_fusion.1), channel_id=1, source_target_pairs={{0,16},{4,20},{8,24},{12,28},{16,0},{20,4},{24,8},{28,12},{1,17},{... | collective-permute-start | bytes 393224 | tf_op jit(solution)/shard_map/ppermute | solution.py:38
  43.3 7.7 %copy-start.10 = (bf16[1,2,128,256]{3,2,1,0:T(8,128)(2,1)}, bf16[1,2,128,256]{3,2,1,0:T(8,128)(2,1)S(1)}, u32[]{:S(2)}) copy-start(bf16[1,2,128,256]{3,2,1,0:T(8,128)(2,1)S(1)} %maximum_bitcast_fusion) | copy-start | bytes 393220
  43.3 11.1 %collective-permute-start.5 = (bf16[448,256]{1,0:T(8,128)(2,1)}, bf16[448,256]{1,0:T(8,128)(2,1)S(1)}, u32[]{:S(2)}, u32[]{:S(2)}) collective-permute-start(bf16[448,256]{1,0:T(8,128)(2,1)} %get-tuple-element.76), channel_id=1, source_target_pairs={{0,1},{1,0},{2,3},{3,2},{4,5},{5,4},{6,7},{7,6},{8,9},{9,8},{10,11... | collective-permute-start | bytes 688136 | tf_op jit(solution)/shard_map/ppermute | solution.py:38
  44.1 6.9 %collective-permute-start.8 = (bf16[1,2,128,256]{3,2,1,0:T(8,128)(2,1)S(1)}, bf16[1,2,128,256]{3,2,1,0:T(8,128)(2,1)}, u32[]{:S(2)}, u32[]{:S(2)}) collective-permute-start(bf16[1,2,128,256]{3,2,1,0:T(8,128)(2,1)S(1)} %maximum_bitcast_fusion), channel_id=1, source_target_pairs={{0,8},{4,12},{8,0},{12,4},{16,24},{20,28},{24,16},{28,20},{1,9},{5... | collective-permute-start | bytes 393224 | tf_op jit(solution)/shard_map/ppermute | solution.py:38
  46.4 18.9 %all-to-all-start = ((bf16[16,128,256]{2,1,0:T(8,128)(2,1)}), bf16[16,128,256]{2,1,0:T(8,128)(2,1)S(1)}, u32[]{:S(2)}, u32[]{:S(2)}) async-start(bf16[16,128,256]{2,1,0:T(8,128)(2,1)} %get-tuple-element.38), calls=%async_computation | async-start | bytes 2097152 | tf_op jit(solution)/shard_map/all_to_all | solution.py:431
  65.4 6.7 %collective-permute-start.13 = (bf16[2,2,128,256]{3,2,1,0:T(8,128)(2,1)S(1)}, bf16[2,2,128,256]{3,2,1,0:T(8,128)(2,1)}, u32[]{:S(2)}, u32[]{:S(2)}) collective-permute-start(bf16[2,2,128,256]{3,2,1,0:T(8,128)(2,1)S(1)} %pad_maximum_fusion.4), channel_id=1, source_target_pairs={{0,16},{4,20},{8,24},{12,28},{16,0},{20,4},{24,8},{28,12},{1,17},{... | collective-permute-start | bytes 786440 | tf_op jit(solution)/shard_map/ppermute | solution.py:38
  66.0 7.1 %collective-permute-start.14 = (bf16[2,2,128,256]{3,2,1,0:T(8,128)(2,1)S(1)}, bf16[2,2,128,256]{3,2,1,0:T(8,128)(2,1)S(1)}, u32[]{:S(2)}, u32[]{:S(2)}) collective-permute-start(bf16[2,2,128,256]{3,2,1,0:T(8,128)(2,1)S(1)} %pad_maximum_fusion.5), channel_id=1, source_target_pairs={{0,8},{4,12},{8,0},{12,4},{16,24},{20,28},{24,16},{28,20},{1,9},{5... | collective-permute-start | bytes 786440 | tf_op jit(solution)/shard_map/ppermute | solution.py:38
  67.6 10.5 %collective-permute-start.12 = (bf16[448,256]{1,0:T(8,128)(2,1)S(1)}, bf16[448,256]{1,0:T(8,128)(2,1)S(1)}, u32[]{:S(2)}, u32[]{:S(2)}) collective-permute-start(bf16[448,256]{1,0:T(8,128)(2,1)S(1)} %get-tuple-element.70), channel_id=1, source_target_pairs={{0,3},{1,2},{2,1},{3,0},{4,7},{5,6},{6,5},{7,4},{8,11},{9,10},{10,... | collective-permute-start | bytes 688136 | tf_op jit(solution)/shard_map/ppermute | solution.py:38
  71.3 18.6 %collective-permute-start.11 = (bf16[448,256]{1,0:T(8,128)(2,1)S(1)}, bf16[448,256]{1,0:T(8,128)(2,1)S(1)}, u32[]{:S(2)}, u32[]{:S(2)}) collective-permute-start(bf16[448,256]{1,0:T(8,128)(2,1)S(1)} %get-tuple-element.71), channel_id=1, source_target_pairs={{0,2},{1,3},{2,0},{3,1},{4,6},{5,7},{6,4},{7,5},{8,10},{9,11},{10,... | collective-permute-start | bytes 688136 | tf_op jit(solution)/shard_map/ppermute | solution.py:38
  71.3 18.6 %collective-permute-start.10 = (bf16[448,256]{1,0:T(8,128)(2,1)S(1)}, bf16[448,256]{1,0:T(8,128)(2,1)S(1)}, u32[]{:S(2)}, u32[]{:S(2)}) collective-permute-start(bf16[448,256]{1,0:T(8,128)(2,1)S(1)} %get-tuple-element.72), channel_id=1, source_target_pairs={{0,1},{1,0},{2,3},{3,2},{4,5},{5,4},{6,7},{7,6},{8,9},{9,8},{10,11... | collective-permute-start | bytes 688136 | tf_op jit(solution)/shard_map/ppermute | solution.py:38
  92.7 2.7 %collective-permute-start.15 = (bf16[2,4,2,128,256]{4,3,2,1,0:T(8,128)(2,1)S(1)}, bf16[2,4,2,128,256]{4,3,2,1,0:T(8,128)(2,1)S(1)}, u32[]{:S(2)}, u32[]{:S(2)}) collective-permute-start(bf16[2,4,2,128,256]{4,3,2,1,0:T(8,128)(2,1)S(1)} %get-tuple-element.57), channel_id=1, source_target_pairs={{0,4},{4,0},{8,12},{12,8},{16,20},{20,16},{24,28},{28,24},{1,5},{5... | collective-permute-start | bytes 3145736 | tf_op jit(solution)/shard_map/ppermute | solution.py:38
  92.7 5.1 %collective-permute-start.23 = (bf16[4,2,128,256]{3,2,1,0:T(8,128)(2,1)S(1)}, bf16[4,2,128,256]{3,2,1,0:T(8,128)(2,1)S(1)}, u32[]{:S(2)}, u32[]{:S(2)}) collective-permute-start(bf16[4,2,128,256]{3,2,1,0:T(8,128)(2,1)S(1)} %pad_maximum_fusion.2), channel_id=1, source_target_pairs={{0,4},{4,0},{8,12},{12,8},{16,20},{20,16},{24,28},{28,24},{1,5},{5... | collective-permute-start | bytes 1572872 | tf_op jit(solution)/shard_map/ppermute | solution.py:38
  93.2 4.7 %collective-permute-start.24 = (bf16[4,2,128,256]{3,2,1,0:T(8,128)(2,1)S(1)}, bf16[4,2,128,256]{3,2,1,0:T(8,128)(2,1)S(1)}, u32[]{:S(2)}, u32[]{:S(2)}) collective-permute-start(bf16[4,2,128,256]{3,2,1,0:T(8,128)(2,1)S(1)} %pad_maximum_fusion.3), channel_id=1, source_target_pairs={{0,4},{4,0},{8,12},{12,8},{16,20},{20,16},{24,28},{28,24},{1,5},{5... | collective-permute-start | bytes 1572872 | tf_op jit(solution)/shard_map/ppermute | solution.py:38
  95.8 8.4 %collective-permute-start.19 = (bf16[2,2,128,256]{3,2,1,0:T(8,128)(2,1)S(1)}, bf16[2,2,128,256]{3,2,1,0:T(8,128)(2,1)S(1)}, u32[]{:S(2)}, u32[]{:S(2)}) collective-permute-start(bf16[2,2,128,256]{3,2,1,0:T(8,128)(2,1)S(1)} %get-tuple-element.64), channel_id=1, source_target_pairs={{0,16},{4,20},{8,24},{12,28},{16,0},{20,4},{24,8},{28,12},{1,17},{... | collective-permute-start | bytes 786440 | tf_op jit(solution)/shard_map/ppermute | solution.py:38
  97.5 8.1 %collective-permute-start.16 = (bf16[2,2,128,256]{3,2,1,0:T(8,128)(2,1)S(1)}, bf16[2,2,128,256]{3,2,1,0:T(8,128)(2,1)S(1)}, u32[]{:S(2)}, u32[]{:S(2)}) collective-permute-start(bf16[2,2,128,256]{3,2,1,0:T(8,128)(2,1)S(1)} %get-tuple-element.65), channel_id=1, source_target_pairs={{0,8},{4,12},{8,0},{12,4},{16,24},{20,28},{24,16},{28,20},{1,9},{5... | collective-permute-start | bytes 786440 | tf_op jit(solution)/shard_map/ppermute | solution.py:38
  105.8 5.3 %collective-permute-start.17 = (bf16[1,2,128,256]{3,2,1,0:T(8,128)(2,1)S(1)}, bf16[1,2,128,256]{3,2,1,0:T(8,128)(2,1)S(1)}, u32[]{:S(2)}, u32[]{:S(2)}) collective-permute-start(bf16[1,2,128,256]{3,2,1,0:T(8,128)(2,1)S(1)} %slice.162), channel_id=1, source_target_pairs={{0,16},{4,20},{8,24},{12,28},{16,0},{20,4},{24,8},{28,12},{1,17},{... | collective-permute-start | bytes 393224 | tf_op jit(solution)/shard_map/ppermute | solution.py:38
  106.2 10.6 %collective-permute-start.27 = (bf16[448,256]{1,0:T(8,128)(2,1)S(1)}, bf16[448,256]{1,0:T(8,128)(2,1)S(1)}, u32[]{:S(2)}, u32[]{:S(2)}) collective-permute-start(bf16[448,256]{1,0:T(8,128)(2,1)S(1)} %get-tuple-element.66), channel_id=1, source_target_pairs={{0,3},{1,2},{2,1},{3,0},{4,7},{5,6},{6,5},{7,4},{8,11},{9,10},{10,... | collective-permute-start | bytes 688136 | tf_op jit(solution)/shard_map/ppermute | solution.py:38
  108.7 22.0 %collective-permute-start.26 = (bf16[448,256]{1,0:T(8,128)(2,1)S(1)}, bf16[448,256]{1,0:T(8,128)(2,1)S(1)}, u32[]{:S(2)}, u32[]{:S(2)}) collective-permute-start(bf16[448,256]{1,0:T(8,128)(2,1)S(1)} %get-tuple-element.67), channel_id=1, source_target_pairs={{0,2},{1,3},{2,0},{3,1},{4,6},{5,7},{6,4},{7,5},{8,10},{9,11},{10,... | collective-permute-start | bytes 688136 | tf_op jit(solution)/shard_map/ppermute | solution.py:38
  108.7 22.0 %collective-permute-start.25 = (bf16[448,256]{1,0:T(8,128)(2,1)S(1)}, bf16[448,256]{1,0:T(8,128)(2,1)S(1)}, u32[]{:S(2)}, u32[]{:S(2)}) collective-permute-start(bf16[448,256]{1,0:T(8,128)(2,1)S(1)} %get-tuple-element.68), channel_id=1, source_target_pairs={{0,1},{1,0},{2,3},{3,2},{4,5},{5,4},{6,7},{7,6},{8,9},{9,8},{10,11... | collective-permute-start | bytes 688136 | tf_op jit(solution)/shard_map/ppermute | solution.py:38
  110.7 5.0 %collective-permute-start.20 = (bf16[1,2,128,256]{3,2,1,0:T(8,128)(2,1)S(1)}, bf16[1,2,128,256]{3,2,1,0:T(8,128)(2,1)S(1)}, u32[]{:S(2)}, u32[]{:S(2)}) collective-permute-start(bf16[1,2,128,256]{3,2,1,0:T(8,128)(2,1)S(1)} %slice.161), channel_id=1, source_target_pairs={{0,8},{4,12},{8,0},{12,4},{16,24},{20,28},{24,16},{28,20},{1,9},{5... | collective-permute-start | bytes 393224 | tf_op jit(solution)/shard_map/ppermute | solution.py:38
  111.1 21.1 %collective-permute-start.18 = (bf16[128,256]{1,0:T(8,128)(2,1)S(1)}, bf16[128,256]{1,0:T(8,128)(2,1)S(1)}, u32[]{:S(2)}, u32[]{:S(2)}) collective-permute-start(bf16[128,256]{1,0:T(8,128)(2,1)S(1)} %fusion.6), channel_id=1, source_target_pairs={{0,1},{1,0},{2,3},{3,2},{4,5},{5,4},{6,7},{7,6},{8,9},{9,8},{10,11... | collective-permute-start | bytes 196616 | tf_op jit(solution)/shard_map/ppermute | solution.py:38
  115.8 16.5 %collective-permute-start.21 = (bf16[128,256]{1,0:T(8,128)(2,1)S(1)}, bf16[128,256]{1,0:T(8,128)(2,1)S(1)}, u32[]{:S(2)}, u32[]{:S(2)}) collective-permute-start(bf16[128,256]{1,0:T(8,128)(2,1)S(1)} %get-tuple-element.78), channel_id=1, source_target_pairs={{0,2},{1,3},{2,0},{3,1},{4,6},{5,7},{6,4},{7,5},{8,10},{9,11},{10,... | collective-permute-start | bytes 196616 | tf_op jit(solution)/shard_map/ppermute | solution.py:38
  116.8 15.5 %collective-permute-start.22 = (bf16[128,256]{1,0:T(8,128)(2,1)S(1)}, bf16[128,256]{1,0:T(8,128)(2,1)S(1)}, u32[]{:S(2)}, u32[]{:S(2)}) collective-permute-start(bf16[128,256]{1,0:T(8,128)(2,1)S(1)} %get-tuple-element.79), channel_id=1, source_target_pairs={{0,3},{1,2},{2,1},{3,0},{4,7},{5,6},{6,5},{7,4},{8,11},{9,10},{10,... | collective-permute-start | bytes 196616 | tf_op jit(solution)/shard_map/ppermute | solution.py:38

commit v3 on v2

--- a/solution.py
+++ b/solution.py
@@ -38,102 +38,59 @@
     return lax.ppermute(value, axis, [(i, i ^ by) for i in range(size)])
 
 
+def exchanged(value, axis):
+    return lax.all_to_all(value, axis, split_axis=0, concat_axis=0, tiled=True)
+
+
 def masked_grad(grad, pre, slope):
     return (wide(grad) * jnp.where(wide(pre) > 0, 1.0, slope)).astype(jnp.bfloat16)
 
 
-def add_products(block, slot, slots, place, data, tiles, slopes, acc):
-    gc, pc, gx, px = (data[i, slot] for i in range(4))
-    slope = slopes[...]
-    rhs = jnp.concatenate([masked_grad(gc, pc, slope), masked_grad(gx, px, slope)], axis=1)
-    rows = tiles.shape[2]
-    lhs = jnp.concatenate([tiles[slot, k].T for k in range(slots)], axis=0)
-    product = jnp.dot(lhs, rhs, preferred_element_type=jnp.float32)
-    for k in range(slots):
-        acc[place(block, k)] += product[k * rows : (k + 1) * rows]
-
-
-def block_copies(block, slot, rows, inputs, adj, data, tiles, sems):
-    span = pl.ds(pl.multiple_of(block * rows, rows), rows)
-    copies = [
-        pltpu.make_async_copy(ref.at[span], data.at[i, slot], sems.at[i, slot])
-        for i, ref in enumerate(inputs)
-    ]
-    return copies + [pltpu.make_async_copy(adj.at[block], tiles.at[slot], sems.at[4, slot])]
-
-
-def border_kernel(
-    reach, me, cols, count, gc, pc, gx, px, slopes, adj, down, up, data, tiles, acc, sems
+def aggregate_kernel(
+    reach, me, cols, count, gc, pc, gx, px, slopes, adj, clean, corrupt, down, up, data, tiles, rhs, stage, sems
 ):
     blocks, slots, rows, _ = adj.shape
     width = gc.shape[1]
-    border = [*range(reach), *range(blocks - reach, blocks)]
-
-    def copies(i):
-        return block_copies(border[i], i, rows, (gc, pc, gx, px), adj, data, tiles, sems)
-
-    for i in range(2 * reach):
-        for copy in copies(i):
-            copy.start()
-    acc[...] = jnp.zeros_like(acc)
-
-    def place(block, k):
-        target = cols[k, block] - me[0] * blocks
-        live = k < count[block]
-        below = live & (target < 0)
-        above = live & (target >= blocks)
-        return jnp.where(below, target + reach, jnp.where(above, target - blocks + reach, 2 * reach))
-
-    for i in range(2 * reach):
-        for copy in copies(i):
-            copy.wait()
-        add_products(border[i], i, slots, place, data, tiles, slopes, acc)
-    for which in range(2):
-        part = acc[: 2 * reach, :, which * width : (which + 1) * width].astype(jnp.bfloat16)
-        down[which] = part[:reach]
-        up[which] = part[reach:]
-
-
-def border(me, cols, count, gc, pc, gx, px, slopes, adj, reach):
-    _, slots, rows, _ = adj.shape
-    width = gc.shape[1]
-    return pl.pallas_call(
-        functools.partial(border_kernel, reach),
-        in_specs=[IN_SMEM] * 3 + [IN_HBM] * 4 + [IN_VMEM, IN_HBM],
-        out_specs=[IN_VMEM] * 2,
-        out_shape=[bf16(2, reach, rows, width)] * 2,
-        scratch_shapes=[
-            pltpu.VMEM((4, 2 * reach, rows, width), jnp.bfloat16),
-            pltpu.VMEM((2 * reach, slots, rows, rows), jnp.bfloat16),
-            pltpu.VMEM((2 * reach + 1, rows, 2 * width), jnp.float32),
-            pltpu.SemaphoreType.DMA((5, 2 * reach)),
-        ],
-        compiler_params=params(VMEM_ALL),
-        cost_estimate=pl.CostEstimate(
-            flops=8 * reach * slots * rows * rows * width,
-            bytes_accessed=16 * reach * rows * width + 4 * reach * slots * rows * rows,
-            transcendentals=0,
-        ),
-        name="border",
-    )(me, cols, count, gc, pc, gx, px, slopes, adj)
-
-
-def inner_kernel(me, cols, count, gc, pc, gx, px, slopes, adj, clean, corrupt, data, tiles, acc, sems):
-    blocks, slots, rows, _ = adj.shape
-    width = gc.shape[1]
+    spare = blocks + 2 * reach
+    pad = 2 * reach * rows
 
     def copies(block):
-        return block_copies(block, block, rows, (gc, pc, gx, px), adj, data, tiles, sems)
+        span = pl.ds(pl.multiple_of(block * rows, rows), rows)
+        out = [
+            pltpu.make_async_copy(ref.at[span], data.at[i, block], sems.at[i, block])
+            for i, ref in enumerate((gc, pc, gx, px))
+        ]
+        return out + [pltpu.make_async_copy(adj.at[block], tiles.at[block], sems.at[4, block])]
 
     for block in range(blocks):
         for copy in copies(block):
             copy.start()
-    acc[...] = jnp.zeros_like(acc)
-
-    def place(block, k):
-        target = cols[k, block] - me[0] * blocks
-        inside = (k < count[block]) & (target >= 0) & (target < blocks)
-        return jnp.where(inside, target, blocks)
+    stage[...] = jnp.zeros_like(stage)
+    rhs[:pad] = jnp.zeros((pad, 2 * width), jnp.bfloat16)
+    rhs[pad + blocks * rows :] = jnp.zeros((pad, 2 * width), jnp.bfloat16)
+    shape = (rows, rows)
+    identity = (
+        lax.broadcasted_iota(jnp.int32, shape, 0) == lax.broadcasted_iota(jnp.int32, shape, 1)
+    ).astype(jnp.float32).astype(jnp.bfloat16)
+    slope = slopes[...]
+
+    def take(block):
+        gradients = [masked_grad(data[i, block], data[i + 1, block], slope) for i in (0, 2)]
+        span = pl.ds(pl.multiple_of(pad + block * rows, rows), rows)
+        rhs[span] = jnp.concatenate(gradients, axis=1)
+        turned = lax.dot_general(
+            identity,
+            tiles[block].reshape(slots * rows, rows),
+            (((1,), (1,)), ((), ())),
+            preferred_element_type=jnp.float32,
+        )
+        for k in range(slots):
+            live = k < count[block]
+            target = cols[k, block] - me[0] * blocks
+            place = jnp.where(live, target + reach, spare)
+            distance = jnp.where(live, block - target + reach, 0)
+            part = turned[:, k * rows : (k + 1) * rows]
+            stage[place, distance] = (wide(stage[place, distance]) + part).astype(jnp.bfloat16)
 
     per_step = 2 - blocks % 2
 
@@ -143,36 +100,59 @@
             for copy in copies(step * per_step + i):
                 copy.wait()
         for i in range(per_step):
-            block = step * per_step + i
-            add_products(block, block, slots, place, data, tiles, slopes, acc)
-
-    @pl.loop(0, blocks)
-    def _(block):
-        clean[block] = acc[block, :, :width].astype(jnp.bfloat16)
-        corrupt[block] = acc[block, :, width:].astype(jnp.bfloat16)
-
-
-def inner(me, cols, count, gc, pc, gx, px, slopes, adj):
+            take(step * per_step + i)
+
+    blank = jnp.zeros(shape, jnp.bfloat16)
+
+    def pair(first):
+        lhs = jnp.concatenate(
+            [
+                jnp.concatenate(
+                    [blank] * i + [stage[first + i, j] for j in range(2 * reach + 1)] + [blank] * (1 - i),
+                    axis=1,
+                )
+                for i in range(2)
+            ],
+            axis=0,
+        )
+        span = pl.ds(pl.multiple_of(first * rows, rows), (2 * reach + 2) * rows)
+        product = jnp.dot(lhs, rhs[span], preferred_element_type=jnp.float32)
+        product = product.astype(jnp.bfloat16).reshape(2, rows, 2 * width)
+        return product[:, :, :width], product[:, :, width:]
+
+    for i in range(0, reach, 2):
+        down[0, i : i + 2], down[1, i : i + 2] = pair(i)
+        up[0, i : i + 2], up[1, i : i + 2] = pair(blocks + reach + i)
+
+    @pl.loop(0, blocks // 2)
+    def _(step):
+        span = pl.ds(2 * step, 2)
+        clean[span], corrupt[span] = pair(reach + 2 * step)
+
+
+def aggregate(me, cols, count, gc, pc, gx, px, slopes, adj, reach):
     blocks, slots, rows, _ = adj.shape
     width = gc.shape[1]
+    assert reach % 2 == 0 and blocks % 2 == 0
     return pl.pallas_call(
-        inner_kernel,
+        functools.partial(aggregate_kernel, reach),
         in_specs=[IN_SMEM] * 3 + [IN_HBM] * 4 + [IN_VMEM, IN_HBM],
-        out_specs=[IN_VMEM] * 2,
-        out_shape=[bf16(blocks, rows, width)] * 2,
+        out_specs=[IN_VMEM] * 4,
+        out_shape=[bf16(blocks, rows, width)] * 2 + [bf16(2, reach, rows, width)] * 2,
         scratch_shapes=[
             pltpu.VMEM((4, blocks, rows, width), jnp.bfloat16),
             pltpu.VMEM((blocks, slots, rows, rows), jnp.bfloat16),
-            pltpu.VMEM((blocks + 1, rows, 2 * width), jnp.float32),
+            pltpu.VMEM(((blocks + 4 * reach) * rows, 2 * width), jnp.bfloat16),
+            pltpu.VMEM((blocks + 2 * reach + 1, 2 * reach + 1, rows, rows), jnp.bfloat16),
             pltpu.SemaphoreType.DMA((5, blocks)),
         ],
-        compiler_params=params(),
+        compiler_params=params(VMEM_ALL),
         cost_estimate=pl.CostEstimate(
             flops=4 * blocks * slots * rows * rows * width,
             bytes_accessed=12 * blocks * rows * width + 2 * blocks * slots * rows * rows,
             transcendentals=0,
         ),
-        name="inner",
+        name="aggregate",
     )(me, cols, count, gc, pc, gx, px, slopes, adj)
 
 
@@ -302,13 +282,13 @@
     *summed, low, high, out = refs
     groups = len(summed)
     devs = low.shape[0]
-    me, group = index[0], index[1]
+    me = index[0]
     shares = devs // groups
     lhs = jnp.concatenate([piece[...] for piece in summed], axis=1)
-    for relative in range(groups):
+    for target in range(groups):
         rows = []
         for share in range(shares):
-            node = ((group ^ relative) * shares + share) ^ me
+            node = (target * shares + share) ^ me
             parts = []
             for half, order in zip((low, high), halving_orders(devs)):
                 place = jnp.int32(0)
@@ -316,7 +296,7 @@
                     place += ((node >> bit) & 1) << j
                 parts += [half[place, i] for i in range(groups // 2)]
             rows.append(jnp.concatenate(parts, axis=1))
-        out[relative] = lax.dot_general(
+        out[target] = lax.dot_general(
             lhs,
             jnp.concatenate(rows, axis=0),
             (((1,), (1,)), ((), ())),
@@ -340,34 +320,6 @@
         ),
         name="feature_rows",
     )(index, *summed, *halves)
-
-
-def gather_kernel(index, *refs):
-    *pieces, out, sems = refs
-    rows = pieces[0].shape[0]
-    copies = [
-        pltpu.make_async_copy(
-            piece, out.at[pl.ds(pl.multiple_of((index[1] ^ i) * rows, rows), rows)], sems.at[i]
-        )
-        for i, piece in enumerate(pieces)
-    ]
-    for copy in copies:
-        copy.start()
-    for copy in copies:
-        copy.wait()
-
-
-def laid_out(index, pieces):
-    rows, width = pieces[0].shape
-    return pl.pallas_call(
-        gather_kernel,
-        in_specs=[IN_SMEM] + [IN_VMEM] * len(pieces),
-        out_specs=IN_HBM,
-        out_shape=bf16(len(pieces) * rows, width),
-        scratch_shapes=[pltpu.SemaphoreType.DMA((len(pieces),))],
-        compiler_params=params(),
-        name="laid_out",
-    )(index, *pieces)
 
 
 def landing_blocks(shuffle_from, me, blocks, devs, slots):
@@ -410,50 +362,44 @@
 
     args = (index, adj_cols.T, adj_count, grad_clean, pre_clean, grad_corrupt, pre_corrupt)
     args += (slopes[None, :], adj_vals)
-    down, up = border(*args, reach)
+    clean, corrupt, down, up = aggregate(*args, reach)
     from_prev = shifted(up, "node", 1)
     from_next = shifted(down, "node", -1)
-
     tiles = [weight] + [swapped(weight, "chan", i) for i in range(1, groups)]
-    clean, corrupt = inner(*args)
-    clean, corrupt, tiles = lax.optimization_barrier((clean, corrupt, tiles))
-    clean, outgoing = route(
-        index, shuffle_from, clean, corrupt, from_prev, from_next, devs, slots
-    )
 
     feats = [None] * groups
     by_quarter = features.reshape(groups, quarter, width)
     for i in [0, *exchange_order(groups)]:
         piece = lax.dynamic_index_in_dim(by_quarter, group ^ i, 0, keepdims=False)
         feats[i] = swapped(piece, "chan", i) if i else piece
-    shuffle_from, outgoing = lax.optimization_barrier((shuffle_from, outgoing))
+
+    clean, outgoing = route(
+        index, shuffle_from, clean, corrupt, from_prev, from_next, devs, slots
+    )
+    shuffle_from, outgoing, tiles = lax.optimization_barrier((shuffle_from, outgoing, tiles))
     landing = landing_blocks(shuffle_from, me, blocks, devs, slots)
-    incoming = lax.all_to_all(outgoing, "node", split_axis=0, concat_axis=0, tiled=True)
+    incoming = exchanged(outgoing, "node")
+
+    halves = [jnp.stack(part)[None] for part in (tiles[: groups // 2], tiles[groups // 2 :])]
     orders = halving_orders(devs)
-    halves = [jnp.stack(part)[None] for part in (tiles[: groups // 2], tiles[groups // 2 :])]
-
-    def gather_hop(halves, hop):
-        return [
+    for hop in range(len(orders[0])):
+        halves = [
             jnp.concatenate([part, swapped(part, "node", 1 << order[hop])], axis=0)
             for part, order in zip(halves, orders)
         ]
-
-    halves = gather_hop(halves, 0)
     incoming, feats, halves = lax.optimization_barrier((incoming, feats, halves))
+
     merged = merge(index, landing, clean, incoming, groups)
     summed = [merged[0]] + [None] * (groups - 1)
     for i in exchange_order(groups):
         summed[i] = swapped(merged[i], "chan", i)
-    for hop in range(1, len(orders[0])):
-        halves = gather_hop(halves, hop)
+    halves = [jnp.concatenate([part, swapped(part, "node", 1)], axis=0) for part in halves]
     summed, halves = lax.optimization_barrier((summed, halves))
-    halves = [jnp.concatenate([part, swapped(part, "node", 1)], axis=0) for part in halves]
 
     rows_out = feature_rows(index, summed, halves)
-    pieces = [rows_out[0]] + [None] * (groups - 1)
-    for i in exchange_order(groups):
-        pieces[i] = swapped(rows_out[i], "chan", i)
-
+    grad_features = exchanged(rows_out, "chan").reshape(row_count, width)
+
+    feats, summed, rows_out = lax.optimization_barrier((feats, summed, rows_out))
     keep, send = weight_partial(index, feats, summed, devs)
     total = wide(keep) + wide(swapped(send, "node", 1))
     shares = []
@@ -468,7 +414,6 @@
     for i in range(1, groups):
         grad_weight = grad_weight + wide(swapped(shares[i].astype(jnp.bfloat16), "chan", i))
 
-    grad_features = laid_out(index, pieces)
     return (grad_weight, grad_features)
 
 

time: 133 us -> 138 us (1.038)
  starting transfers between devices: 39.5 us -> 48.2 us
  Pallas kernels: 26.5 us -> 18.2 us
  waiting for transfers between devices: 53.4 us -> 57.4 us
  other arithmetic: 7.22 us -> 10 us
  local copies, waits for them, and re-layouts: 5.3 us -> 3.19 us
    pallas_call x3 -> x1, Pallas kernels: 19.3 us -> 9.68 us  [aggregate(): pl.pallas_call(functools.partial(aggregate_kernel, reach), in_specs=[IN_S...]
    all_to_all x1 -> x2, starting transfers between devices: 3.56 us -> 11.2 us  [exchanged(): return lax.all_to_all(value, axis, split_axis=0, concat_axis=0, tiled=True)]
    ppermute x26 -> x23, waiting for transfers between devices: 42.4 us -> 44.6 us  [swapped(): return lax.ppermute(value, axis, [(i, i ^ by) for i in range(size)])]
    concatenate x2, other arithmetic: 0.19 us -> 2.27 us  [local(): jnp.concatenate([part, swapped(part, 'node', 1)], axis=0)]
    all_to_all x1 -> x2, waiting for transfers between devices: 11 us -> 12.8 us  [exchanged(): return lax.all_to_all(value, axis, split_axis=0, concat_axis=0, tiled=True)]
    unnamed x26 -> x13, local copies, waits for them, and re-layouts: 2.4 us -> 0.95 us
    squeeze x1, local copies, waits for them, and re-layouts: 2.27 us -> 0.89 us  [local(): piece = lax.dynamic_index_in_dim(by_quarter, group ^ i, 0, keepdims=False)]
    ppermute x26 -> x23, starting transfers between devices: 33.4 us -> 33.2 us  [swapped(): return lax.ppermute(value, axis, [(i, i ^ by) for i in range(size)])]
  transfers between devices with their start and end apart: 29 -> 27, of which waited for: 9 -> 12; matrix products, arithmetic and copies ran while one was open for 7% -> 7% of each run, Pallas kernels for 18% -> 2%
where the time goes in v3:
time: 138 us
  waiting for transfers between devices  57.4 us (42%)
  starting transfers between devices  48.2 us (35%)
  Pallas kernels  18.2 us (13%)
  other arithmetic  10 us (7%)
  local copies, waits for them, and re-layouts  3.19 us (2%)
    ppermute x23, waiting for transfers between devices, swapped(): return lax.ppermute(value, axis, [(i, i ^ by) for i in range(size)])  44.6 us
    ppermute x23, starting transfers between devices, swapped(): return lax.ppermute(value, axis, [(i, i ^ by) for i in range(size)])  33.2 us
    all_to_all x2, waiting for transfers between devices, exchanged(): return lax.all_to_all(value, axis, split_axis=0, concat_axis=0, tiled=True)  12.8 us
    all_to_all x2, starting transfers between devices, exchanged(): return lax.all_to_all(value, axis, split_axis=0, concat_axis=0, tiled=True)  11.2 us
    pallas_call x1, Pallas kernels, aggregate(): pl.pallas_call(functools.partial(aggregate_kernel, reach), in_specs=[IN_S...  9.68 us
    ppermute x2, starting transfers between devices, shifted(): return lax.ppermute(value, axis, pairs)  3.82 us
    concatenate x4, other arithmetic, local(): jnp.concatenate([part, swapped(part, 'node', 1 << order[hop])], axis=0)  3.55 us
    pallas_call x1, Pallas kernels, weight_partial(): pl.pallas_call(functools.partial(weight_kernel, devs), in_specs=[IN_SMEM]...  3.29 us
  transfers between devices with their start and end apart: 27, of which 12 were waited for; matrix products, arithmetic and copies ran while one was open for 7% of the time, Pallas kernels for 2%

profile of v3, /device:TPU:0, one launch (start us, length us, event | category | flops | bytes accessed | tf_op | source)
XLA Modules:
  0.0 137.8 jit_solution(15781013233053843037)
XLA Ops:
  0.6 0.7 pad_add_fusion.me.index
  1.3 9.7 %aggregate.1 = (bf16[14,128,256]{2,1,0:T(8,128)(2,1)}, bf16[14,128,256]{2,1,0:T(8,128)(2,1)}, bf16[2,2,128,256]{3,2,1,0:T(8,128)(2,1)}, bf16[2,2,128,256]{3,2,1,0:T(8,128)(2,1)}) custom-call(s32[2]{0:T(128)} %pad_add_fusion.me.index, s32[5,14]{1,0:T(8,128)} %bitcast.58, s32[14]{0:T(128)} %count.1, bf16[1792,256]{1,0:T(8,128)(2,1)} %gc.1, ...), custom_call_target="tpu_custom_call" | custom-call | flops 1174405120 | bytes 7798784 | tf_op jit(solution)/shard_map/aggregate/pallas_call | solution.py:137
  11.0 2.5 %collective-permute-start = (bf16[2,2,128,256]{3,2,1,0:T(8,128)(2,1)}, bf16[2,2,128,256]{3,2,1,0:T(8,128)(2,1)S(1)}, u32[]{:S(2)}, u32[]{:S(2)}) collective-permute-start(bf16[2,2,128,256]{3,2,1,0:T(8,128)(2,1)} %get-tuple-element.39), channel_id=1, source_target_pairs={{0,4},{4,8},{8,12},{12,16},{16,20},{20,24},{24,28},{1,5},{5,9},{9,... | collective-permute-start | bytes 786440 | tf_op jit(solution)/shard_map/ppermute | solution.py:33
  13.6 1.3 collective-permute-start.1
  14.9 3.5 %collective-permute-start.3 = (bf16[128,256]{1,0:T(8,128)(2,1)}, bf16[128,256]{1,0:T(8,128)(2,1)}, u32[]{:S(2)}, u32[]{:S(2)}) collective-permute-start(bf16[128,256]{1,0:T(8,128)(2,1)} %param.12), channel_id=1, source_target_pairs={{0,2},{1,3},{2,0},{3,1},{4,6},{5,7},{6,4},{7,5},{8,10},{9,11},{10,... | collective-permute-start | bytes 196616 | tf_op jit(solution)/shard_map/ppermute | solution.py:38
  18.3 1.6 %collective-permute-start.2 = (bf16[128,256]{1,0:T(8,128)(2,1)}, bf16[128,256]{1,0:T(8,128)(2,1)}, u32[]{:S(2)}, u32[]{:S(2)}) collective-permute-start(bf16[128,256]{1,0:T(8,128)(2,1)} %param.12), channel_id=1, source_target_pairs={{0,1},{1,0},{2,3},{3,2},{4,5},{5,4},{6,7},{7,6},{8,9},{9,8},{10,11... | collective-permute-start | bytes 196616 | tf_op jit(solution)/shard_map/ppermute | solution.py:38
  19.9 0.9 dynamic-slice_bitcast_fusion
  20.8 3.9 %collective-permute-start.7 = (bf16[448,256]{1,0:T(8,128)(2,1)}, bf16[448,256]{1,0:T(8,128)(2,1)}, u32[]{:S(2)}, u32[]{:S(2)}) collective-permute-start(bf16[448,256]{1,0:T(8,128)(2,1)} %get-tuple-element.82), channel_id=1, source_target_pairs={{0,3},{1,2},{2,1},{3,0},{4,7},{5,6},{6,5},{7,4},{8,11},{9,10},{10,... | collective-permute-start | bytes 688136 | tf_op jit(solution)/shard_map/ppermute | solution.py:38
  24.8 1.7 %route.1 = (bf16[14,128,256]{2,1,0:T(8,128)(2,1)S(1)}, bf16[16,128,256]{2,1,0:T(8,128)(2,1)}) custom-call(s32[2]{0:T(128)S(1)} %copy-done.2, s32[112]{0:T(128)S(1)} %copy-done.3, bf16[14,128,256]{2,1,0:T(8,128)(2,1)S(1)} %copy-done, bf16[14,128,256]{2,1,0:T(8,128)(2,1)S(1)} %copy-done.1, bf16[2,2,128,256]{3,2,1,0:T(8,128)(2,1)S(1)} %collective-permute-done.low, ...), custom_call_target="tpu_custom_call" | custom-call | tf_op jit(solution)/shard_map/route/pallas_call | solution.py:181
  26.4 0.6 collective-permute-start.5
  27.1 6.4 %all-to-all-start = ((bf16[16,128,256]{2,1,0:T(8,128)(2,1)}), bf16[16,128,256]{2,1,0:T(8,128)(2,1)S(1)}, u32[]{:S(2)}, u32[]{:S(2)}) async-start(bf16[16,128,256]{2,1,0:T(8,128)(2,1)} %get-tuple-element.42), calls=%async_computation | async-start | bytes 2097152 | tf_op jit(solution)/shard_map/all_to_all | solution.py:42
  33.4 0.9 maximum_bitcast_fusion.1
  34.3 2.3 %collective-permute-start.10 = (bf16[1,2,128,256]{3,2,1,0:T(8,128)(2,1)S(1)}, bf16[1,2,128,256]{3,2,1,0:T(8,128)(2,1)S(1)}, u32[]{:S(2)}, u32[]{:S(2)}) collective-permute-start(bf16[1,2,128,256]{3,2,1,0:T(8,128)(2,1)S(1)} %maximum_bitcast_fusion.1), channel_id=1, source_target_pairs={{0,16},{4,20},{8,24},{12,28},{16,0},{20,4},{24,8},{28,12},{1,17},{... | collective-permute-start | bytes 393224 | tf_op jit(solution)/shard_map/ppermute | solution.py:38
  36.6 0.9 maximum_bitcast_fusion
  37.5 1.3 collective-permute-start.8
  38.8 11.9 %collective-permute-done.10 = bf16[1,2,128,256]{3,2,1,0:T(8,128)(2,1)S(1)} collective-permute-done((bf16[1,2,128,256]{3,2,1,0:T(8,128)(2,1)S(1)}, bf16[1,2,128,256]{3,2,1,0:T(8,128)(2,1)S(1)}, u32[]{:S(2)}, u32[]{:S(2)}) %collective-permute-start.10) | collective-permute-done | bytes 131104 | tf_op jit(solution)/shard_map/ppermute | solution.py:38
  50.7 1.5 %collective-permute-start.11 = (bf16[2,2,128,256]{3,2,1,0:T(8,128)(2,1)S(1)}, bf16[2,2,128,256]{3,2,1,0:T(8,128)(2,1)}, u32[]{:S(2)}, u32[]{:S(2)}) collective-permute-start(bf16[2,2,128,256]{3,2,1,0:T(8,128)(2,1)S(1)} %pad_maximum_fusion.5), channel_id=1, source_target_pairs={{0,8},{4,12},{8,0},{12,4},{16,24},{20,28},{24,16},{28,20},{1,9},{5... | collective-permute-start | bytes 786440 | tf_op jit(solution)/shard_map/ppermute | solution.py:38
  52.3 0.7 pad_maximum_fusion.4
  53.0 0.4 collective-permute-start.9
  53.4 0.1 eq.30
  53.4 0.1 add.65
  53.5 0.3 convert_reduce_fusion
  53.9 0.1 copy.13
  53.9 5.0 %collective-permute-done.11 = bf16[2,2,128,256]{3,2,1,0:T(8,128)(2,1)} collective-permute-done((bf16[2,2,128,256]{3,2,1,0:T(8,128)(2,1)S(1)}, bf16[2,2,128,256]{3,2,1,0:T(8,128)(2,1)}, u32[]{:S(2)}, u32[]{:S(2)}) %collective-permute-start.11) | collective-permute-done | bytes 262176 | tf_op jit(solution)/shard_map/ppermute | solution.py:38
  58.9 1.0 pad_maximum_fusion.3
  59.9 1.4 %collective-permute-done.9 = bf16[2,2,128,256]{3,2,1,0:T(8,128)(2,1)} collective-permute-done((bf16[2,2,128,256]{3,2,1,0:T(8,128)(2,1)}, bf16[2,2,128,256]{3,2,1,0:T(8,128)(2,1)}, u32[]{:S(2)}, u32[]{:S(2)}) %collective-permute-start.9) | collective-permute-done | bytes 262176 | tf_op jit(solution)/shard_map/ppermute | solution.py:38
  61.3 1.8 %pad_maximum_fusion.2 = bf16[4,2,128,256]{3,2,1,0:T(8,128)(2,1)} fusion(bf16[2,2,128,256]{3,2,1,0:T(8,128)(2,1)} %collective-permute-done.9, bf16[1,2,128,256]{3,2,1,0:T(8,128)(2,1)S(1)} %collective-permute-done.8, bf16[1,2,128,256]{3,2,1,0:T(8,128)(2,1)S(1)} %maximum_bitcast_fusion), kind=kLoop, calls=%fused_computation.7 | loop fusion | flops 524288 | bytes 1048576 | tf_op jit(solution)/shard_map/concatenate | solution.py:387
  63.1 0.1 collective-permute-start.15
  63.2 0.1 select_reduce_fusion
  63.3 0.6 collective-permute-start.16
  63.9 0.1 copy.14
  64.0 0.1 sub.13.landing
  64.1 0.9 merge.1
  65.0 0.1 slice_bitcast_fusion.4
  65.1 7.6 %collective-permute-start.14 = (bf16[448,256]{1,0:T(8,128)(2,1)S(1)}, bf16[448,256]{1,0:T(8,128)(2,1)S(1)}, u32[]{:S(2)}, u32[]{:S(2)}) collective-permute-start(bf16[448,256]{1,0:T(8,128)(2,1)S(1)} %get-tuple-element.78), channel_id=1, source_target_pairs={{0,3},{1,2},{2,1},{3,0},{4,7},{5,6},{6,5},{7,4},{8,11},{9,10},{10,... | collective-permute-start | bytes 688136 | tf_op jit(solution)/shard_map/ppermute | solution.py:38
  72.6 2.3 %collective-permute-start.13 = (bf16[448,256]{1,0:T(8,128)(2,1)S(1)}, bf16[448,256]{1,0:T(8,128)(2,1)S(1)}, u32[]{:S(2)}, u32[]{:S(2)}) collective-permute-start(bf16[448,256]{1,0:T(8,128)(2,1)S(1)} %get-tuple-element.79), channel_id=1, source_target_pairs={{0,2},{1,3},{2,0},{3,1},{4,6},{5,7},{6,4},{7,5},{8,10},{9,11},{10,... | collective-permute-start | bytes 688136 | tf_op jit(solution)/shard_map/ppermute | solution.py:38
  75.0 0.1 collective-permute-start.12
  75.1 1.1 pad_maximum_fusion.refs_4_
  76.3 1.1 pad_maximum_fusion.1.refs_5_
  77.4 1.8 %collective-permute-done.14.refs_3_.refs_7_ = bf16[448,256]{1,0:T(8,128)(2,1)S(1)} collective-permute-done((bf16[448,256]{1,0:T(8,128)(2,1)S(1)}, bf16[448,256]{1,0:T(8,128)(2,1)S(1)}, u32[]{:S(2)}, u32[]{:S(2)}) %collective-permute-start.14) | collective-permute-done | bytes 229408 | tf_op jit(solution)/shard_map/ppermute | solution.py:38
  79.2 14.0 %collective-permute-done.13.refs_2_.refs_6_ = bf16[448,256]{1,0:T(8,128)(2,1)S(1)} collective-permute-done((bf16[448,256]{1,0:T(8,128)(2,1)S(1)}, bf16[448,256]{1,0:T(8,128)(2,1)S(1)}, u32[]{:S(2)}, u32[]{:S(2)}) %collective-permute-start.13) | collective-permute-done | bytes 229408 | tf_op jit(solution)/shard_map/ppermute | solution.py:38
  93.2 2.6 %feature_rows.1 = bf16[4,448,256]{2,1,0:T(8,128)(2,1)} custom-call(s32[2]{0:T(128)S(1)} %copy-done.2, bf16[448,256]{1,0:T(8,128)(2,1)S(1)} %get-tuple-element.66.refs_0_.refs_4_, bf16[448,256]{1,0:T(8,128)(2,1)S(1)} %collective-permute-done.12.refs_1_.refs_5_, bf16[448,256]{1,0:T(8,128)(2,1)S(1)} %collective-permute-done.13.refs_2_.refs_6_, ...), custom_call_target="tpu_custom_call" | custom-call | flops 939524096 | bytes 3932160 | tf_op jit(solution)/shard_map/feature_rows/pallas_call | solution.py:310
  95.8 3.3 %weight_partial.1 = (bf16[2,4,2,128,256]{4,3,2,1,0:T(8,128)(2,1)S(1)}, bf16[2,4,2,128,256]{4,3,2,1,0:T(8,128)(2,1)S(1)}) custom-call(s32[2]{0:T(128)S(1)} %copy-done.2, bf16[448,256]{1,0:T(8,128)(2,1)S(1)} %get-tuple-element.62.refs_0_, bf16[448,256]{1,0:T(8,128)(2,1)S(1)} %collective-permute-done.5.refs_1_, ...), custom_call_target="tpu_custom_call" | custom-call | flops 939524096 | bytes 3932160 | tf_op jit(solution)/shard_map/weight_partial/pallas_call | solution.py:266
  99.1 0.1 collective-permute-start.17
  99.2 2.6 %collective-permute-done.17 = bf16[2,4,2,128,256]{4,3,2,1,0:T(8,128)(2,1)S(1)} collective-permute-done((bf16[2,4,2,128,256]{4,3,2,1,0:T(8,128)(2,1)S(1)}, bf16[2,4,2,128,256]{4,3,2,1,0:T(8,128)(2,1)S(1)}, u32[]{:S(2)}, u32[]{:S(2)}) %collective-permute-start.17) | collective-permute-done | bytes 1048608 | tf_op jit(solution)/shard_map/ppermute | solution.py:38
  101.8 0.4 fusion.10
  102.2 0.8 slice_bitcast_fusion.2
  103.1 0.4 collective-permute-start.21
  103.4 0.4 collective-permute-start.18
  103.9 4.8 %all-to-all-start.1 = ((bf16[4,448,256]{2,1,0:T(8,128)(2,1)}), bf16[4,448,256]{2,1,0:T(8,128)(2,1)S(1)}, u32[]{:S(2)}, u32[]{:S(2)}) async-start(bf16[4,448,256]{2,1,0:T(8,128)(2,1)} %feature_rows.1), calls=%async_computation.1 | async-start | bytes 1835008 | tf_op jit(solution)/shard_map/all_to_all | solution.py:42
  108.7 3.0 %collective-permute-done.21 = bf16[2,2,128,256]{3,2,1,0:T(8,128)(2,1)S(1)} collective-permute-done((bf16[2,2,128,256]{3,2,1,0:T(8,128)(2,1)}, bf16[2,2,128,256]{3,2,1,0:T(8,128)(2,1)S(1)}, u32[]{:S(2)}, u32[]{:S(2)}) %collective-permute-start.21) | collective-permute-done | bytes 262176 | tf_op jit(solution)/shard_map/ppermute | solution.py:38
  111.6 0.1 collective-permute-done.18
  111.7 0.1 fusion
  111.9 1.7 %collective-permute-start.19 = (bf16[1,2,128,256]{3,2,1,0:T(8,128)(2,1)S(1)}, bf16[1,2,128,256]{3,2,1,0:T(8,128)(2,1)S(1)}, u32[]{:S(2)}, u32[]{:S(2)}) collective-permute-start(bf16[1,2,128,256]{3,2,1,0:T(8,128)(2,1)S(1)} %slice.138), channel_id=1, source_target_pairs={{0,16},{4,20},{8,24},{12,28},{16,0},{20,4},{24,8},{28,12},{1,17},{... | collective-permute-start | bytes 393224 | tf_op jit(solution)/shard_map/ppermute | solution.py:38
  113.6 0.4 collective-permute-start.22
  114.0 2.9 %collective-permute-done.19 = bf16[1,2,128,256]{3,2,1,0:T(8,128)(2,1)S(1)} collective-permute-done((bf16[1,2,128,256]{3,2,1,0:T(8,128)(2,1)S(1)}, bf16[1,2,128,256]{3,2,1,0:T(8,128)(2,1)S(1)}, u32[]{:S(2)}, u32[]{:S(2)}) %collective-permute-start.19) | collective-permute-done | bytes 131104 | tf_op jit(solution)/shard_map/ppermute | solution.py:38
  116.9 0.8 collective-permute-start.20
  117.7 0.9 collective-permute-done.22
  118.7 2.5 %collective-permute-start.23 = (bf16[128,256]{1,0:T(8,128)(2,1)S(1)}, bf16[128,256]{1,0:T(8,128)(2,1)S(1)}, u32[]{:S(2)}, u32[]{:S(2)}) collective-permute-start(bf16[128,256]{1,0:T(8,128)(2,1)S(1)} %get-tuple-element.86), channel_id=1, source_target_pairs={{0,2},{1,3},{2,0},{3,1},{4,6},{5,7},{6,4},{7,5},{8,10},{9,11},{10,... | collective-permute-start | bytes 196616 | tf_op jit(solution)/shard_map/ppermute | solution.py:38
  121.2 1.2 collective-permute-start.24
  122.4 12.8 %all-to-all-done.1 = bf16[4,448,256]{2,1,0:T(8,128)(2,1)S(1)} async-done(((bf16[4,448,256]{2,1,0:T(8,128)(2,1)}), bf16[4,448,256]{2,1,0:T(8,128)(2,1)S(1)}, u32[]{:S(2)}, u32[]{:S(2)}) %all-to-all-start.1) | async-done | bytes 917536 | tf_op jit(solution)/shard_map/all_to_all | solution.py:42
  135.2 1.0 collective-permute-done.23
  136.2 0.7 fusion.5
  136.9 0.9 copy.16
  (40 shorter events, 0.2 us)
Async XLA Ops:
  1.3 18.6 %copy-start.5 = (bf16[1792,256]{1,0:T(8,128)(2,1)S(1)}, bf16[1792,256]{1,0:T(8,128)(2,1)}, u32[]{:S(2)}) copy-start(bf16[1792,256]{1,0:T(8,128)(2,1)} %param.11) | copy-start | bytes 2752516
  1.3 23.4 %copy-start.2 = (s32[2]{0:T(128)S(1)}, s32[2]{0:T(128)}, u32[]{:S(2)}) copy-start(s32[2]{0:T(128)} %pad_add_fusion.me.index) | copy-start | bytes 28
  1.3 23.4 %copy-start.3 = (s32[112]{0:T(128)S(1)}, s32[112]{0:T(128)}, u32[]{:S(2)}) copy-start(s32[112]{0:T(128)} %shuffle.1) | copy-start | bytes 1348
  11.0 13.7 %copy-start = (bf16[14,128,256]{2,1,0:T(8,128)(2,1)S(1)}, bf16[14,128,256]{2,1,0:T(8,128)(2,1)}, u32[]{:S(2)}) copy-start(bf16[14,128,256]{2,1,0:T(8,128)(2,1)} %get-tuple-element.37.clean) | copy-start | bytes 2752516
  11.0 13.7 %copy-start.1 = (bf16[14,128,256]{2,1,0:T(8,128)(2,1)S(1)}, bf16[14,128,256]{2,1,0:T(8,128)(2,1)}, u32[]{:S(2)}) copy-start(bf16[14,128,256]{2,1,0:T(8,128)(2,1)} %get-tuple-element.38.corrupt) | copy-start | bytes 2752516
  11.0 9.8 %collective-permute-start = (bf16[2,2,128,256]{3,2,1,0:T(8,128)(2,1)}, bf16[2,2,128,256]{3,2,1,0:T(8,128)(2,1)S(1)}, u32[]{:S(2)}, u32[]{:S(2)}) collective-permute-start(bf16[2,2,128,256]{3,2,1,0:T(8,128)(2,1)} %get-tuple-element.39), channel_id=1, source_target_pairs={{0,4},{4,8},{8,12},{12,16},{16,20},{20,24},{24,28},{1,5},{5,9},{9,... | collective-permute-start | bytes 786440 | tf_op jit(solution)/shard_map/ppermute | solution.py:33
  13.6 11.2 %collective-permute-start.1 = (bf16[2,2,128,256]{3,2,1,0:T(8,128)(2,1)}, bf16[2,2,128,256]{3,2,1,0:T(8,128)(2,1)S(1)}, u32[]{:S(2)}, u32[]{:S(2)}) collective-permute-start(bf16[2,2,128,256]{3,2,1,0:T(8,128)(2,1)} %get-tuple-element.40), channel_id=1, source_target_pairs={{4,0},{8,4},{12,8},{16,12},{20,16},{24,20},{28,24},{5,1},{9,5},{13... | collective-permute-start | bytes 786440 | tf_op jit(solution)/shard_map/ppermute | solution.py:33
  14.9 11.6 %collective-permute-start.3 = (bf16[128,256]{1,0:T(8,128)(2,1)}, bf16[128,256]{1,0:T(8,128)(2,1)}, u32[]{:S(2)}, u32[]{:S(2)}) collective-permute-start(bf16[128,256]{1,0:T(8,128)(2,1)} %param.12), channel_id=1, source_target_pairs={{0,2},{1,3},{2,0},{3,1},{4,6},{5,7},{6,4},{7,5},{8,10},{9,11},{10,... | collective-permute-start | bytes 196616 | tf_op jit(solution)/shard_map/ppermute | solution.py:38
  18.3 8.7 %collective-permute-start.2 = (bf16[128,256]{1,0:T(8,128)(2,1)}, bf16[128,256]{1,0:T(8,128)(2,1)}, u32[]{:S(2)}, u32[]{:S(2)}) collective-permute-start(bf16[128,256]{1,0:T(8,128)(2,1)} %param.12), channel_id=1, source_target_pairs={{0,1},{1,0},{2,3},{3,2},{4,5},{5,4},{6,7},{7,6},{8,9},{9,8},{10,11... | collective-permute-start | bytes 196616 | tf_op jit(solution)/shard_map/ppermute | solution.py:38
  19.9 7.2 %collective-permute-start.4 = (bf16[128,256]{1,0:T(8,128)(2,1)}, bf16[128,256]{1,0:T(8,128)(2,1)}, u32[]{:S(2)}, u32[]{:S(2)}) collective-permute-start(bf16[128,256]{1,0:T(8,128)(2,1)} %param.12), channel_id=1, source_target_pairs={{0,3},{1,2},{2,1},{3,0},{4,7},{5,6},{6,5},{7,4},{8,11},{9,10},{10,... | collective-permute-start | bytes 196616 | tf_op jit(solution)/shard_map/ppermute | solution.py:38
  20.8 42.3 %collective-permute-start.7 = (bf16[448,256]{1,0:T(8,128)(2,1)}, bf16[448,256]{1,0:T(8,128)(2,1)}, u32[]{:S(2)}, u32[]{:S(2)}) collective-permute-start(bf16[448,256]{1,0:T(8,128)(2,1)} %get-tuple-element.82), channel_id=1, source_target_pairs={{0,3},{1,2},{2,1},{3,0},{4,7},{5,6},{6,5},{7,4},{8,11},{9,10},{10,... | collective-permute-start | bytes 688136 | tf_op jit(solution)/shard_map/ppermute | solution.py:38
  24.7 38.4 %collective-permute-start.6 = (bf16[448,256]{1,0:T(8,128)(2,1)}, bf16[448,256]{1,0:T(8,128)(2,1)}, u32[]{:S(2)}, u32[]{:S(2)}) collective-permute-start(bf16[448,256]{1,0:T(8,128)(2,1)} %get-tuple-element.83), channel_id=1, source_target_pairs={{0,2},{1,3},{2,0},{3,1},{4,6},{5,7},{6,4},{7,5},{8,10},{9,11},{10,... | collective-permute-start | bytes 688136 | tf_op jit(solution)/shard_map/ppermute | solution.py:38
  26.4 36.7 %collective-permute-start.5 = (bf16[448,256]{1,0:T(8,128)(2,1)}, bf16[448,256]{1,0:T(8,128)(2,1)S(1)}, u32[]{:S(2)}, u32[]{:S(2)}) collective-permute-start(bf16[448,256]{1,0:T(8,128)(2,1)} %get-tuple-element.84), channel_id=1, source_target_pairs={{0,1},{1,0},{2,3},{3,2},{4,5},{5,4},{6,7},{7,6},{8,9},{9,8},{10,11... | collective-permute-start | bytes 688136 | tf_op jit(solution)/shard_map/ppermute | solution.py:38
  27.1 36.0 %all-to-all-start = ((bf16[16,128,256]{2,1,0:T(8,128)(2,1)}), bf16[16,128,256]{2,1,0:T(8,128)(2,1)S(1)}, u32[]{:S(2)}, u32[]{:S(2)}) async-start(bf16[16,128,256]{2,1,0:T(8,128)(2,1)} %get-tuple-element.42), calls=%async_computation | async-start | bytes 2097152 | tf_op jit(solution)/shard_map/all_to_all | solution.py:42
  34.3 16.4 %collective-permute-start.10 = (bf16[1,2,128,256]{3,2,1,0:T(8,128)(2,1)S(1)}, bf16[1,2,128,256]{3,2,1,0:T(8,128)(2,1)S(1)}, u32[]{:S(2)}, u32[]{:S(2)}) collective-permute-start(bf16[1,2,128,256]{3,2,1,0:T(8,128)(2,1)S(1)} %maximum_bitcast_fusion.1), channel_id=1, source_target_pairs={{0,16},{4,20},{8,24},{12,28},{16,0},{20,4},{24,8},{28,12},{1,17},{... | collective-permute-start | bytes 393224 | tf_op jit(solution)/shard_map/ppermute | solution.py:38
  37.5 14.8 %collective-permute-start.8 = (bf16[1,2,128,256]{3,2,1,0:T(8,128)(2,1)S(1)}, bf16[1,2,128,256]{3,2,1,0:T(8,128)(2,1)S(1)}, u32[]{:S(2)}, u32[]{:S(2)}) collective-permute-start(bf16[1,2,128,256]{3,2,1,0:T(8,128)(2,1)S(1)} %maximum_bitcast_fusion), channel_id=1, source_target_pairs={{0,8},{4,12},{8,0},{12,4},{16,24},{20,28},{24,16},{28,20},{1,9},{5... | collective-permute-start | bytes 393224 | tf_op jit(solution)/shard_map/ppermute | solution.py:38
  50.7 8.2 %collective-permute-start.11 = (bf16[2,2,128,256]{3,2,1,0:T(8,128)(2,1)S(1)}, bf16[2,2,128,256]{3,2,1,0:T(8,128)(2,1)}, u32[]{:S(2)}, u32[]{:S(2)}) collective-permute-start(bf16[2,2,128,256]{3,2,1,0:T(8,128)(2,1)S(1)} %pad_maximum_fusion.5), channel_id=1, source_target_pairs={{0,8},{4,12},{8,0},{12,4},{16,24},{20,28},{24,16},{28,20},{1,9},{5... | collective-permute-start | bytes 786440 | tf_op jit(solution)/shard_map/ppermute | solution.py:38
  53.0 8.3 %collective-permute-start.9 = (bf16[2,2,128,256]{3,2,1,0:T(8,128)(2,1)}, bf16[2,2,128,256]{3,2,1,0:T(8,128)(2,1)}, u32[]{:S(2)}, u32[]{:S(2)}) collective-permute-start(bf16[2,2,128,256]{3,2,1,0:T(8,128)(2,1)} %pad_maximum_fusion.4), channel_id=1, source_target_pairs={{0,16},{4,20},{8,24},{12,28},{16,0},{20,4},{24,8},{28,12},{1,17},{... | collective-permute-start | bytes 786440 | tf_op jit(solution)/shard_map/ppermute | solution.py:38
  63.1 12.0 %collective-permute-start.15 = (bf16[4,2,128,256]{3,2,1,0:T(8,128)(2,1)}, bf16[4,2,128,256]{3,2,1,0:T(8,128)(2,1)}, u32[]{:S(2)}, u32[]{:S(2)}) collective-permute-start(bf16[4,2,128,256]{3,2,1,0:T(8,128)(2,1)} %pad_maximum_fusion.2), channel_id=1, source_target_pairs={{0,4},{4,0},{8,12},{12,8},{16,20},{20,16},{24,28},{28,24},{1,5},{5... | collective-permute-start | bytes 1572872 | tf_op jit(solution)/shard_map/ppermute | solution.py:38
  63.3 12.9 %collective-permute-start.16 = (bf16[4,2,128,256]{3,2,1,0:T(8,128)(2,1)S(1)}, bf16[4,2,128,256]{3,2,1,0:T(8,128)(2,1)}, u32[]{:S(2)}, u32[]{:S(2)}) collective-permute-start(bf16[4,2,128,256]{3,2,1,0:T(8,128)(2,1)S(1)} %pad_maximum_fusion.3), channel_id=1, source_target_pairs={{0,4},{4,0},{8,12},{12,8},{16,20},{20,16},{24,28},{28,24},{1,5},{5... | collective-permute-start | bytes 1572872 | tf_op jit(solution)/shard_map/ppermute | solution.py:38
  64.1 11.0 %copy-start.4 = (bf16[4,2,128,256]{3,2,1,0:T(8,128)(2,1)S(1)}, bf16[4,2,128,256]{3,2,1,0:T(8,128)(2,1)}, u32[]{:S(2)}) copy-start(bf16[4,2,128,256]{3,2,1,0:T(8,128)(2,1)} %pad_maximum_fusion.2) | copy-start | bytes 1572868
  65.1 14.1 %collective-permute-start.14 = (bf16[448,256]{1,0:T(8,128)(2,1)S(1)}, bf16[448,256]{1,0:T(8,128)(2,1)S(1)}, u32[]{:S(2)}, u32[]{:S(2)}) collective-permute-start(bf16[448,256]{1,0:T(8,128)(2,1)S(1)} %get-tuple-element.78), channel_id=1, source_target_pairs={{0,3},{1,2},{2,1},{3,0},{4,7},{5,6},{6,5},{7,4},{8,11},{9,10},{10,... | collective-permute-start | bytes 688136 | tf_op jit(solution)/shard_map/ppermute | solution.py:38
  72.6 20.5 %collective-permute-start.13 = (bf16[448,256]{1,0:T(8,128)(2,1)S(1)}, bf16[448,256]{1,0:T(8,128)(2,1)S(1)}, u32[]{:S(2)}, u32[]{:S(2)}) collective-permute-start(bf16[448,256]{1,0:T(8,128)(2,1)S(1)} %get-tuple-element.79), channel_id=1, source_target_pairs={{0,2},{1,3},{2,0},{3,1},{4,6},{5,7},{6,4},{7,5},{8,10},{9,11},{10,... | collective-permute-start | bytes 688136 | tf_op jit(solution)/shard_map/ppermute | solution.py:38
  75.0 18.2 %collective-permute-start.12 = (bf16[448,256]{1,0:T(8,128)(2,1)S(1)}, bf16[448,256]{1,0:T(8,128)(2,1)S(1)}, u32[]{:S(2)}, u32[]{:S(2)}) collective-permute-start(bf16[448,256]{1,0:T(8,128)(2,1)S(1)} %get-tuple-element.80), channel_id=1, source_target_pairs={{0,1},{1,0},{2,3},{3,2},{4,5},{5,4},{6,7},{7,6},{8,9},{9,8},{10,11... | collective-permute-start | bytes 688136 | tf_op jit(solution)/shard_map/ppermute | solution.py:38
  99.1 2.7 %collective-permute-start.17 = (bf16[2,4,2,128,256]{4,3,2,1,0:T(8,128)(2,1)S(1)}, bf16[2,4,2,128,256]{4,3,2,1,0:T(8,128)(2,1)S(1)}, u32[]{:S(2)}, u32[]{:S(2)}) collective-permute-start(bf16[2,4,2,128,256]{4,3,2,1,0:T(8,128)(2,1)S(1)} %get-tuple-element.71), channel_id=1, source_target_pairs={{0,4},{4,0},{8,12},{12,8},{16,20},{20,16},{24,28},{28,24},{1,5},{5... | collective-permute-start | bytes 3145736 | tf_op jit(solution)/shard_map/ppermute | solution.py:38
  103.1 8.6 %collective-permute-start.21 = (bf16[2,2,128,256]{3,2,1,0:T(8,128)(2,1)}, bf16[2,2,128,256]{3,2,1,0:T(8,128)(2,1)S(1)}, u32[]{:S(2)}, u32[]{:S(2)}) collective-permute-start(bf16[2,2,128,256]{3,2,1,0:T(8,128)(2,1)} %get-tuple-element.76), channel_id=1, source_target_pairs={{0,16},{4,20},{8,24},{12,28},{16,0},{20,4},{24,8},{28,12},{1,17},{... | collective-permute-start | bytes 786440 | tf_op jit(solution)/shard_map/ppermute | solution.py:38
  103.4 8.3 %collective-permute-start.18 = (bf16[2,2,128,256]{3,2,1,0:T(8,128)(2,1)}, bf16[2,2,128,256]{3,2,1,0:T(8,128)(2,1)S(1)}, u32[]{:S(2)}, u32[]{:S(2)}) collective-permute-start(bf16[2,2,128,256]{3,2,1,0:T(8,128)(2,1)} %get-tuple-element.77), channel_id=1, source_target_pairs={{0,8},{4,12},{8,0},{12,4},{16,24},{20,28},{24,16},{28,20},{1,9},{5... | collective-permute-start | bytes 786440 | tf_op jit(solution)/shard_map/ppermute | solution.py:38
  103.9 31.3 %all-to-all-start.1 = ((bf16[4,448,256]{2,1,0:T(8,128)(2,1)}), bf16[4,448,256]{2,1,0:T(8,128)(2,1)S(1)}, u32[]{:S(2)}, u32[]{:S(2)}) async-start(bf16[4,448,256]{2,1,0:T(8,128)(2,1)} %feature_rows.1), calls=%async_computation.1 | async-start | bytes 1835008 | tf_op jit(solution)/shard_map/all_to_all | solution.py:42
  111.9 5.0 %collective-permute-start.19 = (bf16[1,2,128,256]{3,2,1,0:T(8,128)(2,1)S(1)}, bf16[1,2,128,256]{3,2,1,0:T(8,128)(2,1)S(1)}, u32[]{:S(2)}, u32[]{:S(2)}) collective-permute-start(bf16[1,2,128,256]{3,2,1,0:T(8,128)(2,1)S(1)} %slice.138), channel_id=1, source_target_pairs={{0,16},{4,20},{8,24},{12,28},{16,0},{20,4},{24,8},{28,12},{1,17},{... | collective-permute-start | bytes 393224 | tf_op jit(solution)/shard_map/ppermute | solution.py:38
  113.6 5.0 %collective-permute-start.22 = (bf16[1,2,128,256]{3,2,1,0:T(8,128)(2,1)S(1)}, bf16[1,2,128,256]{3,2,1,0:T(8,128)(2,1)S(1)}, u32[]{:S(2)}, u32[]{:S(2)}) collective-permute-start(bf16[1,2,128,256]{3,2,1,0:T(8,128)(2,1)S(1)} %slice.137), channel_id=1, source_target_pairs={{0,8},{4,12},{8,0},{12,4},{16,24},{20,28},{24,16},{28,20},{1,9},{5... | collective-permute-start | bytes 393224 | tf_op jit(solution)/shard_map/ppermute | solution.py:38
  116.9 18.3 %collective-permute-start.20 = (bf16[128,256]{1,0:T(8,128)(2,1)S(1)}, bf16[128,256]{1,0:T(8,128)(2,1)S(1)}, u32[]{:S(2)}, u32[]{:S(2)}) collective-permute-start(bf16[128,256]{1,0:T(8,128)(2,1)S(1)} %fusion.6), channel_id=1, source_target_pairs={{0,1},{1,0},{2,3},{3,2},{4,5},{5,4},{6,7},{7,6},{8,9},{9,8},{10,11... | collective-permute-start | bytes 196616 | tf_op jit(solution)/shard_map/ppermute | solution.py:38
  118.7 17.5 %collective-permute-start.23 = (bf16[128,256]{1,0:T(8,128)(2,1)S(1)}, bf16[128,256]{1,0:T(8,128)(2,1)S(1)}, u32[]{:S(2)}, u32[]{:S(2)}) collective-permute-start(bf16[128,256]{1,0:T(8,128)(2,1)S(1)} %get-tuple-element.86), channel_id=1, source_target_pairs={{0,2},{1,3},{2,0},{3,1},{4,6},{5,7},{6,4},{7,5},{8,10},{9,11},{10,... | collective-permute-start | bytes 196616 | tf_op jit(solution)/shard_map/ppermute | solution.py:38
  121.2 15.0 %collective-permute-start.24 = (bf16[128,256]{1,0:T(8,128)(2,1)S(1)}, bf16[128,256]{1,0:T(8,128)(2,1)S(1)}, u32[]{:S(2)}, u32[]{:S(2)}) collective-permute-start(bf16[128,256]{1,0:T(8,128)(2,1)S(1)} %get-tuple-element.87), channel_id=1, source_target_pairs={{0,3},{1,2},{2,1},{3,0},{4,7},{5,6},{6,5},{7,4},{8,11},{9,10},{10,... | collective-permute-start | bytes 196616 | tf_op jit(solution)/shard_map/ppermute | solution.py:38

commit v4 on v3

--- a/solution.py
+++ b/solution.py
@@ -47,10 +47,13 @@
 
 
 def aggregate_kernel(
-    reach, me, cols, count, gc, pc, gx, px, slopes, adj, clean, corrupt, down, up, data, tiles, rhs, stage, sems
+    reach, groups, me, cols, count, gc, pc, gx, px, slopes, adj, features, weight, *refs
 ):
+    clean, corrupt, down, up, *refs = refs
+    packed, (data, tiles, rhs, stage, sems, pack_sems) = refs[:groups], refs[groups:]
     blocks, slots, rows, _ = adj.shape
     width = gc.shape[1]
+    quarter = features.shape[0] // groups
     spare = blocks + 2 * reach
     pad = 2 * reach * rows
 
@@ -62,9 +65,18 @@
         ]
         return out + [pltpu.make_async_copy(adj.at[block], tiles.at[block], sems.at[4, block])]
 
+    packs = []
+    for i in range(groups):
+        span = pl.ds(pl.multiple_of((me[1] ^ i) * quarter, quarter), quarter)
+        packs.append(
+            pltpu.make_async_copy(features.at[span], packed[i].at[:quarter], pack_sems.at[0, i])
+        )
+        packs.append(pltpu.make_async_copy(weight, packed[i].at[quarter:], pack_sems.at[1, i]))
     for block in range(blocks):
         for copy in copies(block):
             copy.start()
+    for copy in packs:
+        copy.start()
     stage[...] = jnp.zeros_like(stage)
     rhs[:pad] = jnp.zeros((pad, 2 * width), jnp.bfloat16)
     rhs[pad + blocks * rows :] = jnp.zeros((pad, 2 * width), jnp.bfloat16)
@@ -129,22 +141,29 @@
         span = pl.ds(2 * step, 2)
         clean[span], corrupt[span] = pair(reach + 2 * step)
 
-
-def aggregate(me, cols, count, gc, pc, gx, px, slopes, adj, reach):
+    for copy in packs:
+        copy.wait()
+
+
+def aggregate(me, cols, count, gc, pc, gx, px, slopes, adj, features, weight, reach, groups):
     blocks, slots, rows, _ = adj.shape
     width = gc.shape[1]
     assert reach % 2 == 0 and blocks % 2 == 0
-    return pl.pallas_call(
-        functools.partial(aggregate_kernel, reach),
-        in_specs=[IN_SMEM] * 3 + [IN_HBM] * 4 + [IN_VMEM, IN_HBM],
-        out_specs=[IN_VMEM] * 4,
-        out_shape=[bf16(blocks, rows, width)] * 2 + [bf16(2, reach, rows, width)] * 2,
+    packed = features.shape[0] // groups + weight.shape[0]
+    return pl.pallas_call(
+        functools.partial(aggregate_kernel, reach, groups),
+        in_specs=[IN_SMEM] * 3 + [IN_HBM] * 4 + [IN_VMEM] + [IN_HBM] * 3,
+        out_specs=[IN_VMEM] * 4 + [IN_HBM] * groups,
+        out_shape=[bf16(blocks, rows, width)] * 2
+        + [bf16(2, reach, rows, width)] * 2
+        + [bf16(packed, width)] * groups,
         scratch_shapes=[
             pltpu.VMEM((4, blocks, rows, width), jnp.bfloat16),
             pltpu.VMEM((blocks, slots, rows, rows), jnp.bfloat16),
             pltpu.VMEM(((blocks + 4 * reach) * rows, 2 * width), jnp.bfloat16),
             pltpu.VMEM((blocks + 2 * reach + 1, 2 * reach + 1, rows, rows), jnp.bfloat16),
             pltpu.SemaphoreType.DMA((5, blocks)),
+            pltpu.SemaphoreType.DMA((2, groups)),
         ],
         compiler_params=params(VMEM_ALL),
         cost_estimate=pl.CostEstimate(
@@ -153,7 +172,7 @@
             transcendentals=0,
         ),
         name="aggregate",
-    )(me, cols, count, gc, pc, gx, px, slopes, adj)
+    )(me, cols, count, gc, pc, gx, px, slopes, adj, features, weight)
 
 
 def route_kernel(reach, slots, me, shuffle, clean, corrupt, low, high, whole, outgoing, used):
@@ -189,7 +208,10 @@
     )(me, shuffle, clean, corrupt, low, high)
 
 
-def merge_kernel(quarter, index, landing, clean, incoming, out):
+def merge_kernel(quarter, index, landing, clean, incoming, *refs):
+    *packed, out, tiles = refs
+    for i, piece in enumerate(packed):
+        tiles[i] = piece[quarter:]
     _, rows, _ = clean.shape
     group = index[1]
     piece = math.gcd(rows, quarter)
@@ -208,66 +230,56 @@
                 ]
 
 
-def merge(index, landing, clean, incoming, groups):
+def merge(index, landing, clean, incoming, packed):
     blocks, rows, width = clean.shape
+    groups = len(packed)
     quarter = blocks * rows // groups
+    height = packed[0].shape[0] - quarter
     return pl.pallas_call(
         functools.partial(merge_kernel, quarter),
-        in_specs=[IN_SMEM] * 2 + [IN_VMEM] * 2,
-        out_specs=IN_VMEM,
-        out_shape=bf16(groups, quarter, width),
+        in_specs=[IN_SMEM] * 2 + [IN_VMEM] * (2 + groups),
+        out_specs=[IN_VMEM] * 2,
+        out_shape=[bf16(groups, quarter, width), bf16(groups, height, width)],
         compiler_params=params(),
         name="merge",
-    )(index, landing, clean, incoming)
-
-
-def halving_orders(devs):
-    bits = list(range(1, devs.bit_length() - 1))
-    return bits, bits[::-1]
+    )(index, landing, clean, incoming, *packed)
 
 
 def weight_kernel(devs, index, *refs):
     groups = (len(refs) - 2) // 2
-    feats, summed, (keep, send) = refs[:groups], refs[groups : 2 * groups], refs[2 * groups :]
+    packed, summed, (keep, send) = refs[:groups], refs[groups : 2 * groups], refs[2 * groups :]
     me, group = index[0], index[1]
     shares = devs // groups
-    height, width = keep.shape[3:]
+    height, width = keep.shape[2:]
     rhs = jnp.concatenate([piece[...] for piece in summed], axis=1)
     for relative in range(groups):
         product = lax.dot_general(
-            feats[relative][...],
+            packed[relative][: rhs.shape[0]],
             rhs,
             (((0,), (0,)), ((), ())),
             preferred_element_type=jnp.float32,
         ).astype(jnp.bfloat16)
         for share in range(shares):
             node = ((group ^ relative) * shares + share) ^ me
-            for half, order in enumerate(halving_orders(devs)):
-                place = jnp.int32(0)
-                for bit in order:
-                    place = place * 2 + ((node >> bit) & 1)
-                for i in range(groups // 2):
-                    column = (half * (groups // 2) + i) * width
-                    part = product[share * height : (share + 1) * height, column : column + width]
-
-                    @pl.when((node & 1) == 0)
-                    def _():
-                        keep[half, place, i] = part
-
-                    @pl.when((node & 1) == 1)
-                    def _():
-                        send[half, place, i] = part
-
-
-def weight_partial(index, feats, summed, devs):
-    groups = len(feats)
-    rows, width = feats[0].shape
+            rows = product[share * height : (share + 1) * height]
+
+            def store(out):
+                for i in range(groups):
+                    out[node >> 1, i] = rows[:, i * width : (i + 1) * width]
+
+            pl.when((node & 1) == 0)(functools.partial(store, keep))
+            pl.when((node & 1) == 1)(functools.partial(store, send))
+
+
+def weight_partial(index, packed, summed, devs):
+    groups = len(packed)
+    rows, width = summed[0].shape
     height = groups * width // devs
     return pl.pallas_call(
         functools.partial(weight_kernel, devs),
         in_specs=[IN_SMEM] + [IN_VMEM] * (2 * groups),
         out_specs=[IN_VMEM] * 2,
-        out_shape=[bf16(2, devs // 2, groups // 2, height, width)] * 2,
+        out_shape=[bf16(devs // 2, groups, height, width)] * 2,
         compiler_params=params(),
         cost_estimate=pl.CostEstimate(
             flops=2 * rows * (groups * width) ** 2,
@@ -275,36 +287,40 @@
             transcendentals=0,
         ),
         name="weight_partial",
-    )(index, *feats, *summed)
+    )(index, *packed, *summed)
 
 
 def feature_kernel(index, *refs):
-    *summed, low, high, out = refs
+    *summed, even, odd, out = refs
     groups = len(summed)
-    devs = low.shape[0]
-    me = index[0]
+    devs = 2 * even.shape[0]
+    me, group = index[0], index[1]
     shares = devs // groups
+    height = even.shape[2]
+    low = me & (shares - 1)
     lhs = jnp.concatenate([piece[...] for piece in summed], axis=1)
-    for target in range(groups):
+    for relative in range(groups):
         rows = []
-        for share in range(shares):
-            node = (target * shares + share) ^ me
-            parts = []
-            for half, order in zip((low, high), halving_orders(devs)):
-                place = jnp.int32(0)
-                for j, bit in enumerate([*order, 0]):
-                    place += ((node >> bit) & 1) << j
-                parts += [half[place, i] for i in range(groups // 2)]
-            rows.append(jnp.concatenate(parts, axis=1))
-        out[target] = lax.dot_general(
+        for i in range(shares):
+            node = (((group ^ relative) * shares) ^ (me - low)) + i
+            half = odd if i % 2 else even
+            rows.append(jnp.concatenate([half[node >> 1, j] for j in range(groups)], axis=1))
+        product = lax.dot_general(
             lhs,
             jnp.concatenate(rows, axis=0),
             (((1,), (1,)), ((), ())),
             preferred_element_type=jnp.float32,
         ).astype(jnp.bfloat16)
-
-
-def feature_rows(index, summed, halves):
+        parts = [product[:, i * height : (i + 1) * height] for i in range(shares)]
+
+        def store(flip):
+            out[relative] = jnp.concatenate([parts[i ^ flip] for i in range(shares)], axis=1)
+
+        for flip in range(shares):
+            pl.when(low == flip)(functools.partial(store, flip))
+
+
+def feature_rows(index, summed, even, odd):
     groups = len(summed)
     rows, width = summed[0].shape
     return pl.pallas_call(
@@ -319,7 +335,35 @@
             transcendentals=0,
         ),
         name="feature_rows",
-    )(index, *summed, *halves)
+    )(index, *summed, even, odd)
+
+
+def gather_kernel(index, *refs):
+    *pieces, out, sems = refs
+    rows = pieces[0].shape[0]
+    copies = [
+        pltpu.make_async_copy(
+            piece, out.at[pl.ds(pl.multiple_of((index[1] ^ i) * rows, rows), rows)], sems.at[i]
+        )
+        for i, piece in enumerate(pieces)
+    ]
+    for copy in copies:
+        copy.start()
+    for copy in copies:
+        copy.wait()
+
+
+def laid_out(index, pieces):
+    rows, width = pieces[0].shape
+    return pl.pallas_call(
+        gather_kernel,
+        in_specs=[IN_SMEM] + [IN_VMEM] * len(pieces),
+        out_specs=IN_HBM,
+        out_shape=bf16(len(pieces) * rows, width),
+        scratch_shapes=[pltpu.SemaphoreType.DMA((len(pieces),))],
+        compiler_params=params(),
+        name="laid_out",
+    )(index, *pieces)
 
 
 def landing_blocks(shuffle_from, me, blocks, devs, slots):
@@ -349,7 +393,6 @@
     adj_count,
     shuffle_from,
 ):
-    row_count, width = features.shape
     blocks, tile_slots, tile_rows, _ = adj_vals.shape
     reach = (tile_slots - 1) // 2
     me = lax.axis_index("node")
@@ -357,64 +400,51 @@
     devs = lax.axis_size("node")
     groups = lax.axis_size("chan")
     slots = -(-blocks // devs)
-    quarter = row_count // groups
     index = jnp.stack([me, group])
 
     args = (index, adj_cols.T, adj_count, grad_clean, pre_clean, grad_corrupt, pre_corrupt)
     args += (slopes[None, :], adj_vals)
-    clean, corrupt, down, up = aggregate(*args, reach)
+    clean, corrupt, down, up, *packed = aggregate(*args, features, weight, reach, groups)
     from_prev = shifted(up, "node", 1)
     from_next = shifted(down, "node", -1)
-    tiles = [weight] + [swapped(weight, "chan", i) for i in range(1, groups)]
-
-    feats = [None] * groups
-    by_quarter = features.reshape(groups, quarter, width)
-    for i in [0, *exchange_order(groups)]:
-        piece = lax.dynamic_index_in_dim(by_quarter, group ^ i, 0, keepdims=False)
-        feats[i] = swapped(piece, "chan", i) if i else piece
+    for i in exchange_order(groups):
+        packed[i] = swapped(packed[i], "chan", i)
 
     clean, outgoing = route(
         index, shuffle_from, clean, corrupt, from_prev, from_next, devs, slots
     )
-    shuffle_from, outgoing, tiles = lax.optimization_barrier((shuffle_from, outgoing, tiles))
+    shuffle_from, outgoing = lax.optimization_barrier((shuffle_from, outgoing))
     landing = landing_blocks(shuffle_from, me, blocks, devs, slots)
     incoming = exchanged(outgoing, "node")
-
-    halves = [jnp.stack(part)[None] for part in (tiles[: groups // 2], tiles[groups // 2 :])]
-    orders = halving_orders(devs)
-    for hop in range(len(orders[0])):
-        halves = [
-            jnp.concatenate([part, swapped(part, "node", 1 << order[hop])], axis=0)
-            for part, order in zip(halves, orders)
-        ]
-    incoming, feats, halves = lax.optimization_barrier((incoming, feats, halves))
-
-    merged = merge(index, landing, clean, incoming, groups)
+    merged, tiles = merge(index, landing, clean, incoming, packed)
+
     summed = [merged[0]] + [None] * (groups - 1)
     for i in exchange_order(groups):
         summed[i] = swapped(merged[i], "chan", i)
-    halves = [jnp.concatenate([part, swapped(part, "node", 1)], axis=0) for part in halves]
-    summed, halves = lax.optimization_barrier((summed, halves))
-
-    rows_out = feature_rows(index, summed, halves)
-    grad_features = exchanged(rows_out, "chan").reshape(row_count, width)
-
-    feats, summed, rows_out = lax.optimization_barrier((feats, summed, rows_out))
-    keep, send = weight_partial(index, feats, summed, devs)
-    total = wide(keep) + wide(swapped(send, "node", 1))
-    shares = []
-    for part, order in zip((total[0], total[1]), halving_orders(devs)):
-        for bit in order:
-            size = part.shape[0] // 2
-            arrived = swapped(part[size:].astype(jnp.bfloat16), "node", 1 << bit)
-            part = part[:size] + wide(arrived)
-        shares.append(part[0])
-    shares = jnp.concatenate(shares, axis=0)
-    grad_weight = shares[0]
+    even = [tiles] + [swapped(tiles, "node", 2 * i) for i in range(1, devs // 2)]
+    summed, even = lax.optimization_barrier((summed, even))
+    even = jnp.stack(even)
+    odd = swapped(even, "node", 1)
+
+    keep, send = weight_partial(index, packed, summed, devs)
+    odd, send = lax.optimization_barrier((odd, send))
+    arrived = swapped(send, "node", 1)
+    rows_out = feature_rows(index, summed, even, odd)
+    arrived, rows_out = lax.optimization_barrier((arrived, rows_out))
+    pieces = [rows_out[0]] + [None] * (groups - 1)
+    for i in exchange_order(groups):
+        pieces[i] = swapped(rows_out[i], "chan", i)
+
+    total = wide(keep) + wide(arrived)
+    share = total[0]
+    for i in range(1, devs // 2):
+        share = share + wide(swapped(total[i].astype(jnp.bfloat16), "node", 2 * i))
+    pieces, share = lax.optimization_barrier((pieces, share))
+    grad_weight = share[0]
     for i in range(1, groups):
-        grad_weight = grad_weight + wide(swapped(shares[i].astype(jnp.bfloat16), "chan", i))
-
-    return (grad_weight, grad_features)
+        grad_weight = grad_weight + wide(swapped(share[i].astype(jnp.bfloat16), "chan", i))
+
+    return (grad_weight, laid_out(index, pieces))
 
 
 def solution(mesh):

time: 138 us -> 146 us (1.058)
  Pallas kernels: 18.2 us -> 49.9 us
  waiting for transfers between devices: 57.4 us -> 46.8 us
  other arithmetic: 10 us -> 2.49 us
  starting transfers between devices: 48.2 us -> 42.8 us
    pallas_call x1 -> x2, Pallas kernels: 9.68 us -> 41.4 us  [the longest x1 39.9 us: aggregate(): pl.pallas_call(functools.partial(aggregate_kernel, reach, groups), in_spe...]
    concatenate x6 -> x0, other arithmetic: 5.82 us -> none  [the longest x4 3.55 us: local(): jnp.concatenate([part, swapped(part, 'node', 1 << order[hop])], axis=0)]
    ppermute x23 -> x20, waiting for transfers between devices: 44.6 us -> 38.8 us  [swapped(): return lax.ppermute(value, axis, [(i, i ^ by) for i in range(size)])]
    all_to_all x2 -> x1, waiting for transfers between devices: 12.8 us -> 7.95 us  [exchanged(): return lax.all_to_all(value, axis, split_axis=0, concat_axis=0, tiled=True)]
    all_to_all x2 -> x1, starting transfers between devices: 11.2 us -> 7.67 us  [exchanged(): return lax.all_to_all(value, axis, split_axis=0, concat_axis=0, tiled=True)]
    broadcast_in_dim x2 -> x0, other arithmetic: 1.77 us -> none  [local(): jnp.stack(part)[None]]
    ppermute x23 -> x20, starting transfers between devices: 33.2 us -> 31.5 us  [swapped(): return lax.ppermute(value, axis, [(i, i ^ by) for i in range(size)])]
  transfers between devices with their start and end apart: 27 -> 23, of which waited for: 12 -> 11; matrix products, arithmetic and copies ran while one was open for 7% -> 1% of each run, Pallas kernels for 2% -> 6%
where the time goes in v4:
time: 146 us
  Pallas kernels  49.9 us (34%)
  waiting for transfers between devices  46.8 us (32%)
  starting transfers between devices  42.8 us (29%)
  local copies, waits for them, and re-layouts  2.96 us (2%)
  other arithmetic  2.49 us (2%)
    pallas_call x1, Pallas kernels, aggregate(): pl.pallas_call(functools.partial(aggregate_kernel, reach, groups), in_spe...  39.9 us
    ppermute x20, waiting for transfers between devices, swapped(): return lax.ppermute(value, axis, [(i, i ^ by) for i in range(size)])  38.8 us
    ppermute x20, starting transfers between devices, swapped(): return lax.ppermute(value, axis, [(i, i ^ by) for i in range(size)])  31.5 us
    all_to_all x1, waiting for transfers between devices, exchanged(): return lax.all_to_all(value, axis, split_axis=0, concat_axis=0, tiled=True)  7.95 us
    all_to_all x1, starting transfers between devices, exchanged(): return lax.all_to_all(value, axis, split_axis=0, concat_axis=0, tiled=True)  7.67 us
    ppermute x2, starting transfers between devices, shifted(): return lax.ppermute(value, axis, pairs)  3.66 us
    pallas_call x1, Pallas kernels, feature_rows(): pl.pallas_call(feature_kernel, in_specs=[IN_SMEM] + [IN_VMEM] * (groups +...  3.22 us
  transfers between devices with their start and end apart: 23, of which 11 were waited for; matrix products, arithmetic and copies ran while one was open for 1% of the time, Pallas kernels for 6%

profile of v4, /device:TPU:0, one launch (start us, length us, event | category | flops | bytes accessed | tf_op | source)
XLA Modules:
  0.0 145.8 jit_solution(7995573025374312530)
XLA Ops:
  0.6 0.7 pad_add_fusion.me.index
  1.3 39.9 %aggregate.1 = (bf16[14,128,256]{2,1,0:T(8,128)(2,1)}, bf16[14,128,256]{2,1,0:T(8,128)(2,1)}, bf16[2,2,128,256]{3,2,1,0:T(8,128)(2,1)}, bf16[2,2,128,256]{3,2,1,...) custom-call(s32[2]{0:T(128)} %pad_add_fusion.me.index, ...), custom_call_target="tpu_custom_call" | custom-call | flops 1174405120 | bytes 7798784 | tf_op jit(solution)/shard_map/aggregate/pallas_call | solution.py:153
  41.2 2.4 %collective-permute-start = (bf16[2,2,128,256]{3,2,1,0:T(8,128)(2,1)}, bf16[2,2,128,256]{3,2,1,0:T(8,128)(2,1)S(1)}, u32[]{:S(2)}, u32[]{:S(2)}) collective-permute-start(bf16[2,2,128,256]{3,2,1,0:T(8,128)(2,1)} %get-tuple-element.37), channel_id=1, source_target_pairs={{0,4},{4,8},{8,12},{12,16},{16,20},{20,24},{24,28},{1,5},{5,9},{9,... | collective-permute-start | bytes 786440 | tf_op jit(solution)/shard_map/ppermute | solution.py:33
  43.6 1.3 collective-permute-start.1
  44.9 2.5 %collective-permute-start.2 = (bf16[576,256]{1,0:T(8,128)(2,1)}, bf16[576,256]{1,0:T(8,128)(2,1)S(1)}, u32[]{:S(2)}, u32[]{:S(2)}) collective-permute-start(bf16[576,256]{1,0:T(8,128)(2,1)} %get-tuple-element.44), channel_id=1, source_target_pairs={{0,1},{1,0},{2,3},{3,2},{4,5},{5,4},{6,7},{7,6},{8,9},{9,8},{10,11... | collective-permute-start | bytes 884744 | tf_op jit(solution)/shard_map/ppermute | solution.py:38
  47.4 2.6 %collective-permute-start.3 = (bf16[576,256]{1,0:T(8,128)(2,1)}, bf16[576,256]{1,0:T(8,128)(2,1)S(1)}, u32[]{:S(2)}, u32[]{:S(2)}) collective-permute-start(bf16[576,256]{1,0:T(8,128)(2,1)} %get-tuple-element.45), channel_id=1, source_target_pairs={{0,2},{1,3},{2,0},{3,1},{4,6},{5,7},{6,4},{7,5},{8,10},{9,11},{10,... | collective-permute-start | bytes 884744 | tf_op jit(solution)/shard_map/ppermute | solution.py:38
  49.9 0.0 collective-permute-start.4
  50.0 0.0 collective-permute-done.low
  50.0 0.0 collective-permute-done.1.high
  50.0 0.0 copy-start
  50.0 1.2 copy-done
  51.2 1.2 copy-done.1
  52.3 1.7 %route.1 = (bf16[14,128,256]{2,1,0:T(8,128)(2,1)S(1)}, bf16[16,128,256]{2,1,0:T(8,128)(2,1)}) custom-call(s32[2]{0:T(128)S(1)} %copy-done.3, s32[112]{0:T(128)S(1)} %copy-done.4, bf16[14,128,256]{2,1,0:T(8,128)(2,1)S(1)} %copy-done, bf16[14,128,256]{2,1,0:T(8,128)(2,1)S(1)} %copy-done.1, bf16[2,2,128,256]{3,2,1,0:T(8,128)(2,1)S(1)} %collective-permute-done.low, ...), custom_call_target="tpu_custom_call" | custom-call | tf_op jit(solution)/shard_map/route/pallas_call | solution.py:200
  54.0 7.7 %all-to-all-start = ((bf16[16,128,256]{2,1,0:T(8,128)(2,1)}), bf16[16,128,256]{2,1,0:T(8,128)(2,1)S(1)}, u32[]{:S(2)}, u32[]{:S(2)}) async-start(bf16[16,128,256]{2,1,0:T(8,128)(2,1)} %get-tuple-element.42), calls=%async_computation | async-start | bytes 2097152 | tf_op jit(solution)/shard_map/all_to_all | solution.py:42
  61.7 0.1 eq.30
  61.8 0.1 add.45
  61.9 0.3 convert_reduce_fusion
  62.3 0.1 copy.13
  62.3 0.1 select_reduce_fusion
  62.5 0.1 copy.14
  62.6 0.1 sub.13.landing
  62.7 0.0 collective-permute-done.2.refs_1_
  62.7 0.0 collective-permute-done.3.refs_2_
  62.7 6.5 %collective-permute-done.4.refs_3_ = bf16[576,256]{1,0:T(8,128)(2,1)S(1)} collective-permute-done((bf16[576,256]{1,0:T(8,128)(2,1)}, bf16[576,256]{1,0:T(8,128)(2,1)S(1)}, u32[]{:S(2)}, u32[]{:S(2)}) %collective-permute-start.4) | collective-permute-done | bytes 294944 | tf_op jit(solution)/shard_map/ppermute | solution.py:38
  69.2 7.9 %all-to-all-done.incoming = bf16[16,128,256]{2,1,0:T(8,128)(2,1)S(1)} async-done(((bf16[16,128,256]{2,1,0:T(8,128)(2,1)}), bf16[16,128,256]{2,1,0:T(8,128)(2,1)S(1)}, u32[]{:S(2)}, u32[]{:S(2)}) %all-to-all-start) | async-done | bytes 1048608 | tf_op jit(solution)/shard_map/all_to_all | solution.py:42
  77.1 0.9 merge.1
  78.0 0.1 slice_bitcast_fusion.8
  78.1 3.7 %collective-permute-start.7 = (bf16[448,256]{1,0:T(8,128)(2,1)S(1)}, bf16[448,256]{1,0:T(8,128)(2,1)S(1)}, u32[]{:S(2)}, u32[]{:S(2)}) collective-permute-start(bf16[448,256]{1,0:T(8,128)(2,1)S(1)} %get-tuple-element.77), channel_id=1, source_target_pairs={{0,3},{1,2},{2,1},{3,0},{4,7},{5,6},{6,5},{7,4},{8,11},{9,10},{10,... | collective-permute-start | bytes 688136 | tf_op jit(solution)/shard_map/ppermute | solution.py:38
  81.8 0.6 collective-permute-start.10
  82.4 1.4 collective-permute-start.9
  83.8 1.5 %collective-permute-start.8 = (bf16[4,128,256]{2,1,0:T(8,128)(2,1)S(1)}, bf16[4,128,256]{2,1,0:T(8,128)(2,1)S(1)}, u32[]{:S(2)}, u32[]{:S(2)}) collective-permute-start(bf16[4,128,256]{2,1,0:T(8,128)(2,1)S(1)} %get-tuple-element.49), channel_id=1, source_target_pairs={{0,8},{4,12},{8,0},{12,4},{16,24},{20,28},{24,16},{28,20},{1,9},{5... | collective-permute-start | bytes 786440 | tf_op jit(solution)/shard_map/ppermute | solution.py:38
  85.3 2.1 %collective-permute-done.7.refs_7_.refs_3_ = bf16[448,256]{1,0:T(8,128)(2,1)S(1)} collective-permute-done((bf16[448,256]{1,0:T(8,128)(2,1)S(1)}, bf16[448,256]{1,0:T(8,128)(2,1)S(1)}, u32[]{:S(2)}, u32[]{:S(2)}) %collective-permute-start.7) | collective-permute-done | bytes 229408 | tf_op jit(solution)/shard_map/ppermute | solution.py:38
  87.4 7.9 %collective-permute-start.5 = (bf16[448,256]{1,0:T(8,128)(2,1)S(1)}, bf16[448,256]{1,0:T(8,128)(2,1)S(1)}, u32[]{:S(2)}, u32[]{:S(2)}) collective-permute-start(bf16[448,256]{1,0:T(8,128)(2,1)S(1)} %get-tuple-element.79), channel_id=1, source_target_pairs={{0,1},{1,0},{2,3},{3,2},{4,5},{5,4},{6,7},{7,6},{8,9},{9,8},{10,11... | collective-permute-start | bytes 688136 | tf_op jit(solution)/shard_map/ppermute | solution.py:38
  95.3 4.1 %collective-permute-done.6.refs_6_.refs_2_ = bf16[448,256]{1,0:T(8,128)(2,1)S(1)} collective-permute-done((bf16[448,256]{1,0:T(8,128)(2,1)S(1)}, bf16[448,256]{1,0:T(8,128)(2,1)S(1)}, u32[]{:S(2)}, u32[]{:S(2)}) %collective-permute-start.6) | collective-permute-done | bytes 229408 | tf_op jit(solution)/shard_map/ppermute | solution.py:38
  99.5 4.8 %collective-permute-done.5.refs_5_.refs_1_ = bf16[448,256]{1,0:T(8,128)(2,1)S(1)} collective-permute-done((bf16[448,256]{1,0:T(8,128)(2,1)S(1)}, bf16[448,256]{1,0:T(8,128)(2,1)S(1)}, u32[]{:S(2)}, u32[]{:S(2)}) %collective-permute-start.5) | collective-permute-done | bytes 229408 | tf_op jit(solution)/shard_map/ppermute | solution.py:38
  104.3 0.1 pad_maximum_fusion.refs_4_
  104.4 0.1 collective-permute-start.11
  104.5 2.6 %weight_partial.1 = (bf16[4,4,128,256]{3,2,1,0:T(8,128)(2,1)S(1)}, bf16[4,4,128,256]{3,2,1,0:T(8,128)(2,1)S(1)}) custom-call(s32[2]{0:T(128)S(1)} %copy-done.3, bf16[576,256]{1,0:T(8,128)(2,1)S(1)} %copy-done.2, bf16[576,256]{1,0:T(8,128)(2,1)S(1)} %collective-permute-done.2.refs_1_, bf16[576,256]{1,0:T(8,128)(2,1)S(1)} %collective-permute-done.3.refs_2_, ...), custom_call_target="tpu_custom_call" | custom-call | flops 939524096 | bytes 3932160 | tf_op jit(solution)/shard_map/weight_partial/pallas_call | solution.py:278
  107.1 0.0 collective-permute-done.11.refs_5_
  107.2 0.5 collective-permute-start.12
  107.7 3.2 %feature_rows.1 = bf16[4,448,256]{2,1,0:T(8,128)(2,1)S(1)} custom-call(s32[2]{0:T(128)S(1)} %copy-done.3, bf16[448,256]{1,0:T(8,128)(2,1)S(1)} %get-tuple-element.53.refs_4_.refs_0_, bf16[448,256]{1,0:T(8,128)(2,1)S(1)} %collective-permute-done.5.refs_5_.refs_1_, bf16[448,256]{1,0:T(8,128)(2,1)S(1)} %collective-permute-done.6.refs_6_.refs_2_, ...), custom_call_target="tpu_custom_call" | custom-call | flops 939524096 | bytes 3932160 | tf_op jit(solution)/shard_map/feature_rows/pallas_call | solution.py:326
  110.9 0.0 collective-permute-done.12
  110.9 0.3 fusion.8
  111.3 0.1 slice_bitcast_fusion.3
  111.3 2.5 %collective-permute-start.16 = (bf16[4,128,256]{2,1,0:T(8,128)(2,1)S(1)}, bf16[4,128,256]{2,1,0:T(8,128)(2,1)S(1)}, u32[]{:S(2)}, u32[]{:S(2)}) collective-permute-start(bf16[4,128,256]{2,1,0:T(8,128)(2,1)S(1)} %get-tuple-element.70), channel_id=1, source_target_pairs={{0,8},{4,12},{8,0},{12,4},{16,24},{20,28},{24,16},{28,20},{1,9},{5... | collective-permute-start | bytes 786440 | tf_op jit(solution)/shard_map/ppermute | solution.py:38
  113.9 1.5 %collective-permute-start.17 = (bf16[4,128,256]{2,1,0:T(8,128)(2,1)S(1)}, bf16[4,128,256]{2,1,0:T(8,128)(2,1)S(1)}, u32[]{:S(2)}, u32[]{:S(2)}) collective-permute-start(bf16[4,128,256]{2,1,0:T(8,128)(2,1)S(1)} %get-tuple-element.72), channel_id=1, source_target_pairs={{0,16},{4,20},{8,24},{12,28},{16,0},{20,4},{24,8},{28,12},{1,17},{... | collective-permute-start | bytes 786440 | tf_op jit(solution)/shard_map/ppermute | solution.py:38
  115.4 0.1 slice_bitcast_fusion.4
  115.5 3.1 %collective-permute-start.15 = (bf16[448,256]{1,0:T(8,128)(2,1)S(1)}, bf16[448,256]{1,0:T(8,128)(2,1)S(1)}, u32[]{:S(2)}, u32[]{:S(2)}) collective-permute-start(bf16[448,256]{1,0:T(8,128)(2,1)S(1)} %get-tuple-element.73), channel_id=1, source_target_pairs={{0,3},{1,2},{2,1},{3,0},{4,7},{5,6},{6,5},{7,4},{8,11},{9,10},{10,... | collective-permute-start | bytes 688136 | tf_op jit(solution)/shard_map/ppermute | solution.py:38
  118.6 2.4 %collective-permute-done.16 = bf16[4,128,256]{2,1,0:T(8,128)(2,1)S(1)} collective-permute-done((bf16[4,128,256]{2,1,0:T(8,128)(2,1)S(1)}, bf16[4,128,256]{2,1,0:T(8,128)(2,1)S(1)}, u32[]{:S(2)}, u32[]{:S(2)}) %collective-permute-start.16) | collective-permute-done | bytes 262176 | tf_op jit(solution)/shard_map/ppermute | solution.py:38
  121.0 0.0 collective-permute-start.13
  121.0 4.8 %collective-permute-done.18 = bf16[4,128,256]{2,1,0:T(8,128)(2,1)S(1)} collective-permute-done((bf16[4,128,256]{2,1,0:T(8,128)(2,1)S(1)}, bf16[4,128,256]{2,1,0:T(8,128)(2,1)S(1)}, u32[]{:S(2)}, u32[]{:S(2)}) %collective-permute-start.18) | collective-permute-done | bytes 262176 | tf_op jit(solution)/shard_map/ppermute | solution.py:38
  125.8 1.7 %collective-permute-done.17 = bf16[4,128,256]{2,1,0:T(8,128)(2,1)S(1)} collective-permute-done((bf16[4,128,256]{2,1,0:T(8,128)(2,1)S(1)}, bf16[4,128,256]{2,1,0:T(8,128)(2,1)S(1)}, u32[]{:S(2)}, u32[]{:S(2)}) %collective-permute-start.17) | collective-permute-done | bytes 262176 | tf_op jit(solution)/shard_map/ppermute | solution.py:38
  127.5 0.1 fusion.2
  127.6 0.0 collective-permute-done.15.refs_3_
  127.6 8.8 %collective-permute-done.14.refs_2_ = bf16[448,256]{1,0:T(8,128)(2,1)S(1)} collective-permute-done((bf16[448,256]{1,0:T(8,128)(2,1)S(1)}, bf16[448,256]{1,0:T(8,128)(2,1)S(1)}, u32[]{:S(2)}, u32[]{:S(2)}) %collective-permute-start.14) | collective-permute-done | bytes 229408 | tf_op jit(solution)/shard_map/ppermute | solution.py:38
  136.4 0.0 collective-permute-done.13.refs_1_
  136.4 0.1 collective-permute-start.19
  136.5 2.7 %collective-permute-start.21 = (bf16[128,256]{1,0:T(8,128)(2,1)S(1)}, bf16[128,256]{1,0:T(8,128)(2,1)S(1)}, u32[]{:S(2)}, u32[]{:S(2)}) collective-permute-start(bf16[128,256]{1,0:T(8,128)(2,1)S(1)} %get-tuple-element.82), channel_id=1, source_target_pairs={{0,3},{1,2},{2,1},{3,0},{4,7},{5,6},{6,5},{7,4},{8,11},{9,10},{10,... | collective-permute-start | bytes 196616 | tf_op jit(solution)/shard_map/ppermute | solution.py:38
  139.2 0.8 collective-permute-start.20
  140.0 1.5 %laid_out.1 = bf16[1792,256]{1,0:T(8,128)(2,1)} custom-call(s32[2]{0:T(128)S(1)} %copy-done.3, bf16[448,256]{1,0:T(8,128)(2,1)S(1)} %get-tuple-element.64.refs_0_, bf16[448,256]{1,0:T(8,128)(2,1)S(1)} %collective-permute-done.13.refs_1_, bf16[448,256]{1,0:T(8,128)(2,1)S(1)} %collective-permute-done.14.refs_2_, ...), custom_call_target="tpu_custom_call" | custom-call | tf_op jit(solution)/shard_map/laid_out/pallas_call | solution.py:358
  141.5 0.0 collective-permute-done.19
  141.5 1.4 collective-permute-done.21
  142.9 2.2 %collective-permute-done.20 = bf16[128,256]{1,0:T(8,128)(2,1)S(1)} collective-permute-done((bf16[128,256]{1,0:T(8,128)(2,1)S(1)}, bf16[128,256]{1,0:T(8,128)(2,1)S(1)}, u32[]{:S(2)}, u32[]{:S(2)}) %collective-permute-start.20) | collective-permute-done | bytes 65568 | tf_op jit(solution)/shard_map/ppermute | solution.py:38
  145.1 0.7 fusion.4
  (19 shorter events, 0.1 us)
Async XLA Ops:
  1.3 48.7 %copy-start.3 = (s32[2]{0:T(128)S(1)}, s32[2]{0:T(128)}, u32[]{:S(2)}) copy-start(s32[2]{0:T(128)} %pad_add_fusion.me.index) | copy-start | bytes 28
  1.3 48.7 %copy-start.4 = (s32[112]{0:T(128)S(1)}, s32[112]{0:T(128)}, u32[]{:S(2)}) copy-start(s32[112]{0:T(128)} %shuffle.1) | copy-start | bytes 1348
  41.2 8.7 %collective-permute-start = (bf16[2,2,128,256]{3,2,1,0:T(8,128)(2,1)}, bf16[2,2,128,256]{3,2,1,0:T(8,128)(2,1)S(1)}, u32[]{:S(2)}, u32[]{:S(2)}) collective-permute-start(bf16[2,2,128,256]{3,2,1,0:T(8,128)(2,1)} %get-tuple-element.37), channel_id=1, source_target_pairs={{0,4},{4,8},{8,12},{12,16},{16,20},{20,24},{24,28},{1,5},{5,9},{9,... | collective-permute-start | bytes 786440 | tf_op jit(solution)/shard_map/ppermute | solution.py:33
  43.6 6.4 %collective-permute-start.1 = (bf16[2,2,128,256]{3,2,1,0:T(8,128)(2,1)}, bf16[2,2,128,256]{3,2,1,0:T(8,128)(2,1)S(1)}, u32[]{:S(2)}, u32[]{:S(2)}) collective-permute-start(bf16[2,2,128,256]{3,2,1,0:T(8,128)(2,1)} %get-tuple-element.38), channel_id=1, source_target_pairs={{4,0},{8,4},{12,8},{16,12},{20,16},{24,20},{28,24},{5,1},{9,5},{13... | collective-permute-start | bytes 786440 | tf_op jit(solution)/shard_map/ppermute | solution.py:33
  44.9 17.8 %collective-permute-start.2 = (bf16[576,256]{1,0:T(8,128)(2,1)}, bf16[576,256]{1,0:T(8,128)(2,1)S(1)}, u32[]{:S(2)}, u32[]{:S(2)}) collective-permute-start(bf16[576,256]{1,0:T(8,128)(2,1)} %get-tuple-element.44), channel_id=1, source_target_pairs={{0,1},{1,0},{2,3},{3,2},{4,5},{5,4},{6,7},{7,6},{8,9},{9,8},{10,11... | collective-permute-start | bytes 884744 | tf_op jit(solution)/shard_map/ppermute | solution.py:38
  47.4 15.3 %collective-permute-start.3 = (bf16[576,256]{1,0:T(8,128)(2,1)}, bf16[576,256]{1,0:T(8,128)(2,1)S(1)}, u32[]{:S(2)}, u32[]{:S(2)}) collective-permute-start(bf16[576,256]{1,0:T(8,128)(2,1)} %get-tuple-element.45), channel_id=1, source_target_pairs={{0,2},{1,3},{2,0},{3,1},{4,6},{5,7},{6,4},{7,5},{8,10},{9,11},{10,... | collective-permute-start | bytes 884744 | tf_op jit(solution)/shard_map/ppermute | solution.py:38
  49.9 19.2 %collective-permute-start.4 = (bf16[576,256]{1,0:T(8,128)(2,1)}, bf16[576,256]{1,0:T(8,128)(2,1)S(1)}, u32[]{:S(2)}, u32[]{:S(2)}) collective-permute-start(bf16[576,256]{1,0:T(8,128)(2,1)} %get-tuple-element.46), channel_id=1, source_target_pairs={{0,3},{1,2},{2,1},{3,0},{4,7},{5,6},{6,5},{7,4},{8,11},{9,10},{10,... | collective-permute-start | bytes 884744 | tf_op jit(solution)/shard_map/ppermute | solution.py:38
  50.0 1.2 copy-start
  51.2 1.2 copy-start.1
  52.3 24.8 %copy-start.2 = (bf16[576,256]{1,0:T(8,128)(2,1)S(1)}, bf16[576,256]{1,0:T(8,128)(2,1)}, u32[]{:S(2)}) copy-start(bf16[576,256]{1,0:T(8,128)(2,1)} %get-tuple-element.43.refs_0_) | copy-start | bytes 884740
  54.0 23.1 %all-to-all-start = ((bf16[16,128,256]{2,1,0:T(8,128)(2,1)}), bf16[16,128,256]{2,1,0:T(8,128)(2,1)S(1)}, u32[]{:S(2)}, u32[]{:S(2)}) async-start(bf16[16,128,256]{2,1,0:T(8,128)(2,1)} %get-tuple-element.42), calls=%async_computation | async-start | bytes 2097152 | tf_op jit(solution)/shard_map/all_to_all | solution.py:42
  78.1 9.3 %collective-permute-start.7 = (bf16[448,256]{1,0:T(8,128)(2,1)S(1)}, bf16[448,256]{1,0:T(8,128)(2,1)S(1)}, u32[]{:S(2)}, u32[]{:S(2)}) collective-permute-start(bf16[448,256]{1,0:T(8,128)(2,1)S(1)} %get-tuple-element.77), channel_id=1, source_target_pairs={{0,3},{1,2},{2,1},{3,0},{4,7},{5,6},{6,5},{7,4},{8,11},{9,10},{10,... | collective-permute-start | bytes 688136 | tf_op jit(solution)/shard_map/ppermute | solution.py:38
  81.8 22.5 %collective-permute-start.10 = (bf16[4,128,256]{2,1,0:T(8,128)(2,1)S(1)}, bf16[4,128,256]{2,1,0:T(8,128)(2,1)S(1)}, u32[]{:S(2)}, u32[]{:S(2)}) collective-permute-start(bf16[4,128,256]{2,1,0:T(8,128)(2,1)S(1)} %get-tuple-element.49), channel_id=1, source_target_pairs={{0,24},{4,28},{8,16},{12,20},{16,8},{20,12},{24,0},{28,4},{1,25},{... | collective-permute-start | bytes 786440 | tf_op jit(solution)/shard_map/ppermute | solution.py:38
  82.4 21.9 %collective-permute-start.9 = (bf16[4,128,256]{2,1,0:T(8,128)(2,1)S(1)}, bf16[4,128,256]{2,1,0:T(8,128)(2,1)S(1)}, u32[]{:S(2)}, u32[]{:S(2)}) collective-permute-start(bf16[4,128,256]{2,1,0:T(8,128)(2,1)S(1)} %get-tuple-element.49), channel_id=1, source_target_pairs={{0,16},{4,20},{8,24},{12,28},{16,0},{20,4},{24,8},{28,12},{1,17},{... | collective-permute-start | bytes 786440 | tf_op jit(solution)/shard_map/ppermute | solution.py:38
  83.8 20.5 %collective-permute-start.8 = (bf16[4,128,256]{2,1,0:T(8,128)(2,1)S(1)}, bf16[4,128,256]{2,1,0:T(8,128)(2,1)S(1)}, u32[]{:S(2)}, u32[]{:S(2)}) collective-permute-start(bf16[4,128,256]{2,1,0:T(8,128)(2,1)S(1)} %get-tuple-element.49), channel_id=1, source_target_pairs={{0,8},{4,12},{8,0},{12,4},{16,24},{20,28},{24,16},{28,20},{1,9},{5... | collective-permute-start | bytes 786440 | tf_op jit(solution)/shard_map/ppermute | solution.py:38
  85.3 14.2 %collective-permute-start.6 = (bf16[448,256]{1,0:T(8,128)(2,1)S(1)}, bf16[448,256]{1,0:T(8,128)(2,1)S(1)}, u32[]{:S(2)}, u32[]{:S(2)}) collective-permute-start(bf16[448,256]{1,0:T(8,128)(2,1)S(1)} %get-tuple-element.78), channel_id=1, source_target_pairs={{0,2},{1,3},{2,0},{3,1},{4,6},{5,7},{6,4},{7,5},{8,10},{9,11},{10,... | collective-permute-start | bytes 688136 | tf_op jit(solution)/shard_map/ppermute | solution.py:38
  87.4 16.9 %collective-permute-start.5 = (bf16[448,256]{1,0:T(8,128)(2,1)S(1)}, bf16[448,256]{1,0:T(8,128)(2,1)S(1)}, u32[]{:S(2)}, u32[]{:S(2)}) collective-permute-start(bf16[448,256]{1,0:T(8,128)(2,1)S(1)} %get-tuple-element.79), channel_id=1, source_target_pairs={{0,1},{1,0},{2,3},{3,2},{4,5},{5,4},{6,7},{7,6},{8,9},{9,8},{10,11... | collective-permute-start | bytes 688136 | tf_op jit(solution)/shard_map/ppermute | solution.py:38
  104.4 2.7 %collective-permute-start.11 = (bf16[4,4,128,256]{3,2,1,0:T(8,128)(2,1)S(1)}, bf16[4,4,128,256]{3,2,1,0:T(8,128)(2,1)S(1)}, u32[]{:S(2)}, u32[]{:S(2)}) collective-permute-start(bf16[4,4,128,256]{3,2,1,0:T(8,128)(2,1)S(1)} %pad_maximum_fusion.refs_4_), channel_id=1, source_target_pairs={{0,4},{4,0},{8,12},{12,8},{16,20},{20,16},{24,28},{28,24},{1,5},{5... | collective-permute-start | bytes 3145736 | tf_op jit(solution)/shard_map/ppermute | solution.py:38
  107.2 3.8 %collective-permute-start.12 = (bf16[4,4,128,256]{3,2,1,0:T(8,128)(2,1)S(1)}, bf16[4,4,128,256]{3,2,1,0:T(8,128)(2,1)S(1)}, u32[]{:S(2)}, u32[]{:S(2)}) collective-permute-start(bf16[4,4,128,256]{3,2,1,0:T(8,128)(2,1)S(1)} %get-tuple-element.58), channel_id=1, source_target_pairs={{0,4},{4,0},{8,12},{12,8},{16,20},{20,16},{24,28},{28,24},{1,5},{5... | collective-permute-start | bytes 3145736 | tf_op jit(solution)/shard_map/ppermute | solution.py:38
  111.3 9.6 %collective-permute-start.16 = (bf16[4,128,256]{2,1,0:T(8,128)(2,1)S(1)}, bf16[4,128,256]{2,1,0:T(8,128)(2,1)S(1)}, u32[]{:S(2)}, u32[]{:S(2)}) collective-permute-start(bf16[4,128,256]{2,1,0:T(8,128)(2,1)S(1)} %get-tuple-element.70), channel_id=1, source_target_pairs={{0,8},{4,12},{8,0},{12,4},{16,24},{20,28},{24,16},{28,20},{1,9},{5... | collective-permute-start | bytes 786440 | tf_op jit(solution)/shard_map/ppermute | solution.py:38
  113.9 11.9 %collective-permute-start.18 = (bf16[4,128,256]{2,1,0:T(8,128)(2,1)S(1)}, bf16[4,128,256]{2,1,0:T(8,128)(2,1)S(1)}, u32[]{:S(2)}, u32[]{:S(2)}) collective-permute-start(bf16[4,128,256]{2,1,0:T(8,128)(2,1)S(1)} %get-tuple-element.71), channel_id=1, source_target_pairs={{0,24},{4,28},{8,16},{12,20},{16,8},{20,12},{24,0},{28,4},{1,25},{... | collective-permute-start | bytes 786440 | tf_op jit(solution)/shard_map/ppermute | solution.py:38
  113.9 13.6 %collective-permute-start.17 = (bf16[4,128,256]{2,1,0:T(8,128)(2,1)S(1)}, bf16[4,128,256]{2,1,0:T(8,128)(2,1)S(1)}, u32[]{:S(2)}, u32[]{:S(2)}) collective-permute-start(bf16[4,128,256]{2,1,0:T(8,128)(2,1)S(1)} %get-tuple-element.72), channel_id=1, source_target_pairs={{0,16},{4,20},{8,24},{12,28},{16,0},{20,4},{24,8},{28,12},{1,17},{... | collective-permute-start | bytes 786440 | tf_op jit(solution)/shard_map/ppermute | solution.py:38
  115.5 12.1 %collective-permute-start.15 = (bf16[448,256]{1,0:T(8,128)(2,1)S(1)}, bf16[448,256]{1,0:T(8,128)(2,1)S(1)}, u32[]{:S(2)}, u32[]{:S(2)}) collective-permute-start(bf16[448,256]{1,0:T(8,128)(2,1)S(1)} %get-tuple-element.73), channel_id=1, source_target_pairs={{0,3},{1,2},{2,1},{3,0},{4,7},{5,6},{6,5},{7,4},{8,11},{9,10},{10,... | collective-permute-start | bytes 688136 | tf_op jit(solution)/shard_map/ppermute | solution.py:38
  118.6 17.8 %collective-permute-start.14 = (bf16[448,256]{1,0:T(8,128)(2,1)S(1)}, bf16[448,256]{1,0:T(8,128)(2,1)S(1)}, u32[]{:S(2)}, u32[]{:S(2)}) collective-permute-start(bf16[448,256]{1,0:T(8,128)(2,1)S(1)} %get-tuple-element.74), channel_id=1, source_target_pairs={{0,2},{1,3},{2,0},{3,1},{4,6},{5,7},{6,4},{7,5},{8,10},{9,11},{10,... | collective-permute-start | bytes 688136 | tf_op jit(solution)/shard_map/ppermute | solution.py:38
  121.0 15.4 %collective-permute-start.13 = (bf16[448,256]{1,0:T(8,128)(2,1)S(1)}, bf16[448,256]{1,0:T(8,128)(2,1)S(1)}, u32[]{:S(2)}, u32[]{:S(2)}) collective-permute-start(bf16[448,256]{1,0:T(8,128)(2,1)S(1)} %get-tuple-element.75), channel_id=1, source_target_pairs={{0,1},{1,0},{2,3},{3,2},{4,5},{5,4},{6,7},{7,6},{8,9},{9,8},{10,11... | collective-permute-start | bytes 688136 | tf_op jit(solution)/shard_map/ppermute | solution.py:38
  136.4 5.1 %collective-permute-start.19 = (bf16[128,256]{1,0:T(8,128)(2,1)S(1)}, bf16[128,256]{1,0:T(8,128)(2,1)S(1)}, u32[]{:S(2)}, u32[]{:S(2)}) collective-permute-start(bf16[128,256]{1,0:T(8,128)(2,1)S(1)} %get-tuple-element.81), channel_id=1, source_target_pairs={{0,1},{1,0},{2,3},{3,2},{4,5},{5,4},{6,7},{7,6},{8,9},{9,8},{10,11... | collective-permute-start | bytes 196616 | tf_op jit(solution)/shard_map/ppermute | solution.py:38
  136.5 6.4 %collective-permute-start.21 = (bf16[128,256]{1,0:T(8,128)(2,1)S(1)}, bf16[128,256]{1,0:T(8,128)(2,1)S(1)}, u32[]{:S(2)}, u32[]{:S(2)}) collective-permute-start(bf16[128,256]{1,0:T(8,128)(2,1)S(1)} %get-tuple-element.82), channel_id=1, source_target_pairs={{0,3},{1,2},{2,1},{3,0},{4,7},{5,6},{6,5},{7,4},{8,11},{9,10},{10,... | collective-permute-start | bytes 196616 | tf_op jit(solution)/shard_map/ppermute | solution.py:38
  139.2 5.9 %collective-permute-start.20 = (bf16[128,256]{1,0:T(8,128)(2,1)S(1)}, bf16[128,256]{1,0:T(8,128)(2,1)S(1)}, u32[]{:S(2)}, u32[]{:S(2)}) collective-permute-start(bf16[128,256]{1,0:T(8,128)(2,1)S(1)} %get-tuple-element.83), channel_id=1, source_target_pairs={{0,2},{1,3},{2,0},{3,1},{4,6},{5,7},{6,4},{7,5},{8,10},{9,11},{10,... | collective-permute-start | bytes 196616 | tf_op jit(solution)/shard_map/ppermute | solution.py:38

commit v5 on v4

--- a/solution.py
+++ b/solution.py
@@ -46,11 +46,21 @@
     return (wide(grad) * jnp.where(wide(pre) > 0, 1.0, slope)).astype(jnp.bfloat16)
 
 
+def find_places(index, shuffle, blocks, slots, places, used):
+    for i in range(used.shape[0]):
+        used[i] = 0
+    for block in range(blocks):
+        owner = shuffle[index[0] * blocks + block] // blocks
+        slot = used[owner]
+        used[owner] = slot + 1
+        places[block] = owner * slots + slot
+
+
 def aggregate_kernel(
-    reach, groups, me, cols, count, gc, pc, gx, px, slopes, adj, features, weight, *refs
+    reach, groups, send_slots, me, shuffle, cols, count, gc, pc, gx, px, slopes, adj, features, weight, *refs
 ):
-    clean, corrupt, down, up, *refs = refs
-    packed, (data, tiles, rhs, stage, sems, pack_sems) = refs[:groups], refs[groups:]
+    clean, outgoing, down, up, *refs = refs
+    packed, (data, tiles, rhs, stage, places, used, sems, pack_sems) = refs[:groups], refs[groups:]
     blocks, slots, rows, _ = adj.shape
     width = gc.shape[1]
     quarter = features.shape[0] // groups
@@ -104,7 +114,8 @@
             part = turned[:, k * rows : (k + 1) * rows]
             stage[place, distance] = (wide(stage[place, distance]) + part).astype(jnp.bfloat16)
 
-    per_step = 2 - blocks % 2
+    find_places(me, shuffle, blocks, send_slots, places, used)
+    per_step = blocks // 2
 
     @pl.loop(0, blocks // per_step)
     def _(step):
@@ -136,25 +147,26 @@
         down[0, i : i + 2], down[1, i : i + 2] = pair(i)
         up[0, i : i + 2], up[1, i : i + 2] = pair(blocks + reach + i)
 
-    @pl.loop(0, blocks // 2)
-    def _(step):
-        span = pl.ds(2 * step, 2)
-        clean[span], corrupt[span] = pair(reach + 2 * step)
+    for first in range(0, blocks, 2):
+        clean[first : first + 2], sent = pair(reach + first)
+        for i in range(2):
+            outgoing[places[first + i]] = sent[i]
 
     for copy in packs:
         copy.wait()
 
 
-def aggregate(me, cols, count, gc, pc, gx, px, slopes, adj, features, weight, reach, groups):
+def aggregate(index, shuffle, cols, count, gc, pc, gx, px, slopes, adj, features, weight, reach, devs, groups):
     blocks, slots, rows, _ = adj.shape
     width = gc.shape[1]
+    send_slots = -(-blocks // devs)
     assert reach % 2 == 0 and blocks % 2 == 0
     packed = features.shape[0] // groups + weight.shape[0]
     return pl.pallas_call(
-        functools.partial(aggregate_kernel, reach, groups),
-        in_specs=[IN_SMEM] * 3 + [IN_HBM] * 4 + [IN_VMEM] + [IN_HBM] * 3,
-        out_specs=[IN_VMEM] * 4 + [IN_HBM] * groups,
-        out_shape=[bf16(blocks, rows, width)] * 2
+        functools.partial(aggregate_kernel, reach, groups, send_slots),
+        in_specs=[IN_SMEM] * 4 + [IN_HBM] * 4 + [IN_VMEM] + [IN_HBM] * 3,
+        out_specs=[IN_VMEM] * (4 + groups),
+        out_shape=[bf16(blocks, rows, width), bf16(devs * send_slots, rows, width)]
         + [bf16(2, reach, rows, width)] * 2
         + [bf16(packed, width)] * groups,
         scratch_shapes=[
@@ -162,6 +174,8 @@
             pltpu.VMEM((blocks, slots, rows, rows), jnp.bfloat16),
             pltpu.VMEM(((blocks + 4 * reach) * rows, 2 * width), jnp.bfloat16),
             pltpu.VMEM((blocks + 2 * reach + 1, 2 * reach + 1, rows, rows), jnp.bfloat16),
+            pltpu.SMEM((blocks,), jnp.int32),
+            pltpu.SMEM((devs,), jnp.int32),
             pltpu.SemaphoreType.DMA((5, blocks)),
             pltpu.SemaphoreType.DMA((2, groups)),
         ],
@@ -172,46 +186,59 @@
             transcendentals=0,
         ),
         name="aggregate",
-    )(me, cols, count, gc, pc, gx, px, slopes, adj, features, weight)
-
-
-def route_kernel(reach, slots, me, shuffle, clean, corrupt, low, high, whole, outgoing, used):
+    )(index, shuffle, cols, count, gc, pc, gx, px, slopes, adj, features, weight)
+
+
+def patch_kernel(reach, slots, index, shuffle, clean, outgoing, low, high, clean_out, outgoing_out, *scratch):
+    held, ready, places, used, sems = scratch
     blocks = clean.shape[0]
-    for i in range(outgoing.shape[0] // slots):
-        used[i] = 0
-    for block in range(blocks):
-        owner = shuffle[me[0] * blocks + block] // blocks
-        slot = used[owner]
-        used[owner] = slot + 1
-        mine, theirs = clean[block], corrupt[block]
-        if block < reach:
-            mine = (wide(mine) + wide(low[0, block])).astype(jnp.bfloat16)
-            theirs = (wide(theirs) + wide(low[1, block])).astype(jnp.bfloat16)
-        elif block >= blocks - reach:
-            at = block - (blocks - reach)
-            mine = (wide(mine) + wide(high[0, at])).astype(jnp.bfloat16)
-            theirs = (wide(theirs) + wide(high[1, at])).astype(jnp.bfloat16)
-        whole[block] = mine
-        outgoing[owner * slots + slot] = theirs
-
-
-def route(me, shuffle, clean, corrupt, low, high, devs, slots):
+    find_places(index, shuffle, blocks, slots, places, used)
+    border = [*range(reach), *range(blocks - reach, blocks)]
+
+    def spots(i, first, second):
+        return (first.at[border[i]], second.at[places[border[i]]])
+
+    reads, writes = [], []
+    for i in range(2 * reach):
+        for which in range(2):
+            source = spots(i, clean, outgoing)[which]
+            reads.append(pltpu.make_async_copy(source, held.at[which, i], sems.at[0, which, i]))
+            target = spots(i, clean_out, outgoing_out)[which]
+            writes.append(pltpu.make_async_copy(ready.at[which, i], target, sems.at[1, which, i]))
+    for copy in reads:
+        copy.start()
+    for i in range(2 * reach):
+        for which in range(2):
+            reads[2 * i + which].wait()
+            other = low[which, i] if i < reach else high[which, i - reach]
+            ready[which, i] = (wide(held[which, i]) + wide(other)).astype(jnp.bfloat16)
+            writes[2 * i + which].start()
+    for copy in writes:
+        copy.wait()
+
+
+def patch(index, shuffle, clean, outgoing, low, high, slots):
     blocks, rows, width = clean.shape
+    reach = low.shape[1]
     return pl.pallas_call(
-        functools.partial(route_kernel, low.shape[1], slots),
-        in_specs=[IN_SMEM] * 2 + [IN_VMEM] * 4,
-        out_specs=[IN_VMEM] * 2,
-        out_shape=[bf16(blocks, rows, width), bf16(devs * slots, rows, width)],
-        scratch_shapes=[pltpu.SMEM((devs,), jnp.int32)],
-        compiler_params=params(),
-        name="route",
-    )(me, shuffle, clean, corrupt, low, high)
-
-
-def merge_kernel(quarter, index, landing, clean, incoming, *refs):
-    *packed, out, tiles = refs
-    for i, piece in enumerate(packed):
-        tiles[i] = piece[quarter:]
+        functools.partial(patch_kernel, reach, slots),
+        in_specs=[IN_SMEM] * 2 + [IN_HBM] * 2 + [IN_VMEM] * 2,
+        out_specs=[IN_HBM] * 2,
+        out_shape=[bf16(*clean.shape), bf16(*outgoing.shape)],
+        input_output_aliases={2: 0, 3: 1},
+        scratch_shapes=[
+            pltpu.VMEM((2, 2 * reach, rows, width), jnp.bfloat16),
+            pltpu.VMEM((2, 2 * reach, rows, width), jnp.bfloat16),
+            pltpu.SMEM((blocks,), jnp.int32),
+            pltpu.SMEM((outgoing.shape[0] // slots,), jnp.int32),
+            pltpu.SemaphoreType.DMA((2, 2, 2 * reach)),
+        ],
+        compiler_params=params(VMEM_ALL),
+        name="patch",
+    )(index, shuffle, clean, outgoing, low, high)
+
+
+def merge_kernel(quarter, index, landing, clean, incoming, out):
     _, rows, _ = clean.shape
     group = index[1]
     piece = math.gcd(rows, quarter)
@@ -230,19 +257,17 @@
                 ]
 
 
-def merge(index, landing, clean, incoming, packed):
+def merge(index, landing, clean, incoming, groups):
     blocks, rows, width = clean.shape
-    groups = len(packed)
     quarter = blocks * rows // groups
-    height = packed[0].shape[0] - quarter
     return pl.pallas_call(
         functools.partial(merge_kernel, quarter),
-        in_specs=[IN_SMEM] * 2 + [IN_VMEM] * (2 + groups),
-        out_specs=[IN_VMEM] * 2,
-        out_shape=[bf16(groups, quarter, width), bf16(groups, height, width)],
+        in_specs=[IN_SMEM] * 2 + [IN_VMEM] * 2,
+        out_specs=IN_VMEM,
+        out_shape=bf16(groups, quarter, width),
         compiler_params=params(),
         name="merge",
-    )(index, landing, clean, incoming, *packed)
+    )(index, landing, clean, incoming)
 
 
 def weight_kernel(devs, index, *refs):
@@ -339,31 +364,37 @@
 
 
 def gather_kernel(index, *refs):
-    *pieces, out, sems = refs
-    rows = pieces[0].shape[0]
-    copies = [
-        pltpu.make_async_copy(
-            piece, out.at[pl.ds(pl.multiple_of((index[1] ^ i) * rows, rows), rows)], sems.at[i]
-        )
-        for i, piece in enumerate(pieces)
-    ]
+    *parts, out, sems = refs
+    groups = len(parts) // 2
+    sizes = [parts[0].shape[0], out.shape[0] // groups - parts[0].shape[0]]
+    copies = []
+    for i in range(groups):
+        for which, size in enumerate(sizes):
+            start = (index[1] ^ i) * sum(sizes) + which * sizes[0]
+            copies.append(
+                pltpu.make_async_copy(
+                    parts[which * groups + i].at[:size],
+                    out.at[pl.ds(pl.multiple_of(start, 16), size)],
+                    sems.at[which, i],
+                )
+            )
     for copy in copies:
         copy.start()
     for copy in copies:
         copy.wait()
 
 
-def laid_out(index, pieces):
-    rows, width = pieces[0].shape
+def laid_out(index, heads, tails, rows):
+    groups = len(heads)
     return pl.pallas_call(
         gather_kernel,
-        in_specs=[IN_SMEM] + [IN_VMEM] * len(pieces),
+        in_specs=[IN_SMEM] + [IN_VMEM] * (2 * groups),
         out_specs=IN_HBM,
-        out_shape=bf16(len(pieces) * rows, width),
-        scratch_shapes=[pltpu.SemaphoreType.DMA((len(pieces),))],
+        out_shape=bf16(rows, heads[0].shape[1]),
+        scratch_shapes=[pltpu.SemaphoreType.DMA((2, groups))],
         compiler_params=params(),
         name="laid_out",
-    )(index, *pieces)
+    )(index, *heads, *tails)
 
 
 def landing_blocks(shuffle_from, me, blocks, devs, slots):
@@ -393,7 +424,8 @@
     adj_count,
     shuffle_from,
 ):
-    blocks, tile_slots, tile_rows, _ = adj_vals.shape
+    row_count = features.shape[0]
+    blocks, tile_slots, _, _ = adj_vals.shape
     reach = (tile_slots - 1) // 2
     me = lax.axis_index("node")
     group = lax.axis_index("chan")
@@ -402,28 +434,29 @@
     slots = -(-blocks // devs)
     index = jnp.stack([me, group])
 
-    args = (index, adj_cols.T, adj_count, grad_clean, pre_clean, grad_corrupt, pre_corrupt)
-    args += (slopes[None, :], adj_vals)
-    clean, corrupt, down, up, *packed = aggregate(*args, features, weight, reach, groups)
+    args = (index, shuffle_from, adj_cols.T, adj_count)
+    args += (grad_clean, pre_clean, grad_corrupt, pre_corrupt, slopes[None, :], adj_vals)
+    clean, outgoing, down, up, *packed = aggregate(*args, features, weight, reach, devs, groups)
     from_prev = shifted(up, "node", 1)
     from_next = shifted(down, "node", -1)
     for i in exchange_order(groups):
         packed[i] = swapped(packed[i], "chan", i)
 
-    clean, outgoing = route(
-        index, shuffle_from, clean, corrupt, from_prev, from_next, devs, slots
-    )
+    clean, outgoing = patch(index, shuffle_from, clean, outgoing, from_prev, from_next, slots)
     shuffle_from, outgoing = lax.optimization_barrier((shuffle_from, outgoing))
     landing = landing_blocks(shuffle_from, me, blocks, devs, slots)
     incoming = exchanged(outgoing, "node")
-    merged, tiles = merge(index, landing, clean, incoming, packed)
-
+    incoming, packed = lax.optimization_barrier((incoming, packed))
+    merged = merge(index, landing, clean, incoming, groups)
+
+    quarter = row_count // groups
     summed = [merged[0]] + [None] * (groups - 1)
     for i in exchange_order(groups):
         summed[i] = swapped(merged[i], "chan", i)
-    even = [tiles] + [swapped(tiles, "node", 2 * i) for i in range(1, devs // 2)]
+    even = jnp.stack([piece[quarter:] for piece in packed])[None]
+    for bit in range(1, devs.bit_length() - 1):
+        even = jnp.concatenate([even, swapped(even, "node", 1 << bit)], axis=0)
     summed, even = lax.optimization_barrier((summed, even))
-    even = jnp.stack(even)
     odd = swapped(even, "node", 1)
 
     keep, send = weight_partial(index, packed, summed, devs)
@@ -431,20 +464,25 @@
     arrived = swapped(send, "node", 1)
     rows_out = feature_rows(index, summed, even, odd)
     arrived, rows_out = lax.optimization_barrier((arrived, rows_out))
-    pieces = [rows_out[0]] + [None] * (groups - 1)
+
+    cut = quarter - quarter // 64 * 16
+    heads = [rows_out[0]] + [None] * (groups - 1)
     for i in exchange_order(groups):
-        pieces[i] = swapped(rows_out[i], "chan", i)
-
+        heads[i] = swapped(rows_out[i, :cut], "chan", i)
     total = wide(keep) + wide(arrived)
     share = total[0]
     for i in range(1, devs // 2):
         share = share + wide(swapped(total[i].astype(jnp.bfloat16), "node", 2 * i))
-    pieces, share = lax.optimization_barrier((pieces, share))
+    heads, share = lax.optimization_barrier((heads, share))
     grad_weight = share[0]
-    for i in range(1, groups):
-        grad_weight = grad_weight + wide(swapped(share[i].astype(jnp.bfloat16), "chan", i))
-
-    return (grad_weight, laid_out(index, pieces))
+    tails = [rows_out[0, cut:]] + [None] * (groups - 1)
+    for i in exchange_order(groups):
+        tail = jnp.concatenate([rows_out[i, cut:], share[i].astype(jnp.bfloat16)], axis=0)
+        tails[i] = swapped(tail, "chan", i)
+        grad_weight = grad_weight + wide(tails[i][quarter - cut :])
+
+    heads[0] = rows_out[0, :cut]
+    return (grad_weight, laid_out(index, heads, tails, row_count))
 
 
 def solution(mesh):

time: 146 us -> 131 us (0.90)
  Pallas kernels: 49.9 us -> 20.6 us
  waiting for transfers between devices: 46.8 us -> 62.5 us
  starting transfers between devices: 42.8 us -> 38.6 us
  other arithmetic: 2.49 us -> 6.28 us
  local copies, waits for them, and re-layouts: 2.96 us -> 1.34 us
    pallas_call x3, Pallas kernels: 43.1 us -> 13.8 us  [the longest x1 9.32 us: aggregate(): pl.pallas_call(functools.partial(aggregate_kernel, reach, groups, send_sl...]
    ppermute x20 -> x19, waiting for transfers between devices: 38.8 us -> 58 us  [swapped(): return lax.ppermute(value, axis, [(i, i ^ by) for i in range(size)])]
    all_to_all x1, waiting for transfers between devices: 7.95 us -> 0.01 us  [exchanged(): return lax.all_to_all(value, axis, split_axis=0, concat_axis=0, tiled=True)]
    ppermute x20 -> x19, starting transfers between devices: 31.5 us -> 26.8 us  [swapped(): return lax.ppermute(value, axis, [(i, i ^ by) for i in range(size)])]
    ppermute x2, waiting for transfers between devices: 0.01 us -> 4.42 us  [shifted(): return lax.ppermute(value, axis, pairs)]
    concatenate x0 -> x5, other arithmetic: none -> 3.19 us  [the longest x2 3.17 us: local(): even = jnp.concatenate([even, swapped(even, 'node', 1 << bit)], axis=0)]
    unnamed x10 -> x12, local copies, waits for them, and re-layouts: 2.36 us -> 0.72 us
  transfers between devices with their start and end apart: 23 -> 22, of which waited for: 11 -> 12; matrix products, arithmetic and copies ran while one was open for 1% -> 2% of each run, Pallas kernels for 6% -> 5%
where the time goes in v5:
time: 131 us; the launch traced here: 130 us
  waiting for transfers between devices  62.5 us (48%)
  starting transfers between devices  38.6 us (29%)
  Pallas kernels  20.6 us (16%)
  other arithmetic  6.28 us (5%)
  local copies, waits for them, and re-layouts  1.34 us (1%)
    ppermute x19, waiting for transfers between devices, swapped(): return lax.ppermute(value, axis, [(i, i ^ by) for i in range(size)])  58 us
    ppermute x19, starting transfers between devices, swapped(): return lax.ppermute(value, axis, [(i, i ^ by) for i in range(size)])  26.8 us
    pallas_call x1, Pallas kernels, aggregate(): pl.pallas_call(functools.partial(aggregate_kernel, reach, groups, send_sl...  9.32 us
    all_to_all x1, starting transfers between devices, exchanged(): return lax.all_to_all(value, axis, split_axis=0, concat_axis=0, tiled=True)  8.18 us
    ppermute x2, waiting for transfers between devices, shifted(): return lax.ppermute(value, axis, pairs)  4.42 us
    ppermute x2, starting transfers between devices, shifted(): return lax.ppermute(value, axis, pairs)  3.67 us
    pallas_call x1, Pallas kernels, feature_rows(): pl.pallas_call(feature_kernel, in_specs=[IN_SMEM] + [IN_VMEM] * (groups +...  3.23 us
    concatenate x2, other arithmetic, local(): even = jnp.concatenate([even, swapped(even, 'node', 1 << bit)], axis=0)  3.17 us
  transfers between devices with their start and end apart: 22, of which 12 were waited for; matrix products, arithmetic and copies ran while one was open for 2% of the time, Pallas kernels for 5%

profile of v5, /device:TPU:0, one launch (start us, length us, event | category | flops | bytes accessed | tf_op | source)
XLA Modules:
  0.0 130.2 jit_solution(13851471423547751401)
XLA Ops:
  0.6 0.6 pad_add_fusion.me.index
  1.2 9.3 %aggregate.1 = (bf16[14,128,256]{2,1,0:T(8,128)(2,1)}, bf16[16,128,256]{2,1,0:T(8,128)(2,1)}, bf16[2,2,128,256]{3,2,1,0:T(8,128)(2,1)}, bf16[2,2,128,256]{3,2,1,...) custom-call(s32[2]{0:T(128)} %pad_add_fusion.me.index, ...), custom_call_target="tpu_custom_call" | custom-call | flops 1174405120 | bytes 7798784 | tf_op jit(solution)/shard_map/aggregate/pallas_call | solution.py:165
  10.5 2.4 %collective-permute-start = (bf16[2,2,128,256]{3,2,1,0:T(8,128)(2,1)}, bf16[2,2,128,256]{3,2,1,0:T(8,128)(2,1)S(1)}, u32[]{:S(2)}, u32[]{:S(2)}) collective-permute-start(bf16[2,2,128,256]{3,2,1,0:T(8,128)(2,1)} %get-tuple-element.36), channel_id=1, source_target_pairs={{0,4},{4,8},{8,12},{12,16},{16,20},{20,24},{24,28},{1,5},{5,9},{9,... | collective-permute-start | bytes 786440 | tf_op jit(solution)/shard_map/ppermute | solution.py:33
  12.9 1.3 collective-permute-start.1
  14.2 0.0 collective-permute-done.low
  14.3 4.4 %collective-permute-done.1.high = bf16[2,2,128,256]{3,2,1,0:T(8,128)(2,1)S(1)} collective-permute-done((bf16[2,2,128,256]{3,2,1,0:T(8,128)(2,1)}, bf16[2,2,128,256]{3,2,1,0:T(8,128)(2,1)S(1)}, u32[]{:S(2)}, u32[]{:S(2)}) %collective-permute-start.1) | collective-permute-done | bytes 262176 | tf_op jit(solution)/shard_map/ppermute | solution.py:33
  18.7 0.7 copy-done.4
  19.3 2.9 %patch.1 = (bf16[14,128,256]{2,1,0:T(8,128)(2,1)}, bf16[16,128,256]{2,1,0:T(8,128)(2,1)}) custom-call(s32[2]{0:T(128)} %pad_add_fusion.me.index, s32[112]{0:T(128)} %shuffle.3, bf16[14,128,256]{2,1,0:T(8,128)(2,1)} %get-tuple-element.34.clean, bf16[16,128,256]{2,1,0:T(8,128)(2,1)} %get-tuple-element.35.outgoing, ...), custom_call_target="tpu_custom_call", output_to_operand_aliasing={{0}: (2, {}), {1}: (3, {})} | custom-call | tf_op jit(solution)/shard_map/patch/pallas_call | solution.py:223
  22.3 0.0 copy-start
  22.3 8.2 %all-to-all-start = ((bf16[16,128,256]{2,1,0:T(8,128)(2,1)}), bf16[16,128,256]{2,1,0:T(8,128)(2,1)S(1)}, u32[]{:S(2)}, u32[]{:S(2)}) async-start(bf16[16,128,256]{2,1,0:T(8,128)(2,1)} %get-tuple-element.41), calls=%async_computation | async-start | bytes 2097152 | tf_op jit(solution)/shard_map/all_to_all | solution.py:42
  30.5 1.6 %collective-permute-start.2 = (bf16[576,256]{1,0:T(8,128)(2,1)}, bf16[576,256]{1,0:T(8,128)(2,1)S(1)}, u32[]{:S(2)}, u32[]{:S(2)}) collective-permute-start(bf16[576,256]{1,0:T(8,128)(2,1)} %get-tuple-element.43), channel_id=1, source_target_pairs={{0,1},{1,0},{2,3},{3,2},{4,5},{5,4},{6,7},{7,6},{8,9},{9,8},{10,11... | collective-permute-start | bytes 884744 | tf_op jit(solution)/shard_map/ppermute | solution.py:38
  32.1 2.6 %collective-permute-start.3 = (bf16[576,256]{1,0:T(8,128)(2,1)}, bf16[576,256]{1,0:T(8,128)(2,1)S(1)}, u32[]{:S(2)}, u32[]{:S(2)}) collective-permute-start(bf16[576,256]{1,0:T(8,128)(2,1)} %get-tuple-element.44), channel_id=1, source_target_pairs={{0,2},{1,3},{2,0},{3,1},{4,6},{5,7},{6,4},{7,5},{8,10},{9,11},{10,... | collective-permute-start | bytes 884744 | tf_op jit(solution)/shard_map/ppermute | solution.py:38
  34.7 0.2 collective-permute-start.4
  34.9 11.1 %collective-permute-done.2.refs_1_ = bf16[576,256]{1,0:T(8,128)(2,1)S(1)} collective-permute-done((bf16[576,256]{1,0:T(8,128)(2,1)}, bf16[576,256]{1,0:T(8,128)(2,1)S(1)}, u32[]{:S(2)}, u32[]{:S(2)}) %collective-permute-start.2) | collective-permute-done | bytes 294944 | tf_op jit(solution)/shard_map/ppermute | solution.py:38
  46.0 9.7 %collective-permute-done.3.refs_2_ = bf16[576,256]{1,0:T(8,128)(2,1)S(1)} collective-permute-done((bf16[576,256]{1,0:T(8,128)(2,1)}, bf16[576,256]{1,0:T(8,128)(2,1)S(1)}, u32[]{:S(2)}, u32[]{:S(2)}) %collective-permute-start.3) | collective-permute-done | bytes 294944 | tf_op jit(solution)/shard_map/ppermute | solution.py:38
  55.7 0.0 collective-permute-done.4.refs_3_
  55.7 0.0 all-to-all-done.incoming
  55.8 0.7 maximum_bitcast_fusion
  56.5 2.0 %collective-permute-start.8 = (bf16[1,4,128,256]{3,2,1,0:T(8,128)(2,1)}, bf16[1,4,128,256]{3,2,1,0:T(8,128)(2,1)}, u32[]{:S(2)}, u32[]{:S(2)}) collective-permute-start(bf16[1,4,128,256]{3,2,1,0:T(8,128)(2,1)} %maximum_bitcast_fusion), channel_id=1, source_target_pairs={{0,8},{4,12},{8,0},{12,4},{16,24},{20,28},{24,16},{28,20},{1,9},{5... | collective-permute-start | bytes 786440 | tf_op jit(solution)/shard_map/ppermute | solution.py:38
  58.5 0.1 eq.30
  58.6 0.1 add.45
  58.7 0.3 convert_reduce_fusion
  59.0 0.1 copy.15
  59.1 0.1 select_reduce_fusion
  59.2 5.2 %collective-permute-done.8 = bf16[1,4,128,256]{3,2,1,0:T(8,128)(2,1)} collective-permute-done((bf16[1,4,128,256]{3,2,1,0:T(8,128)(2,1)}, bf16[1,4,128,256]{3,2,1,0:T(8,128)(2,1)}, u32[]{:S(2)}, u32[]{:S(2)}) %collective-permute-start.8) | collective-permute-done | bytes 262176 | tf_op jit(solution)/shard_map/ppermute | solution.py:38
  64.4 1.9 %pad_maximum_fusion.1 = bf16[2,4,128,256]{3,2,1,0:T(8,128)(2,1)} fusion(bf16[1,4,128,256]{3,2,1,0:T(8,128)(2,1)} %collective-permute-done.8, bf16[1,4,128,256]{3,2,1,0:T(8,128)(2,1)} %maximum_bitcast_fusion), kind=kLoop, calls=%fused_computation.6 | loop fusion | flops 262144 | bytes 1048576 | tf_op jit(solution)/shard_map/concatenate | solution.py:458
  66.3 0.8 collective-permute-start.9
  67.1 0.1 copy.16
  67.2 0.1 sub.13.landing
  67.3 0.9 merge.1
  68.2 0.1 slice_bitcast_fusion.4
  68.3 2.5 %collective-permute-start.7 = (bf16[448,256]{1,0:T(8,128)(2,1)S(1)}, bf16[448,256]{1,0:T(8,128)(2,1)S(1)}, u32[]{:S(2)}, u32[]{:S(2)}) collective-permute-start(bf16[448,256]{1,0:T(8,128)(2,1)S(1)} %get-tuple-element.79), channel_id=1, source_target_pairs={{0,3},{1,2},{2,1},{3,0},{4,7},{5,6},{6,5},{7,4},{8,11},{9,10},{10,... | collective-permute-start | bytes 688136 | tf_op jit(solution)/shard_map/ppermute | solution.py:38
  70.8 5.7 %collective-permute-start.6 = (bf16[448,256]{1,0:T(8,128)(2,1)S(1)}, bf16[448,256]{1,0:T(8,128)(2,1)S(1)}, u32[]{:S(2)}, u32[]{:S(2)}) collective-permute-start(bf16[448,256]{1,0:T(8,128)(2,1)S(1)} %get-tuple-element.80), channel_id=1, source_target_pairs={{0,2},{1,3},{2,0},{3,1},{4,6},{5,7},{6,4},{7,5},{8,10},{9,11},{10,... | collective-permute-start | bytes 688136 | tf_op jit(solution)/shard_map/ppermute | solution.py:38
  76.5 0.1 collective-permute-start.5
  76.6 2.3 %collective-permute-done.9 = bf16[2,4,128,256]{3,2,1,0:T(8,128)(2,1)} collective-permute-done((bf16[2,4,128,256]{3,2,1,0:T(8,128)(2,1)}, bf16[2,4,128,256]{3,2,1,0:T(8,128)(2,1)}, u32[]{:S(2)}, u32[]{:S(2)}) %collective-permute-start.9) | collective-permute-done | bytes 524320 | tf_op jit(solution)/shard_map/ppermute | solution.py:38
  78.9 1.3 pad_maximum_fusion.refs_4_
  80.2 0.0 collective-permute-done.7.refs_7_.refs_3_
  80.2 10.7 %collective-permute-done.6.refs_6_.refs_2_ = bf16[448,256]{1,0:T(8,128)(2,1)S(1)} collective-permute-done((bf16[448,256]{1,0:T(8,128)(2,1)S(1)}, bf16[448,256]{1,0:T(8,128)(2,1)S(1)}, u32[]{:S(2)}, u32[]{:S(2)}) %collective-permute-start.6) | collective-permute-done | bytes 229408 | tf_op jit(solution)/shard_map/ppermute | solution.py:38
  90.9 0.0 collective-permute-done.5.refs_5_.refs_1_
  90.9 0.0 collective-permute-start.10
  90.9 2.6 %weight_partial.1 = (bf16[4,4,128,256]{3,2,1,0:T(8,128)(2,1)S(1)}, bf16[4,4,128,256]{3,2,1,0:T(8,128)(2,1)S(1)}) custom-call(s32[2]{0:T(128)S(1)} %copy-done.2, bf16[576,256]{1,0:T(8,128)(2,1)S(1)} %copy-done.1, bf16[576,256]{1,0:T(8,128)(2,1)S(1)} %collective-permute-done.2.refs_1_, bf16[576,256]{1,0:T(8,128)(2,1)S(1)} %collective-permute-done.3.refs_2_, ...), custom_call_target="tpu_custom_call" | custom-call | flops 939524096 | bytes 3932160 | tf_op jit(solution)/shard_map/weight_partial/pallas_call | solution.py:303
  93.6 0.0 collective-permute-done.10.refs_5_
  93.6 0.6 collective-permute-start.11
  94.1 3.2 %feature_rows.1 = bf16[4,448,256]{2,1,0:T(8,128)(2,1)S(1)} custom-call(s32[2]{0:T(128)S(1)} %copy-done.2, bf16[448,256]{1,0:T(8,128)(2,1)S(1)} %get-tuple-element.52.refs_4_.refs_0_, bf16[448,256]{1,0:T(8,128)(2,1)S(1)} %collective-permute-done.5.refs_5_.refs_1_, bf16[448,256]{1,0:T(8,128)(2,1)S(1)} %collective-permute-done.6.refs_6_.refs_2_, ...), custom_call_target="tpu_custom_call" | custom-call | flops 939524096 | bytes 3932160 | tf_op jit(solution)/shard_map/feature_rows/pallas_call | solution.py:351
  97.4 0.0 collective-permute-done.11
  97.4 0.4 fusion.8
  97.8 0.1 slice_bitcast_fusion.3
  97.8 1.5 %collective-permute-start.15 = (bf16[4,128,256]{2,1,0:T(8,128)(2,1)S(1)}, bf16[4,128,256]{2,1,0:T(8,128)(2,1)S(1)}, u32[]{:S(2)}, u32[]{:S(2)}) collective-permute-start(bf16[4,128,256]{2,1,0:T(8,128)(2,1)S(1)} %get-tuple-element.68), channel_id=1, source_target_pairs={{0,8},{4,12},{8,0},{12,4},{16,24},{20,28},{24,16},{28,20},{1,9},{5... | collective-permute-start | bytes 786440 | tf_op jit(solution)/shard_map/ppermute | solution.py:38
  99.4 1.2 collective-permute-start.17
  100.6 0.8 collective-permute-start.16
  101.4 2.5 %collective-permute-start.14 = (bf16[336,256]{1,0:T(8,128)(2,1)S(1)}, bf16[336,256]{1,0:T(8,128)(2,1)S(1)}, u32[]{:S(2)}, u32[]{:S(2)}) collective-permute-start(bf16[336,256]{1,0:T(8,128)(2,1)S(1)} %get-tuple-element.76), channel_id=1, source_target_pairs={{0,3},{1,2},{2,1},{3,0},{4,7},{5,6},{6,5},{7,4},{8,11},{9,10},{10,... | collective-permute-start | bytes 516104 | tf_op jit(solution)/shard_map/ppermute | solution.py:38
  104.0 3.1 %collective-permute-done.15 = bf16[4,128,256]{2,1,0:T(8,128)(2,1)S(1)} collective-permute-done((bf16[4,128,256]{2,1,0:T(8,128)(2,1)S(1)}, bf16[4,128,256]{2,1,0:T(8,128)(2,1)S(1)}, u32[]{:S(2)}, u32[]{:S(2)}) %collective-permute-start.15) | collective-permute-done | bytes 262176 | tf_op jit(solution)/shard_map/ppermute | solution.py:38
  107.1 5.5 %collective-permute-done.17 = bf16[4,128,256]{2,1,0:T(8,128)(2,1)S(1)} collective-permute-done((bf16[4,128,256]{2,1,0:T(8,128)(2,1)S(1)}, bf16[4,128,256]{2,1,0:T(8,128)(2,1)S(1)}, u32[]{:S(2)}, u32[]{:S(2)}) %collective-permute-start.17) | collective-permute-done | bytes 262176 | tf_op jit(solution)/shard_map/ppermute | solution.py:38
  112.5 1.4 %collective-permute-done.16 = bf16[4,128,256]{2,1,0:T(8,128)(2,1)S(1)} collective-permute-done((bf16[4,128,256]{2,1,0:T(8,128)(2,1)S(1)}, bf16[4,128,256]{2,1,0:T(8,128)(2,1)S(1)}, u32[]{:S(2)}, u32[]{:S(2)}) %collective-permute-start.16) | collective-permute-done | bytes 262176 | tf_op jit(solution)/shard_map/ppermute | solution.py:38
  114.0 0.1 fusion.2
  114.1 3.0 %collective-permute-done.13.refs_2_ = bf16[336,256]{1,0:T(8,128)(2,1)S(1)} collective-permute-done((bf16[336,256]{1,0:T(8,128)(2,1)S(1)}, bf16[336,256]{1,0:T(8,128)(2,1)S(1)}, u32[]{:S(2)}, u32[]{:S(2)}) %collective-permute-start.13) | collective-permute-done | bytes 172064 | tf_op jit(solution)/shard_map/ppermute | solution.py:38
  117.2 0.1 collective-permute-start.19
  117.3 2.5 %collective-permute-start.20 = (bf16[240,256]{1,0:T(8,128)(2,1)S(1)}, bf16[240,256]{1,0:T(8,128)(2,1)S(1)}, u32[]{:S(2)}, u32[]{:S(2)}) collective-permute-start(bf16[240,256]{1,0:T(8,128)(2,1)S(1)} %pad_maximum_fusion.4), channel_id=1, source_target_pairs={{0,1},{1,0},{2,3},{3,2},{4,5},{5,4},{6,7},{7,6},{8,9},{9,8},{10,11... | collective-permute-start | bytes 368648 | tf_op jit(solution)/shard_map/ppermute | solution.py:38
  119.9 2.0 %collective-permute-start.18 = (bf16[240,256]{1,0:T(8,128)(2,1)S(1)}, bf16[240,256]{1,0:T(8,128)(2,1)S(1)}, u32[]{:S(2)}, u32[]{:S(2)}) collective-permute-start(bf16[240,256]{1,0:T(8,128)(2,1)S(1)} %pad_maximum_fusion.2), channel_id=1, source_target_pairs={{0,3},{1,2},{2,1},{3,0},{4,7},{5,6},{6,5},{7,4},{8,11},{9,10},{10,... | collective-permute-start | bytes 368648 | tf_op jit(solution)/shard_map/ppermute | solution.py:38
  121.8 6.0 %collective-permute-done.19.refs_6_ = bf16[240,256]{1,0:T(8,128)(2,1)S(1)} collective-permute-done((bf16[240,256]{1,0:T(8,128)(2,1)S(1)}, bf16[240,256]{1,0:T(8,128)(2,1)S(1)}, u32[]{:S(2)}, u32[]{:S(2)}) %collective-permute-start.19) | collective-permute-done | bytes 122912 | tf_op jit(solution)/shard_map/ppermute | solution.py:38
  127.8 0.1 collective-permute-done.20.refs_5_
  127.9 0.0 collective-permute-done.18.refs_7_
  127.9 0.7 fusion.4
  128.6 1.5 %laid_out.1 = bf16[1792,256]{1,0:T(8,128)(2,1)} custom-call(s32[2]{0:T(128)S(1)} %copy-done.2, bf16[336,256]{1,0:T(8,128)(2,1)S(1)} %get-tuple-element.75.refs_0_, bf16[336,256]{1,0:T(8,128)(2,1)S(1)} %collective-permute-done.12.refs_1_, bf16[336,256]{1,0:T(8,128)(2,1)S(1)} %collective-permute-done.13.refs_2_, ...), custom_call_target="tpu_custom_call" | custom-call | tf_op jit(solution)/shard_map/laid_out/pallas_call | solution.py:389
  (27 shorter events, 0.2 us)
Async XLA Ops:
  10.5 3.7 %collective-permute-start = (bf16[2,2,128,256]{3,2,1,0:T(8,128)(2,1)}, bf16[2,2,128,256]{3,2,1,0:T(8,128)(2,1)S(1)}, u32[]{:S(2)}, u32[]{:S(2)}) collective-permute-start(bf16[2,2,128,256]{3,2,1,0:T(8,128)(2,1)} %get-tuple-element.36), channel_id=1, source_target_pairs={{0,4},{4,8},{8,12},{12,16},{16,20},{20,24},{24,28},{1,5},{5,9},{9,... | collective-permute-start | bytes 786440 | tf_op jit(solution)/shard_map/ppermute | solution.py:33
  12.9 5.7 %collective-permute-start.1 = (bf16[2,2,128,256]{3,2,1,0:T(8,128)(2,1)}, bf16[2,2,128,256]{3,2,1,0:T(8,128)(2,1)S(1)}, u32[]{:S(2)}, u32[]{:S(2)}) collective-permute-start(bf16[2,2,128,256]{3,2,1,0:T(8,128)(2,1)} %get-tuple-element.37), channel_id=1, source_target_pairs={{4,0},{8,4},{12,8},{16,12},{20,16},{24,20},{28,24},{5,1},{9,5},{13... | collective-permute-start | bytes 786440 | tf_op jit(solution)/shard_map/ppermute | solution.py:33
  14.3 4.4 %copy-start.3 = (bf16[2,2,128,256]{3,2,1,0:T(8,128)(2,1)}, bf16[2,2,128,256]{3,2,1,0:T(8,128)(2,1)S(1)}, u32[]{:S(2)}) copy-start(bf16[2,2,128,256]{3,2,1,0:T(8,128)(2,1)S(1)} %collective-permute-done.low) | copy-start | bytes 786436
  18.6 0.7 copy-start.4
  19.3 15.6 %copy-start.5 = (s32[112]{0:T(128)S(1)}, s32[112]{0:T(128)}, u32[]{:S(2)}) copy-start(s32[112]{0:T(128)} %shuffle.3) | copy-start | bytes 1348
  19.3 36.4 %copy-start.1 = (bf16[576,256]{1,0:T(8,128)(2,1)S(1)}, bf16[576,256]{1,0:T(8,128)(2,1)}, u32[]{:S(2)}) copy-start(bf16[576,256]{1,0:T(8,128)(2,1)} %get-tuple-element.47.refs_0_) | copy-start | bytes 884740
  22.3 45.0 %copy-start = (bf16[14,128,256]{2,1,0:T(8,128)(2,1)S(1)}, bf16[14,128,256]{2,1,0:T(8,128)(2,1)}, u32[]{:S(2)}) copy-start(bf16[14,128,256]{2,1,0:T(8,128)(2,1)} %get-tuple-element.40.clean) | copy-start | bytes 2752516
  22.3 45.0 %copy-start.2 = (s32[2]{0:T(128)S(1)}, s32[2]{0:T(128)}, u32[]{:S(2)}) copy-start(s32[2]{0:T(128)} %pad_add_fusion.me.index) | copy-start | bytes 28
  22.3 33.4 %all-to-all-start = ((bf16[16,128,256]{2,1,0:T(8,128)(2,1)}), bf16[16,128,256]{2,1,0:T(8,128)(2,1)S(1)}, u32[]{:S(2)}, u32[]{:S(2)}) async-start(bf16[16,128,256]{2,1,0:T(8,128)(2,1)} %get-tuple-element.41), calls=%async_computation | async-start | bytes 2097152 | tf_op jit(solution)/shard_map/all_to_all | solution.py:42
  30.5 15.5 %collective-permute-start.2 = (bf16[576,256]{1,0:T(8,128)(2,1)}, bf16[576,256]{1,0:T(8,128)(2,1)S(1)}, u32[]{:S(2)}, u32[]{:S(2)}) collective-permute-start(bf16[576,256]{1,0:T(8,128)(2,1)} %get-tuple-element.43), channel_id=1, source_target_pairs={{0,1},{1,0},{2,3},{3,2},{4,5},{5,4},{6,7},{7,6},{8,9},{9,8},{10,11... | collective-permute-start | bytes 884744 | tf_op jit(solution)/shard_map/ppermute | solution.py:38
  32.1 23.6 %collective-permute-start.3 = (bf16[576,256]{1,0:T(8,128)(2,1)}, bf16[576,256]{1,0:T(8,128)(2,1)S(1)}, u32[]{:S(2)}, u32[]{:S(2)}) collective-permute-start(bf16[576,256]{1,0:T(8,128)(2,1)} %get-tuple-element.44), channel_id=1, source_target_pairs={{0,2},{1,3},{2,0},{3,1},{4,6},{5,7},{6,4},{7,5},{8,10},{9,11},{10,... | collective-permute-start | bytes 884744 | tf_op jit(solution)/shard_map/ppermute | solution.py:38
  34.7 21.0 %collective-permute-start.4 = (bf16[576,256]{1,0:T(8,128)(2,1)}, bf16[576,256]{1,0:T(8,128)(2,1)S(1)}, u32[]{:S(2)}, u32[]{:S(2)}) collective-permute-start(bf16[576,256]{1,0:T(8,128)(2,1)} %get-tuple-element.45), channel_id=1, source_target_pairs={{0,3},{1,2},{2,1},{3,0},{4,7},{5,6},{6,5},{7,4},{8,11},{9,10},{10,... | collective-permute-start | bytes 884744 | tf_op jit(solution)/shard_map/ppermute | solution.py:38
  56.5 7.9 %collective-permute-start.8 = (bf16[1,4,128,256]{3,2,1,0:T(8,128)(2,1)}, bf16[1,4,128,256]{3,2,1,0:T(8,128)(2,1)}, u32[]{:S(2)}, u32[]{:S(2)}) collective-permute-start(bf16[1,4,128,256]{3,2,1,0:T(8,128)(2,1)} %maximum_bitcast_fusion), channel_id=1, source_target_pairs={{0,8},{4,12},{8,0},{12,4},{16,24},{20,28},{24,16},{28,20},{1,9},{5... | collective-permute-start | bytes 786440 | tf_op jit(solution)/shard_map/ppermute | solution.py:38
  66.3 12.6 %collective-permute-start.9 = (bf16[2,4,128,256]{3,2,1,0:T(8,128)(2,1)}, bf16[2,4,128,256]{3,2,1,0:T(8,128)(2,1)}, u32[]{:S(2)}, u32[]{:S(2)}) collective-permute-start(bf16[2,4,128,256]{3,2,1,0:T(8,128)(2,1)} %pad_maximum_fusion.1), channel_id=1, source_target_pairs={{0,16},{4,20},{8,24},{12,28},{16,0},{20,4},{24,8},{28,12},{1,17},{... | collective-permute-start | bytes 1572872 | tf_op jit(solution)/shard_map/ppermute | solution.py:38
  68.3 11.9 %collective-permute-start.7 = (bf16[448,256]{1,0:T(8,128)(2,1)S(1)}, bf16[448,256]{1,0:T(8,128)(2,1)S(1)}, u32[]{:S(2)}, u32[]{:S(2)}) collective-permute-start(bf16[448,256]{1,0:T(8,128)(2,1)S(1)} %get-tuple-element.79), channel_id=1, source_target_pairs={{0,3},{1,2},{2,1},{3,0},{4,7},{5,6},{6,5},{7,4},{8,11},{9,10},{10,... | collective-permute-start | bytes 688136 | tf_op jit(solution)/shard_map/ppermute | solution.py:38
  70.8 20.1 %collective-permute-start.6 = (bf16[448,256]{1,0:T(8,128)(2,1)S(1)}, bf16[448,256]{1,0:T(8,128)(2,1)S(1)}, u32[]{:S(2)}, u32[]{:S(2)}) collective-permute-start(bf16[448,256]{1,0:T(8,128)(2,1)S(1)} %get-tuple-element.80), channel_id=1, source_target_pairs={{0,2},{1,3},{2,0},{3,1},{4,6},{5,7},{6,4},{7,5},{8,10},{9,11},{10,... | collective-permute-start | bytes 688136 | tf_op jit(solution)/shard_map/ppermute | solution.py:38
  76.5 14.4 %collective-permute-start.5 = (bf16[448,256]{1,0:T(8,128)(2,1)S(1)}, bf16[448,256]{1,0:T(8,128)(2,1)S(1)}, u32[]{:S(2)}, u32[]{:S(2)}) collective-permute-start(bf16[448,256]{1,0:T(8,128)(2,1)S(1)} %get-tuple-element.81), channel_id=1, source_target_pairs={{0,1},{1,0},{2,3},{3,2},{4,5},{5,4},{6,7},{7,6},{8,9},{9,8},{10,11... | collective-permute-start | bytes 688136 | tf_op jit(solution)/shard_map/ppermute | solution.py:38
  90.9 2.7 %collective-permute-start.10 = (bf16[4,4,128,256]{3,2,1,0:T(8,128)(2,1)S(1)}, bf16[4,4,128,256]{3,2,1,0:T(8,128)(2,1)S(1)}, u32[]{:S(2)}, u32[]{:S(2)}) collective-permute-start(bf16[4,4,128,256]{3,2,1,0:T(8,128)(2,1)S(1)} %pad_maximum_fusion.refs_4_), channel_id=1, source_target_pairs={{0,4},{4,0},{8,12},{12,8},{16,20},{20,16},{24,28},{28,24},{1,5},{5... | collective-permute-start | bytes 3145736 | tf_op jit(solution)/shard_map/ppermute | solution.py:38
  93.6 3.8 %collective-permute-start.11 = (bf16[4,4,128,256]{3,2,1,0:T(8,128)(2,1)S(1)}, bf16[4,4,128,256]{3,2,1,0:T(8,128)(2,1)S(1)}, u32[]{:S(2)}, u32[]{:S(2)}) collective-permute-start(bf16[4,4,128,256]{3,2,1,0:T(8,128)(2,1)S(1)} %get-tuple-element.57), channel_id=1, source_target_pairs={{0,4},{4,0},{8,12},{12,8},{16,20},{20,16},{24,28},{28,24},{1,5},{5... | collective-permute-start | bytes 3145736 | tf_op jit(solution)/shard_map/ppermute | solution.py:38
  97.8 9.2 %collective-permute-start.15 = (bf16[4,128,256]{2,1,0:T(8,128)(2,1)S(1)}, bf16[4,128,256]{2,1,0:T(8,128)(2,1)S(1)}, u32[]{:S(2)}, u32[]{:S(2)}) collective-permute-start(bf16[4,128,256]{2,1,0:T(8,128)(2,1)S(1)} %get-tuple-element.68), channel_id=1, source_target_pairs={{0,8},{4,12},{8,0},{12,4},{16,24},{20,28},{24,16},{28,20},{1,9},{5... | collective-permute-start | bytes 786440 | tf_op jit(solution)/shard_map/ppermute | solution.py:38
  99.4 13.2 %collective-permute-start.17 = (bf16[4,128,256]{2,1,0:T(8,128)(2,1)S(1)}, bf16[4,128,256]{2,1,0:T(8,128)(2,1)S(1)}, u32[]{:S(2)}, u32[]{:S(2)}) collective-permute-start(bf16[4,128,256]{2,1,0:T(8,128)(2,1)S(1)} %get-tuple-element.69), channel_id=1, source_target_pairs={{0,24},{4,28},{8,16},{12,20},{16,8},{20,12},{24,0},{28,4},{1,25},{... | collective-permute-start | bytes 786440 | tf_op jit(solution)/shard_map/ppermute | solution.py:38
  100.6 13.4 %collective-permute-start.16 = (bf16[4,128,256]{2,1,0:T(8,128)(2,1)S(1)}, bf16[4,128,256]{2,1,0:T(8,128)(2,1)S(1)}, u32[]{:S(2)}, u32[]{:S(2)}) collective-permute-start(bf16[4,128,256]{2,1,0:T(8,128)(2,1)S(1)} %get-tuple-element.70), channel_id=1, source_target_pairs={{0,16},{4,20},{8,24},{12,28},{16,0},{20,4},{24,8},{28,12},{1,17},{... | collective-permute-start | bytes 786440 | tf_op jit(solution)/shard_map/ppermute | solution.py:38
  101.4 12.7 %collective-permute-start.14 = (bf16[336,256]{1,0:T(8,128)(2,1)S(1)}, bf16[336,256]{1,0:T(8,128)(2,1)S(1)}, u32[]{:S(2)}, u32[]{:S(2)}) collective-permute-start(bf16[336,256]{1,0:T(8,128)(2,1)S(1)} %get-tuple-element.76), channel_id=1, source_target_pairs={{0,3},{1,2},{2,1},{3,0},{4,7},{5,6},{6,5},{7,4},{8,11},{9,10},{10,... | collective-permute-start | bytes 516104 | tf_op jit(solution)/shard_map/ppermute | solution.py:38
  104.0 13.1 %collective-permute-start.13 = (bf16[336,256]{1,0:T(8,128)(2,1)S(1)}, bf16[336,256]{1,0:T(8,128)(2,1)S(1)}, u32[]{:S(2)}, u32[]{:S(2)}) collective-permute-start(bf16[336,256]{1,0:T(8,128)(2,1)S(1)} %get-tuple-element.77), channel_id=1, source_target_pairs={{0,2},{1,3},{2,0},{3,1},{4,6},{5,7},{6,4},{7,5},{8,10},{9,11},{10,... | collective-permute-start | bytes 516104 | tf_op jit(solution)/shard_map/ppermute | solution.py:38
  107.1 10.1 %collective-permute-start.12 = (bf16[336,256]{1,0:T(8,128)(2,1)S(1)}, bf16[336,256]{1,0:T(8,128)(2,1)S(1)}, u32[]{:S(2)}, u32[]{:S(2)}) collective-permute-start(bf16[336,256]{1,0:T(8,128)(2,1)S(1)} %get-tuple-element.78), channel_id=1, source_target_pairs={{0,1},{1,0},{2,3},{3,2},{4,5},{5,4},{6,7},{7,6},{8,9},{9,8},{10,11... | collective-permute-start | bytes 516104 | tf_op jit(solution)/shard_map/ppermute | solution.py:38
  117.2 10.6 %collective-permute-start.19 = (bf16[240,256]{1,0:T(8,128)(2,1)S(1)}, bf16[240,256]{1,0:T(8,128)(2,1)S(1)}, u32[]{:S(2)}, u32[]{:S(2)}) collective-permute-start(bf16[240,256]{1,0:T(8,128)(2,1)S(1)} %pad_maximum_fusion.3), channel_id=1, source_target_pairs={{0,2},{1,3},{2,0},{3,1},{4,6},{5,7},{6,4},{7,5},{8,10},{9,11},{10,... | collective-permute-start | bytes 368648 | tf_op jit(solution)/shard_map/ppermute | solution.py:38
  117.3 10.6 %collective-permute-start.20 = (bf16[240,256]{1,0:T(8,128)(2,1)S(1)}, bf16[240,256]{1,0:T(8,128)(2,1)S(1)}, u32[]{:S(2)}, u32[]{:S(2)}) collective-permute-start(bf16[240,256]{1,0:T(8,128)(2,1)S(1)} %pad_maximum_fusion.4), channel_id=1, source_target_pairs={{0,1},{1,0},{2,3},{3,2},{4,5},{5,4},{6,7},{7,6},{8,9},{9,8},{10,11... | collective-permute-start | bytes 368648 | tf_op jit(solution)/shard_map/ppermute | solution.py:38
  119.9 8.1 %collective-permute-start.18 = (bf16[240,256]{1,0:T(8,128)(2,1)S(1)}, bf16[240,256]{1,0:T(8,128)(2,1)S(1)}, u32[]{:S(2)}, u32[]{:S(2)}) collective-permute-start(bf16[240,256]{1,0:T(8,128)(2,1)S(1)} %pad_maximum_fusion.2), channel_id=1, source_target_pairs={{0,3},{1,2},{2,1},{3,0},{4,7},{5,6},{6,5},{7,4},{8,11},{9,10},{10,... | collective-permute-start | bytes 368648 | tf_op jit(solution)/shard_map/ppermute | solution.py:38

commit v6 on v5

--- a/solution.py
+++ b/solution.py
@@ -60,7 +60,8 @@
     reach, groups, send_slots, me, shuffle, cols, count, gc, pc, gx, px, slopes, adj, features, weight, *refs
 ):
     clean, outgoing, down, up, *refs = refs
-    packed, (data, tiles, rhs, stage, places, used, sems, pack_sems) = refs[:groups], refs[groups:]
+    packed, refs = refs[:groups], refs[groups:]
+    data, tiles, rhs, stage, results, halos, packs, places, used, sems, tile_sems, pack_sems, out_sems = refs
     blocks, slots, rows, _ = adj.shape
     width = gc.shape[1]
     quarter = features.shape[0] // groups
@@ -69,23 +70,32 @@
 
     def copies(block):
         span = pl.ds(pl.multiple_of(block * rows, rows), rows)
-        out = [
+        return [
             pltpu.make_async_copy(ref.at[span], data.at[i, block], sems.at[i, block])
             for i, ref in enumerate((gc, pc, gx, px))
         ]
-        return out + [pltpu.make_async_copy(adj.at[block], tiles.at[block], sems.at[4, block])]
-
-    packs = []
-    for i in range(groups):
-        span = pl.ds(pl.multiple_of((me[1] ^ i) * quarter, quarter), quarter)
-        packs.append(
-            pltpu.make_async_copy(features.at[span], packed[i].at[:quarter], pack_sems.at[0, i])
-        )
-        packs.append(pltpu.make_async_copy(weight, packed[i].at[quarter:], pack_sems.at[1, i]))
+
+    def each_tile(block, act):
+        for k in range(slots):
+            pl.when(k < count[block])(
+                lambda k=k: act(
+                    pltpu.make_async_copy(adj.at[block, k], tiles.at[block, k], tile_sems.at[block, k])
+                )
+            )
+
     for block in range(blocks):
         for copy in copies(block):
             copy.start()
-    for copy in packs:
+        each_tile(block, lambda copy: copy.start())
+    to_vmem, to_hbm = [], []
+    for i in range(groups):
+        span = pl.ds(pl.multiple_of((me[1] ^ i) * quarter, quarter), quarter)
+        to_vmem.append(
+            pltpu.make_async_copy(features.at[span], packs.at[i, :quarter], pack_sems.at[0, i])
+        )
+        to_vmem.append(pltpu.make_async_copy(weight, packs.at[i, quarter:], pack_sems.at[1, i]))
+        to_hbm.append(pltpu.make_async_copy(packs.at[i], packed[i], pack_sems.at[2, i]))
+    for copy in to_vmem:
         copy.start()
     stage[...] = jnp.zeros_like(stage)
     rhs[:pad] = jnp.zeros((pad, 2 * width), jnp.bfloat16)
@@ -95,6 +105,7 @@
         lax.broadcasted_iota(jnp.int32, shape, 0) == lax.broadcasted_iota(jnp.int32, shape, 1)
     ).astype(jnp.float32).astype(jnp.bfloat16)
     slope = slopes[...]
+    find_places(me, shuffle, blocks, send_slots, places, used)
 
     def take(block):
         gradients = [masked_grad(data[i, block], data[i + 1, block], slope) for i in (0, 2)]
@@ -114,17 +125,22 @@
             part = turned[:, k * rows : (k + 1) * rows]
             stage[place, distance] = (wide(stage[place, distance]) + part).astype(jnp.bfloat16)
 
-    find_places(me, shuffle, blocks, send_slots, places, used)
     per_step = blocks // 2
 
     @pl.loop(0, blocks // per_step)
     def _(step):
         for i in range(per_step):
-            for copy in copies(step * per_step + i):
+            block = step * per_step + i
+            for copy in copies(block):
                 copy.wait()
+            each_tile(block, lambda copy: copy.wait())
         for i in range(per_step):
             take(step * per_step + i)
 
+    for copy in to_vmem:
+        copy.wait()
+    for copy in to_hbm:
+        copy.start()
     blank = jnp.zeros(shape, jnp.bfloat16)
 
     def pair(first):
@@ -144,15 +160,25 @@
         return product[:, :, :width], product[:, :, width:]
 
     for i in range(0, reach, 2):
-        down[0, i : i + 2], down[1, i : i + 2] = pair(i)
-        up[0, i : i + 2], up[1, i : i + 2] = pair(blocks + reach + i)
-
+        halos[0, 0, i : i + 2], halos[0, 1, i : i + 2] = pair(i)
+        halos[1, 0, i : i + 2], halos[1, 1, i : i + 2] = pair(blocks + reach + i)
+    writes = [
+        pltpu.make_async_copy(halos.at[0], down, out_sems.at[2, 0]),
+        pltpu.make_async_copy(halos.at[1], up, out_sems.at[2, 1]),
+    ]
+    for copy in writes:
+        copy.start()
     for first in range(0, blocks, 2):
-        clean[first : first + 2], sent = pair(reach + first)
-        for i in range(2):
-            outgoing[places[first + i]] = sent[i]
-
-    for copy in packs:
+        span = pl.ds(first, 2)
+        results[0, span], results[1, span] = pair(reach + first)
+        done = [pltpu.make_async_copy(results.at[0, span], clean.at[span], out_sems.at[0, first])]
+        for block in range(first, first + 2):
+            target = outgoing.at[places[block]]
+            done.append(pltpu.make_async_copy(results.at[1, block], target, out_sems.at[1, block]))
+        for copy in done:
+            copy.start()
+        writes += done
+    for copy in writes + to_hbm:
         copy.wait()
 
 
@@ -165,7 +191,7 @@
     return pl.pallas_call(
         functools.partial(aggregate_kernel, reach, groups, send_slots),
         in_specs=[IN_SMEM] * 4 + [IN_HBM] * 4 + [IN_VMEM] + [IN_HBM] * 3,
-        out_specs=[IN_VMEM] * (4 + groups),
+        out_specs=[IN_HBM] * (4 + groups),
         out_shape=[bf16(blocks, rows, width), bf16(devs * send_slots, rows, width)]
         + [bf16(2, reach, rows, width)] * 2
         + [bf16(packed, width)] * groups,
@@ -174,10 +200,15 @@
             pltpu.VMEM((blocks, slots, rows, rows), jnp.bfloat16),
             pltpu.VMEM(((blocks + 4 * reach) * rows, 2 * width), jnp.bfloat16),
             pltpu.VMEM((blocks + 2 * reach + 1, 2 * reach + 1, rows, rows), jnp.bfloat16),
+            pltpu.VMEM((2, blocks, rows, width), jnp.bfloat16),
+            pltpu.VMEM((2, 2, reach, rows, width), jnp.bfloat16),
+            pltpu.VMEM((groups, packed, width), jnp.bfloat16),
             pltpu.SMEM((blocks,), jnp.int32),
             pltpu.SMEM((devs,), jnp.int32),
-            pltpu.SemaphoreType.DMA((5, blocks)),
-            pltpu.SemaphoreType.DMA((2, groups)),
+            pltpu.SemaphoreType.DMA((4, blocks)),
+            pltpu.SemaphoreType.DMA((blocks, slots)),
+            pltpu.SemaphoreType.DMA((3, groups)),
+            pltpu.SemaphoreType.DMA((3, blocks)),
         ],
         compiler_params=params(VMEM_ALL),
         cost_estimate=pl.CostEstimate(
@@ -190,29 +221,35 @@
 
 
 def patch_kernel(reach, slots, index, shuffle, clean, outgoing, low, high, clean_out, outgoing_out, *scratch):
-    held, ready, places, used, sems = scratch
+    held, other, ready, places, used, sems = scratch
     blocks = clean.shape[0]
+    border = [*range(reach), *range(blocks - reach, blocks)]
+    arrivals = [
+        pltpu.make_async_copy(low, other.at[0], sems.at[2, 0, 0]),
+        pltpu.make_async_copy(high, other.at[1], sems.at[2, 0, 1]),
+    ]
+    for copy in arrivals:
+        copy.start()
     find_places(index, shuffle, blocks, slots, places, used)
-    border = [*range(reach), *range(blocks - reach, blocks)]
-
-    def spots(i, first, second):
-        return (first.at[border[i]], second.at[places[border[i]]])
-
+
+    def spot(i, which, first, second):
+        return second.at[places[border[i]]] if which else first.at[border[i]]
+
+    order = [(i, which) for i in range(2 * reach) for which in range(2)]
     reads, writes = [], []
-    for i in range(2 * reach):
-        for which in range(2):
-            source = spots(i, clean, outgoing)[which]
-            reads.append(pltpu.make_async_copy(source, held.at[which, i], sems.at[0, which, i]))
-            target = spots(i, clean_out, outgoing_out)[which]
-            writes.append(pltpu.make_async_copy(ready.at[which, i], target, sems.at[1, which, i]))
+    for i, which in order:
+        source, target = spot(i, which, clean, outgoing), spot(i, which, clean_out, outgoing_out)
+        reads.append(pltpu.make_async_copy(source, held.at[which, i], sems.at[0, which, i]))
+        writes.append(pltpu.make_async_copy(ready.at[which, i], target, sems.at[1, which, i]))
     for copy in reads:
         copy.start()
-    for i in range(2 * reach):
-        for which in range(2):
-            reads[2 * i + which].wait()
-            other = low[which, i] if i < reach else high[which, i - reach]
-            ready[which, i] = (wide(held[which, i]) + wide(other)).astype(jnp.bfloat16)
-            writes[2 * i + which].start()
+    for copy in arrivals:
+        copy.wait()
+    for (i, which), read, write in zip(order, reads, writes):
+        read.wait()
+        total = wide(held[which, i]) + wide(other[i // reach, which, i % reach])
+        ready[which, i] = total.astype(jnp.bfloat16)
+        write.start()
     for copy in writes:
         copy.wait()
 
@@ -220,18 +257,20 @@
 def patch(index, shuffle, clean, outgoing, low, high, slots):
     blocks, rows, width = clean.shape
     reach = low.shape[1]
+    blocks_shape = (2, 2 * reach, rows, width)
     return pl.pallas_call(
         functools.partial(patch_kernel, reach, slots),
-        in_specs=[IN_SMEM] * 2 + [IN_HBM] * 2 + [IN_VMEM] * 2,
+        in_specs=[IN_SMEM] * 2 + [IN_HBM] * 4,
         out_specs=[IN_HBM] * 2,
         out_shape=[bf16(*clean.shape), bf16(*outgoing.shape)],
         input_output_aliases={2: 0, 3: 1},
         scratch_shapes=[
-            pltpu.VMEM((2, 2 * reach, rows, width), jnp.bfloat16),
-            pltpu.VMEM((2, 2 * reach, rows, width), jnp.bfloat16),
+            pltpu.VMEM(blocks_shape, jnp.bfloat16),
+            pltpu.VMEM((2, 2, reach, rows, width), jnp.bfloat16),
+            pltpu.VMEM(blocks_shape, jnp.bfloat16),
             pltpu.SMEM((blocks,), jnp.int32),
             pltpu.SMEM((outgoing.shape[0] // slots,), jnp.int32),
-            pltpu.SemaphoreType.DMA((2, 2, 2 * reach)),
+            pltpu.SemaphoreType.DMA((3, 2, 2 * reach)),
         ],
         compiler_params=params(VMEM_ALL),
         name="patch",
@@ -453,10 +492,11 @@
     summed = [merged[0]] + [None] * (groups - 1)
     for i in exchange_order(groups):
         summed[i] = swapped(merged[i], "chan", i)
-    even = jnp.stack([piece[quarter:] for piece in packed])[None]
-    for bit in range(1, devs.bit_length() - 1):
-        even = jnp.concatenate([even, swapped(even, "node", 1 << bit)], axis=0)
-    summed, even = lax.optimization_barrier((summed, even))
+    tiles = jnp.stack([piece[quarter:] for piece in packed])
+    even = [tiles] + [swapped(tiles, "node", 2 * i) for i in range(1, devs // 2)]
+    early = devs // 2 - 1
+    summed, even[:early] = lax.optimization_barrier((summed, even[:early]))
+    even = jnp.stack(even)
     odd = swapped(even, "node", 1)
 
     keep, send = weight_partial(index, packed, summed, devs)
@@ -470,10 +510,13 @@
     for i in exchange_order(groups):
         heads[i] = swapped(rows_out[i, :cut], "chan", i)
     total = wide(keep) + wide(arrived)
+    sums = [
+        swapped(total[i].astype(jnp.bfloat16), "node", 2 * i) for i in range(1, devs // 2)
+    ]
+    heads, sums = lax.optimization_barrier((heads, sums))
     share = total[0]
-    for i in range(1, devs // 2):
-        share = share + wide(swapped(total[i].astype(jnp.bfloat16), "node", 2 * i))
-    heads, share = lax.optimization_barrier((heads, share))
+    for part in sums:
+        share = share + wide(part)
     grad_weight = share[0]
     tails = [rows_out[0, cut:]] + [None] * (groups - 1)
     for i in exchange_order(groups):

time: 131 us -> 114 us (0.87)
  waiting for transfers between devices: 62.5 us -> 38.3 us
  starting transfers between devices: 38.6 us -> 50.7 us
  other arithmetic: 6.28 us -> 2.53 us
    ppermute x19 -> x20, waiting for transfers between devices: 58 us -> 30.5 us  [swapped(): return lax.ppermute(value, axis, [(i, i ^ by) for i in range(size)])]
    ppermute x19 -> x20, starting transfers between devices: 26.8 us -> 39.2 us  [swapped(): return lax.ppermute(value, axis, [(i, i ^ by) for i in range(size)])]
    all_to_all x1, waiting for transfers between devices: 0.01 us -> 7.8 us  [exchanged(): return lax.all_to_all(value, axis, split_axis=0, concat_axis=0, tiled=True)]
    ppermute x2, waiting for transfers between devices: 4.42 us -> 0.01 us  [shifted(): return lax.ppermute(value, axis, pairs)]
    concatenate x2 -> x0, other arithmetic: 3.17 us -> none  [local(): even = jnp.concatenate([even, swapped(even, 'node', 1 << bit)], axis=0)]
  transfers between devices with their start and end apart: 22 -> 23, of which waited for: 12 -> 10; matrix products, arithmetic and copies ran while one was open for 2% -> 1% of each run, Pallas kernels for 5% -> 8%
where the time goes in v6:
time: 114 us
  starting transfers between devices  50.7 us (44%)
  waiting for transfers between devices  38.3 us (34%)
  Pallas kernels  19.9 us (17%)
  other arithmetic  2.53 us (2%)
  local copies, waits for them, and re-layouts  1.43 us (1%)
    ppermute x20, starting transfers between devices, swapped(): return lax.ppermute(value, axis, [(i, i ^ by) for i in range(size)])  39.2 us
    ppermute x20, waiting for transfers between devices, swapped(): return lax.ppermute(value, axis, [(i, i ^ by) for i in range(size)])  30.5 us
    pallas_call x1, Pallas kernels, aggregate(): pl.pallas_call(functools.partial(aggregate_kernel, reach, groups, send_sl...  8.75 us
    all_to_all x1, starting transfers between devices, exchanged(): return lax.all_to_all(value, axis, split_axis=0, concat_axis=0, tiled=True)  7.85 us
    all_to_all x1, waiting for transfers between devices, exchanged(): return lax.all_to_all(value, axis, split_axis=0, concat_axis=0, tiled=True)  7.8 us
    ppermute x2, starting transfers between devices, shifted(): return lax.ppermute(value, axis, pairs)  3.63 us
    pallas_call x1, Pallas kernels, feature_rows(): pl.pallas_call(feature_kernel, in_specs=[IN_SMEM] + [IN_VMEM] * (groups +...  3.22 us
    pallas_call x1, Pallas kernels, patch(): pl.pallas_call(functools.partial(patch_kernel, reach, slots), in_specs=[I...  2.84 us
  transfers between devices with their start and end apart: 23, of which 10 were waited for; matrix products, arithmetic and copies ran while one was open for 1% of the time, Pallas kernels for 8%

profile of v6, /device:TPU:0, one launch (start us, length us, event | category | flops | bytes accessed | tf_op | source)
XLA Modules:
  0.0 113.7 jit_solution(8029811235556825733)
XLA Ops:
  0.6 0.6 pad_add_fusion.me.index
  1.2 8.8 %aggregate.1 = (bf16[14,128,256]{2,1,0:T(8,128)(2,1)}, bf16[16,128,256]{2,1,0:T(8,128)(2,1)}, bf16[2,2,128,256]{3,2,1,0:T(8,128)(2,1)}, bf16[2,2,128,256]{3,2,1,...) custom-call(s32[2]{0:T(128)} %pad_add_fusion.me.index, ...), custom_call_target="tpu_custom_call" | custom-call | flops 1174405120 | bytes 7798784 | tf_op jit(solution)/shard_map/aggregate/pallas_call | solution.py:191
  10.0 2.3 %collective-permute-start = (bf16[2,2,128,256]{3,2,1,0:T(8,128)(2,1)}, bf16[2,2,128,256]{3,2,1,0:T(8,128)(2,1)S(1)}, u32[]{:S(2)}, u32[]{:S(2)}) collective-permute-start(bf16[2,2,128,256]{3,2,1,0:T(8,128)(2,1)} %get-tuple-element.40), channel_id=1, source_target_pairs={{0,4},{4,8},{8,12},{12,16},{16,20},{20,24},{24,28},{1,5},{5,9},{9,... | collective-permute-start | bytes 786440 | tf_op jit(solution)/shard_map/ppermute | solution.py:33
  12.4 1.3 %collective-permute-start.1 = (bf16[2,2,128,256]{3,2,1,0:T(8,128)(2,1)}, bf16[2,2,128,256]{3,2,1,0:T(8,128)(2,1)S(1)}, u32[]{:S(2)}, u32[]{:S(2)}) collective-permute-start(bf16[2,2,128,256]{3,2,1,0:T(8,128)(2,1)} %get-tuple-element.41), channel_id=1, source_target_pairs={{4,0},{8,4},{12,8},{16,12},{20,16},{24,20},{28,24},{5,1},{9,5},{13... | collective-permute-start | bytes 786440 | tf_op jit(solution)/shard_map/ppermute | solution.py:33
  13.7 2.5 %collective-permute-start.2 = (bf16[576,256]{1,0:T(8,128)(2,1)}, bf16[576,256]{1,0:T(8,128)(2,1)S(1)}, u32[]{:S(2)}, u32[]{:S(2)}) collective-permute-start(bf16[576,256]{1,0:T(8,128)(2,1)} %get-tuple-element.45), channel_id=1, source_target_pairs={{0,1},{1,0},{2,3},{3,2},{4,5},{5,4},{6,7},{7,6},{8,9},{9,8},{10,11... | collective-permute-start | bytes 884744 | tf_op jit(solution)/shard_map/ppermute | solution.py:38
  16.1 2.6 %collective-permute-start.3 = (bf16[576,256]{1,0:T(8,128)(2,1)}, bf16[576,256]{1,0:T(8,128)(2,1)S(1)}, u32[]{:S(2)}, u32[]{:S(2)}) collective-permute-start(bf16[576,256]{1,0:T(8,128)(2,1)} %get-tuple-element.46), channel_id=1, source_target_pairs={{0,2},{1,3},{2,0},{3,1},{4,6},{5,7},{6,4},{7,5},{8,10},{9,11},{10,... | collective-permute-start | bytes 884744 | tf_op jit(solution)/shard_map/ppermute | solution.py:38
  18.7 0.0 collective-permute-start.4
  18.7 0.0 collective-permute-done.low
  18.7 0.0 collective-permute-done.1.high
  18.7 0.7 copy-done.3
  19.5 0.1 copy-done.4
  19.5 2.8 %patch.1 = (bf16[14,128,256]{2,1,0:T(8,128)(2,1)}, bf16[16,128,256]{2,1,0:T(8,128)(2,1)}) custom-call(s32[2]{0:T(128)} %pad_add_fusion.me.index, s32[112]{0:T(128)} %shuffle.3, bf16[14,128,256]{2,1,0:T(8,128)(2,1)} %get-tuple-element.38.clean, bf16[16,128,256]{2,1,0:T(8,128)(2,1)} %get-tuple-element.39.outgoing, ...), custom_call_target="tpu_custom_call", output_to_operand_aliasing={{0}: (2, {}), {1}: (3, {})} | custom-call | tf_op jit(solution)/shard_map/patch/pallas_call | solution.py:261
  22.4 0.0 copy-start
  22.4 7.8 %all-to-all-start = ((bf16[16,128,256]{2,1,0:T(8,128)(2,1)}), bf16[16,128,256]{2,1,0:T(8,128)(2,1)S(1)}, u32[]{:S(2)}, u32[]{:S(2)}) async-start(bf16[16,128,256]{2,1,0:T(8,128)(2,1)} %get-tuple-element.43), calls=%async_computation | async-start | bytes 2097152 | tf_op jit(solution)/shard_map/all_to_all | solution.py:42
  30.3 0.1 eq.30
  30.4 0.1 add.45
  30.5 0.3 convert_reduce_fusion
  30.8 0.1 copy.15
  30.9 0.1 select_reduce_fusion
  31.0 0.1 copy.16
  31.1 0.1 sub.13.landing
  31.2 0.0 collective-permute-done.2.refs_1_
  31.2 0.0 collective-permute-done.3.refs_2_
  31.2 6.6 %collective-permute-done.4.refs_3_ = bf16[576,256]{1,0:T(8,128)(2,1)S(1)} collective-permute-done((bf16[576,256]{1,0:T(8,128)(2,1)}, bf16[576,256]{1,0:T(8,128)(2,1)S(1)}, u32[]{:S(2)}, u32[]{:S(2)}) %collective-permute-start.4) | collective-permute-done | bytes 294944 | tf_op jit(solution)/shard_map/ppermute | solution.py:38
  37.9 7.8 %all-to-all-done.incoming = bf16[16,128,256]{2,1,0:T(8,128)(2,1)S(1)} async-done(((bf16[16,128,256]{2,1,0:T(8,128)(2,1)}), bf16[16,128,256]{2,1,0:T(8,128)(2,1)S(1)}, u32[]{:S(2)}, u32[]{:S(2)}) %all-to-all-start) | async-done | bytes 1048608 | tf_op jit(solution)/shard_map/all_to_all | solution.py:42
  45.7 0.9 merge.1
  46.6 0.1 slice_bitcast_fusion.4
  46.6 3.7 %collective-permute-start.7 = (bf16[448,256]{1,0:T(8,128)(2,1)S(1)}, bf16[448,256]{1,0:T(8,128)(2,1)S(1)}, u32[]{:S(2)}, u32[]{:S(2)}) collective-permute-start(bf16[448,256]{1,0:T(8,128)(2,1)S(1)} %get-tuple-element.89), channel_id=1, source_target_pairs={{0,3},{1,2},{2,1},{3,0},{4,7},{5,6},{6,5},{7,4},{8,11},{9,10},{10,... | collective-permute-start | bytes 688136 | tf_op jit(solution)/shard_map/ppermute | solution.py:38
  50.4 1.1 collective-permute-start.9
  51.4 0.2 collective-permute-start.8
  51.6 2.3 %collective-permute-start.10 = (bf16[4,128,256]{2,1,0:T(8,128)(2,1)S(1)}, bf16[4,128,256]{2,1,0:T(8,128)(2,1)S(1)}, u32[]{:S(2)}, u32[]{:S(2)}) collective-permute-start(bf16[4,128,256]{2,1,0:T(8,128)(2,1)S(1)} %pad_maximum_fusion.1), channel_id=1, source_target_pairs={{0,24},{4,28},{8,16},{12,20},{16,8},{20,12},{24,0},{28,4},{1,25},{... | collective-permute-start | bytes 786440 | tf_op jit(solution)/shard_map/ppermute | solution.py:38
  53.9 0.0 collective-permute-start.6
  54.0 1.8 %collective-permute-done.7.refs_7_.refs_3_ = bf16[448,256]{1,0:T(8,128)(2,1)S(1)} collective-permute-done((bf16[448,256]{1,0:T(8,128)(2,1)S(1)}, bf16[448,256]{1,0:T(8,128)(2,1)S(1)}, u32[]{:S(2)}, u32[]{:S(2)}) %collective-permute-start.7) | collective-permute-done | bytes 229408 | tf_op jit(solution)/shard_map/ppermute | solution.py:38
  55.7 8.1 %collective-permute-start.5 = (bf16[448,256]{1,0:T(8,128)(2,1)S(1)}, bf16[448,256]{1,0:T(8,128)(2,1)S(1)}, u32[]{:S(2)}, u32[]{:S(2)}) collective-permute-start(bf16[448,256]{1,0:T(8,128)(2,1)S(1)} %get-tuple-element.91), channel_id=1, source_target_pairs={{0,1},{1,0},{2,3},{3,2},{4,5},{5,4},{6,7},{7,6},{8,9},{9,8},{10,11... | collective-permute-start | bytes 688136 | tf_op jit(solution)/shard_map/ppermute | solution.py:38
  63.8 4.1 %collective-permute-done.6.refs_6_.refs_2_ = bf16[448,256]{1,0:T(8,128)(2,1)S(1)} collective-permute-done((bf16[448,256]{1,0:T(8,128)(2,1)S(1)}, bf16[448,256]{1,0:T(8,128)(2,1)S(1)}, u32[]{:S(2)}, u32[]{:S(2)}) %collective-permute-start.6) | collective-permute-done | bytes 229408 | tf_op jit(solution)/shard_map/ppermute | solution.py:38
  68.0 4.8 %collective-permute-done.5.refs_5_.refs_1_ = bf16[448,256]{1,0:T(8,128)(2,1)S(1)} collective-permute-done((bf16[448,256]{1,0:T(8,128)(2,1)S(1)}, bf16[448,256]{1,0:T(8,128)(2,1)S(1)}, u32[]{:S(2)}, u32[]{:S(2)}) %collective-permute-start.5) | collective-permute-done | bytes 229408 | tf_op jit(solution)/shard_map/ppermute | solution.py:38
  72.8 0.0 collective-permute-done.8
  72.8 0.0 collective-permute-done.10
  72.8 0.1 pad_maximum_fusion.refs_4_
  73.0 0.1 collective-permute-start.11
  73.1 2.7 %weight_partial.1 = (bf16[4,4,128,256]{3,2,1,0:T(8,128)(2,1)S(1)}, bf16[4,4,128,256]{3,2,1,0:T(8,128)(2,1)S(1)}) custom-call(s32[2]{0:T(128)S(1)} %copy-done.2, bf16[576,256]{1,0:T(8,128)(2,1)S(1)} %copy-done.1, bf16[576,256]{1,0:T(8,128)(2,1)S(1)} %collective-permute-done.2.refs_1_, bf16[576,256]{1,0:T(8,128)(2,1)S(1)} %collective-permute-done.3.refs_2_, ...), custom_call_target="tpu_custom_call" | custom-call | flops 939524096 | bytes 3932160 | tf_op jit(solution)/shard_map/weight_partial/pallas_call | solution.py:342
  75.7 0.0 collective-permute-done.11.refs_5_
  75.7 0.5 collective-permute-start.12
  76.3 3.2 %feature_rows.1 = bf16[4,448,256]{2,1,0:T(8,128)(2,1)S(1)} custom-call(s32[2]{0:T(128)S(1)} %copy-done.2, bf16[448,256]{1,0:T(8,128)(2,1)S(1)} %get-tuple-element.55.refs_4_.refs_0_, bf16[448,256]{1,0:T(8,128)(2,1)S(1)} %collective-permute-done.5.refs_5_.refs_1_, bf16[448,256]{1,0:T(8,128)(2,1)S(1)} %collective-permute-done.6.refs_6_.refs_2_, ...), custom_call_target="tpu_custom_call" | custom-call | flops 939524096 | bytes 3932160 | tf_op jit(solution)/shard_map/feature_rows/pallas_call | solution.py:390
  79.5 0.0 collective-permute-done.12
  79.5 3.6 %collective-permute-start.15 = (bf16[336,256]{1,0:T(8,128)(2,1)S(1)}, bf16[336,256]{1,0:T(8,128)(2,1)S(1)}, u32[]{:S(2)}, u32[]{:S(2)}) collective-permute-start(bf16[336,256]{1,0:T(8,128)(2,1)S(1)} %get-tuple-element.86), channel_id=1, source_target_pairs={{0,3},{1,2},{2,1},{3,0},{4,7},{5,6},{6,5},{7,4},{8,11},{9,10},{10,... | collective-permute-start | bytes 516104 | tf_op jit(solution)/shard_map/ppermute | solution.py:38
  83.2 0.3 convert_add_fusion
  83.5 0.1 slice_bitcast_fusion.1
  83.6 0.1 collective-permute-start.18
  83.6 2.6 %collective-permute-start.17 = (bf16[4,128,256]{2,1,0:T(8,128)(2,1)S(1)}, bf16[4,128,256]{2,1,0:T(8,128)(2,1)S(1)}, u32[]{:S(2)}, u32[]{:S(2)}) collective-permute-start(bf16[4,128,256]{2,1,0:T(8,128)(2,1)S(1)} %get-tuple-element.79), channel_id=1, source_target_pairs={{0,16},{4,20},{8,24},{12,28},{16,0},{20,4},{24,8},{28,12},{1,17},{... | collective-permute-start | bytes 786440 | tf_op jit(solution)/shard_map/ppermute | solution.py:38
  86.2 0.9 collective-permute-start.16
  87.1 0.7 collective-permute-done.15.refs_3_
  87.9 6.5 %collective-permute-start.13 = (bf16[336,256]{1,0:T(8,128)(2,1)S(1)}, bf16[336,256]{1,0:T(8,128)(2,1)S(1)}, u32[]{:S(2)}, u32[]{:S(2)}) collective-permute-start(bf16[336,256]{1,0:T(8,128)(2,1)S(1)} %get-tuple-element.88), channel_id=1, source_target_pairs={{0,1},{1,0},{2,3},{3,2},{4,5},{5,4},{6,7},{7,6},{8,9},{9,8},{10,11... | collective-permute-start | bytes 516104 | tf_op jit(solution)/shard_map/ppermute | solution.py:38
  94.4 2.6 %collective-permute-done.14.refs_2_ = bf16[336,256]{1,0:T(8,128)(2,1)S(1)} collective-permute-done((bf16[336,256]{1,0:T(8,128)(2,1)S(1)}, bf16[336,256]{1,0:T(8,128)(2,1)S(1)}, u32[]{:S(2)}, u32[]{:S(2)}) %collective-permute-start.14) | collective-permute-done | bytes 172064 | tf_op jit(solution)/shard_map/ppermute | solution.py:38
  97.0 3.6 %collective-permute-done.13.refs_1_ = bf16[336,256]{1,0:T(8,128)(2,1)S(1)} collective-permute-done((bf16[336,256]{1,0:T(8,128)(2,1)S(1)}, bf16[336,256]{1,0:T(8,128)(2,1)S(1)}, u32[]{:S(2)}, u32[]{:S(2)}) %collective-permute-start.13) | collective-permute-done | bytes 172064 | tf_op jit(solution)/shard_map/ppermute | solution.py:38
  100.6 0.0 collective-permute-done.18
  100.6 0.2 fusion.10
  100.8 0.6 collective-permute-start.20
  101.4 0.9 collective-permute-start.21
  102.3 3.1 %collective-permute-start.19 = (bf16[240,256]{1,0:T(8,128)(2,1)S(1)}, bf16[240,256]{1,0:T(8,128)(2,1)S(1)}, u32[]{:S(2)}, u32[]{:S(2)}) collective-permute-start(bf16[240,256]{1,0:T(8,128)(2,1)S(1)} %pad_maximum_fusion.2), channel_id=1, source_target_pairs={{0,3},{1,2},{2,1},{3,0},{4,7},{5,6},{6,5},{7,4},{8,11},{9,10},{10,... | collective-permute-start | bytes 368648 | tf_op jit(solution)/shard_map/ppermute | solution.py:38
  105.4 6.0 %collective-permute-done.20.refs_6_ = bf16[240,256]{1,0:T(8,128)(2,1)S(1)} collective-permute-done((bf16[240,256]{1,0:T(8,128)(2,1)S(1)}, bf16[240,256]{1,0:T(8,128)(2,1)S(1)}, u32[]{:S(2)}, u32[]{:S(2)}) %collective-permute-start.20) | collective-permute-done | bytes 122912 | tf_op jit(solution)/shard_map/ppermute | solution.py:38
  111.4 0.1 collective-permute-done.21.refs_5_
  111.5 0.7 fusion.5
  112.2 1.5 %laid_out.1 = bf16[1792,256]{1,0:T(8,128)(2,1)} custom-call(s32[2]{0:T(128)S(1)} %copy-done.2, bf16[336,256]{1,0:T(8,128)(2,1)S(1)} %get-tuple-element.85.refs_0_, bf16[336,256]{1,0:T(8,128)(2,1)S(1)} %collective-permute-done.13.refs_1_, bf16[336,256]{1,0:T(8,128)(2,1)S(1)} %collective-permute-done.14.refs_2_, ...), custom_call_target="tpu_custom_call" | custom-call | tf_op jit(solution)/shard_map/laid_out/pallas_call | solution.py:428
  (27 shorter events, 0.2 us)
Async XLA Ops:
  10.0 8.7 %collective-permute-start = (bf16[2,2,128,256]{3,2,1,0:T(8,128)(2,1)}, bf16[2,2,128,256]{3,2,1,0:T(8,128)(2,1)S(1)}, u32[]{:S(2)}, u32[]{:S(2)}) collective-permute-start(bf16[2,2,128,256]{3,2,1,0:T(8,128)(2,1)} %get-tuple-element.40), channel_id=1, source_target_pairs={{0,4},{4,8},{8,12},{12,16},{16,20},{20,24},{24,28},{1,5},{5,9},{9,... | collective-permute-start | bytes 786440 | tf_op jit(solution)/shard_map/ppermute | solution.py:33
  12.4 6.4 %collective-permute-start.1 = (bf16[2,2,128,256]{3,2,1,0:T(8,128)(2,1)}, bf16[2,2,128,256]{3,2,1,0:T(8,128)(2,1)S(1)}, u32[]{:S(2)}, u32[]{:S(2)}) collective-permute-start(bf16[2,2,128,256]{3,2,1,0:T(8,128)(2,1)} %get-tuple-element.41), channel_id=1, source_target_pairs={{4,0},{8,4},{12,8},{16,12},{20,16},{24,20},{28,24},{5,1},{9,5},{13... | collective-permute-start | bytes 786440 | tf_op jit(solution)/shard_map/ppermute | solution.py:33
  13.7 17.6 %collective-permute-start.2 = (bf16[576,256]{1,0:T(8,128)(2,1)}, bf16[576,256]{1,0:T(8,128)(2,1)S(1)}, u32[]{:S(2)}, u32[]{:S(2)}) collective-permute-start(bf16[576,256]{1,0:T(8,128)(2,1)} %get-tuple-element.45), channel_id=1, source_target_pairs={{0,1},{1,0},{2,3},{3,2},{4,5},{5,4},{6,7},{7,6},{8,9},{9,8},{10,11... | collective-permute-start | bytes 884744 | tf_op jit(solution)/shard_map/ppermute | solution.py:38
  16.1 15.1 %collective-permute-start.3 = (bf16[576,256]{1,0:T(8,128)(2,1)}, bf16[576,256]{1,0:T(8,128)(2,1)S(1)}, u32[]{:S(2)}, u32[]{:S(2)}) collective-permute-start(bf16[576,256]{1,0:T(8,128)(2,1)} %get-tuple-element.46), channel_id=1, source_target_pairs={{0,2},{1,3},{2,0},{3,1},{4,6},{5,7},{6,4},{7,5},{8,10},{9,11},{10,... | collective-permute-start | bytes 884744 | tf_op jit(solution)/shard_map/ppermute | solution.py:38
  18.7 19.1 %collective-permute-start.4 = (bf16[576,256]{1,0:T(8,128)(2,1)}, bf16[576,256]{1,0:T(8,128)(2,1)S(1)}, u32[]{:S(2)}, u32[]{:S(2)}) collective-permute-start(bf16[576,256]{1,0:T(8,128)(2,1)} %get-tuple-element.47), channel_id=1, source_target_pairs={{0,3},{1,2},{2,1},{3,0},{4,7},{5,6},{6,5},{7,4},{8,11},{9,10},{10,... | collective-permute-start | bytes 884744 | tf_op jit(solution)/shard_map/ppermute | solution.py:38
  18.7 0.7 copy-start.3
  18.7 0.8 copy-start.4
  19.5 10.7 %copy-start.5 = (s32[112]{0:T(128)S(1)}, s32[112]{0:T(128)}, u32[]{:S(2)}) copy-start(s32[112]{0:T(128)} %shuffle.3) | copy-start | bytes 1348
  19.5 26.1 %copy-start.2 = (s32[2]{0:T(128)S(1)}, s32[2]{0:T(128)}, u32[]{:S(2)}) copy-start(s32[2]{0:T(128)} %pad_add_fusion.me.index) | copy-start | bytes 28
  22.4 23.3 %copy-start = (bf16[14,128,256]{2,1,0:T(8,128)(2,1)S(1)}, bf16[14,128,256]{2,1,0:T(8,128)(2,1)}, u32[]{:S(2)}) copy-start(bf16[14,128,256]{2,1,0:T(8,128)(2,1)} %get-tuple-element.53.clean) | copy-start | bytes 2752516
  22.4 23.3 %all-to-all-start = ((bf16[16,128,256]{2,1,0:T(8,128)(2,1)}), bf16[16,128,256]{2,1,0:T(8,128)(2,1)S(1)}, u32[]{:S(2)}, u32[]{:S(2)}) async-start(bf16[16,128,256]{2,1,0:T(8,128)(2,1)} %get-tuple-element.43), calls=%async_computation | async-start | bytes 2097152 | tf_op jit(solution)/shard_map/all_to_all | solution.py:42
  45.7 4.7 %copy-start.1 = (bf16[576,256]{1,0:T(8,128)(2,1)S(1)}, bf16[576,256]{1,0:T(8,128)(2,1)}, u32[]{:S(2)}) copy-start(bf16[576,256]{1,0:T(8,128)(2,1)} %get-tuple-element.48.refs_0_) | copy-start | bytes 884740
  46.6 9.1 %collective-permute-start.7 = (bf16[448,256]{1,0:T(8,128)(2,1)S(1)}, bf16[448,256]{1,0:T(8,128)(2,1)S(1)}, u32[]{:S(2)}, u32[]{:S(2)}) collective-permute-start(bf16[448,256]{1,0:T(8,128)(2,1)S(1)} %get-tuple-element.89), channel_id=1, source_target_pairs={{0,3},{1,2},{2,1},{3,0},{4,7},{5,6},{6,5},{7,4},{8,11},{9,10},{10,... | collective-permute-start | bytes 688136 | tf_op jit(solution)/shard_map/ppermute | solution.py:38
  50.4 22.4 %collective-permute-start.9 = (bf16[4,128,256]{2,1,0:T(8,128)(2,1)S(1)}, bf16[4,128,256]{2,1,0:T(8,128)(2,1)S(1)}, u32[]{:S(2)}, u32[]{:S(2)}) collective-permute-start(bf16[4,128,256]{2,1,0:T(8,128)(2,1)S(1)} %pad_maximum_fusion.1), channel_id=1, source_target_pairs={{0,16},{4,20},{8,24},{12,28},{16,0},{20,4},{24,8},{28,12},{1,17},{... | collective-permute-start | bytes 786440 | tf_op jit(solution)/shard_map/ppermute | solution.py:38
  51.4 21.4 %collective-permute-start.8 = (bf16[4,128,256]{2,1,0:T(8,128)(2,1)S(1)}, bf16[4,128,256]{2,1,0:T(8,128)(2,1)S(1)}, u32[]{:S(2)}, u32[]{:S(2)}) collective-permute-start(bf16[4,128,256]{2,1,0:T(8,128)(2,1)S(1)} %pad_maximum_fusion.1), channel_id=1, source_target_pairs={{0,8},{4,12},{8,0},{12,4},{16,24},{20,28},{24,16},{28,20},{1,9},{5... | collective-permute-start | bytes 786440 | tf_op jit(solution)/shard_map/ppermute | solution.py:38
  51.6 21.2 %collective-permute-start.10 = (bf16[4,128,256]{2,1,0:T(8,128)(2,1)S(1)}, bf16[4,128,256]{2,1,0:T(8,128)(2,1)S(1)}, u32[]{:S(2)}, u32[]{:S(2)}) collective-permute-start(bf16[4,128,256]{2,1,0:T(8,128)(2,1)S(1)} %pad_maximum_fusion.1), channel_id=1, source_target_pairs={{0,24},{4,28},{8,16},{12,20},{16,8},{20,12},{24,0},{28,4},{1,25},{... | collective-permute-start | bytes 786440 | tf_op jit(solution)/shard_map/ppermute | solution.py:38
  53.9 14.0 %collective-permute-start.6 = (bf16[448,256]{1,0:T(8,128)(2,1)S(1)}, bf16[448,256]{1,0:T(8,128)(2,1)S(1)}, u32[]{:S(2)}, u32[]{:S(2)}) collective-permute-start(bf16[448,256]{1,0:T(8,128)(2,1)S(1)} %get-tuple-element.90), channel_id=1, source_target_pairs={{0,2},{1,3},{2,0},{3,1},{4,6},{5,7},{6,4},{7,5},{8,10},{9,11},{10,... | collective-permute-start | bytes 688136 | tf_op jit(solution)/shard_map/ppermute | solution.py:38
  55.7 17.1 %collective-permute-start.5 = (bf16[448,256]{1,0:T(8,128)(2,1)S(1)}, bf16[448,256]{1,0:T(8,128)(2,1)S(1)}, u32[]{:S(2)}, u32[]{:S(2)}) collective-permute-start(bf16[448,256]{1,0:T(8,128)(2,1)S(1)} %get-tuple-element.91), channel_id=1, source_target_pairs={{0,1},{1,0},{2,3},{3,2},{4,5},{5,4},{6,7},{7,6},{8,9},{9,8},{10,11... | collective-permute-start | bytes 688136 | tf_op jit(solution)/shard_map/ppermute | solution.py:38
  73.0 2.8 %collective-permute-start.11 = (bf16[4,4,128,256]{3,2,1,0:T(8,128)(2,1)S(1)}, bf16[4,4,128,256]{3,2,1,0:T(8,128)(2,1)S(1)}, u32[]{:S(2)}, u32[]{:S(2)}) collective-permute-start(bf16[4,4,128,256]{3,2,1,0:T(8,128)(2,1)S(1)} %pad_maximum_fusion.refs_4_), channel_id=1, source_target_pairs={{0,4},{4,0},{8,12},{12,8},{16,20},{20,16},{24,28},{28,24},{1,5},{5... | collective-permute-start | bytes 3145736 | tf_op jit(solution)/shard_map/ppermute | solution.py:38
  75.7 3.8 %collective-permute-start.12 = (bf16[4,4,128,256]{3,2,1,0:T(8,128)(2,1)S(1)}, bf16[4,4,128,256]{3,2,1,0:T(8,128)(2,1)S(1)}, u32[]{:S(2)}, u32[]{:S(2)}) collective-permute-start(bf16[4,4,128,256]{3,2,1,0:T(8,128)(2,1)S(1)} %get-tuple-element.64), channel_id=1, source_target_pairs={{0,4},{4,0},{8,12},{12,8},{16,20},{20,16},{24,28},{28,24},{1,5},{5... | collective-permute-start | bytes 3145736 | tf_op jit(solution)/shard_map/ppermute | solution.py:38
  79.5 8.3 %collective-permute-start.15 = (bf16[336,256]{1,0:T(8,128)(2,1)S(1)}, bf16[336,256]{1,0:T(8,128)(2,1)S(1)}, u32[]{:S(2)}, u32[]{:S(2)}) collective-permute-start(bf16[336,256]{1,0:T(8,128)(2,1)S(1)} %get-tuple-element.86), channel_id=1, source_target_pairs={{0,3},{1,2},{2,1},{3,0},{4,7},{5,6},{6,5},{7,4},{8,11},{9,10},{10,... | collective-permute-start | bytes 516104 | tf_op jit(solution)/shard_map/ppermute | solution.py:38
  83.6 17.0 %collective-permute-start.18 = (bf16[4,128,256]{2,1,0:T(8,128)(2,1)S(1)}, bf16[4,128,256]{2,1,0:T(8,128)(2,1)S(1)}, u32[]{:S(2)}, u32[]{:S(2)}) collective-permute-start(bf16[4,128,256]{2,1,0:T(8,128)(2,1)S(1)} %get-tuple-element.78), channel_id=1, source_target_pairs={{0,24},{4,28},{8,16},{12,20},{16,8},{20,12},{24,0},{28,4},{1,25},{... | collective-permute-start | bytes 786440 | tf_op jit(solution)/shard_map/ppermute | solution.py:38
  83.6 16.9 %collective-permute-start.17 = (bf16[4,128,256]{2,1,0:T(8,128)(2,1)S(1)}, bf16[4,128,256]{2,1,0:T(8,128)(2,1)S(1)}, u32[]{:S(2)}, u32[]{:S(2)}) collective-permute-start(bf16[4,128,256]{2,1,0:T(8,128)(2,1)S(1)} %get-tuple-element.79), channel_id=1, source_target_pairs={{0,16},{4,20},{8,24},{12,28},{16,0},{20,4},{24,8},{28,12},{1,17},{... | collective-permute-start | bytes 786440 | tf_op jit(solution)/shard_map/ppermute | solution.py:38
  86.2 14.3 %collective-permute-start.16 = (bf16[4,128,256]{2,1,0:T(8,128)(2,1)S(1)}, bf16[4,128,256]{2,1,0:T(8,128)(2,1)S(1)}, u32[]{:S(2)}, u32[]{:S(2)}) collective-permute-start(bf16[4,128,256]{2,1,0:T(8,128)(2,1)S(1)} %get-tuple-element.80), channel_id=1, source_target_pairs={{0,8},{4,12},{8,0},{12,4},{16,24},{20,28},{24,16},{28,20},{1,9},{5... | collective-permute-start | bytes 786440 | tf_op jit(solution)/shard_map/ppermute | solution.py:38
  87.1 9.9 %collective-permute-start.14 = (bf16[336,256]{1,0:T(8,128)(2,1)S(1)}, bf16[336,256]{1,0:T(8,128)(2,1)S(1)}, u32[]{:S(2)}, u32[]{:S(2)}) collective-permute-start(bf16[336,256]{1,0:T(8,128)(2,1)S(1)} %get-tuple-element.87), channel_id=1, source_target_pairs={{0,2},{1,3},{2,0},{3,1},{4,6},{5,7},{6,4},{7,5},{8,10},{9,11},{10,... | collective-permute-start | bytes 516104 | tf_op jit(solution)/shard_map/ppermute | solution.py:38
  87.9 12.7 %collective-permute-start.13 = (bf16[336,256]{1,0:T(8,128)(2,1)S(1)}, bf16[336,256]{1,0:T(8,128)(2,1)S(1)}, u32[]{:S(2)}, u32[]{:S(2)}) collective-permute-start(bf16[336,256]{1,0:T(8,128)(2,1)S(1)} %get-tuple-element.88), channel_id=1, source_target_pairs={{0,1},{1,0},{2,3},{3,2},{4,5},{5,4},{6,7},{7,6},{8,9},{9,8},{10,11... | collective-permute-start | bytes 516104 | tf_op jit(solution)/shard_map/ppermute | solution.py:38
  100.8 10.6 %collective-permute-start.20 = (bf16[240,256]{1,0:T(8,128)(2,1)S(1)}, bf16[240,256]{1,0:T(8,128)(2,1)S(1)}, u32[]{:S(2)}, u32[]{:S(2)}) collective-permute-start(bf16[240,256]{1,0:T(8,128)(2,1)S(1)} %pad_maximum_fusion.3), channel_id=1, source_target_pairs={{0,2},{1,3},{2,0},{3,1},{4,6},{5,7},{6,4},{7,5},{8,10},{9,11},{10,... | collective-permute-start | bytes 368648 | tf_op jit(solution)/shard_map/ppermute | solution.py:38
  101.4 10.2 %collective-permute-start.21 = (bf16[240,256]{1,0:T(8,128)(2,1)S(1)}, bf16[240,256]{1,0:T(8,128)(2,1)S(1)}, u32[]{:S(2)}, u32[]{:S(2)}) collective-permute-start(bf16[240,256]{1,0:T(8,128)(2,1)S(1)} %pad_maximum_fusion.4), channel_id=1, source_target_pairs={{0,1},{1,0},{2,3},{3,2},{4,5},{5,4},{6,7},{7,6},{8,9},{9,8},{10,11... | collective-permute-start | bytes 368648 | tf_op jit(solution)/shard_map/ppermute | solution.py:38
  102.3 9.2 %collective-permute-start.19 = (bf16[240,256]{1,0:T(8,128)(2,1)S(1)}, bf16[240,256]{1,0:T(8,128)(2,1)S(1)}, u32[]{:S(2)}, u32[]{:S(2)}) collective-permute-start(bf16[240,256]{1,0:T(8,128)(2,1)S(1)} %pad_maximum_fusion.2), channel_id=1, source_target_pairs={{0,3},{1,2},{2,1},{3,0},{4,7},{5,6},{6,5},{7,4},{8,11},{9,10},{10,... | collective-permute-start | bytes 368648 | tf_op jit(solution)/shard_map/ppermute | solution.py:38

commit v7 on v6

v7 whole, which is shorter than its diff:
```python
import functools
import math

import jax
import jax.numpy as jnp
from jax import lax
from jax.experimental import pallas as pl
from jax.experimental.pallas import tpu as pltpu
from jax.sharding import PartitionSpec as P

VMEM_LIMIT = 32 * 1024 * 1024
VMEM_ALL = 61 * 1024 * 1024
IN_VMEM = pl.BlockSpec(memory_space=pltpu.VMEM)
IN_SMEM = pl.BlockSpec(memory_space=pltpu.SMEM)
IN_HBM = pl.BlockSpec(memory_space=pltpu.HBM)


def params(limit=VMEM_LIMIT):
    return pltpu.CompilerParams(vmem_limit_bytes=limit)


def bf16(*shape):
    return jax.ShapeDtypeStruct(shape, jnp.bfloat16)


def wide(value):
    return value.astype(jnp.float32)


def shifted(value, axis, by):
    size = lax.axis_size(axis)
    pairs = [(i, i + by) for i in range(size) if 0 <= i + by < size]
    return lax.ppermute(value, axis, pairs)


def swapped(value, axis, by):
    size = lax.axis_size(axis)
    return lax.ppermute(value, axis, [(i, i ^ by) for i in range(size)])


def exchanged(value, axis):
    return lax.all_to_all(value, axis, split_axis=0, concat_axis=0, tiled=True)


def masked_grad(grad, pre, slope):
    return (wide(grad) * jnp.where(wide(pre) > 0, 1.0, slope)).astype(jnp.bfloat16)


def find_places(index, shuffle, blocks, slots, places, used):
    for i in range(used.shape[0]):
        used[i] = 0
    for block in range(blocks):
        owner = shuffle[index[0] * blocks + block] // blocks
        slot = used[owner]
        used[owner] = slot + 1
        places[block] = owner * slots + slot


def identity_of(size):
    shape = (size, size)
    same = lax.broadcasted_iota(jnp.int32, shape, 0) == lax.broadcasted_iota(jnp.int32, shape, 1)
    return same.astype(jnp.float32).astype(jnp.bfloat16)


def both_grads(data, block, slope):
    return jnp.concatenate(
        [masked_grad(data[i, block], data[i + 1, block], slope) for i in (0, 2)], axis=1
    )


def turned_tiles(identity, tiles):
    slots, rows, _ = tiles.shape
    return lax.dot_general(
        identity,
        tiles.reshape(slots * rows, rows),
        (((1,), (1,)), ((), ())),
        preferred_element_type=jnp.float32,
    )


def border_kernel(reach, groups, index, cols, count, gc, pc, gx, px, slopes, adj, features, weight, *refs):
    down, up, *refs = refs
    packed, refs = refs[:groups], refs[groups:]
    data, tiles, rhs, stage, halos, packs, held, sems, tile_sems, pack_sems, out_sems = refs
    blocks, slots, rows, _ = adj.shape
    quarter = features.shape[0] // groups
    height, width = weight.shape
    spare = 2 * reach
    border = [*range(reach), *range(blocks - reach, blocks)]

    def target_of(block, k):
        target = cols[k, block] - index[0] * blocks
        outside = (k < count[block]) & ((target < 0) | (target >= blocks))
        return outside, jnp.where(target < 0, target + reach, target - blocks + reach)

    def each_tile(i, act):
        for k in range(slots):
            copy = pltpu.make_async_copy(adj.at[border[i], k], tiles.at[i, k], tile_sems.at[i, k])
            pl.when(target_of(border[i], k)[0])(functools.partial(act, copy))

    inputs = []
    for i, block in enumerate(border):
        for j, ref in enumerate((gc, pc, gx, px)):
            source = ref.at[block * rows : (block + 1) * rows]
            inputs.append(pltpu.make_async_copy(source, data.at[j, i], sems.at[j, i]))
    for copy in inputs:
        copy.start()
    for i in range(2 * reach):
        each_tile(i, lambda copy: copy.start())
    to_vmem, to_hbm = [pltpu.make_async_copy(weight, held, pack_sems.at[1, 0])], []
    for i in range(groups):
        span = pl.ds(pl.multiple_of((index[1] ^ i) * quarter, quarter), quarter)
        to_vmem.append(
            pltpu.make_async_copy(features.at[span], packs.at[i, :quarter], pack_sems.at[0, i])
        )
        to_hbm.append(pltpu.make_async_copy(packs.at[i], packed[i], pack_sems.at[2, i]))
    for copy in to_vmem:
        copy.start()

    stage[...] = jnp.zeros_like(stage)
    identity = identity_of(rows)
    slope = slopes[...]
    for copy in inputs:
        copy.wait()
    for i in range(2 * reach):
        each_tile(i, lambda copy: copy.wait())
    for i in range(2 * reach):
        rhs[i * rows : (i + 1) * rows] = both_grads(data, i, slope)
        turned = turned_tiles(identity, tiles[i])
        for k in range(slots):
            outside, place = target_of(border[i], k)
            place = jnp.where(outside, place, spare)
            part = turned[:, k * rows : (k + 1) * rows]
            stage[place, i % reach] = (wide(stage[place, i % reach]) + part).astype(jnp.bfloat16)
    writes = []
    for side, out in enumerate((down, up)):
        lhs = jnp.concatenate(
            [
                jnp.concatenate([stage[side * reach + t, j] for j in range(reach)], axis=1)
                for t in range(reach)
            ],
            axis=0,
        )
        span = slice(side * reach * rows, (side + 1) * reach * rows)
        product = jnp.dot(lhs, rhs[span], preferred_element_type=jnp.float32)
        product = product.astype(jnp.bfloat16).reshape(reach, rows, 2 * width)
        halos[side, 0] = product[:, :, :width]
        halos[side, 1] = product[:, :, width:]
        writes.append(pltpu.make_async_copy(halos.at[side], out, out_sems.at[side]))
        writes[-1].start()

    for copy in to_vmem:
        copy.wait()
    turned = wide(held[...]).T.astype(jnp.bfloat16)
    tile = jnp.concatenate(
        [turned[i * height : (i + 1) * height] for i in range(width // height)], axis=1
    )
    for i in range(groups):
        packs[i, quarter:] = tile
        to_hbm[i].start()
    for copy in writes + to_hbm:
        copy.wait()


def border(index, cols, count, gc, pc, gx, px, slopes, adj, features, weight, reach, groups):
    _, slots, rows, _ = adj.shape
    width = gc.shape[1]
    packed = features.shape[0] // groups + weight.shape[0]
    return pl.pallas_call(
        functools.partial(border_kernel, reach, groups),
        in_specs=[IN_SMEM] * 3 + [IN_HBM] * 4 + [IN_VMEM] + [IN_HBM] * 3,
        out_specs=[IN_HBM] * (2 + groups),
        out_shape=[bf16(2, reach, rows, width)] * 2 + [bf16(packed, width)] * groups,
        scratch_shapes=[
            pltpu.VMEM((4, 2 * reach, rows, width), jnp.bfloat16),
            pltpu.VMEM((2 * reach, slots, rows, rows), jnp.bfloat16),
            pltpu.VMEM((2 * reach * rows, 2 * width), jnp.bfloat16),
            pltpu.VMEM((2 * reach + 1, reach, rows, rows), jnp.bfloat16),
            pltpu.VMEM((2, 2, reach, rows, width), jnp.bfloat16),
            pltpu.VMEM((groups, packed, width), jnp.bfloat16),
            pltpu.VMEM(weight.shape, jnp.bfloat16),
            pltpu.SemaphoreType.DMA((4, 2 * reach)),
            pltpu.SemaphoreType.DMA((2 * reach, slots)),
            pltpu.SemaphoreType.DMA((3, groups)),
            pltpu.SemaphoreType.DMA((2,)),
        ],
        compiler_params=params(VMEM_ALL),
        name="border",
    )(index, cols, count, gc, pc, gx, px, slopes, adj, features, weight)


def inner_kernel(
    reach, send_slots, index, shuffle, cols, count, gc, pc, gx, px, slopes, adj, clean, outgoing, *refs
):
    data, tiles, rhs, stage, results, places, used, sems, tile_sems, out_sems = refs
    blocks, slots, rows, _ = adj.shape
    width = gc.shape[1]
    pad = reach * rows

    def copies(block):
        span = pl.ds(pl.multiple_of(block * rows, rows), rows)
        return [
            pltpu.make_async_copy(ref.at[span], data.at[i, block], sems.at[i, block])
            for i, ref in enumerate((gc, pc, gx, px))
        ]

    def each_tile(block, act):
        for k in range(slots):
            copy = pltpu.make_async_copy(adj.at[block, k], tiles.at[block, k], tile_sems.at[block, k])
            pl.when(k < count[block])(functools.partial(act, copy))

    for block in range(blocks):
        for copy in copies(block):
            copy.start()
        each_tile(block, lambda copy: copy.start())
    stage[...] = jnp.zeros_like(stage)
    rhs[:pad] = jnp.zeros((pad, 2 * width), jnp.bfloat16)
    rhs[pad + blocks * rows :] = jnp.zeros((pad, 2 * width), jnp.bfloat16)
    identity = identity_of(rows)
    slope = slopes[...]
    find_places(index, shuffle, blocks, send_slots, places, used)

    def take(block):
        span = pl.ds(pl.multiple_of(pad + block * rows, rows), rows)
        rhs[span] = both_grads(data, block, slope)
        turned = turned_tiles(identity, tiles[block])
        for k in range(slots):
            target = cols[k, block] - index[0] * blocks
            inside = (k < count[block]) & (target >= 0) & (target < blocks)
            place = jnp.where(inside, target, blocks)
            distance = jnp.where(inside, block - target + reach, 0)
            part = turned[:, k * rows : (k + 1) * rows]
            stage[place, distance] = (wide(stage[place, distance]) + part).astype(jnp.bfloat16)

    blank = jnp.zeros((rows, rows), jnp.bfloat16)

    def writes(first):
        span = pl.ds(first, 2)
        out = [pltpu.make_async_copy(results.at[0, span], clean.at[span], out_sems.at[0, first])]
        for i in range(2):
            source, target = results.at[1, first + i], outgoing.at[places[first + i]]
            out.append(pltpu.make_async_copy(source, target, out_sems.at[1, first + i]))
        return out

    def pair(first):
        lhs = jnp.concatenate(
            [
                jnp.concatenate(
                    [blank] * i + [stage[first + i, j] for j in range(2 * reach + 1)] + [blank] * (1 - i),
                    axis=1,
                )
                for i in range(2)
            ],
            axis=0,
        )
        span = pl.ds(pl.multiple_of(first * rows, rows), (2 * reach + 2) * rows)
        product = jnp.dot(lhs, rhs[span], preferred_element_type=jnp.float32)
        product = product.astype(jnp.bfloat16).reshape(2, rows, 2 * width)
        for i in range(2):
            results[0, first + i] = product[i, :, :width]
            results[1, first + i] = product[i, :, width:]
        for copy in writes(first):
            copy.start()

    lag = reach // 2

    @pl.loop(0, blocks // 2)
    def _(step):
        for i in range(2):
            for copy in copies(2 * step + i):
                copy.wait()
            each_tile(2 * step + i, lambda copy: copy.wait())
        for i in range(2):
            take(2 * step + i)

        @pl.when(step >= lag)
        def _():
            pair(2 * (step - lag))

    for i in range(lag):
        pair(blocks - 2 * (lag - i))
    for first in range(0, blocks, 2):
        for copy in writes(first):
            copy.wait()


def inner(index, shuffle, cols, count, gc, pc, gx, px, slopes, adj, reach, devs):
    blocks, slots, rows, _ = adj.shape
    width = gc.shape[1]
    send_slots = -(-blocks // devs)
    assert reach % 2 == 0 and blocks % 2 == 0
    return pl.pallas_call(
        functools.partial(inner_kernel, reach, send_slots),
        in_specs=[IN_SMEM] * 4 + [IN_HBM] * 4 + [IN_VMEM, IN_HBM],
        out_specs=[IN_HBM] * 2,
        out_shape=[bf16(blocks, rows, width), bf16(devs * send_slots, rows, width)],
        scratch_shapes=[
            pltpu.VMEM((4, blocks, rows, width), jnp.bfloat16),
            pltpu.VMEM((blocks, slots, rows, rows), jnp.bfloat16),
            pltpu.VMEM(((blocks + 2 * reach) * rows, 2 * width), jnp.bfloat16),
            pltpu.VMEM((blocks + 1, 2 * reach + 1, rows, rows), jnp.bfloat16),
            pltpu.VMEM((2, blocks, rows, width), jnp.bfloat16),
            pltpu.SMEM((blocks,), jnp.int32),
            pltpu.SMEM((devs,), jnp.int32),
            pltpu.SemaphoreType.DMA((4, blocks)),
            pltpu.SemaphoreType.DMA((blocks, slots)),
            pltpu.SemaphoreType.DMA((2, blocks)),
        ],
        compiler_params=params(VMEM_ALL),
        cost_estimate=pl.CostEstimate(
            flops=4 * blocks * slots * rows * rows * width,
            bytes_accessed=12 * blocks * rows * width + 2 * blocks * slots * rows * rows,
            transcendentals=0,
        ),
        name="inner",
    )(index, shuffle, cols, count, gc, pc, gx, px, slopes, adj)


def patch_kernel(reach, slots, index, shuffle, clean, outgoing, low, high, clean_out, outgoing_out, *scratch):
    held, other, ready, places, used, sems = scratch
    blocks = clean.shape[0]
    border = [*range(reach), *range(blocks - reach, blocks)]
    arrivals = [
        pltpu.make_async_copy(low, other.at[0], sems.at[2, 0, 0]),
        pltpu.make_async_copy(high, other.at[1], sems.at[2, 0, 1]),
    ]
    for copy in arrivals:
        copy.start()
    find_places(index, shuffle, blocks, slots, places, used)

    def spot(i, which, first, second):
        return second.at[places[border[i]]] if which else first.at[border[i]]

    order = [(i, which) for i in range(2 * reach) for which in range(2)]
    reads, writes = [], []
    for i, which in order:
        source, target = spot(i, which, clean, outgoing), spot(i, which, clean_out, outgoing_out)
        reads.append(pltpu.make_async_copy(source, held.at[which, i], sems.at[0, which, i]))
        writes.append(pltpu.make_async_copy(ready.at[which, i], target, sems.at[1, which, i]))
    for copy in reads:
        copy.start()
    for copy in arrivals:
        copy.wait()
    for (i, which), read, write in zip(order, reads, writes):
        read.wait()
        total = wide(held[which, i]) + wide(other[i // reach, which, i % reach])
        ready[which, i] = total.astype(jnp.bfloat16)
        write.start()
    for copy in writes:
        copy.wait()


def patch(index, shuffle, clean, outgoing, low, high, slots):
    blocks, rows, width = clean.shape
    reach = low.shape[1]
    blocks_shape = (2, 2 * reach, rows, width)
    return pl.pallas_call(
        functools.partial(patch_kernel, reach, slots),
        in_specs=[IN_SMEM] * 2 + [IN_HBM] * 4,
        out_specs=[IN_HBM] * 2,
        out_shape=[bf16(*clean.shape), bf16(*outgoing.shape)],
        input_output_aliases={2: 0, 3: 1},
        scratch_shapes=[
            pltpu.VMEM(blocks_shape, jnp.bfloat16),
            pltpu.VMEM((2, 2, reach, rows, width), jnp.bfloat16),
            pltpu.VMEM(blocks_shape, jnp.bfloat16),
            pltpu.SMEM((blocks,), jnp.int32),
            pltpu.SMEM((outgoing.shape[0] // slots,), jnp.int32),
            pltpu.SemaphoreType.DMA((3, 2, 2 * reach)),
        ],
        compiler_params=params(VMEM_ALL),
        name="patch",
    )(index, shuffle, clean, outgoing, low, high)


def slot_of(target, group):
    relative = target ^ group
    return jnp.where(relative < 2, target & 1, relative)


def arrived_piece(pair, others, group, relative):
    return pair[(group & 1) ^ relative] if relative < 2 else others[relative - 2][...]


def merge_kernel(quarter, index, landing, clean, incoming, out):
    _, rows, _ = clean.shape
    group = index[1]
    piece = math.gcd(rows, quarter)
    for place in range(incoming.shape[0]):
        block = landing[place]

        @pl.when(block >= 0)
        def _():
            total = (wide(clean[block]) + wide(incoming[place])).astype(jnp.bfloat16)
            for part in range(rows // piece):
                at = block * (rows // piece) + part
                owner = at // (quarter // piece)
                offset = (at - owner * (quarter // piece)) * piece
                out[slot_of(owner, group), pl.ds(pl.multiple_of(offset, piece), piece)] = total[
                    part * piece : (part + 1) * piece
                ]


def merge(index, landing, clean, incoming, groups):
    blocks, rows, width = clean.shape
    quarter = blocks * rows // groups
    return pl.pallas_call(
        functools.partial(merge_kernel, quarter),
        in_specs=[IN_SMEM] * 2 + [IN_VMEM] * 2,
        out_specs=IN_VMEM,
        out_shape=bf16(groups, quarter, width),
        compiler_params=params(),
        name="merge",
    )(index, landing, clean, incoming)


def weight_kernel(devs, index, *refs):
    groups = len(refs) // 2
    packed, (pair, *others), (keep, send) = refs[:groups], refs[groups:-2], refs[-2:]
    me, group = index[0], index[1]
    shares = devs // groups
    height, width = keep.shape[2:]
    rhs = jnp.concatenate([arrived_piece(pair, others, group, i) for i in range(groups)], axis=1)
    for relative in range(groups):
        product = lax.dot_general(
            packed[relative][: rhs.shape[0]],
            rhs,
            (((0,), (0,)), ((), ())),
            preferred_element_type=jnp.float32,
        ).astype(jnp.bfloat16)
        for share in range(shares):
            node = ((group ^ relative) * shares + share) ^ me
            rows = product[share * height : (share + 1) * height]

            def store(out):
                for i in range(groups):
                    out[node >> 1, i] = rows[:, i * width : (i + 1) * width]

            pl.when((node & 1) == 0)(functools.partial(store, keep))
            pl.when((node & 1) == 1)(functools.partial(store, send))


def weight_partial(index, packed, pair, others, devs):
    groups = len(packed)
    _, rows, width = pair.shape
    height = groups * width // devs
    return pl.pallas_call(
        functools.partial(weight_kernel, devs),
        in_specs=[IN_SMEM] + [IN_VMEM] * (2 * groups - 1),
        out_specs=[IN_VMEM] * 2,
        out_shape=[bf16(devs // 2, groups, height, width)] * 2,
        compiler_params=params(),
        cost_estimate=pl.CostEstimate(
            flops=2 * rows * (groups * width) ** 2,
            bytes_accessed=2 * (groups * width) ** 2 + 4 * groups * rows * width,
            transcendentals=0,
        ),
        name="weight_partial",
    )(index, *packed, pair, *others)


def feature_kernel(index, *refs):
    pair, *others, even, odd, heads, tails = refs
    groups = even.shape[1]
    devs = 2 * even.shape[0]
    me, group = index[0], index[1]
    shares = devs // groups
    height, width = even.shape[2:]
    low = me & (shares - 1)
    cut = heads.shape[1]
    lhs = jnp.concatenate([arrived_piece(pair, others, group, i) for i in range(groups)], axis=1)

    def tile(half, place, i):
        held = half[place, i]
        parts = [held[:, j * height : (j + 1) * height] for j in range(width // height)]
        return jnp.concatenate(parts, axis=0)

    for relative in range(groups):
        columns = []
        for i in range(shares):
            node = (((group ^ relative) * shares) ^ (me - low)) + i
            half = odd if i % 2 else even
            columns.append(jnp.concatenate([tile(half, node >> 1, j) for j in range(groups)], axis=0))
        product = jnp.dot(
            lhs, jnp.concatenate(columns, axis=1), preferred_element_type=jnp.float32
        ).astype(jnp.bfloat16)
        parts = [product[:, i * height : (i + 1) * height] for i in range(shares)]

        def store(flip):
            ordered = jnp.concatenate([parts[i ^ flip] for i in range(shares)], axis=1)
            heads[slot_of(group ^ relative, group)] = ordered[:cut]
            tails[relative] = ordered[cut:]

        for flip in range(shares):
            pl.when(low == flip)(functools.partial(store, flip))


def feature_rows(index, pair, others, even, odd, cut):
    groups = len(others) + 2
    _, rows, width = pair.shape
    return pl.pallas_call(
        feature_kernel,
        in_specs=[IN_SMEM] + [IN_VMEM] * (groups + 1),
        out_specs=[IN_VMEM] * 2,
        out_shape=[bf16(groups, cut, width), bf16(groups, rows - cut, width)],
        compiler_params=params(),
        cost_estimate=pl.CostEstimate(
            flops=2 * rows * (groups * width) ** 2,
            bytes_accessed=2 * (groups * width) ** 2 + 4 * groups * rows * width,
            transcendentals=0,
        ),
        name="feature_rows",
    )(index, pair, *others, even, odd)


def heads_kernel(quarter, index, pair, *refs):
    *others, out, sems = refs
    group = index[1]
    cut = pair.shape[1]
    copies = []
    for i in range(len(others) + 2):
        source = pair.at[i] if i < 2 else others[i - 2]
        owner = (group & ~1) + i if i < 2 else group ^ i
        span = pl.ds(pl.multiple_of(owner * quarter, 16), cut)
        copies.append(pltpu.make_async_copy(source, out.at[span], sems.at[i]))
    for copy in copies:
        copy.start()
    for copy in copies:
        copy.wait()


def place_heads(index, pair, others, rows):
    groups = len(others) + 2
    return pl.pallas_call(
        functools.partial(heads_kernel, rows // groups),
        in_specs=[IN_SMEM] + [IN_VMEM] * (groups - 1),
        out_specs=IN_HBM,
        out_shape=bf16(rows, pair.shape[2]),
        scratch_shapes=[pltpu.SemaphoreType.DMA((groups,))],
        compiler_params=params(),
        name="place_heads",
    )(index, pair, *others)


def tails_kernel(index, head_rows, own, share, *refs):
    *others, out, total, sems = refs
    groups = len(others) + 1
    size = own.shape[0]
    quarter = out.shape[0] // groups
    copies = []
    for i, source in enumerate([own, *others]):
        span = pl.ds(pl.multiple_of((index[1] ^ i) * quarter + quarter - size, 16), size)
        copies.append(pltpu.make_async_copy(source.at[:size], out.at[span], sems.at[i]))
    for copy in copies:
        copy.start()
    sum_of = share[...]
    for other in others:
        sum_of = sum_of + wide(other[size:])
    total[...] = sum_of
    for copy in copies:
        copy.wait()


def place_tails(index, head_rows, own, share, others):
    groups = len(others) + 1
    return pl.pallas_call(
        tails_kernel,
        in_specs=[IN_SMEM, IN_HBM] + [IN_VMEM] * (groups + 1),
        out_specs=[IN_HBM, IN_VMEM],
        out_shape=[bf16(*head_rows.shape), jax.ShapeDtypeStruct(share.shape, jnp.float32)],
        input_output_aliases={1: 0},
        scratch_shapes=[pltpu.SemaphoreType.DMA((groups,))],
        compiler_params=params(),
        name="place_tails",
    )(index, head_rows, own, share, *others)


def landing_blocks(shuffle_from, me, blocks, devs, slots):
    owner = (shuffle_from // blocks).reshape(devs, blocks)
    within = (shuffle_from % blocks).reshape(devs, blocks)
    for_me = owner == me
    earlier = jnp.arange(blocks)[None, :] < jnp.arange(blocks)[:, None]
    rank = jnp.sum((for_me[:, None, :] & earlier[None]).astype(jnp.int32), axis=2)
    picked = for_me[:, None, :] & (rank[:, None, :] == jnp.arange(slots)[None, :, None])
    return (jnp.sum(jnp.where(picked, within[:, None, :] + 1, 0), axis=2) - 1).reshape(-1)


def exchange_order(groups, first):
    return range(groups - 1, first - 1, -1)


def chan_exchanged(value, groups):
    pairs = [[i, i + 1] for i in range(0, groups, 2)]
    others = [None] * (groups - 2)
    for i in exchange_order(groups, 2):
        others[i - 2] = swapped(value[i], "chan", i)
    pair = lax.all_to_all(
        value[:2], "chan", split_axis=0, concat_axis=0, tiled=True, axis_index_groups=pairs
    )
    return pair, others


def local(
    features,
    weight,
    pre_clean,
    pre_corrupt,
    grad_clean,
    grad_corrupt,
    slopes,
    adj_vals,
    adj_cols,
    adj_count,
    shuffle_from,
):
    row_count = features.shape[0]
    blocks, tile_slots, _, _ = adj_vals.shape
    reach = (tile_slots - 1) // 2
    me = lax.axis_index("node")
    group = lax.axis_index("chan")
    devs = lax.axis_size("node")
    groups = lax.axis_size("chan")
    slots = -(-blocks // devs)
    index = jnp.stack([me, group])

    args = (adj_cols.T, adj_count, grad_clean, pre_clean, grad_corrupt, pre_corrupt)
    args += (slopes[None, :], adj_vals)
    down, up, *packed = border(index, *args, features, weight, reach, groups)
    from_prev = shifted(up, "node", 1)
    from_next = shifted(down, "node", -1)
    clean, outgoing = inner(index, shuffle_from, *args, reach, devs)
    for i in exchange_order(groups, 1):
        packed[i] = swapped(packed[i], "chan", i)

    clean, outgoing = patch(index, shuffle_from, clean, outgoing, from_prev, from_next, slots)
    shuffle_from, outgoing = lax.optimization_barrier((shuffle_from, outgoing))
    landing = landing_blocks(shuffle_from, me, blocks, devs, slots)
    incoming = exchanged(outgoing, "node")
    incoming, packed = lax.optimization_barrier((incoming, packed))
    merged = merge(index, landing, clean, incoming, groups)

    quarter = row_count // groups
    pair, others = chan_exchanged(merged, groups)
    tiles = jnp.stack([piece[quarter:] for piece in packed])
    even = [tiles] + [swapped(tiles, "node", 2 * i) for i in range(1, devs // 2)]
    pair, others, even = lax.optimization_barrier((pair, others, even))
    even = jnp.stack(even)
    odd = swapped(even, "node", 1)

    keep, send = weight_partial(index, packed, pair, others, devs)
    odd, send = lax.optimization_barrier((odd, send))
    arrived = swapped(send, "node", 1)
    cut = quarter - quarter // 64 * 16
    heads, tails = feature_rows(index, pair, others, even, odd, cut)
    arrived, heads, tails = lax.optimization_barrier((arrived, heads, tails))
    pair, others = chan_exchanged(heads, groups)
    total = wide(keep) + wide(arrived)
    sums = [
        swapped(total[i].astype(jnp.bfloat16), "node", 2 * i) for i in range(1, devs // 2)
    ]
    pair, others, sums = lax.optimization_barrier((pair, others, sums))
    share = total[0]
    for part in sums:
        share = share + wide(part)
    last = [None] * (groups - 1)
    for i in exchange_order(groups, 1):
        tail = jnp.concatenate([tails[i], share[i].astype(jnp.bfloat16)], axis=0)
        last[i - 1] = swapped(tail, "chan", i)
    head_rows = place_heads(index, pair, others, row_count)
    grad_features, grad_weight = place_tails(index, head_rows, tails[0], share[0], last)
    return (grad_weight, grad_features)


def solution(mesh):
    placed = (
        P("node", "chan"),
        P("node", "chan"),
        P("node", "chan"),
        P("node", "chan"),
        P("node", "chan"),
        P("node", "chan"),
        P("chan"),
        P("node", None, None, None),
        P("node", None),
        P("node"),
        P(),
    )
    return jax.shard_map(
        local,
        mesh=mesh,
        in_specs=placed,
        out_specs=(P("node", "chan"), P("node", "chan")),
        check_vma=False,
    )
```

time: 114 us -> 136 us (1.19)
  waiting for transfers between devices: 38.3 us -> 53.3 us
  starting transfers between devices: 50.7 us -> 41.9 us
  Pallas kernels: 19.9 us -> 26.8 us
  other arithmetic: 2.53 us -> 7.41 us
  local copies, waits for them, and re-layouts: 1.43 us -> 4.83 us
    ppermute x20 -> x18, starting transfers between devices: 39.2 us -> 24.5 us  [swapped(): return lax.ppermute(value, axis, [(i, i ^ by) for i in range(size)])]
    ppermute x20 -> x18, waiting for transfers between devices: 30.5 us -> 38.9 us  [swapped(): return lax.ppermute(value, axis, [(i, i ^ by) for i in range(size)])]
    all_to_all x0 -> x2, starting transfers between devices: none -> 7.07 us  [chan_exchanged(): lax.all_to_all(value[:2], 'chan', split_axis=0, concat_axis=0, tiled=True...]
    pallas_call x2 -> x4, Pallas kernels: 10.3 us -> 17.3 us  [the longest x1 9.21 us: inner(): pl.pallas_call(functools.partial(inner_kernel, reach, send_slots), in_spe...]
    all_to_all x1, waiting for transfers between devices: 7.8 us -> 14.4 us  [exchanged(): return lax.all_to_all(value, axis, split_axis=0, concat_axis=0, tiled=True)]
    add x1, other arithmetic: 0.34 us -> 2.91 us  [local(): total = wide(keep) + wide(arrived)]
    unnamed x12 -> x28, local copies, waits for them, and re-layouts: 0.81 us -> 2.71 us
    slice x0 -> x2, local copies, waits for them, and re-layouts: none -> 1.55 us  [chan_exchanged(): value[:2]]
  transfers between devices with their start and end apart: 23 -> 23, of which waited for: 10 -> 7; matrix products, arithmetic and copies ran while one was open for 1% -> 4% of each run, Pallas kernels for 8% -> 15%
where the time goes in v7:
time: 136 us; the launch traced here: 135 us
  waiting for transfers between devices  53.3 us (39%)
  starting transfers between devices  41.9 us (31%)
  Pallas kernels  26.8 us (20%)
  other arithmetic  7.41 us (5%)
  local copies, waits for them, and re-layouts  4.83 us (4%)
    ppermute x18, waiting for transfers between devices, swapped(): return lax.ppermute(value, axis, [(i, i ^ by) for i in range(size)])  38.9 us
    ppermute x18, starting transfers between devices, swapped(): return lax.ppermute(value, axis, [(i, i ^ by) for i in range(size)])  24.5 us
    all_to_all x1, waiting for transfers between devices, exchanged(): return lax.all_to_all(value, axis, split_axis=0, concat_axis=0, tiled=True)  14.4 us
    pallas_call x1, Pallas kernels, inner(): pl.pallas_call(functools.partial(inner_kernel, reach, send_slots), in_spe...  9.21 us
    all_to_all x2, starting transfers between devices, chan_exchanged(): lax.all_to_all(value[:2], 'chan', split_axis=0, concat_axis=0, tiled=True...  7.07 us
    all_to_all x1, starting transfers between devices, exchanged(): return lax.all_to_all(value, axis, split_axis=0, concat_axis=0, tiled=True)  6.62 us
    pallas_call x1, Pallas kernels, border(): pl.pallas_call(functools.partial(border_kernel, reach, groups), in_specs=...  4.73 us
    ppermute x2, starting transfers between devices, shifted(): return lax.ppermute(value, axis, pairs)  3.69 us
  transfers between devices with their start and end apart: 23, of which 7 were waited for; matrix products, arithmetic and copies ran while one was open for 4% of the time, Pallas kernels for 15%

profile of v7, /device:TPU:0, one launch (start us, length us, event | category | flops | bytes accessed | tf_op | source)
XLA Modules:
  0.0 135.2 jit_solution(13960559928091375685)
XLA Ops:
  0.6 0.6 pad_add_fusion.index
  1.2 4.7 %border.1 = (bf16[2,2,128,256]{3,2,1,0:T(8,128)(2,1)}, bf16[2,2,128,256]{3,2,1,0:T(8,128)(2,1)}, bf16[576,256]{1,0:T(8,128)(2,1)}, bf16[576,256]{1,0:T(8,128)(2,...) custom-call(s32[2]{0:T(128)} %pad_add_fusion.index, s32[5,14]{1,0:T(8,128)} %bitcast.55, s32[14]{0:T(128)} %count.3, ...), custom_call_target="tpu_custom_call" | custom-call | tf_op jit(solution)/shard_map/border/pallas_call | solution.py:169
  5.9 2.4 %collective-permute-start = (bf16[2,2,128,256]{3,2,1,0:T(8,128)(2,1)}, bf16[2,2,128,256]{3,2,1,0:T(8,128)(2,1)S(1)}, u32[]{:S(2)}, u32[]{:S(2)}) collective-permute-start(bf16[2,2,128,256]{3,2,1,0:T(8,128)(2,1)} %get-tuple-element.45), channel_id=1, source_target_pairs={{0,4},{4,8},{8,12},{12,16},{16,20},{20,24},{24,28},{1,5},{5,9},{9,... | collective-permute-start | bytes 786440 | tf_op jit(solution)/shard_map/ppermute | solution.py:33
  8.3 1.3 collective-permute-start.1
  9.6 2.5 %collective-permute-start.2 = (bf16[576,256]{1,0:T(8,128)(2,1)}, bf16[576,256]{1,0:T(8,128)(2,1)S(1)}, u32[]{:S(2)}, u32[]{:S(2)}) collective-permute-start(bf16[576,256]{1,0:T(8,128)(2,1)} %get-tuple-element.52), channel_id=1, source_target_pairs={{0,1},{1,0},{2,3},{3,2},{4,5},{5,4},{6,7},{7,6},{8,9},{9,8},{10,11... | collective-permute-start | bytes 884744 | tf_op jit(solution)/shard_map/ppermute | solution.py:38
  12.1 2.6 %collective-permute-start.3 = (bf16[576,256]{1,0:T(8,128)(2,1)}, bf16[576,256]{1,0:T(8,128)(2,1)S(1)}, u32[]{:S(2)}, u32[]{:S(2)}) collective-permute-start(bf16[576,256]{1,0:T(8,128)(2,1)} %get-tuple-element.53), channel_id=1, source_target_pairs={{0,2},{1,3},{2,0},{3,1},{4,6},{5,7},{6,4},{7,5},{8,10},{9,11},{10,... | collective-permute-start | bytes 884744 | tf_op jit(solution)/shard_map/ppermute | solution.py:38
  14.7 9.2 %inner.1 = (bf16[14,128,256]{2,1,0:T(8,128)(2,1)}, bf16[16,128,256]{2,1,0:T(8,128)(2,1)}) custom-call(s32[2]{0:T(128)} %pad_add_fusion.index, s32[112]{0:T(128)} %shuffle.3, s32[5,14]{1,0:T(8,128)} %bitcast.56, s32[14]{0:T(128)} %count.3, bf16[1792,256]{1,0:T(8,128)(2,1)} %gc.3, bf16[1792,256]{1,0:T(8,128)(2,1)} %pc.3, bf16[1792,256]{1,0:T(8,128)(2,1)} %gx.3, ...), custom_call_target="tpu_custom_call" | custom-call | flops 1174405120 | bytes 7798784 | tf_op jit(solution)/shard_map/inner/pallas_call | solution.py:292
  23.9 0.0 collective-permute-done.low
  23.9 0.0 collective-permute-done.1.high
  24.0 0.7 copy-done.11
  24.6 0.1 copy-done.12
  24.8 2.8 %patch.1 = (bf16[14,128,256]{2,1,0:T(8,128)(2,1)}, bf16[16,128,256]{2,1,0:T(8,128)(2,1)}) custom-call(s32[2]{0:T(128)} %pad_add_fusion.index, s32[112]{0:T(128)} %shuffle.3, bf16[14,128,256]{2,1,0:T(8,128)(2,1)} %get-tuple-element.43.clean, bf16[16,128,256]{2,1,0:T(8,128)(2,1)} %get-tuple-element.44.outgoing, ...), custom_call_target="tpu_custom_call", output_to_operand_aliasing={{0}: (2, {}), {1}: (3, {})} | custom-call | tf_op jit(solution)/shard_map/patch/pallas_call | solution.py:357
  27.6 0.0 copy-start
  27.6 6.6 %all-to-all-start = ((bf16[16,128,256]{2,1,0:T(8,128)(2,1)}), bf16[16,128,256]{2,1,0:T(8,128)(2,1)S(1)}, u32[]{:S(2)}, u32[]{:S(2)}) async-start(bf16[16,128,256]{2,1,0:T(8,128)(2,1)} %get-tuple-element.50), calls=%async_computation | async-start | bytes 2097152 | tf_op jit(solution)/shard_map/all_to_all | solution.py:42
  34.3 0.1 eq.30
  34.4 0.1 add.36
  34.5 0.3 convert_reduce_fusion
  34.8 0.1 copy.16
  34.9 0.1 select_reduce_fusion
  35.0 0.1 copy.17
  35.1 0.1 sub.13.landing
  35.2 0.0 collective-permute-done.2.refs_1_
  35.2 0.0 collective-permute-done.4.refs_3_
  35.2 14.4 %all-to-all-done.incoming = bf16[16,128,256]{2,1,0:T(8,128)(2,1)S(1)} async-done(((bf16[16,128,256]{2,1,0:T(8,128)(2,1)}), bf16[16,128,256]{2,1,0:T(8,128)(2,1)S(1)}, u32[]{:S(2)}, u32[]{:S(2)}) %all-to-all-start) | async-done | bytes 1048608 | tf_op jit(solution)/shard_map/all_to_all | solution.py:42
  49.7 0.7 pad_maximum_fusion.1
  50.4 0.6 collective-permute-start.9
  51.0 1.4 %collective-permute-start.8 = (bf16[4,128,256]{2,1,0:T(8,128)(2,1)}, bf16[4,128,256]{2,1,0:T(8,128)(2,1)}, u32[]{:S(2)}, u32[]{:S(2)}) collective-permute-start(bf16[4,128,256]{2,1,0:T(8,128)(2,1)} %pad_maximum_fusion.1), channel_id=1, source_target_pairs={{0,16},{4,20},{8,24},{12,28},{16,0},{20,4},{24,8},{28,12},{1,17},{... | collective-permute-start | bytes 786440 | tf_op jit(solution)/shard_map/ppermute | solution.py:38
  52.4 1.5 %collective-permute-start.7 = (bf16[4,128,256]{2,1,0:T(8,128)(2,1)}, bf16[4,128,256]{2,1,0:T(8,128)(2,1)}, u32[]{:S(2)}, u32[]{:S(2)}) collective-permute-start(bf16[4,128,256]{2,1,0:T(8,128)(2,1)} %pad_maximum_fusion.1), channel_id=1, source_target_pairs={{0,8},{4,12},{8,0},{12,4},{16,24},{20,28},{24,16},{28,20},{1,9},{5... | collective-permute-start | bytes 786440 | tf_op jit(solution)/shard_map/ppermute | solution.py:38
  53.9 0.9 merge.1
  54.9 0.8 slice.94
  55.7 3.6 %all-to-all-start.1 = ((bf16[2,448,256]{2,1,0:T(8,128)(2,1)}), bf16[2,448,256]{2,1,0:T(8,128)(2,1)S(1)}, u32[]{:S(2)}, u32[]{:S(2)}) async-start(bf16[2,448,256]{2,1,0:T(8,128)(2,1)} %slice.94), calls=%async_computation.1 | async-start | bytes 917504 | tf_op jit(solution)/shard_map/all_to_all | solution.py:597
  59.3 3.7 %collective-permute-start.6 = (bf16[448,256]{1,0:T(8,128)(2,1)S(1)}, bf16[448,256]{1,0:T(8,128)(2,1)S(1)}, u32[]{:S(2)}, u32[]{:S(2)}) collective-permute-start(bf16[448,256]{1,0:T(8,128)(2,1)S(1)} %get-tuple-element.91), channel_id=1, source_target_pairs={{0,3},{1,2},{2,1},{3,0},{4,7},{5,6},{6,5},{7,4},{8,11},{9,10},{10,... | collective-permute-start | bytes 688136 | tf_op jit(solution)/shard_map/ppermute | solution.py:38
  63.0 11.2 %collective-permute-done.6.refs_6_.refs_2_ = bf16[448,256]{1,0:T(8,128)(2,1)S(1)} collective-permute-done((bf16[448,256]{1,0:T(8,128)(2,1)S(1)}, bf16[448,256]{1,0:T(8,128)(2,1)S(1)}, u32[]{:S(2)}, u32[]{:S(2)}) %collective-permute-start.6) | collective-permute-done | bytes 229408 | tf_op jit(solution)/shard_map/ppermute | solution.py:38
  74.3 7.2 %collective-permute-done.5.refs_5_.refs_1_ = bf16[448,256]{1,0:T(8,128)(2,1)S(1)} collective-permute-done((bf16[448,256]{1,0:T(8,128)(2,1)S(1)}, bf16[448,256]{1,0:T(8,128)(2,1)S(1)}, u32[]{:S(2)}, u32[]{:S(2)}) %collective-permute-start.5) | collective-permute-done | bytes 229408 | tf_op jit(solution)/shard_map/ppermute | solution.py:38
  81.4 0.0 collective-permute-done.7
  81.5 1.4 %pad_maximum_fusion.refs_3_ = bf16[4,4,128,256]{3,2,1,0:T(8,128)(2,1)S(1)} fusion(bf16[1,4,128,256]{3,2,1,0:T(8,128)(2,1)} %bitcast.13, bf16[1,4,128,256]{3,2,1,0:T(8,128)(2,1)} %bitcast.12, bf16[1,4,128,256]{3,2,1,0:T(8,128)(2,1)} %bitcast.11, bf16[1,4,128,256]{3,2,1,0:T(8,128)(2,1)} %bitcast.10), kind=kLoop, calls=%fused_computation.1 | loop fusion | flops 1572864 | bytes 2097152 | tf_op jit(solution)/shard_map/stack | solution.py:647
  82.9 0.1 collective-permute-start.10
  83.0 2.6 %weight_partial.1 = (bf16[4,4,128,256]{3,2,1,0:T(8,128)(2,1)S(1)}, bf16[4,4,128,256]{3,2,1,0:T(8,128)(2,1)S(1)}) custom-call(s32[2]{0:T(128)S(1)} %copy-done.1, bf16[576,256]{1,0:T(8,128)(2,1)S(1)} %copy-done.2, bf16[576,256]{1,0:T(8,128)(2,1)S(1)} %collective-permute-done.2.refs_1_, bf16[576,256]{1,0:T(8,128)(2,1)S(1)} %copy-done.4, ...), custom_call_target="tpu_custom_call" | custom-call | flops 939524096 | bytes 3932160 | tf_op jit(solution)/shard_map/weight_partial/pallas_call | solution.py:447
  85.6 0.0 collective-permute-done.10.refs_4_
  85.6 0.5 collective-permute-start.11
  86.2 0.9 copy-done.8
  87.1 0.9 copy-done.10
  88.0 3.1 %feature_rows.1 = (bf16[4,336,256]{2,1,0:T(8,128)(2,1)S(1)}, bf16[4,112,256]{2,1,0:T(8,128)(2,1)S(1)}) custom-call(s32[2]{0:T(128)S(1)} %copy-done.1, bf16[2,448,256]{2,1,0:T(8,128)(2,1)S(1)} %all-to-all-done.1.refs_4_.refs_0_, bf16[448,256]{1,0:T(8,128)(2,1)S(1)} %copy-done.10, bf16[448,256]{1,0:T(8,128)(2,1)S(1)} %copy-done.8, ...), custom_call_target="tpu_custom_call" | custom-call | flops 939524096 | bytes 3932160 | tf_op jit(solution)/shard_map/feature_rows/pallas_call | solution.py:501
  91.2 0.8 slice.79
  91.9 3.5 %all-to-all-start.2 = ((bf16[2,336,256]{2,1,0:T(8,128)(2,1)}), bf16[2,336,256]{2,1,0:T(8,128)(2,1)S(1)}, u32[]{:S(2)}, u32[]{:S(2)}) async-start(bf16[2,336,256]{2,1,0:T(8,128)(2,1)} %slice.79), calls=%async_computation.2 | async-start | bytes 688128 | tf_op jit(solution)/shard_map/all_to_all | solution.py:597
  95.4 2.9 %convert_add_fusion = (f32[4,4,128,256]{3,2,1,0:T(8,128)}, bf16[4,4,128,256]{3,2,1,0:T(8,128)(2,1)S(1)}) fusion(bf16[4,4,128,256]{3,2,1,0:T(8,128)(2,1)} %collective-permute-done.11, bf16[4,4,128,256]{3,2,1,0:T(8,128)(2,1)S(1)} %get-tuple-element.73), kind=kLoop, calls=%fused_computation | loop fusion | flops 2097152 | bytes 5242880 | tf_op jit(solution)/shard_map/add | solution.py:657
  98.3 0.1 slice_bitcast_fusion.1
  98.3 1.0 collective-permute-start.16
  99.3 1.7 %collective-permute-start.15 = (bf16[4,128,256]{2,1,0:T(8,128)(2,1)S(1)}, bf16[4,128,256]{2,1,0:T(8,128)(2,1)S(1)}, u32[]{:S(2)}, u32[]{:S(2)}) collective-permute-start(bf16[4,128,256]{2,1,0:T(8,128)(2,1)S(1)} %get-tuple-element.89), channel_id=1, source_target_pairs={{0,16},{4,20},{8,24},{12,28},{16,0},{20,4},{24,8},{28,12},{1,17},{... | collective-permute-start | bytes 786440 | tf_op jit(solution)/shard_map/ppermute | solution.py:38
  101.0 0.9 collective-permute-start.14
  101.9 1.1 collective-permute-start.13
  103.0 2.5 %collective-permute-start.12 = (bf16[336,256]{1,0:T(8,128)(2,1)S(1)}, bf16[336,256]{1,0:T(8,128)(2,1)S(1)}, u32[]{:S(2)}, u32[]{:S(2)}) collective-permute-start(bf16[336,256]{1,0:T(8,128)(2,1)S(1)} %get-tuple-element.94), channel_id=1, source_target_pairs={{0,2},{1,3},{2,0},{3,1},{4,6},{5,7},{6,4},{7,5},{8,10},{9,11},{10,... | collective-permute-start | bytes 516104 | tf_op jit(solution)/shard_map/ppermute | solution.py:38
  105.5 5.7 %collective-permute-done.13.refs_1_ = bf16[336,256]{1,0:T(8,128)(2,1)S(1)} collective-permute-done((bf16[336,256]{1,0:T(8,128)(2,1)S(1)}, bf16[336,256]{1,0:T(8,128)(2,1)S(1)}, u32[]{:S(2)}, u32[]{:S(2)}) %collective-permute-start.13) | collective-permute-done | bytes 172064 | tf_op jit(solution)/shard_map/ppermute | solution.py:38
  111.2 8.5 %collective-permute-done.12.refs_0_ = bf16[336,256]{1,0:T(8,128)(2,1)S(1)} collective-permute-done((bf16[336,256]{1,0:T(8,128)(2,1)S(1)}, bf16[336,256]{1,0:T(8,128)(2,1)S(1)}, u32[]{:S(2)}, u32[]{:S(2)}) %collective-permute-start.12) | collective-permute-done | bytes 172064 | tf_op jit(solution)/shard_map/ppermute | solution.py:38
  119.7 0.0 collective-permute-done.16
  119.7 0.0 collective-permute-done.15
  119.7 1.3 fusion.7
  121.0 0.1 collective-permute-start.17
  121.1 1.8 %collective-permute-start.18 = (bf16[240,256]{1,0:T(8,128)(2,1)S(1)}, bf16[240,256]{1,0:T(8,128)(2,1)S(1)}, u32[]{:S(2)}, u32[]{:S(2)}) collective-permute-start(bf16[240,256]{1,0:T(8,128)(2,1)S(1)} %pad_maximum_fusion.3), channel_id=1, source_target_pairs={{0,2},{1,3},{2,0},{3,1},{4,6},{5,7},{6,4},{7,5},{8,10},{9,11},{10,... | collective-permute-start | bytes 368648 | tf_op jit(solution)/shard_map/ppermute | solution.py:38
  122.9 2.7 %collective-permute-start.19 = (bf16[240,256]{1,0:T(8,128)(2,1)S(1)}, bf16[240,256]{1,0:T(8,128)(2,1)S(1)}, u32[]{:S(2)}, u32[]{:S(2)}) collective-permute-start(bf16[240,256]{1,0:T(8,128)(2,1)S(1)} %pad_maximum_fusion.4), channel_id=1, source_target_pairs={{0,3},{1,2},{2,1},{3,0},{4,7},{5,6},{6,5},{7,4},{8,11},{9,10},{10,... | collective-permute-start | bytes 368648 | tf_op jit(solution)/shard_map/ppermute | solution.py:38
  125.7 1.4 %place_heads.1.head_rows = bf16[1792,256]{1,0:T(8,128)(2,1)} custom-call(s32[2]{0:T(128)S(1)} %copy-done.1, bf16[2,336,256]{2,1,0:T(8,128)(2,1)S(1)} %all-to-all-done.2.pair, bf16[336,256]{1,0:T(8,128)(2,1)S(1)} %collective-permute-done.12.refs_0_, bf16[336,256]{1,0:T(8,128)(2,1)S(1)} %collective-permute-done.13.refs_1_), custom_call_target="tpu_custom_call" | custom-call | tf_op jit(solution)/shard_map/place_heads/pallas_call | solution.py:534
  127.1 0.4 collective-permute-done.17.refs_0_
  127.5 5.8 %collective-permute-done.18.refs_1_ = bf16[240,256]{1,0:T(8,128)(2,1)S(1)} collective-permute-done((bf16[240,256]{1,0:T(8,128)(2,1)S(1)}, bf16[240,256]{1,0:T(8,128)(2,1)S(1)}, u32[]{:S(2)}, u32[]{:S(2)}) %collective-permute-start.18) | collective-permute-done | bytes 122912 | tf_op jit(solution)/shard_map/ppermute | solution.py:38
  133.3 1.9 %place_tails.1 = (bf16[1792,256]{1,0:T(8,128)(2,1)}, f32[128,256]{1,0:T(8,128)}) custom-call(s32[2]{0:T(128)S(1)} %copy-done.1, bf16[1792,256]{1,0:T(8,128)(2,1)} %place_heads.1.head_rows, bf16[112,256]{1,0:T(8,128)(2,1)S(1)} %get-tuple-element.101.own, f32[128,256]{1,0:T(8,128)S(1)} %slice_bitcast_fusion.8.share, ...), custom_call_target="tpu_custom_call", output_to_operand_aliasing={{0}: (1, {})} | custom-call | tf_op jit(solution)/shard_map/place_tails/pallas_call | solution.py:566
  (47 shorter events, 0.3 us)
Async XLA Ops:
  5.9 18.0 %collective-permute-start = (bf16[2,2,128,256]{3,2,1,0:T(8,128)(2,1)}, bf16[2,2,128,256]{3,2,1,0:T(8,128)(2,1)S(1)}, u32[]{:S(2)}, u32[]{:S(2)}) collective-permute-start(bf16[2,2,128,256]{3,2,1,0:T(8,128)(2,1)} %get-tuple-element.45), channel_id=1, source_target_pairs={{0,4},{4,8},{8,12},{12,16},{16,20},{20,24},{24,28},{1,5},{5,9},{9,... | collective-permute-start | bytes 786440 | tf_op jit(solution)/shard_map/ppermute | solution.py:33
  8.3 15.6 %collective-permute-start.1 = (bf16[2,2,128,256]{3,2,1,0:T(8,128)(2,1)}, bf16[2,2,128,256]{3,2,1,0:T(8,128)(2,1)S(1)}, u32[]{:S(2)}, u32[]{:S(2)}) collective-permute-start(bf16[2,2,128,256]{3,2,1,0:T(8,128)(2,1)} %get-tuple-element.46), channel_id=1, source_target_pairs={{4,0},{8,4},{12,8},{16,12},{20,16},{24,20},{28,24},{5,1},{9,5},{13... | collective-permute-start | bytes 786440 | tf_op jit(solution)/shard_map/ppermute | solution.py:33
  9.6 25.6 %collective-permute-start.2 = (bf16[576,256]{1,0:T(8,128)(2,1)}, bf16[576,256]{1,0:T(8,128)(2,1)S(1)}, u32[]{:S(2)}, u32[]{:S(2)}) collective-permute-start(bf16[576,256]{1,0:T(8,128)(2,1)} %get-tuple-element.52), channel_id=1, source_target_pairs={{0,1},{1,0},{2,3},{3,2},{4,5},{5,4},{6,7},{7,6},{8,9},{9,8},{10,11... | collective-permute-start | bytes 884744 | tf_op jit(solution)/shard_map/ppermute | solution.py:38
  12.1 23.1 %collective-permute-start.3 = (bf16[576,256]{1,0:T(8,128)(2,1)}, bf16[576,256]{1,0:T(8,128)(2,1)S(1)}, u32[]{:S(2)}, u32[]{:S(2)}) collective-permute-start(bf16[576,256]{1,0:T(8,128)(2,1)} %get-tuple-element.53), channel_id=1, source_target_pairs={{0,2},{1,3},{2,0},{3,1},{4,6},{5,7},{6,4},{7,5},{8,10},{9,11},{10,... | collective-permute-start | bytes 884744 | tf_op jit(solution)/shard_map/ppermute | solution.py:38
  14.7 20.5 %collective-permute-start.4 = (bf16[576,256]{1,0:T(8,128)(2,1)}, bf16[576,256]{1,0:T(8,128)(2,1)S(1)}, u32[]{:S(2)}, u32[]{:S(2)}) collective-permute-start(bf16[576,256]{1,0:T(8,128)(2,1)} %get-tuple-element.54), channel_id=1, source_target_pairs={{0,3},{1,2},{2,1},{3,0},{4,7},{5,6},{6,5},{7,4},{8,11},{9,10},{10,... | collective-permute-start | bytes 884744 | tf_op jit(solution)/shard_map/ppermute | solution.py:38
  23.9 0.7 copy-start.11
  24.0 0.8 copy-start.12
  24.7 9.5 %copy-start.13 = (s32[112]{0:T(128)S(1)}, s32[112]{0:T(128)}, u32[]{:S(2)}) copy-start(s32[112]{0:T(128)} %shuffle.3) | copy-start | bytes 1348
  24.8 24.9 %copy-start.2 = (bf16[576,256]{1,0:T(8,128)(2,1)S(1)}, bf16[576,256]{1,0:T(8,128)(2,1)}, u32[]{:S(2)}) copy-start(bf16[576,256]{1,0:T(8,128)(2,1)} %get-tuple-element.56.refs_0_) | copy-start | bytes 884740
  27.6 26.3 %copy-start = (bf16[14,128,256]{2,1,0:T(8,128)(2,1)S(1)}, bf16[14,128,256]{2,1,0:T(8,128)(2,1)}, u32[]{:S(2)}) copy-start(bf16[14,128,256]{2,1,0:T(8,128)(2,1)} %get-tuple-element.49.clean) | copy-start | bytes 2752516
  27.6 26.3 %copy-start.1 = (s32[2]{0:T(128)S(1)}, s32[2]{0:T(128)}, u32[]{:S(2)}) copy-start(s32[2]{0:T(128)} %pad_add_fusion.index) | copy-start | bytes 28
  27.6 22.0 %all-to-all-start = ((bf16[16,128,256]{2,1,0:T(8,128)(2,1)}), bf16[16,128,256]{2,1,0:T(8,128)(2,1)S(1)}, u32[]{:S(2)}, u32[]{:S(2)}) async-start(bf16[16,128,256]{2,1,0:T(8,128)(2,1)} %get-tuple-element.50), calls=%async_computation | async-start | bytes 2097152 | tf_op jit(solution)/shard_map/all_to_all | solution.py:42
  35.2 18.7 %copy-start.3 = (bf16[576,256]{1,0:T(8,128)(2,1)}, bf16[576,256]{1,0:T(8,128)(2,1)S(1)}, u32[]{:S(2)}) copy-start(bf16[576,256]{1,0:T(8,128)(2,1)S(1)} %collective-permute-done.3.refs_2_) | copy-start | bytes 884740
  35.2 18.7 %copy-start.5 = (bf16[576,256]{1,0:T(8,128)(2,1)}, bf16[576,256]{1,0:T(8,128)(2,1)S(1)}, u32[]{:S(2)}) copy-start(bf16[576,256]{1,0:T(8,128)(2,1)S(1)} %collective-permute-done.4.refs_3_) | copy-start | bytes 884740
  50.4 31.0 %collective-permute-start.9 = (bf16[4,128,256]{2,1,0:T(8,128)(2,1)}, bf16[4,128,256]{2,1,0:T(8,128)(2,1)}, u32[]{:S(2)}, u32[]{:S(2)}) collective-permute-start(bf16[4,128,256]{2,1,0:T(8,128)(2,1)} %pad_maximum_fusion.1), channel_id=1, source_target_pairs={{0,24},{4,28},{8,16},{12,20},{16,8},{20,12},{24,0},{28,4},{1,25},{... | collective-permute-start | bytes 786440 | tf_op jit(solution)/shard_map/ppermute | solution.py:38
  51.0 30.4 %collective-permute-start.8 = (bf16[4,128,256]{2,1,0:T(8,128)(2,1)}, bf16[4,128,256]{2,1,0:T(8,128)(2,1)}, u32[]{:S(2)}, u32[]{:S(2)}) collective-permute-start(bf16[4,128,256]{2,1,0:T(8,128)(2,1)} %pad_maximum_fusion.1), channel_id=1, source_target_pairs={{0,16},{4,20},{8,24},{12,28},{16,0},{20,4},{24,8},{28,12},{1,17},{... | collective-permute-start | bytes 786440 | tf_op jit(solution)/shard_map/ppermute | solution.py:38
  52.4 29.0 %collective-permute-start.7 = (bf16[4,128,256]{2,1,0:T(8,128)(2,1)}, bf16[4,128,256]{2,1,0:T(8,128)(2,1)}, u32[]{:S(2)}, u32[]{:S(2)}) collective-permute-start(bf16[4,128,256]{2,1,0:T(8,128)(2,1)} %pad_maximum_fusion.1), channel_id=1, source_target_pairs={{0,8},{4,12},{8,0},{12,4},{16,24},{20,28},{24,16},{28,20},{1,9},{5... | collective-permute-start | bytes 786440 | tf_op jit(solution)/shard_map/ppermute | solution.py:38
  55.7 27.3 %copy-start.4 = (bf16[576,256]{1,0:T(8,128)(2,1)S(1)}, bf16[576,256]{1,0:T(8,128)(2,1)}, u32[]{:S(2)}) copy-start(bf16[576,256]{1,0:T(8,128)(2,1)} %copy-done.3) | copy-start | bytes 884740
  55.7 27.3 %copy-start.6 = (bf16[576,256]{1,0:T(8,128)(2,1)S(1)}, bf16[576,256]{1,0:T(8,128)(2,1)}, u32[]{:S(2)}) copy-start(bf16[576,256]{1,0:T(8,128)(2,1)} %copy-done.5) | copy-start | bytes 884740
  55.7 25.8 %all-to-all-start.1 = ((bf16[2,448,256]{2,1,0:T(8,128)(2,1)}), bf16[2,448,256]{2,1,0:T(8,128)(2,1)S(1)}, u32[]{:S(2)}, u32[]{:S(2)}) async-start(bf16[2,448,256]{2,1,0:T(8,128)(2,1)} %slice.94), calls=%async_computation.1 | async-start | bytes 917504 | tf_op jit(solution)/shard_map/all_to_all | solution.py:597
  59.3 14.9 %collective-permute-start.6 = (bf16[448,256]{1,0:T(8,128)(2,1)S(1)}, bf16[448,256]{1,0:T(8,128)(2,1)S(1)}, u32[]{:S(2)}, u32[]{:S(2)}) collective-permute-start(bf16[448,256]{1,0:T(8,128)(2,1)S(1)} %get-tuple-element.91), channel_id=1, source_target_pairs={{0,3},{1,2},{2,1},{3,0},{4,7},{5,6},{6,5},{7,4},{8,11},{9,10},{10,... | collective-permute-start | bytes 688136 | tf_op jit(solution)/shard_map/ppermute | solution.py:38
  63.0 18.4 %collective-permute-start.5 = (bf16[448,256]{1,0:T(8,128)(2,1)S(1)}, bf16[448,256]{1,0:T(8,128)(2,1)S(1)}, u32[]{:S(2)}, u32[]{:S(2)}) collective-permute-start(bf16[448,256]{1,0:T(8,128)(2,1)S(1)} %get-tuple-element.92), channel_id=1, source_target_pairs={{0,2},{1,3},{2,0},{3,1},{4,6},{5,7},{6,4},{7,5},{8,10},{9,11},{10,... | collective-permute-start | bytes 688136 | tf_op jit(solution)/shard_map/ppermute | solution.py:38
  74.3 11.3 %copy-start.7 = (bf16[448,256]{1,0:T(8,128)(2,1)}, bf16[448,256]{1,0:T(8,128)(2,1)S(1)}, u32[]{:S(2)}) copy-start(bf16[448,256]{1,0:T(8,128)(2,1)S(1)} %collective-permute-done.6.refs_6_.refs_2_) | copy-start | bytes 688132
  81.4 4.2 %copy-start.9 = (bf16[448,256]{1,0:T(8,128)(2,1)}, bf16[448,256]{1,0:T(8,128)(2,1)S(1)}, u32[]{:S(2)}) copy-start(bf16[448,256]{1,0:T(8,128)(2,1)S(1)} %collective-permute-done.5.refs_5_.refs_1_) | copy-start | bytes 688132
  82.9 2.8 %collective-permute-start.10 = (bf16[4,4,128,256]{3,2,1,0:T(8,128)(2,1)S(1)}, bf16[4,4,128,256]{3,2,1,0:T(8,128)(2,1)S(1)}, u32[]{:S(2)}, u32[]{:S(2)}) collective-permute-start(bf16[4,4,128,256]{3,2,1,0:T(8,128)(2,1)S(1)} %pad_maximum_fusion.refs_3_), channel_id=1, source_target_pairs={{0,4},{4,0},{8,12},{12,8},{16,20},{20,16},{24,28},{28,24},{1,5},{5... | collective-permute-start | bytes 3145736 | tf_op jit(solution)/shard_map/ppermute | solution.py:38
  85.6 5.5 %collective-permute-start.11 = (bf16[4,4,128,256]{3,2,1,0:T(8,128)(2,1)S(1)}, bf16[4,4,128,256]{3,2,1,0:T(8,128)(2,1)}, u32[]{:S(2)}, u32[]{:S(2)}) collective-permute-start(bf16[4,4,128,256]{3,2,1,0:T(8,128)(2,1)S(1)} %get-tuple-element.68), channel_id=1, source_target_pairs={{0,4},{4,0},{8,12},{12,8},{16,20},{20,16},{24,28},{28,24},{1,5},{5... | collective-permute-start | bytes 3145736 | tf_op jit(solution)/shard_map/ppermute | solution.py:38
  86.2 0.9 copy-start.8
  87.1 0.9 copy-start.10
  91.9 27.8 %all-to-all-start.2 = ((bf16[2,336,256]{2,1,0:T(8,128)(2,1)}), bf16[2,336,256]{2,1,0:T(8,128)(2,1)S(1)}, u32[]{:S(2)}, u32[]{:S(2)}) async-start(bf16[2,336,256]{2,1,0:T(8,128)(2,1)} %slice.79), calls=%async_computation.2 | async-start | bytes 688128 | tf_op jit(solution)/shard_map/all_to_all | solution.py:597
  98.3 21.4 %collective-permute-start.16 = (bf16[4,128,256]{2,1,0:T(8,128)(2,1)S(1)}, bf16[4,128,256]{2,1,0:T(8,128)(2,1)S(1)}, u32[]{:S(2)}, u32[]{:S(2)}) collective-permute-start(bf16[4,128,256]{2,1,0:T(8,128)(2,1)S(1)} %get-tuple-element.88), channel_id=1, source_target_pairs={{0,24},{4,28},{8,16},{12,20},{16,8},{20,12},{24,0},{28,4},{1,25},{... | collective-permute-start | bytes 786440 | tf_op jit(solution)/shard_map/ppermute | solution.py:38
  99.3 20.4 %collective-permute-start.15 = (bf16[4,128,256]{2,1,0:T(8,128)(2,1)S(1)}, bf16[4,128,256]{2,1,0:T(8,128)(2,1)S(1)}, u32[]{:S(2)}, u32[]{:S(2)}) collective-permute-start(bf16[4,128,256]{2,1,0:T(8,128)(2,1)S(1)} %get-tuple-element.89), channel_id=1, source_target_pairs={{0,16},{4,20},{8,24},{12,28},{16,0},{20,4},{24,8},{28,12},{1,17},{... | collective-permute-start | bytes 786440 | tf_op jit(solution)/shard_map/ppermute | solution.py:38
  101.0 18.7 %collective-permute-start.14 = (bf16[4,128,256]{2,1,0:T(8,128)(2,1)S(1)}, bf16[4,128,256]{2,1,0:T(8,128)(2,1)}, u32[]{:S(2)}, u32[]{:S(2)}) collective-permute-start(bf16[4,128,256]{2,1,0:T(8,128)(2,1)S(1)} %get-tuple-element.90), channel_id=1, source_target_pairs={{0,8},{4,12},{8,0},{12,4},{16,24},{20,28},{24,16},{28,20},{1,9},{5... | collective-permute-start | bytes 786440 | tf_op jit(solution)/shard_map/ppermute | solution.py:38
  101.9 9.2 %collective-permute-start.13 = (bf16[336,256]{1,0:T(8,128)(2,1)S(1)}, bf16[336,256]{1,0:T(8,128)(2,1)S(1)}, u32[]{:S(2)}, u32[]{:S(2)}) collective-permute-start(bf16[336,256]{1,0:T(8,128)(2,1)S(1)} %get-tuple-element.93), channel_id=1, source_target_pairs={{0,3},{1,2},{2,1},{3,0},{4,7},{5,6},{6,5},{7,4},{8,11},{9,10},{10,... | collective-permute-start | bytes 516104 | tf_op jit(solution)/shard_map/ppermute | solution.py:38
  103.0 16.7 %collective-permute-start.12 = (bf16[336,256]{1,0:T(8,128)(2,1)S(1)}, bf16[336,256]{1,0:T(8,128)(2,1)S(1)}, u32[]{:S(2)}, u32[]{:S(2)}) collective-permute-start(bf16[336,256]{1,0:T(8,128)(2,1)S(1)} %get-tuple-element.94), channel_id=1, source_target_pairs={{0,2},{1,3},{2,0},{3,1},{4,6},{5,7},{6,4},{7,5},{8,10},{9,11},{10,... | collective-permute-start | bytes 516104 | tf_op jit(solution)/shard_map/ppermute | solution.py:38
  121.0 6.4 %collective-permute-start.17 = (bf16[240,256]{1,0:T(8,128)(2,1)S(1)}, bf16[240,256]{1,0:T(8,128)(2,1)S(1)}, u32[]{:S(2)}, u32[]{:S(2)}) collective-permute-start(bf16[240,256]{1,0:T(8,128)(2,1)S(1)} %pad_maximum_fusion.2), channel_id=1, source_target_pairs={{0,1},{1,0},{2,3},{3,2},{4,5},{5,4},{6,7},{7,6},{8,9},{9,8},{10,11... | collective-permute-start | bytes 368648 | tf_op jit(solution)/shard_map/ppermute | solution.py:38
  121.1 12.1 %collective-permute-start.18 = (bf16[240,256]{1,0:T(8,128)(2,1)S(1)}, bf16[240,256]{1,0:T(8,128)(2,1)S(1)}, u32[]{:S(2)}, u32[]{:S(2)}) collective-permute-start(bf16[240,256]{1,0:T(8,128)(2,1)S(1)} %pad_maximum_fusion.3), channel_id=1, source_target_pairs={{0,2},{1,3},{2,0},{3,1},{4,6},{5,7},{6,4},{7,5},{8,10},{9,11},{10,... | collective-permute-start | bytes 368648 | tf_op jit(solution)/shard_map/ppermute | solution.py:38
  122.9 10.3 %collective-permute-start.19 = (bf16[240,256]{1,0:T(8,128)(2,1)S(1)}, bf16[240,256]{1,0:T(8,128)(2,1)S(1)}, u32[]{:S(2)}, u32[]{:S(2)}) collective-permute-start(bf16[240,256]{1,0:T(8,128)(2,1)S(1)} %pad_maximum_fusion.4), channel_id=1, source_target_pairs={{0,3},{1,2},{2,1},{3,0},{4,7},{5,6},{6,5},{7,4},{8,11},{9,10},{10,... | collective-permute-start | bytes 368648 | tf_op jit(solution)/shard_map/ppermute | solution.py:38

commit v8 on v6

--- a/solution.py
+++ b/solution.py
@@ -10,6 +10,7 @@
 
 VMEM_LIMIT = 32 * 1024 * 1024
 VMEM_ALL = 61 * 1024 * 1024
+VMEM_MOST = 52 * 1024 * 1024
 IN_VMEM = pl.BlockSpec(memory_space=pltpu.VMEM)
 IN_SMEM = pl.BlockSpec(memory_space=pltpu.SMEM)
 IN_HBM = pl.BlockSpec(memory_space=pltpu.HBM)
@@ -61,32 +62,26 @@
 ):
     clean, outgoing, down, up, *refs = refs
     packed, refs = refs[:groups], refs[groups:]
-    data, tiles, rhs, stage, results, halos, packs, places, used, sems, tile_sems, pack_sems, out_sems = refs
+    data, tiles, rhs, stage, results, halos, packs, places, used, sems, pack_sems, out_sems = refs
     blocks, slots, rows, _ = adj.shape
     width = gc.shape[1]
     quarter = features.shape[0] // groups
     spare = blocks + 2 * reach
     pad = 2 * reach * rows
 
-    def copies(block):
-        span = pl.ds(pl.multiple_of(block * rows, rows), rows)
-        return [
-            pltpu.make_async_copy(ref.at[span], data.at[i, block], sems.at[i, block])
+    def copies(step):
+        span = slice(2 * step, 2 * step + 2)
+        out = [
+            pltpu.make_async_copy(
+                ref.at[2 * step * rows : (2 * step + 2) * rows], data.at[i, step], sems.at[i, step]
+            )
             for i, ref in enumerate((gc, pc, gx, px))
         ]
-
-    def each_tile(block, act):
-        for k in range(slots):
-            pl.when(k < count[block])(
-                lambda k=k: act(
-                    pltpu.make_async_copy(adj.at[block, k], tiles.at[block, k], tile_sems.at[block, k])
-                )
-            )
-
-    for block in range(blocks):
-        for copy in copies(block):
-            copy.start()
-        each_tile(block, lambda copy: copy.start())
+        return out + [pltpu.make_async_copy(adj.at[span], tiles.at[span], sems.at[4, step])]
+
+    inputs = [copies(step) for step in range(blocks // 2)]
+    for copy in sum(inputs, []):
+        copy.start()
     to_vmem, to_hbm = [], []
     for i in range(groups):
         span = pl.ds(pl.multiple_of((me[1] ^ i) * quarter, quarter), quarter)
@@ -107,40 +102,24 @@
     slope = slopes[...]
     find_places(me, shuffle, blocks, send_slots, places, used)
 
-    def take(block):
-        gradients = [masked_grad(data[i, block], data[i + 1, block], slope) for i in (0, 2)]
-        span = pl.ds(pl.multiple_of(pad + block * rows, rows), rows)
-        rhs[span] = jnp.concatenate(gradients, axis=1)
+    def take(step):
+        gradients = [masked_grad(data[i, step], data[i + 1, step], slope) for i in (0, 2)]
+        rhs[pad + 2 * step * rows : pad + (2 * step + 2) * rows] = jnp.concatenate(gradients, axis=1)
         turned = lax.dot_general(
             identity,
-            tiles[block].reshape(slots * rows, rows),
+            tiles[2 * step : 2 * step + 2].reshape(2 * slots * rows, rows),
             (((1,), (1,)), ((), ())),
             preferred_element_type=jnp.float32,
         )
-        for k in range(slots):
+        for i in range(2 * slots):
+            block, k = 2 * step + i // slots, i % slots
             live = k < count[block]
             target = cols[k, block] - me[0] * blocks
             place = jnp.where(live, target + reach, spare)
             distance = jnp.where(live, block - target + reach, 0)
-            part = turned[:, k * rows : (k + 1) * rows]
+            part = turned[:, i * rows : (i + 1) * rows]
             stage[place, distance] = (wide(stage[place, distance]) + part).astype(jnp.bfloat16)
 
-    per_step = blocks // 2
-
-    @pl.loop(0, blocks // per_step)
-    def _(step):
-        for i in range(per_step):
-            block = step * per_step + i
-            for copy in copies(block):
-                copy.wait()
-            each_tile(block, lambda copy: copy.wait())
-        for i in range(per_step):
-            take(step * per_step + i)
-
-    for copy in to_vmem:
-        copy.wait()
-    for copy in to_hbm:
-        copy.start()
     blank = jnp.zeros(shape, jnp.bfloat16)
 
     def pair(first):
@@ -154,30 +133,45 @@
             ],
             axis=0,
         )
-        span = pl.ds(pl.multiple_of(first * rows, rows), (2 * reach + 2) * rows)
+        span = slice(first * rows, (first + 2 * reach + 2) * rows)
         product = jnp.dot(lhs, rhs[span], preferred_element_type=jnp.float32)
         product = product.astype(jnp.bfloat16).reshape(2, rows, 2 * width)
         return product[:, :, :width], product[:, :, width:]
 
-    for i in range(0, reach, 2):
-        halos[0, 0, i : i + 2], halos[0, 1, i : i + 2] = pair(i)
-        halos[1, 0, i : i + 2], halos[1, 1, i : i + 2] = pair(blocks + reach + i)
-    writes = [
-        pltpu.make_async_copy(halos.at[0], down, out_sems.at[2, 0]),
-        pltpu.make_async_copy(halos.at[1], up, out_sems.at[2, 1]),
-    ]
-    for copy in writes:
-        copy.start()
-    for first in range(0, blocks, 2):
-        span = pl.ds(first, 2)
-        results[0, span], results[1, span] = pair(reach + first)
-        done = [pltpu.make_async_copy(results.at[0, span], clean.at[span], out_sems.at[0, first])]
-        for block in range(first, first + 2):
-            target = outgoing.at[places[block]]
-            done.append(pltpu.make_async_copy(results.at[1, block], target, out_sems.at[1, block]))
+    writes = []
+
+    def finish(first):
+        block = first - reach
+        if 0 <= block < blocks:
+            span = slice(block, block + 2)
+            results[0, span], results[1, span] = pair(first)
+            done = [pltpu.make_async_copy(results.at[0, span], clean.at[span], out_sems.at[0, block])]
+            for i in range(block, block + 2):
+                target = outgoing.at[places[i]]
+                done.append(pltpu.make_async_copy(results.at[1, i], target, out_sems.at[1, i]))
+        else:
+            side, at = int(block >= 0), first % (blocks + reach)
+            halos[side, 0, at : at + 2], halos[side, 1, at : at + 2] = pair(first)
+            out = (down, up)[side]
+            done = []
+            for i in range(2):
+                source, target = halos.at[side, i, at : at + 2], out.at[i, at : at + 2]
+                done.append(pltpu.make_async_copy(source, target, out_sems.at[2 + i, first]))
         for copy in done:
             copy.start()
-        writes += done
+        writes.extend(done)
+
+    for step in range(blocks // 2):
+        for copy in inputs[step]:
+            copy.wait()
+        take(step)
+        finish(2 * step)
+    for copy in to_vmem:
+        copy.wait()
+    for copy in to_hbm:
+        copy.start()
+    for first in range(blocks, blocks + 2 * reach, 2):
+        finish(first)
     for copy in writes + to_hbm:
         copy.wait()
 
@@ -196,7 +190,7 @@
         + [bf16(2, reach, rows, width)] * 2
         + [bf16(packed, width)] * groups,
         scratch_shapes=[
-            pltpu.VMEM((4, blocks, rows, width), jnp.bfloat16),
+            pltpu.VMEM((4, blocks // 2, 2 * rows, width), jnp.bfloat16),
             pltpu.VMEM((blocks, slots, rows, rows), jnp.bfloat16),
             pltpu.VMEM(((blocks + 4 * reach) * rows, 2 * width), jnp.bfloat16),
             pltpu.VMEM((blocks + 2 * reach + 1, 2 * reach + 1, rows, rows), jnp.bfloat16),
@@ -205,10 +199,9 @@
             pltpu.VMEM((groups, packed, width), jnp.bfloat16),
             pltpu.SMEM((blocks,), jnp.int32),
             pltpu.SMEM((devs,), jnp.int32),
-            pltpu.SemaphoreType.DMA((4, blocks)),
-            pltpu.SemaphoreType.DMA((blocks, slots)),
+            pltpu.SemaphoreType.DMA((5, blocks // 2)),
             pltpu.SemaphoreType.DMA((3, groups)),
-            pltpu.SemaphoreType.DMA((3, blocks)),
+            pltpu.SemaphoreType.DMA((4, blocks + 2 * reach)),
         ],
         compiler_params=params(VMEM_ALL),
         cost_estimate=pl.CostEstimate(
@@ -220,73 +213,63 @@
     )(index, shuffle, cols, count, gc, pc, gx, px, slopes, adj, features, weight)
 
 
-def patch_kernel(reach, slots, index, shuffle, clean, outgoing, low, high, clean_out, outgoing_out, *scratch):
-    held, other, ready, places, used, sems = scratch
-    blocks = clean.shape[0]
+def patch_kernel(reach, blocks, slots, index, shuffle, outgoing, low, high, out, held, ready, places, used, sems):
+    find_places(index, shuffle, blocks, slots, places, used)
     border = [*range(reach), *range(blocks - reach, blocks)]
-    arrivals = [
-        pltpu.make_async_copy(low, other.at[0], sems.at[2, 0, 0]),
-        pltpu.make_async_copy(high, other.at[1], sems.at[2, 0, 1]),
-    ]
-    for copy in arrivals:
-        copy.start()
-    find_places(index, shuffle, blocks, slots, places, used)
-
-    def spot(i, which, first, second):
-        return second.at[places[border[i]]] if which else first.at[border[i]]
-
-    order = [(i, which) for i in range(2 * reach) for which in range(2)]
     reads, writes = [], []
-    for i, which in order:
-        source, target = spot(i, which, clean, outgoing), spot(i, which, clean_out, outgoing_out)
-        reads.append(pltpu.make_async_copy(source, held.at[which, i], sems.at[0, which, i]))
-        writes.append(pltpu.make_async_copy(ready.at[which, i], target, sems.at[1, which, i]))
+    for i, block in enumerate(border):
+        place = places[block]
+        reads.append(pltpu.make_async_copy(outgoing.at[place], held.at[i], sems.at[0, i]))
+        writes.append(pltpu.make_async_copy(ready.at[i], out.at[place], sems.at[1, i]))
     for copy in reads:
         copy.start()
-    for copy in arrivals:
-        copy.wait()
-    for (i, which), read, write in zip(order, reads, writes):
+    for i, (read, write) in enumerate(zip(reads, writes)):
         read.wait()
-        total = wide(held[which, i]) + wide(other[i // reach, which, i % reach])
-        ready[which, i] = total.astype(jnp.bfloat16)
+        other = low[1, i] if i < reach else high[1, i - reach]
+        ready[i] = (wide(held[i]) + wide(other)).astype(jnp.bfloat16)
         write.start()
     for copy in writes:
         copy.wait()
 
 
-def patch(index, shuffle, clean, outgoing, low, high, slots):
-    blocks, rows, width = clean.shape
+def patch(index, shuffle, outgoing, low, high, blocks, slots):
+    sent, rows, width = outgoing.shape
     reach = low.shape[1]
-    blocks_shape = (2, 2 * reach, rows, width)
+    border = pltpu.VMEM((2 * reach, rows, width), jnp.bfloat16)
     return pl.pallas_call(
-        functools.partial(patch_kernel, reach, slots),
-        in_specs=[IN_SMEM] * 2 + [IN_HBM] * 4,
-        out_specs=[IN_HBM] * 2,
-        out_shape=[bf16(*clean.shape), bf16(*outgoing.shape)],
-        input_output_aliases={2: 0, 3: 1},
+        functools.partial(patch_kernel, reach, blocks, slots),
+        in_specs=[IN_SMEM] * 2 + [IN_HBM] + [IN_VMEM] * 2,
+        out_specs=IN_HBM,
+        out_shape=bf16(*outgoing.shape),
+        input_output_aliases={2: 0},
         scratch_shapes=[
-            pltpu.VMEM(blocks_shape, jnp.bfloat16),
-            pltpu.VMEM((2, 2, reach, rows, width), jnp.bfloat16),
-            pltpu.VMEM(blocks_shape, jnp.bfloat16),
+            border,
+            border,
             pltpu.SMEM((blocks,), jnp.int32),
-            pltpu.SMEM((outgoing.shape[0] // slots,), jnp.int32),
-            pltpu.SemaphoreType.DMA((3, 2, 2 * reach)),
+            pltpu.SMEM((sent // slots,), jnp.int32),
+            pltpu.SemaphoreType.DMA((2, 2 * reach)),
         ],
-        compiler_params=params(VMEM_ALL),
+        compiler_params=params(VMEM_MOST),
         name="patch",
-    )(index, shuffle, clean, outgoing, low, high)
-
-
-def merge_kernel(quarter, index, landing, clean, incoming, out):
-    _, rows, _ = clean.shape
+    )(index, shuffle, outgoing, low, high)
+
+
+def merge_kernel(quarter, index, landing, clean, low, high, incoming, out, whole):
+    blocks, rows, _ = clean.shape
+    reach = low.shape[1]
     group = index[1]
     piece = math.gcd(rows, quarter)
+    for block in range(blocks):
+        whole[block] = wide(clean[block])
+    for i in range(reach):
+        whole[i] += wide(low[0, i])
+        whole[blocks - reach + i] += wide(high[0, i])
     for place in range(incoming.shape[0]):
         block = landing[place]
 
         @pl.when(block >= 0)
         def _():
-            total = (wide(clean[block]) + wide(incoming[place])).astype(jnp.bfloat16)
+            total = (whole[block] + wide(incoming[place])).astype(jnp.bfloat16)
             for part in range(rows // piece):
                 at = block * (rows // piece) + part
                 owner = at // (quarter // piece)
@@ -296,17 +279,18 @@
                 ]
 
 
-def merge(index, landing, clean, incoming, groups):
+def merge(index, landing, clean, low, high, incoming, groups):
     blocks, rows, width = clean.shape
     quarter = blocks * rows // groups
     return pl.pallas_call(
         functools.partial(merge_kernel, quarter),
-        in_specs=[IN_SMEM] * 2 + [IN_VMEM] * 2,
+        in_specs=[IN_SMEM] * 2 + [IN_VMEM] * 4,
         out_specs=IN_VMEM,
         out_shape=bf16(groups, quarter, width),
+        scratch_shapes=[pltpu.VMEM((blocks, rows, width), jnp.float32)],
         compiler_params=params(),
         name="merge",
-    )(index, landing, clean, incoming)
+    )(index, landing, clean, low, high, incoming)
 
 
 def weight_kernel(devs, index, *refs):
@@ -481,21 +465,22 @@
     for i in exchange_order(groups):
         packed[i] = swapped(packed[i], "chan", i)
 
-    clean, outgoing = patch(index, shuffle_from, clean, outgoing, from_prev, from_next, slots)
+    outgoing = patch(index, shuffle_from, outgoing, from_prev, from_next, blocks, slots)
     shuffle_from, outgoing = lax.optimization_barrier((shuffle_from, outgoing))
     landing = landing_blocks(shuffle_from, me, blocks, devs, slots)
     incoming = exchanged(outgoing, "node")
     incoming, packed = lax.optimization_barrier((incoming, packed))
-    merged = merge(index, landing, clean, incoming, groups)
+    merged = merge(index, landing, clean, from_prev, from_next, incoming, groups)
 
     quarter = row_count // groups
     summed = [merged[0]] + [None] * (groups - 1)
-    for i in exchange_order(groups):
+    for i in [1, *exchange_order(groups)[:-1]]:
         summed[i] = swapped(merged[i], "chan", i)
     tiles = jnp.stack([piece[quarter:] for piece in packed])
     even = [tiles] + [swapped(tiles, "node", 2 * i) for i in range(1, devs // 2)]
     early = devs // 2 - 1
-    summed, even[:early] = lax.optimization_barrier((summed, even[:early]))
+    rest, even[:early] = lax.optimization_barrier((summed[::-1], even[:early]))
+    summed = rest[::-1]
     even = jnp.stack(even)
     odd = swapped(even, "node", 1)
 

time: 114 us -> 114 us (level)
  starting transfers between devices: 50.7 us -> 47.1 us
  waiting for transfers between devices: 38.3 us -> 41.6 us
  local copies, waits for them, and re-layouts: 1.43 us -> 2.83 us
    ppermute x20, waiting for transfers between devices: 30.5 us -> 34.1 us  [swapped(): return lax.ppermute(value, axis, [(i, i ^ by) for i in range(size)])]
    ppermute x20, starting transfers between devices: 39.2 us -> 35.7 us  [swapped(): return lax.ppermute(value, axis, [(i, i ^ by) for i in range(size)])]
    unnamed x12, local copies, waits for them, and re-layouts: 0.81 us -> 2.21 us
    pallas_call x1, Pallas kernels: 2.84 us -> 1.46 us  [patch(): pl.pallas_call(functools.partial(patch_kernel, reach, blocks, slots), in_...]
  transfers between devices with their start and end apart: 23 -> 23, of which waited for: 10 -> 7; matrix products, arithmetic and copies ran while one was open for 1% -> 1% of each run, Pallas kernels for 8% -> 6%
where the time goes in v8:
time: 114 us
  starting transfers between devices  47.1 us (41%)
  waiting for transfers between devices  41.6 us (36%)
  Pallas kernels  19 us (17%)
  local copies, waits for them, and re-layouts  2.83 us (2%)
  other arithmetic  2.54 us (2%)
    ppermute x20, starting transfers between devices, swapped(): return lax.ppermute(value, axis, [(i, i ^ by) for i in range(size)])  35.7 us
    ppermute x20, waiting for transfers between devices, swapped(): return lax.ppermute(value, axis, [(i, i ^ by) for i in range(size)])  34.1 us
    pallas_call x1, Pallas kernels, aggregate(): pl.pallas_call(functools.partial(aggregate_kernel, reach, groups, send_sl...  9.09 us
    all_to_all x1, starting transfers between devices, exchanged(): return lax.all_to_all(value, axis, split_axis=0, concat_axis=0, tiled=True)  7.67 us
    all_to_all x1, waiting for transfers between devices, exchanged(): return lax.all_to_all(value, axis, split_axis=0, concat_axis=0, tiled=True)  7.53 us
    ppermute x2, starting transfers between devices, shifted(): return lax.ppermute(value, axis, pairs)  3.71 us
    pallas_call x1, Pallas kernels, feature_rows(): pl.pallas_call(feature_kernel, in_specs=[IN_SMEM] + [IN_VMEM] * (groups +...  3.23 us
    pallas_call x1, Pallas kernels, weight_partial(): pl.pallas_call(functools.partial(weight_kernel, devs), in_specs=[IN_SMEM]...  2.62 us
  transfers between devices with their start and end apart: 23, of which 7 were waited for; matrix products, arithmetic and copies ran while one was open for 1% of the time, Pallas kernels for 6%

profile of v8, /device:TPU:0, one launch (start us, length us, event | category | flops | bytes accessed | tf_op | source)
XLA Modules:
  0.0 113.9 jit_solution(15517050158034774301)
XLA Ops:
  0.6 0.6 pad_add_fusion.me.index
  1.2 9.1 %aggregate.1 = (bf16[14,128,256]{2,1,0:T(8,128)(2,1)}, bf16[16,128,256]{2,1,0:T(8,128)(2,1)}, bf16[2,2,128,256]{3,2,1,0:T(8,128)(2,1)}, bf16[2,2,128,256]{3,2,1,...) custom-call(s32[2]{0:T(128)} %pad_add_fusion.me.index, ...), custom_call_target="tpu_custom_call" | custom-call | flops 1174405120 | bytes 7798784 | tf_op jit(solution)/shard_map/aggregate/pallas_call | solution.py:185
  10.3 2.4 %collective-permute-start = (bf16[2,2,128,256]{3,2,1,0:T(8,128)(2,1)}, bf16[2,2,128,256]{3,2,1,0:T(8,128)(2,1)S(1)}, u32[]{:S(2)}, u32[]{:S(2)}) collective-permute-start(bf16[2,2,128,256]{3,2,1,0:T(8,128)(2,1)} %get-tuple-element.37), channel_id=1, source_target_pairs={{0,4},{4,8},{8,12},{12,16},{16,20},{20,24},{24,28},{1,5},{5,9},{9,... | collective-permute-start | bytes 786440 | tf_op jit(solution)/shard_map/ppermute | solution.py:34
  12.8 1.3 %collective-permute-start.1 = (bf16[2,2,128,256]{3,2,1,0:T(8,128)(2,1)}, bf16[2,2,128,256]{3,2,1,0:T(8,128)(2,1)S(1)}, u32[]{:S(2)}, u32[]{:S(2)}) collective-permute-start(bf16[2,2,128,256]{3,2,1,0:T(8,128)(2,1)} %get-tuple-element.38), channel_id=1, source_target_pairs={{4,0},{8,4},{12,8},{16,12},{20,16},{24,20},{28,24},{5,1},{9,5},{13... | collective-permute-start | bytes 786440 | tf_op jit(solution)/shard_map/ppermute | solution.py:34
  14.1 2.5 %collective-permute-start.2 = (bf16[576,256]{1,0:T(8,128)(2,1)}, bf16[576,256]{1,0:T(8,128)(2,1)S(1)}, u32[]{:S(2)}, u32[]{:S(2)}) collective-permute-start(bf16[576,256]{1,0:T(8,128)(2,1)} %get-tuple-element.41), channel_id=1, source_target_pairs={{0,1},{1,0},{2,3},{3,2},{4,5},{5,4},{6,7},{7,6},{8,9},{9,8},{10,11... | collective-permute-start | bytes 884744 | tf_op jit(solution)/shard_map/ppermute | solution.py:39
  16.5 2.6 %collective-permute-start.3 = (bf16[576,256]{1,0:T(8,128)(2,1)}, bf16[576,256]{1,0:T(8,128)(2,1)S(1)}, u32[]{:S(2)}, u32[]{:S(2)}) collective-permute-start(bf16[576,256]{1,0:T(8,128)(2,1)} %get-tuple-element.42), channel_id=1, source_target_pairs={{0,2},{1,3},{2,0},{3,1},{4,6},{5,7},{6,4},{7,5},{8,10},{9,11},{10,... | collective-permute-start | bytes 884744 | tf_op jit(solution)/shard_map/ppermute | solution.py:39
  19.1 0.0 collective-permute-start.4
  19.1 0.0 collective-permute-done.low
  19.1 0.0 collective-permute-done.1.high
  19.2 1.2 %copy-done = bf16[16,128,256]{2,1,0:T(8,128)(2,1)S(1)} copy-done((bf16[16,128,256]{2,1,0:T(8,128)(2,1)S(1)}, bf16[16,128,256]{2,1,0:T(8,128)(2,1)}, u32[]{:S(2)}) %copy-start) | copy-done | bytes 1048600
  20.4 1.5 %patch.1 = bf16[16,128,256]{2,1,0:T(8,128)(2,1)S(1)} custom-call(s32[2]{0:T(128)S(1)} %copy-done.4, s32[112]{0:T(128)S(1)} %copy-done.5, bf16[16,128,256]{2,1,0:T(8,128)(2,1)S(1)} %copy-done, bf16[2,2,128,256]{3,2,1,0:T(8,128)(2,1)S(1)} %collective-permute-done.low, ...), custom_call_target="tpu_custom_call", output_to_operand_aliasing={{}: (2, {})} | custom-call | tf_op jit(solution)/shard_map/patch/pallas_call | solution.py:239
  21.9 1.0 copy-done.1
  22.8 7.7 %all-to-all-start = ((bf16[16,128,256]{2,1,0:T(8,128)(2,1)}), bf16[16,128,256]{2,1,0:T(8,128)(2,1)S(1)}, u32[]{:S(2)}, u32[]{:S(2)}) async-start(bf16[16,128,256]{2,1,0:T(8,128)(2,1)} %copy-done.1), calls=%async_computation | async-start | bytes 2097152 | tf_op jit(solution)/shard_map/all_to_all | solution.py:43
  30.6 0.1 eq.30
  30.7 0.1 add.45
  30.7 0.3 convert_reduce_fusion
  31.1 0.1 copy.14
  31.1 0.1 select_reduce_fusion
  31.3 0.1 copy.15
  31.4 0.1 sub.13.landing
  31.5 0.0 collective-permute-done.2.refs_1_
  31.5 0.0 collective-permute-done.3.refs_2_
  31.5 6.9 %collective-permute-done.4.refs_3_ = bf16[576,256]{1,0:T(8,128)(2,1)S(1)} collective-permute-done((bf16[576,256]{1,0:T(8,128)(2,1)}, bf16[576,256]{1,0:T(8,128)(2,1)S(1)}, u32[]{:S(2)}, u32[]{:S(2)}) %collective-permute-start.4) | collective-permute-done | bytes 294944 | tf_op jit(solution)/shard_map/ppermute | solution.py:39
  38.4 7.5 %all-to-all-done.incoming = bf16[16,128,256]{2,1,0:T(8,128)(2,1)S(1)} async-done(((bf16[16,128,256]{2,1,0:T(8,128)(2,1)}), bf16[16,128,256]{2,1,0:T(8,128)(2,1)S(1)}, u32[]{:S(2)}, u32[]{:S(2)}) %all-to-all-start) | async-done | bytes 1048608 | tf_op jit(solution)/shard_map/all_to_all | solution.py:43
  45.9 1.0 merge.1
  47.0 0.1 slice_bitcast_fusion.4
  47.1 1.4 %collective-permute-start.7 = (bf16[448,256]{1,0:T(8,128)(2,1)S(1)}, bf16[448,256]{1,0:T(8,128)(2,1)S(1)}, u32[]{:S(2)}, u32[]{:S(2)}) collective-permute-start(bf16[448,256]{1,0:T(8,128)(2,1)S(1)} %get-tuple-element.86), channel_id=1, source_target_pairs={{0,1},{1,0},{2,3},{3,2},{4,5},{5,4},{6,7},{7,6},{8,9},{9,8},{10,11... | collective-permute-start | bytes 688136 | tf_op jit(solution)/shard_map/ppermute | solution.py:39
  48.5 2.6 %collective-permute-start.9 = (bf16[4,128,256]{2,1,0:T(8,128)(2,1)S(1)}, bf16[4,128,256]{2,1,0:T(8,128)(2,1)S(1)}, u32[]{:S(2)}, u32[]{:S(2)}) collective-permute-start(bf16[4,128,256]{2,1,0:T(8,128)(2,1)S(1)} %pad_maximum_fusion.1), channel_id=1, source_target_pairs={{0,16},{4,20},{8,24},{12,28},{16,0},{20,4},{24,8},{28,12},{1,17},{... | collective-permute-start | bytes 786440 | tf_op jit(solution)/shard_map/ppermute | solution.py:39
  51.1 0.4 collective-permute-start.8
  51.5 1.1 collective-permute-start.10
  52.7 2.3 %collective-permute-start.6 = (bf16[448,256]{1,0:T(8,128)(2,1)S(1)}, bf16[448,256]{1,0:T(8,128)(2,1)S(1)}, u32[]{:S(2)}, u32[]{:S(2)}) collective-permute-start(bf16[448,256]{1,0:T(8,128)(2,1)S(1)} %get-tuple-element.87), channel_id=1, source_target_pairs={{0,2},{1,3},{2,0},{3,1},{4,6},{5,7},{6,4},{7,5},{8,10},{9,11},{10,... | collective-permute-start | bytes 688136 | tf_op jit(solution)/shard_map/ppermute | solution.py:39
  54.9 0.0 collective-permute-done.7.refs_5_.refs_1_
  54.9 1.9 %collective-permute-start.5 = (bf16[448,256]{1,0:T(8,128)(2,1)S(1)}, bf16[448,256]{1,0:T(8,128)(2,1)S(1)}, u32[]{:S(2)}, u32[]{:S(2)}) collective-permute-start(bf16[448,256]{1,0:T(8,128)(2,1)S(1)} %get-tuple-element.88), channel_id=1, source_target_pairs={{0,3},{1,2},{2,1},{3,0},{4,7},{5,6},{6,5},{7,4},{8,11},{9,10},{10,... | collective-permute-start | bytes 688136 | tf_op jit(solution)/shard_map/ppermute | solution.py:39
  56.9 14.2 %collective-permute-done.6.refs_6_.refs_2_ = bf16[448,256]{1,0:T(8,128)(2,1)S(1)} collective-permute-done((bf16[448,256]{1,0:T(8,128)(2,1)S(1)}, bf16[448,256]{1,0:T(8,128)(2,1)S(1)}, u32[]{:S(2)}, u32[]{:S(2)}) %collective-permute-start.6) | collective-permute-done | bytes 229408 | tf_op jit(solution)/shard_map/ppermute | solution.py:39
  71.1 0.0 collective-permute-done.5.refs_7_.refs_3_
  71.1 0.0 collective-permute-done.9
  71.1 0.0 collective-permute-done.8
  71.1 0.0 collective-permute-done.10
  71.1 0.1 pad_maximum_fusion.refs_4_
  71.3 0.1 collective-permute-start.11
  71.3 2.6 %weight_partial.1 = (bf16[4,4,128,256]{3,2,1,0:T(8,128)(2,1)S(1)}, bf16[4,4,128,256]{3,2,1,0:T(8,128)(2,1)S(1)}) custom-call(s32[2]{0:T(128)S(1)} %copy-done.4, bf16[576,256]{1,0:T(8,128)(2,1)S(1)} %copy-done.3, bf16[576,256]{1,0:T(8,128)(2,1)S(1)} %collective-permute-done.2.refs_1_, bf16[576,256]{1,0:T(8,128)(2,1)S(1)} %collective-permute-done.3.refs_2_, ...), custom_call_target="tpu_custom_call" | custom-call | flops 939524096 | bytes 3932160 | tf_op jit(solution)/shard_map/weight_partial/pallas_call | solution.py:326
  74.0 0.0 collective-permute-done.11.refs_5_
  74.0 0.5 collective-permute-start.12
  74.5 3.2 %feature_rows.1 = bf16[4,448,256]{2,1,0:T(8,128)(2,1)S(1)} custom-call(s32[2]{0:T(128)S(1)} %copy-done.4, bf16[448,256]{1,0:T(8,128)(2,1)S(1)} %get-tuple-element.51.refs_4_.refs_0_, bf16[448,256]{1,0:T(8,128)(2,1)S(1)} %collective-permute-done.7.refs_5_.refs_1_, bf16[448,256]{1,0:T(8,128)(2,1)S(1)} %collective-permute-done.6.refs_6_.refs_2_, ...), custom_call_target="tpu_custom_call" | custom-call | flops 939524096 | bytes 3932160 | tf_op jit(solution)/shard_map/feature_rows/pallas_call | solution.py:374
  77.8 0.0 collective-permute-done.12
  77.8 1.6 %collective-permute-start.15 = (bf16[336,256]{1,0:T(8,128)(2,1)S(1)}, bf16[336,256]{1,0:T(8,128)(2,1)S(1)}, u32[]{:S(2)}, u32[]{:S(2)}) collective-permute-start(bf16[336,256]{1,0:T(8,128)(2,1)S(1)} %get-tuple-element.82), channel_id=1, source_target_pairs={{0,3},{1,2},{2,1},{3,0},{4,7},{5,6},{6,5},{7,4},{8,11},{9,10},{10,... | collective-permute-start | bytes 516104 | tf_op jit(solution)/shard_map/ppermute | solution.py:39
  79.4 0.4 convert_add_fusion
  79.8 0.1 slice_bitcast_fusion.1
  79.9 1.0 collective-permute-start.18
  80.8 1.9 %collective-permute-start.17 = (bf16[4,128,256]{2,1,0:T(8,128)(2,1)S(1)}, bf16[4,128,256]{2,1,0:T(8,128)(2,1)S(1)}, u32[]{:S(2)}, u32[]{:S(2)}) collective-permute-start(bf16[4,128,256]{2,1,0:T(8,128)(2,1)S(1)} %get-tuple-element.75), channel_id=1, source_target_pairs={{0,16},{4,20},{8,24},{12,28},{16,0},{20,4},{24,8},{28,12},{1,17},{... | collective-permute-start | bytes 786440 | tf_op jit(solution)/shard_map/ppermute | solution.py:39
  82.7 0.7 collective-permute-start.16
  83.4 3.5 %collective-permute-start.14 = (bf16[336,256]{1,0:T(8,128)(2,1)S(1)}, bf16[336,256]{1,0:T(8,128)(2,1)S(1)}, u32[]{:S(2)}, u32[]{:S(2)}) collective-permute-start(bf16[336,256]{1,0:T(8,128)(2,1)S(1)} %get-tuple-element.83), channel_id=1, source_target_pairs={{0,2},{1,3},{2,0},{3,1},{4,6},{5,7},{6,4},{7,5},{8,10},{9,11},{10,... | collective-permute-start | bytes 516104 | tf_op jit(solution)/shard_map/ppermute | solution.py:39
  86.9 0.0 collective-permute-done.15.refs_3_
  86.9 7.1 %collective-permute-start.13 = (bf16[336,256]{1,0:T(8,128)(2,1)S(1)}, bf16[336,256]{1,0:T(8,128)(2,1)S(1)}, u32[]{:S(2)}, u32[]{:S(2)}) collective-permute-start(bf16[336,256]{1,0:T(8,128)(2,1)S(1)} %get-tuple-element.84), channel_id=1, source_target_pairs={{0,1},{1,0},{2,3},{3,2},{4,5},{5,4},{6,7},{7,6},{8,9},{9,8},{10,11... | collective-permute-start | bytes 516104 | tf_op jit(solution)/shard_map/ppermute | solution.py:39
  94.0 3.1 %collective-permute-done.14.refs_2_ = bf16[336,256]{1,0:T(8,128)(2,1)S(1)} collective-permute-done((bf16[336,256]{1,0:T(8,128)(2,1)S(1)}, bf16[336,256]{1,0:T(8,128)(2,1)S(1)}, u32[]{:S(2)}, u32[]{:S(2)}) %collective-permute-start.14) | collective-permute-done | bytes 172064 | tf_op jit(solution)/shard_map/ppermute | solution.py:39
  97.2 3.6 %collective-permute-done.13.refs_1_ = bf16[336,256]{1,0:T(8,128)(2,1)S(1)} collective-permute-done((bf16[336,256]{1,0:T(8,128)(2,1)S(1)}, bf16[336,256]{1,0:T(8,128)(2,1)S(1)}, u32[]{:S(2)}, u32[]{:S(2)}) %collective-permute-start.13) | collective-permute-done | bytes 172064 | tf_op jit(solution)/shard_map/ppermute | solution.py:39
  100.8 0.2 fusion.10
  101.0 0.1 collective-permute-start.20
  101.1 2.2 %collective-permute-start.21 = (bf16[240,256]{1,0:T(8,128)(2,1)S(1)}, bf16[240,256]{1,0:T(8,128)(2,1)S(1)}, u32[]{:S(2)}, u32[]{:S(2)}) collective-permute-start(bf16[240,256]{1,0:T(8,128)(2,1)S(1)} %pad_maximum_fusion.4), channel_id=1, source_target_pairs={{0,1},{1,0},{2,3},{3,2},{4,5},{5,4},{6,7},{7,6},{8,9},{9,8},{10,11... | collective-permute-start | bytes 368648 | tf_op jit(solution)/shard_map/ppermute | solution.py:39
  103.2 2.3 %collective-permute-start.19 = (bf16[240,256]{1,0:T(8,128)(2,1)S(1)}, bf16[240,256]{1,0:T(8,128)(2,1)S(1)}, u32[]{:S(2)}, u32[]{:S(2)}) collective-permute-start(bf16[240,256]{1,0:T(8,128)(2,1)S(1)} %pad_maximum_fusion.2), channel_id=1, source_target_pairs={{0,3},{1,2},{2,1},{3,0},{4,7},{5,6},{6,5},{7,4},{8,11},{9,10},{10,... | collective-permute-start | bytes 368648 | tf_op jit(solution)/shard_map/ppermute | solution.py:39
  105.6 6.0 %collective-permute-done.20.refs_6_ = bf16[240,256]{1,0:T(8,128)(2,1)S(1)} collective-permute-done((bf16[240,256]{1,0:T(8,128)(2,1)S(1)}, bf16[240,256]{1,0:T(8,128)(2,1)S(1)}, u32[]{:S(2)}, u32[]{:S(2)}) %collective-permute-start.20) | collective-permute-done | bytes 122912 | tf_op jit(solution)/shard_map/ppermute | solution.py:39
  111.6 0.1 collective-permute-done.21.refs_5_
  111.7 0.7 fusion.5
  112.4 1.5 %laid_out.1 = bf16[1792,256]{1,0:T(8,128)(2,1)} custom-call(s32[2]{0:T(128)S(1)} %copy-done.4, bf16[336,256]{1,0:T(8,128)(2,1)S(1)} %get-tuple-element.81.refs_0_, bf16[336,256]{1,0:T(8,128)(2,1)S(1)} %collective-permute-done.13.refs_1_, bf16[336,256]{1,0:T(8,128)(2,1)S(1)} %collective-permute-done.14.refs_2_, ...), custom_call_target="tpu_custom_call" | custom-call | tf_op jit(solution)/shard_map/laid_out/pallas_call | solution.py:412
  (27 shorter events, 0.2 us)
Async XLA Ops:
  1.2 17.9 %copy-start.4 = (s32[2]{0:T(128)S(1)}, s32[2]{0:T(128)}, u32[]{:S(2)}) copy-start(s32[2]{0:T(128)} %pad_add_fusion.me.index) | copy-start | bytes 28
  1.2 17.9 %copy-start.5 = (s32[112]{0:T(128)S(1)}, s32[112]{0:T(128)}, u32[]{:S(2)}) copy-start(s32[112]{0:T(128)} %shuffle.3) | copy-start | bytes 1348
  10.3 8.8 %collective-permute-start = (bf16[2,2,128,256]{3,2,1,0:T(8,128)(2,1)}, bf16[2,2,128,256]{3,2,1,0:T(8,128)(2,1)S(1)}, u32[]{:S(2)}, u32[]{:S(2)}) collective-permute-start(bf16[2,2,128,256]{3,2,1,0:T(8,128)(2,1)} %get-tuple-element.37), channel_id=1, source_target_pairs={{0,4},{4,8},{8,12},{12,16},{16,20},{20,24},{24,28},{1,5},{5,9},{9,... | collective-permute-start | bytes 786440 | tf_op jit(solution)/shard_map/ppermute | solution.py:34
  12.8 6.4 %collective-permute-start.1 = (bf16[2,2,128,256]{3,2,1,0:T(8,128)(2,1)}, bf16[2,2,128,256]{3,2,1,0:T(8,128)(2,1)S(1)}, u32[]{:S(2)}, u32[]{:S(2)}) collective-permute-start(bf16[2,2,128,256]{3,2,1,0:T(8,128)(2,1)} %get-tuple-element.38), channel_id=1, source_target_pairs={{4,0},{8,4},{12,8},{16,12},{20,16},{24,20},{28,24},{5,1},{9,5},{13... | collective-permute-start | bytes 786440 | tf_op jit(solution)/shard_map/ppermute | solution.py:34
  14.1 17.4 %collective-permute-start.2 = (bf16[576,256]{1,0:T(8,128)(2,1)}, bf16[576,256]{1,0:T(8,128)(2,1)S(1)}, u32[]{:S(2)}, u32[]{:S(2)}) collective-permute-start(bf16[576,256]{1,0:T(8,128)(2,1)} %get-tuple-element.41), channel_id=1, source_target_pairs={{0,1},{1,0},{2,3},{3,2},{4,5},{5,4},{6,7},{7,6},{8,9},{9,8},{10,11... | collective-permute-start | bytes 884744 | tf_op jit(solution)/shard_map/ppermute | solution.py:39
  16.5 14.9 %collective-permute-start.3 = (bf16[576,256]{1,0:T(8,128)(2,1)}, bf16[576,256]{1,0:T(8,128)(2,1)S(1)}, u32[]{:S(2)}, u32[]{:S(2)}) collective-permute-start(bf16[576,256]{1,0:T(8,128)(2,1)} %get-tuple-element.42), channel_id=1, source_target_pairs={{0,2},{1,3},{2,0},{3,1},{4,6},{5,7},{6,4},{7,5},{8,10},{9,11},{10,... | collective-permute-start | bytes 884744 | tf_op jit(solution)/shard_map/ppermute | solution.py:39
  19.1 19.3 %collective-permute-start.4 = (bf16[576,256]{1,0:T(8,128)(2,1)}, bf16[576,256]{1,0:T(8,128)(2,1)S(1)}, u32[]{:S(2)}, u32[]{:S(2)}) collective-permute-start(bf16[576,256]{1,0:T(8,128)(2,1)} %get-tuple-element.43), channel_id=1, source_target_pairs={{0,3},{1,2},{2,1},{3,0},{4,7},{5,6},{6,5},{7,4},{8,11},{9,10},{10,... | collective-permute-start | bytes 884744 | tf_op jit(solution)/shard_map/ppermute | solution.py:39
  19.2 1.2 %copy-start = (bf16[16,128,256]{2,1,0:T(8,128)(2,1)S(1)}, bf16[16,128,256]{2,1,0:T(8,128)(2,1)}, u32[]{:S(2)}) copy-start(bf16[16,128,256]{2,1,0:T(8,128)(2,1)} %get-tuple-element.36.outgoing) | copy-start | bytes 3145732
  20.4 25.5 %copy-start.2 = (bf16[14,128,256]{2,1,0:T(8,128)(2,1)S(1)}, bf16[14,128,256]{2,1,0:T(8,128)(2,1)}, u32[]{:S(2)}) copy-start(bf16[14,128,256]{2,1,0:T(8,128)(2,1)} %get-tuple-element.49.clean) | copy-start | bytes 2752516
  21.9 1.0 copy-start.1
  22.8 23.1 %all-to-all-start = ((bf16[16,128,256]{2,1,0:T(8,128)(2,1)}), bf16[16,128,256]{2,1,0:T(8,128)(2,1)S(1)}, u32[]{:S(2)}, u32[]{:S(2)}) async-start(bf16[16,128,256]{2,1,0:T(8,128)(2,1)} %copy-done.1), calls=%async_computation | async-start | bytes 2097152 | tf_op jit(solution)/shard_map/all_to_all | solution.py:43
  45.9 2.5 %copy-start.3 = (bf16[576,256]{1,0:T(8,128)(2,1)S(1)}, bf16[576,256]{1,0:T(8,128)(2,1)}, u32[]{:S(2)}) copy-start(bf16[576,256]{1,0:T(8,128)(2,1)} %get-tuple-element.44.refs_0_) | copy-start | bytes 884740
  47.1 7.9 %collective-permute-start.7 = (bf16[448,256]{1,0:T(8,128)(2,1)S(1)}, bf16[448,256]{1,0:T(8,128)(2,1)S(1)}, u32[]{:S(2)}, u32[]{:S(2)}) collective-permute-start(bf16[448,256]{1,0:T(8,128)(2,1)S(1)} %get-tuple-element.86), channel_id=1, source_target_pairs={{0,1},{1,0},{2,3},{3,2},{4,5},{5,4},{6,7},{7,6},{8,9},{9,8},{10,11... | collective-permute-start | bytes 688136 | tf_op jit(solution)/shard_map/ppermute | solution.py:39
  48.5 22.6 %collective-permute-start.9 = (bf16[4,128,256]{2,1,0:T(8,128)(2,1)S(1)}, bf16[4,128,256]{2,1,0:T(8,128)(2,1)S(1)}, u32[]{:S(2)}, u32[]{:S(2)}) collective-permute-start(bf16[4,128,256]{2,1,0:T(8,128)(2,1)S(1)} %pad_maximum_fusion.1), channel_id=1, source_target_pairs={{0,16},{4,20},{8,24},{12,28},{16,0},{20,4},{24,8},{28,12},{1,17},{... | collective-permute-start | bytes 786440 | tf_op jit(solution)/shard_map/ppermute | solution.py:39
  51.1 20.0 %collective-permute-start.8 = (bf16[4,128,256]{2,1,0:T(8,128)(2,1)S(1)}, bf16[4,128,256]{2,1,0:T(8,128)(2,1)S(1)}, u32[]{:S(2)}, u32[]{:S(2)}) collective-permute-start(bf16[4,128,256]{2,1,0:T(8,128)(2,1)S(1)} %pad_maximum_fusion.1), channel_id=1, source_target_pairs={{0,8},{4,12},{8,0},{12,4},{16,24},{20,28},{24,16},{28,20},{1,9},{5... | collective-permute-start | bytes 786440 | tf_op jit(solution)/shard_map/ppermute | solution.py:39
  51.5 19.6 %collective-permute-start.10 = (bf16[4,128,256]{2,1,0:T(8,128)(2,1)S(1)}, bf16[4,128,256]{2,1,0:T(8,128)(2,1)S(1)}, u32[]{:S(2)}, u32[]{:S(2)}) collective-permute-start(bf16[4,128,256]{2,1,0:T(8,128)(2,1)S(1)} %pad_maximum_fusion.1), channel_id=1, source_target_pairs={{0,24},{4,28},{8,16},{12,20},{16,8},{20,12},{24,0},{28,4},{1,25},{... | collective-permute-start | bytes 786440 | tf_op jit(solution)/shard_map/ppermute | solution.py:39
  52.7 18.4 %collective-permute-start.6 = (bf16[448,256]{1,0:T(8,128)(2,1)S(1)}, bf16[448,256]{1,0:T(8,128)(2,1)S(1)}, u32[]{:S(2)}, u32[]{:S(2)}) collective-permute-start(bf16[448,256]{1,0:T(8,128)(2,1)S(1)} %get-tuple-element.87), channel_id=1, source_target_pairs={{0,2},{1,3},{2,0},{3,1},{4,6},{5,7},{6,4},{7,5},{8,10},{9,11},{10,... | collective-permute-start | bytes 688136 | tf_op jit(solution)/shard_map/ppermute | solution.py:39
  54.9 16.2 %collective-permute-start.5 = (bf16[448,256]{1,0:T(8,128)(2,1)S(1)}, bf16[448,256]{1,0:T(8,128)(2,1)S(1)}, u32[]{:S(2)}, u32[]{:S(2)}) collective-permute-start(bf16[448,256]{1,0:T(8,128)(2,1)S(1)} %get-tuple-element.88), channel_id=1, source_target_pairs={{0,3},{1,2},{2,1},{3,0},{4,7},{5,6},{6,5},{7,4},{8,11},{9,10},{10,... | collective-permute-start | bytes 688136 | tf_op jit(solution)/shard_map/ppermute | solution.py:39
  71.3 2.7 %collective-permute-start.11 = (bf16[4,4,128,256]{3,2,1,0:T(8,128)(2,1)S(1)}, bf16[4,4,128,256]{3,2,1,0:T(8,128)(2,1)S(1)}, u32[]{:S(2)}, u32[]{:S(2)}) collective-permute-start(bf16[4,4,128,256]{3,2,1,0:T(8,128)(2,1)S(1)} %pad_maximum_fusion.refs_4_), channel_id=1, source_target_pairs={{0,4},{4,0},{8,12},{12,8},{16,20},{20,16},{24,28},{28,24},{1,5},{5... | collective-permute-start | bytes 3145736 | tf_op jit(solution)/shard_map/ppermute | solution.py:39
  74.0 3.8 %collective-permute-start.12 = (bf16[4,4,128,256]{3,2,1,0:T(8,128)(2,1)S(1)}, bf16[4,4,128,256]{3,2,1,0:T(8,128)(2,1)S(1)}, u32[]{:S(2)}, u32[]{:S(2)}) collective-permute-start(bf16[4,4,128,256]{3,2,1,0:T(8,128)(2,1)S(1)} %get-tuple-element.60), channel_id=1, source_target_pairs={{0,4},{4,0},{8,12},{12,8},{16,20},{20,16},{24,28},{28,24},{1,5},{5... | collective-permute-start | bytes 3145736 | tf_op jit(solution)/shard_map/ppermute | solution.py:39
  77.8 9.1 %collective-permute-start.15 = (bf16[336,256]{1,0:T(8,128)(2,1)S(1)}, bf16[336,256]{1,0:T(8,128)(2,1)S(1)}, u32[]{:S(2)}, u32[]{:S(2)}) collective-permute-start(bf16[336,256]{1,0:T(8,128)(2,1)S(1)} %get-tuple-element.82), channel_id=1, source_target_pairs={{0,3},{1,2},{2,1},{3,0},{4,7},{5,6},{6,5},{7,4},{8,11},{9,10},{10,... | collective-permute-start | bytes 516104 | tf_op jit(solution)/shard_map/ppermute | solution.py:39
  79.9 20.9 %collective-permute-start.18 = (bf16[4,128,256]{2,1,0:T(8,128)(2,1)S(1)}, bf16[4,128,256]{2,1,0:T(8,128)(2,1)S(1)}, u32[]{:S(2)}, u32[]{:S(2)}) collective-permute-start(bf16[4,128,256]{2,1,0:T(8,128)(2,1)S(1)} %get-tuple-element.74), channel_id=1, source_target_pairs={{0,24},{4,28},{8,16},{12,20},{16,8},{20,12},{24,0},{28,4},{1,25},{... | collective-permute-start | bytes 786440 | tf_op jit(solution)/shard_map/ppermute | solution.py:39
  80.8 19.9 %collective-permute-start.17 = (bf16[4,128,256]{2,1,0:T(8,128)(2,1)S(1)}, bf16[4,128,256]{2,1,0:T(8,128)(2,1)S(1)}, u32[]{:S(2)}, u32[]{:S(2)}) collective-permute-start(bf16[4,128,256]{2,1,0:T(8,128)(2,1)S(1)} %get-tuple-element.75), channel_id=1, source_target_pairs={{0,16},{4,20},{8,24},{12,28},{16,0},{20,4},{24,8},{28,12},{1,17},{... | collective-permute-start | bytes 786440 | tf_op jit(solution)/shard_map/ppermute | solution.py:39
  82.7 18.0 %collective-permute-start.16 = (bf16[4,128,256]{2,1,0:T(8,128)(2,1)S(1)}, bf16[4,128,256]{2,1,0:T(8,128)(2,1)S(1)}, u32[]{:S(2)}, u32[]{:S(2)}) collective-permute-start(bf16[4,128,256]{2,1,0:T(8,128)(2,1)S(1)} %get-tuple-element.76), channel_id=1, source_target_pairs={{0,8},{4,12},{8,0},{12,4},{16,24},{20,28},{24,16},{28,20},{1,9},{5... | collective-permute-start | bytes 786440 | tf_op jit(solution)/shard_map/ppermute | solution.py:39
  83.4 13.7 %collective-permute-start.14 = (bf16[336,256]{1,0:T(8,128)(2,1)S(1)}, bf16[336,256]{1,0:T(8,128)(2,1)S(1)}, u32[]{:S(2)}, u32[]{:S(2)}) collective-permute-start(bf16[336,256]{1,0:T(8,128)(2,1)S(1)} %get-tuple-element.83), channel_id=1, source_target_pairs={{0,2},{1,3},{2,0},{3,1},{4,6},{5,7},{6,4},{7,5},{8,10},{9,11},{10,... | collective-permute-start | bytes 516104 | tf_op jit(solution)/shard_map/ppermute | solution.py:39
  86.9 13.8 %collective-permute-start.13 = (bf16[336,256]{1,0:T(8,128)(2,1)S(1)}, bf16[336,256]{1,0:T(8,128)(2,1)S(1)}, u32[]{:S(2)}, u32[]{:S(2)}) collective-permute-start(bf16[336,256]{1,0:T(8,128)(2,1)S(1)} %get-tuple-element.84), channel_id=1, source_target_pairs={{0,1},{1,0},{2,3},{3,2},{4,5},{5,4},{6,7},{7,6},{8,9},{9,8},{10,11... | collective-permute-start | bytes 516104 | tf_op jit(solution)/shard_map/ppermute | solution.py:39
  101.0 10.7 %collective-permute-start.20 = (bf16[240,256]{1,0:T(8,128)(2,1)S(1)}, bf16[240,256]{1,0:T(8,128)(2,1)S(1)}, u32[]{:S(2)}, u32[]{:S(2)}) collective-permute-start(bf16[240,256]{1,0:T(8,128)(2,1)S(1)} %pad_maximum_fusion.3), channel_id=1, source_target_pairs={{0,2},{1,3},{2,0},{3,1},{4,6},{5,7},{6,4},{7,5},{8,10},{9,11},{10,... | collective-permute-start | bytes 368648 | tf_op jit(solution)/shard_map/ppermute | solution.py:39
  101.1 10.7 %collective-permute-start.21 = (bf16[240,256]{1,0:T(8,128)(2,1)S(1)}, bf16[240,256]{1,0:T(8,128)(2,1)S(1)}, u32[]{:S(2)}, u32[]{:S(2)}) collective-permute-start(bf16[240,256]{1,0:T(8,128)(2,1)S(1)} %pad_maximum_fusion.4), channel_id=1, source_target_pairs={{0,1},{1,0},{2,3},{3,2},{4,5},{5,4},{6,7},{7,6},{8,9},{9,8},{10,11... | collective-permute-start | bytes 368648 | tf_op jit(solution)/shard_map/ppermute | solution.py:39
  103.2 8.5 %collective-permute-start.19 = (bf16[240,256]{1,0:T(8,128)(2,1)S(1)}, bf16[240,256]{1,0:T(8,128)(2,1)S(1)}, u32[]{:S(2)}, u32[]{:S(2)}) collective-permute-start(bf16[240,256]{1,0:T(8,128)(2,1)S(1)} %pad_maximum_fusion.2), channel_id=1, source_target_pairs={{0,3},{1,2},{2,1},{3,0},{4,7},{5,6},{6,5},{7,4},{8,11},{9,10},{10,... | collective-permute-start | bytes 368648 | tf_op jit(solution)/shard_map/ppermute | solution.py:39

commit v9 on v8

--- a/solution.py
+++ b/solution.py
@@ -44,7 +44,7 @@
 
 
 def masked_grad(grad, pre, slope):
-    return (wide(grad) * jnp.where(wide(pre) > 0, 1.0, slope)).astype(jnp.bfloat16)
+    return jnp.where(pre > 0, grad, (wide(grad) * slope).astype(jnp.bfloat16))
 
 
 def find_places(index, shuffle, blocks, slots, places, used):
@@ -387,37 +387,31 @@
 
 
 def gather_kernel(index, *refs):
-    *parts, out, sems = refs
-    groups = len(parts) // 2
-    sizes = [parts[0].shape[0], out.shape[0] // groups - parts[0].shape[0]]
-    copies = []
-    for i in range(groups):
-        for which, size in enumerate(sizes):
-            start = (index[1] ^ i) * sum(sizes) + which * sizes[0]
-            copies.append(
-                pltpu.make_async_copy(
-                    parts[which * groups + i].at[:size],
-                    out.at[pl.ds(pl.multiple_of(start, 16), size)],
-                    sems.at[which, i],
-                )
-            )
+    *pieces, out, sems = refs
+    rows = pieces[0].shape[0]
+    copies = [
+        pltpu.make_async_copy(
+            piece, out.at[pl.ds(pl.multiple_of((index[1] ^ i) * rows, rows), rows)], sems.at[i]
+        )
+        for i, piece in enumerate(pieces)
+    ]
     for copy in copies:
         copy.start()
     for copy in copies:
         copy.wait()
 
 
-def laid_out(index, heads, tails, rows):
-    groups = len(heads)
+def laid_out(index, pieces):
+    rows, width = pieces[0].shape
     return pl.pallas_call(
         gather_kernel,
-        in_specs=[IN_SMEM] + [IN_VMEM] * (2 * groups),
+        in_specs=[IN_SMEM] + [IN_VMEM] * len(pieces),
         out_specs=IN_HBM,
-        out_shape=bf16(rows, heads[0].shape[1]),
-        scratch_shapes=[pltpu.SemaphoreType.DMA((2, groups))],
+        out_shape=bf16(len(pieces) * rows, width),
+        scratch_shapes=[pltpu.SemaphoreType.DMA((len(pieces),))],
         compiler_params=params(),
         name="laid_out",
-    )(index, *heads, *tails)
+    )(index, *pieces)
 
 
 def landing_blocks(shuffle_from, me, blocks, devs, slots):
@@ -466,7 +460,7 @@
         packed[i] = swapped(packed[i], "chan", i)
 
     outgoing = patch(index, shuffle_from, outgoing, from_prev, from_next, blocks, slots)
-    shuffle_from, outgoing = lax.optimization_barrier((shuffle_from, outgoing))
+    shuffle_from, outgoing, clean = lax.optimization_barrier((shuffle_from, outgoing, clean))
     landing = landing_blocks(shuffle_from, me, blocks, devs, slots)
     incoming = exchanged(outgoing, "node")
     incoming, packed = lax.optimization_barrier((incoming, packed))
@@ -478,9 +472,7 @@
         summed[i] = swapped(merged[i], "chan", i)
     tiles = jnp.stack([piece[quarter:] for piece in packed])
     even = [tiles] + [swapped(tiles, "node", 2 * i) for i in range(1, devs // 2)]
-    early = devs // 2 - 1
-    rest, even[:early] = lax.optimization_barrier((summed[::-1], even[:early]))
-    summed = rest[::-1]
+    summed, even = lax.optimization_barrier((summed, even))
     even = jnp.stack(even)
     odd = swapped(even, "node", 1)
 
@@ -490,27 +482,17 @@
     rows_out = feature_rows(index, summed, even, odd)
     arrived, rows_out = lax.optimization_barrier((arrived, rows_out))
 
-    cut = quarter - quarter // 64 * 16
-    heads = [rows_out[0]] + [None] * (groups - 1)
+    pieces = [rows_out[0]] + [None] * (groups - 1)
     for i in exchange_order(groups):
-        heads[i] = swapped(rows_out[i, :cut], "chan", i)
+        pieces[i] = swapped(rows_out[i], "chan", i)
     total = wide(keep) + wide(arrived)
-    sums = [
-        swapped(total[i].astype(jnp.bfloat16), "node", 2 * i) for i in range(1, devs // 2)
-    ]
-    heads, sums = lax.optimization_barrier((heads, sums))
     share = total[0]
-    for part in sums:
-        share = share + wide(part)
+    for i in range(1, devs // 2):
+        share = share + wide(swapped(total[i].astype(jnp.bfloat16), "node", 2 * i))
     grad_weight = share[0]
-    tails = [rows_out[0, cut:]] + [None] * (groups - 1)
-    for i in exchange_order(groups):
-        tail = jnp.concatenate([rows_out[i, cut:], share[i].astype(jnp.bfloat16)], axis=0)
-        tails[i] = swapped(tail, "chan", i)
-        grad_weight = grad_weight + wide(tails[i][quarter - cut :])
-
-    heads[0] = rows_out[0, :cut]
-    return (grad_weight, laid_out(index, heads, tails, row_count))
+    for i in range(1, groups):
+        grad_weight = grad_weight + wide(swapped(share[i].astype(jnp.bfloat16), "chan", i))
+    return (grad_weight, laid_out(index, pieces))
 
 
 def solution(mesh):

time: 114 us -> 113 us (level)
  transfers between devices with their start and end apart: 23 -> 23, of which waited for: 7 -> 9; matrix products, arithmetic and copies ran while one was open for 1% -> 1% of each run, Pallas kernels for 6% -> 8%
where the time goes in v9:
time: 113 us; the launch traced here: 112 us
  starting transfers between devices  46.4 us (41%)
  waiting for transfers between devices  40.6 us (36%)
  Pallas kernels  19 us (17%)
  local copies, waits for them, and re-layouts  2.83 us (3%)
  other arithmetic  2.56 us (2%)
    ppermute x20, starting transfers between devices, swapped(): return lax.ppermute(value, axis, [(i, i ^ by) for i in range(size)])  35.1 us
    ppermute x20, waiting for transfers between devices, swapped(): return lax.ppermute(value, axis, [(i, i ^ by) for i in range(size)])  33 us
    pallas_call x1, Pallas kernels, aggregate(): pl.pallas_call(functools.partial(aggregate_kernel, reach, groups, send_sl...  9.14 us
    all_to_all x1, starting transfers between devices, exchanged(): return lax.all_to_all(value, axis, split_axis=0, concat_axis=0, tiled=True)  7.62 us
    all_to_all x1, waiting for transfers between devices, exchanged(): return lax.all_to_all(value, axis, split_axis=0, concat_axis=0, tiled=True)  7.5 us
    ppermute x2, starting transfers between devices, shifted(): return lax.ppermute(value, axis, pairs)  3.67 us
    pallas_call x1, Pallas kernels, feature_rows(): pl.pallas_call(feature_kernel, in_specs=[IN_SMEM] + [IN_VMEM] * (groups +...  3.23 us
    pallas_call x1, Pallas kernels, weight_partial(): pl.pallas_call(functools.partial(weight_kernel, devs), in_specs=[IN_SMEM]...  2.61 us
  transfers between devices with their start and end apart: 23, of which 9 were waited for; matrix products, arithmetic and copies ran while one was open for 1% of the time, Pallas kernels for 8%

profile of v9, /device:TPU:0, one launch (start us, length us, event | category | flops | bytes accessed | tf_op | source)
XLA Modules:
  0.0 112.2 jit_solution(11272413360150871460)
XLA Ops:
  0.6 0.6 pad_add_fusion.me.index
  1.3 9.1 %aggregate.1 = (bf16[14,128,256]{2,1,0:T(8,128)(2,1)}, bf16[16,128,256]{2,1,0:T(8,128)(2,1)}, bf16[2,2,128,256]{3,2,1,0:T(8,128)(2,1)}, bf16[2,2,128,256]{3,2,1,...) custom-call(s32[2]{0:T(128)} %pad_add_fusion.me.index, ...), custom_call_target="tpu_custom_call" | custom-call | flops 1174405120 | bytes 7798784 | tf_op jit(solution)/shard_map/aggregate/pallas_call | solution.py:185
  10.4 2.4 %collective-permute-start = (bf16[2,2,128,256]{3,2,1,0:T(8,128)(2,1)}, bf16[2,2,128,256]{3,2,1,0:T(8,128)(2,1)S(1)}, u32[]{:S(2)}, u32[]{:S(2)}) collective-permute-start(bf16[2,2,128,256]{3,2,1,0:T(8,128)(2,1)} %get-tuple-element.33), channel_id=1, source_target_pairs={{0,4},{4,8},{8,12},{12,16},{16,20},{20,24},{24,28},{1,5},{5,9},{9,... | collective-permute-start | bytes 786440 | tf_op jit(solution)/shard_map/ppermute | solution.py:34
  12.8 1.3 %collective-permute-start.1 = (bf16[2,2,128,256]{3,2,1,0:T(8,128)(2,1)}, bf16[2,2,128,256]{3,2,1,0:T(8,128)(2,1)S(1)}, u32[]{:S(2)}, u32[]{:S(2)}) collective-permute-start(bf16[2,2,128,256]{3,2,1,0:T(8,128)(2,1)} %get-tuple-element.34), channel_id=1, source_target_pairs={{4,0},{8,4},{12,8},{16,12},{20,16},{24,20},{28,24},{5,1},{9,5},{13... | collective-permute-start | bytes 786440 | tf_op jit(solution)/shard_map/ppermute | solution.py:34
  14.1 2.5 %collective-permute-start.2 = (bf16[576,256]{1,0:T(8,128)(2,1)}, bf16[576,256]{1,0:T(8,128)(2,1)S(1)}, u32[]{:S(2)}, u32[]{:S(2)}) collective-permute-start(bf16[576,256]{1,0:T(8,128)(2,1)} %get-tuple-element.38), channel_id=1, source_target_pairs={{0,1},{1,0},{2,3},{3,2},{4,5},{5,4},{6,7},{7,6},{8,9},{9,8},{10,11... | collective-permute-start | bytes 884744 | tf_op jit(solution)/shard_map/ppermute | solution.py:39
  16.6 2.6 %collective-permute-start.3 = (bf16[576,256]{1,0:T(8,128)(2,1)}, bf16[576,256]{1,0:T(8,128)(2,1)S(1)}, u32[]{:S(2)}, u32[]{:S(2)}) collective-permute-start(bf16[576,256]{1,0:T(8,128)(2,1)} %get-tuple-element.39), channel_id=1, source_target_pairs={{0,2},{1,3},{2,0},{3,1},{4,6},{5,7},{6,4},{7,5},{8,10},{9,11},{10,... | collective-permute-start | bytes 884744 | tf_op jit(solution)/shard_map/ppermute | solution.py:39
  19.2 0.0 collective-permute-start.4
  19.2 0.0 collective-permute-done.low
  19.2 0.0 collective-permute-done.1.high
  19.2 1.2 %copy-done = bf16[16,128,256]{2,1,0:T(8,128)(2,1)S(1)} copy-done((bf16[16,128,256]{2,1,0:T(8,128)(2,1)S(1)}, bf16[16,128,256]{2,1,0:T(8,128)(2,1)}, u32[]{:S(2)}) %copy-start) | copy-done | bytes 1048600
  20.4 1.5 %patch.1 = bf16[16,128,256]{2,1,0:T(8,128)(2,1)S(1)} custom-call(s32[2]{0:T(128)S(1)} %copy-done.4, s32[112]{0:T(128)S(1)} %copy-done.5, bf16[16,128,256]{2,1,0:T(8,128)(2,1)S(1)} %copy-done, bf16[2,2,128,256]{3,2,1,0:T(8,128)(2,1)S(1)} %collective-permute-done.low, ...), custom_call_target="tpu_custom_call", output_to_operand_aliasing={{}: (2, {})} | custom-call | tf_op jit(solution)/shard_map/patch/pallas_call | solution.py:239
  21.9 1.0 copy-done.1
  22.9 7.6 %all-to-all-start = ((bf16[16,128,256]{2,1,0:T(8,128)(2,1)}), bf16[16,128,256]{2,1,0:T(8,128)(2,1)S(1)}, u32[]{:S(2)}, u32[]{:S(2)}) async-start(bf16[16,128,256]{2,1,0:T(8,128)(2,1)} %copy-done.1), calls=%async_computation | async-start | bytes 2097152 | tf_op jit(solution)/shard_map/all_to_all | solution.py:43
  30.6 0.1 eq.30
  30.7 0.1 add.45
  30.7 0.3 convert_reduce_fusion
  31.1 0.1 copy.14
  31.1 0.1 select_reduce_fusion
  31.3 0.1 copy.15
  31.4 0.1 sub.13.landing
  31.5 0.0 collective-permute-done.2.refs_1_
  31.5 0.0 collective-permute-done.3.refs_2_
  31.5 6.9 %collective-permute-done.4.refs_3_ = bf16[576,256]{1,0:T(8,128)(2,1)S(1)} collective-permute-done((bf16[576,256]{1,0:T(8,128)(2,1)}, bf16[576,256]{1,0:T(8,128)(2,1)S(1)}, u32[]{:S(2)}, u32[]{:S(2)}) %collective-permute-start.4) | collective-permute-done | bytes 294944 | tf_op jit(solution)/shard_map/ppermute | solution.py:39
  38.4 7.5 %all-to-all-done.incoming = bf16[16,128,256]{2,1,0:T(8,128)(2,1)S(1)} async-done(((bf16[16,128,256]{2,1,0:T(8,128)(2,1)}), bf16[16,128,256]{2,1,0:T(8,128)(2,1)S(1)}, u32[]{:S(2)}, u32[]{:S(2)}) %all-to-all-start) | async-done | bytes 1048608 | tf_op jit(solution)/shard_map/all_to_all | solution.py:43
  45.9 1.0 merge.1
  47.0 0.1 slice_bitcast_fusion.4
  47.1 3.7 %collective-permute-start.7 = (bf16[448,256]{1,0:T(8,128)(2,1)S(1)}, bf16[448,256]{1,0:T(8,128)(2,1)S(1)}, u32[]{:S(2)}, u32[]{:S(2)}) collective-permute-start(bf16[448,256]{1,0:T(8,128)(2,1)S(1)} %get-tuple-element.73), channel_id=1, source_target_pairs={{0,3},{1,2},{2,1},{3,0},{4,7},{5,6},{6,5},{7,4},{8,11},{9,10},{10,... | collective-permute-start | bytes 688136 | tf_op jit(solution)/shard_map/ppermute | solution.py:39
  50.8 0.7 collective-permute-start.10
  51.5 1.4 %collective-permute-start.9 = (bf16[4,128,256]{2,1,0:T(8,128)(2,1)S(1)}, bf16[4,128,256]{2,1,0:T(8,128)(2,1)S(1)}, u32[]{:S(2)}, u32[]{:S(2)}) collective-permute-start(bf16[4,128,256]{2,1,0:T(8,128)(2,1)S(1)} %pad_maximum_fusion.1), channel_id=1, source_target_pairs={{0,16},{4,20},{8,24},{12,28},{16,0},{20,4},{24,8},{28,12},{1,17},{... | collective-permute-start | bytes 786440 | tf_op jit(solution)/shard_map/ppermute | solution.py:39
  52.9 1.5 %collective-permute-start.8 = (bf16[4,128,256]{2,1,0:T(8,128)(2,1)S(1)}, bf16[4,128,256]{2,1,0:T(8,128)(2,1)S(1)}, u32[]{:S(2)}, u32[]{:S(2)}) collective-permute-start(bf16[4,128,256]{2,1,0:T(8,128)(2,1)S(1)} %pad_maximum_fusion.1), channel_id=1, source_target_pairs={{0,8},{4,12},{8,0},{12,4},{16,24},{20,28},{24,16},{28,20},{1,9},{5... | collective-permute-start | bytes 786440 | tf_op jit(solution)/shard_map/ppermute | solution.py:39
  54.4 0.0 collective-permute-start.6
  54.4 1.7 %collective-permute-done.7.refs_7_.refs_3_ = bf16[448,256]{1,0:T(8,128)(2,1)S(1)} collective-permute-done((bf16[448,256]{1,0:T(8,128)(2,1)S(1)}, bf16[448,256]{1,0:T(8,128)(2,1)S(1)}, u32[]{:S(2)}, u32[]{:S(2)}) %collective-permute-start.7) | collective-permute-done | bytes 229408 | tf_op jit(solution)/shard_map/ppermute | solution.py:39
  56.1 8.2 %collective-permute-start.5 = (bf16[448,256]{1,0:T(8,128)(2,1)S(1)}, bf16[448,256]{1,0:T(8,128)(2,1)S(1)}, u32[]{:S(2)}, u32[]{:S(2)}) collective-permute-start(bf16[448,256]{1,0:T(8,128)(2,1)S(1)} %get-tuple-element.75), channel_id=1, source_target_pairs={{0,1},{1,0},{2,3},{3,2},{4,5},{5,4},{6,7},{7,6},{8,9},{9,8},{10,11... | collective-permute-start | bytes 688136 | tf_op jit(solution)/shard_map/ppermute | solution.py:39
  64.3 4.1 %collective-permute-done.6.refs_6_.refs_2_ = bf16[448,256]{1,0:T(8,128)(2,1)S(1)} collective-permute-done((bf16[448,256]{1,0:T(8,128)(2,1)S(1)}, bf16[448,256]{1,0:T(8,128)(2,1)S(1)}, u32[]{:S(2)}, u32[]{:S(2)}) %collective-permute-start.6) | collective-permute-done | bytes 229408 | tf_op jit(solution)/shard_map/ppermute | solution.py:39
  68.4 4.8 %collective-permute-done.5.refs_5_.refs_1_ = bf16[448,256]{1,0:T(8,128)(2,1)S(1)} collective-permute-done((bf16[448,256]{1,0:T(8,128)(2,1)S(1)}, bf16[448,256]{1,0:T(8,128)(2,1)S(1)}, u32[]{:S(2)}, u32[]{:S(2)}) %collective-permute-start.5) | collective-permute-done | bytes 229408 | tf_op jit(solution)/shard_map/ppermute | solution.py:39
  73.2 0.0 collective-permute-done.10
  73.2 0.0 collective-permute-done.9
  73.2 0.0 collective-permute-done.8
  73.2 0.1 pad_maximum_fusion.refs_4_
  73.4 0.1 collective-permute-start.11
  73.5 2.6 %weight_partial.1 = (bf16[4,4,128,256]{3,2,1,0:T(8,128)(2,1)S(1)}, bf16[4,4,128,256]{3,2,1,0:T(8,128)(2,1)S(1)}) custom-call(s32[2]{0:T(128)S(1)} %copy-done.4, bf16[576,256]{1,0:T(8,128)(2,1)S(1)} %copy-done.3, bf16[576,256]{1,0:T(8,128)(2,1)S(1)} %collective-permute-done.2.refs_1_, bf16[576,256]{1,0:T(8,128)(2,1)S(1)} %collective-permute-done.3.refs_2_, ...), custom_call_target="tpu_custom_call" | custom-call | flops 939524096 | bytes 3932160 | tf_op jit(solution)/shard_map/weight_partial/pallas_call | solution.py:326
  76.1 0.0 collective-permute-done.11.refs_5_
  76.1 0.5 collective-permute-start.12
  76.6 3.2 %feature_rows.1 = bf16[4,448,256]{2,1,0:T(8,128)(2,1)S(1)} custom-call(s32[2]{0:T(128)S(1)} %copy-done.4, bf16[448,256]{1,0:T(8,128)(2,1)S(1)} %get-tuple-element.48.refs_4_.refs_0_, bf16[448,256]{1,0:T(8,128)(2,1)S(1)} %collective-permute-done.5.refs_5_.refs_1_, bf16[448,256]{1,0:T(8,128)(2,1)S(1)} %collective-permute-done.6.refs_6_.refs_2_, ...), custom_call_target="tpu_custom_call" | custom-call | flops 939524096 | bytes 3932160 | tf_op jit(solution)/shard_map/feature_rows/pallas_call | solution.py:374
  79.9 0.0 collective-permute-done.12
  79.9 0.4 convert_add_fusion
  80.3 0.1 slice_bitcast_fusion.3
  80.3 3.1 %collective-permute-start.13 = (bf16[4,128,256]{2,1,0:T(8,128)(2,1)S(1)}, bf16[4,128,256]{2,1,0:T(8,128)(2,1)S(1)}, u32[]{:S(2)}, u32[]{:S(2)}) collective-permute-start(bf16[4,128,256]{2,1,0:T(8,128)(2,1)S(1)} %get-tuple-element.66), channel_id=1, source_target_pairs={{0,8},{4,12},{8,0},{12,4},{16,24},{20,28},{24,16},{28,20},{1,9},{5... | collective-permute-start | bytes 786440 | tf_op jit(solution)/shard_map/ppermute | solution.py:39
  83.4 0.0 collective-permute-start.15
  83.4 1.5 %collective-permute-start.14 = (bf16[4,128,256]{2,1,0:T(8,128)(2,1)S(1)}, bf16[4,128,256]{2,1,0:T(8,128)(2,1)S(1)}, u32[]{:S(2)}, u32[]{:S(2)}) collective-permute-start(bf16[4,128,256]{2,1,0:T(8,128)(2,1)S(1)} %get-tuple-element.68), channel_id=1, source_target_pairs={{0,16},{4,20},{8,24},{12,28},{16,0},{20,4},{24,8},{28,12},{1,17},{... | collective-permute-start | bytes 786440 | tf_op jit(solution)/shard_map/ppermute | solution.py:39
  84.9 0.1 slice_bitcast_fusion.8
  85.0 2.5 %collective-permute-start.21 = (bf16[448,256]{1,0:T(8,128)(2,1)S(1)}, bf16[448,256]{1,0:T(8,128)(2,1)S(1)}, u32[]{:S(2)}, u32[]{:S(2)}) collective-permute-start(bf16[448,256]{1,0:T(8,128)(2,1)S(1)} %get-tuple-element.69), channel_id=1, source_target_pairs={{0,3},{1,2},{2,1},{3,0},{4,7},{5,6},{6,5},{7,4},{8,11},{9,10},{10,... | collective-permute-start | bytes 688136 | tf_op jit(solution)/shard_map/ppermute | solution.py:39
  87.5 3.0 %collective-permute-done.13 = bf16[4,128,256]{2,1,0:T(8,128)(2,1)S(1)} collective-permute-done((bf16[4,128,256]{2,1,0:T(8,128)(2,1)S(1)}, bf16[4,128,256]{2,1,0:T(8,128)(2,1)S(1)}, u32[]{:S(2)}, u32[]{:S(2)}) %collective-permute-start.13) | collective-permute-done | bytes 262176 | tf_op jit(solution)/shard_map/ppermute | solution.py:39
  90.5 4.5 %collective-permute-done.15 = bf16[4,128,256]{2,1,0:T(8,128)(2,1)S(1)} collective-permute-done((bf16[4,128,256]{2,1,0:T(8,128)(2,1)S(1)}, bf16[4,128,256]{2,1,0:T(8,128)(2,1)S(1)}, u32[]{:S(2)}, u32[]{:S(2)}) %collective-permute-start.15) | collective-permute-done | bytes 262176 | tf_op jit(solution)/shard_map/ppermute | solution.py:39
  95.0 2.0 %collective-permute-done.14 = bf16[4,128,256]{2,1,0:T(8,128)(2,1)S(1)} collective-permute-done((bf16[4,128,256]{2,1,0:T(8,128)(2,1)S(1)}, bf16[4,128,256]{2,1,0:T(8,128)(2,1)S(1)}, u32[]{:S(2)}, u32[]{:S(2)}) %collective-permute-start.14) | collective-permute-done | bytes 262176 | tf_op jit(solution)/shard_map/ppermute | solution.py:39
  97.0 0.2 fusion.10
  97.2 0.1 collective-permute-start.16
  97.2 3.0 %collective-permute-start.18 = (bf16[128,256]{1,0:T(8,128)(2,1)S(1)}, bf16[128,256]{1,0:T(8,128)(2,1)S(1)}, u32[]{:S(2)}, u32[]{:S(2)}) collective-permute-start(bf16[128,256]{1,0:T(8,128)(2,1)S(1)} %get-tuple-element.78), channel_id=1, source_target_pairs={{0,3},{1,2},{2,1},{3,0},{4,7},{5,6},{6,5},{7,4},{8,11},{9,10},{10,... | collective-permute-start | bytes 196616 | tf_op jit(solution)/shard_map/ppermute | solution.py:39
  100.2 3.7 %collective-permute-start.17 = (bf16[128,256]{1,0:T(8,128)(2,1)S(1)}, bf16[128,256]{1,0:T(8,128)(2,1)S(1)}, u32[]{:S(2)}, u32[]{:S(2)}) collective-permute-start(bf16[128,256]{1,0:T(8,128)(2,1)S(1)} %get-tuple-element.79), channel_id=1, source_target_pairs={{0,2},{1,3},{2,0},{3,1},{4,6},{5,7},{6,4},{7,5},{8,10},{9,11},{10,... | collective-permute-start | bytes 196616 | tf_op jit(solution)/shard_map/ppermute | solution.py:39
  104.0 6.0 %collective-permute-done.20.refs_2_ = bf16[448,256]{1,0:T(8,128)(2,1)S(1)} collective-permute-done((bf16[448,256]{1,0:T(8,128)(2,1)S(1)}, bf16[448,256]{1,0:T(8,128)(2,1)S(1)}, u32[]{:S(2)}, u32[]{:S(2)}) %collective-permute-start.20) | collective-permute-done | bytes 229408 | tf_op jit(solution)/shard_map/ppermute | solution.py:39
  110.0 1.5 %laid_out.1 = bf16[1792,256]{1,0:T(8,128)(2,1)} custom-call(s32[2]{0:T(128)S(1)} %copy-done.4, bf16[448,256]{1,0:T(8,128)(2,1)S(1)} %get-tuple-element.72.refs_0_, bf16[448,256]{1,0:T(8,128)(2,1)S(1)} %collective-permute-done.19.refs_1_, bf16[448,256]{1,0:T(8,128)(2,1)S(1)} %collective-permute-done.20.refs_2_, ...), custom_call_target="tpu_custom_call" | custom-call | tf_op jit(solution)/shard_map/laid_out/pallas_call | solution.py:406
  111.5 0.0 collective-permute-done.18
  111.5 0.0 collective-permute-done.17
  111.5 0.7 fusion.5
  (23 shorter events, 0.2 us)
Async XLA Ops:
  1.3 17.9 %copy-start.4 = (s32[2]{0:T(128)S(1)}, s32[2]{0:T(128)}, u32[]{:S(2)}) copy-start(s32[2]{0:T(128)} %pad_add_fusion.me.index) | copy-start | bytes 28
  1.3 17.9 %copy-start.5 = (s32[112]{0:T(128)S(1)}, s32[112]{0:T(128)}, u32[]{:S(2)}) copy-start(s32[112]{0:T(128)} %shuffle.3) | copy-start | bytes 1348
  10.4 8.8 %collective-permute-start = (bf16[2,2,128,256]{3,2,1,0:T(8,128)(2,1)}, bf16[2,2,128,256]{3,2,1,0:T(8,128)(2,1)S(1)}, u32[]{:S(2)}, u32[]{:S(2)}) collective-permute-start(bf16[2,2,128,256]{3,2,1,0:T(8,128)(2,1)} %get-tuple-element.33), channel_id=1, source_target_pairs={{0,4},{4,8},{8,12},{12,16},{16,20},{20,24},{24,28},{1,5},{5,9},{9,... | collective-permute-start | bytes 786440 | tf_op jit(solution)/shard_map/ppermute | solution.py:34
  12.8 6.4 %collective-permute-start.1 = (bf16[2,2,128,256]{3,2,1,0:T(8,128)(2,1)}, bf16[2,2,128,256]{3,2,1,0:T(8,128)(2,1)S(1)}, u32[]{:S(2)}, u32[]{:S(2)}) collective-permute-start(bf16[2,2,128,256]{3,2,1,0:T(8,128)(2,1)} %get-tuple-element.34), channel_id=1, source_target_pairs={{4,0},{8,4},{12,8},{16,12},{20,16},{24,20},{28,24},{5,1},{9,5},{13... | collective-permute-start | bytes 786440 | tf_op jit(solution)/shard_map/ppermute | solution.py:34
  14.1 17.3 %collective-permute-start.2 = (bf16[576,256]{1,0:T(8,128)(2,1)}, bf16[576,256]{1,0:T(8,128)(2,1)S(1)}, u32[]{:S(2)}, u32[]{:S(2)}) collective-permute-start(bf16[576,256]{1,0:T(8,128)(2,1)} %get-tuple-element.38), channel_id=1, source_target_pairs={{0,1},{1,0},{2,3},{3,2},{4,5},{5,4},{6,7},{7,6},{8,9},{9,8},{10,11... | collective-permute-start | bytes 884744 | tf_op jit(solution)/shard_map/ppermute | solution.py:39
  16.6 14.9 %collective-permute-start.3 = (bf16[576,256]{1,0:T(8,128)(2,1)}, bf16[576,256]{1,0:T(8,128)(2,1)S(1)}, u32[]{:S(2)}, u32[]{:S(2)}) collective-permute-start(bf16[576,256]{1,0:T(8,128)(2,1)} %get-tuple-element.39), channel_id=1, source_target_pairs={{0,2},{1,3},{2,0},{3,1},{4,6},{5,7},{6,4},{7,5},{8,10},{9,11},{10,... | collective-permute-start | bytes 884744 | tf_op jit(solution)/shard_map/ppermute | solution.py:39
  19.2 19.2 %collective-permute-start.4 = (bf16[576,256]{1,0:T(8,128)(2,1)}, bf16[576,256]{1,0:T(8,128)(2,1)S(1)}, u32[]{:S(2)}, u32[]{:S(2)}) collective-permute-start(bf16[576,256]{1,0:T(8,128)(2,1)} %get-tuple-element.40), channel_id=1, source_target_pairs={{0,3},{1,2},{2,1},{3,0},{4,7},{5,6},{6,5},{7,4},{8,11},{9,10},{10,... | collective-permute-start | bytes 884744 | tf_op jit(solution)/shard_map/ppermute | solution.py:39
  19.2 1.2 %copy-start = (bf16[16,128,256]{2,1,0:T(8,128)(2,1)S(1)}, bf16[16,128,256]{2,1,0:T(8,128)(2,1)}, u32[]{:S(2)}) copy-start(bf16[16,128,256]{2,1,0:T(8,128)(2,1)} %get-tuple-element.32.outgoing) | copy-start | bytes 3145732
  20.4 25.5 %copy-start.2 = (bf16[14,128,256]{2,1,0:T(8,128)(2,1)S(1)}, bf16[14,128,256]{2,1,0:T(8,128)(2,1)}, u32[]{:S(2)}) copy-start(bf16[14,128,256]{2,1,0:T(8,128)(2,1)} %get-tuple-element.46.clean) | copy-start | bytes 2752516
  21.9 1.0 copy-start.1
  22.9 23.0 %all-to-all-start = ((bf16[16,128,256]{2,1,0:T(8,128)(2,1)}), bf16[16,128,256]{2,1,0:T(8,128)(2,1)S(1)}, u32[]{:S(2)}, u32[]{:S(2)}) async-start(bf16[16,128,256]{2,1,0:T(8,128)(2,1)} %copy-done.1), calls=%async_computation | async-start | bytes 2097152 | tf_op jit(solution)/shard_map/all_to_all | solution.py:43
  45.9 4.8 %copy-start.3 = (bf16[576,256]{1,0:T(8,128)(2,1)S(1)}, bf16[576,256]{1,0:T(8,128)(2,1)}, u32[]{:S(2)}) copy-start(bf16[576,256]{1,0:T(8,128)(2,1)} %get-tuple-element.41.refs_0_) | copy-start | bytes 884740
  47.1 9.0 %collective-permute-start.7 = (bf16[448,256]{1,0:T(8,128)(2,1)S(1)}, bf16[448,256]{1,0:T(8,128)(2,1)S(1)}, u32[]{:S(2)}, u32[]{:S(2)}) collective-permute-start(bf16[448,256]{1,0:T(8,128)(2,1)S(1)} %get-tuple-element.73), channel_id=1, source_target_pairs={{0,3},{1,2},{2,1},{3,0},{4,7},{5,6},{6,5},{7,4},{8,11},{9,10},{10,... | collective-permute-start | bytes 688136 | tf_op jit(solution)/shard_map/ppermute | solution.py:39
  50.8 22.4 %collective-permute-start.10 = (bf16[4,128,256]{2,1,0:T(8,128)(2,1)S(1)}, bf16[4,128,256]{2,1,0:T(8,128)(2,1)S(1)}, u32[]{:S(2)}, u32[]{:S(2)}) collective-permute-start(bf16[4,128,256]{2,1,0:T(8,128)(2,1)S(1)} %pad_maximum_fusion.1), channel_id=1, source_target_pairs={{0,24},{4,28},{8,16},{12,20},{16,8},{20,12},{24,0},{28,4},{1,25},{... | collective-permute-start | bytes 786440 | tf_op jit(solution)/shard_map/ppermute | solution.py:39
  51.5 21.7 %collective-permute-start.9 = (bf16[4,128,256]{2,1,0:T(8,128)(2,1)S(1)}, bf16[4,128,256]{2,1,0:T(8,128)(2,1)S(1)}, u32[]{:S(2)}, u32[]{:S(2)}) collective-permute-start(bf16[4,128,256]{2,1,0:T(8,128)(2,1)S(1)} %pad_maximum_fusion.1), channel_id=1, source_target_pairs={{0,16},{4,20},{8,24},{12,28},{16,0},{20,4},{24,8},{28,12},{1,17},{... | collective-permute-start | bytes 786440 | tf_op jit(solution)/shard_map/ppermute | solution.py:39
  52.9 20.4 %collective-permute-start.8 = (bf16[4,128,256]{2,1,0:T(8,128)(2,1)S(1)}, bf16[4,128,256]{2,1,0:T(8,128)(2,1)S(1)}, u32[]{:S(2)}, u32[]{:S(2)}) collective-permute-start(bf16[4,128,256]{2,1,0:T(8,128)(2,1)S(1)} %pad_maximum_fusion.1), channel_id=1, source_target_pairs={{0,8},{4,12},{8,0},{12,4},{16,24},{20,28},{24,16},{28,20},{1,9},{5... | collective-permute-start | bytes 786440 | tf_op jit(solution)/shard_map/ppermute | solution.py:39
  54.4 14.0 %collective-permute-start.6 = (bf16[448,256]{1,0:T(8,128)(2,1)S(1)}, bf16[448,256]{1,0:T(8,128)(2,1)S(1)}, u32[]{:S(2)}, u32[]{:S(2)}) collective-permute-start(bf16[448,256]{1,0:T(8,128)(2,1)S(1)} %get-tuple-element.74), channel_id=1, source_target_pairs={{0,2},{1,3},{2,0},{3,1},{4,6},{5,7},{6,4},{7,5},{8,10},{9,11},{10,... | collective-permute-start | bytes 688136 | tf_op jit(solution)/shard_map/ppermute | solution.py:39
  56.1 17.2 %collective-permute-start.5 = (bf16[448,256]{1,0:T(8,128)(2,1)S(1)}, bf16[448,256]{1,0:T(8,128)(2,1)S(1)}, u32[]{:S(2)}, u32[]{:S(2)}) collective-permute-start(bf16[448,256]{1,0:T(8,128)(2,1)S(1)} %get-tuple-element.75), channel_id=1, source_target_pairs={{0,1},{1,0},{2,3},{3,2},{4,5},{5,4},{6,7},{7,6},{8,9},{9,8},{10,11... | collective-permute-start | bytes 688136 | tf_op jit(solution)/shard_map/ppermute | solution.py:39
  73.4 2.7 %collective-permute-start.11 = (bf16[4,4,128,256]{3,2,1,0:T(8,128)(2,1)S(1)}, bf16[4,4,128,256]{3,2,1,0:T(8,128)(2,1)S(1)}, u32[]{:S(2)}, u32[]{:S(2)}) collective-permute-start(bf16[4,4,128,256]{3,2,1,0:T(8,128)(2,1)S(1)} %pad_maximum_fusion.refs_4_), channel_id=1, source_target_pairs={{0,4},{4,0},{8,12},{12,8},{16,20},{20,16},{24,28},{28,24},{1,5},{5... | collective-permute-start | bytes 3145736 | tf_op jit(solution)/shard_map/ppermute | solution.py:39
  76.1 3.8 %collective-permute-start.12 = (bf16[4,4,128,256]{3,2,1,0:T(8,128)(2,1)S(1)}, bf16[4,4,128,256]{3,2,1,0:T(8,128)(2,1)S(1)}, u32[]{:S(2)}, u32[]{:S(2)}) collective-permute-start(bf16[4,4,128,256]{3,2,1,0:T(8,128)(2,1)S(1)} %get-tuple-element.58), channel_id=1, source_target_pairs={{0,4},{4,0},{8,12},{12,8},{16,20},{20,16},{24,28},{28,24},{1,5},{5... | collective-permute-start | bytes 3145736 | tf_op jit(solution)/shard_map/ppermute | solution.py:39
  80.3 10.2 %collective-permute-start.13 = (bf16[4,128,256]{2,1,0:T(8,128)(2,1)S(1)}, bf16[4,128,256]{2,1,0:T(8,128)(2,1)S(1)}, u32[]{:S(2)}, u32[]{:S(2)}) collective-permute-start(bf16[4,128,256]{2,1,0:T(8,128)(2,1)S(1)} %get-tuple-element.66), channel_id=1, source_target_pairs={{0,8},{4,12},{8,0},{12,4},{16,24},{20,28},{24,16},{28,20},{1,9},{5... | collective-permute-start | bytes 786440 | tf_op jit(solution)/shard_map/ppermute | solution.py:39
  83.4 11.6 %collective-permute-start.15 = (bf16[4,128,256]{2,1,0:T(8,128)(2,1)S(1)}, bf16[4,128,256]{2,1,0:T(8,128)(2,1)S(1)}, u32[]{:S(2)}, u32[]{:S(2)}) collective-permute-start(bf16[4,128,256]{2,1,0:T(8,128)(2,1)S(1)} %get-tuple-element.67), channel_id=1, source_target_pairs={{0,24},{4,28},{8,16},{12,20},{16,8},{20,12},{24,0},{28,4},{1,25},{... | collective-permute-start | bytes 786440 | tf_op jit(solution)/shard_map/ppermute | solution.py:39
  83.4 13.6 %collective-permute-start.14 = (bf16[4,128,256]{2,1,0:T(8,128)(2,1)S(1)}, bf16[4,128,256]{2,1,0:T(8,128)(2,1)S(1)}, u32[]{:S(2)}, u32[]{:S(2)}) collective-permute-start(bf16[4,128,256]{2,1,0:T(8,128)(2,1)S(1)} %get-tuple-element.68), channel_id=1, source_target_pairs={{0,16},{4,20},{8,24},{12,28},{16,0},{20,4},{24,8},{28,12},{1,17},{... | collective-permute-start | bytes 786440 | tf_op jit(solution)/shard_map/ppermute | solution.py:39
  85.0 15.2 %collective-permute-start.21 = (bf16[448,256]{1,0:T(8,128)(2,1)S(1)}, bf16[448,256]{1,0:T(8,128)(2,1)S(1)}, u32[]{:S(2)}, u32[]{:S(2)}) collective-permute-start(bf16[448,256]{1,0:T(8,128)(2,1)S(1)} %get-tuple-element.69), channel_id=1, source_target_pairs={{0,3},{1,2},{2,1},{3,0},{4,7},{5,6},{6,5},{7,4},{8,11},{9,10},{10,... | collective-permute-start | bytes 688136 | tf_op jit(solution)/shard_map/ppermute | solution.py:39
  87.5 22.5 %collective-permute-start.20 = (bf16[448,256]{1,0:T(8,128)(2,1)S(1)}, bf16[448,256]{1,0:T(8,128)(2,1)S(1)}, u32[]{:S(2)}, u32[]{:S(2)}) collective-permute-start(bf16[448,256]{1,0:T(8,128)(2,1)S(1)} %get-tuple-element.70), channel_id=1, source_target_pairs={{0,2},{1,3},{2,0},{3,1},{4,6},{5,7},{6,4},{7,5},{8,10},{9,11},{10,... | collective-permute-start | bytes 688136 | tf_op jit(solution)/shard_map/ppermute | solution.py:39
  90.5 19.5 %collective-permute-start.19 = (bf16[448,256]{1,0:T(8,128)(2,1)S(1)}, bf16[448,256]{1,0:T(8,128)(2,1)S(1)}, u32[]{:S(2)}, u32[]{:S(2)}) collective-permute-start(bf16[448,256]{1,0:T(8,128)(2,1)S(1)} %get-tuple-element.71), channel_id=1, source_target_pairs={{0,1},{1,0},{2,3},{3,2},{4,5},{5,4},{6,7},{7,6},{8,9},{9,8},{10,11... | collective-permute-start | bytes 688136 | tf_op jit(solution)/shard_map/ppermute | solution.py:39
  97.2 14.3 %collective-permute-start.16 = (bf16[128,256]{1,0:T(8,128)(2,1)S(1)}, bf16[128,256]{1,0:T(8,128)(2,1)S(1)}, u32[]{:S(2)}, u32[]{:S(2)}) collective-permute-start(bf16[128,256]{1,0:T(8,128)(2,1)S(1)} %get-tuple-element.77), channel_id=1, source_target_pairs={{0,1},{1,0},{2,3},{3,2},{4,5},{5,4},{6,7},{7,6},{8,9},{9,8},{10,11... | collective-permute-start | bytes 196616 | tf_op jit(solution)/shard_map/ppermute | solution.py:39
  97.2 14.3 %collective-permute-start.18 = (bf16[128,256]{1,0:T(8,128)(2,1)S(1)}, bf16[128,256]{1,0:T(8,128)(2,1)S(1)}, u32[]{:S(2)}, u32[]{:S(2)}) collective-permute-start(bf16[128,256]{1,0:T(8,128)(2,1)S(1)} %get-tuple-element.78), channel_id=1, source_target_pairs={{0,3},{1,2},{2,1},{3,0},{4,7},{5,6},{6,5},{7,4},{8,11},{9,10},{10,... | collective-permute-start | bytes 196616 | tf_op jit(solution)/shard_map/ppermute | solution.py:39
  100.2 11.3 %collective-permute-start.17 = (bf16[128,256]{1,0:T(8,128)(2,1)S(1)}, bf16[128,256]{1,0:T(8,128)(2,1)S(1)}, u32[]{:S(2)}, u32[]{:S(2)}) collective-permute-start(bf16[128,256]{1,0:T(8,128)(2,1)S(1)} %get-tuple-element.79), channel_id=1, source_target_pairs={{0,2},{1,3},{2,0},{3,1},{4,6},{5,7},{6,4},{7,5},{8,10},{9,11},{10,... | collective-permute-start | bytes 196616 | tf_op jit(solution)/shard_map/ppermute | solution.py:39

commit v10 on v9

--- a/solution.py
+++ b/solution.py
@@ -60,8 +60,8 @@
 def aggregate_kernel(
     reach, groups, send_slots, me, shuffle, cols, count, gc, pc, gx, px, slopes, adj, features, weight, *refs
 ):
-    clean, outgoing, down, up, *refs = refs
-    packed, refs = refs[:groups], refs[groups:]
+    clean, outgoing, *refs = refs
+    sides, packed, refs = refs[:4], refs[4 : 4 + groups], refs[4 + groups :]
     data, tiles, rhs, stage, results, halos, packs, places, used, sems, pack_sems, out_sems = refs
     blocks, slots, rows, _ = adj.shape
     width = gc.shape[1]
@@ -152,10 +152,9 @@
         else:
             side, at = int(block >= 0), first % (blocks + reach)
             halos[side, 0, at : at + 2], halos[side, 1, at : at + 2] = pair(first)
-            out = (down, up)[side]
             done = []
             for i in range(2):
-                source, target = halos.at[side, i, at : at + 2], out.at[i, at : at + 2]
+                source, target = halos.at[side, i, at : at + 2], sides[2 * i + side].at[at : at + 2]
                 done.append(pltpu.make_async_copy(source, target, out_sems.at[2 + i, first]))
         for copy in done:
             copy.start()
@@ -164,13 +163,14 @@
     for step in range(blocks // 2):
         for copy in inputs[step]:
             copy.wait()
+        if step:
+            finish(2 * step - 2)
         take(step)
-        finish(2 * step)
     for copy in to_vmem:
         copy.wait()
     for copy in to_hbm:
         copy.start()
-    for first in range(blocks, blocks + 2 * reach, 2):
+    for first in range(blocks + 2 * reach - 2, blocks - 4, -2):
         finish(first)
     for copy in writes + to_hbm:
         copy.wait()
@@ -185,9 +185,9 @@
     return pl.pallas_call(
         functools.partial(aggregate_kernel, reach, groups, send_slots),
         in_specs=[IN_SMEM] * 4 + [IN_HBM] * 4 + [IN_VMEM] + [IN_HBM] * 3,
-        out_specs=[IN_HBM] * (4 + groups),
+        out_specs=[IN_HBM] * (6 + groups),
         out_shape=[bf16(blocks, rows, width), bf16(devs * send_slots, rows, width)]
-        + [bf16(2, reach, rows, width)] * 2
+        + [bf16(reach, rows, width)] * 4
         + [bf16(packed, width)] * groups,
         scratch_shapes=[
             pltpu.VMEM((4, blocks // 2, 2 * rows, width), jnp.bfloat16),
@@ -225,7 +225,7 @@
         copy.start()
     for i, (read, write) in enumerate(zip(reads, writes)):
         read.wait()
-        other = low[1, i] if i < reach else high[1, i - reach]
+        other = low[i] if i < reach else high[i - reach]
         ready[i] = (wide(held[i]) + wide(other)).astype(jnp.bfloat16)
         write.start()
     for copy in writes:
@@ -234,7 +234,7 @@
 
 def patch(index, shuffle, outgoing, low, high, blocks, slots):
     sent, rows, width = outgoing.shape
-    reach = low.shape[1]
+    reach = low.shape[0]
     border = pltpu.VMEM((2 * reach, rows, width), jnp.bfloat16)
     return pl.pallas_call(
         functools.partial(patch_kernel, reach, blocks, slots),
@@ -256,14 +256,14 @@
 
 def merge_kernel(quarter, index, landing, clean, low, high, incoming, out, whole):
     blocks, rows, _ = clean.shape
-    reach = low.shape[1]
+    reach = low.shape[0]
     group = index[1]
     piece = math.gcd(rows, quarter)
     for block in range(blocks):
         whole[block] = wide(clean[block])
     for i in range(reach):
-        whole[i] += wide(low[0, i])
-        whole[blocks - reach + i] += wide(high[0, i])
+        whole[i] += wide(low[i])
+        whole[blocks - reach + i] += wide(high[i])
     for place in range(incoming.shape[0]):
         block = landing[place]
 
@@ -386,8 +386,10 @@
     )(index, *summed, even, odd)
 
 
-def gather_kernel(index, *refs):
-    *pieces, out, sems = refs
+def finish_kernel(index, share, *refs):
+    *refs, out, total, sems = refs
+    groups = (len(refs) + 1) // 2
+    pieces, others = refs[:groups], refs[groups:]
     rows = pieces[0].shape[0]
     copies = [
         pltpu.make_async_copy(
@@ -397,21 +399,28 @@
     ]
     for copy in copies:
         copy.start()
+    sum_of = share[...]
+    for other in others:
+        sum_of = sum_of + wide(other[...])
+    total[...] = sum_of
     for copy in copies:
         copy.wait()
 
 
-def laid_out(index, pieces):
+def finish(index, pieces, share, others):
     rows, width = pieces[0].shape
     return pl.pallas_call(
-        gather_kernel,
-        in_specs=[IN_SMEM] + [IN_VMEM] * len(pieces),
-        out_specs=IN_HBM,
-        out_shape=bf16(len(pieces) * rows, width),
+        finish_kernel,
+        in_specs=[IN_SMEM] + [IN_VMEM] * (2 * len(pieces)),
+        out_specs=[IN_HBM, IN_VMEM],
+        out_shape=[
+            bf16(len(pieces) * rows, width),
+            jax.ShapeDtypeStruct(share.shape, jnp.float32),
+        ],
         scratch_shapes=[pltpu.SemaphoreType.DMA((len(pieces),))],
         compiler_params=params(),
-        name="laid_out",
-    )(index, *pieces)
+        name="finish",
+    )(index, share, *pieces, *others)
 
 
 def landing_blocks(shuffle_from, me, blocks, devs, slots):
@@ -453,26 +462,31 @@
 
     args = (index, shuffle_from, adj_cols.T, adj_count)
     args += (grad_clean, pre_clean, grad_corrupt, pre_corrupt, slopes[None, :], adj_vals)
-    clean, outgoing, down, up, *packed = aggregate(*args, features, weight, reach, devs, groups)
-    from_prev = shifted(up, "node", 1)
-    from_next = shifted(down, "node", -1)
+    clean, outgoing, *sides = aggregate(*args, features, weight, reach, devs, groups)
+    sides, packed = sides[:4], sides[4:]
+    low, high = shifted(sides[3], "node", 1), shifted(sides[2], "node", -1)
     for i in exchange_order(groups):
         packed[i] = swapped(packed[i], "chan", i)
 
-    outgoing = patch(index, shuffle_from, outgoing, from_prev, from_next, blocks, slots)
-    shuffle_from, outgoing, clean = lax.optimization_barrier((shuffle_from, outgoing, clean))
+    outgoing = patch(index, shuffle_from, outgoing, low, high, blocks, slots)
+    shuffle_from, outgoing, clean, sides = lax.optimization_barrier(
+        (shuffle_from, outgoing, clean, sides)
+    )
+    low, high = shifted(sides[1], "node", 1), shifted(sides[0], "node", -1)
     landing = landing_blocks(shuffle_from, me, blocks, devs, slots)
     incoming = exchanged(outgoing, "node")
     incoming, packed = lax.optimization_barrier((incoming, packed))
-    merged = merge(index, landing, clean, from_prev, from_next, incoming, groups)
+    merged = merge(index, landing, clean, low, high, incoming, groups)
 
     quarter = row_count // groups
     summed = [merged[0]] + [None] * (groups - 1)
-    for i in [1, *exchange_order(groups)[:-1]]:
+    for i in exchange_order(groups):
         summed[i] = swapped(merged[i], "chan", i)
     tiles = jnp.stack([piece[quarter:] for piece in packed])
     even = [tiles] + [swapped(tiles, "node", 2 * i) for i in range(1, devs // 2)]
-    summed, even = lax.optimization_barrier((summed, even))
+    order = [0, *range(2, groups - 1), 1, groups - 1]
+    listed, even = lax.optimization_barrier(([summed[i] for i in order], even))
+    summed = [listed[order.index(i)] for i in range(groups)]
     even = jnp.stack(even)
     odd = swapped(even, "node", 1)
 
@@ -489,10 +503,9 @@
     share = total[0]
     for i in range(1, devs // 2):
         share = share + wide(swapped(total[i].astype(jnp.bfloat16), "node", 2 * i))
-    grad_weight = share[0]
-    for i in range(1, groups):
-        grad_weight = grad_weight + wide(swapped(share[i].astype(jnp.bfloat16), "chan", i))
-    return (grad_weight, laid_out(index, pieces))
+    others = [swapped(share[i].astype(jnp.bfloat16), "chan", i) for i in range(1, groups)]
+    grad_features, grad_weight = finish(index, pieces, share[0], others)
+    return (grad_weight, grad_features)
 
 
 def solution(mesh):

time: 113 us -> 110 us (0.973)
  starting transfers between devices: 46.4 us -> 43.7 us
    ppermute x20, starting transfers between devices: 35.1 us -> 29.9 us  [swapped(): return lax.ppermute(value, axis, [(i, i ^ by) for i in range(size)])]
    ppermute x2 -> x4, starting transfers between devices: 3.67 us -> 7.39 us  [shifted(): return lax.ppermute(value, axis, pairs)]
    ppermute x20, waiting for transfers between devices: 33 us -> 34.9 us  [swapped(): return lax.ppermute(value, axis, [(i, i ^ by) for i in range(size)])]
    all_to_all x1, starting transfers between devices: 7.62 us -> 6.45 us  [exchanged(): return lax.all_to_all(value, axis, split_axis=0, concat_axis=0, tiled=True)]
  transfers between devices with their start and end apart: 23 -> 25, of which waited for: 9 -> 10; matrix products, arithmetic and copies ran while one was open for 1% -> 1% of each run, Pallas kernels for 8% -> 7%
where the time goes in v10:
time: 110 us; the launch traced here: 109 us
  starting transfers between devices  43.7 us (40%)
  waiting for transfers between devices  41.3 us (38%)
  Pallas kernels  18.7 us (17%)
  local copies, waits for them, and re-layouts  2.84 us (3%)
  other arithmetic  1.82 us (2%)
    ppermute x20, waiting for transfers between devices, swapped(): return lax.ppermute(value, axis, [(i, i ^ by) for i in range(size)])  34.9 us
    ppermute x20, starting transfers between devices, swapped(): return lax.ppermute(value, axis, [(i, i ^ by) for i in range(size)])  29.9 us
    pallas_call x1, Pallas kernels, aggregate(): pl.pallas_call(functools.partial(aggregate_kernel, reach, groups, send_sl...  8.2 us
    ppermute x4, starting transfers between devices, shifted(): return lax.ppermute(value, axis, pairs)  7.39 us
    all_to_all x1, starting transfers between devices, exchanged(): return lax.all_to_all(value, axis, split_axis=0, concat_axis=0, tiled=True)  6.45 us
    all_to_all x1, waiting for transfers between devices, exchanged(): return lax.all_to_all(value, axis, split_axis=0, concat_axis=0, tiled=True)  6.38 us
    pallas_call x1, Pallas kernels, feature_rows(): pl.pallas_call(feature_kernel, in_specs=[IN_SMEM] + [IN_VMEM] * (groups +...  3.22 us
    pallas_call x1, Pallas kernels, weight_partial(): pl.pallas_call(functools.partial(weight_kernel, devs), in_specs=[IN_SMEM]...  2.62 us
  transfers between devices with their start and end apart: 25, of which 10 were waited for; matrix products, arithmetic and copies ran while one was open for 1% of the time, Pallas kernels for 7%

profile of v10, /device:TPU:0, one launch (start us, length us, event | category | flops | bytes accessed | tf_op | source)
XLA Modules:
  0.0 109.3 jit_solution(13242614598105032966)
XLA Ops:
  0.6 0.6 pad_add_fusion.me.index
  1.2 8.2 %aggregate.1 = (bf16[14,128,256]{2,1,0:T(8,128)(2,1)}, bf16[16,128,256]{2,1,0:T(8,128)(2,1)}, bf16[2,128,256]{2,1,0:T(8,128)(2,1)}, bf16[2,128,256]{2,1,0:T(8,12...) custom-call(s32[2]{0:T(128)} %pad_add_fusion.me.index, ...), custom_call_target="tpu_custom_call" | custom-call | flops 1174405120 | bytes 7798784 | tf_op jit(solution)/shard_map/aggregate/pallas_call | solution.py:185
  9.5 2.4 %collective-permute-start = (bf16[2,128,256]{2,1,0:T(8,128)(2,1)}, bf16[2,128,256]{2,1,0:T(8,128)(2,1)S(1)}, u32[]{:S(2)}, u32[]{:S(2)}) collective-permute-start(bf16[2,128,256]{2,1,0:T(8,128)(2,1)} %get-tuple-element.39), channel_id=1, source_target_pairs={{0,4},{4,8},{8,12},{12,16},{16,20},{20,24},{24,28},{1,5},{5,9},{9,... | collective-permute-start | bytes 393224 | tf_op jit(solution)/shard_map/ppermute | solution.py:34
  11.9 1.3 %collective-permute-start.1 = (bf16[2,128,256]{2,1,0:T(8,128)(2,1)}, bf16[2,128,256]{2,1,0:T(8,128)(2,1)S(1)}, u32[]{:S(2)}, u32[]{:S(2)}) collective-permute-start(bf16[2,128,256]{2,1,0:T(8,128)(2,1)} %get-tuple-element.40), channel_id=1, source_target_pairs={{4,0},{8,4},{12,8},{16,12},{20,16},{24,20},{28,24},{5,1},{9,5},{13... | collective-permute-start | bytes 393224 | tf_op jit(solution)/shard_map/ppermute | solution.py:34
  13.2 2.5 %collective-permute-start.2 = (bf16[576,256]{1,0:T(8,128)(2,1)}, bf16[576,256]{1,0:T(8,128)(2,1)S(1)}, u32[]{:S(2)}, u32[]{:S(2)}) collective-permute-start(bf16[576,256]{1,0:T(8,128)(2,1)} %get-tuple-element.46), channel_id=1, source_target_pairs={{0,1},{1,0},{2,3},{3,2},{4,5},{5,4},{6,7},{7,6},{8,9},{9,8},{10,11... | collective-permute-start | bytes 884744 | tf_op jit(solution)/shard_map/ppermute | solution.py:39
  15.6 2.6 %collective-permute-start.3 = (bf16[576,256]{1,0:T(8,128)(2,1)}, bf16[576,256]{1,0:T(8,128)(2,1)S(1)}, u32[]{:S(2)}, u32[]{:S(2)}) collective-permute-start(bf16[576,256]{1,0:T(8,128)(2,1)} %get-tuple-element.47), channel_id=1, source_target_pairs={{0,2},{1,3},{2,0},{3,1},{4,6},{5,7},{6,4},{7,5},{8,10},{9,11},{10,... | collective-permute-start | bytes 884744 | tf_op jit(solution)/shard_map/ppermute | solution.py:39
  18.2 0.0 collective-permute-start.4
  18.2 0.0 collective-permute-done.low
  18.2 0.0 collective-permute-done.1.high
  18.3 1.2 %copy-done = bf16[16,128,256]{2,1,0:T(8,128)(2,1)S(1)} copy-done((bf16[16,128,256]{2,1,0:T(8,128)(2,1)S(1)}, bf16[16,128,256]{2,1,0:T(8,128)(2,1)}, u32[]{:S(2)}) %copy-start) | copy-done | bytes 1048600
  19.5 1.5 %patch.1 = bf16[16,128,256]{2,1,0:T(8,128)(2,1)S(1)} custom-call(s32[2]{0:T(128)S(1)} %copy-done.4, s32[112]{0:T(128)S(1)} %copy-done.5, bf16[16,128,256]{2,1,0:T(8,128)(2,1)S(1)} %copy-done, bf16[2,128,256]{2,1,0:T(8,128)(2,1)S(1)} %collective-permute-done.low, bf16[2,128,256]{2,1,0:T(8,128)(2,1)S(1)} %collective-permute-done.1.high), custom_call_target="tpu_custom_call", output_to_operand_aliasing={{}: (2, {})} | custom-call | tf_op jit(solution)/shard_map/patch/pallas_call | solution.py:239
  21.0 1.0 copy-done.1
  21.9 6.4 %all-to-all-start = ((bf16[16,128,256]{2,1,0:T(8,128)(2,1)}), bf16[16,128,256]{2,1,0:T(8,128)(2,1)S(1)}, u32[]{:S(2)}, u32[]{:S(2)}) async-start(bf16[16,128,256]{2,1,0:T(8,128)(2,1)} %copy-done.1), calls=%async_computation | async-start | bytes 2097152 | tf_op jit(solution)/shard_map/all_to_all | solution.py:43
  28.4 0.1 eq.30
  28.5 0.1 add.36
  28.6 0.3 convert_reduce_fusion
  28.9 0.1 copy.14
  29.0 2.4 %collective-permute-start.5 = (bf16[2,128,256]{2,1,0:T(8,128)(2,1)S(1)}, bf16[2,128,256]{2,1,0:T(8,128)(2,1)S(1)}, u32[]{:S(2)}, u32[]{:S(2)}) collective-permute-start(bf16[2,128,256]{2,1,0:T(8,128)(2,1)S(1)} %copy-done.7), channel_id=1, source_target_pairs={{0,4},{4,8},{8,12},{12,16},{16,20},{20,24},{24,28},{1,5},{5,9},{9,... | collective-permute-start | bytes 393224 | tf_op jit(solution)/shard_map/ppermute | solution.py:34
  31.4 1.3 %collective-permute-start.6 = (bf16[2,128,256]{2,1,0:T(8,128)(2,1)S(1)}, bf16[2,128,256]{2,1,0:T(8,128)(2,1)S(1)}, u32[]{:S(2)}, u32[]{:S(2)}) collective-permute-start(bf16[2,128,256]{2,1,0:T(8,128)(2,1)S(1)} %copy-done.6), channel_id=1, source_target_pairs={{4,0},{8,4},{12,8},{16,12},{20,16},{24,20},{28,24},{5,1},{9,5},{13... | collective-permute-start | bytes 393224 | tf_op jit(solution)/shard_map/ppermute | solution.py:34
  32.7 0.1 select_reduce_fusion
  32.9 0.1 copy.15
  33.0 0.1 sub.13.landing
  33.1 0.0 collective-permute-done.2.refs_1_
  33.1 4.3 %collective-permute-done.4.refs_3_ = bf16[576,256]{1,0:T(8,128)(2,1)S(1)} collective-permute-done((bf16[576,256]{1,0:T(8,128)(2,1)}, bf16[576,256]{1,0:T(8,128)(2,1)S(1)}, u32[]{:S(2)}, u32[]{:S(2)}) %collective-permute-start.4) | collective-permute-done | bytes 294944 | tf_op jit(solution)/shard_map/ppermute | solution.py:39
  37.4 6.4 %all-to-all-done.incoming = bf16[16,128,256]{2,1,0:T(8,128)(2,1)S(1)} async-done(((bf16[16,128,256]{2,1,0:T(8,128)(2,1)}), bf16[16,128,256]{2,1,0:T(8,128)(2,1)S(1)}, u32[]{:S(2)}, u32[]{:S(2)}) %all-to-all-start) | async-done | bytes 1048608 | tf_op jit(solution)/shard_map/all_to_all | solution.py:43
  43.8 0.0 collective-permute-done.5.low
  43.8 1.0 merge.1
  44.9 0.1 slice_bitcast_fusion.4
  44.9 3.7 %collective-permute-start.9 = (bf16[448,256]{1,0:T(8,128)(2,1)S(1)}, bf16[448,256]{1,0:T(8,128)(2,1)S(1)}, u32[]{:S(2)}, u32[]{:S(2)}) collective-permute-start(bf16[448,256]{1,0:T(8,128)(2,1)S(1)} %get-tuple-element.85), channel_id=1, source_target_pairs={{0,3},{1,2},{2,1},{3,0},{4,7},{5,6},{6,5},{7,4},{8,11},{9,10},{10,... | collective-permute-start | bytes 688136 | tf_op jit(solution)/shard_map/ppermute | solution.py:39
  48.7 2.8 %collective-permute-start.12 = (bf16[4,128,256]{2,1,0:T(8,128)(2,1)S(1)}, bf16[4,128,256]{2,1,0:T(8,128)(2,1)S(1)}, u32[]{:S(2)}, u32[]{:S(2)}) collective-permute-start(bf16[4,128,256]{2,1,0:T(8,128)(2,1)S(1)} %pad_maximum_fusion.1), channel_id=1, source_target_pairs={{0,24},{4,28},{8,16},{12,20},{16,8},{20,12},{24,0},{28,4},{1,25},{... | collective-permute-start | bytes 786440 | tf_op jit(solution)/shard_map/ppermute | solution.py:39
  51.5 0.6 collective-permute-start.11
  52.1 1.4 %collective-permute-start.10 = (bf16[4,128,256]{2,1,0:T(8,128)(2,1)S(1)}, bf16[4,128,256]{2,1,0:T(8,128)(2,1)S(1)}, u32[]{:S(2)}, u32[]{:S(2)}) collective-permute-start(bf16[4,128,256]{2,1,0:T(8,128)(2,1)S(1)} %pad_maximum_fusion.1), channel_id=1, source_target_pairs={{0,8},{4,12},{8,0},{12,4},{16,24},{20,28},{24,16},{28,20},{1,9},{5... | collective-permute-start | bytes 786440 | tf_op jit(solution)/shard_map/ppermute | solution.py:39
  53.5 0.0 collective-permute-start.8
  53.5 0.9 collective-permute-done.9.refs_7_.refs_3_
  54.4 5.3 %collective-permute-start.7 = (bf16[448,256]{1,0:T(8,128)(2,1)S(1)}, bf16[448,256]{1,0:T(8,128)(2,1)S(1)}, u32[]{:S(2)}, u32[]{:S(2)}) collective-permute-start(bf16[448,256]{1,0:T(8,128)(2,1)S(1)} %get-tuple-element.87), channel_id=1, source_target_pairs={{0,2},{1,3},{2,0},{3,1},{4,6},{5,7},{6,4},{7,5},{8,10},{9,11},{10,... | collective-permute-start | bytes 688136 | tf_op jit(solution)/shard_map/ppermute | solution.py:39
  59.7 0.9 collective-permute-done.8.refs_5_.refs_1_
  60.6 10.2 %collective-permute-done.7.refs_6_.refs_2_ = bf16[448,256]{1,0:T(8,128)(2,1)S(1)} collective-permute-done((bf16[448,256]{1,0:T(8,128)(2,1)S(1)}, bf16[448,256]{1,0:T(8,128)(2,1)S(1)}, u32[]{:S(2)}, u32[]{:S(2)}) %collective-permute-start.7) | collective-permute-done | bytes 229408 | tf_op jit(solution)/shard_map/ppermute | solution.py:39
  70.8 0.0 collective-permute-done.11
  70.8 0.0 collective-permute-done.10
  70.8 0.1 pad_maximum_fusion.refs_4_
  70.9 0.2 collective-permute-start.13
  71.1 2.6 %weight_partial.1 = (bf16[4,4,128,256]{3,2,1,0:T(8,128)(2,1)S(1)}, bf16[4,4,128,256]{3,2,1,0:T(8,128)(2,1)S(1)}) custom-call(s32[2]{0:T(128)S(1)} %copy-done.4, bf16[576,256]{1,0:T(8,128)(2,1)S(1)} %copy-done.3, bf16[576,256]{1,0:T(8,128)(2,1)S(1)} %collective-permute-done.2.refs_1_, bf16[576,256]{1,0:T(8,128)(2,1)S(1)} %collective-permute-done.3.refs_2_, ...), custom_call_target="tpu_custom_call" | custom-call | flops 939524096 | bytes 3932160 | tf_op jit(solution)/shard_map/weight_partial/pallas_call | solution.py:326
  73.8 0.0 collective-permute-done.13.refs_5_
  73.8 0.4 collective-permute-start.14
  74.2 3.2 %feature_rows.1 = bf16[4,448,256]{2,1,0:T(8,128)(2,1)S(1)} custom-call(s32[2]{0:T(128)S(1)} %copy-done.4, bf16[448,256]{1,0:T(8,128)(2,1)S(1)} %get-tuple-element.58.refs_4_.refs_0_, bf16[448,256]{1,0:T(8,128)(2,1)S(1)} %collective-permute-done.8.refs_5_.refs_1_, bf16[448,256]{1,0:T(8,128)(2,1)S(1)} %collective-permute-done.7.refs_6_.refs_2_, ...), custom_call_target="tpu_custom_call" | custom-call | flops 939524096 | bytes 3932160 | tf_op jit(solution)/shard_map/feature_rows/pallas_call | solution.py:374
  77.4 0.0 collective-permute-done.14
  77.4 0.4 convert_add_fusion
  77.8 0.1 slice_bitcast_fusion.3
  77.9 1.1 collective-permute-start.15
  79.0 0.0 collective-permute-start.17
  79.0 2.5 %collective-permute-start.16 = (bf16[4,128,256]{2,1,0:T(8,128)(2,1)S(1)}, bf16[4,128,256]{2,1,0:T(8,128)(2,1)S(1)}, u32[]{:S(2)}, u32[]{:S(2)}) collective-permute-start(bf16[4,128,256]{2,1,0:T(8,128)(2,1)S(1)} %get-tuple-element.80), channel_id=1, source_target_pairs={{0,16},{4,20},{8,24},{12,28},{16,0},{20,4},{24,8},{28,12},{1,17},{... | collective-permute-start | bytes 786440 | tf_op jit(solution)/shard_map/ppermute | solution.py:39
  81.4 0.1 slice_bitcast_fusion.8
  81.5 1.6 %collective-permute-start.20 = (bf16[448,256]{1,0:T(8,128)(2,1)S(1)}, bf16[448,256]{1,0:T(8,128)(2,1)S(1)}, u32[]{:S(2)}, u32[]{:S(2)}) collective-permute-start(bf16[448,256]{1,0:T(8,128)(2,1)S(1)} %get-tuple-element.81), channel_id=1, source_target_pairs={{0,3},{1,2},{2,1},{3,0},{4,7},{5,6},{6,5},{7,4},{8,11},{9,10},{10,... | collective-permute-start | bytes 688136 | tf_op jit(solution)/shard_map/ppermute | solution.py:39
  83.2 3.9 %collective-permute-done.15 = bf16[4,128,256]{2,1,0:T(8,128)(2,1)S(1)} collective-permute-done((bf16[4,128,256]{2,1,0:T(8,128)(2,1)S(1)}, bf16[4,128,256]{2,1,0:T(8,128)(2,1)S(1)}, u32[]{:S(2)}, u32[]{:S(2)}) %collective-permute-start.15) | collective-permute-done | bytes 262176 | tf_op jit(solution)/shard_map/ppermute | solution.py:39
  87.1 0.0 collective-permute-start.18
  87.1 3.3 %collective-permute-done.17 = bf16[4,128,256]{2,1,0:T(8,128)(2,1)S(1)} collective-permute-done((bf16[4,128,256]{2,1,0:T(8,128)(2,1)S(1)}, bf16[4,128,256]{2,1,0:T(8,128)(2,1)S(1)}, u32[]{:S(2)}, u32[]{:S(2)}) %collective-permute-start.17) | collective-permute-done | bytes 262176 | tf_op jit(solution)/shard_map/ppermute | solution.py:39
  90.4 2.7 %collective-permute-done.16 = bf16[4,128,256]{2,1,0:T(8,128)(2,1)S(1)} collective-permute-done((bf16[4,128,256]{2,1,0:T(8,128)(2,1)S(1)}, bf16[4,128,256]{2,1,0:T(8,128)(2,1)S(1)}, u32[]{:S(2)}, u32[]{:S(2)}) %collective-permute-start.16) | collective-permute-done | bytes 262176 | tf_op jit(solution)/shard_map/ppermute | solution.py:39
  93.1 0.2 fusion.7
  93.3 2.0 %collective-permute-start.23 = (bf16[128,256]{1,0:T(8,128)(2,1)S(1)}, bf16[128,256]{1,0:T(8,128)(2,1)S(1)}, u32[]{:S(2)}, u32[]{:S(2)}) collective-permute-start(bf16[128,256]{1,0:T(8,128)(2,1)S(1)} %get-tuple-element.89), channel_id=1, source_target_pairs={{0,3},{1,2},{2,1},{3,0},{4,7},{5,6},{6,5},{7,4},{8,11},{9,10},{10,... | collective-permute-start | bytes 196616 | tf_op jit(solution)/shard_map/ppermute | solution.py:39
  95.3 0.0 collective-permute-start.22
  95.3 3.1 %collective-permute-start.21 = (bf16[128,256]{1,0:T(8,128)(2,1)S(1)}, bf16[128,256]{1,0:T(8,128)(2,1)S(1)}, u32[]{:S(2)}, u32[]{:S(2)}) collective-permute-start(bf16[128,256]{1,0:T(8,128)(2,1)S(1)} %get-tuple-element.91), channel_id=1, source_target_pairs={{0,1},{1,0},{2,3},{3,2},{4,5},{5,4},{6,7},{7,6},{8,9},{9,8},{10,11... | collective-permute-start | bytes 196616 | tf_op jit(solution)/shard_map/ppermute | solution.py:39
  98.5 7.2 %collective-permute-done.19.refs_2_ = bf16[448,256]{1,0:T(8,128)(2,1)S(1)} collective-permute-done((bf16[448,256]{1,0:T(8,128)(2,1)S(1)}, bf16[448,256]{1,0:T(8,128)(2,1)S(1)}, u32[]{:S(2)}, u32[]{:S(2)}) %collective-permute-start.19) | collective-permute-done | bytes 229408 | tf_op jit(solution)/shard_map/ppermute | solution.py:39
  105.7 1.5 %collective-permute-done.22.refs_5_ = bf16[128,256]{1,0:T(8,128)(2,1)S(1)} collective-permute-done((bf16[128,256]{1,0:T(8,128)(2,1)S(1)}, bf16[128,256]{1,0:T(8,128)(2,1)S(1)}, u32[]{:S(2)}, u32[]{:S(2)}) %collective-permute-start.22) | collective-permute-done | bytes 65568 | tf_op jit(solution)/shard_map/ppermute | solution.py:39
  107.2 2.1 %finish.1 = (bf16[1792,256]{1,0:T(8,128)(2,1)}, f32[128,256]{1,0:T(8,128)}) custom-call(s32[2]{0:T(128)S(1)} %copy-done.4, f32[128,256]{1,0:T(8,128)S(1)} %slice_bitcast_fusion.12.share, bf16[448,256]{1,0:T(8,128)(2,1)S(1)} %get-tuple-element.84.refs_0_, bf16[448,256]{1,0:T(8,128)(2,1)S(1)} %collective-permute-done.18.refs_1_, ...), custom_call_target="tpu_custom_call" | custom-call | tf_op jit(solution)/shard_map/finish/pallas_call | solution.py:412
  (31 shorter events, 0.2 us)
Async XLA Ops:
  1.2 17.0 %copy-start.4 = (s32[2]{0:T(128)S(1)}, s32[2]{0:T(128)}, u32[]{:S(2)}) copy-start(s32[2]{0:T(128)} %pad_add_fusion.me.index) | copy-start | bytes 28
  1.2 17.0 %copy-start.5 = (s32[112]{0:T(128)S(1)}, s32[112]{0:T(128)}, u32[]{:S(2)}) copy-start(s32[112]{0:T(128)} %shuffle.3) | copy-start | bytes 1348
  9.5 8.8 %collective-permute-start = (bf16[2,128,256]{2,1,0:T(8,128)(2,1)}, bf16[2,128,256]{2,1,0:T(8,128)(2,1)S(1)}, u32[]{:S(2)}, u32[]{:S(2)}) collective-permute-start(bf16[2,128,256]{2,1,0:T(8,128)(2,1)} %get-tuple-element.39), channel_id=1, source_target_pairs={{0,4},{4,8},{8,12},{12,16},{16,20},{20,24},{24,28},{1,5},{5,9},{9,... | collective-permute-start | bytes 393224 | tf_op jit(solution)/shard_map/ppermute | solution.py:34
  11.9 6.4 %collective-permute-start.1 = (bf16[2,128,256]{2,1,0:T(8,128)(2,1)}, bf16[2,128,256]{2,1,0:T(8,128)(2,1)S(1)}, u32[]{:S(2)}, u32[]{:S(2)}) collective-permute-start(bf16[2,128,256]{2,1,0:T(8,128)(2,1)} %get-tuple-element.40), channel_id=1, source_target_pairs={{4,0},{8,4},{12,8},{16,12},{20,16},{24,20},{28,24},{5,1},{9,5},{13... | collective-permute-start | bytes 393224 | tf_op jit(solution)/shard_map/ppermute | solution.py:34
  13.2 19.9 %collective-permute-start.2 = (bf16[576,256]{1,0:T(8,128)(2,1)}, bf16[576,256]{1,0:T(8,128)(2,1)S(1)}, u32[]{:S(2)}, u32[]{:S(2)}) collective-permute-start(bf16[576,256]{1,0:T(8,128)(2,1)} %get-tuple-element.46), channel_id=1, source_target_pairs={{0,1},{1,0},{2,3},{3,2},{4,5},{5,4},{6,7},{7,6},{8,9},{9,8},{10,11... | collective-permute-start | bytes 884744 | tf_op jit(solution)/shard_map/ppermute | solution.py:39
  15.6 17.4 %collective-permute-start.3 = (bf16[576,256]{1,0:T(8,128)(2,1)}, bf16[576,256]{1,0:T(8,128)(2,1)S(1)}, u32[]{:S(2)}, u32[]{:S(2)}) collective-permute-start(bf16[576,256]{1,0:T(8,128)(2,1)} %get-tuple-element.47), channel_id=1, source_target_pairs={{0,2},{1,3},{2,0},{3,1},{4,6},{5,7},{6,4},{7,5},{8,10},{9,11},{10,... | collective-permute-start | bytes 884744 | tf_op jit(solution)/shard_map/ppermute | solution.py:39
  18.2 19.2 %collective-permute-start.4 = (bf16[576,256]{1,0:T(8,128)(2,1)}, bf16[576,256]{1,0:T(8,128)(2,1)S(1)}, u32[]{:S(2)}, u32[]{:S(2)}) collective-permute-start(bf16[576,256]{1,0:T(8,128)(2,1)} %get-tuple-element.48), channel_id=1, source_target_pairs={{0,3},{1,2},{2,1},{3,0},{4,7},{5,6},{6,5},{7,4},{8,11},{9,10},{10,... | collective-permute-start | bytes 884744 | tf_op jit(solution)/shard_map/ppermute | solution.py:39
  18.3 1.2 %copy-start = (bf16[16,128,256]{2,1,0:T(8,128)(2,1)S(1)}, bf16[16,128,256]{2,1,0:T(8,128)(2,1)}, u32[]{:S(2)}) copy-start(bf16[16,128,256]{2,1,0:T(8,128)(2,1)} %get-tuple-element.38.outgoing) | copy-start | bytes 3145732
  19.5 9.5 %copy-start.7 = (bf16[2,128,256]{2,1,0:T(8,128)(2,1)S(1)}, bf16[2,128,256]{2,1,0:T(8,128)(2,1)}, u32[]{:S(2)}) copy-start(bf16[2,128,256]{2,1,0:T(8,128)(2,1)} %get-tuple-element.55) | copy-start | bytes 393220
  19.5 11.9 %copy-start.6 = (bf16[2,128,256]{2,1,0:T(8,128)(2,1)S(1)}, bf16[2,128,256]{2,1,0:T(8,128)(2,1)}, u32[]{:S(2)}) copy-start(bf16[2,128,256]{2,1,0:T(8,128)(2,1)} %get-tuple-element.56) | copy-start | bytes 393220
  19.5 24.3 %copy-start.2 = (bf16[14,128,256]{2,1,0:T(8,128)(2,1)S(1)}, bf16[14,128,256]{2,1,0:T(8,128)(2,1)}, u32[]{:S(2)}) copy-start(bf16[14,128,256]{2,1,0:T(8,128)(2,1)} %get-tuple-element.54.clean) | copy-start | bytes 2752516
  21.0 1.0 copy-start.1
  21.9 21.9 %all-to-all-start = ((bf16[16,128,256]{2,1,0:T(8,128)(2,1)}), bf16[16,128,256]{2,1,0:T(8,128)(2,1)S(1)}, u32[]{:S(2)}, u32[]{:S(2)}) async-start(bf16[16,128,256]{2,1,0:T(8,128)(2,1)} %copy-done.1), calls=%async_computation | async-start | bytes 2097152 | tf_op jit(solution)/shard_map/all_to_all | solution.py:43
  29.0 14.8 %collective-permute-start.5 = (bf16[2,128,256]{2,1,0:T(8,128)(2,1)S(1)}, bf16[2,128,256]{2,1,0:T(8,128)(2,1)S(1)}, u32[]{:S(2)}, u32[]{:S(2)}) collective-permute-start(bf16[2,128,256]{2,1,0:T(8,128)(2,1)S(1)} %copy-done.7), channel_id=1, source_target_pairs={{0,4},{4,8},{8,12},{12,16},{16,20},{20,24},{24,28},{1,5},{5,9},{9,... | collective-permute-start | bytes 393224 | tf_op jit(solution)/shard_map/ppermute | solution.py:34
  31.4 12.4 %collective-permute-start.6 = (bf16[2,128,256]{2,1,0:T(8,128)(2,1)S(1)}, bf16[2,128,256]{2,1,0:T(8,128)(2,1)S(1)}, u32[]{:S(2)}, u32[]{:S(2)}) collective-permute-start(bf16[2,128,256]{2,1,0:T(8,128)(2,1)S(1)} %copy-done.6), channel_id=1, source_target_pairs={{4,0},{8,4},{12,8},{16,12},{20,16},{24,20},{28,24},{5,1},{9,5},{13... | collective-permute-start | bytes 393224 | tf_op jit(solution)/shard_map/ppermute | solution.py:34
  43.8 4.8 %copy-start.3 = (bf16[576,256]{1,0:T(8,128)(2,1)S(1)}, bf16[576,256]{1,0:T(8,128)(2,1)}, u32[]{:S(2)}) copy-start(bf16[576,256]{1,0:T(8,128)(2,1)} %get-tuple-element.49.refs_0_) | copy-start | bytes 884740
  44.9 9.4 %collective-permute-start.9 = (bf16[448,256]{1,0:T(8,128)(2,1)S(1)}, bf16[448,256]{1,0:T(8,128)(2,1)S(1)}, u32[]{:S(2)}, u32[]{:S(2)}) collective-permute-start(bf16[448,256]{1,0:T(8,128)(2,1)S(1)} %get-tuple-element.85), channel_id=1, source_target_pairs={{0,3},{1,2},{2,1},{3,0},{4,7},{5,6},{6,5},{7,4},{8,11},{9,10},{10,... | collective-permute-start | bytes 688136 | tf_op jit(solution)/shard_map/ppermute | solution.py:39
  48.7 22.1 %collective-permute-start.12 = (bf16[4,128,256]{2,1,0:T(8,128)(2,1)S(1)}, bf16[4,128,256]{2,1,0:T(8,128)(2,1)S(1)}, u32[]{:S(2)}, u32[]{:S(2)}) collective-permute-start(bf16[4,128,256]{2,1,0:T(8,128)(2,1)S(1)} %pad_maximum_fusion.1), channel_id=1, source_target_pairs={{0,24},{4,28},{8,16},{12,20},{16,8},{20,12},{24,0},{28,4},{1,25},{... | collective-permute-start | bytes 786440 | tf_op jit(solution)/shard_map/ppermute | solution.py:39
  51.5 19.3 %collective-permute-start.11 = (bf16[4,128,256]{2,1,0:T(8,128)(2,1)S(1)}, bf16[4,128,256]{2,1,0:T(8,128)(2,1)S(1)}, u32[]{:S(2)}, u32[]{:S(2)}) collective-permute-start(bf16[4,128,256]{2,1,0:T(8,128)(2,1)S(1)} %pad_maximum_fusion.1), channel_id=1, source_target_pairs={{0,16},{4,20},{8,24},{12,28},{16,0},{20,4},{24,8},{28,12},{1,17},{... | collective-permute-start | bytes 786440 | tf_op jit(solution)/shard_map/ppermute | solution.py:39
  52.1 18.7 %collective-permute-start.10 = (bf16[4,128,256]{2,1,0:T(8,128)(2,1)S(1)}, bf16[4,128,256]{2,1,0:T(8,128)(2,1)S(1)}, u32[]{:S(2)}, u32[]{:S(2)}) collective-permute-start(bf16[4,128,256]{2,1,0:T(8,128)(2,1)S(1)} %pad_maximum_fusion.1), channel_id=1, source_target_pairs={{0,8},{4,12},{8,0},{12,4},{16,24},{20,28},{24,16},{28,20},{1,9},{5... | collective-permute-start | bytes 786440 | tf_op jit(solution)/shard_map/ppermute | solution.py:39
  53.5 7.1 %collective-permute-start.8 = (bf16[448,256]{1,0:T(8,128)(2,1)S(1)}, bf16[448,256]{1,0:T(8,128)(2,1)S(1)}, u32[]{:S(2)}, u32[]{:S(2)}) collective-permute-start(bf16[448,256]{1,0:T(8,128)(2,1)S(1)} %get-tuple-element.86), channel_id=1, source_target_pairs={{0,1},{1,0},{2,3},{3,2},{4,5},{5,4},{6,7},{7,6},{8,9},{9,8},{10,11... | collective-permute-start | bytes 688136 | tf_op jit(solution)/shard_map/ppermute | solution.py:39
  54.4 16.4 %collective-permute-start.7 = (bf16[448,256]{1,0:T(8,128)(2,1)S(1)}, bf16[448,256]{1,0:T(8,128)(2,1)S(1)}, u32[]{:S(2)}, u32[]{:S(2)}) collective-permute-start(bf16[448,256]{1,0:T(8,128)(2,1)S(1)} %get-tuple-element.87), channel_id=1, source_target_pairs={{0,2},{1,3},{2,0},{3,1},{4,6},{5,7},{6,4},{7,5},{8,10},{9,11},{10,... | collective-permute-start | bytes 688136 | tf_op jit(solution)/shard_map/ppermute | solution.py:39
  70.9 2.8 %collective-permute-start.13 = (bf16[4,4,128,256]{3,2,1,0:T(8,128)(2,1)S(1)}, bf16[4,4,128,256]{3,2,1,0:T(8,128)(2,1)S(1)}, u32[]{:S(2)}, u32[]{:S(2)}) collective-permute-start(bf16[4,4,128,256]{3,2,1,0:T(8,128)(2,1)S(1)} %pad_maximum_fusion.refs_4_), channel_id=1, source_target_pairs={{0,4},{4,0},{8,12},{12,8},{16,20},{20,16},{24,28},{28,24},{1,5},{5... | collective-permute-start | bytes 3145736 | tf_op jit(solution)/shard_map/ppermute | solution.py:39
  73.8 3.7 %collective-permute-start.14 = (bf16[4,4,128,256]{3,2,1,0:T(8,128)(2,1)S(1)}, bf16[4,4,128,256]{3,2,1,0:T(8,128)(2,1)S(1)}, u32[]{:S(2)}, u32[]{:S(2)}) collective-permute-start(bf16[4,4,128,256]{3,2,1,0:T(8,128)(2,1)S(1)} %get-tuple-element.68), channel_id=1, source_target_pairs={{0,4},{4,0},{8,12},{12,8},{16,20},{20,16},{24,28},{28,24},{1,5},{5... | collective-permute-start | bytes 3145736 | tf_op jit(solution)/shard_map/ppermute | solution.py:39
  77.9 9.2 %collective-permute-start.15 = (bf16[4,128,256]{2,1,0:T(8,128)(2,1)S(1)}, bf16[4,128,256]{2,1,0:T(8,128)(2,1)S(1)}, u32[]{:S(2)}, u32[]{:S(2)}) collective-permute-start(bf16[4,128,256]{2,1,0:T(8,128)(2,1)S(1)} %get-tuple-element.78), channel_id=1, source_target_pairs={{0,8},{4,12},{8,0},{12,4},{16,24},{20,28},{24,16},{28,20},{1,9},{5... | collective-permute-start | bytes 786440 | tf_op jit(solution)/shard_map/ppermute | solution.py:39
  79.0 11.5 %collective-permute-start.17 = (bf16[4,128,256]{2,1,0:T(8,128)(2,1)S(1)}, bf16[4,128,256]{2,1,0:T(8,128)(2,1)S(1)}, u32[]{:S(2)}, u32[]{:S(2)}) collective-permute-start(bf16[4,128,256]{2,1,0:T(8,128)(2,1)S(1)} %get-tuple-element.79), channel_id=1, source_target_pairs={{0,24},{4,28},{8,16},{12,20},{16,8},{20,12},{24,0},{28,4},{1,25},{... | collective-permute-start | bytes 786440 | tf_op jit(solution)/shard_map/ppermute | solution.py:39
  79.0 14.2 %collective-permute-start.16 = (bf16[4,128,256]{2,1,0:T(8,128)(2,1)S(1)}, bf16[4,128,256]{2,1,0:T(8,128)(2,1)S(1)}, u32[]{:S(2)}, u32[]{:S(2)}) collective-permute-start(bf16[4,128,256]{2,1,0:T(8,128)(2,1)S(1)} %get-tuple-element.80), channel_id=1, source_target_pairs={{0,16},{4,20},{8,24},{12,28},{16,0},{20,4},{24,8},{28,12},{1,17},{... | collective-permute-start | bytes 786440 | tf_op jit(solution)/shard_map/ppermute | solution.py:39
  81.5 13.8 %collective-permute-start.20 = (bf16[448,256]{1,0:T(8,128)(2,1)S(1)}, bf16[448,256]{1,0:T(8,128)(2,1)S(1)}, u32[]{:S(2)}, u32[]{:S(2)}) collective-permute-start(bf16[448,256]{1,0:T(8,128)(2,1)S(1)} %get-tuple-element.81), channel_id=1, source_target_pairs={{0,3},{1,2},{2,1},{3,0},{4,7},{5,6},{6,5},{7,4},{8,11},{9,10},{10,... | collective-permute-start | bytes 688136 | tf_op jit(solution)/shard_map/ppermute | solution.py:39
  83.1 22.5 %collective-permute-start.19 = (bf16[448,256]{1,0:T(8,128)(2,1)S(1)}, bf16[448,256]{1,0:T(8,128)(2,1)S(1)}, u32[]{:S(2)}, u32[]{:S(2)}) collective-permute-start(bf16[448,256]{1,0:T(8,128)(2,1)S(1)} %get-tuple-element.82), channel_id=1, source_target_pairs={{0,2},{1,3},{2,0},{3,1},{4,6},{5,7},{6,4},{7,5},{8,10},{9,11},{10,... | collective-permute-start | bytes 688136 | tf_op jit(solution)/shard_map/ppermute | solution.py:39
  87.1 18.6 %collective-permute-start.18 = (bf16[448,256]{1,0:T(8,128)(2,1)S(1)}, bf16[448,256]{1,0:T(8,128)(2,1)S(1)}, u32[]{:S(2)}, u32[]{:S(2)}) collective-permute-start(bf16[448,256]{1,0:T(8,128)(2,1)S(1)} %get-tuple-element.83), channel_id=1, source_target_pairs={{0,1},{1,0},{2,3},{3,2},{4,5},{5,4},{6,7},{7,6},{8,9},{9,8},{10,11... | collective-permute-start | bytes 688136 | tf_op jit(solution)/shard_map/ppermute | solution.py:39
  93.3 12.4 %collective-permute-start.23 = (bf16[128,256]{1,0:T(8,128)(2,1)S(1)}, bf16[128,256]{1,0:T(8,128)(2,1)S(1)}, u32[]{:S(2)}, u32[]{:S(2)}) collective-permute-start(bf16[128,256]{1,0:T(8,128)(2,1)S(1)} %get-tuple-element.89), channel_id=1, source_target_pairs={{0,3},{1,2},{2,1},{3,0},{4,7},{5,6},{6,5},{7,4},{8,11},{9,10},{10,... | collective-permute-start | bytes 196616 | tf_op jit(solution)/shard_map/ppermute | solution.py:39
  95.3 11.8 %collective-permute-start.22 = (bf16[128,256]{1,0:T(8,128)(2,1)S(1)}, bf16[128,256]{1,0:T(8,128)(2,1)S(1)}, u32[]{:S(2)}, u32[]{:S(2)}) collective-permute-start(bf16[128,256]{1,0:T(8,128)(2,1)S(1)} %get-tuple-element.90), channel_id=1, source_target_pairs={{0,2},{1,3},{2,0},{3,1},{4,6},{5,7},{6,4},{7,5},{8,10},{9,11},{10,... | collective-permute-start | bytes 196616 | tf_op jit(solution)/shard_map/ppermute | solution.py:39
  95.3 11.8 %collective-permute-start.21 = (bf16[128,256]{1,0:T(8,128)(2,1)S(1)}, bf16[128,256]{1,0:T(8,128)(2,1)S(1)}, u32[]{:S(2)}, u32[]{:S(2)}) collective-permute-start(bf16[128,256]{1,0:T(8,128)(2,1)S(1)} %get-tuple-element.91), channel_id=1, source_target_pairs={{0,1},{1,0},{2,3},{3,2},{4,5},{5,4},{6,7},{7,6},{8,9},{9,8},{10,11... | collective-permute-start | bytes 196616 | tf_op jit(solution)/shard_map/ppermute | solution.py:39

commit v11 on v10

--- a/solution.py
+++ b/solution.py
@@ -58,14 +58,12 @@
 
 
 def aggregate_kernel(
-    reach, groups, send_slots, me, shuffle, cols, count, gc, pc, gx, px, slopes, adj, features, weight, *refs
+    reach, send_slots, me, shuffle, cols, count, gc, pc, gx, px, slopes, adj, clean, outgoing, *refs
 ):
-    clean, outgoing, *refs = refs
-    sides, packed, refs = refs[:4], refs[4 : 4 + groups], refs[4 + groups :]
-    data, tiles, rhs, stage, results, halos, packs, places, used, sems, pack_sems, out_sems = refs
+    sides, refs = refs[:4], refs[4:]
+    data, tiles, rhs, stage, results, halos, places, used, sems, out_sems = refs
     blocks, slots, rows, _ = adj.shape
     width = gc.shape[1]
-    quarter = features.shape[0] // groups
     spare = blocks + 2 * reach
     pad = 2 * reach * rows
 
@@ -81,16 +79,6 @@
 
     inputs = [copies(step) for step in range(blocks // 2)]
     for copy in sum(inputs, []):
-        copy.start()
-    to_vmem, to_hbm = [], []
-    for i in range(groups):
-        span = pl.ds(pl.multiple_of((me[1] ^ i) * quarter, quarter), quarter)
-        to_vmem.append(
-            pltpu.make_async_copy(features.at[span], packs.at[i, :quarter], pack_sems.at[0, i])
-        )
-        to_vmem.append(pltpu.make_async_copy(weight, packs.at[i, quarter:], pack_sems.at[1, i]))
-        to_hbm.append(pltpu.make_async_copy(packs.at[i], packed[i], pack_sems.at[2, i]))
-    for copy in to_vmem:
         copy.start()
     stage[...] = jnp.zeros_like(stage)
     rhs[:pad] = jnp.zeros((pad, 2 * width), jnp.bfloat16)
@@ -166,29 +154,23 @@
         if step:
             finish(2 * step - 2)
         take(step)
-    for copy in to_vmem:
-        copy.wait()
-    for copy in to_hbm:
-        copy.start()
     for first in range(blocks + 2 * reach - 2, blocks - 4, -2):
         finish(first)
-    for copy in writes + to_hbm:
+    for copy in writes:
         copy.wait()
 
 
-def aggregate(index, shuffle, cols, count, gc, pc, gx, px, slopes, adj, features, weight, reach, devs, groups):
+def aggregate(index, shuffle, cols, count, gc, pc, gx, px, slopes, adj, reach, devs):
     blocks, slots, rows, _ = adj.shape
     width = gc.shape[1]
     send_slots = -(-blocks // devs)
     assert reach % 2 == 0 and blocks % 2 == 0
-    packed = features.shape[0] // groups + weight.shape[0]
     return pl.pallas_call(
-        functools.partial(aggregate_kernel, reach, groups, send_slots),
-        in_specs=[IN_SMEM] * 4 + [IN_HBM] * 4 + [IN_VMEM] + [IN_HBM] * 3,
-        out_specs=[IN_HBM] * (6 + groups),
+        functools.partial(aggregate_kernel, reach, send_slots),
+        in_specs=[IN_SMEM] * 4 + [IN_HBM] * 4 + [IN_VMEM, IN_HBM],
+        out_specs=[IN_HBM] * 6,
         out_shape=[bf16(blocks, rows, width), bf16(devs * send_slots, rows, width)]
-        + [bf16(reach, rows, width)] * 4
-        + [bf16(packed, width)] * groups,
+        + [bf16(reach, rows, width)] * 4,
         scratch_shapes=[
             pltpu.VMEM((4, blocks // 2, 2 * rows, width), jnp.bfloat16),
             pltpu.VMEM((blocks, slots, rows, rows), jnp.bfloat16),
@@ -196,11 +178,9 @@
             pltpu.VMEM((blocks + 2 * reach + 1, 2 * reach + 1, rows, rows), jnp.bfloat16),
             pltpu.VMEM((2, blocks, rows, width), jnp.bfloat16),
             pltpu.VMEM((2, 2, reach, rows, width), jnp.bfloat16),
-            pltpu.VMEM((groups, packed, width), jnp.bfloat16),
             pltpu.SMEM((blocks,), jnp.int32),
             pltpu.SMEM((devs,), jnp.int32),
             pltpu.SemaphoreType.DMA((5, blocks // 2)),
-            pltpu.SemaphoreType.DMA((3, groups)),
             pltpu.SemaphoreType.DMA((4, blocks + 2 * reach)),
         ],
         compiler_params=params(VMEM_ALL),
@@ -210,7 +190,7 @@
             transcendentals=0,
         ),
         name="aggregate",
-    )(index, shuffle, cols, count, gc, pc, gx, px, slopes, adj, features, weight)
+    )(index, shuffle, cols, count, gc, pc, gx, px, slopes, adj)
 
 
 def patch_kernel(reach, blocks, slots, index, shuffle, outgoing, low, high, out, held, ready, places, used, sems):
@@ -293,16 +273,16 @@
     )(index, landing, clean, low, high, incoming)
 
 
-def weight_kernel(devs, index, *refs):
-    groups = (len(refs) - 2) // 2
-    packed, summed, (keep, send) = refs[:groups], refs[groups : 2 * groups], refs[2 * groups :]
+def weight_kernel(devs, index, feats, *refs):
+    *summed, keep, send = refs
+    groups = len(summed)
     me, group = index[0], index[1]
     shares = devs // groups
     height, width = keep.shape[2:]
     rhs = jnp.concatenate([piece[...] for piece in summed], axis=1)
     for relative in range(groups):
         product = lax.dot_general(
-            packed[relative][: rhs.shape[0]],
+            feats[group ^ relative],
             rhs,
             (((0,), (0,)), ((), ())),
             preferred_element_type=jnp.float32,
@@ -319,13 +299,13 @@
             pl.when((node & 1) == 1)(functools.partial(store, send))
 
 
-def weight_partial(index, packed, summed, devs):
-    groups = len(packed)
+def weight_partial(index, feats, summed, devs):
+    groups = len(summed)
     rows, width = summed[0].shape
     height = groups * width // devs
     return pl.pallas_call(
         functools.partial(weight_kernel, devs),
-        in_specs=[IN_SMEM] + [IN_VMEM] * (2 * groups),
+        in_specs=[IN_SMEM] + [IN_VMEM] * (1 + groups),
         out_specs=[IN_VMEM] * 2,
         out_shape=[bf16(devs // 2, groups, height, width)] * 2,
         compiler_params=params(),
@@ -335,7 +315,7 @@
             transcendentals=0,
         ),
         name="weight_partial",
-    )(index, *packed, *summed)
+    )(index, feats, *summed)
 
 
 def feature_kernel(index, *refs):
@@ -450,7 +430,7 @@
     adj_count,
     shuffle_from,
 ):
-    row_count = features.shape[0]
+    row_count, width = features.shape
     blocks, tile_slots, _, _ = adj_vals.shape
     reach = (tile_slots - 1) // 2
     me = lax.axis_index("node")
@@ -462,27 +442,25 @@
 
     args = (index, shuffle_from, adj_cols.T, adj_count)
     args += (grad_clean, pre_clean, grad_corrupt, pre_corrupt, slopes[None, :], adj_vals)
-    clean, outgoing, *sides = aggregate(*args, features, weight, reach, devs, groups)
-    sides, packed = sides[:4], sides[4:]
+    quarter = row_count // groups
+    feats = exchanged(features.reshape(groups, quarter, width), "chan")
+    clean, outgoing, *sides = aggregate(*args, reach, devs)
     low, high = shifted(sides[3], "node", 1), shifted(sides[2], "node", -1)
-    for i in exchange_order(groups):
-        packed[i] = swapped(packed[i], "chan", i)
-
     outgoing = patch(index, shuffle_from, outgoing, low, high, blocks, slots)
-    shuffle_from, outgoing, clean, sides = lax.optimization_barrier(
-        (shuffle_from, outgoing, clean, sides)
+    shuffle_from, weight, outgoing, feats, clean, sides = lax.optimization_barrier(
+        (shuffle_from, weight, outgoing, feats, clean, sides)
     )
     low, high = shifted(sides[1], "node", 1), shifted(sides[0], "node", -1)
+    tiles = [weight] + [swapped(weight, "chan", i) for i in range(1, groups)]
     landing = landing_blocks(shuffle_from, me, blocks, devs, slots)
     incoming = exchanged(outgoing, "node")
-    incoming, packed = lax.optimization_barrier((incoming, packed))
+    incoming, tiles = lax.optimization_barrier((incoming, tiles))
     merged = merge(index, landing, clean, low, high, incoming, groups)
 
-    quarter = row_count // groups
     summed = [merged[0]] + [None] * (groups - 1)
     for i in exchange_order(groups):
         summed[i] = swapped(merged[i], "chan", i)
-    tiles = jnp.stack([piece[quarter:] for piece in packed])
+    tiles = jnp.stack(tiles)
     even = [tiles] + [swapped(tiles, "node", 2 * i) for i in range(1, devs // 2)]
     order = [0, *range(2, groups - 1), 1, groups - 1]
     listed, even = lax.optimization_barrier(([summed[i] for i in order], even))
@@ -490,7 +468,7 @@
     even = jnp.stack(even)
     odd = swapped(even, "node", 1)
 
-    keep, send = weight_partial(index, packed, summed, devs)
+    keep, send = weight_partial(index, feats, summed, devs)
     odd, send = lax.optimization_barrier((odd, send))
     arrived = swapped(send, "node", 1)
     rows_out = feature_rows(index, summed, even, odd)

time: 110 us -> 115 us (1.045)
  waiting for transfers between devices: 41.3 us -> 46.3 us
    all_to_all x1 -> x2, waiting for transfers between devices: 6.38 us -> 10.2 us  [exchanged(): return lax.all_to_all(value, axis, split_axis=0, concat_axis=0, tiled=True)]
    ppermute x4, waiting for transfers between devices: 0.01 us -> 3.7 us  [shifted(): return lax.ppermute(value, axis, pairs)]
    all_to_all x1 -> x2, starting transfers between devices: 6.45 us -> 10.1 us  [exchanged(): return lax.all_to_all(value, axis, split_axis=0, concat_axis=0, tiled=True)]
    ppermute x20, waiting for transfers between devices: 34.9 us -> 32.4 us  [swapped(): return lax.ppermute(value, axis, [(i, i ^ by) for i in range(size)])]
    ppermute x4, starting transfers between devices: 7.39 us -> 5.62 us  [shifted(): return lax.ppermute(value, axis, pairs)]
    ppermute x20, starting transfers between devices: 29.9 us -> 28.7 us  [swapped(): return lax.ppermute(value, axis, [(i, i ^ by) for i in range(size)])]
  transfers between devices with their start and end apart: 25 -> 26, of which waited for: 10 -> 12; matrix products, arithmetic and copies ran while one was open for 1% -> 2% of each run, Pallas kernels for 7% -> 13%
where the time goes in v11:
time: 115 us
  waiting for transfers between devices  46.3 us (40%)
  starting transfers between devices  44.4 us (39%)
  Pallas kernels  18.6 us (16%)
  local copies, waits for them, and re-layouts  2.81 us (2%)
  other arithmetic  1.83 us (2%)
    ppermute x20, waiting for transfers between devices, swapped(): return lax.ppermute(value, axis, [(i, i ^ by) for i in range(size)])  32.4 us
    ppermute x20, starting transfers between devices, swapped(): return lax.ppermute(value, axis, [(i, i ^ by) for i in range(size)])  28.7 us
    all_to_all x2, waiting for transfers between devices, exchanged(): return lax.all_to_all(value, axis, split_axis=0, concat_axis=0, tiled=True)  10.2 us
    all_to_all x2, starting transfers between devices, exchanged(): return lax.all_to_all(value, axis, split_axis=0, concat_axis=0, tiled=True)  10.1 us
    pallas_call x1, Pallas kernels, aggregate(): pl.pallas_call(functools.partial(aggregate_kernel, reach, send_slots), in...  8.09 us
    ppermute x4, starting transfers between devices, shifted(): return lax.ppermute(value, axis, pairs)  5.62 us
    ppermute x4, waiting for transfers between devices, shifted(): return lax.ppermute(value, axis, pairs)  3.7 us
    pallas_call x1, Pallas kernels, feature_rows(): pl.pallas_call(feature_kernel, in_specs=[IN_SMEM] + [IN_VMEM] * (groups +...  3.23 us
  transfers between devices with their start and end apart: 26, of which 12 were waited for; matrix products, arithmetic and copies ran while one was open for 2% of the time, Pallas kernels for 13%

profile of v11, /device:TPU:0, one launch (start us, length us, event | category | flops | bytes accessed | tf_op | source)
XLA Modules:
  0.0 114.8 jit_solution(11433859788361747404)
XLA Ops:
  0.6 6.3 %all-to-all-start = ((bf16[4,448,256]{2,1,0:T(8,128)(2,1)}), bf16[4,448,256]{2,1,0:T(8,128)(2,1)S(1)}, u32[]{:S(2)}, u32[]{:S(2)}) async-start(bf16[4,448,256]{2,1,0:T(8,128)(2,1)} %bitcast.53), calls=%async_computation | async-start | bytes 1835008 | tf_op jit(solution)/shard_map/all_to_all | solution.py:43
  7.0 0.6 pad_add_fusion.me.index
  7.6 8.1 %aggregate.1 = (bf16[14,128,256]{2,1,0:T(8,128)(2,1)}, bf16[16,128,256]{2,1,0:T(8,128)(2,1)}, bf16[2,128,256]{2,1,0:T(8,128)(2,1)}, bf16[2,128,256]{2,1,0:T(8,12...) custom-call(s32[2]{0:T(128)} %pad_add_fusion.me.index, s32[112]{0:T(128)} %shuffle.3, ...), custom_call_target="tpu_custom_call" | custom-call | flops 1174405120 | bytes 7798784 | tf_op jit(solution)/shard_map/aggregate/pallas_call | solution.py:168
  15.7 1.5 %collective-permute-start = (bf16[2,128,256]{2,1,0:T(8,128)(2,1)}, bf16[2,128,256]{2,1,0:T(8,128)(2,1)S(1)}, u32[]{:S(2)}, u32[]{:S(2)}) collective-permute-start(bf16[2,128,256]{2,1,0:T(8,128)(2,1)} %get-tuple-element.37), channel_id=1, source_target_pairs={{0,4},{4,8},{8,12},{12,16},{16,20},{20,24},{24,28},{1,5},{5,9},{9,... | collective-permute-start | bytes 393224 | tf_op jit(solution)/shard_map/ppermute | solution.py:34
  17.1 1.3 %collective-permute-start.1 = (bf16[2,128,256]{2,1,0:T(8,128)(2,1)}, bf16[2,128,256]{2,1,0:T(8,128)(2,1)S(1)}, u32[]{:S(2)}, u32[]{:S(2)}) collective-permute-start(bf16[2,128,256]{2,1,0:T(8,128)(2,1)} %get-tuple-element.38), channel_id=1, source_target_pairs={{4,0},{8,4},{12,8},{16,12},{20,16},{24,20},{28,24},{5,1},{9,5},{13... | collective-permute-start | bytes 393224 | tf_op jit(solution)/shard_map/ppermute | solution.py:34
  18.4 3.7 %collective-permute-done.1.high = bf16[2,128,256]{2,1,0:T(8,128)(2,1)S(1)} collective-permute-done((bf16[2,128,256]{2,1,0:T(8,128)(2,1)}, bf16[2,128,256]{2,1,0:T(8,128)(2,1)S(1)}, u32[]{:S(2)}, u32[]{:S(2)}) %collective-permute-start.1) | collective-permute-done | bytes 131104 | tf_op jit(solution)/shard_map/ppermute | solution.py:34
  22.1 1.2 %copy-done = bf16[16,128,256]{2,1,0:T(8,128)(2,1)S(1)} copy-done((bf16[16,128,256]{2,1,0:T(8,128)(2,1)S(1)}, bf16[16,128,256]{2,1,0:T(8,128)(2,1)}, u32[]{:S(2)}) %copy-start) | copy-done | bytes 1048600
  23.4 1.5 %patch.1 = bf16[16,128,256]{2,1,0:T(8,128)(2,1)S(1)} custom-call(s32[2]{0:T(128)S(1)} %copy-done.3, s32[112]{0:T(128)S(1)} %copy-done.4, bf16[16,128,256]{2,1,0:T(8,128)(2,1)S(1)} %copy-done, bf16[2,128,256]{2,1,0:T(8,128)(2,1)S(1)} %collective-permute-done.low, bf16[2,128,256]{2,1,0:T(8,128)(2,1)S(1)} %collective-permute-done.1.high), custom_call_target="tpu_custom_call", output_to_operand_aliasing={{}: (2, {})} | custom-call | tf_op jit(solution)/shard_map/patch/pallas_call | solution.py:219
  24.9 1.0 copy-done.1
  25.8 4.1 %all-to-all-done.feats = bf16[4,448,256]{2,1,0:T(8,128)(2,1)S(1)} async-done(((bf16[4,448,256]{2,1,0:T(8,128)(2,1)}), bf16[4,448,256]{2,1,0:T(8,128)(2,1)S(1)}, u32[]{:S(2)}, u32[]{:S(2)}) %all-to-all-start) | async-done | bytes 917536 | tf_op jit(solution)/shard_map/all_to_all | solution.py:43
  29.9 3.7 %all-to-all-start.1 = ((bf16[16,128,256]{2,1,0:T(8,128)(2,1)}), bf16[16,128,256]{2,1,0:T(8,128)(2,1)S(1)}, u32[]{:S(2)}, u32[]{:S(2)}) async-start(bf16[16,128,256]{2,1,0:T(8,128)(2,1)} %copy-done.1), calls=%async_computation.1 | async-start | bytes 2097152 | tf_op jit(solution)/shard_map/all_to_all | solution.py:43
  33.6 3.2 %collective-permute-start.6 = (bf16[128,256]{1,0:T(8,128)(2,1)S(1)}, bf16[128,256]{1,0:T(8,128)(2,1)S(1)}, u32[]{:S(2)}, u32[]{:S(2)}) collective-permute-start(bf16[128,256]{1,0:T(8,128)(2,1)S(1)} %copy-done.5), channel_id=1, source_target_pairs={{0,3},{1,2},{2,1},{3,0},{4,7},{5,6},{6,5},{7,4},{8,11},{9,10},{10,... | collective-permute-start | bytes 196616 | tf_op jit(solution)/shard_map/ppermute | solution.py:39
  36.8 0.0 collective-permute-start.5
  36.8 1.2 %collective-permute-start.4 = (bf16[128,256]{1,0:T(8,128)(2,1)S(1)}, bf16[128,256]{1,0:T(8,128)(2,1)S(1)}, u32[]{:S(2)}, u32[]{:S(2)}) collective-permute-start(bf16[128,256]{1,0:T(8,128)(2,1)S(1)} %copy-done.5), channel_id=1, source_target_pairs={{0,1},{1,0},{2,3},{3,2},{4,5},{5,4},{6,7},{7,6},{8,9},{9,8},{10,11... | collective-permute-start | bytes 196616 | tf_op jit(solution)/shard_map/ppermute | solution.py:39
  38.1 0.1 eq.30
  38.2 0.1 add.36
  38.3 0.3 convert_reduce_fusion
  38.6 0.1 copy.14
  38.7 1.6 %collective-permute-start.2 = (bf16[2,128,256]{2,1,0:T(8,128)(2,1)}, bf16[2,128,256]{2,1,0:T(8,128)(2,1)S(1)}, u32[]{:S(2)}, u32[]{:S(2)}) collective-permute-start(bf16[2,128,256]{2,1,0:T(8,128)(2,1)} %get-tuple-element.45), channel_id=1, source_target_pairs={{0,4},{4,8},{8,12},{12,16},{16,20},{20,24},{24,28},{1,5},{5,9},{9,... | collective-permute-start | bytes 393224 | tf_op jit(solution)/shard_map/ppermute | solution.py:34
  40.3 1.3 %collective-permute-start.3 = (bf16[2,128,256]{2,1,0:T(8,128)(2,1)S(1)}, bf16[2,128,256]{2,1,0:T(8,128)(2,1)S(1)}, u32[]{:S(2)}, u32[]{:S(2)}) collective-permute-start(bf16[2,128,256]{2,1,0:T(8,128)(2,1)S(1)} %copy-done.6), channel_id=1, source_target_pairs={{4,0},{8,4},{12,8},{16,12},{20,16},{24,20},{28,24},{5,1},{9,5},{13... | collective-permute-start | bytes 393224 | tf_op jit(solution)/shard_map/ppermute | solution.py:34
  41.6 0.1 select_reduce_fusion
  41.7 0.1 copy.15
  41.8 0.1 sub.13.landing
  41.9 0.0 collective-permute-done.6
  41.9 1.0 collective-permute-done.5
  42.9 6.1 %all-to-all-done.1.incoming = bf16[16,128,256]{2,1,0:T(8,128)(2,1)S(1)} async-done(((bf16[16,128,256]{2,1,0:T(8,128)(2,1)}), bf16[16,128,256]{2,1,0:T(8,128)(2,1)S(1)}, u32[]{:S(2)}, u32[]{:S(2)}) %all-to-all-start.1) | async-done | bytes 1048608 | tf_op jit(solution)/shard_map/all_to_all | solution.py:43
  49.0 0.0 collective-permute-done.2.low
  49.0 0.0 collective-permute-done.3.high
  49.0 1.0 merge.1
  50.1 0.1 slice_bitcast_fusion.4
  50.1 3.2 %collective-permute-start.9 = (bf16[448,256]{1,0:T(8,128)(2,1)S(1)}, bf16[448,256]{1,0:T(8,128)(2,1)S(1)}, u32[]{:S(2)}, u32[]{:S(2)}) collective-permute-start(bf16[448,256]{1,0:T(8,128)(2,1)S(1)} %get-tuple-element.81), channel_id=1, source_target_pairs={{0,3},{1,2},{2,1},{3,0},{4,7},{5,6},{6,5},{7,4},{8,11},{9,10},{10,... | collective-permute-start | bytes 688136 | tf_op jit(solution)/shard_map/ppermute | solution.py:39
  53.4 2.8 %collective-permute-start.12 = (bf16[4,128,256]{2,1,0:T(8,128)(2,1)S(1)}, bf16[4,128,256]{2,1,0:T(8,128)(2,1)S(1)}, u32[]{:S(2)}, u32[]{:S(2)}) collective-permute-start(bf16[4,128,256]{2,1,0:T(8,128)(2,1)S(1)} %pad_maximum_fusion.1), channel_id=1, source_target_pairs={{0,24},{4,28},{8,16},{12,20},{16,8},{20,12},{24,0},{28,4},{1,25},{... | collective-permute-start | bytes 786440 | tf_op jit(solution)/shard_map/ppermute | solution.py:39
  56.3 1.0 collective-permute-start.11
  57.2 1.4 %collective-permute-start.10 = (bf16[4,128,256]{2,1,0:T(8,128)(2,1)S(1)}, bf16[4,128,256]{2,1,0:T(8,128)(2,1)S(1)}, u32[]{:S(2)}, u32[]{:S(2)}) collective-permute-start(bf16[4,128,256]{2,1,0:T(8,128)(2,1)S(1)} %pad_maximum_fusion.1), channel_id=1, source_target_pairs={{0,8},{4,12},{8,0},{12,4},{16,24},{20,28},{24,16},{28,20},{1,9},{5... | collective-permute-start | bytes 786440 | tf_op jit(solution)/shard_map/ppermute | solution.py:39
  58.6 0.0 collective-permute-start.8
  58.6 1.2 %collective-permute-done.9.refs_3_ = bf16[448,256]{1,0:T(8,128)(2,1)S(1)} collective-permute-done((bf16[448,256]{1,0:T(8,128)(2,1)S(1)}, bf16[448,256]{1,0:T(8,128)(2,1)S(1)}, u32[]{:S(2)}, u32[]{:S(2)}) %collective-permute-start.9) | collective-permute-done | bytes 229408 | tf_op jit(solution)/shard_map/ppermute | solution.py:39
  59.8 4.5 %collective-permute-start.7 = (bf16[448,256]{1,0:T(8,128)(2,1)S(1)}, bf16[448,256]{1,0:T(8,128)(2,1)S(1)}, u32[]{:S(2)}, u32[]{:S(2)}) collective-permute-start(bf16[448,256]{1,0:T(8,128)(2,1)S(1)} %get-tuple-element.83), channel_id=1, source_target_pairs={{0,2},{1,3},{2,0},{3,1},{4,6},{5,7},{6,4},{7,5},{8,10},{9,11},{10,... | collective-permute-start | bytes 688136 | tf_op jit(solution)/shard_map/ppermute | solution.py:39
  64.4 1.1 collective-permute-done.8.refs_1_
  65.5 9.7 %collective-permute-done.7.refs_2_ = bf16[448,256]{1,0:T(8,128)(2,1)S(1)} collective-permute-done((bf16[448,256]{1,0:T(8,128)(2,1)S(1)}, bf16[448,256]{1,0:T(8,128)(2,1)S(1)}, u32[]{:S(2)}, u32[]{:S(2)}) %collective-permute-start.7) | collective-permute-done | bytes 229408 | tf_op jit(solution)/shard_map/ppermute | solution.py:39
  75.2 0.0 collective-permute-done.12
  75.2 0.0 collective-permute-done.11
  75.2 0.0 collective-permute-done.10
  75.2 0.1 pad_maximum_fusion.refs_4_
  75.3 0.5 collective-permute-start.13
  75.8 2.6 %weight_partial.1 = (bf16[4,4,128,256]{3,2,1,0:T(8,128)(2,1)S(1)}, bf16[4,4,128,256]{3,2,1,0:T(8,128)(2,1)S(1)}) custom-call(s32[2]{0:T(128)S(1)} %copy-done.3, bf16[4,448,256]{2,1,0:T(8,128)(2,1)S(1)} %all-to-all-done.feats, bf16[448,256]{1,0:T(8,128)(2,1)S(1)} %get-tuple-element.54.refs_0_, bf16[448,256]{1,0:T(8,128)(2,1)S(1)} %collective-permute-done.8.refs_1_, ...), custom_call_target="tpu_custom_call" | custom-call | flops 939524096 | bytes 3932160 | tf_op jit(solution)/shard_map/weight_partial/pallas_call | solution.py:306
  78.5 0.2 collective-permute-start.14
  78.6 3.2 %feature_rows.1 = bf16[4,448,256]{2,1,0:T(8,128)(2,1)S(1)} custom-call(s32[2]{0:T(128)S(1)} %copy-done.3, bf16[448,256]{1,0:T(8,128)(2,1)S(1)} %get-tuple-element.54.refs_0_, bf16[448,256]{1,0:T(8,128)(2,1)S(1)} %collective-permute-done.8.refs_1_, bf16[448,256]{1,0:T(8,128)(2,1)S(1)} %collective-permute-done.7.refs_2_, ...), custom_call_target="tpu_custom_call" | custom-call | flops 939524096 | bytes 3932160 | tf_op jit(solution)/shard_map/feature_rows/pallas_call | solution.py:354
  81.9 0.0 collective-permute-done.14
  81.9 0.4 convert_add_fusion
  82.3 0.1 slice_bitcast_fusion.3
  82.3 3.1 %collective-permute-start.15 = (bf16[4,128,256]{2,1,0:T(8,128)(2,1)S(1)}, bf16[4,128,256]{2,1,0:T(8,128)(2,1)S(1)}, u32[]{:S(2)}, u32[]{:S(2)}) collective-permute-start(bf16[4,128,256]{2,1,0:T(8,128)(2,1)S(1)} %get-tuple-element.74), channel_id=1, source_target_pairs={{0,8},{4,12},{8,0},{12,4},{16,24},{20,28},{24,16},{28,20},{1,9},{5... | collective-permute-start | bytes 786440 | tf_op jit(solution)/shard_map/ppermute | solution.py:39
  85.5 0.0 collective-permute-start.17
  85.5 1.5 %collective-permute-start.16 = (bf16[4,128,256]{2,1,0:T(8,128)(2,1)S(1)}, bf16[4,128,256]{2,1,0:T(8,128)(2,1)S(1)}, u32[]{:S(2)}, u32[]{:S(2)}) collective-permute-start(bf16[4,128,256]{2,1,0:T(8,128)(2,1)S(1)} %get-tuple-element.76), channel_id=1, source_target_pairs={{0,16},{4,20},{8,24},{12,28},{16,0},{20,4},{24,8},{28,12},{1,17},{... | collective-permute-start | bytes 786440 | tf_op jit(solution)/shard_map/ppermute | solution.py:39
  87.0 0.1 slice_bitcast_fusion.8
  87.1 1.6 %collective-permute-start.20 = (bf16[448,256]{1,0:T(8,128)(2,1)S(1)}, bf16[448,256]{1,0:T(8,128)(2,1)S(1)}, u32[]{:S(2)}, u32[]{:S(2)}) collective-permute-start(bf16[448,256]{1,0:T(8,128)(2,1)S(1)} %get-tuple-element.77), channel_id=1, source_target_pairs={{0,3},{1,2},{2,1},{3,0},{4,7},{5,6},{6,5},{7,4},{8,11},{9,10},{10,... | collective-permute-start | bytes 688136 | tf_op jit(solution)/shard_map/ppermute | solution.py:39
  88.6 3.9 %collective-permute-done.15 = bf16[4,128,256]{2,1,0:T(8,128)(2,1)S(1)} collective-permute-done((bf16[4,128,256]{2,1,0:T(8,128)(2,1)S(1)}, bf16[4,128,256]{2,1,0:T(8,128)(2,1)S(1)}, u32[]{:S(2)}, u32[]{:S(2)}) %collective-permute-start.15) | collective-permute-done | bytes 262176 | tf_op jit(solution)/shard_map/ppermute | solution.py:39
  92.6 4.3 %collective-permute-done.17 = bf16[4,128,256]{2,1,0:T(8,128)(2,1)S(1)} collective-permute-done((bf16[4,128,256]{2,1,0:T(8,128)(2,1)S(1)}, bf16[4,128,256]{2,1,0:T(8,128)(2,1)S(1)}, u32[]{:S(2)}, u32[]{:S(2)}) %collective-permute-start.17) | collective-permute-done | bytes 262176 | tf_op jit(solution)/shard_map/ppermute | solution.py:39
  96.9 2.2 %collective-permute-done.16 = bf16[4,128,256]{2,1,0:T(8,128)(2,1)S(1)} collective-permute-done((bf16[4,128,256]{2,1,0:T(8,128)(2,1)S(1)}, bf16[4,128,256]{2,1,0:T(8,128)(2,1)S(1)}, u32[]{:S(2)}, u32[]{:S(2)}) %collective-permute-start.16) | collective-permute-done | bytes 262176 | tf_op jit(solution)/shard_map/ppermute | solution.py:39
  99.1 0.2 fusion.7
  99.2 1.6 %collective-permute-start.23 = (bf16[128,256]{1,0:T(8,128)(2,1)S(1)}, bf16[128,256]{1,0:T(8,128)(2,1)S(1)}, u32[]{:S(2)}, u32[]{:S(2)}) collective-permute-start(bf16[128,256]{1,0:T(8,128)(2,1)S(1)} %get-tuple-element.85), channel_id=1, source_target_pairs={{0,3},{1,2},{2,1},{3,0},{4,7},{5,6},{6,5},{7,4},{8,11},{9,10},{10,... | collective-permute-start | bytes 196616 | tf_op jit(solution)/shard_map/ppermute | solution.py:39
  100.8 2.9 %collective-permute-start.21 = (bf16[128,256]{1,0:T(8,128)(2,1)S(1)}, bf16[128,256]{1,0:T(8,128)(2,1)S(1)}, u32[]{:S(2)}, u32[]{:S(2)}) collective-permute-start(bf16[128,256]{1,0:T(8,128)(2,1)S(1)} %get-tuple-element.87), channel_id=1, source_target_pairs={{0,1},{1,0},{2,3},{3,2},{4,5},{5,4},{6,7},{7,6},{8,9},{9,8},{10,11... | collective-permute-start | bytes 196616 | tf_op jit(solution)/shard_map/ppermute | solution.py:39
  103.7 7.2 %collective-permute-done.19.refs_2_ = bf16[448,256]{1,0:T(8,128)(2,1)S(1)} collective-permute-done((bf16[448,256]{1,0:T(8,128)(2,1)S(1)}, bf16[448,256]{1,0:T(8,128)(2,1)S(1)}, u32[]{:S(2)}, u32[]{:S(2)}) %collective-permute-start.19) | collective-permute-done | bytes 229408 | tf_op jit(solution)/shard_map/ppermute | solution.py:39
  110.9 1.7 %collective-permute-done.22.refs_5_ = bf16[128,256]{1,0:T(8,128)(2,1)S(1)} collective-permute-done((bf16[128,256]{1,0:T(8,128)(2,1)S(1)}, bf16[128,256]{1,0:T(8,128)(2,1)S(1)}, u32[]{:S(2)}, u32[]{:S(2)}) %collective-permute-start.22) | collective-permute-done | bytes 65568 | tf_op jit(solution)/shard_map/ppermute | solution.py:39
  112.7 2.1 %finish.1 = (bf16[1792,256]{1,0:T(8,128)(2,1)}, f32[128,256]{1,0:T(8,128)}) custom-call(s32[2]{0:T(128)S(1)} %copy-done.3, f32[128,256]{1,0:T(8,128)S(1)} %slice_bitcast_fusion.12.share, bf16[448,256]{1,0:T(8,128)(2,1)S(1)} %get-tuple-element.80.refs_0_, bf16[448,256]{1,0:T(8,128)(2,1)S(1)} %collective-permute-done.18.refs_1_, ...), custom_call_target="tpu_custom_call" | custom-call | tf_op jit(solution)/shard_map/finish/pallas_call | solution.py:392
  (29 shorter events, 0.2 us)
Async XLA Ops:
  0.6 29.2 %all-to-all-start = ((bf16[4,448,256]{2,1,0:T(8,128)(2,1)}), bf16[4,448,256]{2,1,0:T(8,128)(2,1)S(1)}, u32[]{:S(2)}, u32[]{:S(2)}) async-start(bf16[4,448,256]{2,1,0:T(8,128)(2,1)} %bitcast.53), calls=%async_computation | async-start | bytes 1835008 | tf_op jit(solution)/shard_map/all_to_all | solution.py:43
  7.6 14.6 %copy-start.3 = (s32[2]{0:T(128)S(1)}, s32[2]{0:T(128)}, u32[]{:S(2)}) copy-start(s32[2]{0:T(128)} %pad_add_fusion.me.index) | copy-start | bytes 28
  7.6 14.6 %copy-start.4 = (s32[112]{0:T(128)S(1)}, s32[112]{0:T(128)}, u32[]{:S(2)}) copy-start(s32[112]{0:T(128)} %shuffle.3) | copy-start | bytes 1348
  15.7 2.8 %collective-permute-start = (bf16[2,128,256]{2,1,0:T(8,128)(2,1)}, bf16[2,128,256]{2,1,0:T(8,128)(2,1)S(1)}, u32[]{:S(2)}, u32[]{:S(2)}) collective-permute-start(bf16[2,128,256]{2,1,0:T(8,128)(2,1)} %get-tuple-element.37), channel_id=1, source_target_pairs={{0,4},{4,8},{8,12},{12,16},{16,20},{20,24},{24,28},{1,5},{5,9},{9,... | collective-permute-start | bytes 393224 | tf_op jit(solution)/shard_map/ppermute | solution.py:34
  17.1 5.0 %collective-permute-start.1 = (bf16[2,128,256]{2,1,0:T(8,128)(2,1)}, bf16[2,128,256]{2,1,0:T(8,128)(2,1)S(1)}, u32[]{:S(2)}, u32[]{:S(2)}) collective-permute-start(bf16[2,128,256]{2,1,0:T(8,128)(2,1)} %get-tuple-element.38), channel_id=1, source_target_pairs={{4,0},{8,4},{12,8},{16,12},{20,16},{24,20},{28,24},{5,1},{9,5},{13... | collective-permute-start | bytes 393224 | tf_op jit(solution)/shard_map/ppermute | solution.py:34
  22.1 1.2 %copy-start = (bf16[16,128,256]{2,1,0:T(8,128)(2,1)S(1)}, bf16[16,128,256]{2,1,0:T(8,128)(2,1)}, u32[]{:S(2)}) copy-start(bf16[16,128,256]{2,1,0:T(8,128)(2,1)} %get-tuple-element.36.outgoing) | copy-start | bytes 3145732
  23.4 10.2 %copy-start.5 = (bf16[128,256]{1,0:T(8,128)(2,1)S(1)}, bf16[128,256]{1,0:T(8,128)(2,1)}, u32[]{:S(2)}) copy-start(bf16[128,256]{1,0:T(8,128)(2,1)} %param.12) | copy-start | bytes 196612
  23.4 16.9 %copy-start.6 = (bf16[2,128,256]{2,1,0:T(8,128)(2,1)S(1)}, bf16[2,128,256]{2,1,0:T(8,128)(2,1)}, u32[]{:S(2)}) copy-start(bf16[2,128,256]{2,1,0:T(8,128)(2,1)} %get-tuple-element.46) | copy-start | bytes 393220
  23.4 25.7 %copy-start.2 = (bf16[14,128,256]{2,1,0:T(8,128)(2,1)S(1)}, bf16[14,128,256]{2,1,0:T(8,128)(2,1)}, u32[]{:S(2)}) copy-start(bf16[14,128,256]{2,1,0:T(8,128)(2,1)} %get-tuple-element.44.clean) | copy-start | bytes 2752516
  24.8 1.0 copy-start.1
  29.9 19.1 %all-to-all-start.1 = ((bf16[16,128,256]{2,1,0:T(8,128)(2,1)}), bf16[16,128,256]{2,1,0:T(8,128)(2,1)S(1)}, u32[]{:S(2)}, u32[]{:S(2)}) async-start(bf16[16,128,256]{2,1,0:T(8,128)(2,1)} %copy-done.1), calls=%async_computation.1 | async-start | bytes 2097152 | tf_op jit(solution)/shard_map/all_to_all | solution.py:43
  33.6 8.3 %collective-permute-start.6 = (bf16[128,256]{1,0:T(8,128)(2,1)S(1)}, bf16[128,256]{1,0:T(8,128)(2,1)S(1)}, u32[]{:S(2)}, u32[]{:S(2)}) collective-permute-start(bf16[128,256]{1,0:T(8,128)(2,1)S(1)} %copy-done.5), channel_id=1, source_target_pairs={{0,3},{1,2},{2,1},{3,0},{4,7},{5,6},{6,5},{7,4},{8,11},{9,10},{10,... | collective-permute-start | bytes 196616 | tf_op jit(solution)/shard_map/ppermute | solution.py:39
  36.8 6.1 %collective-permute-start.5 = (bf16[128,256]{1,0:T(8,128)(2,1)S(1)}, bf16[128,256]{1,0:T(8,128)(2,1)S(1)}, u32[]{:S(2)}, u32[]{:S(2)}) collective-permute-start(bf16[128,256]{1,0:T(8,128)(2,1)S(1)} %copy-done.5), channel_id=1, source_target_pairs={{0,2},{1,3},{2,0},{3,1},{4,6},{5,7},{6,4},{7,5},{8,10},{9,11},{10,... | collective-permute-start | bytes 196616 | tf_op jit(solution)/shard_map/ppermute | solution.py:39
  36.8 6.1 %collective-permute-start.4 = (bf16[128,256]{1,0:T(8,128)(2,1)S(1)}, bf16[128,256]{1,0:T(8,128)(2,1)S(1)}, u32[]{:S(2)}, u32[]{:S(2)}) collective-permute-start(bf16[128,256]{1,0:T(8,128)(2,1)S(1)} %copy-done.5), channel_id=1, source_target_pairs={{0,1},{1,0},{2,3},{3,2},{4,5},{5,4},{6,7},{7,6},{8,9},{9,8},{10,11... | collective-permute-start | bytes 196616 | tf_op jit(solution)/shard_map/ppermute | solution.py:39
  38.7 10.3 %collective-permute-start.2 = (bf16[2,128,256]{2,1,0:T(8,128)(2,1)}, bf16[2,128,256]{2,1,0:T(8,128)(2,1)S(1)}, u32[]{:S(2)}, u32[]{:S(2)}) collective-permute-start(bf16[2,128,256]{2,1,0:T(8,128)(2,1)} %get-tuple-element.45), channel_id=1, source_target_pairs={{0,4},{4,8},{8,12},{12,16},{16,20},{20,24},{24,28},{1,5},{5,9},{9,... | collective-permute-start | bytes 393224 | tf_op jit(solution)/shard_map/ppermute | solution.py:34
  40.3 8.7 %collective-permute-start.3 = (bf16[2,128,256]{2,1,0:T(8,128)(2,1)S(1)}, bf16[2,128,256]{2,1,0:T(8,128)(2,1)S(1)}, u32[]{:S(2)}, u32[]{:S(2)}) collective-permute-start(bf16[2,128,256]{2,1,0:T(8,128)(2,1)S(1)} %copy-done.6), channel_id=1, source_target_pairs={{4,0},{8,4},{12,8},{16,12},{20,16},{24,20},{28,24},{5,1},{9,5},{13... | collective-permute-start | bytes 393224 | tf_op jit(solution)/shard_map/ppermute | solution.py:34
  50.1 9.7 %collective-permute-start.9 = (bf16[448,256]{1,0:T(8,128)(2,1)S(1)}, bf16[448,256]{1,0:T(8,128)(2,1)S(1)}, u32[]{:S(2)}, u32[]{:S(2)}) collective-permute-start(bf16[448,256]{1,0:T(8,128)(2,1)S(1)} %get-tuple-element.81), channel_id=1, source_target_pairs={{0,3},{1,2},{2,1},{3,0},{4,7},{5,6},{6,5},{7,4},{8,11},{9,10},{10,... | collective-permute-start | bytes 688136 | tf_op jit(solution)/shard_map/ppermute | solution.py:39
  53.4 21.8 %collective-permute-start.12 = (bf16[4,128,256]{2,1,0:T(8,128)(2,1)S(1)}, bf16[4,128,256]{2,1,0:T(8,128)(2,1)S(1)}, u32[]{:S(2)}, u32[]{:S(2)}) collective-permute-start(bf16[4,128,256]{2,1,0:T(8,128)(2,1)S(1)} %pad_maximum_fusion.1), channel_id=1, source_target_pairs={{0,24},{4,28},{8,16},{12,20},{16,8},{20,12},{24,0},{28,4},{1,25},{... | collective-permute-start | bytes 786440 | tf_op jit(solution)/shard_map/ppermute | solution.py:39
  56.3 18.9 %collective-permute-start.11 = (bf16[4,128,256]{2,1,0:T(8,128)(2,1)S(1)}, bf16[4,128,256]{2,1,0:T(8,128)(2,1)S(1)}, u32[]{:S(2)}, u32[]{:S(2)}) collective-permute-start(bf16[4,128,256]{2,1,0:T(8,128)(2,1)S(1)} %pad_maximum_fusion.1), channel_id=1, source_target_pairs={{0,16},{4,20},{8,24},{12,28},{16,0},{20,4},{24,8},{28,12},{1,17},{... | collective-permute-start | bytes 786440 | tf_op jit(solution)/shard_map/ppermute | solution.py:39
  57.2 18.0 %collective-permute-start.10 = (bf16[4,128,256]{2,1,0:T(8,128)(2,1)S(1)}, bf16[4,128,256]{2,1,0:T(8,128)(2,1)S(1)}, u32[]{:S(2)}, u32[]{:S(2)}) collective-permute-start(bf16[4,128,256]{2,1,0:T(8,128)(2,1)S(1)} %pad_maximum_fusion.1), channel_id=1, source_target_pairs={{0,8},{4,12},{8,0},{12,4},{16,24},{20,28},{24,16},{28,20},{1,9},{5... | collective-permute-start | bytes 786440 | tf_op jit(solution)/shard_map/ppermute | solution.py:39
  58.6 6.9 %collective-permute-start.8 = (bf16[448,256]{1,0:T(8,128)(2,1)S(1)}, bf16[448,256]{1,0:T(8,128)(2,1)S(1)}, u32[]{:S(2)}, u32[]{:S(2)}) collective-permute-start(bf16[448,256]{1,0:T(8,128)(2,1)S(1)} %get-tuple-element.82), channel_id=1, source_target_pairs={{0,1},{1,0},{2,3},{3,2},{4,5},{5,4},{6,7},{7,6},{8,9},{9,8},{10,11... | collective-permute-start | bytes 688136 | tf_op jit(solution)/shard_map/ppermute | solution.py:39
  59.8 15.3 %collective-permute-start.7 = (bf16[448,256]{1,0:T(8,128)(2,1)S(1)}, bf16[448,256]{1,0:T(8,128)(2,1)S(1)}, u32[]{:S(2)}, u32[]{:S(2)}) collective-permute-start(bf16[448,256]{1,0:T(8,128)(2,1)S(1)} %get-tuple-element.83), channel_id=1, source_target_pairs={{0,2},{1,3},{2,0},{3,1},{4,6},{5,7},{6,4},{7,5},{8,10},{9,11},{10,... | collective-permute-start | bytes 688136 | tf_op jit(solution)/shard_map/ppermute | solution.py:39
  75.3 3.1 %collective-permute-start.13 = (bf16[4,4,128,256]{3,2,1,0:T(8,128)(2,1)S(1)}, bf16[4,4,128,256]{3,2,1,0:T(8,128)(2,1)S(1)}, u32[]{:S(2)}, u32[]{:S(2)}) collective-permute-start(bf16[4,4,128,256]{3,2,1,0:T(8,128)(2,1)S(1)} %pad_maximum_fusion.refs_4_), channel_id=1, source_target_pairs={{0,4},{4,0},{8,12},{12,8},{16,20},{20,16},{24,28},{28,24},{1,5},{5... | collective-permute-start | bytes 3145736 | tf_op jit(solution)/shard_map/ppermute | solution.py:39
  78.5 3.4 %collective-permute-start.14 = (bf16[4,4,128,256]{3,2,1,0:T(8,128)(2,1)S(1)}, bf16[4,4,128,256]{3,2,1,0:T(8,128)(2,1)S(1)}, u32[]{:S(2)}, u32[]{:S(2)}) collective-permute-start(bf16[4,4,128,256]{3,2,1,0:T(8,128)(2,1)S(1)} %get-tuple-element.64), channel_id=1, source_target_pairs={{0,4},{4,0},{8,12},{12,8},{16,20},{20,16},{24,28},{28,24},{1,5},{5... | collective-permute-start | bytes 3145736 | tf_op jit(solution)/shard_map/ppermute | solution.py:39
  82.3 10.2 %collective-permute-start.15 = (bf16[4,128,256]{2,1,0:T(8,128)(2,1)S(1)}, bf16[4,128,256]{2,1,0:T(8,128)(2,1)S(1)}, u32[]{:S(2)}, u32[]{:S(2)}) collective-permute-start(bf16[4,128,256]{2,1,0:T(8,128)(2,1)S(1)} %get-tuple-element.74), channel_id=1, source_target_pairs={{0,8},{4,12},{8,0},{12,4},{16,24},{20,28},{24,16},{28,20},{1,9},{5... | collective-permute-start | bytes 786440 | tf_op jit(solution)/shard_map/ppermute | solution.py:39
  85.5 11.4 %collective-permute-start.17 = (bf16[4,128,256]{2,1,0:T(8,128)(2,1)S(1)}, bf16[4,128,256]{2,1,0:T(8,128)(2,1)S(1)}, u32[]{:S(2)}, u32[]{:S(2)}) collective-permute-start(bf16[4,128,256]{2,1,0:T(8,128)(2,1)S(1)} %get-tuple-element.75), channel_id=1, source_target_pairs={{0,24},{4,28},{8,16},{12,20},{16,8},{20,12},{24,0},{28,4},{1,25},{... | collective-permute-start | bytes 786440 | tf_op jit(solution)/shard_map/ppermute | solution.py:39
  85.5 13.6 %collective-permute-start.16 = (bf16[4,128,256]{2,1,0:T(8,128)(2,1)S(1)}, bf16[4,128,256]{2,1,0:T(8,128)(2,1)S(1)}, u32[]{:S(2)}, u32[]{:S(2)}) collective-permute-start(bf16[4,128,256]{2,1,0:T(8,128)(2,1)S(1)} %get-tuple-element.76), channel_id=1, source_target_pairs={{0,16},{4,20},{8,24},{12,28},{16,0},{20,4},{24,8},{28,12},{1,17},{... | collective-permute-start | bytes 786440 | tf_op jit(solution)/shard_map/ppermute | solution.py:39
  87.1 13.7 %collective-permute-start.20 = (bf16[448,256]{1,0:T(8,128)(2,1)S(1)}, bf16[448,256]{1,0:T(8,128)(2,1)S(1)}, u32[]{:S(2)}, u32[]{:S(2)}) collective-permute-start(bf16[448,256]{1,0:T(8,128)(2,1)S(1)} %get-tuple-element.77), channel_id=1, source_target_pairs={{0,3},{1,2},{2,1},{3,0},{4,7},{5,6},{6,5},{7,4},{8,11},{9,10},{10,... | collective-permute-start | bytes 688136 | tf_op jit(solution)/shard_map/ppermute | solution.py:39
  88.6 22.3 %collective-permute-start.19 = (bf16[448,256]{1,0:T(8,128)(2,1)S(1)}, bf16[448,256]{1,0:T(8,128)(2,1)S(1)}, u32[]{:S(2)}, u32[]{:S(2)}) collective-permute-start(bf16[448,256]{1,0:T(8,128)(2,1)S(1)} %get-tuple-element.78), channel_id=1, source_target_pairs={{0,2},{1,3},{2,0},{3,1},{4,6},{5,7},{6,4},{7,5},{8,10},{9,11},{10,... | collective-permute-start | bytes 688136 | tf_op jit(solution)/shard_map/ppermute | solution.py:39
  92.6 18.3 %collective-permute-start.18 = (bf16[448,256]{1,0:T(8,128)(2,1)S(1)}, bf16[448,256]{1,0:T(8,128)(2,1)S(1)}, u32[]{:S(2)}, u32[]{:S(2)}) collective-permute-start(bf16[448,256]{1,0:T(8,128)(2,1)S(1)} %get-tuple-element.79), channel_id=1, source_target_pairs={{0,1},{1,0},{2,3},{3,2},{4,5},{5,4},{6,7},{7,6},{8,9},{9,8},{10,11... | collective-permute-start | bytes 688136 | tf_op jit(solution)/shard_map/ppermute | solution.py:39
  99.2 11.7 %collective-permute-start.23 = (bf16[128,256]{1,0:T(8,128)(2,1)S(1)}, bf16[128,256]{1,0:T(8,128)(2,1)S(1)}, u32[]{:S(2)}, u32[]{:S(2)}) collective-permute-start(bf16[128,256]{1,0:T(8,128)(2,1)S(1)} %get-tuple-element.85), channel_id=1, source_target_pairs={{0,3},{1,2},{2,1},{3,0},{4,7},{5,6},{6,5},{7,4},{8,11},{9,10},{10,... | collective-permute-start | bytes 196616 | tf_op jit(solution)/shard_map/ppermute | solution.py:39
  100.8 11.8 %collective-permute-start.22 = (bf16[128,256]{1,0:T(8,128)(2,1)S(1)}, bf16[128,256]{1,0:T(8,128)(2,1)S(1)}, u32[]{:S(2)}, u32[]{:S(2)}) collective-permute-start(bf16[128,256]{1,0:T(8,128)(2,1)S(1)} %get-tuple-element.86), channel_id=1, source_target_pairs={{0,2},{1,3},{2,0},{3,1},{4,6},{5,7},{6,4},{7,5},{8,10},{9,11},{10,... | collective-permute-start | bytes 196616 | tf_op jit(solution)/shard_map/ppermute | solution.py:39
  100.8 11.8 %collective-permute-start.21 = (bf16[128,256]{1,0:T(8,128)(2,1)S(1)}, bf16[128,256]{1,0:T(8,128)(2,1)S(1)}, u32[]{:S(2)}, u32[]{:S(2)}) collective-permute-start(bf16[128,256]{1,0:T(8,128)(2,1)S(1)} %get-tuple-element.87), channel_id=1, source_target_pairs={{0,1},{1,0},{2,3},{3,2},{4,5},{5,4},{6,7},{7,6},{8,9},{9,8},{10,11... | collective-permute-start | bytes 196616 | tf_op jit(solution)/shard_map/ppermute | solution.py:39

commit v12 on v10

--- a/solution.py
+++ b/solution.py
@@ -10,7 +10,6 @@
 
 VMEM_LIMIT = 32 * 1024 * 1024
 VMEM_ALL = 61 * 1024 * 1024
-VMEM_MOST = 52 * 1024 * 1024
 IN_VMEM = pl.BlockSpec(memory_space=pltpu.VMEM)
 IN_SMEM = pl.BlockSpec(memory_space=pltpu.SMEM)
 IN_HBM = pl.BlockSpec(memory_space=pltpu.HBM)
@@ -213,7 +212,14 @@
     )(index, shuffle, cols, count, gc, pc, gx, px, slopes, adj, features, weight)
 
 
-def patch_kernel(reach, blocks, slots, index, shuffle, outgoing, low, high, out, held, ready, places, used, sems):
+def patch_kernel(reach, blocks, slots, index, shuffle, outgoing, low, high, out, *scratch):
+    held, other, ready, places, used, sems = scratch
+    arrivals = [
+        pltpu.make_async_copy(side, other.at[i * reach : (i + 1) * reach], sems.at[2, i])
+        for i, side in enumerate((low, high))
+    ]
+    for copy in arrivals:
+        copy.start()
     find_places(index, shuffle, blocks, slots, places, used)
     border = [*range(reach), *range(blocks - reach, blocks)]
     reads, writes = [], []
@@ -223,10 +229,11 @@
         writes.append(pltpu.make_async_copy(ready.at[i], out.at[place], sems.at[1, i]))
     for copy in reads:
         copy.start()
+    for copy in arrivals:
+        copy.wait()
     for i, (read, write) in enumerate(zip(reads, writes)):
         read.wait()
-        other = low[i] if i < reach else high[i - reach]
-        ready[i] = (wide(held[i]) + wide(other)).astype(jnp.bfloat16)
+        ready[i] = (wide(held[i]) + wide(other[i])).astype(jnp.bfloat16)
         write.start()
     for copy in writes:
         copy.wait()
@@ -238,18 +245,19 @@
     border = pltpu.VMEM((2 * reach, rows, width), jnp.bfloat16)
     return pl.pallas_call(
         functools.partial(patch_kernel, reach, blocks, slots),
-        in_specs=[IN_SMEM] * 2 + [IN_HBM] + [IN_VMEM] * 2,
+        in_specs=[IN_SMEM] * 2 + [IN_HBM] * 3,
         out_specs=IN_HBM,
         out_shape=bf16(*outgoing.shape),
         input_output_aliases={2: 0},
         scratch_shapes=[
             border,
             border,
+            border,
             pltpu.SMEM((blocks,), jnp.int32),
             pltpu.SMEM((sent // slots,), jnp.int32),
-            pltpu.SemaphoreType.DMA((2, 2 * reach)),
+            pltpu.SemaphoreType.DMA((3, 2 * reach)),
         ],
-        compiler_params=params(VMEM_MOST),
+        compiler_params=params(VMEM_ALL),
         name="patch",
     )(index, shuffle, outgoing, low, high)
 
@@ -338,7 +346,7 @@
     )(index, *packed, *summed)
 
 
-def feature_kernel(index, *refs):
+def feature_kernel(first, index, *refs):
     *summed, even, odd, out = refs
     groups = len(summed)
     devs = 2 * even.shape[0]
@@ -347,7 +355,7 @@
     height = even.shape[2]
     low = me & (shares - 1)
     lhs = jnp.concatenate([piece[...] for piece in summed], axis=1)
-    for relative in range(groups):
+    for relative in range(first, first + out.shape[0]):
         rows = []
         for i in range(shares):
             node = (((group ^ relative) * shares) ^ (me - low)) + i
@@ -362,34 +370,32 @@
         parts = [product[:, i * height : (i + 1) * height] for i in range(shares)]
 
         def store(flip):
-            out[relative] = jnp.concatenate([parts[i ^ flip] for i in range(shares)], axis=1)
+            out[relative - first] = jnp.concatenate([parts[i ^ flip] for i in range(shares)], axis=1)
 
         for flip in range(shares):
             pl.when(low == flip)(functools.partial(store, flip))
 
 
-def feature_rows(index, summed, even, odd):
+def feature_rows(index, summed, even, odd, first, count):
     groups = len(summed)
     rows, width = summed[0].shape
     return pl.pallas_call(
-        feature_kernel,
+        functools.partial(feature_kernel, first),
         in_specs=[IN_SMEM] + [IN_VMEM] * (groups + 2),
         out_specs=IN_VMEM,
-        out_shape=bf16(groups, rows, width),
+        out_shape=bf16(count, rows, width),
         compiler_params=params(),
         cost_estimate=pl.CostEstimate(
-            flops=2 * rows * (groups * width) ** 2,
-            bytes_accessed=2 * (groups * width) ** 2 + 4 * groups * rows * width,
+            flops=2 * rows * groups * count * width**2,
+            bytes_accessed=2 * groups * count * width**2 + 2 * (groups + count) * rows * width,
             transcendentals=0,
         ),
         name="feature_rows",
     )(index, *summed, even, odd)
 
 
-def finish_kernel(index, share, *refs):
-    *refs, out, total, sems = refs
-    groups = (len(refs) + 1) // 2
-    pieces, others = refs[:groups], refs[groups:]
+def gather_kernel(index, *refs):
+    *pieces, out, sems = refs
     rows = pieces[0].shape[0]
     copies = [
         pltpu.make_async_copy(
@@ -399,28 +405,21 @@
     ]
     for copy in copies:
         copy.start()
-    sum_of = share[...]
-    for other in others:
-        sum_of = sum_of + wide(other[...])
-    total[...] = sum_of
     for copy in copies:
         copy.wait()
 
 
-def finish(index, pieces, share, others):
+def laid_out(index, pieces):
     rows, width = pieces[0].shape
     return pl.pallas_call(
-        finish_kernel,
-        in_specs=[IN_SMEM] + [IN_VMEM] * (2 * len(pieces)),
-        out_specs=[IN_HBM, IN_VMEM],
-        out_shape=[
-            bf16(len(pieces) * rows, width),
-            jax.ShapeDtypeStruct(share.shape, jnp.float32),
-        ],
+        gather_kernel,
+        in_specs=[IN_SMEM] + [IN_VMEM] * len(pieces),
+        out_specs=IN_HBM,
+        out_shape=bf16(len(pieces) * rows, width),
         scratch_shapes=[pltpu.SemaphoreType.DMA((len(pieces),))],
         compiler_params=params(),
-        name="finish",
-    )(index, share, *pieces, *others)
+        name="laid_out",
+    )(index, *pieces)
 
 
 def landing_blocks(shuffle_from, me, blocks, devs, slots):
@@ -493,19 +492,19 @@
     keep, send = weight_partial(index, packed, summed, devs)
     odd, send = lax.optimization_barrier((odd, send))
     arrived = swapped(send, "node", 1)
-    rows_out = feature_rows(index, summed, even, odd)
-    arrived, rows_out = lax.optimization_barrier((arrived, rows_out))
-
-    pieces = [rows_out[0]] + [None] * (groups - 1)
+    sent = feature_rows(index, summed, even, odd, 1, groups - 1)
+    arrived, sent, summed, even, odd = lax.optimization_barrier((arrived, sent, summed, even, odd))
+    pieces = [feature_rows(index, summed, even, odd, 0, 1)[0]] + [None] * (groups - 1)
     for i in exchange_order(groups):
-        pieces[i] = swapped(rows_out[i], "chan", i)
+        pieces[i] = swapped(sent[i - 1], "chan", i)
     total = wide(keep) + wide(arrived)
     share = total[0]
     for i in range(1, devs // 2):
         share = share + wide(swapped(total[i].astype(jnp.bfloat16), "node", 2 * i))
-    others = [swapped(share[i].astype(jnp.bfloat16), "chan", i) for i in range(1, groups)]
-    grad_features, grad_weight = finish(index, pieces, share[0], others)
-    return (grad_weight, grad_features)
+    grad_weight = share[0]
+    for i in range(1, groups):
+        grad_weight = grad_weight + wide(swapped(share[i].astype(jnp.bfloat16), "chan", i))
+    return (grad_weight, laid_out(index, pieces))
 
 
 def solution(mesh):

time: 110 us -> 108 us (0.982)
  waiting for transfers between devices: 41.3 us -> 38.2 us
  local copies, waits for them, and re-layouts: 2.84 us -> 1.32 us
  starting transfers between devices: 43.7 us -> 45 us
    ppermute x20, waiting for transfers between devices: 34.9 us -> 32.1 us  [swapped(): return lax.ppermute(value, axis, [(i, i ^ by) for i in range(size)])]
    unnamed x16, local copies, waits for them, and re-layouts: 2.21 us -> 0.72 us
    ppermute x20, starting transfers between devices: 29.9 us -> 31.1 us  [swapped(): return lax.ppermute(value, axis, [(i, i ^ by) for i in range(size)])]
    pallas_call x1, Pallas kernels: 1.46 us -> 2.62 us  [patch(): pl.pallas_call(functools.partial(patch_kernel, reach, blocks, slots), in_...]
    pallas_call x2 -> x3, Pallas kernels: 5.37 us -> 4.83 us  [the longest x2 3.34 us: feature_rows(): pl.pallas_call(functools.partial(feature_kernel, first), in_specs=[IN_SME...]
  transfers between devices with their start and end apart: 25 -> 25, of which waited for: 10 -> 10; matrix products, arithmetic and copies ran while one was open for 1% -> 1% of each run, Pallas kernels for 7% -> 9%
where the time goes in v12:
time: 108 us; the launch traced here: 107 us
  starting transfers between devices  45 us (42%)
  waiting for transfers between devices  38.2 us (35%)
  Pallas kernels  19.3 us (18%)
  other arithmetic  2.5 us (2%)
  local copies, waits for them, and re-layouts  1.32 us (1%)
    ppermute x20, waiting for transfers between devices, swapped(): return lax.ppermute(value, axis, [(i, i ^ by) for i in range(size)])  32.1 us
    ppermute x20, starting transfers between devices, swapped(): return lax.ppermute(value, axis, [(i, i ^ by) for i in range(size)])  31.1 us
    pallas_call x1, Pallas kernels, aggregate(): pl.pallas_call(functools.partial(aggregate_kernel, reach, groups, send_sl...  8.11 us
    ppermute x4, starting transfers between devices, shifted(): return lax.ppermute(value, axis, pairs)  7.36 us
    all_to_all x1, starting transfers between devices, exchanged(): return lax.all_to_all(value, axis, split_axis=0, concat_axis=0, tiled=True)  6.57 us
    all_to_all x1, waiting for transfers between devices, exchanged(): return lax.all_to_all(value, axis, split_axis=0, concat_axis=0, tiled=True)  6.13 us
    pallas_call x2, Pallas kernels, feature_rows(): pl.pallas_call(functools.partial(feature_kernel, first), in_specs=[IN_SME...  3.34 us
    pallas_call x1, Pallas kernels, weight_partial(): pl.pallas_call(functools.partial(weight_kernel, devs), in_specs=[IN_SMEM]...  2.65 us
  transfers between devices with their start and end apart: 25, of which 10 were waited for; matrix products, arithmetic and copies ran while one was open for 1% of the time, Pallas kernels for 9%

profile of v12, /device:TPU:0, one launch (start us, length us, event | category | flops | bytes accessed | tf_op | source)
XLA Modules:
  0.0 107.3 jit_solution(13007039409460410202)
XLA Ops:
  0.6 0.6 pad_add_fusion.me.index
  1.2 8.1 %aggregate.1 = (bf16[14,128,256]{2,1,0:T(8,128)(2,1)}, bf16[16,128,256]{2,1,0:T(8,128)(2,1)}, bf16[2,128,256]{2,1,0:T(8,128)(2,1)}, bf16[2,128,256]{2,1,0:T(8,12...) custom-call(s32[2]{0:T(128)} %pad_add_fusion.me.index, ...), custom_call_target="tpu_custom_call" | custom-call | flops 1174405120 | bytes 7798784 | tf_op jit(solution)/shard_map/aggregate/pallas_call | solution.py:184
  9.3 2.4 %collective-permute-start = (bf16[2,128,256]{2,1,0:T(8,128)(2,1)}, bf16[2,128,256]{2,1,0:T(8,128)(2,1)S(1)}, u32[]{:S(2)}, u32[]{:S(2)}) collective-permute-start(bf16[2,128,256]{2,1,0:T(8,128)(2,1)} %get-tuple-element.43), channel_id=1, source_target_pairs={{0,4},{4,8},{8,12},{12,16},{16,20},{20,24},{24,28},{1,5},{5,9},{9,... | collective-permute-start | bytes 393224 | tf_op jit(solution)/shard_map/ppermute | solution.py:33
  11.7 1.3 %collective-permute-start.1 = (bf16[2,128,256]{2,1,0:T(8,128)(2,1)}, bf16[2,128,256]{2,1,0:T(8,128)(2,1)S(1)}, u32[]{:S(2)}, u32[]{:S(2)}) collective-permute-start(bf16[2,128,256]{2,1,0:T(8,128)(2,1)} %get-tuple-element.44), channel_id=1, source_target_pairs={{4,0},{8,4},{12,8},{16,12},{20,16},{24,20},{28,24},{5,1},{9,5},{13... | collective-permute-start | bytes 393224 | tf_op jit(solution)/shard_map/ppermute | solution.py:33
  13.0 2.5 %collective-permute-start.2 = (bf16[576,256]{1,0:T(8,128)(2,1)}, bf16[576,256]{1,0:T(8,128)(2,1)S(1)}, u32[]{:S(2)}, u32[]{:S(2)}) collective-permute-start(bf16[576,256]{1,0:T(8,128)(2,1)} %get-tuple-element.50), channel_id=1, source_target_pairs={{0,1},{1,0},{2,3},{3,2},{4,5},{5,4},{6,7},{7,6},{8,9},{9,8},{10,11... | collective-permute-start | bytes 884744 | tf_op jit(solution)/shard_map/ppermute | solution.py:38
  15.5 2.6 %collective-permute-start.3 = (bf16[576,256]{1,0:T(8,128)(2,1)}, bf16[576,256]{1,0:T(8,128)(2,1)S(1)}, u32[]{:S(2)}, u32[]{:S(2)}) collective-permute-start(bf16[576,256]{1,0:T(8,128)(2,1)} %get-tuple-element.51), channel_id=1, source_target_pairs={{0,2},{1,3},{2,0},{3,1},{4,6},{5,7},{6,4},{7,5},{8,10},{9,11},{10,... | collective-permute-start | bytes 884744 | tf_op jit(solution)/shard_map/ppermute | solution.py:38
  18.1 0.0 collective-permute-start.4
  18.1 0.0 collective-permute-done.low
  18.1 0.6 copy-done.3
  18.8 0.1 copy-done.4
  18.8 2.6 %patch.1 = bf16[16,128,256]{2,1,0:T(8,128)(2,1)} custom-call(s32[2]{0:T(128)} %pad_add_fusion.me.index, s32[112]{0:T(128)} %shuffle.3, bf16[16,128,256]{2,1,0:T(8,128)(2,1)} %get-tuple-element.42.outgoing, bf16[2,128,256]{2,1,0:T(8,128)(2,1)} %copy-done.3, bf16[2,128,256]{2,1,0:T(8,128)(2,1)} %copy-done.4), custom_call_target="tpu_custom_call", output_to_operand_aliasing={{}: (2, {})} | custom-call | tf_op jit(solution)/shard_map/patch/pallas_call | solution.py:246
  21.5 6.6 %all-to-all-start = ((bf16[16,128,256]{2,1,0:T(8,128)(2,1)}), bf16[16,128,256]{2,1,0:T(8,128)(2,1)S(1)}, u32[]{:S(2)}, u32[]{:S(2)}) async-start(bf16[16,128,256]{2,1,0:T(8,128)(2,1)} %patch.1), calls=%async_computation | async-start | bytes 2097152 | tf_op jit(solution)/shard_map/all_to_all | solution.py:42
  28.1 0.1 eq.30
  28.2 0.1 add.45
  28.3 0.3 convert_reduce_fusion
  28.6 0.1 copy.14
  28.7 2.4 %collective-permute-start.5 = (bf16[2,128,256]{2,1,0:T(8,128)(2,1)S(1)}, bf16[2,128,256]{2,1,0:T(8,128)(2,1)S(1)}, u32[]{:S(2)}, u32[]{:S(2)}) collective-permute-start(bf16[2,128,256]{2,1,0:T(8,128)(2,1)S(1)} %copy-done.7), channel_id=1, source_target_pairs={{0,4},{4,8},{8,12},{12,16},{16,20},{20,24},{24,28},{1,5},{5,9},{9,... | collective-permute-start | bytes 393224 | tf_op jit(solution)/shard_map/ppermute | solution.py:33
  31.1 1.3 %collective-permute-start.6 = (bf16[2,128,256]{2,1,0:T(8,128)(2,1)S(1)}, bf16[2,128,256]{2,1,0:T(8,128)(2,1)S(1)}, u32[]{:S(2)}, u32[]{:S(2)}) collective-permute-start(bf16[2,128,256]{2,1,0:T(8,128)(2,1)S(1)} %copy-done.6), channel_id=1, source_target_pairs={{4,0},{8,4},{12,8},{16,12},{20,16},{24,20},{28,24},{5,1},{9,5},{13... | collective-permute-start | bytes 393224 | tf_op jit(solution)/shard_map/ppermute | solution.py:33
  32.4 0.1 select_reduce_fusion
  32.6 0.1 copy.15
  32.6 0.1 sub.13.landing
  32.7 0.0 collective-permute-done.2.refs_1_
  32.7 4.6 %collective-permute-done.4.refs_3_ = bf16[576,256]{1,0:T(8,128)(2,1)S(1)} collective-permute-done((bf16[576,256]{1,0:T(8,128)(2,1)}, bf16[576,256]{1,0:T(8,128)(2,1)S(1)}, u32[]{:S(2)}, u32[]{:S(2)}) %collective-permute-start.4) | collective-permute-done | bytes 294944 | tf_op jit(solution)/shard_map/ppermute | solution.py:38
  37.3 6.1 %all-to-all-done.incoming = bf16[16,128,256]{2,1,0:T(8,128)(2,1)S(1)} async-done(((bf16[16,128,256]{2,1,0:T(8,128)(2,1)}), bf16[16,128,256]{2,1,0:T(8,128)(2,1)S(1)}, u32[]{:S(2)}, u32[]{:S(2)}) %all-to-all-start) | async-done | bytes 1048608 | tf_op jit(solution)/shard_map/all_to_all | solution.py:42
  43.5 0.0 collective-permute-done.5.low
  43.5 0.0 collective-permute-done.6.high
  43.5 1.0 merge.1
  44.5 0.1 slice_bitcast_fusion.4
  44.6 3.7 %collective-permute-start.9 = (bf16[448,256]{1,0:T(8,128)(2,1)S(1)}, bf16[448,256]{1,0:T(8,128)(2,1)S(1)}, u32[]{:S(2)}, u32[]{:S(2)}) collective-permute-start(bf16[448,256]{1,0:T(8,128)(2,1)S(1)} %get-tuple-element.89), channel_id=1, source_target_pairs={{0,3},{1,2},{2,1},{3,0},{4,7},{5,6},{6,5},{7,4},{8,11},{9,10},{10,... | collective-permute-start | bytes 688136 | tf_op jit(solution)/shard_map/ppermute | solution.py:38
  48.4 2.8 %collective-permute-start.12 = (bf16[4,128,256]{2,1,0:T(8,128)(2,1)S(1)}, bf16[4,128,256]{2,1,0:T(8,128)(2,1)S(1)}, u32[]{:S(2)}, u32[]{:S(2)}) collective-permute-start(bf16[4,128,256]{2,1,0:T(8,128)(2,1)S(1)} %pad_maximum_fusion.1), channel_id=1, source_target_pairs={{0,24},{4,28},{8,16},{12,20},{16,8},{20,12},{24,0},{28,4},{1,25},{... | collective-permute-start | bytes 786440 | tf_op jit(solution)/shard_map/ppermute | solution.py:38
  51.1 0.6 collective-permute-start.11
  51.7 1.4 %collective-permute-start.10 = (bf16[4,128,256]{2,1,0:T(8,128)(2,1)S(1)}, bf16[4,128,256]{2,1,0:T(8,128)(2,1)S(1)}, u32[]{:S(2)}, u32[]{:S(2)}) collective-permute-start(bf16[4,128,256]{2,1,0:T(8,128)(2,1)S(1)} %pad_maximum_fusion.1), channel_id=1, source_target_pairs={{0,8},{4,12},{8,0},{12,4},{16,24},{20,28},{24,16},{28,20},{1,9},{5... | collective-permute-start | bytes 786440 | tf_op jit(solution)/shard_map/ppermute | solution.py:38
  53.1 0.0 collective-permute-start.8
  53.1 1.0 collective-permute-done.9.refs_7_.refs_3_
  54.1 5.9 %collective-permute-start.7 = (bf16[448,256]{1,0:T(8,128)(2,1)S(1)}, bf16[448,256]{1,0:T(8,128)(2,1)S(1)}, u32[]{:S(2)}, u32[]{:S(2)}) collective-permute-start(bf16[448,256]{1,0:T(8,128)(2,1)S(1)} %get-tuple-element.91), channel_id=1, source_target_pairs={{0,2},{1,3},{2,0},{3,1},{4,6},{5,7},{6,4},{7,5},{8,10},{9,11},{10,... | collective-permute-start | bytes 688136 | tf_op jit(solution)/shard_map/ppermute | solution.py:38
  59.9 0.3 collective-permute-done.8.refs_5_.refs_1_
  60.2 11.0 %collective-permute-done.7.refs_6_.refs_2_ = bf16[448,256]{1,0:T(8,128)(2,1)S(1)} collective-permute-done((bf16[448,256]{1,0:T(8,128)(2,1)S(1)}, bf16[448,256]{1,0:T(8,128)(2,1)S(1)}, u32[]{:S(2)}, u32[]{:S(2)}) %collective-permute-start.7) | collective-permute-done | bytes 229408 | tf_op jit(solution)/shard_map/ppermute | solution.py:38
  71.2 0.0 collective-permute-done.12
  71.2 0.0 collective-permute-done.11
  71.2 0.0 collective-permute-done.10
  71.2 0.1 pad_maximum_fusion.refs_4_
  71.4 0.2 collective-permute-start.13
  71.6 2.6 %weight_partial.1 = (bf16[4,4,128,256]{3,2,1,0:T(8,128)(2,1)S(1)}, bf16[4,4,128,256]{3,2,1,0:T(8,128)(2,1)S(1)}) custom-call(s32[2]{0:T(128)S(1)} %copy-done.1, bf16[576,256]{1,0:T(8,128)(2,1)S(1)} %copy-done.2, bf16[576,256]{1,0:T(8,128)(2,1)S(1)} %collective-permute-done.2.refs_1_, bf16[576,256]{1,0:T(8,128)(2,1)S(1)} %collective-permute-done.3.refs_2_, ...), custom_call_target="tpu_custom_call" | custom-call | flops 939524096 | bytes 3932160 | tf_op jit(solution)/shard_map/weight_partial/pallas_call | solution.py:334
  74.2 0.0 collective-permute-done.13.refs_5_
  74.2 0.4 collective-permute-start.14
  74.7 2.3 %feature_rows.2 = bf16[3,448,256]{2,1,0:T(8,128)(2,1)S(1)} custom-call(s32[2]{0:T(128)S(1)} %copy-done.1, bf16[448,256]{1,0:T(8,128)(2,1)S(1)} %get-tuple-element.75.refs_4_.refs_0_, bf16[448,256]{1,0:T(8,128)(2,1)S(1)} %collective-permute-done.8.refs_5_.refs_1_, bf16[448,256]{1,0:T(8,128)(2,1)S(1)} %collective-permute-done.7.refs_6_.refs_2_, ...), custom_call_target="tpu_custom_call" | custom-call | flops 704643072 | bytes 3178496 | tf_op jit(solution)/shard_map/feature_rows/pallas_call | solution.py:382
  77.0 0.4 convert_add_fusion
  77.4 0.1 slice_bitcast_fusion.3
  77.5 0.1 collective-permute-start.15
  77.6 0.1 collective-permute-start.17
  77.7 3.4 %collective-permute-start.16 = (bf16[4,128,256]{2,1,0:T(8,128)(2,1)S(1)}, bf16[4,128,256]{2,1,0:T(8,128)(2,1)S(1)}, u32[]{:S(2)}, u32[]{:S(2)}) collective-permute-start(bf16[4,128,256]{2,1,0:T(8,128)(2,1)S(1)} %get-tuple-element.88), channel_id=1, source_target_pairs={{0,16},{4,20},{8,24},{12,28},{16,0},{20,4},{24,8},{28,12},{1,17},{... | collective-permute-start | bytes 786440 | tf_op jit(solution)/shard_map/ppermute | solution.py:38
  81.1 1.5 %collective-permute-start.23 = (bf16[448,256]{1,0:T(8,128)(2,1)S(1)}, bf16[448,256]{1,0:T(8,128)(2,1)S(1)}, u32[]{:S(2)}, u32[]{:S(2)}) collective-permute-start(bf16[448,256]{1,0:T(8,128)(2,1)S(1)} %get-tuple-element.93), channel_id=1, source_target_pairs={{0,3},{1,2},{2,1},{3,0},{4,7},{5,6},{6,5},{7,4},{8,11},{9,10},{10,... | collective-permute-start | bytes 688136 | tf_op jit(solution)/shard_map/ppermute | solution.py:38
  82.6 4.1 %collective-permute-done.15 = bf16[4,128,256]{2,1,0:T(8,128)(2,1)S(1)} collective-permute-done((bf16[4,128,256]{2,1,0:T(8,128)(2,1)S(1)}, bf16[4,128,256]{2,1,0:T(8,128)(2,1)S(1)}, u32[]{:S(2)}, u32[]{:S(2)}) %collective-permute-start.15) | collective-permute-done | bytes 262176 | tf_op jit(solution)/shard_map/ppermute | solution.py:38
  86.7 2.8 %collective-permute-done.17 = bf16[4,128,256]{2,1,0:T(8,128)(2,1)S(1)} collective-permute-done((bf16[4,128,256]{2,1,0:T(8,128)(2,1)S(1)}, bf16[4,128,256]{2,1,0:T(8,128)(2,1)S(1)}, u32[]{:S(2)}, u32[]{:S(2)}) %collective-permute-start.17) | collective-permute-done | bytes 262176 | tf_op jit(solution)/shard_map/ppermute | solution.py:38
  89.5 3.3 %collective-permute-done.16 = bf16[4,128,256]{2,1,0:T(8,128)(2,1)S(1)} collective-permute-done((bf16[4,128,256]{2,1,0:T(8,128)(2,1)S(1)}, bf16[4,128,256]{2,1,0:T(8,128)(2,1)S(1)}, u32[]{:S(2)}, u32[]{:S(2)}) %collective-permute-start.16) | collective-permute-done | bytes 262176 | tf_op jit(solution)/shard_map/ppermute | solution.py:38
  92.9 0.2 fusion.10
  93.1 0.1 collective-permute-start.18
  93.1 1.5 %collective-permute-start.20 = (bf16[128,256]{1,0:T(8,128)(2,1)S(1)}, bf16[128,256]{1,0:T(8,128)(2,1)S(1)}, u32[]{:S(2)}, u32[]{:S(2)}) collective-permute-start(bf16[128,256]{1,0:T(8,128)(2,1)S(1)} %get-tuple-element.97), channel_id=1, source_target_pairs={{0,3},{1,2},{2,1},{3,0},{4,7},{5,6},{6,5},{7,4},{8,11},{9,10},{10,... | collective-permute-start | bytes 196616 | tf_op jit(solution)/shard_map/ppermute | solution.py:38
  94.6 4.5 %collective-permute-start.19 = (bf16[128,256]{1,0:T(8,128)(2,1)S(1)}, bf16[128,256]{1,0:T(8,128)(2,1)S(1)}, u32[]{:S(2)}, u32[]{:S(2)}) collective-permute-start(bf16[128,256]{1,0:T(8,128)(2,1)S(1)} %get-tuple-element.98), channel_id=1, source_target_pairs={{0,2},{1,3},{2,0},{3,1},{4,6},{5,7},{6,4},{7,5},{8,10},{9,11},{10,... | collective-permute-start | bytes 196616 | tf_op jit(solution)/shard_map/ppermute | solution.py:38
  99.2 1.0 feature_rows.3
  100.2 4.6 %collective-permute-done.22.refs_2_ = bf16[448,256]{1,0:T(8,128)(2,1)S(1)} collective-permute-done((bf16[448,256]{1,0:T(8,128)(2,1)S(1)}, bf16[448,256]{1,0:T(8,128)(2,1)S(1)}, u32[]{:S(2)}, u32[]{:S(2)}) %collective-permute-start.22) | collective-permute-done | bytes 229408 | tf_op jit(solution)/shard_map/ppermute | solution.py:38
  104.8 1.5 %laid_out.1 = bf16[1792,256]{1,0:T(8,128)(2,1)} custom-call(s32[2]{0:T(128)S(1)} %copy-done.1, bf16[448,256]{1,0:T(8,128)(2,1)S(1)} %bitcast.60, bf16[448,256]{1,0:T(8,128)(2,1)S(1)} %collective-permute-done.21.refs_1_, bf16[448,256]{1,0:T(8,128)(2,1)S(1)} %collective-permute-done.22.refs_2_, bf16[448,256]{1,0:T(8,128)(2,1)S(1)} %collective-permute-done.23.refs_3_), custom_call_target="tpu_custom_call" | custom-call | tf_op jit(solution)/shard_map/laid_out/pallas_call | solution.py:414
  106.3 0.3 collective-permute-done.19
  106.6 0.7 fusion.5
  (32 shorter events, 0.2 us)
Async XLA Ops:
  9.3 8.8 %collective-permute-start = (bf16[2,128,256]{2,1,0:T(8,128)(2,1)}, bf16[2,128,256]{2,1,0:T(8,128)(2,1)S(1)}, u32[]{:S(2)}, u32[]{:S(2)}) collective-permute-start(bf16[2,128,256]{2,1,0:T(8,128)(2,1)} %get-tuple-element.43), channel_id=1, source_target_pairs={{0,4},{4,8},{8,12},{12,16},{16,20},{20,24},{24,28},{1,5},{5,9},{9,... | collective-permute-start | bytes 393224 | tf_op jit(solution)/shard_map/ppermute | solution.py:33
  11.7 6.4 %collective-permute-start.1 = (bf16[2,128,256]{2,1,0:T(8,128)(2,1)}, bf16[2,128,256]{2,1,0:T(8,128)(2,1)S(1)}, u32[]{:S(2)}, u32[]{:S(2)}) collective-permute-start(bf16[2,128,256]{2,1,0:T(8,128)(2,1)} %get-tuple-element.44), channel_id=1, source_target_pairs={{4,0},{8,4},{12,8},{16,12},{20,16},{24,20},{28,24},{5,1},{9,5},{13... | collective-permute-start | bytes 393224 | tf_op jit(solution)/shard_map/ppermute | solution.py:33
  13.0 19.7 %collective-permute-start.2 = (bf16[576,256]{1,0:T(8,128)(2,1)}, bf16[576,256]{1,0:T(8,128)(2,1)S(1)}, u32[]{:S(2)}, u32[]{:S(2)}) collective-permute-start(bf16[576,256]{1,0:T(8,128)(2,1)} %get-tuple-element.50), channel_id=1, source_target_pairs={{0,1},{1,0},{2,3},{3,2},{4,5},{5,4},{6,7},{7,6},{8,9},{9,8},{10,11... | collective-permute-start | bytes 884744 | tf_op jit(solution)/shard_map/ppermute | solution.py:38
  15.5 17.2 %collective-permute-start.3 = (bf16[576,256]{1,0:T(8,128)(2,1)}, bf16[576,256]{1,0:T(8,128)(2,1)S(1)}, u32[]{:S(2)}, u32[]{:S(2)}) collective-permute-start(bf16[576,256]{1,0:T(8,128)(2,1)} %get-tuple-element.51), channel_id=1, source_target_pairs={{0,2},{1,3},{2,0},{3,1},{4,6},{5,7},{6,4},{7,5},{8,10},{9,11},{10,... | collective-permute-start | bytes 884744 | tf_op jit(solution)/shard_map/ppermute | solution.py:38
  18.1 19.2 %collective-permute-start.4 = (bf16[576,256]{1,0:T(8,128)(2,1)}, bf16[576,256]{1,0:T(8,128)(2,1)S(1)}, u32[]{:S(2)}, u32[]{:S(2)}) collective-permute-start(bf16[576,256]{1,0:T(8,128)(2,1)} %get-tuple-element.52), channel_id=1, source_target_pairs={{0,3},{1,2},{2,1},{3,0},{4,7},{5,6},{6,5},{7,4},{8,11},{9,10},{10,... | collective-permute-start | bytes 884744 | tf_op jit(solution)/shard_map/ppermute | solution.py:38
  18.1 0.7 copy-start.3
  18.1 0.7 copy-start.4
  18.8 9.2 %copy-start.5 = (s32[112]{0:T(128)S(1)}, s32[112]{0:T(128)}, u32[]{:S(2)}) copy-start(s32[112]{0:T(128)} %shuffle.3) | copy-start | bytes 1348
  18.8 12.3 %copy-start.6 = (bf16[2,128,256]{2,1,0:T(8,128)(2,1)S(1)}, bf16[2,128,256]{2,1,0:T(8,128)(2,1)}, u32[]{:S(2)}) copy-start(bf16[2,128,256]{2,1,0:T(8,128)(2,1)} %get-tuple-element.60) | copy-start | bytes 393220
  18.8 24.6 %copy-start = (bf16[14,128,256]{2,1,0:T(8,128)(2,1)S(1)}, bf16[14,128,256]{2,1,0:T(8,128)(2,1)}, u32[]{:S(2)}) copy-start(bf16[14,128,256]{2,1,0:T(8,128)(2,1)} %get-tuple-element.58.clean) | copy-start | bytes 2752516
  18.8 24.7 %copy-start.1 = (s32[2]{0:T(128)S(1)}, s32[2]{0:T(128)}, u32[]{:S(2)}) copy-start(s32[2]{0:T(128)} %pad_add_fusion.me.index) | copy-start | bytes 28
  21.5 7.2 %copy-start.7 = (bf16[2,128,256]{2,1,0:T(8,128)(2,1)S(1)}, bf16[2,128,256]{2,1,0:T(8,128)(2,1)}, u32[]{:S(2)}) copy-start(bf16[2,128,256]{2,1,0:T(8,128)(2,1)} %get-tuple-element.59) | copy-start | bytes 393220
  21.5 22.0 %all-to-all-start = ((bf16[16,128,256]{2,1,0:T(8,128)(2,1)}), bf16[16,128,256]{2,1,0:T(8,128)(2,1)S(1)}, u32[]{:S(2)}, u32[]{:S(2)}) async-start(bf16[16,128,256]{2,1,0:T(8,128)(2,1)} %patch.1), calls=%async_computation | async-start | bytes 2097152 | tf_op jit(solution)/shard_map/all_to_all | solution.py:42
  28.7 14.8 %collective-permute-start.5 = (bf16[2,128,256]{2,1,0:T(8,128)(2,1)S(1)}, bf16[2,128,256]{2,1,0:T(8,128)(2,1)S(1)}, u32[]{:S(2)}, u32[]{:S(2)}) collective-permute-start(bf16[2,128,256]{2,1,0:T(8,128)(2,1)S(1)} %copy-done.7), channel_id=1, source_target_pairs={{0,4},{4,8},{8,12},{12,16},{16,20},{20,24},{24,28},{1,5},{5,9},{9,... | collective-permute-start | bytes 393224 | tf_op jit(solution)/shard_map/ppermute | solution.py:33
  31.1 12.4 %collective-permute-start.6 = (bf16[2,128,256]{2,1,0:T(8,128)(2,1)S(1)}, bf16[2,128,256]{2,1,0:T(8,128)(2,1)S(1)}, u32[]{:S(2)}, u32[]{:S(2)}) collective-permute-start(bf16[2,128,256]{2,1,0:T(8,128)(2,1)S(1)} %copy-done.6), channel_id=1, source_target_pairs={{4,0},{8,4},{12,8},{16,12},{20,16},{24,20},{28,24},{5,1},{9,5},{13... | collective-permute-start | bytes 393224 | tf_op jit(solution)/shard_map/ppermute | solution.py:33
  43.4 4.8 %copy-start.2 = (bf16[576,256]{1,0:T(8,128)(2,1)S(1)}, bf16[576,256]{1,0:T(8,128)(2,1)}, u32[]{:S(2)}) copy-start(bf16[576,256]{1,0:T(8,128)(2,1)} %get-tuple-element.53.refs_0_) | copy-start | bytes 884740
  44.6 9.5 %collective-permute-start.9 = (bf16[448,256]{1,0:T(8,128)(2,1)S(1)}, bf16[448,256]{1,0:T(8,128)(2,1)S(1)}, u32[]{:S(2)}, u32[]{:S(2)}) collective-permute-start(bf16[448,256]{1,0:T(8,128)(2,1)S(1)} %get-tuple-element.89), channel_id=1, source_target_pairs={{0,3},{1,2},{2,1},{3,0},{4,7},{5,6},{6,5},{7,4},{8,11},{9,10},{10,... | collective-permute-start | bytes 688136 | tf_op jit(solution)/shard_map/ppermute | solution.py:38
  48.4 22.9 %collective-permute-start.12 = (bf16[4,128,256]{2,1,0:T(8,128)(2,1)S(1)}, bf16[4,128,256]{2,1,0:T(8,128)(2,1)S(1)}, u32[]{:S(2)}, u32[]{:S(2)}) collective-permute-start(bf16[4,128,256]{2,1,0:T(8,128)(2,1)S(1)} %pad_maximum_fusion.1), channel_id=1, source_target_pairs={{0,24},{4,28},{8,16},{12,20},{16,8},{20,12},{24,0},{28,4},{1,25},{... | collective-permute-start | bytes 786440 | tf_op jit(solution)/shard_map/ppermute | solution.py:38
  51.1 20.1 %collective-permute-start.11 = (bf16[4,128,256]{2,1,0:T(8,128)(2,1)S(1)}, bf16[4,128,256]{2,1,0:T(8,128)(2,1)S(1)}, u32[]{:S(2)}, u32[]{:S(2)}) collective-permute-start(bf16[4,128,256]{2,1,0:T(8,128)(2,1)S(1)} %pad_maximum_fusion.1), channel_id=1, source_target_pairs={{0,16},{4,20},{8,24},{12,28},{16,0},{20,4},{24,8},{28,12},{1,17},{... | collective-permute-start | bytes 786440 | tf_op jit(solution)/shard_map/ppermute | solution.py:38
  51.7 19.5 %collective-permute-start.10 = (bf16[4,128,256]{2,1,0:T(8,128)(2,1)S(1)}, bf16[4,128,256]{2,1,0:T(8,128)(2,1)S(1)}, u32[]{:S(2)}, u32[]{:S(2)}) collective-permute-start(bf16[4,128,256]{2,1,0:T(8,128)(2,1)S(1)} %pad_maximum_fusion.1), channel_id=1, source_target_pairs={{0,8},{4,12},{8,0},{12,4},{16,24},{20,28},{24,16},{28,20},{1,9},{5... | collective-permute-start | bytes 786440 | tf_op jit(solution)/shard_map/ppermute | solution.py:38
  53.1 7.1 %collective-permute-start.8 = (bf16[448,256]{1,0:T(8,128)(2,1)S(1)}, bf16[448,256]{1,0:T(8,128)(2,1)S(1)}, u32[]{:S(2)}, u32[]{:S(2)}) collective-permute-start(bf16[448,256]{1,0:T(8,128)(2,1)S(1)} %get-tuple-element.90), channel_id=1, source_target_pairs={{0,1},{1,0},{2,3},{3,2},{4,5},{5,4},{6,7},{7,6},{8,9},{9,8},{10,11... | collective-permute-start | bytes 688136 | tf_op jit(solution)/shard_map/ppermute | solution.py:38
  54.1 17.1 %collective-permute-start.7 = (bf16[448,256]{1,0:T(8,128)(2,1)S(1)}, bf16[448,256]{1,0:T(8,128)(2,1)S(1)}, u32[]{:S(2)}, u32[]{:S(2)}) collective-permute-start(bf16[448,256]{1,0:T(8,128)(2,1)S(1)} %get-tuple-element.91), channel_id=1, source_target_pairs={{0,2},{1,3},{2,0},{3,1},{4,6},{5,7},{6,4},{7,5},{8,10},{9,11},{10,... | collective-permute-start | bytes 688136 | tf_op jit(solution)/shard_map/ppermute | solution.py:38
  71.4 2.8 %collective-permute-start.13 = (bf16[4,4,128,256]{3,2,1,0:T(8,128)(2,1)S(1)}, bf16[4,4,128,256]{3,2,1,0:T(8,128)(2,1)S(1)}, u32[]{:S(2)}, u32[]{:S(2)}) collective-permute-start(bf16[4,4,128,256]{3,2,1,0:T(8,128)(2,1)S(1)} %pad_maximum_fusion.refs_4_), channel_id=1, source_target_pairs={{0,4},{4,0},{8,12},{12,8},{16,20},{20,16},{24,28},{28,24},{1,5},{5... | collective-permute-start | bytes 3145736 | tf_op jit(solution)/shard_map/ppermute | solution.py:38
  74.2 2.8 %collective-permute-start.14 = (bf16[4,4,128,256]{3,2,1,0:T(8,128)(2,1)S(1)}, bf16[4,4,128,256]{3,2,1,0:T(8,128)(2,1)S(1)}, u32[]{:S(2)}, u32[]{:S(2)}) collective-permute-start(bf16[4,4,128,256]{3,2,1,0:T(8,128)(2,1)S(1)} %get-tuple-element.72), channel_id=1, source_target_pairs={{0,4},{4,0},{8,12},{12,8},{16,20},{20,16},{24,28},{28,24},{1,5},{5... | collective-permute-start | bytes 3145736 | tf_op jit(solution)/shard_map/ppermute | solution.py:38
  77.5 9.2 %collective-permute-start.15 = (bf16[4,128,256]{2,1,0:T(8,128)(2,1)S(1)}, bf16[4,128,256]{2,1,0:T(8,128)(2,1)S(1)}, u32[]{:S(2)}, u32[]{:S(2)}) collective-permute-start(bf16[4,128,256]{2,1,0:T(8,128)(2,1)S(1)} %get-tuple-element.86), channel_id=1, source_target_pairs={{0,8},{4,12},{8,0},{12,4},{16,24},{20,28},{24,16},{28,20},{1,9},{5... | collective-permute-start | bytes 786440 | tf_op jit(solution)/shard_map/ppermute | solution.py:38
  77.6 12.0 %collective-permute-start.17 = (bf16[4,128,256]{2,1,0:T(8,128)(2,1)S(1)}, bf16[4,128,256]{2,1,0:T(8,128)(2,1)S(1)}, u32[]{:S(2)}, u32[]{:S(2)}) collective-permute-start(bf16[4,128,256]{2,1,0:T(8,128)(2,1)S(1)} %get-tuple-element.87), channel_id=1, source_target_pairs={{0,24},{4,28},{8,16},{12,20},{16,8},{20,12},{24,0},{28,4},{1,25},{... | collective-permute-start | bytes 786440 | tf_op jit(solution)/shard_map/ppermute | solution.py:38
  77.7 15.2 %collective-permute-start.16 = (bf16[4,128,256]{2,1,0:T(8,128)(2,1)S(1)}, bf16[4,128,256]{2,1,0:T(8,128)(2,1)S(1)}, u32[]{:S(2)}, u32[]{:S(2)}) collective-permute-start(bf16[4,128,256]{2,1,0:T(8,128)(2,1)S(1)} %get-tuple-element.88), channel_id=1, source_target_pairs={{0,16},{4,20},{8,24},{12,28},{16,0},{20,4},{24,8},{28,12},{1,17},{... | collective-permute-start | bytes 786440 | tf_op jit(solution)/shard_map/ppermute | solution.py:38
  81.1 13.5 %collective-permute-start.23 = (bf16[448,256]{1,0:T(8,128)(2,1)S(1)}, bf16[448,256]{1,0:T(8,128)(2,1)S(1)}, u32[]{:S(2)}, u32[]{:S(2)}) collective-permute-start(bf16[448,256]{1,0:T(8,128)(2,1)S(1)} %get-tuple-element.93), channel_id=1, source_target_pairs={{0,3},{1,2},{2,1},{3,0},{4,7},{5,6},{6,5},{7,4},{8,11},{9,10},{10,... | collective-permute-start | bytes 688136 | tf_op jit(solution)/shard_map/ppermute | solution.py:38
  82.6 22.2 %collective-permute-start.22 = (bf16[448,256]{1,0:T(8,128)(2,1)S(1)}, bf16[448,256]{1,0:T(8,128)(2,1)S(1)}, u32[]{:S(2)}, u32[]{:S(2)}) collective-permute-start(bf16[448,256]{1,0:T(8,128)(2,1)S(1)} %get-tuple-element.94), channel_id=1, source_target_pairs={{0,2},{1,3},{2,0},{3,1},{4,6},{5,7},{6,4},{7,5},{8,10},{9,11},{10,... | collective-permute-start | bytes 688136 | tf_op jit(solution)/shard_map/ppermute | solution.py:38
  86.7 18.1 %collective-permute-start.21 = (bf16[448,256]{1,0:T(8,128)(2,1)S(1)}, bf16[448,256]{1,0:T(8,128)(2,1)S(1)}, u32[]{:S(2)}, u32[]{:S(2)}) collective-permute-start(bf16[448,256]{1,0:T(8,128)(2,1)S(1)} %get-tuple-element.95), channel_id=1, source_target_pairs={{0,1},{1,0},{2,3},{3,2},{4,5},{5,4},{6,7},{7,6},{8,9},{9,8},{10,11... | collective-permute-start | bytes 688136 | tf_op jit(solution)/shard_map/ppermute | solution.py:38
  93.1 13.2 %collective-permute-start.18 = (bf16[128,256]{1,0:T(8,128)(2,1)S(1)}, bf16[128,256]{1,0:T(8,128)(2,1)S(1)}, u32[]{:S(2)}, u32[]{:S(2)}) collective-permute-start(bf16[128,256]{1,0:T(8,128)(2,1)S(1)} %get-tuple-element.96), channel_id=1, source_target_pairs={{0,1},{1,0},{2,3},{3,2},{4,5},{5,4},{6,7},{7,6},{8,9},{9,8},{10,11... | collective-permute-start | bytes 196616 | tf_op jit(solution)/shard_map/ppermute | solution.py:38
  93.1 13.1 %collective-permute-start.20 = (bf16[128,256]{1,0:T(8,128)(2,1)S(1)}, bf16[128,256]{1,0:T(8,128)(2,1)S(1)}, u32[]{:S(2)}, u32[]{:S(2)}) collective-permute-start(bf16[128,256]{1,0:T(8,128)(2,1)S(1)} %get-tuple-element.97), channel_id=1, source_target_pairs={{0,3},{1,2},{2,1},{3,0},{4,7},{5,6},{6,5},{7,4},{8,11},{9,10},{10,... | collective-permute-start | bytes 196616 | tf_op jit(solution)/shard_map/ppermute | solution.py:38
  94.6 12.0 %collective-permute-start.19 = (bf16[128,256]{1,0:T(8,128)(2,1)S(1)}, bf16[128,256]{1,0:T(8,128)(2,1)S(1)}, u32[]{:S(2)}, u32[]{:S(2)}) collective-permute-start(bf16[128,256]{1,0:T(8,128)(2,1)S(1)} %get-tuple-element.98), channel_id=1, source_target_pairs={{0,2},{1,3},{2,0},{3,1},{4,6},{5,7},{6,4},{7,5},{8,10},{9,11},{10,... | collective-permute-start | bytes 196616 | tf_op jit(solution)/shard_map/ppermute | solution.py:38

commit v13 on v12

--- a/solution.py
+++ b/solution.py
@@ -483,10 +483,8 @@
         summed[i] = swapped(merged[i], "chan", i)
     tiles = jnp.stack([piece[quarter:] for piece in packed])
     even = [tiles] + [swapped(tiles, "node", 2 * i) for i in range(1, devs // 2)]
-    order = [0, *range(2, groups - 1), 1, groups - 1]
-    listed, even = lax.optimization_barrier(([summed[i] for i in order], even))
-    summed = [listed[order.index(i)] for i in range(groups)]
     even = jnp.stack(even)
+    summed, even = lax.optimization_barrier((summed, even))
     odd = swapped(even, "node", 1)
 
     keep, send = weight_partial(index, packed, summed, devs)

time: 108 us -> 119 us (1.10)
  waiting for transfers between devices: 38.2 us -> 51.4 us
  starting transfers between devices: 45 us -> 41.3 us
  other arithmetic: 2.5 us -> 4.27 us
    ppermute x20, waiting for transfers between devices: 32.1 us -> 47.1 us  [swapped(): return lax.ppermute(value, axis, [(i, i ^ by) for i in range(size)])]
    all_to_all x1, waiting for transfers between devices: 6.13 us -> 0.01 us  [exchanged(): return lax.all_to_all(value, axis, split_axis=0, concat_axis=0, tiled=True)]
    ppermute x4, waiting for transfers between devices: 0.01 us -> 4.24 us  [shifted(): return lax.ppermute(value, axis, pairs)]
    ppermute x20, starting transfers between devices: 31.1 us -> 27.8 us  [swapped(): return lax.ppermute(value, axis, [(i, i ^ by) for i in range(size)])]
    another operation x1 -> x2, other arithmetic: 0.13 us -> 1.93 us  [local(): even = jnp.stack(even)]
  transfers between devices with their start and end apart: 25 -> 25, of which waited for: 10 -> 9; matrix products, arithmetic and copies ran while one was open for 1% -> 3% of each run, Pallas kernels for 9% -> 7%
where the time goes in v13:
time: 119 us; the launch traced here: 118 us
  waiting for transfers between devices  51.4 us (43%)
  starting transfers between devices  41.3 us (35%)
  Pallas kernels  19.3 us (16%)
  other arithmetic  4.27 us (4%)
  local copies, waits for them, and re-layouts  1.28 us (1%)
    ppermute x20, waiting for transfers between devices, swapped(): return lax.ppermute(value, axis, [(i, i ^ by) for i in range(size)])  47.1 us
    ppermute x20, starting transfers between devices, swapped(): return lax.ppermute(value, axis, [(i, i ^ by) for i in range(size)])  27.8 us
    pallas_call x1, Pallas kernels, aggregate(): pl.pallas_call(functools.partial(aggregate_kernel, reach, groups, send_sl...  8.14 us
    all_to_all x1, starting transfers between devices, exchanged(): return lax.all_to_all(value, axis, split_axis=0, concat_axis=0, tiled=True)  6.96 us
    ppermute x4, starting transfers between devices, shifted(): return lax.ppermute(value, axis, pairs)  6.54 us
    ppermute x4, waiting for transfers between devices, shifted(): return lax.ppermute(value, axis, pairs)  4.24 us
    pallas_call x2, Pallas kernels, feature_rows(): pl.pallas_call(functools.partial(feature_kernel, first), in_specs=[IN_SME...  3.33 us
    pallas_call x1, Pallas kernels, weight_partial(): pl.pallas_call(functools.partial(weight_kernel, devs), in_specs=[IN_SMEM]...  2.65 us
  transfers between devices with their start and end apart: 25, of which 9 were waited for; matrix products, arithmetic and copies ran while one was open for 3% of the time, Pallas kernels for 7%

profile of v13, /device:TPU:0, one launch (start us, length us, event | category | flops | bytes accessed | tf_op | source)
XLA Modules:
  0.0 118.4 jit_solution(15037024216990930387)
XLA Ops:
  0.6 0.6 pad_add_fusion.me.index
  1.2 8.1 %aggregate.1 = (bf16[14,128,256]{2,1,0:T(8,128)(2,1)}, bf16[16,128,256]{2,1,0:T(8,128)(2,1)}, bf16[2,128,256]{2,1,0:T(8,128)(2,1)}, bf16[2,128,256]{2,1,0:T(8,12...) custom-call(s32[2]{0:T(128)} %pad_add_fusion.me.index, ...), custom_call_target="tpu_custom_call" | custom-call | flops 1174405120 | bytes 7798784 | tf_op jit(solution)/shard_map/aggregate/pallas_call | solution.py:184
  9.4 2.3 %collective-permute-start = (bf16[2,128,256]{2,1,0:T(8,128)(2,1)}, bf16[2,128,256]{2,1,0:T(8,128)(2,1)S(1)}, u32[]{:S(2)}, u32[]{:S(2)}) collective-permute-start(bf16[2,128,256]{2,1,0:T(8,128)(2,1)} %get-tuple-element.40), channel_id=1, source_target_pairs={{0,4},{4,8},{8,12},{12,16},{16,20},{20,24},{24,28},{1,5},{5,9},{9,... | collective-permute-start | bytes 393224 | tf_op jit(solution)/shard_map/ppermute | solution.py:33
  11.7 1.3 %collective-permute-start.1 = (bf16[2,128,256]{2,1,0:T(8,128)(2,1)}, bf16[2,128,256]{2,1,0:T(8,128)(2,1)S(1)}, u32[]{:S(2)}, u32[]{:S(2)}) collective-permute-start(bf16[2,128,256]{2,1,0:T(8,128)(2,1)} %get-tuple-element.41), channel_id=1, source_target_pairs={{4,0},{8,4},{12,8},{16,12},{20,16},{24,20},{28,24},{5,1},{9,5},{13... | collective-permute-start | bytes 393224 | tf_op jit(solution)/shard_map/ppermute | solution.py:33
  13.0 4.2 %collective-permute-done.1.high = bf16[2,128,256]{2,1,0:T(8,128)(2,1)S(1)} collective-permute-done((bf16[2,128,256]{2,1,0:T(8,128)(2,1)}, bf16[2,128,256]{2,1,0:T(8,128)(2,1)S(1)}, u32[]{:S(2)}, u32[]{:S(2)}) %collective-permute-start.1) | collective-permute-done | bytes 131104 | tf_op jit(solution)/shard_map/ppermute | solution.py:33
  17.3 0.6 copy-done.5
  17.9 2.6 %patch.1 = bf16[16,128,256]{2,1,0:T(8,128)(2,1)} custom-call(s32[2]{0:T(128)} %pad_add_fusion.me.index, s32[112]{0:T(128)} %shuffle.3, bf16[16,128,256]{2,1,0:T(8,128)(2,1)} %get-tuple-element.39.outgoing, bf16[2,128,256]{2,1,0:T(8,128)(2,1)} %copy-done.4, bf16[2,128,256]{2,1,0:T(8,128)(2,1)} %copy-done.5), custom_call_target="tpu_custom_call", output_to_operand_aliasing={{}: (2, {})} | custom-call | tf_op jit(solution)/shard_map/patch/pallas_call | solution.py:246
  20.5 0.0 copy-start
  20.6 7.0 %all-to-all-start = ((bf16[16,128,256]{2,1,0:T(8,128)(2,1)}), bf16[16,128,256]{2,1,0:T(8,128)(2,1)S(1)}, u32[]{:S(2)}, u32[]{:S(2)}) async-start(bf16[16,128,256]{2,1,0:T(8,128)(2,1)} %patch.1), calls=%async_computation | async-start | bytes 2097152 | tf_op jit(solution)/shard_map/all_to_all | solution.py:42
  27.5 1.6 %collective-permute-start.2 = (bf16[576,256]{1,0:T(8,128)(2,1)}, bf16[576,256]{1,0:T(8,128)(2,1)S(1)}, u32[]{:S(2)}, u32[]{:S(2)}) collective-permute-start(bf16[576,256]{1,0:T(8,128)(2,1)} %get-tuple-element.47), channel_id=1, source_target_pairs={{0,1},{1,0},{2,3},{3,2},{4,5},{5,4},{6,7},{7,6},{8,9},{9,8},{10,11... | collective-permute-start | bytes 884744 | tf_op jit(solution)/shard_map/ppermute | solution.py:38
  29.1 2.6 %collective-permute-start.3 = (bf16[576,256]{1,0:T(8,128)(2,1)}, bf16[576,256]{1,0:T(8,128)(2,1)S(1)}, u32[]{:S(2)}, u32[]{:S(2)}) collective-permute-start(bf16[576,256]{1,0:T(8,128)(2,1)} %get-tuple-element.48), channel_id=1, source_target_pairs={{0,2},{1,3},{2,0},{3,1},{4,6},{5,7},{6,4},{7,5},{8,10},{9,11},{10,... | collective-permute-start | bytes 884744 | tf_op jit(solution)/shard_map/ppermute | solution.py:38
  31.7 0.2 collective-permute-start.4
  32.0 0.1 eq.30
  32.1 0.1 add.45
  32.1 0.3 convert_reduce_fusion
  32.5 0.1 copy.14
  32.5 1.6 %collective-permute-start.5 = (bf16[2,128,256]{2,1,0:T(8,128)(2,1)}, bf16[2,128,256]{2,1,0:T(8,128)(2,1)S(1)}, u32[]{:S(2)}, u32[]{:S(2)}) collective-permute-start(bf16[2,128,256]{2,1,0:T(8,128)(2,1)} %get-tuple-element.56), channel_id=1, source_target_pairs={{0,4},{4,8},{8,12},{12,16},{16,20},{20,24},{24,28},{1,5},{5,9},{9,... | collective-permute-start | bytes 393224 | tf_op jit(solution)/shard_map/ppermute | solution.py:33
  34.2 1.3 %collective-permute-start.6 = (bf16[2,128,256]{2,1,0:T(8,128)(2,1)}, bf16[2,128,256]{2,1,0:T(8,128)(2,1)S(1)}, u32[]{:S(2)}, u32[]{:S(2)}) collective-permute-start(bf16[2,128,256]{2,1,0:T(8,128)(2,1)} %get-tuple-element.57), channel_id=1, source_target_pairs={{4,0},{8,4},{12,8},{16,12},{20,16},{24,20},{28,24},{5,1},{9,5},{13... | collective-permute-start | bytes 393224 | tf_op jit(solution)/shard_map/ppermute | solution.py:33
  35.5 0.1 select_reduce_fusion
  35.6 7.4 %collective-permute-done.2.refs_1_ = bf16[576,256]{1,0:T(8,128)(2,1)S(1)} collective-permute-done((bf16[576,256]{1,0:T(8,128)(2,1)}, bf16[576,256]{1,0:T(8,128)(2,1)S(1)}, u32[]{:S(2)}, u32[]{:S(2)}) %collective-permute-start.2) | collective-permute-done | bytes 294944 | tf_op jit(solution)/shard_map/ppermute | solution.py:38
  43.1 9.7 %collective-permute-done.3.refs_2_ = bf16[576,256]{1,0:T(8,128)(2,1)S(1)} collective-permute-done((bf16[576,256]{1,0:T(8,128)(2,1)}, bf16[576,256]{1,0:T(8,128)(2,1)S(1)}, u32[]{:S(2)}, u32[]{:S(2)}) %collective-permute-start.3) | collective-permute-done | bytes 294944 | tf_op jit(solution)/shard_map/ppermute | solution.py:38
  52.8 0.8 fusion.10
  53.6 2.0 %collective-permute-start.11 = (bf16[4,128,256]{2,1,0:T(8,128)(2,1)}, bf16[4,128,256]{2,1,0:T(8,128)(2,1)}, u32[]{:S(2)}, u32[]{:S(2)}) collective-permute-start(bf16[4,128,256]{2,1,0:T(8,128)(2,1)} %get-tuple-element.94), channel_id=1, source_target_pairs={{0,16},{4,20},{8,24},{12,28},{16,0},{20,4},{24,8},{28,12},{1,17},{... | collective-permute-start | bytes 786440 | tf_op jit(solution)/shard_map/ppermute | solution.py:38
  55.7 0.1 copy.15
  55.7 0.1 sub.13.landing
  55.8 1.5 %collective-permute-start.10 = (bf16[4,128,256]{2,1,0:T(8,128)(2,1)}, bf16[4,128,256]{2,1,0:T(8,128)(2,1)S(1)}, u32[]{:S(2)}, u32[]{:S(2)}) collective-permute-start(bf16[4,128,256]{2,1,0:T(8,128)(2,1)} %get-tuple-element.94), channel_id=1, source_target_pairs={{0,8},{4,12},{8,0},{12,4},{16,24},{20,28},{24,16},{28,20},{1,9},{5... | collective-permute-start | bytes 786440 | tf_op jit(solution)/shard_map/ppermute | solution.py:38
  57.3 0.0 collective-permute-start.12
  57.4 1.0 merge.1
  58.5 0.1 slice_bitcast_fusion.4
  58.5 2.5 %collective-permute-start.9 = (bf16[448,256]{1,0:T(8,128)(2,1)S(1)}, bf16[448,256]{1,0:T(8,128)(2,1)S(1)}, u32[]{:S(2)}, u32[]{:S(2)}) collective-permute-start(bf16[448,256]{1,0:T(8,128)(2,1)S(1)} %get-tuple-element.83), channel_id=1, source_target_pairs={{0,3},{1,2},{2,1},{3,0},{4,7},{5,6},{6,5},{7,4},{8,11},{9,10},{10,... | collective-permute-start | bytes 688136 | tf_op jit(solution)/shard_map/ppermute | solution.py:38
  61.1 5.4 %collective-permute-start.8 = (bf16[448,256]{1,0:T(8,128)(2,1)S(1)}, bf16[448,256]{1,0:T(8,128)(2,1)S(1)}, u32[]{:S(2)}, u32[]{:S(2)}) collective-permute-start(bf16[448,256]{1,0:T(8,128)(2,1)S(1)} %get-tuple-element.84), channel_id=1, source_target_pairs={{0,2},{1,3},{2,0},{3,1},{4,6},{5,7},{6,4},{7,5},{8,10},{9,11},{10,... | collective-permute-start | bytes 688136 | tf_op jit(solution)/shard_map/ppermute | solution.py:38
  66.5 1.3 %collective-permute-start.7 = (bf16[448,256]{1,0:T(8,128)(2,1)S(1)}, bf16[448,256]{1,0:T(8,128)(2,1)S(1)}, u32[]{:S(2)}, u32[]{:S(2)}) collective-permute-start(bf16[448,256]{1,0:T(8,128)(2,1)S(1)} %get-tuple-element.85), channel_id=1, source_target_pairs={{0,1},{1,0},{2,3},{3,2},{4,5},{5,4},{6,7},{7,6},{8,9},{9,8},{10,11... | collective-permute-start | bytes 688136 | tf_op jit(solution)/shard_map/ppermute | solution.py:38
  67.7 0.0 collective-permute-done.10
  67.7 0.7 collective-permute-done.12
  68.5 1.1 pad_maximum_fusion.refs_4_
  69.5 0.0 collective-permute-done.9.refs_7_.refs_3_
  69.6 11.7 %collective-permute-done.8.refs_6_.refs_2_ = bf16[448,256]{1,0:T(8,128)(2,1)S(1)} collective-permute-done((bf16[448,256]{1,0:T(8,128)(2,1)S(1)}, bf16[448,256]{1,0:T(8,128)(2,1)S(1)}, u32[]{:S(2)}, u32[]{:S(2)}) %collective-permute-start.8) | collective-permute-done | bytes 229408 | tf_op jit(solution)/shard_map/ppermute | solution.py:38
  81.2 0.0 collective-permute-done.7.refs_5_.refs_1_
  81.2 0.0 collective-permute-start.13
  81.2 2.6 %weight_partial.1 = (bf16[4,4,128,256]{3,2,1,0:T(8,128)(2,1)S(1)}, bf16[4,4,128,256]{3,2,1,0:T(8,128)(2,1)S(1)}) custom-call(s32[2]{0:T(128)S(1)} %copy-done.1, bf16[576,256]{1,0:T(8,128)(2,1)S(1)} %copy-done.2, bf16[576,256]{1,0:T(8,128)(2,1)S(1)} %collective-permute-done.2.refs_1_, bf16[576,256]{1,0:T(8,128)(2,1)S(1)} %collective-permute-done.3.refs_2_, ...), custom_call_target="tpu_custom_call" | custom-call | flops 939524096 | bytes 3932160 | tf_op jit(solution)/shard_map/weight_partial/pallas_call | solution.py:334
  83.9 0.0 collective-permute-done.13.refs_5_
  83.9 0.6 collective-permute-start.14
  84.5 2.3 %feature_rows.2 = bf16[3,448,256]{2,1,0:T(8,128)(2,1)S(1)} custom-call(s32[2]{0:T(128)S(1)} %copy-done.1, bf16[448,256]{1,0:T(8,128)(2,1)S(1)} %get-tuple-element.69.refs_4_.refs_0_, bf16[448,256]{1,0:T(8,128)(2,1)S(1)} %collective-permute-done.7.refs_5_.refs_1_, bf16[448,256]{1,0:T(8,128)(2,1)S(1)} %collective-permute-done.8.refs_6_.refs_2_, ...), custom_call_target="tpu_custom_call" | custom-call | flops 704643072 | bytes 3178496 | tf_op jit(solution)/shard_map/feature_rows/pallas_call | solution.py:382
  86.8 0.0 collective-permute-done.14
  86.8 0.4 convert_add_fusion
  87.2 0.1 slice_bitcast_fusion.3
  87.3 2.0 %collective-permute-start.15 = (bf16[4,128,256]{2,1,0:T(8,128)(2,1)S(1)}, bf16[4,128,256]{2,1,0:T(8,128)(2,1)S(1)}, u32[]{:S(2)}, u32[]{:S(2)}) collective-permute-start(bf16[4,128,256]{2,1,0:T(8,128)(2,1)S(1)} %get-tuple-element.80), channel_id=1, source_target_pairs={{0,8},{4,12},{8,0},{12,4},{16,24},{20,28},{24,16},{28,20},{1,9},{5... | collective-permute-start | bytes 786440 | tf_op jit(solution)/shard_map/ppermute | solution.py:38
  89.2 1.5 %collective-permute-start.17 = (bf16[4,128,256]{2,1,0:T(8,128)(2,1)S(1)}, bf16[4,128,256]{2,1,0:T(8,128)(2,1)S(1)}, u32[]{:S(2)}, u32[]{:S(2)}) collective-permute-start(bf16[4,128,256]{2,1,0:T(8,128)(2,1)S(1)} %get-tuple-element.81), channel_id=1, source_target_pairs={{0,24},{4,28},{8,16},{12,20},{16,8},{20,12},{24,0},{28,4},{1,25},{... | collective-permute-start | bytes 786440 | tf_op jit(solution)/shard_map/ppermute | solution.py:38
  90.7 0.1 collective-permute-start.16
  90.9 2.6 %collective-permute-start.23 = (bf16[448,256]{1,0:T(8,128)(2,1)S(1)}, bf16[448,256]{1,0:T(8,128)(2,1)S(1)}, u32[]{:S(2)}, u32[]{:S(2)}) collective-permute-start(bf16[448,256]{1,0:T(8,128)(2,1)S(1)} %get-tuple-element.87), channel_id=1, source_target_pairs={{0,3},{1,2},{2,1},{3,0},{4,7},{5,6},{6,5},{7,4},{8,11},{9,10},{10,... | collective-permute-start | bytes 688136 | tf_op jit(solution)/shard_map/ppermute | solution.py:38
  93.5 0.0 collective-permute-start.22
  93.5 3.0 %collective-permute-done.15 = bf16[4,128,256]{2,1,0:T(8,128)(2,1)S(1)} collective-permute-done((bf16[4,128,256]{2,1,0:T(8,128)(2,1)S(1)}, bf16[4,128,256]{2,1,0:T(8,128)(2,1)S(1)}, u32[]{:S(2)}, u32[]{:S(2)}) %collective-permute-start.15) | collective-permute-done | bytes 262176 | tf_op jit(solution)/shard_map/ppermute | solution.py:38
  96.4 0.0 collective-permute-start.21
  96.5 6.5 %collective-permute-done.17 = bf16[4,128,256]{2,1,0:T(8,128)(2,1)S(1)} collective-permute-done((bf16[4,128,256]{2,1,0:T(8,128)(2,1)S(1)}, bf16[4,128,256]{2,1,0:T(8,128)(2,1)S(1)}, u32[]{:S(2)}, u32[]{:S(2)}) %collective-permute-start.17) | collective-permute-done | bytes 262176 | tf_op jit(solution)/shard_map/ppermute | solution.py:38
  102.9 1.4 %collective-permute-done.16 = bf16[4,128,256]{2,1,0:T(8,128)(2,1)S(1)} collective-permute-done((bf16[4,128,256]{2,1,0:T(8,128)(2,1)S(1)}, bf16[4,128,256]{2,1,0:T(8,128)(2,1)S(1)}, u32[]{:S(2)}, u32[]{:S(2)}) %collective-permute-start.16) | collective-permute-done | bytes 262176 | tf_op jit(solution)/shard_map/ppermute | solution.py:38
  104.3 0.2 fusion.11
  104.5 0.1 collective-permute-start.18
  104.6 2.5 %collective-permute-start.20 = (bf16[128,256]{1,0:T(8,128)(2,1)S(1)}, bf16[128,256]{1,0:T(8,128)(2,1)S(1)}, u32[]{:S(2)}, u32[]{:S(2)}) collective-permute-start(bf16[128,256]{1,0:T(8,128)(2,1)S(1)} %get-tuple-element.91), channel_id=1, source_target_pairs={{0,3},{1,2},{2,1},{3,0},{4,7},{5,6},{6,5},{7,4},{8,11},{9,10},{10,... | collective-permute-start | bytes 196616 | tf_op jit(solution)/shard_map/ppermute | solution.py:38
  107.1 0.0 collective-permute-done.23.refs_3_
  107.1 1.3 %collective-permute-start.19 = (bf16[128,256]{1,0:T(8,128)(2,1)S(1)}, bf16[128,256]{1,0:T(8,128)(2,1)S(1)}, u32[]{:S(2)}, u32[]{:S(2)}) collective-permute-start(bf16[128,256]{1,0:T(8,128)(2,1)S(1)} %get-tuple-element.92), channel_id=1, source_target_pairs={{0,2},{1,3},{2,0},{3,1},{4,6},{5,7},{6,4},{7,5},{8,10},{9,11},{10,... | collective-permute-start | bytes 196616 | tf_op jit(solution)/shard_map/ppermute | solution.py:38
  108.4 1.0 feature_rows.3
  109.4 6.7 %collective-permute-done.22.refs_2_ = bf16[448,256]{1,0:T(8,128)(2,1)S(1)} collective-permute-done((bf16[448,256]{1,0:T(8,128)(2,1)S(1)}, bf16[448,256]{1,0:T(8,128)(2,1)S(1)}, u32[]{:S(2)}, u32[]{:S(2)}) %collective-permute-start.22) | collective-permute-done | bytes 229408 | tf_op jit(solution)/shard_map/ppermute | solution.py:38
  116.2 1.5 %laid_out.1 = bf16[1792,256]{1,0:T(8,128)(2,1)} custom-call(s32[2]{0:T(128)S(1)} %copy-done.1, bf16[448,256]{1,0:T(8,128)(2,1)S(1)} %bitcast.61, bf16[448,256]{1,0:T(8,128)(2,1)S(1)} %collective-permute-done.21.refs_1_, bf16[448,256]{1,0:T(8,128)(2,1)S(1)} %collective-permute-done.22.refs_2_, bf16[448,256]{1,0:T(8,128)(2,1)S(1)} %collective-permute-done.23.refs_3_), custom_call_target="tpu_custom_call" | custom-call | tf_op jit(solution)/shard_map/laid_out/pallas_call | solution.py:414
  117.7 0.7 fusion.5
  (30 shorter events, 0.2 us)
Async XLA Ops:
  9.4 3.6 %collective-permute-start = (bf16[2,128,256]{2,1,0:T(8,128)(2,1)}, bf16[2,128,256]{2,1,0:T(8,128)(2,1)S(1)}, u32[]{:S(2)}, u32[]{:S(2)}) collective-permute-start(bf16[2,128,256]{2,1,0:T(8,128)(2,1)} %get-tuple-element.40), channel_id=1, source_target_pairs={{0,4},{4,8},{8,12},{12,16},{16,20},{20,24},{24,28},{1,5},{5,9},{9,... | collective-permute-start | bytes 393224 | tf_op jit(solution)/shard_map/ppermute | solution.py:33
  11.7 5.6 %collective-permute-start.1 = (bf16[2,128,256]{2,1,0:T(8,128)(2,1)}, bf16[2,128,256]{2,1,0:T(8,128)(2,1)S(1)}, u32[]{:S(2)}, u32[]{:S(2)}) collective-permute-start(bf16[2,128,256]{2,1,0:T(8,128)(2,1)} %get-tuple-element.41), channel_id=1, source_target_pairs={{4,0},{8,4},{12,8},{16,12},{20,16},{24,20},{28,24},{5,1},{9,5},{13... | collective-permute-start | bytes 393224 | tf_op jit(solution)/shard_map/ppermute | solution.py:33
  13.0 4.2 %copy-start.4 = (bf16[2,128,256]{2,1,0:T(8,128)(2,1)}, bf16[2,128,256]{2,1,0:T(8,128)(2,1)S(1)}, u32[]{:S(2)}) copy-start(bf16[2,128,256]{2,1,0:T(8,128)(2,1)S(1)} %collective-permute-done.low) | copy-start | bytes 393220
  17.3 0.7 copy-start.5
  17.9 14.0 %copy-start.6 = (s32[112]{0:T(128)S(1)}, s32[112]{0:T(128)}, u32[]{:S(2)}) copy-start(s32[112]{0:T(128)} %shuffle.3) | copy-start | bytes 1348
  17.9 34.8 %copy-start.2 = (bf16[576,256]{1,0:T(8,128)(2,1)S(1)}, bf16[576,256]{1,0:T(8,128)(2,1)}, u32[]{:S(2)}) copy-start(bf16[576,256]{1,0:T(8,128)(2,1)} %get-tuple-element.50.refs_0_) | copy-start | bytes 884740
  20.5 36.9 %copy-start = (bf16[14,128,256]{2,1,0:T(8,128)(2,1)S(1)}, bf16[14,128,256]{2,1,0:T(8,128)(2,1)}, u32[]{:S(2)}) copy-start(bf16[14,128,256]{2,1,0:T(8,128)(2,1)} %get-tuple-element.55.clean) | copy-start | bytes 2752516
  20.6 36.8 %copy-start.1 = (s32[2]{0:T(128)S(1)}, s32[2]{0:T(128)}, u32[]{:S(2)}) copy-start(s32[2]{0:T(128)} %pad_add_fusion.me.index) | copy-start | bytes 28
  20.6 32.2 %all-to-all-start = ((bf16[16,128,256]{2,1,0:T(8,128)(2,1)}), bf16[16,128,256]{2,1,0:T(8,128)(2,1)S(1)}, u32[]{:S(2)}, u32[]{:S(2)}) async-start(bf16[16,128,256]{2,1,0:T(8,128)(2,1)} %patch.1), calls=%async_computation | async-start | bytes 2097152 | tf_op jit(solution)/shard_map/all_to_all | solution.py:42
  27.5 15.5 %collective-permute-start.2 = (bf16[576,256]{1,0:T(8,128)(2,1)}, bf16[576,256]{1,0:T(8,128)(2,1)S(1)}, u32[]{:S(2)}, u32[]{:S(2)}) collective-permute-start(bf16[576,256]{1,0:T(8,128)(2,1)} %get-tuple-element.47), channel_id=1, source_target_pairs={{0,1},{1,0},{2,3},{3,2},{4,5},{5,4},{6,7},{7,6},{8,9},{9,8},{10,11... | collective-permute-start | bytes 884744 | tf_op jit(solution)/shard_map/ppermute | solution.py:38
  29.1 23.6 %collective-permute-start.3 = (bf16[576,256]{1,0:T(8,128)(2,1)}, bf16[576,256]{1,0:T(8,128)(2,1)S(1)}, u32[]{:S(2)}, u32[]{:S(2)}) collective-permute-start(bf16[576,256]{1,0:T(8,128)(2,1)} %get-tuple-element.48), channel_id=1, source_target_pairs={{0,2},{1,3},{2,0},{3,1},{4,6},{5,7},{6,4},{7,5},{8,10},{9,11},{10,... | collective-permute-start | bytes 884744 | tf_op jit(solution)/shard_map/ppermute | solution.py:38
  31.7 21.0 %collective-permute-start.4 = (bf16[576,256]{1,0:T(8,128)(2,1)}, bf16[576,256]{1,0:T(8,128)(2,1)S(1)}, u32[]{:S(2)}, u32[]{:S(2)}) collective-permute-start(bf16[576,256]{1,0:T(8,128)(2,1)} %get-tuple-element.49), channel_id=1, source_target_pairs={{0,3},{1,2},{2,1},{3,0},{4,7},{5,6},{6,5},{7,4},{8,11},{9,10},{10,... | collective-permute-start | bytes 884744 | tf_op jit(solution)/shard_map/ppermute | solution.py:38
  32.5 24.8 %collective-permute-start.5 = (bf16[2,128,256]{2,1,0:T(8,128)(2,1)}, bf16[2,128,256]{2,1,0:T(8,128)(2,1)S(1)}, u32[]{:S(2)}, u32[]{:S(2)}) collective-permute-start(bf16[2,128,256]{2,1,0:T(8,128)(2,1)} %get-tuple-element.56), channel_id=1, source_target_pairs={{0,4},{4,8},{8,12},{12,16},{16,20},{20,24},{24,28},{1,5},{5,9},{9,... | collective-permute-start | bytes 393224 | tf_op jit(solution)/shard_map/ppermute | solution.py:33
  34.2 23.2 %collective-permute-start.6 = (bf16[2,128,256]{2,1,0:T(8,128)(2,1)}, bf16[2,128,256]{2,1,0:T(8,128)(2,1)S(1)}, u32[]{:S(2)}, u32[]{:S(2)}) collective-permute-start(bf16[2,128,256]{2,1,0:T(8,128)(2,1)} %get-tuple-element.57), channel_id=1, source_target_pairs={{4,0},{8,4},{12,8},{16,12},{20,16},{24,20},{28,24},{5,1},{9,5},{13... | collective-permute-start | bytes 393224 | tf_op jit(solution)/shard_map/ppermute | solution.py:33
  53.6 12.8 %collective-permute-start.11 = (bf16[4,128,256]{2,1,0:T(8,128)(2,1)}, bf16[4,128,256]{2,1,0:T(8,128)(2,1)}, u32[]{:S(2)}, u32[]{:S(2)}) collective-permute-start(bf16[4,128,256]{2,1,0:T(8,128)(2,1)} %get-tuple-element.94), channel_id=1, source_target_pairs={{0,16},{4,20},{8,24},{12,28},{16,0},{20,4},{24,8},{28,12},{1,17},{... | collective-permute-start | bytes 786440 | tf_op jit(solution)/shard_map/ppermute | solution.py:38
  55.8 12.6 %copy-start.3 = (bf16[1,4,128,256]{3,2,1,0:T(8,128)(2,1)S(1)}, bf16[1,4,128,256]{3,2,1,0:T(8,128)(2,1)}, u32[]{:S(2)}) copy-start(bf16[1,4,128,256]{3,2,1,0:T(8,128)(2,1)} %get-tuple-element.93) | copy-start | bytes 786436
  55.8 11.9 %collective-permute-start.10 = (bf16[4,128,256]{2,1,0:T(8,128)(2,1)}, bf16[4,128,256]{2,1,0:T(8,128)(2,1)S(1)}, u32[]{:S(2)}, u32[]{:S(2)}) collective-permute-start(bf16[4,128,256]{2,1,0:T(8,128)(2,1)} %get-tuple-element.94), channel_id=1, source_target_pairs={{0,8},{4,12},{8,0},{12,4},{16,24},{20,28},{24,16},{28,20},{1,9},{5... | collective-permute-start | bytes 786440 | tf_op jit(solution)/shard_map/ppermute | solution.py:38
  57.3 11.1 %collective-permute-start.12 = (bf16[4,128,256]{2,1,0:T(8,128)(2,1)}, bf16[4,128,256]{2,1,0:T(8,128)(2,1)S(1)}, u32[]{:S(2)}, u32[]{:S(2)}) collective-permute-start(bf16[4,128,256]{2,1,0:T(8,128)(2,1)} %get-tuple-element.94), channel_id=1, source_target_pairs={{0,24},{4,28},{8,16},{12,20},{16,8},{20,12},{24,0},{28,4},{1,25},{... | collective-permute-start | bytes 786440 | tf_op jit(solution)/shard_map/ppermute | solution.py:38
  58.5 11.0 %collective-permute-start.9 = (bf16[448,256]{1,0:T(8,128)(2,1)S(1)}, bf16[448,256]{1,0:T(8,128)(2,1)S(1)}, u32[]{:S(2)}, u32[]{:S(2)}) collective-permute-start(bf16[448,256]{1,0:T(8,128)(2,1)S(1)} %get-tuple-element.83), channel_id=1, source_target_pairs={{0,3},{1,2},{2,1},{3,0},{4,7},{5,6},{6,5},{7,4},{8,11},{9,10},{10,... | collective-permute-start | bytes 688136 | tf_op jit(solution)/shard_map/ppermute | solution.py:38
  61.1 20.2 %collective-permute-start.8 = (bf16[448,256]{1,0:T(8,128)(2,1)S(1)}, bf16[448,256]{1,0:T(8,128)(2,1)S(1)}, u32[]{:S(2)}, u32[]{:S(2)}) collective-permute-start(bf16[448,256]{1,0:T(8,128)(2,1)S(1)} %get-tuple-element.84), channel_id=1, source_target_pairs={{0,2},{1,3},{2,0},{3,1},{4,6},{5,7},{6,4},{7,5},{8,10},{9,11},{10,... | collective-permute-start | bytes 688136 | tf_op jit(solution)/shard_map/ppermute | solution.py:38
  66.5 14.8 %collective-permute-start.7 = (bf16[448,256]{1,0:T(8,128)(2,1)S(1)}, bf16[448,256]{1,0:T(8,128)(2,1)S(1)}, u32[]{:S(2)}, u32[]{:S(2)}) collective-permute-start(bf16[448,256]{1,0:T(8,128)(2,1)S(1)} %get-tuple-element.85), channel_id=1, source_target_pairs={{0,1},{1,0},{2,3},{3,2},{4,5},{5,4},{6,7},{7,6},{8,9},{9,8},{10,11... | collective-permute-start | bytes 688136 | tf_op jit(solution)/shard_map/ppermute | solution.py:38
  81.2 2.7 %collective-permute-start.13 = (bf16[4,4,128,256]{3,2,1,0:T(8,128)(2,1)S(1)}, bf16[4,4,128,256]{3,2,1,0:T(8,128)(2,1)S(1)}, u32[]{:S(2)}, u32[]{:S(2)}) collective-permute-start(bf16[4,4,128,256]{3,2,1,0:T(8,128)(2,1)S(1)} %pad_maximum_fusion.refs_4_), channel_id=1, source_target_pairs={{0,4},{4,0},{8,12},{12,8},{16,20},{20,16},{24,28},{28,24},{1,5},{5... | collective-permute-start | bytes 3145736 | tf_op jit(solution)/shard_map/ppermute | solution.py:38
  83.9 2.9 %collective-permute-start.14 = (bf16[4,4,128,256]{3,2,1,0:T(8,128)(2,1)S(1)}, bf16[4,4,128,256]{3,2,1,0:T(8,128)(2,1)S(1)}, u32[]{:S(2)}, u32[]{:S(2)}) collective-permute-start(bf16[4,4,128,256]{3,2,1,0:T(8,128)(2,1)S(1)} %get-tuple-element.66), channel_id=1, source_target_pairs={{0,4},{4,0},{8,12},{12,8},{16,20},{20,16},{24,28},{28,24},{1,5},{5... | collective-permute-start | bytes 3145736 | tf_op jit(solution)/shard_map/ppermute | solution.py:38
  87.3 9.2 %collective-permute-start.15 = (bf16[4,128,256]{2,1,0:T(8,128)(2,1)S(1)}, bf16[4,128,256]{2,1,0:T(8,128)(2,1)S(1)}, u32[]{:S(2)}, u32[]{:S(2)}) collective-permute-start(bf16[4,128,256]{2,1,0:T(8,128)(2,1)S(1)} %get-tuple-element.80), channel_id=1, source_target_pairs={{0,8},{4,12},{8,0},{12,4},{16,24},{20,28},{24,16},{28,20},{1,9},{5... | collective-permute-start | bytes 786440 | tf_op jit(solution)/shard_map/ppermute | solution.py:38
  89.2 13.7 %collective-permute-start.17 = (bf16[4,128,256]{2,1,0:T(8,128)(2,1)S(1)}, bf16[4,128,256]{2,1,0:T(8,128)(2,1)S(1)}, u32[]{:S(2)}, u32[]{:S(2)}) collective-permute-start(bf16[4,128,256]{2,1,0:T(8,128)(2,1)S(1)} %get-tuple-element.81), channel_id=1, source_target_pairs={{0,24},{4,28},{8,16},{12,20},{16,8},{20,12},{24,0},{28,4},{1,25},{... | collective-permute-start | bytes 786440 | tf_op jit(solution)/shard_map/ppermute | solution.py:38
  90.7 13.6 %collective-permute-start.16 = (bf16[4,128,256]{2,1,0:T(8,128)(2,1)S(1)}, bf16[4,128,256]{2,1,0:T(8,128)(2,1)S(1)}, u32[]{:S(2)}, u32[]{:S(2)}) collective-permute-start(bf16[4,128,256]{2,1,0:T(8,128)(2,1)S(1)} %get-tuple-element.82), channel_id=1, source_target_pairs={{0,16},{4,20},{8,24},{12,28},{16,0},{20,4},{24,8},{28,12},{1,17},{... | collective-permute-start | bytes 786440 | tf_op jit(solution)/shard_map/ppermute | solution.py:38
  90.9 16.2 %collective-permute-start.23 = (bf16[448,256]{1,0:T(8,128)(2,1)S(1)}, bf16[448,256]{1,0:T(8,128)(2,1)S(1)}, u32[]{:S(2)}, u32[]{:S(2)}) collective-permute-start(bf16[448,256]{1,0:T(8,128)(2,1)S(1)} %get-tuple-element.87), channel_id=1, source_target_pairs={{0,3},{1,2},{2,1},{3,0},{4,7},{5,6},{6,5},{7,4},{8,11},{9,10},{10,... | collective-permute-start | bytes 688136 | tf_op jit(solution)/shard_map/ppermute | solution.py:38
  93.5 22.7 %collective-permute-start.22 = (bf16[448,256]{1,0:T(8,128)(2,1)S(1)}, bf16[448,256]{1,0:T(8,128)(2,1)S(1)}, u32[]{:S(2)}, u32[]{:S(2)}) collective-permute-start(bf16[448,256]{1,0:T(8,128)(2,1)S(1)} %get-tuple-element.88), channel_id=1, source_target_pairs={{0,2},{1,3},{2,0},{3,1},{4,6},{5,7},{6,4},{7,5},{8,10},{9,11},{10,... | collective-permute-start | bytes 688136 | tf_op jit(solution)/shard_map/ppermute | solution.py:38
  96.4 19.7 %collective-permute-start.21 = (bf16[448,256]{1,0:T(8,128)(2,1)S(1)}, bf16[448,256]{1,0:T(8,128)(2,1)S(1)}, u32[]{:S(2)}, u32[]{:S(2)}) collective-permute-start(bf16[448,256]{1,0:T(8,128)(2,1)S(1)} %get-tuple-element.89), channel_id=1, source_target_pairs={{0,1},{1,0},{2,3},{3,2},{4,5},{5,4},{6,7},{7,6},{8,9},{9,8},{10,11... | collective-permute-start | bytes 688136 | tf_op jit(solution)/shard_map/ppermute | solution.py:38
  104.5 13.2 %collective-permute-start.18 = (bf16[128,256]{1,0:T(8,128)(2,1)S(1)}, bf16[128,256]{1,0:T(8,128)(2,1)S(1)}, u32[]{:S(2)}, u32[]{:S(2)}) collective-permute-start(bf16[128,256]{1,0:T(8,128)(2,1)S(1)} %get-tuple-element.90), channel_id=1, source_target_pairs={{0,1},{1,0},{2,3},{3,2},{4,5},{5,4},{6,7},{7,6},{8,9},{9,8},{10,11... | collective-permute-start | bytes 196616 | tf_op jit(solution)/shard_map/ppermute | solution.py:38
  104.6 13.1 %collective-permute-start.20 = (bf16[128,256]{1,0:T(8,128)(2,1)S(1)}, bf16[128,256]{1,0:T(8,128)(2,1)S(1)}, u32[]{:S(2)}, u32[]{:S(2)}) collective-permute-start(bf16[128,256]{1,0:T(8,128)(2,1)S(1)} %get-tuple-element.91), channel_id=1, source_target_pairs={{0,3},{1,2},{2,1},{3,0},{4,7},{5,6},{6,5},{7,4},{8,11},{9,10},{10,... | collective-permute-start | bytes 196616 | tf_op jit(solution)/shard_map/ppermute | solution.py:38
  107.1 10.6 %collective-permute-start.19 = (bf16[128,256]{1,0:T(8,128)(2,1)S(1)}, bf16[128,256]{1,0:T(8,128)(2,1)S(1)}, u32[]{:S(2)}, u32[]{:S(2)}) collective-permute-start(bf16[128,256]{1,0:T(8,128)(2,1)S(1)} %get-tuple-element.92), channel_id=1, source_target_pairs={{0,2},{1,3},{2,0},{3,1},{4,6},{5,7},{6,4},{7,5},{8,10},{9,11},{10,... | collective-permute-start | bytes 196616 | tf_op jit(solution)/shard_map/ppermute | solution.py:38

commit v14 on v13

--- a/solution.py
+++ b/solution.py
@@ -262,8 +262,11 @@
     )(index, shuffle, outgoing, low, high)
 
 
-def merge_kernel(quarter, index, landing, clean, low, high, incoming, out, whole):
+def merge_kernel(quarter, index, landing, clean, low, high, incoming, *refs):
+    *packed, out, tiles, whole = refs
     blocks, rows, _ = clean.shape
+    for i, piece in enumerate(packed):
+        tiles[i] = piece[quarter:]
     reach = low.shape[0]
     group = index[1]
     piece = math.gcd(rows, quarter)
@@ -287,18 +290,20 @@
                 ]
 
 
-def merge(index, landing, clean, low, high, incoming, groups):
+def merge(index, landing, clean, low, high, incoming, packed):
     blocks, rows, width = clean.shape
+    groups = len(packed)
     quarter = blocks * rows // groups
+    height = packed[0].shape[0] - quarter
     return pl.pallas_call(
         functools.partial(merge_kernel, quarter),
-        in_specs=[IN_SMEM] * 2 + [IN_VMEM] * 4,
-        out_specs=IN_VMEM,
-        out_shape=bf16(groups, quarter, width),
+        in_specs=[IN_SMEM] * 2 + [IN_VMEM] * (4 + groups),
+        out_specs=[IN_VMEM] * 2,
+        out_shape=[bf16(groups, quarter, width), bf16(groups, height, width)],
         scratch_shapes=[pltpu.VMEM((blocks, rows, width), jnp.float32)],
         compiler_params=params(),
         name="merge",
-    )(index, landing, clean, low, high, incoming)
+    )(index, landing, clean, low, high, incoming, *packed)
 
 
 def weight_kernel(devs, index, *refs):
@@ -475,13 +480,11 @@
     landing = landing_blocks(shuffle_from, me, blocks, devs, slots)
     incoming = exchanged(outgoing, "node")
     incoming, packed = lax.optimization_barrier((incoming, packed))
-    merged = merge(index, landing, clean, low, high, incoming, groups)
-
-    quarter = row_count // groups
+    merged, tiles = merge(index, landing, clean, low, high, incoming, packed)
+
     summed = [merged[0]] + [None] * (groups - 1)
     for i in exchange_order(groups):
         summed[i] = swapped(merged[i], "chan", i)
-    tiles = jnp.stack([piece[quarter:] for piece in packed])
     even = [tiles] + [swapped(tiles, "node", 2 * i) for i in range(1, devs // 2)]
     even = jnp.stack(even)
     summed, even = lax.optimization_barrier((summed, even))

time: 119 us -> 109 us (0.916)
  waiting for transfers between devices: 51.4 us -> 43 us
  other arithmetic: 4.27 us -> 2.48 us
    ppermute x20, waiting for transfers between devices: 47.1 us -> 36.9 us  [swapped(): return lax.ppermute(value, axis, [(i, i ^ by) for i in range(size)])]
    all_to_all x1, waiting for transfers between devices: 0.01 us -> 6.05 us  [exchanged(): return lax.all_to_all(value, axis, split_axis=0, concat_axis=0, tiled=True)]
    ppermute x4, waiting for transfers between devices: 4.24 us -> 0.01 us  [shifted(): return lax.ppermute(value, axis, pairs)]
    another operation x2 -> x1, other arithmetic: 1.93 us -> 0.13 us  [local(): even = jnp.stack(even)]
  transfers between devices with their start and end apart: 25 -> 25, of which waited for: 9 -> 9; matrix products, arithmetic and copies ran while one was open for 3% -> 1% of each run, Pallas kernels for 7% -> 9%
where the time goes in v14:
time: 109 us
  waiting for transfers between devices  43 us (39%)
  starting transfers between devices  42.2 us (39%)
  Pallas kernels  19.2 us (18%)
  other arithmetic  2.48 us (2%)
  local copies, waits for them, and re-layouts  1.3 us (1%)
    ppermute x20, waiting for transfers between devices, swapped(): return lax.ppermute(value, axis, [(i, i ^ by) for i in range(size)])  36.9 us
    ppermute x20, starting transfers between devices, swapped(): return lax.ppermute(value, axis, [(i, i ^ by) for i in range(size)])  28.4 us
    pallas_call x1, Pallas kernels, aggregate(): pl.pallas_call(functools.partial(aggregate_kernel, reach, groups, send_sl...  8.1 us
    ppermute x4, starting transfers between devices, shifted(): return lax.ppermute(value, axis, pairs)  7.38 us
    all_to_all x1, starting transfers between devices, exchanged(): return lax.all_to_all(value, axis, split_axis=0, concat_axis=0, tiled=True)  6.47 us
    all_to_all x1, waiting for transfers between devices, exchanged(): return lax.all_to_all(value, axis, split_axis=0, concat_axis=0, tiled=True)  6.05 us
    pallas_call x2, Pallas kernels, feature_rows(): pl.pallas_call(functools.partial(feature_kernel, first), in_specs=[IN_SME...  3.34 us
    pallas_call x1, Pallas kernels, patch(): pl.pallas_call(functools.partial(patch_kernel, reach, blocks, slots), in_...  2.62 us
  transfers between devices with their start and end apart: 25, of which 9 were waited for; matrix products, arithmetic and copies ran while one was open for 1% of the time, Pallas kernels for 9%

profile of v14, /device:TPU:0, one launch (start us, length us, event | category | flops | bytes accessed | tf_op | source)
XLA Modules:
  0.0 109.1 jit_solution(9157975497543207132)
XLA Ops:
  0.6 0.6 pad_add_fusion.me.index
  1.3 8.1 %aggregate.1 = (bf16[14,128,256]{2,1,0:T(8,128)(2,1)}, bf16[16,128,256]{2,1,0:T(8,128)(2,1)}, bf16[2,128,256]{2,1,0:T(8,128)(2,1)}, bf16[2,128,256]{2,1,0:T(8,12...) custom-call(s32[2]{0:T(128)} %pad_add_fusion.me.index, ...), custom_call_target="tpu_custom_call" | custom-call | flops 1174405120 | bytes 7798784 | tf_op jit(solution)/shard_map/aggregate/pallas_call | solution.py:184
  9.4 2.4 %collective-permute-start = (bf16[2,128,256]{2,1,0:T(8,128)(2,1)}, bf16[2,128,256]{2,1,0:T(8,128)(2,1)S(1)}, u32[]{:S(2)}, u32[]{:S(2)}) collective-permute-start(bf16[2,128,256]{2,1,0:T(8,128)(2,1)} %get-tuple-element.42), channel_id=1, source_target_pairs={{0,4},{4,8},{8,12},{12,16},{16,20},{20,24},{24,28},{1,5},{5,9},{9,... | collective-permute-start | bytes 393224 | tf_op jit(solution)/shard_map/ppermute | solution.py:33
  11.8 1.3 %collective-permute-start.1 = (bf16[2,128,256]{2,1,0:T(8,128)(2,1)}, bf16[2,128,256]{2,1,0:T(8,128)(2,1)S(1)}, u32[]{:S(2)}, u32[]{:S(2)}) collective-permute-start(bf16[2,128,256]{2,1,0:T(8,128)(2,1)} %get-tuple-element.43), channel_id=1, source_target_pairs={{4,0},{8,4},{12,8},{16,12},{20,16},{24,20},{28,24},{5,1},{9,5},{13... | collective-permute-start | bytes 393224 | tf_op jit(solution)/shard_map/ppermute | solution.py:33
  13.1 2.5 %collective-permute-start.2 = (bf16[576,256]{1,0:T(8,128)(2,1)}, bf16[576,256]{1,0:T(8,128)(2,1)S(1)}, u32[]{:S(2)}, u32[]{:S(2)}) collective-permute-start(bf16[576,256]{1,0:T(8,128)(2,1)} %get-tuple-element.49), channel_id=1, source_target_pairs={{0,1},{1,0},{2,3},{3,2},{4,5},{5,4},{6,7},{7,6},{8,9},{9,8},{10,11... | collective-permute-start | bytes 884744 | tf_op jit(solution)/shard_map/ppermute | solution.py:38
  15.5 2.6 %collective-permute-start.3 = (bf16[576,256]{1,0:T(8,128)(2,1)}, bf16[576,256]{1,0:T(8,128)(2,1)S(1)}, u32[]{:S(2)}, u32[]{:S(2)}) collective-permute-start(bf16[576,256]{1,0:T(8,128)(2,1)} %get-tuple-element.50), channel_id=1, source_target_pairs={{0,2},{1,3},{2,0},{3,1},{4,6},{5,7},{6,4},{7,5},{8,10},{9,11},{10,... | collective-permute-start | bytes 884744 | tf_op jit(solution)/shard_map/ppermute | solution.py:38
  18.1 0.0 collective-permute-done.1.high
  18.2 0.6 copy-done.3
  18.8 0.1 copy-done.4
  18.9 2.6 %patch.1 = bf16[16,128,256]{2,1,0:T(8,128)(2,1)} custom-call(s32[2]{0:T(128)} %pad_add_fusion.me.index, s32[112]{0:T(128)} %shuffle.3, bf16[16,128,256]{2,1,0:T(8,128)(2,1)} %get-tuple-element.41.outgoing, bf16[2,128,256]{2,1,0:T(8,128)(2,1)} %copy-done.3, bf16[2,128,256]{2,1,0:T(8,128)(2,1)} %copy-done.4), custom_call_target="tpu_custom_call", output_to_operand_aliasing={{}: (2, {})} | custom-call | tf_op jit(solution)/shard_map/patch/pallas_call | solution.py:246
  21.5 6.5 %all-to-all-start = ((bf16[16,128,256]{2,1,0:T(8,128)(2,1)}), bf16[16,128,256]{2,1,0:T(8,128)(2,1)S(1)}, u32[]{:S(2)}, u32[]{:S(2)}) async-start(bf16[16,128,256]{2,1,0:T(8,128)(2,1)} %patch.1), calls=%async_computation | async-start | bytes 2097152 | tf_op jit(solution)/shard_map/all_to_all | solution.py:42
  28.0 0.1 eq.30
  28.1 0.1 add.45
  28.2 0.3 convert_reduce_fusion
  28.5 0.1 copy.14
  28.6 2.4 %collective-permute-start.5 = (bf16[2,128,256]{2,1,0:T(8,128)(2,1)}, bf16[2,128,256]{2,1,0:T(8,128)(2,1)S(1)}, u32[]{:S(2)}, u32[]{:S(2)}) collective-permute-start(bf16[2,128,256]{2,1,0:T(8,128)(2,1)} %get-tuple-element.58), channel_id=1, source_target_pairs={{0,4},{4,8},{8,12},{12,16},{16,20},{20,24},{24,28},{1,5},{5,9},{9,... | collective-permute-start | bytes 393224 | tf_op jit(solution)/shard_map/ppermute | solution.py:33
  31.1 1.3 %collective-permute-start.6 = (bf16[2,128,256]{2,1,0:T(8,128)(2,1)S(1)}, bf16[2,128,256]{2,1,0:T(8,128)(2,1)S(1)}, u32[]{:S(2)}, u32[]{:S(2)}) collective-permute-start(bf16[2,128,256]{2,1,0:T(8,128)(2,1)S(1)} %copy-done.6), channel_id=1, source_target_pairs={{4,0},{8,4},{12,8},{16,12},{20,16},{24,20},{28,24},{5,1},{9,5},{13... | collective-permute-start | bytes 393224 | tf_op jit(solution)/shard_map/ppermute | solution.py:33
  32.4 0.1 select_reduce_fusion
  32.5 0.1 copy.15
  32.6 0.1 sub.13.landing
  32.7 0.0 collective-permute-done.2.refs_1_
  32.7 0.0 collective-permute-done.3.refs_2_
  32.7 4.7 %collective-permute-done.4.refs_3_ = bf16[576,256]{1,0:T(8,128)(2,1)S(1)} collective-permute-done((bf16[576,256]{1,0:T(8,128)(2,1)}, bf16[576,256]{1,0:T(8,128)(2,1)S(1)}, u32[]{:S(2)}, u32[]{:S(2)}) %collective-permute-start.4) | collective-permute-done | bytes 294944 | tf_op jit(solution)/shard_map/ppermute | solution.py:38
  37.4 6.0 %all-to-all-done.incoming = bf16[16,128,256]{2,1,0:T(8,128)(2,1)S(1)} async-done(((bf16[16,128,256]{2,1,0:T(8,128)(2,1)}), bf16[16,128,256]{2,1,0:T(8,128)(2,1)S(1)}, u32[]{:S(2)}, u32[]{:S(2)}) %all-to-all-start) | async-done | bytes 1048608 | tf_op jit(solution)/shard_map/all_to_all | solution.py:42
  43.4 0.0 collective-permute-done.5.low
  43.4 0.0 collective-permute-done.6.high
  43.4 1.1 merge.1
  44.5 2.8 %collective-permute-start.12 = (bf16[4,128,256]{2,1,0:T(8,128)(2,1)S(1)}, bf16[4,128,256]{2,1,0:T(8,128)(2,1)S(1)}, u32[]{:S(2)}, u32[]{:S(2)}) collective-permute-start(bf16[4,128,256]{2,1,0:T(8,128)(2,1)S(1)} %get-tuple-element.62), channel_id=1, source_target_pairs={{0,24},{4,28},{8,16},{12,20},{16,8},{20,12},{24,0},{28,4},{1,25},{... | collective-permute-start | bytes 786440 | tf_op jit(solution)/shard_map/ppermute | solution.py:38
  47.3 0.2 collective-permute-start.11
  47.5 1.4 %collective-permute-start.10 = (bf16[4,128,256]{2,1,0:T(8,128)(2,1)S(1)}, bf16[4,128,256]{2,1,0:T(8,128)(2,1)S(1)}, u32[]{:S(2)}, u32[]{:S(2)}) collective-permute-start(bf16[4,128,256]{2,1,0:T(8,128)(2,1)S(1)} %get-tuple-element.62), channel_id=1, source_target_pairs={{0,8},{4,12},{8,0},{12,4},{16,24},{20,28},{24,16},{28,20},{1,9},{5... | collective-permute-start | bytes 786440 | tf_op jit(solution)/shard_map/ppermute | solution.py:38
  48.9 0.1 slice_bitcast_fusion.7
  49.0 4.0 %collective-permute-start.9 = (bf16[448,256]{1,0:T(8,128)(2,1)S(1)}, bf16[448,256]{1,0:T(8,128)(2,1)S(1)}, u32[]{:S(2)}, u32[]{:S(2)}) collective-permute-start(bf16[448,256]{1,0:T(8,128)(2,1)S(1)} %get-tuple-element.87), channel_id=1, source_target_pairs={{0,3},{1,2},{2,1},{3,0},{4,7},{5,6},{6,5},{7,4},{8,11},{9,10},{10,... | collective-permute-start | bytes 688136 | tf_op jit(solution)/shard_map/ppermute | solution.py:38
  53.0 0.0 collective-permute-start.8
  53.0 1.1 %collective-permute-done.12 = bf16[4,128,256]{2,1,0:T(8,128)(2,1)S(1)} collective-permute-done((bf16[4,128,256]{2,1,0:T(8,128)(2,1)S(1)}, bf16[4,128,256]{2,1,0:T(8,128)(2,1)S(1)}, u32[]{:S(2)}, u32[]{:S(2)}) %collective-permute-start.12) | collective-permute-done | bytes 262176 | tf_op jit(solution)/shard_map/ppermute | solution.py:38
  54.1 2.9 %collective-permute-start.7 = (bf16[448,256]{1,0:T(8,128)(2,1)S(1)}, bf16[448,256]{1,0:T(8,128)(2,1)S(1)}, u32[]{:S(2)}, u32[]{:S(2)}) collective-permute-start(bf16[448,256]{1,0:T(8,128)(2,1)S(1)} %get-tuple-element.89), channel_id=1, source_target_pairs={{0,1},{1,0},{2,3},{3,2},{4,5},{5,4},{6,7},{7,6},{8,9},{9,8},{10,11... | collective-permute-start | bytes 688136 | tf_op jit(solution)/shard_map/ppermute | solution.py:38
  57.0 3.3 %collective-permute-done.11 = bf16[4,128,256]{2,1,0:T(8,128)(2,1)S(1)} collective-permute-done((bf16[4,128,256]{2,1,0:T(8,128)(2,1)S(1)}, bf16[4,128,256]{2,1,0:T(8,128)(2,1)S(1)}, u32[]{:S(2)}, u32[]{:S(2)}) %collective-permute-start.11) | collective-permute-done | bytes 262176 | tf_op jit(solution)/shard_map/ppermute | solution.py:38
  60.3 0.1 pad_maximum_fusion.refs_4_
  60.4 0.0 collective-permute-done.9.refs_7_.refs_3_
  60.4 11.8 %collective-permute-done.8.refs_6_.refs_2_ = bf16[448,256]{1,0:T(8,128)(2,1)S(1)} collective-permute-done((bf16[448,256]{1,0:T(8,128)(2,1)S(1)}, bf16[448,256]{1,0:T(8,128)(2,1)S(1)}, u32[]{:S(2)}, u32[]{:S(2)}) %collective-permute-start.8) | collective-permute-done | bytes 229408 | tf_op jit(solution)/shard_map/ppermute | solution.py:38
  72.2 2.6 %weight_partial.1 = (bf16[4,4,128,256]{3,2,1,0:T(8,128)(2,1)S(1)}, bf16[4,4,128,256]{3,2,1,0:T(8,128)(2,1)S(1)}) custom-call(s32[2]{0:T(128)S(1)} %copy-done.2, bf16[576,256]{1,0:T(8,128)(2,1)S(1)} %copy-done.1, bf16[576,256]{1,0:T(8,128)(2,1)S(1)} %collective-permute-done.2.refs_1_, bf16[576,256]{1,0:T(8,128)(2,1)S(1)} %collective-permute-done.3.refs_2_, ...), custom_call_target="tpu_custom_call" | custom-call | flops 939524096 | bytes 3932160 | tf_op jit(solution)/shard_map/weight_partial/pallas_call | solution.py:339
  74.9 0.0 collective-permute-done.13.refs_5_
  74.9 0.5 collective-permute-start.14
  75.4 2.3 %feature_rows.2 = bf16[3,448,256]{2,1,0:T(8,128)(2,1)S(1)} custom-call(s32[2]{0:T(128)S(1)} %copy-done.2, bf16[448,256]{1,0:T(8,128)(2,1)S(1)} %get-tuple-element.73.refs_4_.refs_0_, bf16[448,256]{1,0:T(8,128)(2,1)S(1)} %collective-permute-done.7.refs_5_.refs_1_, bf16[448,256]{1,0:T(8,128)(2,1)S(1)} %collective-permute-done.8.refs_6_.refs_2_, ...), custom_call_target="tpu_custom_call" | custom-call | flops 704643072 | bytes 3178496 | tf_op jit(solution)/shard_map/feature_rows/pallas_call | solution.py:387
  77.8 0.0 collective-permute-done.14
  77.8 0.4 convert_add_fusion
  78.2 0.1 slice_bitcast_fusion.3
  78.2 1.1 %collective-permute-start.15 = (bf16[4,128,256]{2,1,0:T(8,128)(2,1)S(1)}, bf16[4,128,256]{2,1,0:T(8,128)(2,1)S(1)}, u32[]{:S(2)}, u32[]{:S(2)}) collective-permute-start(bf16[4,128,256]{2,1,0:T(8,128)(2,1)S(1)} %get-tuple-element.84), channel_id=1, source_target_pairs={{0,8},{4,12},{8,0},{12,4},{16,24},{20,28},{24,16},{28,20},{1,9},{5... | collective-permute-start | bytes 786440 | tf_op jit(solution)/shard_map/ppermute | solution.py:38
  79.4 0.7 collective-permute-start.17
  80.0 1.7 %collective-permute-start.16 = (bf16[4,128,256]{2,1,0:T(8,128)(2,1)S(1)}, bf16[4,128,256]{2,1,0:T(8,128)(2,1)S(1)}, u32[]{:S(2)}, u32[]{:S(2)}) collective-permute-start(bf16[4,128,256]{2,1,0:T(8,128)(2,1)S(1)} %get-tuple-element.86), channel_id=1, source_target_pairs={{0,16},{4,20},{8,24},{12,28},{16,0},{20,4},{24,8},{28,12},{1,17},{... | collective-permute-start | bytes 786440 | tf_op jit(solution)/shard_map/ppermute | solution.py:38
  81.8 2.5 %collective-permute-start.23 = (bf16[448,256]{1,0:T(8,128)(2,1)S(1)}, bf16[448,256]{1,0:T(8,128)(2,1)S(1)}, u32[]{:S(2)}, u32[]{:S(2)}) collective-permute-start(bf16[448,256]{1,0:T(8,128)(2,1)S(1)} %get-tuple-element.91), channel_id=1, source_target_pairs={{0,3},{1,2},{2,1},{3,0},{4,7},{5,6},{6,5},{7,4},{8,11},{9,10},{10,... | collective-permute-start | bytes 688136 | tf_op jit(solution)/shard_map/ppermute | solution.py:38
  84.4 3.0 %collective-permute-done.15 = bf16[4,128,256]{2,1,0:T(8,128)(2,1)S(1)} collective-permute-done((bf16[4,128,256]{2,1,0:T(8,128)(2,1)S(1)}, bf16[4,128,256]{2,1,0:T(8,128)(2,1)S(1)}, u32[]{:S(2)}, u32[]{:S(2)}) %collective-permute-start.15) | collective-permute-done | bytes 262176 | tf_op jit(solution)/shard_map/ppermute | solution.py:38
  87.4 0.0 collective-permute-start.21
  87.4 4.8 %collective-permute-done.17 = bf16[4,128,256]{2,1,0:T(8,128)(2,1)S(1)} collective-permute-done((bf16[4,128,256]{2,1,0:T(8,128)(2,1)S(1)}, bf16[4,128,256]{2,1,0:T(8,128)(2,1)S(1)}, u32[]{:S(2)}, u32[]{:S(2)}) %collective-permute-start.17) | collective-permute-done | bytes 262176 | tf_op jit(solution)/shard_map/ppermute | solution.py:38
  92.2 1.4 %collective-permute-done.16 = bf16[4,128,256]{2,1,0:T(8,128)(2,1)S(1)} collective-permute-done((bf16[4,128,256]{2,1,0:T(8,128)(2,1)S(1)}, bf16[4,128,256]{2,1,0:T(8,128)(2,1)S(1)}, u32[]{:S(2)}, u32[]{:S(2)}) %collective-permute-start.16) | collective-permute-done | bytes 262176 | tf_op jit(solution)/shard_map/ppermute | solution.py:38
  93.6 0.1 fusion.10
  93.8 0.1 collective-permute-start.18
  93.8 2.5 %collective-permute-start.20 = (bf16[128,256]{1,0:T(8,128)(2,1)S(1)}, bf16[128,256]{1,0:T(8,128)(2,1)S(1)}, u32[]{:S(2)}, u32[]{:S(2)}) collective-permute-start(bf16[128,256]{1,0:T(8,128)(2,1)S(1)} %get-tuple-element.95), channel_id=1, source_target_pairs={{0,3},{1,2},{2,1},{3,0},{4,7},{5,6},{6,5},{7,4},{8,11},{9,10},{10,... | collective-permute-start | bytes 196616 | tf_op jit(solution)/shard_map/ppermute | solution.py:38
  96.4 0.0 collective-permute-done.23.refs_3_
  96.4 2.8 %collective-permute-start.19 = (bf16[128,256]{1,0:T(8,128)(2,1)S(1)}, bf16[128,256]{1,0:T(8,128)(2,1)S(1)}, u32[]{:S(2)}, u32[]{:S(2)}) collective-permute-start(bf16[128,256]{1,0:T(8,128)(2,1)S(1)} %get-tuple-element.96), channel_id=1, source_target_pairs={{0,2},{1,3},{2,0},{3,1},{4,6},{5,7},{6,4},{7,5},{8,10},{9,11},{10,... | collective-permute-start | bytes 196616 | tf_op jit(solution)/shard_map/ppermute | solution.py:38
  99.2 1.0 feature_rows.3
  100.2 6.8 %collective-permute-done.22.refs_2_ = bf16[448,256]{1,0:T(8,128)(2,1)S(1)} collective-permute-done((bf16[448,256]{1,0:T(8,128)(2,1)S(1)}, bf16[448,256]{1,0:T(8,128)(2,1)S(1)}, u32[]{:S(2)}, u32[]{:S(2)}) %collective-permute-start.22) | collective-permute-done | bytes 229408 | tf_op jit(solution)/shard_map/ppermute | solution.py:38
  106.9 0.0 collective-permute-done.21.refs_1_
  106.9 1.5 %laid_out.1 = bf16[1792,256]{1,0:T(8,128)(2,1)} custom-call(s32[2]{0:T(128)S(1)} %copy-done.2, bf16[448,256]{1,0:T(8,128)(2,1)S(1)} %bitcast.52, bf16[448,256]{1,0:T(8,128)(2,1)S(1)} %collective-permute-done.21.refs_1_, bf16[448,256]{1,0:T(8,128)(2,1)S(1)} %collective-permute-done.22.refs_2_, bf16[448,256]{1,0:T(8,128)(2,1)S(1)} %collective-permute-done.23.refs_3_), custom_call_target="tpu_custom_call" | custom-call | tf_op jit(solution)/shard_map/laid_out/pallas_call | solution.py:419
  108.5 0.7 fusion.5
  (27 shorter events, 0.2 us)
Async XLA Ops:
  9.4 8.8 %collective-permute-start = (bf16[2,128,256]{2,1,0:T(8,128)(2,1)}, bf16[2,128,256]{2,1,0:T(8,128)(2,1)S(1)}, u32[]{:S(2)}, u32[]{:S(2)}) collective-permute-start(bf16[2,128,256]{2,1,0:T(8,128)(2,1)} %get-tuple-element.42), channel_id=1, source_target_pairs={{0,4},{4,8},{8,12},{12,16},{16,20},{20,24},{24,28},{1,5},{5,9},{9,... | collective-permute-start | bytes 393224 | tf_op jit(solution)/shard_map/ppermute | solution.py:33
  11.8 6.4 %collective-permute-start.1 = (bf16[2,128,256]{2,1,0:T(8,128)(2,1)}, bf16[2,128,256]{2,1,0:T(8,128)(2,1)S(1)}, u32[]{:S(2)}, u32[]{:S(2)}) collective-permute-start(bf16[2,128,256]{2,1,0:T(8,128)(2,1)} %get-tuple-element.43), channel_id=1, source_target_pairs={{4,0},{8,4},{12,8},{16,12},{20,16},{24,20},{28,24},{5,1},{9,5},{13... | collective-permute-start | bytes 393224 | tf_op jit(solution)/shard_map/ppermute | solution.py:33
  13.1 19.6 %collective-permute-start.2 = (bf16[576,256]{1,0:T(8,128)(2,1)}, bf16[576,256]{1,0:T(8,128)(2,1)S(1)}, u32[]{:S(2)}, u32[]{:S(2)}) collective-permute-start(bf16[576,256]{1,0:T(8,128)(2,1)} %get-tuple-element.49), channel_id=1, source_target_pairs={{0,1},{1,0},{2,3},{3,2},{4,5},{5,4},{6,7},{7,6},{8,9},{9,8},{10,11... | collective-permute-start | bytes 884744 | tf_op jit(solution)/shard_map/ppermute | solution.py:38
  15.5 17.1 %collective-permute-start.3 = (bf16[576,256]{1,0:T(8,128)(2,1)}, bf16[576,256]{1,0:T(8,128)(2,1)S(1)}, u32[]{:S(2)}, u32[]{:S(2)}) collective-permute-start(bf16[576,256]{1,0:T(8,128)(2,1)} %get-tuple-element.50), channel_id=1, source_target_pairs={{0,2},{1,3},{2,0},{3,1},{4,6},{5,7},{6,4},{7,5},{8,10},{9,11},{10,... | collective-permute-start | bytes 884744 | tf_op jit(solution)/shard_map/ppermute | solution.py:38
  18.1 19.2 %collective-permute-start.4 = (bf16[576,256]{1,0:T(8,128)(2,1)}, bf16[576,256]{1,0:T(8,128)(2,1)S(1)}, u32[]{:S(2)}, u32[]{:S(2)}) collective-permute-start(bf16[576,256]{1,0:T(8,128)(2,1)} %get-tuple-element.51), channel_id=1, source_target_pairs={{0,3},{1,2},{2,1},{3,0},{4,7},{5,6},{6,5},{7,4},{8,11},{9,10},{10,... | collective-permute-start | bytes 884744 | tf_op jit(solution)/shard_map/ppermute | solution.py:38
  18.1 0.7 copy-start.3
  18.2 0.7 copy-start.4
  18.9 9.1 %copy-start.5 = (s32[112]{0:T(128)S(1)}, s32[112]{0:T(128)}, u32[]{:S(2)}) copy-start(s32[112]{0:T(128)} %shuffle.3) | copy-start | bytes 1348
  18.9 12.2 %copy-start.6 = (bf16[2,128,256]{2,1,0:T(8,128)(2,1)S(1)}, bf16[2,128,256]{2,1,0:T(8,128)(2,1)}, u32[]{:S(2)}) copy-start(bf16[2,128,256]{2,1,0:T(8,128)(2,1)} %get-tuple-element.59) | copy-start | bytes 393220
  18.9 24.5 %copy-start = (bf16[14,128,256]{2,1,0:T(8,128)(2,1)S(1)}, bf16[14,128,256]{2,1,0:T(8,128)(2,1)}, u32[]{:S(2)}) copy-start(bf16[14,128,256]{2,1,0:T(8,128)(2,1)} %get-tuple-element.57.clean) | copy-start | bytes 2752516
  18.9 24.5 %copy-start.1 = (bf16[576,256]{1,0:T(8,128)(2,1)S(1)}, bf16[576,256]{1,0:T(8,128)(2,1)}, u32[]{:S(2)}) copy-start(bf16[576,256]{1,0:T(8,128)(2,1)} %get-tuple-element.52.refs_0_) | copy-start | bytes 884740
  18.9 24.5 %copy-start.2 = (s32[2]{0:T(128)S(1)}, s32[2]{0:T(128)}, u32[]{:S(2)}) copy-start(s32[2]{0:T(128)} %pad_add_fusion.me.index) | copy-start | bytes 28
  21.5 21.9 %all-to-all-start = ((bf16[16,128,256]{2,1,0:T(8,128)(2,1)}), bf16[16,128,256]{2,1,0:T(8,128)(2,1)S(1)}, u32[]{:S(2)}, u32[]{:S(2)}) async-start(bf16[16,128,256]{2,1,0:T(8,128)(2,1)} %patch.1), calls=%async_computation | async-start | bytes 2097152 | tf_op jit(solution)/shard_map/all_to_all | solution.py:42
  28.6 14.8 %collective-permute-start.5 = (bf16[2,128,256]{2,1,0:T(8,128)(2,1)}, bf16[2,128,256]{2,1,0:T(8,128)(2,1)S(1)}, u32[]{:S(2)}, u32[]{:S(2)}) collective-permute-start(bf16[2,128,256]{2,1,0:T(8,128)(2,1)} %get-tuple-element.58), channel_id=1, source_target_pairs={{0,4},{4,8},{8,12},{12,16},{16,20},{20,24},{24,28},{1,5},{5,9},{9,... | collective-permute-start | bytes 393224 | tf_op jit(solution)/shard_map/ppermute | solution.py:33
  31.1 12.4 %collective-permute-start.6 = (bf16[2,128,256]{2,1,0:T(8,128)(2,1)S(1)}, bf16[2,128,256]{2,1,0:T(8,128)(2,1)S(1)}, u32[]{:S(2)}, u32[]{:S(2)}) collective-permute-start(bf16[2,128,256]{2,1,0:T(8,128)(2,1)S(1)} %copy-done.6), channel_id=1, source_target_pairs={{4,0},{8,4},{12,8},{16,12},{20,16},{24,20},{28,24},{5,1},{9,5},{13... | collective-permute-start | bytes 393224 | tf_op jit(solution)/shard_map/ppermute | solution.py:33
  44.5 9.6 %collective-permute-start.12 = (bf16[4,128,256]{2,1,0:T(8,128)(2,1)S(1)}, bf16[4,128,256]{2,1,0:T(8,128)(2,1)S(1)}, u32[]{:S(2)}, u32[]{:S(2)}) collective-permute-start(bf16[4,128,256]{2,1,0:T(8,128)(2,1)S(1)} %get-tuple-element.62), channel_id=1, source_target_pairs={{0,24},{4,28},{8,16},{12,20},{16,8},{20,12},{24,0},{28,4},{1,25},{... | collective-permute-start | bytes 786440 | tf_op jit(solution)/shard_map/ppermute | solution.py:38
  47.3 13.0 %collective-permute-start.11 = (bf16[4,128,256]{2,1,0:T(8,128)(2,1)S(1)}, bf16[4,128,256]{2,1,0:T(8,128)(2,1)S(1)}, u32[]{:S(2)}, u32[]{:S(2)}) collective-permute-start(bf16[4,128,256]{2,1,0:T(8,128)(2,1)S(1)} %get-tuple-element.62), channel_id=1, source_target_pairs={{0,16},{4,20},{8,24},{12,28},{16,0},{20,4},{24,8},{28,12},{1,17},{... | collective-permute-start | bytes 786440 | tf_op jit(solution)/shard_map/ppermute | solution.py:38
  47.5 12.7 %collective-permute-start.10 = (bf16[4,128,256]{2,1,0:T(8,128)(2,1)S(1)}, bf16[4,128,256]{2,1,0:T(8,128)(2,1)S(1)}, u32[]{:S(2)}, u32[]{:S(2)}) collective-permute-start(bf16[4,128,256]{2,1,0:T(8,128)(2,1)S(1)} %get-tuple-element.62), channel_id=1, source_target_pairs={{0,8},{4,12},{8,0},{12,4},{16,24},{20,28},{24,16},{28,20},{1,9},{5... | collective-permute-start | bytes 786440 | tf_op jit(solution)/shard_map/ppermute | solution.py:38
  49.0 11.4 %collective-permute-start.9 = (bf16[448,256]{1,0:T(8,128)(2,1)S(1)}, bf16[448,256]{1,0:T(8,128)(2,1)S(1)}, u32[]{:S(2)}, u32[]{:S(2)}) collective-permute-start(bf16[448,256]{1,0:T(8,128)(2,1)S(1)} %get-tuple-element.87), channel_id=1, source_target_pairs={{0,3},{1,2},{2,1},{3,0},{4,7},{5,6},{6,5},{7,4},{8,11},{9,10},{10,... | collective-permute-start | bytes 688136 | tf_op jit(solution)/shard_map/ppermute | solution.py:38
  53.0 19.2 %collective-permute-start.8 = (bf16[448,256]{1,0:T(8,128)(2,1)S(1)}, bf16[448,256]{1,0:T(8,128)(2,1)S(1)}, u32[]{:S(2)}, u32[]{:S(2)}) collective-permute-start(bf16[448,256]{1,0:T(8,128)(2,1)S(1)} %get-tuple-element.88), channel_id=1, source_target_pairs={{0,2},{1,3},{2,0},{3,1},{4,6},{5,7},{6,4},{7,5},{8,10},{9,11},{10,... | collective-permute-start | bytes 688136 | tf_op jit(solution)/shard_map/ppermute | solution.py:38
  54.1 18.1 %collective-permute-start.7 = (bf16[448,256]{1,0:T(8,128)(2,1)S(1)}, bf16[448,256]{1,0:T(8,128)(2,1)S(1)}, u32[]{:S(2)}, u32[]{:S(2)}) collective-permute-start(bf16[448,256]{1,0:T(8,128)(2,1)S(1)} %get-tuple-element.89), channel_id=1, source_target_pairs={{0,1},{1,0},{2,3},{3,2},{4,5},{5,4},{6,7},{7,6},{8,9},{9,8},{10,11... | collective-permute-start | bytes 688136 | tf_op jit(solution)/shard_map/ppermute | solution.py:38
  72.2 2.7 %collective-permute-start.13 = (bf16[4,4,128,256]{3,2,1,0:T(8,128)(2,1)S(1)}, bf16[4,4,128,256]{3,2,1,0:T(8,128)(2,1)S(1)}, u32[]{:S(2)}, u32[]{:S(2)}) collective-permute-start(bf16[4,4,128,256]{3,2,1,0:T(8,128)(2,1)S(1)} %pad_maximum_fusion.refs_4_), channel_id=1, source_target_pairs={{0,4},{4,0},{8,12},{12,8},{16,20},{20,16},{24,28},{28,24},{1,5},{5... | collective-permute-start | bytes 3145736 | tf_op jit(solution)/shard_map/ppermute | solution.py:38
  74.9 2.9 %collective-permute-start.14 = (bf16[4,4,128,256]{3,2,1,0:T(8,128)(2,1)S(1)}, bf16[4,4,128,256]{3,2,1,0:T(8,128)(2,1)S(1)}, u32[]{:S(2)}, u32[]{:S(2)}) collective-permute-start(bf16[4,4,128,256]{3,2,1,0:T(8,128)(2,1)S(1)} %get-tuple-element.70), channel_id=1, source_target_pairs={{0,4},{4,0},{8,12},{12,8},{16,20},{20,16},{24,28},{28,24},{1,5},{5... | collective-permute-start | bytes 3145736 | tf_op jit(solution)/shard_map/ppermute | solution.py:38
  78.2 9.2 %collective-permute-start.15 = (bf16[4,128,256]{2,1,0:T(8,128)(2,1)S(1)}, bf16[4,128,256]{2,1,0:T(8,128)(2,1)S(1)}, u32[]{:S(2)}, u32[]{:S(2)}) collective-permute-start(bf16[4,128,256]{2,1,0:T(8,128)(2,1)S(1)} %get-tuple-element.84), channel_id=1, source_target_pairs={{0,8},{4,12},{8,0},{12,4},{16,24},{20,28},{24,16},{28,20},{1,9},{5... | collective-permute-start | bytes 786440 | tf_op jit(solution)/shard_map/ppermute | solution.py:38
  79.4 12.9 %collective-permute-start.17 = (bf16[4,128,256]{2,1,0:T(8,128)(2,1)S(1)}, bf16[4,128,256]{2,1,0:T(8,128)(2,1)S(1)}, u32[]{:S(2)}, u32[]{:S(2)}) collective-permute-start(bf16[4,128,256]{2,1,0:T(8,128)(2,1)S(1)} %get-tuple-element.85), channel_id=1, source_target_pairs={{0,24},{4,28},{8,16},{12,20},{16,8},{20,12},{24,0},{28,4},{1,25},{... | collective-permute-start | bytes 786440 | tf_op jit(solution)/shard_map/ppermute | solution.py:38
  80.0 13.6 %collective-permute-start.16 = (bf16[4,128,256]{2,1,0:T(8,128)(2,1)S(1)}, bf16[4,128,256]{2,1,0:T(8,128)(2,1)S(1)}, u32[]{:S(2)}, u32[]{:S(2)}) collective-permute-start(bf16[4,128,256]{2,1,0:T(8,128)(2,1)S(1)} %get-tuple-element.86), channel_id=1, source_target_pairs={{0,16},{4,20},{8,24},{12,28},{16,0},{20,4},{24,8},{28,12},{1,17},{... | collective-permute-start | bytes 786440 | tf_op jit(solution)/shard_map/ppermute | solution.py:38
  81.8 14.6 %collective-permute-start.23 = (bf16[448,256]{1,0:T(8,128)(2,1)S(1)}, bf16[448,256]{1,0:T(8,128)(2,1)S(1)}, u32[]{:S(2)}, u32[]{:S(2)}) collective-permute-start(bf16[448,256]{1,0:T(8,128)(2,1)S(1)} %get-tuple-element.91), channel_id=1, source_target_pairs={{0,3},{1,2},{2,1},{3,0},{4,7},{5,6},{6,5},{7,4},{8,11},{9,10},{10,... | collective-permute-start | bytes 688136 | tf_op jit(solution)/shard_map/ppermute | solution.py:38
  84.4 22.5 %collective-permute-start.22 = (bf16[448,256]{1,0:T(8,128)(2,1)S(1)}, bf16[448,256]{1,0:T(8,128)(2,1)S(1)}, u32[]{:S(2)}, u32[]{:S(2)}) collective-permute-start(bf16[448,256]{1,0:T(8,128)(2,1)S(1)} %get-tuple-element.92), channel_id=1, source_target_pairs={{0,2},{1,3},{2,0},{3,1},{4,6},{5,7},{6,4},{7,5},{8,10},{9,11},{10,... | collective-permute-start | bytes 688136 | tf_op jit(solution)/shard_map/ppermute | solution.py:38
  87.4 19.5 %collective-permute-start.21 = (bf16[448,256]{1,0:T(8,128)(2,1)S(1)}, bf16[448,256]{1,0:T(8,128)(2,1)S(1)}, u32[]{:S(2)}, u32[]{:S(2)}) collective-permute-start(bf16[448,256]{1,0:T(8,128)(2,1)S(1)} %get-tuple-element.93), channel_id=1, source_target_pairs={{0,1},{1,0},{2,3},{3,2},{4,5},{5,4},{6,7},{7,6},{8,9},{9,8},{10,11... | collective-permute-start | bytes 688136 | tf_op jit(solution)/shard_map/ppermute | solution.py:38
  93.8 14.7 %collective-permute-start.18 = (bf16[128,256]{1,0:T(8,128)(2,1)S(1)}, bf16[128,256]{1,0:T(8,128)(2,1)S(1)}, u32[]{:S(2)}, u32[]{:S(2)}) collective-permute-start(bf16[128,256]{1,0:T(8,128)(2,1)S(1)} %get-tuple-element.94), channel_id=1, source_target_pairs={{0,1},{1,0},{2,3},{3,2},{4,5},{5,4},{6,7},{7,6},{8,9},{9,8},{10,11... | collective-permute-start | bytes 196616 | tf_op jit(solution)/shard_map/ppermute | solution.py:38
  93.8 14.6 %collective-permute-start.20 = (bf16[128,256]{1,0:T(8,128)(2,1)S(1)}, bf16[128,256]{1,0:T(8,128)(2,1)S(1)}, u32[]{:S(2)}, u32[]{:S(2)}) collective-permute-start(bf16[128,256]{1,0:T(8,128)(2,1)S(1)} %get-tuple-element.95), channel_id=1, source_target_pairs={{0,3},{1,2},{2,1},{3,0},{4,7},{5,6},{6,5},{7,4},{8,11},{9,10},{10,... | collective-permute-start | bytes 196616 | tf_op jit(solution)/shard_map/ppermute | solution.py:38
  96.4 12.1 %collective-permute-start.19 = (bf16[128,256]{1,0:T(8,128)(2,1)S(1)}, bf16[128,256]{1,0:T(8,128)(2,1)S(1)}, u32[]{:S(2)}, u32[]{:S(2)}) collective-permute-start(bf16[128,256]{1,0:T(8,128)(2,1)S(1)} %get-tuple-element.96), channel_id=1, source_target_pairs={{0,2},{1,3},{2,0},{3,1},{4,6},{5,7},{6,4},{7,5},{8,10},{9,11},{10,... | collective-permute-start | bytes 196616 | tf_op jit(solution)/shard_map/ppermute | solution.py:38

commit v15 on v12

--- a/solution.py
+++ b/solution.py
@@ -57,13 +57,14 @@
 
 
 def aggregate_kernel(
-    reach, groups, send_slots, me, shuffle, cols, count, gc, pc, gx, px, slopes, adj, features, weight, *refs
+    reach, groups, send_slots, shuffle, cols, count, gc, pc, gx, px, slopes, adj, features, weight, *refs
 ):
     clean, outgoing, *refs = refs
     sides, packed, refs = refs[:4], refs[4 : 4 + groups], refs[4 + groups :]
     data, tiles, rhs, stage, results, halos, packs, places, used, sems, pack_sems, out_sems = refs
     blocks, slots, rows, _ = adj.shape
     width = gc.shape[1]
+    me = (lax.axis_index("node"), lax.axis_index("chan"))
     quarter = features.shape[0] // groups
     spare = blocks + 2 * reach
     pad = 2 * reach * rows
@@ -79,7 +80,8 @@
         return out + [pltpu.make_async_copy(adj.at[span], tiles.at[span], sems.at[4, step])]
 
     inputs = [copies(step) for step in range(blocks // 2)]
-    for copy in sum(inputs, []):
+    ahead = 3
+    for copy in sum(inputs[:ahead], []):
         copy.start()
     to_vmem, to_hbm = [], []
     for i in range(groups):
@@ -89,8 +91,6 @@
         )
         to_vmem.append(pltpu.make_async_copy(weight, packs.at[i, quarter:], pack_sems.at[1, i]))
         to_hbm.append(pltpu.make_async_copy(packs.at[i], packed[i], pack_sems.at[2, i]))
-    for copy in to_vmem:
-        copy.start()
     stage[...] = jnp.zeros_like(stage)
     rhs[:pad] = jnp.zeros((pad, 2 * width), jnp.bfloat16)
     rhs[pad + blocks * rows :] = jnp.zeros((pad, 2 * width), jnp.bfloat16)
@@ -162,6 +162,11 @@
     for step in range(blocks // 2):
         for copy in inputs[step]:
             copy.wait()
+        for copy in inputs[step + ahead] if step + ahead < blocks // 2 else []:
+            copy.start()
+        if step == 1:
+            for copy in to_vmem:
+                copy.start()
         if step:
             finish(2 * step - 2)
         take(step)
@@ -175,7 +180,7 @@
         copy.wait()
 
 
-def aggregate(index, shuffle, cols, count, gc, pc, gx, px, slopes, adj, features, weight, reach, devs, groups):
+def aggregate(shuffle, cols, count, gc, pc, gx, px, slopes, adj, features, weight, reach, devs, groups):
     blocks, slots, rows, _ = adj.shape
     width = gc.shape[1]
     send_slots = -(-blocks // devs)
@@ -183,7 +188,7 @@
     packed = features.shape[0] // groups + weight.shape[0]
     return pl.pallas_call(
         functools.partial(aggregate_kernel, reach, groups, send_slots),
-        in_specs=[IN_SMEM] * 4 + [IN_HBM] * 4 + [IN_VMEM] + [IN_HBM] * 3,
+        in_specs=[IN_SMEM] * 3 + [IN_HBM] * 4 + [IN_VMEM] + [IN_HBM] * 3,
         out_specs=[IN_HBM] * (6 + groups),
         out_shape=[bf16(blocks, rows, width), bf16(devs * send_slots, rows, width)]
         + [bf16(reach, rows, width)] * 4
@@ -209,7 +214,7 @@
             transcendentals=0,
         ),
         name="aggregate",
-    )(index, shuffle, cols, count, gc, pc, gx, px, slopes, adj, features, weight)
+    )(shuffle, cols, count, gc, pc, gx, px, slopes, adj, features, weight)
 
 
 def patch_kernel(reach, blocks, slots, index, shuffle, outgoing, low, high, out, *scratch):
@@ -459,7 +464,7 @@
     slots = -(-blocks // devs)
     index = jnp.stack([me, group])
 
-    args = (index, shuffle_from, adj_cols.T, adj_count)
+    args = (shuffle_from, adj_cols.T, adj_count)
     args += (grad_clean, pre_clean, grad_corrupt, pre_corrupt, slopes[None, :], adj_vals)
     clean, outgoing, *sides = aggregate(*args, features, weight, reach, devs, groups)
     sides, packed = sides[:4], sides[4:]

time: 108 us -> 108 us (level)
  transfers between devices with their start and end apart: 25 -> 25, of which waited for: 10 -> 10; matrix products, arithmetic and copies ran while one was open for 1% -> 2% of each run, Pallas kernels for 9% -> 9%
where the time goes in v15:
time: 108 us; the launch traced here: 107 us
  starting transfers between devices  44.1 us (41%)
  waiting for transfers between devices  38.7 us (36%)
  Pallas kernels  19.6 us (18%)
  other arithmetic  2.5 us (2%)
  local copies, waits for them, and re-layouts  1.33 us (1%)
    ppermute x20, waiting for transfers between devices, swapped(): return lax.ppermute(value, axis, [(i, i ^ by) for i in range(size)])  32 us
    ppermute x20, starting transfers between devices, swapped(): return lax.ppermute(value, axis, [(i, i ^ by) for i in range(size)])  30.2 us
    pallas_call x1, Pallas kernels, aggregate(): pl.pallas_call(functools.partial(aggregate_kernel, reach, groups, send_sl...  8.41 us
    ppermute x4, starting transfers between devices, shifted(): return lax.ppermute(value, axis, pairs)  7.36 us
    all_to_all x1, waiting for transfers between devices, exchanged(): return lax.all_to_all(value, axis, split_axis=0, concat_axis=0, tiled=True)  6.73 us
    all_to_all x1, starting transfers between devices, exchanged(): return lax.all_to_all(value, axis, split_axis=0, concat_axis=0, tiled=True)  6.57 us
    pallas_call x2, Pallas kernels, feature_rows(): pl.pallas_call(functools.partial(feature_kernel, first), in_specs=[IN_SME...  3.33 us
    pallas_call x1, Pallas kernels, weight_partial(): pl.pallas_call(functools.partial(weight_kernel, devs), in_specs=[IN_SMEM]...  2.65 us
  transfers between devices with their start and end apart: 25, of which 10 were waited for; matrix products, arithmetic and copies ran while one was open for 2% of the time, Pallas kernels for 9%

profile of v15, /device:TPU:0, one launch (start us, length us, event | category | flops | bytes accessed | tf_op | source)
XLA Modules:
  0.0 107.2 jit_solution(6279060805983816170)
XLA Ops:
  0.6 8.4 %aggregate.1 = (bf16[14,128,256]{2,1,0:T(8,128)(2,1)}, bf16[16,128,256]{2,1,0:T(8,128)(2,1)}, bf16[2,128,256]{2,1,0:T(8,128)(2,1)}, bf16[2,128,256]{2,1,0:T(8,12...) custom-call(s32[112]{0:T(128)} %shuffle.3, ...), custom_call_target="tpu_custom_call" | custom-call | flops 1174405120 | bytes 7798784 | tf_op jit(solution)/shard_map/aggregate/pallas_call | solution.py:189
  9.1 2.4 %collective-permute-start = (bf16[2,128,256]{2,1,0:T(8,128)(2,1)}, bf16[2,128,256]{2,1,0:T(8,128)(2,1)S(1)}, u32[]{:S(2)}, u32[]{:S(2)}) collective-permute-start(bf16[2,128,256]{2,1,0:T(8,128)(2,1)} %get-tuple-element.43), channel_id=1, source_target_pairs={{0,4},{4,8},{8,12},{12,16},{16,20},{20,24},{24,28},{1,5},{5,9},{9,... | collective-permute-start | bytes 393224 | tf_op jit(solution)/shard_map/ppermute | solution.py:33
  11.4 1.3 %collective-permute-start.1 = (bf16[2,128,256]{2,1,0:T(8,128)(2,1)}, bf16[2,128,256]{2,1,0:T(8,128)(2,1)S(1)}, u32[]{:S(2)}, u32[]{:S(2)}) collective-permute-start(bf16[2,128,256]{2,1,0:T(8,128)(2,1)} %get-tuple-element.44), channel_id=1, source_target_pairs={{4,0},{8,4},{12,8},{16,12},{20,16},{24,20},{28,24},{5,1},{9,5},{13... | collective-permute-start | bytes 393224 | tf_op jit(solution)/shard_map/ppermute | solution.py:33
  12.7 2.5 %collective-permute-start.2 = (bf16[576,256]{1,0:T(8,128)(2,1)}, bf16[576,256]{1,0:T(8,128)(2,1)S(1)}, u32[]{:S(2)}, u32[]{:S(2)}) collective-permute-start(bf16[576,256]{1,0:T(8,128)(2,1)} %get-tuple-element.50), channel_id=1, source_target_pairs={{0,1},{1,0},{2,3},{3,2},{4,5},{5,4},{6,7},{7,6},{8,9},{9,8},{10,11... | collective-permute-start | bytes 884744 | tf_op jit(solution)/shard_map/ppermute | solution.py:38
  15.2 2.6 %collective-permute-start.3 = (bf16[576,256]{1,0:T(8,128)(2,1)}, bf16[576,256]{1,0:T(8,128)(2,1)S(1)}, u32[]{:S(2)}, u32[]{:S(2)}) collective-permute-start(bf16[576,256]{1,0:T(8,128)(2,1)} %get-tuple-element.51), channel_id=1, source_target_pairs={{0,2},{1,3},{2,0},{3,1},{4,6},{5,7},{6,4},{7,5},{8,10},{9,11},{10,... | collective-permute-start | bytes 884744 | tf_op jit(solution)/shard_map/ppermute | solution.py:38
  17.8 0.6 pad_add_fusion.index
  18.4 0.0 collective-permute-done.low
  18.4 0.0 collective-permute-done.1.high
  18.4 0.6 copy-done.3
  19.1 0.1 copy-done.4
  19.1 2.6 %patch.1 = bf16[16,128,256]{2,1,0:T(8,128)(2,1)} custom-call(s32[2]{0:T(128)} %pad_add_fusion.index, s32[112]{0:T(128)} %shuffle.3, bf16[16,128,256]{2,1,0:T(8,128)(2,1)} %get-tuple-element.42.outgoing, bf16[2,128,256]{2,1,0:T(8,128)(2,1)} %copy-done.3, bf16[2,128,256]{2,1,0:T(8,128)(2,1)} %copy-done.4), custom_call_target="tpu_custom_call", output_to_operand_aliasing={{}: (2, {})} | custom-call | tf_op jit(solution)/shard_map/patch/pallas_call | solution.py:251
  21.8 6.6 %all-to-all-start = ((bf16[16,128,256]{2,1,0:T(8,128)(2,1)}), bf16[16,128,256]{2,1,0:T(8,128)(2,1)S(1)}, u32[]{:S(2)}, u32[]{:S(2)}) async-start(bf16[16,128,256]{2,1,0:T(8,128)(2,1)} %patch.1), calls=%async_computation | async-start | bytes 2097152 | tf_op jit(solution)/shard_map/all_to_all | solution.py:42
  28.4 0.1 eq.30
  28.5 0.1 add.45
  28.6 0.3 convert_reduce_fusion
  28.9 0.1 copy.14
  29.0 2.4 %collective-permute-start.5 = (bf16[2,128,256]{2,1,0:T(8,128)(2,1)S(1)}, bf16[2,128,256]{2,1,0:T(8,128)(2,1)S(1)}, u32[]{:S(2)}, u32[]{:S(2)}) collective-permute-start(bf16[2,128,256]{2,1,0:T(8,128)(2,1)S(1)} %copy-done.7), channel_id=1, source_target_pairs={{0,4},{4,8},{8,12},{12,16},{16,20},{20,24},{24,28},{1,5},{5,9},{9,... | collective-permute-start | bytes 393224 | tf_op jit(solution)/shard_map/ppermute | solution.py:33
  31.4 1.3 %collective-permute-start.6 = (bf16[2,128,256]{2,1,0:T(8,128)(2,1)S(1)}, bf16[2,128,256]{2,1,0:T(8,128)(2,1)S(1)}, u32[]{:S(2)}, u32[]{:S(2)}) collective-permute-start(bf16[2,128,256]{2,1,0:T(8,128)(2,1)S(1)} %copy-done.6), channel_id=1, source_target_pairs={{4,0},{8,4},{12,8},{16,12},{20,16},{24,20},{28,24},{5,1},{9,5},{13... | collective-permute-start | bytes 393224 | tf_op jit(solution)/shard_map/ppermute | solution.py:33
  32.7 0.1 select_reduce_fusion
  32.9 0.1 copy.15
  33.0 0.1 sub.13.landing
  33.0 0.0 collective-permute-done.2.refs_1_
  33.1 0.0 collective-permute-done.3.refs_2_
  33.1 4.0 %collective-permute-done.4.refs_3_ = bf16[576,256]{1,0:T(8,128)(2,1)S(1)} collective-permute-done((bf16[576,256]{1,0:T(8,128)(2,1)}, bf16[576,256]{1,0:T(8,128)(2,1)S(1)}, u32[]{:S(2)}, u32[]{:S(2)}) %collective-permute-start.4) | collective-permute-done | bytes 294944 | tf_op jit(solution)/shard_map/ppermute | solution.py:38
  37.0 6.7 %all-to-all-done.incoming = bf16[16,128,256]{2,1,0:T(8,128)(2,1)S(1)} async-done(((bf16[16,128,256]{2,1,0:T(8,128)(2,1)}), bf16[16,128,256]{2,1,0:T(8,128)(2,1)S(1)}, u32[]{:S(2)}, u32[]{:S(2)}) %all-to-all-start) | async-done | bytes 1048608 | tf_op jit(solution)/shard_map/all_to_all | solution.py:42
  43.8 0.0 collective-permute-done.6.high
  43.8 1.0 merge.1
  44.9 0.1 slice_bitcast_fusion.4
  44.9 3.7 %collective-permute-start.9 = (bf16[448,256]{1,0:T(8,128)(2,1)S(1)}, bf16[448,256]{1,0:T(8,128)(2,1)S(1)}, u32[]{:S(2)}, u32[]{:S(2)}) collective-permute-start(bf16[448,256]{1,0:T(8,128)(2,1)S(1)} %get-tuple-element.89), channel_id=1, source_target_pairs={{0,3},{1,2},{2,1},{3,0},{4,7},{5,6},{6,5},{7,4},{8,11},{9,10},{10,... | collective-permute-start | bytes 688136 | tf_op jit(solution)/shard_map/ppermute | solution.py:38
  48.7 2.8 %collective-permute-start.12 = (bf16[4,128,256]{2,1,0:T(8,128)(2,1)S(1)}, bf16[4,128,256]{2,1,0:T(8,128)(2,1)S(1)}, u32[]{:S(2)}, u32[]{:S(2)}) collective-permute-start(bf16[4,128,256]{2,1,0:T(8,128)(2,1)S(1)} %pad_maximum_fusion.1), channel_id=1, source_target_pairs={{0,24},{4,28},{8,16},{12,20},{16,8},{20,12},{24,0},{28,4},{1,25},{... | collective-permute-start | bytes 786440 | tf_op jit(solution)/shard_map/ppermute | solution.py:38
  51.5 0.2 collective-permute-start.11
  51.7 1.4 %collective-permute-start.10 = (bf16[4,128,256]{2,1,0:T(8,128)(2,1)S(1)}, bf16[4,128,256]{2,1,0:T(8,128)(2,1)S(1)}, u32[]{:S(2)}, u32[]{:S(2)}) collective-permute-start(bf16[4,128,256]{2,1,0:T(8,128)(2,1)S(1)} %pad_maximum_fusion.1), channel_id=1, source_target_pairs={{0,8},{4,12},{8,0},{12,4},{16,24},{20,28},{24,16},{28,20},{1,9},{5... | collective-permute-start | bytes 786440 | tf_op jit(solution)/shard_map/ppermute | solution.py:38
  53.1 0.0 collective-permute-start.8
  53.1 1.5 %collective-permute-done.9.refs_7_.refs_3_ = bf16[448,256]{1,0:T(8,128)(2,1)S(1)} collective-permute-done((bf16[448,256]{1,0:T(8,128)(2,1)S(1)}, bf16[448,256]{1,0:T(8,128)(2,1)S(1)}, u32[]{:S(2)}, u32[]{:S(2)}) %collective-permute-start.9) | collective-permute-done | bytes 229408 | tf_op jit(solution)/shard_map/ppermute | solution.py:38
  54.6 5.1 %collective-permute-start.7 = (bf16[448,256]{1,0:T(8,128)(2,1)S(1)}, bf16[448,256]{1,0:T(8,128)(2,1)S(1)}, u32[]{:S(2)}, u32[]{:S(2)}) collective-permute-start(bf16[448,256]{1,0:T(8,128)(2,1)S(1)} %get-tuple-element.91), channel_id=1, source_target_pairs={{0,2},{1,3},{2,0},{3,1},{4,6},{5,7},{6,4},{7,5},{8,10},{9,11},{10,... | collective-permute-start | bytes 688136 | tf_op jit(solution)/shard_map/ppermute | solution.py:38
  59.7 0.6 collective-permute-done.8.refs_5_.refs_1_
  60.3 10.6 %collective-permute-done.7.refs_6_.refs_2_ = bf16[448,256]{1,0:T(8,128)(2,1)S(1)} collective-permute-done((bf16[448,256]{1,0:T(8,128)(2,1)S(1)}, bf16[448,256]{1,0:T(8,128)(2,1)S(1)}, u32[]{:S(2)}, u32[]{:S(2)}) %collective-permute-start.7) | collective-permute-done | bytes 229408 | tf_op jit(solution)/shard_map/ppermute | solution.py:38
  71.0 0.0 collective-permute-done.11
  71.0 0.0 collective-permute-done.10
  71.0 0.1 pad_maximum_fusion.refs_4_
  71.1 0.2 collective-permute-start.13
  71.3 2.6 %weight_partial.1 = (bf16[4,4,128,256]{3,2,1,0:T(8,128)(2,1)S(1)}, bf16[4,4,128,256]{3,2,1,0:T(8,128)(2,1)S(1)}) custom-call(s32[2]{0:T(128)S(1)} %copy-done.2, bf16[576,256]{1,0:T(8,128)(2,1)S(1)} %copy-done.1, bf16[576,256]{1,0:T(8,128)(2,1)S(1)} %collective-permute-done.2.refs_1_, bf16[576,256]{1,0:T(8,128)(2,1)S(1)} %collective-permute-done.3.refs_2_, ...), custom_call_target="tpu_custom_call" | custom-call | flops 939524096 | bytes 3932160 | tf_op jit(solution)/shard_map/weight_partial/pallas_call | solution.py:339
  74.0 0.5 collective-permute-start.14
  74.4 2.3 %feature_rows.2 = bf16[3,448,256]{2,1,0:T(8,128)(2,1)S(1)} custom-call(s32[2]{0:T(128)S(1)} %copy-done.2, bf16[448,256]{1,0:T(8,128)(2,1)S(1)} %get-tuple-element.75.refs_4_.refs_0_, bf16[448,256]{1,0:T(8,128)(2,1)S(1)} %collective-permute-done.8.refs_5_.refs_1_, bf16[448,256]{1,0:T(8,128)(2,1)S(1)} %collective-permute-done.7.refs_6_.refs_2_, ...), custom_call_target="tpu_custom_call" | custom-call | flops 704643072 | bytes 3178496 | tf_op jit(solution)/shard_map/feature_rows/pallas_call | solution.py:387
  76.8 0.4 convert_add_fusion
  77.1 0.1 slice_bitcast_fusion.3
  77.2 0.5 collective-permute-start.15
  77.7 0.0 collective-permute-start.17
  77.7 3.1 %collective-permute-start.16 = (bf16[4,128,256]{2,1,0:T(8,128)(2,1)S(1)}, bf16[4,128,256]{2,1,0:T(8,128)(2,1)S(1)}, u32[]{:S(2)}, u32[]{:S(2)}) collective-permute-start(bf16[4,128,256]{2,1,0:T(8,128)(2,1)S(1)} %get-tuple-element.88), channel_id=1, source_target_pairs={{0,16},{4,20},{8,24},{12,28},{16,0},{20,4},{24,8},{28,12},{1,17},{... | collective-permute-start | bytes 786440 | tf_op jit(solution)/shard_map/ppermute | solution.py:38
  80.8 1.7 %collective-permute-start.23 = (bf16[448,256]{1,0:T(8,128)(2,1)S(1)}, bf16[448,256]{1,0:T(8,128)(2,1)S(1)}, u32[]{:S(2)}, u32[]{:S(2)}) collective-permute-start(bf16[448,256]{1,0:T(8,128)(2,1)S(1)} %get-tuple-element.93), channel_id=1, source_target_pairs={{0,3},{1,2},{2,1},{3,0},{4,7},{5,6},{6,5},{7,4},{8,11},{9,10},{10,... | collective-permute-start | bytes 688136 | tf_op jit(solution)/shard_map/ppermute | solution.py:38
  82.5 0.0 collective-permute-start.22
  82.5 3.9 %collective-permute-done.15 = bf16[4,128,256]{2,1,0:T(8,128)(2,1)S(1)} collective-permute-done((bf16[4,128,256]{2,1,0:T(8,128)(2,1)S(1)}, bf16[4,128,256]{2,1,0:T(8,128)(2,1)S(1)}, u32[]{:S(2)}, u32[]{:S(2)}) %collective-permute-start.15) | collective-permute-done | bytes 262176 | tf_op jit(solution)/shard_map/ppermute | solution.py:38
  86.4 0.0 collective-permute-start.21
  86.4 3.0 %collective-permute-done.17 = bf16[4,128,256]{2,1,0:T(8,128)(2,1)S(1)} collective-permute-done((bf16[4,128,256]{2,1,0:T(8,128)(2,1)S(1)}, bf16[4,128,256]{2,1,0:T(8,128)(2,1)S(1)}, u32[]{:S(2)}, u32[]{:S(2)}) %collective-permute-start.17) | collective-permute-done | bytes 262176 | tf_op jit(solution)/shard_map/ppermute | solution.py:38
  89.4 3.2 %collective-permute-done.16 = bf16[4,128,256]{2,1,0:T(8,128)(2,1)S(1)} collective-permute-done((bf16[4,128,256]{2,1,0:T(8,128)(2,1)S(1)}, bf16[4,128,256]{2,1,0:T(8,128)(2,1)S(1)}, u32[]{:S(2)}, u32[]{:S(2)}) %collective-permute-start.16) | collective-permute-done | bytes 262176 | tf_op jit(solution)/shard_map/ppermute | solution.py:38
  92.6 0.2 fusion.10
  92.8 0.1 collective-permute-start.18
  92.9 1.7 %collective-permute-start.20 = (bf16[128,256]{1,0:T(8,128)(2,1)S(1)}, bf16[128,256]{1,0:T(8,128)(2,1)S(1)}, u32[]{:S(2)}, u32[]{:S(2)}) collective-permute-start(bf16[128,256]{1,0:T(8,128)(2,1)S(1)} %get-tuple-element.97), channel_id=1, source_target_pairs={{0,3},{1,2},{2,1},{3,0},{4,7},{5,6},{6,5},{7,4},{8,11},{9,10},{10,... | collective-permute-start | bytes 196616 | tf_op jit(solution)/shard_map/ppermute | solution.py:38
  94.6 4.3 %collective-permute-start.19 = (bf16[128,256]{1,0:T(8,128)(2,1)S(1)}, bf16[128,256]{1,0:T(8,128)(2,1)S(1)}, u32[]{:S(2)}, u32[]{:S(2)}) collective-permute-start(bf16[128,256]{1,0:T(8,128)(2,1)S(1)} %get-tuple-element.98), channel_id=1, source_target_pairs={{0,2},{1,3},{2,0},{3,1},{4,6},{5,7},{6,4},{7,5},{8,10},{9,11},{10,... | collective-permute-start | bytes 196616 | tf_op jit(solution)/shard_map/ppermute | solution.py:38
  98.9 1.0 feature_rows.3
  99.9 5.0 %collective-permute-done.22.refs_2_ = bf16[448,256]{1,0:T(8,128)(2,1)S(1)} collective-permute-done((bf16[448,256]{1,0:T(8,128)(2,1)S(1)}, bf16[448,256]{1,0:T(8,128)(2,1)S(1)}, u32[]{:S(2)}, u32[]{:S(2)}) %collective-permute-start.22) | collective-permute-done | bytes 229408 | tf_op jit(solution)/shard_map/ppermute | solution.py:38
  104.9 1.5 %laid_out.1 = bf16[1792,256]{1,0:T(8,128)(2,1)} custom-call(s32[2]{0:T(128)S(1)} %copy-done.2, bf16[448,256]{1,0:T(8,128)(2,1)S(1)} %bitcast.60, bf16[448,256]{1,0:T(8,128)(2,1)S(1)} %collective-permute-done.21.refs_1_, bf16[448,256]{1,0:T(8,128)(2,1)S(1)} %collective-permute-done.22.refs_2_, bf16[448,256]{1,0:T(8,128)(2,1)S(1)} %collective-permute-done.23.refs_3_), custom_call_target="tpu_custom_call" | custom-call | tf_op jit(solution)/shard_map/laid_out/pallas_call | solution.py:419
  106.4 0.1 collective-permute-done.19
  106.5 0.7 fusion.5
  (32 shorter events, 0.2 us)
Async XLA Ops:
  9.1 9.3 %collective-permute-start = (bf16[2,128,256]{2,1,0:T(8,128)(2,1)}, bf16[2,128,256]{2,1,0:T(8,128)(2,1)S(1)}, u32[]{:S(2)}, u32[]{:S(2)}) collective-permute-start(bf16[2,128,256]{2,1,0:T(8,128)(2,1)} %get-tuple-element.43), channel_id=1, source_target_pairs={{0,4},{4,8},{8,12},{12,16},{16,20},{20,24},{24,28},{1,5},{5,9},{9,... | collective-permute-start | bytes 393224 | tf_op jit(solution)/shard_map/ppermute | solution.py:33
  11.4 7.0 %collective-permute-start.1 = (bf16[2,128,256]{2,1,0:T(8,128)(2,1)}, bf16[2,128,256]{2,1,0:T(8,128)(2,1)S(1)}, u32[]{:S(2)}, u32[]{:S(2)}) collective-permute-start(bf16[2,128,256]{2,1,0:T(8,128)(2,1)} %get-tuple-element.44), channel_id=1, source_target_pairs={{4,0},{8,4},{12,8},{16,12},{20,16},{24,20},{28,24},{5,1},{9,5},{13... | collective-permute-start | bytes 393224 | tf_op jit(solution)/shard_map/ppermute | solution.py:33
  12.7 20.3 %collective-permute-start.2 = (bf16[576,256]{1,0:T(8,128)(2,1)}, bf16[576,256]{1,0:T(8,128)(2,1)S(1)}, u32[]{:S(2)}, u32[]{:S(2)}) collective-permute-start(bf16[576,256]{1,0:T(8,128)(2,1)} %get-tuple-element.50), channel_id=1, source_target_pairs={{0,1},{1,0},{2,3},{3,2},{4,5},{5,4},{6,7},{7,6},{8,9},{9,8},{10,11... | collective-permute-start | bytes 884744 | tf_op jit(solution)/shard_map/ppermute | solution.py:38
  15.2 17.8 %collective-permute-start.3 = (bf16[576,256]{1,0:T(8,128)(2,1)}, bf16[576,256]{1,0:T(8,128)(2,1)S(1)}, u32[]{:S(2)}, u32[]{:S(2)}) collective-permute-start(bf16[576,256]{1,0:T(8,128)(2,1)} %get-tuple-element.51), channel_id=1, source_target_pairs={{0,2},{1,3},{2,0},{3,1},{4,6},{5,7},{6,4},{7,5},{8,10},{9,11},{10,... | collective-permute-start | bytes 884744 | tf_op jit(solution)/shard_map/ppermute | solution.py:38
  17.8 19.2 %collective-permute-start.4 = (bf16[576,256]{1,0:T(8,128)(2,1)}, bf16[576,256]{1,0:T(8,128)(2,1)S(1)}, u32[]{:S(2)}, u32[]{:S(2)}) collective-permute-start(bf16[576,256]{1,0:T(8,128)(2,1)} %get-tuple-element.52), channel_id=1, source_target_pairs={{0,3},{1,2},{2,1},{3,0},{4,7},{5,6},{6,5},{7,4},{8,11},{9,10},{10,... | collective-permute-start | bytes 884744 | tf_op jit(solution)/shard_map/ppermute | solution.py:38
  18.4 0.7 copy-start.3
  18.4 0.7 copy-start.4
  19.1 9.3 %copy-start.5 = (s32[112]{0:T(128)S(1)}, s32[112]{0:T(128)}, u32[]{:S(2)}) copy-start(s32[112]{0:T(128)} %shuffle.3) | copy-start | bytes 1348
  19.1 12.3 %copy-start.6 = (bf16[2,128,256]{2,1,0:T(8,128)(2,1)S(1)}, bf16[2,128,256]{2,1,0:T(8,128)(2,1)}, u32[]{:S(2)}) copy-start(bf16[2,128,256]{2,1,0:T(8,128)(2,1)} %get-tuple-element.60) | copy-start | bytes 393220
  19.1 24.7 %copy-start = (bf16[14,128,256]{2,1,0:T(8,128)(2,1)S(1)}, bf16[14,128,256]{2,1,0:T(8,128)(2,1)}, u32[]{:S(2)}) copy-start(bf16[14,128,256]{2,1,0:T(8,128)(2,1)} %get-tuple-element.58.clean) | copy-start | bytes 2752516
  19.1 24.7 %copy-start.2 = (s32[2]{0:T(128)S(1)}, s32[2]{0:T(128)}, u32[]{:S(2)}) copy-start(s32[2]{0:T(128)} %pad_add_fusion.index) | copy-start | bytes 28
  21.8 7.2 %copy-start.7 = (bf16[2,128,256]{2,1,0:T(8,128)(2,1)S(1)}, bf16[2,128,256]{2,1,0:T(8,128)(2,1)}, u32[]{:S(2)}) copy-start(bf16[2,128,256]{2,1,0:T(8,128)(2,1)} %get-tuple-element.59) | copy-start | bytes 393220
  21.8 22.0 %all-to-all-start = ((bf16[16,128,256]{2,1,0:T(8,128)(2,1)}), bf16[16,128,256]{2,1,0:T(8,128)(2,1)S(1)}, u32[]{:S(2)}, u32[]{:S(2)}) async-start(bf16[16,128,256]{2,1,0:T(8,128)(2,1)} %patch.1), calls=%async_computation | async-start | bytes 2097152 | tf_op jit(solution)/shard_map/all_to_all | solution.py:42
  29.0 14.8 %collective-permute-start.5 = (bf16[2,128,256]{2,1,0:T(8,128)(2,1)S(1)}, bf16[2,128,256]{2,1,0:T(8,128)(2,1)S(1)}, u32[]{:S(2)}, u32[]{:S(2)}) collective-permute-start(bf16[2,128,256]{2,1,0:T(8,128)(2,1)S(1)} %copy-done.7), channel_id=1, source_target_pairs={{0,4},{4,8},{8,12},{12,16},{16,20},{20,24},{24,28},{1,5},{5,9},{9,... | collective-permute-start | bytes 393224 | tf_op jit(solution)/shard_map/ppermute | solution.py:33
  31.4 12.4 %collective-permute-start.6 = (bf16[2,128,256]{2,1,0:T(8,128)(2,1)S(1)}, bf16[2,128,256]{2,1,0:T(8,128)(2,1)S(1)}, u32[]{:S(2)}, u32[]{:S(2)}) collective-permute-start(bf16[2,128,256]{2,1,0:T(8,128)(2,1)S(1)} %copy-done.6), channel_id=1, source_target_pairs={{4,0},{8,4},{12,8},{16,12},{20,16},{24,20},{28,24},{5,1},{9,5},{13... | collective-permute-start | bytes 393224 | tf_op jit(solution)/shard_map/ppermute | solution.py:33
  43.8 4.8 %copy-start.1 = (bf16[576,256]{1,0:T(8,128)(2,1)S(1)}, bf16[576,256]{1,0:T(8,128)(2,1)}, u32[]{:S(2)}) copy-start(bf16[576,256]{1,0:T(8,128)(2,1)} %get-tuple-element.53.refs_0_) | copy-start | bytes 884740
  44.9 9.7 %collective-permute-start.9 = (bf16[448,256]{1,0:T(8,128)(2,1)S(1)}, bf16[448,256]{1,0:T(8,128)(2,1)S(1)}, u32[]{:S(2)}, u32[]{:S(2)}) collective-permute-start(bf16[448,256]{1,0:T(8,128)(2,1)S(1)} %get-tuple-element.89), channel_id=1, source_target_pairs={{0,3},{1,2},{2,1},{3,0},{4,7},{5,6},{6,5},{7,4},{8,11},{9,10},{10,... | collective-permute-start | bytes 688136 | tf_op jit(solution)/shard_map/ppermute | solution.py:38
  48.7 22.3 %collective-permute-start.12 = (bf16[4,128,256]{2,1,0:T(8,128)(2,1)S(1)}, bf16[4,128,256]{2,1,0:T(8,128)(2,1)S(1)}, u32[]{:S(2)}, u32[]{:S(2)}) collective-permute-start(bf16[4,128,256]{2,1,0:T(8,128)(2,1)S(1)} %pad_maximum_fusion.1), channel_id=1, source_target_pairs={{0,24},{4,28},{8,16},{12,20},{16,8},{20,12},{24,0},{28,4},{1,25},{... | collective-permute-start | bytes 786440 | tf_op jit(solution)/shard_map/ppermute | solution.py:38
  51.5 19.5 %collective-permute-start.11 = (bf16[4,128,256]{2,1,0:T(8,128)(2,1)S(1)}, bf16[4,128,256]{2,1,0:T(8,128)(2,1)S(1)}, u32[]{:S(2)}, u32[]{:S(2)}) collective-permute-start(bf16[4,128,256]{2,1,0:T(8,128)(2,1)S(1)} %pad_maximum_fusion.1), channel_id=1, source_target_pairs={{0,16},{4,20},{8,24},{12,28},{16,0},{20,4},{24,8},{28,12},{1,17},{... | collective-permute-start | bytes 786440 | tf_op jit(solution)/shard_map/ppermute | solution.py:38
  51.7 19.3 %collective-permute-start.10 = (bf16[4,128,256]{2,1,0:T(8,128)(2,1)S(1)}, bf16[4,128,256]{2,1,0:T(8,128)(2,1)S(1)}, u32[]{:S(2)}, u32[]{:S(2)}) collective-permute-start(bf16[4,128,256]{2,1,0:T(8,128)(2,1)S(1)} %pad_maximum_fusion.1), channel_id=1, source_target_pairs={{0,8},{4,12},{8,0},{12,4},{16,24},{20,28},{24,16},{28,20},{1,9},{5... | collective-permute-start | bytes 786440 | tf_op jit(solution)/shard_map/ppermute | solution.py:38
  53.1 7.2 %collective-permute-start.8 = (bf16[448,256]{1,0:T(8,128)(2,1)S(1)}, bf16[448,256]{1,0:T(8,128)(2,1)S(1)}, u32[]{:S(2)}, u32[]{:S(2)}) collective-permute-start(bf16[448,256]{1,0:T(8,128)(2,1)S(1)} %get-tuple-element.90), channel_id=1, source_target_pairs={{0,1},{1,0},{2,3},{3,2},{4,5},{5,4},{6,7},{7,6},{8,9},{9,8},{10,11... | collective-permute-start | bytes 688136 | tf_op jit(solution)/shard_map/ppermute | solution.py:38
  54.6 16.3 %collective-permute-start.7 = (bf16[448,256]{1,0:T(8,128)(2,1)S(1)}, bf16[448,256]{1,0:T(8,128)(2,1)S(1)}, u32[]{:S(2)}, u32[]{:S(2)}) collective-permute-start(bf16[448,256]{1,0:T(8,128)(2,1)S(1)} %get-tuple-element.91), channel_id=1, source_target_pairs={{0,2},{1,3},{2,0},{3,1},{4,6},{5,7},{6,4},{7,5},{8,10},{9,11},{10,... | collective-permute-start | bytes 688136 | tf_op jit(solution)/shard_map/ppermute | solution.py:38
  71.1 2.8 %collective-permute-start.13 = (bf16[4,4,128,256]{3,2,1,0:T(8,128)(2,1)S(1)}, bf16[4,4,128,256]{3,2,1,0:T(8,128)(2,1)S(1)}, u32[]{:S(2)}, u32[]{:S(2)}) collective-permute-start(bf16[4,4,128,256]{3,2,1,0:T(8,128)(2,1)S(1)} %pad_maximum_fusion.refs_4_), channel_id=1, source_target_pairs={{0,4},{4,0},{8,12},{12,8},{16,20},{20,16},{24,28},{28,24},{1,5},{5... | collective-permute-start | bytes 3145736 | tf_op jit(solution)/shard_map/ppermute | solution.py:38
  74.0 2.8 %collective-permute-start.14 = (bf16[4,4,128,256]{3,2,1,0:T(8,128)(2,1)S(1)}, bf16[4,4,128,256]{3,2,1,0:T(8,128)(2,1)S(1)}, u32[]{:S(2)}, u32[]{:S(2)}) collective-permute-start(bf16[4,4,128,256]{3,2,1,0:T(8,128)(2,1)S(1)} %get-tuple-element.72), channel_id=1, source_target_pairs={{0,4},{4,0},{8,12},{12,8},{16,20},{20,16},{24,28},{28,24},{1,5},{5... | collective-permute-start | bytes 3145736 | tf_op jit(solution)/shard_map/ppermute | solution.py:38
  77.2 9.2 %collective-permute-start.15 = (bf16[4,128,256]{2,1,0:T(8,128)(2,1)S(1)}, bf16[4,128,256]{2,1,0:T(8,128)(2,1)S(1)}, u32[]{:S(2)}, u32[]{:S(2)}) collective-permute-start(bf16[4,128,256]{2,1,0:T(8,128)(2,1)S(1)} %get-tuple-element.86), channel_id=1, source_target_pairs={{0,8},{4,12},{8,0},{12,4},{16,24},{20,28},{24,16},{28,20},{1,9},{5... | collective-permute-start | bytes 786440 | tf_op jit(solution)/shard_map/ppermute | solution.py:38
  77.7 11.7 %collective-permute-start.17 = (bf16[4,128,256]{2,1,0:T(8,128)(2,1)S(1)}, bf16[4,128,256]{2,1,0:T(8,128)(2,1)S(1)}, u32[]{:S(2)}, u32[]{:S(2)}) collective-permute-start(bf16[4,128,256]{2,1,0:T(8,128)(2,1)S(1)} %get-tuple-element.87), channel_id=1, source_target_pairs={{0,24},{4,28},{8,16},{12,20},{16,8},{20,12},{24,0},{28,4},{1,25},{... | collective-permute-start | bytes 786440 | tf_op jit(solution)/shard_map/ppermute | solution.py:38
  77.7 14.9 %collective-permute-start.16 = (bf16[4,128,256]{2,1,0:T(8,128)(2,1)S(1)}, bf16[4,128,256]{2,1,0:T(8,128)(2,1)S(1)}, u32[]{:S(2)}, u32[]{:S(2)}) collective-permute-start(bf16[4,128,256]{2,1,0:T(8,128)(2,1)S(1)} %get-tuple-element.88), channel_id=1, source_target_pairs={{0,16},{4,20},{8,24},{12,28},{16,0},{20,4},{24,8},{28,12},{1,17},{... | collective-permute-start | bytes 786440 | tf_op jit(solution)/shard_map/ppermute | solution.py:38
  80.8 13.7 %collective-permute-start.23 = (bf16[448,256]{1,0:T(8,128)(2,1)S(1)}, bf16[448,256]{1,0:T(8,128)(2,1)S(1)}, u32[]{:S(2)}, u32[]{:S(2)}) collective-permute-start(bf16[448,256]{1,0:T(8,128)(2,1)S(1)} %get-tuple-element.93), channel_id=1, source_target_pairs={{0,3},{1,2},{2,1},{3,0},{4,7},{5,6},{6,5},{7,4},{8,11},{9,10},{10,... | collective-permute-start | bytes 688136 | tf_op jit(solution)/shard_map/ppermute | solution.py:38
  82.5 22.4 %collective-permute-start.22 = (bf16[448,256]{1,0:T(8,128)(2,1)S(1)}, bf16[448,256]{1,0:T(8,128)(2,1)S(1)}, u32[]{:S(2)}, u32[]{:S(2)}) collective-permute-start(bf16[448,256]{1,0:T(8,128)(2,1)S(1)} %get-tuple-element.94), channel_id=1, source_target_pairs={{0,2},{1,3},{2,0},{3,1},{4,6},{5,7},{6,4},{7,5},{8,10},{9,11},{10,... | collective-permute-start | bytes 688136 | tf_op jit(solution)/shard_map/ppermute | solution.py:38
  86.4 18.5 %collective-permute-start.21 = (bf16[448,256]{1,0:T(8,128)(2,1)S(1)}, bf16[448,256]{1,0:T(8,128)(2,1)S(1)}, u32[]{:S(2)}, u32[]{:S(2)}) collective-permute-start(bf16[448,256]{1,0:T(8,128)(2,1)S(1)} %get-tuple-element.95), channel_id=1, source_target_pairs={{0,1},{1,0},{2,3},{3,2},{4,5},{5,4},{6,7},{7,6},{8,9},{9,8},{10,11... | collective-permute-start | bytes 688136 | tf_op jit(solution)/shard_map/ppermute | solution.py:38
  92.8 13.6 %collective-permute-start.18 = (bf16[128,256]{1,0:T(8,128)(2,1)S(1)}, bf16[128,256]{1,0:T(8,128)(2,1)S(1)}, u32[]{:S(2)}, u32[]{:S(2)}) collective-permute-start(bf16[128,256]{1,0:T(8,128)(2,1)S(1)} %get-tuple-element.96), channel_id=1, source_target_pairs={{0,1},{1,0},{2,3},{3,2},{4,5},{5,4},{6,7},{7,6},{8,9},{9,8},{10,11... | collective-permute-start | bytes 196616 | tf_op jit(solution)/shard_map/ppermute | solution.py:38
  92.9 13.6 %collective-permute-start.20 = (bf16[128,256]{1,0:T(8,128)(2,1)S(1)}, bf16[128,256]{1,0:T(8,128)(2,1)S(1)}, u32[]{:S(2)}, u32[]{:S(2)}) collective-permute-start(bf16[128,256]{1,0:T(8,128)(2,1)S(1)} %get-tuple-element.97), channel_id=1, source_target_pairs={{0,3},{1,2},{2,1},{3,0},{4,7},{5,6},{6,5},{7,4},{8,11},{9,10},{10,... | collective-permute-start | bytes 196616 | tf_op jit(solution)/shard_map/ppermute | solution.py:38
  94.6 12.0 %collective-permute-start.19 = (bf16[128,256]{1,0:T(8,128)(2,1)S(1)}, bf16[128,256]{1,0:T(8,128)(2,1)S(1)}, u32[]{:S(2)}, u32[]{:S(2)}) collective-permute-start(bf16[128,256]{1,0:T(8,128)(2,1)S(1)} %get-tuple-element.98), channel_id=1, source_target_pairs={{0,2},{1,3},{2,0},{3,1},{4,6},{5,7},{6,4},{7,5},{8,10},{9,11},{10,... | collective-permute-start | bytes 196616 | tf_op jit(solution)/shard_map/ppermute | solution.py:38

commit v16 on v15

--- a/solution.py
+++ b/solution.py
@@ -43,7 +43,7 @@
 
 
 def masked_grad(grad, pre, slope):
-    return jnp.where(pre > 0, grad, (wide(grad) * slope).astype(jnp.bfloat16))
+    return jnp.where(pre > 0, grad, grad * slope)
 
 
 def find_places(index, shuffle, blocks, slots, places, used):
@@ -67,7 +67,6 @@
     me = (lax.axis_index("node"), lax.axis_index("chan"))
     quarter = features.shape[0] // groups
     spare = blocks + 2 * reach
-    pad = 2 * reach * rows
 
     def copies(step):
         span = slice(2 * step, 2 * step + 2)
@@ -92,18 +91,16 @@
         to_vmem.append(pltpu.make_async_copy(weight, packs.at[i, quarter:], pack_sems.at[1, i]))
         to_hbm.append(pltpu.make_async_copy(packs.at[i], packed[i], pack_sems.at[2, i]))
     stage[...] = jnp.zeros_like(stage)
-    rhs[:pad] = jnp.zeros((pad, 2 * width), jnp.bfloat16)
-    rhs[pad + blocks * rows :] = jnp.zeros((pad, 2 * width), jnp.bfloat16)
     shape = (rows, rows)
     identity = (
         lax.broadcasted_iota(jnp.int32, shape, 0) == lax.broadcasted_iota(jnp.int32, shape, 1)
     ).astype(jnp.float32).astype(jnp.bfloat16)
-    slope = slopes[...]
+    slope = slopes[...].astype(jnp.bfloat16)
     find_places(me, shuffle, blocks, send_slots, places, used)
 
     def take(step):
         gradients = [masked_grad(data[i, step], data[i + 1, step], slope) for i in (0, 2)]
-        rhs[pad + 2 * step * rows : pad + (2 * step + 2) * rows] = jnp.concatenate(gradients, axis=1)
+        rhs[2 * step * rows : (2 * step + 2) * rows] = jnp.concatenate(gradients, axis=1)
         turned = lax.dot_general(
             identity,
             tiles[2 * step : 2 * step + 2].reshape(2 * slots * rows, rows),
@@ -116,23 +113,22 @@
             target = cols[k, block] - me[0] * blocks
             place = jnp.where(live, target + reach, spare)
             distance = jnp.where(live, block - target + reach, 0)
-            part = turned[:, i * rows : (i + 1) * rows]
-            stage[place, distance] = (wide(stage[place, distance]) + part).astype(jnp.bfloat16)
+            stage[place, distance] += turned[:, i * rows : (i + 1) * rows].astype(jnp.bfloat16)
 
     blank = jnp.zeros(shape, jnp.bfloat16)
 
     def pair(first):
+        targets = [first - reach, first - reach + 1]
+        sources = range(max(0, targets[0] - reach), min(blocks, targets[1] + reach + 1))
+
+        def tile(i, source):
+            distance = source - targets[i] + reach
+            return stage[first + i, distance] if 0 <= distance <= 2 * reach else blank
+
         lhs = jnp.concatenate(
-            [
-                jnp.concatenate(
-                    [blank] * i + [stage[first + i, j] for j in range(2 * reach + 1)] + [blank] * (1 - i),
-                    axis=1,
-                )
-                for i in range(2)
-            ],
-            axis=0,
+            [jnp.concatenate([tile(i, b) for b in sources], axis=1) for i in range(2)], axis=0
         )
-        span = slice(first * rows, (first + 2 * reach + 2) * rows)
+        span = slice(sources.start * rows, sources.stop * rows)
         product = jnp.dot(lhs, rhs[span], preferred_element_type=jnp.float32)
         product = product.astype(jnp.bfloat16).reshape(2, rows, 2 * width)
         return product[:, :, :width], product[:, :, width:]
@@ -196,7 +192,7 @@
         scratch_shapes=[
             pltpu.VMEM((4, blocks // 2, 2 * rows, width), jnp.bfloat16),
             pltpu.VMEM((blocks, slots, rows, rows), jnp.bfloat16),
-            pltpu.VMEM(((blocks + 4 * reach) * rows, 2 * width), jnp.bfloat16),
+            pltpu.VMEM((blocks * rows, 2 * width), jnp.bfloat16),
             pltpu.VMEM((blocks + 2 * reach + 1, 2 * reach + 1, rows, rows), jnp.bfloat16),
             pltpu.VMEM((2, blocks, rows, width), jnp.bfloat16),
             pltpu.VMEM((2, 2, reach, rows, width), jnp.bfloat16),

time: 108 us -> 107 us (level)
  transfers between devices with their start and end apart: 25 -> 25, of which waited for: 10 -> 9; matrix products, arithmetic and copies ran while one was open for 2% -> 2% of each run, Pallas kernels for 9% -> 9%
where the time goes in v16:
time: 107 us
  starting transfers between devices  44.2 us (41%)
  waiting for transfers between devices  38.7 us (36%)
  Pallas kernels  19 us (18%)
  other arithmetic  2.5 us (2%)
  local copies, waits for them, and re-layouts  1.33 us (1%)
    ppermute x20, waiting for transfers between devices, swapped(): return lax.ppermute(value, axis, [(i, i ^ by) for i in range(size)])  31.9 us
    ppermute x20, starting transfers between devices, swapped(): return lax.ppermute(value, axis, [(i, i ^ by) for i in range(size)])  30.3 us
    pallas_call x1, Pallas kernels, aggregate(): pl.pallas_call(functools.partial(aggregate_kernel, reach, groups, send_sl...  7.9 us
    ppermute x4, starting transfers between devices, shifted(): return lax.ppermute(value, axis, pairs)  7.35 us
    all_to_all x1, waiting for transfers between devices, exchanged(): return lax.all_to_all(value, axis, split_axis=0, concat_axis=0, tiled=True)  6.8 us
    all_to_all x1, starting transfers between devices, exchanged(): return lax.all_to_all(value, axis, split_axis=0, concat_axis=0, tiled=True)  6.63 us
    pallas_call x2, Pallas kernels, feature_rows(): pl.pallas_call(functools.partial(feature_kernel, first), in_specs=[IN_SME...  3.33 us
    pallas_call x1, Pallas kernels, weight_partial(): pl.pallas_call(functools.partial(weight_kernel, devs), in_specs=[IN_SMEM]...  2.65 us
  transfers between devices with their start and end apart: 25, of which 9 were waited for; matrix products, arithmetic and copies ran while one was open for 2% of the time, Pallas kernels for 9%

profile of v16, /device:TPU:0, one launch (start us, length us, event | category | flops | bytes accessed | tf_op | source)
XLA Modules:
  0.0 106.8 jit_solution(2658601320368574349)
XLA Ops:
  0.6 7.9 %aggregate.1 = (bf16[14,128,256]{2,1,0:T(8,128)(2,1)}, bf16[16,128,256]{2,1,0:T(8,128)(2,1)}, bf16[2,128,256]{2,1,0:T(8,128)(2,1)}, bf16[2,128,256]{2,1,0:T(8,12...) custom-call(s32[112]{0:T(128)} %shuffle.3, ...), custom_call_target="tpu_custom_call" | custom-call | flops 1174405120 | bytes 7798784 | tf_op jit(solution)/shard_map/aggregate/pallas_call | solution.py:185
  8.5 2.4 %collective-permute-start = (bf16[2,128,256]{2,1,0:T(8,128)(2,1)}, bf16[2,128,256]{2,1,0:T(8,128)(2,1)S(1)}, u32[]{:S(2)}, u32[]{:S(2)}) collective-permute-start(bf16[2,128,256]{2,1,0:T(8,128)(2,1)} %get-tuple-element.43), channel_id=1, source_target_pairs={{0,4},{4,8},{8,12},{12,16},{16,20},{20,24},{24,28},{1,5},{5,9},{9,... | collective-permute-start | bytes 393224 | tf_op jit(solution)/shard_map/ppermute | solution.py:33
  10.9 1.3 %collective-permute-start.1 = (bf16[2,128,256]{2,1,0:T(8,128)(2,1)}, bf16[2,128,256]{2,1,0:T(8,128)(2,1)S(1)}, u32[]{:S(2)}, u32[]{:S(2)}) collective-permute-start(bf16[2,128,256]{2,1,0:T(8,128)(2,1)} %get-tuple-element.44), channel_id=1, source_target_pairs={{4,0},{8,4},{12,8},{16,12},{20,16},{24,20},{28,24},{5,1},{9,5},{13... | collective-permute-start | bytes 393224 | tf_op jit(solution)/shard_map/ppermute | solution.py:33
  12.2 2.5 %collective-permute-start.2 = (bf16[576,256]{1,0:T(8,128)(2,1)}, bf16[576,256]{1,0:T(8,128)(2,1)S(1)}, u32[]{:S(2)}, u32[]{:S(2)}) collective-permute-start(bf16[576,256]{1,0:T(8,128)(2,1)} %get-tuple-element.50), channel_id=1, source_target_pairs={{0,1},{1,0},{2,3},{3,2},{4,5},{5,4},{6,7},{7,6},{8,9},{9,8},{10,11... | collective-permute-start | bytes 884744 | tf_op jit(solution)/shard_map/ppermute | solution.py:38
  14.7 2.6 %collective-permute-start.3 = (bf16[576,256]{1,0:T(8,128)(2,1)}, bf16[576,256]{1,0:T(8,128)(2,1)S(1)}, u32[]{:S(2)}, u32[]{:S(2)}) collective-permute-start(bf16[576,256]{1,0:T(8,128)(2,1)} %get-tuple-element.51), channel_id=1, source_target_pairs={{0,2},{1,3},{2,0},{3,1},{4,6},{5,7},{6,4},{7,5},{8,10},{9,11},{10,... | collective-permute-start | bytes 884744 | tf_op jit(solution)/shard_map/ppermute | solution.py:38
  17.3 0.6 pad_add_fusion.index
  17.9 0.0 collective-permute-done.1.high
  17.9 0.6 copy-done.3
  18.5 0.1 copy-done.4
  18.6 2.6 %patch.1 = bf16[16,128,256]{2,1,0:T(8,128)(2,1)} custom-call(s32[2]{0:T(128)} %pad_add_fusion.index, s32[112]{0:T(128)} %shuffle.3, bf16[16,128,256]{2,1,0:T(8,128)(2,1)} %get-tuple-element.42.outgoing, bf16[2,128,256]{2,1,0:T(8,128)(2,1)} %copy-done.3, bf16[2,128,256]{2,1,0:T(8,128)(2,1)} %copy-done.4), custom_call_target="tpu_custom_call", output_to_operand_aliasing={{}: (2, {})} | custom-call | tf_op jit(solution)/shard_map/patch/pallas_call | solution.py:247
  21.2 6.6 %all-to-all-start = ((bf16[16,128,256]{2,1,0:T(8,128)(2,1)}), bf16[16,128,256]{2,1,0:T(8,128)(2,1)S(1)}, u32[]{:S(2)}, u32[]{:S(2)}) async-start(bf16[16,128,256]{2,1,0:T(8,128)(2,1)} %patch.1), calls=%async_computation | async-start | bytes 2097152 | tf_op jit(solution)/shard_map/all_to_all | solution.py:42
  27.9 0.1 eq.30
  28.0 0.1 add.45
  28.1 0.3 convert_reduce_fusion
  28.4 0.1 copy.14
  28.5 2.4 %collective-permute-start.5 = (bf16[2,128,256]{2,1,0:T(8,128)(2,1)S(1)}, bf16[2,128,256]{2,1,0:T(8,128)(2,1)S(1)}, u32[]{:S(2)}, u32[]{:S(2)}) collective-permute-start(bf16[2,128,256]{2,1,0:T(8,128)(2,1)S(1)} %copy-done.7), channel_id=1, source_target_pairs={{0,4},{4,8},{8,12},{12,16},{16,20},{20,24},{24,28},{1,5},{5,9},{9,... | collective-permute-start | bytes 393224 | tf_op jit(solution)/shard_map/ppermute | solution.py:33
  30.9 1.3 %collective-permute-start.6 = (bf16[2,128,256]{2,1,0:T(8,128)(2,1)S(1)}, bf16[2,128,256]{2,1,0:T(8,128)(2,1)S(1)}, u32[]{:S(2)}, u32[]{:S(2)}) collective-permute-start(bf16[2,128,256]{2,1,0:T(8,128)(2,1)S(1)} %copy-done.6), channel_id=1, source_target_pairs={{4,0},{8,4},{12,8},{16,12},{20,16},{24,20},{28,24},{5,1},{9,5},{13... | collective-permute-start | bytes 393224 | tf_op jit(solution)/shard_map/ppermute | solution.py:33
  32.2 0.1 select_reduce_fusion
  32.4 0.1 copy.15
  32.5 0.1 sub.13.landing
  32.5 0.0 collective-permute-done.2.refs_1_
  32.6 0.0 collective-permute-done.3.refs_2_
  32.6 3.9 %collective-permute-done.4.refs_3_ = bf16[576,256]{1,0:T(8,128)(2,1)S(1)} collective-permute-done((bf16[576,256]{1,0:T(8,128)(2,1)}, bf16[576,256]{1,0:T(8,128)(2,1)S(1)}, u32[]{:S(2)}, u32[]{:S(2)}) %collective-permute-start.4) | collective-permute-done | bytes 294944 | tf_op jit(solution)/shard_map/ppermute | solution.py:38
  36.5 6.8 %all-to-all-done.incoming = bf16[16,128,256]{2,1,0:T(8,128)(2,1)S(1)} async-done(((bf16[16,128,256]{2,1,0:T(8,128)(2,1)}), bf16[16,128,256]{2,1,0:T(8,128)(2,1)S(1)}, u32[]{:S(2)}, u32[]{:S(2)}) %all-to-all-start) | async-done | bytes 1048608 | tf_op jit(solution)/shard_map/all_to_all | solution.py:42
  43.3 1.0 merge.1
  44.4 0.1 slice_bitcast_fusion.4
  44.4 3.7 %collective-permute-start.9 = (bf16[448,256]{1,0:T(8,128)(2,1)S(1)}, bf16[448,256]{1,0:T(8,128)(2,1)S(1)}, u32[]{:S(2)}, u32[]{:S(2)}) collective-permute-start(bf16[448,256]{1,0:T(8,128)(2,1)S(1)} %get-tuple-element.89), channel_id=1, source_target_pairs={{0,3},{1,2},{2,1},{3,0},{4,7},{5,6},{6,5},{7,4},{8,11},{9,10},{10,... | collective-permute-start | bytes 688136 | tf_op jit(solution)/shard_map/ppermute | solution.py:38
  48.2 2.8 %collective-permute-start.12 = (bf16[4,128,256]{2,1,0:T(8,128)(2,1)S(1)}, bf16[4,128,256]{2,1,0:T(8,128)(2,1)S(1)}, u32[]{:S(2)}, u32[]{:S(2)}) collective-permute-start(bf16[4,128,256]{2,1,0:T(8,128)(2,1)S(1)} %pad_maximum_fusion.1), channel_id=1, source_target_pairs={{0,24},{4,28},{8,16},{12,20},{16,8},{20,12},{24,0},{28,4},{1,25},{... | collective-permute-start | bytes 786440 | tf_op jit(solution)/shard_map/ppermute | solution.py:38
  51.0 0.2 collective-permute-start.11
  51.2 1.4 %collective-permute-start.10 = (bf16[4,128,256]{2,1,0:T(8,128)(2,1)S(1)}, bf16[4,128,256]{2,1,0:T(8,128)(2,1)S(1)}, u32[]{:S(2)}, u32[]{:S(2)}) collective-permute-start(bf16[4,128,256]{2,1,0:T(8,128)(2,1)S(1)} %pad_maximum_fusion.1), channel_id=1, source_target_pairs={{0,8},{4,12},{8,0},{12,4},{16,24},{20,28},{24,16},{28,20},{1,9},{5... | collective-permute-start | bytes 786440 | tf_op jit(solution)/shard_map/ppermute | solution.py:38
  52.6 0.0 collective-permute-start.8
  52.6 1.5 %collective-permute-done.9.refs_7_.refs_3_ = bf16[448,256]{1,0:T(8,128)(2,1)S(1)} collective-permute-done((bf16[448,256]{1,0:T(8,128)(2,1)S(1)}, bf16[448,256]{1,0:T(8,128)(2,1)S(1)}, u32[]{:S(2)}, u32[]{:S(2)}) %collective-permute-start.9) | collective-permute-done | bytes 229408 | tf_op jit(solution)/shard_map/ppermute | solution.py:38
  54.1 4.9 %collective-permute-start.7 = (bf16[448,256]{1,0:T(8,128)(2,1)S(1)}, bf16[448,256]{1,0:T(8,128)(2,1)S(1)}, u32[]{:S(2)}, u32[]{:S(2)}) collective-permute-start(bf16[448,256]{1,0:T(8,128)(2,1)S(1)} %get-tuple-element.91), channel_id=1, source_target_pairs={{0,2},{1,3},{2,0},{3,1},{4,6},{5,7},{6,4},{7,5},{8,10},{9,11},{10,... | collective-permute-start | bytes 688136 | tf_op jit(solution)/shard_map/ppermute | solution.py:38
  59.1 0.8 collective-permute-done.8.refs_5_.refs_1_
  59.8 10.5 %collective-permute-done.7.refs_6_.refs_2_ = bf16[448,256]{1,0:T(8,128)(2,1)S(1)} collective-permute-done((bf16[448,256]{1,0:T(8,128)(2,1)S(1)}, bf16[448,256]{1,0:T(8,128)(2,1)S(1)}, u32[]{:S(2)}, u32[]{:S(2)}) %collective-permute-start.7) | collective-permute-done | bytes 229408 | tf_op jit(solution)/shard_map/ppermute | solution.py:38
  70.3 0.0 collective-permute-done.12
  70.3 0.0 collective-permute-done.11
  70.3 0.0 collective-permute-done.10
  70.3 0.1 pad_maximum_fusion.refs_4_
  70.4 0.2 collective-permute-start.13
  70.6 2.6 %weight_partial.1 = (bf16[4,4,128,256]{3,2,1,0:T(8,128)(2,1)S(1)}, bf16[4,4,128,256]{3,2,1,0:T(8,128)(2,1)S(1)}) custom-call(s32[2]{0:T(128)S(1)} %copy-done.2, bf16[576,256]{1,0:T(8,128)(2,1)S(1)} %copy-done.1, bf16[576,256]{1,0:T(8,128)(2,1)S(1)} %collective-permute-done.2.refs_1_, bf16[576,256]{1,0:T(8,128)(2,1)S(1)} %collective-permute-done.3.refs_2_, ...), custom_call_target="tpu_custom_call" | custom-call | flops 939524096 | bytes 3932160 | tf_op jit(solution)/shard_map/weight_partial/pallas_call | solution.py:335
  73.3 0.0 collective-permute-done.13.refs_5_
  73.3 0.5 collective-permute-start.14
  73.7 2.3 %feature_rows.2 = bf16[3,448,256]{2,1,0:T(8,128)(2,1)S(1)} custom-call(s32[2]{0:T(128)S(1)} %copy-done.2, bf16[448,256]{1,0:T(8,128)(2,1)S(1)} %get-tuple-element.75.refs_4_.refs_0_, bf16[448,256]{1,0:T(8,128)(2,1)S(1)} %collective-permute-done.8.refs_5_.refs_1_, bf16[448,256]{1,0:T(8,128)(2,1)S(1)} %collective-permute-done.7.refs_6_.refs_2_, ...), custom_call_target="tpu_custom_call" | custom-call | flops 704643072 | bytes 3178496 | tf_op jit(solution)/shard_map/feature_rows/pallas_call | solution.py:383
  76.1 0.4 convert_add_fusion
  76.5 0.1 slice_bitcast_fusion.3
  76.6 0.7 collective-permute-start.15
  77.2 2.9 %collective-permute-start.16 = (bf16[4,128,256]{2,1,0:T(8,128)(2,1)S(1)}, bf16[4,128,256]{2,1,0:T(8,128)(2,1)S(1)}, u32[]{:S(2)}, u32[]{:S(2)}) collective-permute-start(bf16[4,128,256]{2,1,0:T(8,128)(2,1)S(1)} %get-tuple-element.88), channel_id=1, source_target_pairs={{0,16},{4,20},{8,24},{12,28},{16,0},{20,4},{24,8},{28,12},{1,17},{... | collective-permute-start | bytes 786440 | tf_op jit(solution)/shard_map/ppermute | solution.py:38
  80.2 1.9 %collective-permute-start.23 = (bf16[448,256]{1,0:T(8,128)(2,1)S(1)}, bf16[448,256]{1,0:T(8,128)(2,1)S(1)}, u32[]{:S(2)}, u32[]{:S(2)}) collective-permute-start(bf16[448,256]{1,0:T(8,128)(2,1)S(1)} %get-tuple-element.93), channel_id=1, source_target_pairs={{0,3},{1,2},{2,1},{3,0},{4,7},{5,6},{6,5},{7,4},{8,11},{9,10},{10,... | collective-permute-start | bytes 688136 | tf_op jit(solution)/shard_map/ppermute | solution.py:38
  82.0 0.0 collective-permute-start.22
  82.0 3.7 %collective-permute-done.15 = bf16[4,128,256]{2,1,0:T(8,128)(2,1)S(1)} collective-permute-done((bf16[4,128,256]{2,1,0:T(8,128)(2,1)S(1)}, bf16[4,128,256]{2,1,0:T(8,128)(2,1)S(1)}, u32[]{:S(2)}, u32[]{:S(2)}) %collective-permute-start.15) | collective-permute-done | bytes 262176 | tf_op jit(solution)/shard_map/ppermute | solution.py:38
  85.8 3.2 %collective-permute-done.17 = bf16[4,128,256]{2,1,0:T(8,128)(2,1)S(1)} collective-permute-done((bf16[4,128,256]{2,1,0:T(8,128)(2,1)S(1)}, bf16[4,128,256]{2,1,0:T(8,128)(2,1)S(1)}, u32[]{:S(2)}, u32[]{:S(2)}) %collective-permute-start.17) | collective-permute-done | bytes 262176 | tf_op jit(solution)/shard_map/ppermute | solution.py:38
  88.9 3.0 %collective-permute-done.16 = bf16[4,128,256]{2,1,0:T(8,128)(2,1)S(1)} collective-permute-done((bf16[4,128,256]{2,1,0:T(8,128)(2,1)S(1)}, bf16[4,128,256]{2,1,0:T(8,128)(2,1)S(1)}, u32[]{:S(2)}, u32[]{:S(2)}) %collective-permute-start.16) | collective-permute-done | bytes 262176 | tf_op jit(solution)/shard_map/ppermute | solution.py:38
  91.9 0.2 fusion.10
  92.1 0.1 collective-permute-start.18
  92.2 1.9 %collective-permute-start.20 = (bf16[128,256]{1,0:T(8,128)(2,1)S(1)}, bf16[128,256]{1,0:T(8,128)(2,1)S(1)}, u32[]{:S(2)}, u32[]{:S(2)}) collective-permute-start(bf16[128,256]{1,0:T(8,128)(2,1)S(1)} %get-tuple-element.97), channel_id=1, source_target_pairs={{0,3},{1,2},{2,1},{3,0},{4,7},{5,6},{6,5},{7,4},{8,11},{9,10},{10,... | collective-permute-start | bytes 196616 | tf_op jit(solution)/shard_map/ppermute | solution.py:38
  94.1 0.0 collective-permute-done.23.refs_3_
  94.1 4.2 %collective-permute-start.19 = (bf16[128,256]{1,0:T(8,128)(2,1)S(1)}, bf16[128,256]{1,0:T(8,128)(2,1)S(1)}, u32[]{:S(2)}, u32[]{:S(2)}) collective-permute-start(bf16[128,256]{1,0:T(8,128)(2,1)S(1)} %get-tuple-element.98), channel_id=1, source_target_pairs={{0,2},{1,3},{2,0},{3,1},{4,6},{5,7},{6,4},{7,5},{8,10},{9,11},{10,... | collective-permute-start | bytes 196616 | tf_op jit(solution)/shard_map/ppermute | solution.py:38
  98.3 1.0 feature_rows.3
  99.3 5.3 %collective-permute-done.22.refs_2_ = bf16[448,256]{1,0:T(8,128)(2,1)S(1)} collective-permute-done((bf16[448,256]{1,0:T(8,128)(2,1)S(1)}, bf16[448,256]{1,0:T(8,128)(2,1)S(1)}, u32[]{:S(2)}, u32[]{:S(2)}) %collective-permute-start.22) | collective-permute-done | bytes 229408 | tf_op jit(solution)/shard_map/ppermute | solution.py:38
  104.6 0.0 collective-permute-done.21.refs_1_
  104.6 1.5 %laid_out.1 = bf16[1792,256]{1,0:T(8,128)(2,1)} custom-call(s32[2]{0:T(128)S(1)} %copy-done.2, bf16[448,256]{1,0:T(8,128)(2,1)S(1)} %bitcast.60, bf16[448,256]{1,0:T(8,128)(2,1)S(1)} %collective-permute-done.21.refs_1_, bf16[448,256]{1,0:T(8,128)(2,1)S(1)} %collective-permute-done.22.refs_2_, bf16[448,256]{1,0:T(8,128)(2,1)S(1)} %collective-permute-done.23.refs_3_), custom_call_target="tpu_custom_call" | custom-call | tf_op jit(solution)/shard_map/laid_out/pallas_call | solution.py:415
  106.1 0.0 collective-permute-done.18
  106.1 0.7 fusion.5
  (32 shorter events, 0.2 us)
Async XLA Ops:
  8.5 9.3 %collective-permute-start = (bf16[2,128,256]{2,1,0:T(8,128)(2,1)}, bf16[2,128,256]{2,1,0:T(8,128)(2,1)S(1)}, u32[]{:S(2)}, u32[]{:S(2)}) collective-permute-start(bf16[2,128,256]{2,1,0:T(8,128)(2,1)} %get-tuple-element.43), channel_id=1, source_target_pairs={{0,4},{4,8},{8,12},{12,16},{16,20},{20,24},{24,28},{1,5},{5,9},{9,... | collective-permute-start | bytes 393224 | tf_op jit(solution)/shard_map/ppermute | solution.py:33
  10.9 7.0 %collective-permute-start.1 = (bf16[2,128,256]{2,1,0:T(8,128)(2,1)}, bf16[2,128,256]{2,1,0:T(8,128)(2,1)S(1)}, u32[]{:S(2)}, u32[]{:S(2)}) collective-permute-start(bf16[2,128,256]{2,1,0:T(8,128)(2,1)} %get-tuple-element.44), channel_id=1, source_target_pairs={{4,0},{8,4},{12,8},{16,12},{20,16},{24,20},{28,24},{5,1},{9,5},{13... | collective-permute-start | bytes 393224 | tf_op jit(solution)/shard_map/ppermute | solution.py:33
  12.2 20.3 %collective-permute-start.2 = (bf16[576,256]{1,0:T(8,128)(2,1)}, bf16[576,256]{1,0:T(8,128)(2,1)S(1)}, u32[]{:S(2)}, u32[]{:S(2)}) collective-permute-start(bf16[576,256]{1,0:T(8,128)(2,1)} %get-tuple-element.50), channel_id=1, source_target_pairs={{0,1},{1,0},{2,3},{3,2},{4,5},{5,4},{6,7},{7,6},{8,9},{9,8},{10,11... | collective-permute-start | bytes 884744 | tf_op jit(solution)/shard_map/ppermute | solution.py:38
  14.7 17.9 %collective-permute-start.3 = (bf16[576,256]{1,0:T(8,128)(2,1)}, bf16[576,256]{1,0:T(8,128)(2,1)S(1)}, u32[]{:S(2)}, u32[]{:S(2)}) collective-permute-start(bf16[576,256]{1,0:T(8,128)(2,1)} %get-tuple-element.51), channel_id=1, source_target_pairs={{0,2},{1,3},{2,0},{3,1},{4,6},{5,7},{6,4},{7,5},{8,10},{9,11},{10,... | collective-permute-start | bytes 884744 | tf_op jit(solution)/shard_map/ppermute | solution.py:38
  17.3 19.2 %collective-permute-start.4 = (bf16[576,256]{1,0:T(8,128)(2,1)}, bf16[576,256]{1,0:T(8,128)(2,1)S(1)}, u32[]{:S(2)}, u32[]{:S(2)}) collective-permute-start(bf16[576,256]{1,0:T(8,128)(2,1)} %get-tuple-element.52), channel_id=1, source_target_pairs={{0,3},{1,2},{2,1},{3,0},{4,7},{5,6},{6,5},{7,4},{8,11},{9,10},{10,... | collective-permute-start | bytes 884744 | tf_op jit(solution)/shard_map/ppermute | solution.py:38
  17.9 0.7 copy-start.3
  17.9 0.7 copy-start.4
  18.6 9.3 %copy-start.5 = (s32[112]{0:T(128)S(1)}, s32[112]{0:T(128)}, u32[]{:S(2)}) copy-start(s32[112]{0:T(128)} %shuffle.3) | copy-start | bytes 1348
  18.6 12.3 %copy-start.6 = (bf16[2,128,256]{2,1,0:T(8,128)(2,1)S(1)}, bf16[2,128,256]{2,1,0:T(8,128)(2,1)}, u32[]{:S(2)}) copy-start(bf16[2,128,256]{2,1,0:T(8,128)(2,1)} %get-tuple-element.60) | copy-start | bytes 393220
  18.6 24.7 %copy-start = (bf16[14,128,256]{2,1,0:T(8,128)(2,1)S(1)}, bf16[14,128,256]{2,1,0:T(8,128)(2,1)}, u32[]{:S(2)}) copy-start(bf16[14,128,256]{2,1,0:T(8,128)(2,1)} %get-tuple-element.58.clean) | copy-start | bytes 2752516
  18.6 24.7 %copy-start.2 = (s32[2]{0:T(128)S(1)}, s32[2]{0:T(128)}, u32[]{:S(2)}) copy-start(s32[2]{0:T(128)} %pad_add_fusion.index) | copy-start | bytes 28
  21.2 7.3 %copy-start.7 = (bf16[2,128,256]{2,1,0:T(8,128)(2,1)S(1)}, bf16[2,128,256]{2,1,0:T(8,128)(2,1)}, u32[]{:S(2)}) copy-start(bf16[2,128,256]{2,1,0:T(8,128)(2,1)} %get-tuple-element.59) | copy-start | bytes 393220
  21.2 22.0 %all-to-all-start = ((bf16[16,128,256]{2,1,0:T(8,128)(2,1)}), bf16[16,128,256]{2,1,0:T(8,128)(2,1)S(1)}, u32[]{:S(2)}, u32[]{:S(2)}) async-start(bf16[16,128,256]{2,1,0:T(8,128)(2,1)} %patch.1), calls=%async_computation | async-start | bytes 2097152 | tf_op jit(solution)/shard_map/all_to_all | solution.py:42
  28.5 14.8 %collective-permute-start.5 = (bf16[2,128,256]{2,1,0:T(8,128)(2,1)S(1)}, bf16[2,128,256]{2,1,0:T(8,128)(2,1)S(1)}, u32[]{:S(2)}, u32[]{:S(2)}) collective-permute-start(bf16[2,128,256]{2,1,0:T(8,128)(2,1)S(1)} %copy-done.7), channel_id=1, source_target_pairs={{0,4},{4,8},{8,12},{12,16},{16,20},{20,24},{24,28},{1,5},{5,9},{9,... | collective-permute-start | bytes 393224 | tf_op jit(solution)/shard_map/ppermute | solution.py:33
  30.9 12.4 %collective-permute-start.6 = (bf16[2,128,256]{2,1,0:T(8,128)(2,1)S(1)}, bf16[2,128,256]{2,1,0:T(8,128)(2,1)S(1)}, u32[]{:S(2)}, u32[]{:S(2)}) collective-permute-start(bf16[2,128,256]{2,1,0:T(8,128)(2,1)S(1)} %copy-done.6), channel_id=1, source_target_pairs={{4,0},{8,4},{12,8},{16,12},{20,16},{24,20},{28,24},{5,1},{9,5},{13... | collective-permute-start | bytes 393224 | tf_op jit(solution)/shard_map/ppermute | solution.py:33
  43.3 4.8 %copy-start.1 = (bf16[576,256]{1,0:T(8,128)(2,1)S(1)}, bf16[576,256]{1,0:T(8,128)(2,1)}, u32[]{:S(2)}) copy-start(bf16[576,256]{1,0:T(8,128)(2,1)} %get-tuple-element.53.refs_0_) | copy-start | bytes 884740
  44.4 9.7 %collective-permute-start.9 = (bf16[448,256]{1,0:T(8,128)(2,1)S(1)}, bf16[448,256]{1,0:T(8,128)(2,1)S(1)}, u32[]{:S(2)}, u32[]{:S(2)}) collective-permute-start(bf16[448,256]{1,0:T(8,128)(2,1)S(1)} %get-tuple-element.89), channel_id=1, source_target_pairs={{0,3},{1,2},{2,1},{3,0},{4,7},{5,6},{6,5},{7,4},{8,11},{9,10},{10,... | collective-permute-start | bytes 688136 | tf_op jit(solution)/shard_map/ppermute | solution.py:38
  48.2 22.1 %collective-permute-start.12 = (bf16[4,128,256]{2,1,0:T(8,128)(2,1)S(1)}, bf16[4,128,256]{2,1,0:T(8,128)(2,1)S(1)}, u32[]{:S(2)}, u32[]{:S(2)}) collective-permute-start(bf16[4,128,256]{2,1,0:T(8,128)(2,1)S(1)} %pad_maximum_fusion.1), channel_id=1, source_target_pairs={{0,24},{4,28},{8,16},{12,20},{16,8},{20,12},{24,0},{28,4},{1,25},{... | collective-permute-start | bytes 786440 | tf_op jit(solution)/shard_map/ppermute | solution.py:38
  51.0 19.3 %collective-permute-start.11 = (bf16[4,128,256]{2,1,0:T(8,128)(2,1)S(1)}, bf16[4,128,256]{2,1,0:T(8,128)(2,1)S(1)}, u32[]{:S(2)}, u32[]{:S(2)}) collective-permute-start(bf16[4,128,256]{2,1,0:T(8,128)(2,1)S(1)} %pad_maximum_fusion.1), channel_id=1, source_target_pairs={{0,16},{4,20},{8,24},{12,28},{16,0},{20,4},{24,8},{28,12},{1,17},{... | collective-permute-start | bytes 786440 | tf_op jit(solution)/shard_map/ppermute | solution.py:38
  51.2 19.1 %collective-permute-start.10 = (bf16[4,128,256]{2,1,0:T(8,128)(2,1)S(1)}, bf16[4,128,256]{2,1,0:T(8,128)(2,1)S(1)}, u32[]{:S(2)}, u32[]{:S(2)}) collective-permute-start(bf16[4,128,256]{2,1,0:T(8,128)(2,1)S(1)} %pad_maximum_fusion.1), channel_id=1, source_target_pairs={{0,8},{4,12},{8,0},{12,4},{16,24},{20,28},{24,16},{28,20},{1,9},{5... | collective-permute-start | bytes 786440 | tf_op jit(solution)/shard_map/ppermute | solution.py:38
  52.6 7.2 %collective-permute-start.8 = (bf16[448,256]{1,0:T(8,128)(2,1)S(1)}, bf16[448,256]{1,0:T(8,128)(2,1)S(1)}, u32[]{:S(2)}, u32[]{:S(2)}) collective-permute-start(bf16[448,256]{1,0:T(8,128)(2,1)S(1)} %get-tuple-element.90), channel_id=1, source_target_pairs={{0,1},{1,0},{2,3},{3,2},{4,5},{5,4},{6,7},{7,6},{8,9},{9,8},{10,11... | collective-permute-start | bytes 688136 | tf_op jit(solution)/shard_map/ppermute | solution.py:38
  54.1 16.2 %collective-permute-start.7 = (bf16[448,256]{1,0:T(8,128)(2,1)S(1)}, bf16[448,256]{1,0:T(8,128)(2,1)S(1)}, u32[]{:S(2)}, u32[]{:S(2)}) collective-permute-start(bf16[448,256]{1,0:T(8,128)(2,1)S(1)} %get-tuple-element.91), channel_id=1, source_target_pairs={{0,2},{1,3},{2,0},{3,1},{4,6},{5,7},{6,4},{7,5},{8,10},{9,11},{10,... | collective-permute-start | bytes 688136 | tf_op jit(solution)/shard_map/ppermute | solution.py:38
  70.4 2.8 %collective-permute-start.13 = (bf16[4,4,128,256]{3,2,1,0:T(8,128)(2,1)S(1)}, bf16[4,4,128,256]{3,2,1,0:T(8,128)(2,1)S(1)}, u32[]{:S(2)}, u32[]{:S(2)}) collective-permute-start(bf16[4,4,128,256]{3,2,1,0:T(8,128)(2,1)S(1)} %pad_maximum_fusion.refs_4_), channel_id=1, source_target_pairs={{0,4},{4,0},{8,12},{12,8},{16,20},{20,16},{24,28},{28,24},{1,5},{5... | collective-permute-start | bytes 3145736 | tf_op jit(solution)/shard_map/ppermute | solution.py:38
  73.3 2.8 %collective-permute-start.14 = (bf16[4,4,128,256]{3,2,1,0:T(8,128)(2,1)S(1)}, bf16[4,4,128,256]{3,2,1,0:T(8,128)(2,1)S(1)}, u32[]{:S(2)}, u32[]{:S(2)}) collective-permute-start(bf16[4,4,128,256]{3,2,1,0:T(8,128)(2,1)S(1)} %get-tuple-element.72), channel_id=1, source_target_pairs={{0,4},{4,0},{8,12},{12,8},{16,20},{20,16},{24,28},{28,24},{1,5},{5... | collective-permute-start | bytes 3145736 | tf_op jit(solution)/shard_map/ppermute | solution.py:38
  76.6 9.2 %collective-permute-start.15 = (bf16[4,128,256]{2,1,0:T(8,128)(2,1)S(1)}, bf16[4,128,256]{2,1,0:T(8,128)(2,1)S(1)}, u32[]{:S(2)}, u32[]{:S(2)}) collective-permute-start(bf16[4,128,256]{2,1,0:T(8,128)(2,1)S(1)} %get-tuple-element.86), channel_id=1, source_target_pairs={{0,8},{4,12},{8,0},{12,4},{16,24},{20,28},{24,16},{28,20},{1,9},{5... | collective-permute-start | bytes 786440 | tf_op jit(solution)/shard_map/ppermute | solution.py:38
  77.2 11.7 %collective-permute-start.17 = (bf16[4,128,256]{2,1,0:T(8,128)(2,1)S(1)}, bf16[4,128,256]{2,1,0:T(8,128)(2,1)S(1)}, u32[]{:S(2)}, u32[]{:S(2)}) collective-permute-start(bf16[4,128,256]{2,1,0:T(8,128)(2,1)S(1)} %get-tuple-element.87), channel_id=1, source_target_pairs={{0,24},{4,28},{8,16},{12,20},{16,8},{20,12},{24,0},{28,4},{1,25},{... | collective-permute-start | bytes 786440 | tf_op jit(solution)/shard_map/ppermute | solution.py:38
  77.2 14.7 %collective-permute-start.16 = (bf16[4,128,256]{2,1,0:T(8,128)(2,1)S(1)}, bf16[4,128,256]{2,1,0:T(8,128)(2,1)S(1)}, u32[]{:S(2)}, u32[]{:S(2)}) collective-permute-start(bf16[4,128,256]{2,1,0:T(8,128)(2,1)S(1)} %get-tuple-element.88), channel_id=1, source_target_pairs={{0,16},{4,20},{8,24},{12,28},{16,0},{20,4},{24,8},{28,12},{1,17},{... | collective-permute-start | bytes 786440 | tf_op jit(solution)/shard_map/ppermute | solution.py:38
  80.2 13.9 %collective-permute-start.23 = (bf16[448,256]{1,0:T(8,128)(2,1)S(1)}, bf16[448,256]{1,0:T(8,128)(2,1)S(1)}, u32[]{:S(2)}, u32[]{:S(2)}) collective-permute-start(bf16[448,256]{1,0:T(8,128)(2,1)S(1)} %get-tuple-element.93), channel_id=1, source_target_pairs={{0,3},{1,2},{2,1},{3,0},{4,7},{5,6},{6,5},{7,4},{8,11},{9,10},{10,... | collective-permute-start | bytes 688136 | tf_op jit(solution)/shard_map/ppermute | solution.py:38
  82.0 22.5 %collective-permute-start.22 = (bf16[448,256]{1,0:T(8,128)(2,1)S(1)}, bf16[448,256]{1,0:T(8,128)(2,1)S(1)}, u32[]{:S(2)}, u32[]{:S(2)}) collective-permute-start(bf16[448,256]{1,0:T(8,128)(2,1)S(1)} %get-tuple-element.94), channel_id=1, source_target_pairs={{0,2},{1,3},{2,0},{3,1},{4,6},{5,7},{6,4},{7,5},{8,10},{9,11},{10,... | collective-permute-start | bytes 688136 | tf_op jit(solution)/shard_map/ppermute | solution.py:38
  85.7 18.8 %collective-permute-start.21 = (bf16[448,256]{1,0:T(8,128)(2,1)S(1)}, bf16[448,256]{1,0:T(8,128)(2,1)S(1)}, u32[]{:S(2)}, u32[]{:S(2)}) collective-permute-start(bf16[448,256]{1,0:T(8,128)(2,1)S(1)} %get-tuple-element.95), channel_id=1, source_target_pairs={{0,1},{1,0},{2,3},{3,2},{4,5},{5,4},{6,7},{7,6},{8,9},{9,8},{10,11... | collective-permute-start | bytes 688136 | tf_op jit(solution)/shard_map/ppermute | solution.py:38
  92.1 14.0 %collective-permute-start.18 = (bf16[128,256]{1,0:T(8,128)(2,1)S(1)}, bf16[128,256]{1,0:T(8,128)(2,1)S(1)}, u32[]{:S(2)}, u32[]{:S(2)}) collective-permute-start(bf16[128,256]{1,0:T(8,128)(2,1)S(1)} %get-tuple-element.96), channel_id=1, source_target_pairs={{0,1},{1,0},{2,3},{3,2},{4,5},{5,4},{6,7},{7,6},{8,9},{9,8},{10,11... | collective-permute-start | bytes 196616 | tf_op jit(solution)/shard_map/ppermute | solution.py:38
  92.2 13.9 %collective-permute-start.20 = (bf16[128,256]{1,0:T(8,128)(2,1)S(1)}, bf16[128,256]{1,0:T(8,128)(2,1)S(1)}, u32[]{:S(2)}, u32[]{:S(2)}) collective-permute-start(bf16[128,256]{1,0:T(8,128)(2,1)S(1)} %get-tuple-element.97), channel_id=1, source_target_pairs={{0,3},{1,2},{2,1},{3,0},{4,7},{5,6},{6,5},{7,4},{8,11},{9,10},{10,... | collective-permute-start | bytes 196616 | tf_op jit(solution)/shard_map/ppermute | solution.py:38
  94.1 12.0 %collective-permute-start.19 = (bf16[128,256]{1,0:T(8,128)(2,1)S(1)}, bf16[128,256]{1,0:T(8,128)(2,1)S(1)}, u32[]{:S(2)}, u32[]{:S(2)}) collective-permute-start(bf16[128,256]{1,0:T(8,128)(2,1)S(1)} %get-tuple-element.98), channel_id=1, source_target_pairs={{0,2},{1,3},{2,0},{3,1},{4,6},{5,7},{6,4},{7,5},{8,10},{9,11},{10,... | collective-permute-start | bytes 196616 | tf_op jit(solution)/shard_map/ppermute | solution.py:38

commit v17 on v16

--- a/solution.py
+++ b/solution.py
@@ -27,10 +27,10 @@
     return value.astype(jnp.float32)
 
 
-def shifted(value, axis, by):
+def swapped_beside(value, axis):
     size = lax.axis_size(axis)
-    pairs = [(i, i + by) for i in range(size) if 0 <= i + by < size]
-    return lax.ppermute(value, axis, pairs)
+    pairs = [(i, (i + 1) % size) for i in range(1, size, 2)]
+    return lax.ppermute(value, axis, pairs + [(j, i) for i, j in pairs])
 
 
 def swapped(value, axis, by):
@@ -60,7 +60,7 @@
     reach, groups, send_slots, shuffle, cols, count, gc, pc, gx, px, slopes, adj, features, weight, *refs
 ):
     clean, outgoing, *refs = refs
-    sides, packed, refs = refs[:4], refs[4 : 4 + groups], refs[4 + groups :]
+    sides, packed, refs = refs[:2], refs[2 : 2 + groups], refs[2 + groups :]
     data, tiles, rhs, stage, results, halos, packs, places, used, sems, pack_sems, out_sems = refs
     blocks, slots, rows, _ = adj.shape
     width = gc.shape[1]
@@ -147,9 +147,10 @@
         else:
             side, at = int(block >= 0), first % (blocks + reach)
             halos[side, 0, at : at + 2], halos[side, 1, at : at + 2] = pair(first)
+            slot = (me[0] & 1) ^ (1 - side)
             done = []
             for i in range(2):
-                source, target = halos.at[side, i, at : at + 2], sides[2 * i + side].at[at : at + 2]
+                source, target = halos.at[side, i, at : at + 2], sides[i].at[slot, at : at + 2]
                 done.append(pltpu.make_async_copy(source, target, out_sems.at[2 + i, first]))
         for copy in done:
             copy.start()
@@ -185,9 +186,9 @@
     return pl.pallas_call(
         functools.partial(aggregate_kernel, reach, groups, send_slots),
         in_specs=[IN_SMEM] * 3 + [IN_HBM] * 4 + [IN_VMEM] + [IN_HBM] * 3,
-        out_specs=[IN_HBM] * (6 + groups),
+        out_specs=[IN_HBM] * (4 + groups),
         out_shape=[bf16(blocks, rows, width), bf16(devs * send_slots, rows, width)]
-        + [bf16(reach, rows, width)] * 4
+        + [bf16(2, reach, rows, width)] * 2
         + [bf16(packed, width)] * groups,
         scratch_shapes=[
             pltpu.VMEM((4, blocks // 2, 2 * rows, width), jnp.bfloat16),
@@ -213,11 +214,12 @@
     )(shuffle, cols, count, gc, pc, gx, px, slopes, adj, features, weight)
 
 
-def patch_kernel(reach, blocks, slots, index, shuffle, outgoing, low, high, out, *scratch):
+def patch_kernel(reach, blocks, slots, index, shuffle, outgoing, pair, beside, out, *scratch):
     held, other, ready, places, used, sems = scratch
+    odd = index[0] & 1
     arrivals = [
-        pltpu.make_async_copy(side, other.at[i * reach : (i + 1) * reach], sems.at[2, i])
-        for i, side in enumerate((low, high))
+        pltpu.make_async_copy(pair, other.at[pl.ds((1 - odd) * reach, reach)], sems.at[2, 0]),
+        pltpu.make_async_copy(beside, other.at[pl.ds(odd * reach, reach)], sems.at[2, 1]),
     ]
     for copy in arrivals:
         copy.start()
@@ -240,9 +242,9 @@
         copy.wait()
 
 
-def patch(index, shuffle, outgoing, low, high, blocks, slots):
+def patch(index, shuffle, outgoing, pair, beside, blocks, slots):
     sent, rows, width = outgoing.shape
-    reach = low.shape[0]
+    reach = pair.shape[0]
     border = pltpu.VMEM((2 * reach, rows, width), jnp.bfloat16)
     return pl.pallas_call(
         functools.partial(patch_kernel, reach, blocks, slots),
@@ -260,19 +262,20 @@
         ],
         compiler_params=params(VMEM_ALL),
         name="patch",
-    )(index, shuffle, outgoing, low, high)
-
-
-def merge_kernel(quarter, index, landing, clean, low, high, incoming, out, whole):
+    )(index, shuffle, outgoing, pair, beside)
+
+
+def merge_kernel(quarter, index, landing, clean, pair, beside, incoming, out, whole):
     blocks, rows, _ = clean.shape
-    reach = low.shape[0]
+    reach = pair.shape[0]
     group = index[1]
     piece = math.gcd(rows, quarter)
     for block in range(blocks):
         whole[block] = wide(clean[block])
+    odd = index[0] & 1
     for i in range(reach):
-        whole[i] += wide(low[i])
-        whole[blocks - reach + i] += wide(high[i])
+        whole[(1 - odd) * (blocks - reach) + i] += wide(pair[i])
+        whole[odd * (blocks - reach) + i] += wide(beside[i])
     for place in range(incoming.shape[0]):
         block = landing[place]
 
@@ -288,7 +291,7 @@
                 ]
 
 
-def merge(index, landing, clean, low, high, incoming, groups):
+def merge(index, landing, clean, pair, beside, incoming, groups):
     blocks, rows, width = clean.shape
     quarter = blocks * rows // groups
     return pl.pallas_call(
@@ -299,7 +302,7 @@
         scratch_shapes=[pltpu.VMEM((blocks, rows, width), jnp.float32)],
         compiler_params=params(),
         name="merge",
-    )(index, landing, clean, low, high, incoming)
+    )(index, landing, clean, pair, beside, incoming)
 
 
 def weight_kernel(devs, index, *refs):
@@ -463,20 +466,21 @@
     args = (shuffle_from, adj_cols.T, adj_count)
     args += (grad_clean, pre_clean, grad_corrupt, pre_corrupt, slopes[None, :], adj_vals)
     clean, outgoing, *sides = aggregate(*args, features, weight, reach, devs, groups)
-    sides, packed = sides[:4], sides[4:]
-    low, high = shifted(sides[3], "node", 1), shifted(sides[2], "node", -1)
+    (clean_side, side), packed = sides[:2], sides[2:]
+    pair, beside = swapped(side[0], "node", 1), swapped_beside(side[1], "node")
     for i in exchange_order(groups):
         packed[i] = swapped(packed[i], "chan", i)
 
-    outgoing = patch(index, shuffle_from, outgoing, low, high, blocks, slots)
-    shuffle_from, outgoing, clean, sides = lax.optimization_barrier(
-        (shuffle_from, outgoing, clean, sides)
+    outgoing = patch(index, shuffle_from, outgoing, pair, beside, blocks, slots)
+    shuffle_from, outgoing, clean, clean_side = lax.optimization_barrier(
+        (shuffle_from, outgoing, clean, clean_side)
     )
-    low, high = shifted(sides[1], "node", 1), shifted(sides[0], "node", -1)
+    clean_pair = swapped(clean_side[0], "node", 1)
+    clean_beside = swapped_beside(clean_side[1], "node")
     landing = landing_blocks(shuffle_from, me, blocks, devs, slots)
     incoming = exchanged(outgoing, "node")
     incoming, packed = lax.optimization_barrier((incoming, packed))
-    merged = merge(index, landing, clean, low, high, incoming, groups)
+    merged = merge(index, landing, clean, clean_pair, clean_beside, incoming, groups)
 
     quarter = row_count // groups
     summed = [merged[0]] + [None] * (groups - 1)

time: 107 us -> 104 us (0.972)
  starting transfers between devices: 44.2 us -> 36.1 us
  waiting for transfers between devices: 38.7 us -> 43.2 us
    ppermute x20 -> x22, waiting for transfers between devices: 31.9 us -> 38.7 us  [swapped(): return lax.ppermute(value, axis, [(i, i ^ by) for i in range(size)])]
    all_to_all x1, waiting for transfers between devices: 6.8 us -> 2.63 us  [exchanged(): return lax.all_to_all(value, axis, split_axis=0, concat_axis=0, tiled=True)]
    ppermute x20 -> x22, starting transfers between devices: 30.3 us -> 26.3 us  [swapped(): return lax.ppermute(value, axis, [(i, i ^ by) for i in range(size)])]
    all_to_all x1, starting transfers between devices: 6.63 us -> 3.7 us  [exchanged(): return lax.all_to_all(value, axis, split_axis=0, concat_axis=0, tiled=True)]
    ppermute x4 -> x2, waiting for transfers between devices: 0.01 us -> 1.86 us  [swapped_beside(): return lax.ppermute(value, axis, pairs + [(j, i) for i, j in pairs])]
    ppermute x4 -> x2, starting transfers between devices: 7.35 us -> 6.05 us  [swapped_beside(): return lax.ppermute(value, axis, pairs + [(j, i) for i, j in pairs])]
  transfers between devices with their start and end apart: 25 -> 25, of which waited for: 9 -> 11; matrix products, arithmetic and copies ran while one was open for 2% -> 2% of each run, Pallas kernels for 9% -> 10%
where the time goes in v17:
time: 104 us
  waiting for transfers between devices  43.2 us (42%)
  starting transfers between devices  36.1 us (35%)
  Pallas kernels  19.1 us (18%)
  other arithmetic  2.5 us (2%)
  local copies, waits for them, and re-layouts  2.3 us (2%)
    ppermute x22, waiting for transfers between devices, swapped(): return lax.ppermute(value, axis, [(i, i ^ by) for i in range(size)])  38.7 us
    ppermute x22, starting transfers between devices, swapped(): return lax.ppermute(value, axis, [(i, i ^ by) for i in range(size)])  26.3 us
    pallas_call x1, Pallas kernels, aggregate(): pl.pallas_call(functools.partial(aggregate_kernel, reach, groups, send_sl...  7.92 us
    ppermute x2, starting transfers between devices, swapped_beside(): return lax.ppermute(value, axis, pairs + [(j, i) for i, j in pairs])  6.05 us
    all_to_all x1, starting transfers between devices, exchanged(): return lax.all_to_all(value, axis, split_axis=0, concat_axis=0, tiled=True)  3.7 us
    pallas_call x2, Pallas kernels, feature_rows(): pl.pallas_call(functools.partial(feature_kernel, first), in_specs=[IN_SME...  3.33 us
    pallas_call x1, Pallas kernels, weight_partial(): pl.pallas_call(functools.partial(weight_kernel, devs), in_specs=[IN_SMEM]...  2.65 us
    all_to_all x1, waiting for transfers between devices, exchanged(): return lax.all_to_all(value, axis, split_axis=0, concat_axis=0, tiled=True)  2.63 us
  transfers between devices with their start and end apart: 25, of which 11 were waited for; matrix products, arithmetic and copies ran while one was open for 2% of the time, Pallas kernels for 10%

profile of v17, /device:TPU:0, one launch (start us, length us, event | category | flops | bytes accessed | tf_op | source)
XLA Modules:
  0.0 104.1 jit_solution(1693116864542382802)
XLA Ops:
  0.6 7.9 %aggregate.1 = (bf16[14,128,256]{2,1,0:T(8,128)(2,1)}, bf16[16,128,256]{2,1,0:T(8,128)(2,1)}, bf16[2,2,128,256]{3,2,1,0:T(8,128)(2,1)}, bf16[2,2,128,256]{3,2,1,...) custom-call(s32[112]{0:T(128)} %shuffle.3, ...), custom_call_target="tpu_custom_call" | custom-call | flops 1174405120 | bytes 7798784 | tf_op jit(solution)/shard_map/aggregate/pallas_call | solution.py:186
  8.6 1.0 slice_bitcast_fusion.14
  9.6 3.4 %collective-permute-start.1 = (bf16[2,128,256]{2,1,0:T(8,128)(2,1)S(1)}, bf16[2,128,256]{2,1,0:T(8,128)(2,1)S(1)}, u32[]{:S(2)}, u32[]{:S(2)}) collective-permute-start(bf16[2,128,256]{2,1,0:T(8,128)(2,1)S(1)} %get-tuple-element.95), channel_id=1, source_target_pairs={{4,8},{12,16},{20,24},{28,0},{8,4},{16,12},{24,20},{0,28},{5,9},{1... | collective-permute-start | bytes 393224 | tf_op jit(solution)/shard_map/ppermute | solution.py:33
  12.9 0.0 collective-permute-start
  12.9 1.6 %collective-permute-start.2 = (bf16[576,256]{1,0:T(8,128)(2,1)}, bf16[576,256]{1,0:T(8,128)(2,1)S(1)}, u32[]{:S(2)}, u32[]{:S(2)}) collective-permute-start(bf16[576,256]{1,0:T(8,128)(2,1)} %get-tuple-element.45), channel_id=1, source_target_pairs={{0,1},{1,0},{2,3},{3,2},{4,5},{5,4},{6,7},{7,6},{8,9},{9,8},{10,11... | collective-permute-start | bytes 884744 | tf_op jit(solution)/shard_map/ppermute | solution.py:38
  14.5 2.6 %collective-permute-start.3 = (bf16[576,256]{1,0:T(8,128)(2,1)}, bf16[576,256]{1,0:T(8,128)(2,1)S(1)}, u32[]{:S(2)}, u32[]{:S(2)}) collective-permute-start(bf16[576,256]{1,0:T(8,128)(2,1)} %get-tuple-element.46), channel_id=1, source_target_pairs={{0,2},{1,3},{2,0},{3,1},{4,6},{5,7},{6,4},{7,5},{8,10},{9,11},{10,... | collective-permute-start | bytes 884744 | tf_op jit(solution)/shard_map/ppermute | solution.py:38
  17.1 0.2 collective-permute-start.4
  17.3 0.6 pad_add_fusion.index
  17.9 0.0 collective-permute-done.1.beside
  17.9 0.0 collective-permute-done.pair
  17.9 0.0 copy-start.5
  18.0 0.6 copy-done.4
  18.6 0.1 copy-done.5
  18.6 2.6 %patch.1 = bf16[16,128,256]{2,1,0:T(8,128)(2,1)} custom-call(s32[2]{0:T(128)} %pad_add_fusion.index, s32[112]{0:T(128)} %shuffle.3, bf16[16,128,256]{2,1,0:T(8,128)(2,1)} %get-tuple-element.39.outgoing, bf16[2,128,256]{2,1,0:T(8,128)(2,1)} %copy-done.5, bf16[2,128,256]{2,1,0:T(8,128)(2,1)} %copy-done.4), custom_call_target="tpu_custom_call", output_to_operand_aliasing={{}: (2, {})} | custom-call | tf_op jit(solution)/shard_map/patch/pallas_call | solution.py:249
  21.3 3.7 %all-to-all-start = ((bf16[16,128,256]{2,1,0:T(8,128)(2,1)}), bf16[16,128,256]{2,1,0:T(8,128)(2,1)S(1)}, u32[]{:S(2)}, u32[]{:S(2)}) async-start(bf16[16,128,256]{2,1,0:T(8,128)(2,1)} %patch.1), calls=%async_computation | async-start | bytes 2097152 | tf_op jit(solution)/shard_map/all_to_all | solution.py:42
  25.0 0.1 eq.30
  25.1 0.1 add.45
  25.2 0.3 convert_reduce_fusion
  25.5 0.1 copy.14
  25.6 2.7 %collective-permute-start.6 = (bf16[2,128,256]{2,1,0:T(8,128)(2,1)S(1)}, bf16[2,128,256]{2,1,0:T(8,128)(2,1)S(1)}, u32[]{:S(2)}, u32[]{:S(2)}) collective-permute-start(bf16[2,128,256]{2,1,0:T(8,128)(2,1)S(1)} %get-tuple-element.93), channel_id=1, source_target_pairs={{4,8},{12,16},{20,24},{28,0},{8,4},{16,12},{24,20},{0,28},{5,9},{1... | collective-permute-start | bytes 393224 | tf_op jit(solution)/shard_map/ppermute | solution.py:33
  28.3 0.1 select_reduce_fusion
  28.5 0.1 copy.15
  28.5 0.1 sub.13.landing
  28.6 0.0 collective-permute-done.2.refs_1_
  28.6 9.5 %collective-permute-done.3.refs_2_ = bf16[576,256]{1,0:T(8,128)(2,1)S(1)} collective-permute-done((bf16[576,256]{1,0:T(8,128)(2,1)}, bf16[576,256]{1,0:T(8,128)(2,1)S(1)}, u32[]{:S(2)}, u32[]{:S(2)}) %collective-permute-start.3) | collective-permute-done | bytes 294944 | tf_op jit(solution)/shard_map/ppermute | solution.py:38
  38.2 0.0 collective-permute-done.4.refs_3_
  38.2 2.6 %all-to-all-done.incoming = bf16[16,128,256]{2,1,0:T(8,128)(2,1)S(1)} async-done(((bf16[16,128,256]{2,1,0:T(8,128)(2,1)}), bf16[16,128,256]{2,1,0:T(8,128)(2,1)S(1)}, u32[]{:S(2)}, u32[]{:S(2)}) %all-to-all-start) | async-done | bytes 1048608 | tf_op jit(solution)/shard_map/all_to_all | solution.py:42
  40.8 1.9 %collective-permute-done.6.beside = bf16[2,128,256]{2,1,0:T(8,128)(2,1)S(1)} collective-permute-done((bf16[2,128,256]{2,1,0:T(8,128)(2,1)S(1)}, bf16[2,128,256]{2,1,0:T(8,128)(2,1)S(1)}, u32[]{:S(2)}, u32[]{:S(2)}) %collective-permute-start.6) | collective-permute-done | bytes 131104 | tf_op jit(solution)/shard_map/ppermute | solution.py:33
  42.7 0.0 collective-permute-done.5.pair
  42.7 1.1 %merge.1 = bf16[4,448,256]{2,1,0:T(8,128)(2,1)S(1)} custom-call(s32[2]{0:T(128)S(1)} %copy-done.2, s32[16]{0:T(128)S(1)} %sub.13.landing, bf16[14,128,256]{2,1,0:T(8,128)(2,1)S(1)} %copy-done, bf16[2,128,256]{2,1,0:T(8,128)(2,1)S(1)} %collective-permute-done.5.pair, bf16[2,128,256]{2,1,0:T(8,128)(2,1)S(1)} %collective-permute-done.6.beside, ...), custom_call_target="tpu_custom_call" | custom-call | tf_op jit(solution)/shard_map/merge/pallas_call | solution.py:297
  43.7 0.1 slice_bitcast_fusion.4
  43.8 3.7 %collective-permute-start.9 = (bf16[448,256]{1,0:T(8,128)(2,1)S(1)}, bf16[448,256]{1,0:T(8,128)(2,1)S(1)}, u32[]{:S(2)}, u32[]{:S(2)}) collective-permute-start(bf16[448,256]{1,0:T(8,128)(2,1)S(1)} %get-tuple-element.83), channel_id=1, source_target_pairs={{0,3},{1,2},{2,1},{3,0},{4,7},{5,6},{6,5},{7,4},{8,11},{9,10},{10,... | collective-permute-start | bytes 688136 | tf_op jit(solution)/shard_map/ppermute | solution.py:38
  47.6 0.7 collective-permute-start.12
  48.2 0.6 collective-permute-start.11
  48.8 2.3 %collective-permute-start.10 = (bf16[4,128,256]{2,1,0:T(8,128)(2,1)S(1)}, bf16[4,128,256]{2,1,0:T(8,128)(2,1)S(1)}, u32[]{:S(2)}, u32[]{:S(2)}) collective-permute-start(bf16[4,128,256]{2,1,0:T(8,128)(2,1)S(1)} %pad_maximum_fusion.1), channel_id=1, source_target_pairs={{0,8},{4,12},{8,0},{12,4},{16,24},{20,28},{24,16},{28,20},{1,9},{5... | collective-permute-start | bytes 786440 | tf_op jit(solution)/shard_map/ppermute | solution.py:38
  51.1 0.0 collective-permute-start.8
  51.1 3.1 %collective-permute-done.9.refs_7_.refs_3_ = bf16[448,256]{1,0:T(8,128)(2,1)S(1)} collective-permute-done((bf16[448,256]{1,0:T(8,128)(2,1)S(1)}, bf16[448,256]{1,0:T(8,128)(2,1)S(1)}, u32[]{:S(2)}, u32[]{:S(2)}) %collective-permute-start.9) | collective-permute-done | bytes 229408 | tf_op jit(solution)/shard_map/ppermute | solution.py:38
  54.2 4.3 %collective-permute-start.7 = (bf16[448,256]{1,0:T(8,128)(2,1)S(1)}, bf16[448,256]{1,0:T(8,128)(2,1)S(1)}, u32[]{:S(2)}, u32[]{:S(2)}) collective-permute-start(bf16[448,256]{1,0:T(8,128)(2,1)S(1)} %get-tuple-element.85), channel_id=1, source_target_pairs={{0,2},{1,3},{2,0},{3,1},{4,6},{5,7},{6,4},{7,5},{8,10},{9,11},{10,... | collective-permute-start | bytes 688136 | tf_op jit(solution)/shard_map/ppermute | solution.py:38
  58.4 1.4 %collective-permute-done.8.refs_5_.refs_1_ = bf16[448,256]{1,0:T(8,128)(2,1)S(1)} collective-permute-done((bf16[448,256]{1,0:T(8,128)(2,1)S(1)}, bf16[448,256]{1,0:T(8,128)(2,1)S(1)}, u32[]{:S(2)}, u32[]{:S(2)}) %collective-permute-start.8) | collective-permute-done | bytes 229408 | tf_op jit(solution)/shard_map/ppermute | solution.py:38
  59.9 7.7 %collective-permute-done.7.refs_6_.refs_2_ = bf16[448,256]{1,0:T(8,128)(2,1)S(1)} collective-permute-done((bf16[448,256]{1,0:T(8,128)(2,1)S(1)}, bf16[448,256]{1,0:T(8,128)(2,1)S(1)}, u32[]{:S(2)}, u32[]{:S(2)}) %collective-permute-start.7) | collective-permute-done | bytes 229408 | tf_op jit(solution)/shard_map/ppermute | solution.py:38
  67.5 0.0 collective-permute-done.12
  67.5 0.0 collective-permute-done.11
  67.5 0.1 pad_maximum_fusion.refs_4_
  67.7 0.1 collective-permute-start.13
  67.8 2.7 %weight_partial.1 = (bf16[4,4,128,256]{3,2,1,0:T(8,128)(2,1)S(1)}, bf16[4,4,128,256]{3,2,1,0:T(8,128)(2,1)S(1)}) custom-call(s32[2]{0:T(128)S(1)} %copy-done.2, bf16[576,256]{1,0:T(8,128)(2,1)S(1)} %copy-done.1, bf16[576,256]{1,0:T(8,128)(2,1)S(1)} %collective-permute-done.2.refs_1_, bf16[576,256]{1,0:T(8,128)(2,1)S(1)} %collective-permute-done.3.refs_2_, ...), custom_call_target="tpu_custom_call" | custom-call | flops 939524096 | bytes 3932160 | tf_op jit(solution)/shard_map/weight_partial/pallas_call | solution.py:338
  70.4 0.5 collective-permute-start.14
  71.0 2.3 %feature_rows.2 = bf16[3,448,256]{2,1,0:T(8,128)(2,1)S(1)} custom-call(s32[2]{0:T(128)S(1)} %copy-done.2, bf16[448,256]{1,0:T(8,128)(2,1)S(1)} %get-tuple-element.69.refs_4_.refs_0_, bf16[448,256]{1,0:T(8,128)(2,1)S(1)} %collective-permute-done.8.refs_5_.refs_1_, bf16[448,256]{1,0:T(8,128)(2,1)S(1)} %collective-permute-done.7.refs_6_.refs_2_, ...), custom_call_target="tpu_custom_call" | custom-call | flops 704643072 | bytes 3178496 | tf_op jit(solution)/shard_map/feature_rows/pallas_call | solution.py:386
  73.3 0.4 convert_add_fusion
  73.7 0.1 slice_bitcast_fusion.3
  73.8 1.7 %collective-permute-start.15 = (bf16[4,128,256]{2,1,0:T(8,128)(2,1)S(1)}, bf16[4,128,256]{2,1,0:T(8,128)(2,1)S(1)}, u32[]{:S(2)}, u32[]{:S(2)}) collective-permute-start(bf16[4,128,256]{2,1,0:T(8,128)(2,1)S(1)} %get-tuple-element.80), channel_id=1, source_target_pairs={{0,8},{4,12},{8,0},{12,4},{16,24},{20,28},{24,16},{28,20},{1,9},{5... | collective-permute-start | bytes 786440 | tf_op jit(solution)/shard_map/ppermute | solution.py:38
  75.5 2.0 %collective-permute-start.17 = (bf16[4,128,256]{2,1,0:T(8,128)(2,1)S(1)}, bf16[4,128,256]{2,1,0:T(8,128)(2,1)S(1)}, u32[]{:S(2)}, u32[]{:S(2)}) collective-permute-start(bf16[4,128,256]{2,1,0:T(8,128)(2,1)S(1)} %get-tuple-element.81), channel_id=1, source_target_pairs={{0,24},{4,28},{8,16},{12,20},{16,8},{20,12},{24,0},{28,4},{1,25},{... | collective-permute-start | bytes 786440 | tf_op jit(solution)/shard_map/ppermute | solution.py:38
  77.5 1.9 %collective-permute-start.23 = (bf16[448,256]{1,0:T(8,128)(2,1)S(1)}, bf16[448,256]{1,0:T(8,128)(2,1)S(1)}, u32[]{:S(2)}, u32[]{:S(2)}) collective-permute-start(bf16[448,256]{1,0:T(8,128)(2,1)S(1)} %get-tuple-element.87), channel_id=1, source_target_pairs={{0,3},{1,2},{2,1},{3,0},{4,7},{5,6},{6,5},{7,4},{8,11},{9,10},{10,... | collective-permute-start | bytes 688136 | tf_op jit(solution)/shard_map/ppermute | solution.py:38
  79.4 3.6 %collective-permute-done.15 = bf16[4,128,256]{2,1,0:T(8,128)(2,1)S(1)} collective-permute-done((bf16[4,128,256]{2,1,0:T(8,128)(2,1)S(1)}, bf16[4,128,256]{2,1,0:T(8,128)(2,1)S(1)}, u32[]{:S(2)}, u32[]{:S(2)}) %collective-permute-start.15) | collective-permute-done | bytes 262176 | tf_op jit(solution)/shard_map/ppermute | solution.py:38
  83.0 6.7 %collective-permute-done.17 = bf16[4,128,256]{2,1,0:T(8,128)(2,1)S(1)} collective-permute-done((bf16[4,128,256]{2,1,0:T(8,128)(2,1)S(1)}, bf16[4,128,256]{2,1,0:T(8,128)(2,1)S(1)}, u32[]{:S(2)}, u32[]{:S(2)}) %collective-permute-start.17) | collective-permute-done | bytes 262176 | tf_op jit(solution)/shard_map/ppermute | solution.py:38
  89.7 1.4 %collective-permute-done.16 = bf16[4,128,256]{2,1,0:T(8,128)(2,1)S(1)} collective-permute-done((bf16[4,128,256]{2,1,0:T(8,128)(2,1)S(1)}, bf16[4,128,256]{2,1,0:T(8,128)(2,1)S(1)}, u32[]{:S(2)}, u32[]{:S(2)}) %collective-permute-start.16) | collective-permute-done | bytes 262176 | tf_op jit(solution)/shard_map/ppermute | solution.py:38
  91.0 0.2 fusion.10
  91.2 0.1 collective-permute-start.18
  91.3 1.4 %collective-permute-start.20 = (bf16[128,256]{1,0:T(8,128)(2,1)S(1)}, bf16[128,256]{1,0:T(8,128)(2,1)S(1)}, u32[]{:S(2)}, u32[]{:S(2)}) collective-permute-start(bf16[128,256]{1,0:T(8,128)(2,1)S(1)} %get-tuple-element.91), channel_id=1, source_target_pairs={{0,3},{1,2},{2,1},{3,0},{4,7},{5,6},{6,5},{7,4},{8,11},{9,10},{10,... | collective-permute-start | bytes 196616 | tf_op jit(solution)/shard_map/ppermute | solution.py:38
  92.8 2.7 %collective-permute-start.19 = (bf16[128,256]{1,0:T(8,128)(2,1)S(1)}, bf16[128,256]{1,0:T(8,128)(2,1)S(1)}, u32[]{:S(2)}, u32[]{:S(2)}) collective-permute-start(bf16[128,256]{1,0:T(8,128)(2,1)S(1)} %get-tuple-element.92), channel_id=1, source_target_pairs={{0,2},{1,3},{2,0},{3,1},{4,6},{5,7},{6,4},{7,5},{8,10},{9,11},{10,... | collective-permute-start | bytes 196616 | tf_op jit(solution)/shard_map/ppermute | solution.py:38
  95.5 1.0 feature_rows.3
  96.5 5.3 %collective-permute-done.22.refs_2_ = bf16[448,256]{1,0:T(8,128)(2,1)S(1)} collective-permute-done((bf16[448,256]{1,0:T(8,128)(2,1)S(1)}, bf16[448,256]{1,0:T(8,128)(2,1)S(1)}, u32[]{:S(2)}, u32[]{:S(2)}) %collective-permute-start.22) | collective-permute-done | bytes 229408 | tf_op jit(solution)/shard_map/ppermute | solution.py:38
  101.7 1.5 %laid_out.1 = bf16[1792,256]{1,0:T(8,128)(2,1)} custom-call(s32[2]{0:T(128)S(1)} %copy-done.2, bf16[448,256]{1,0:T(8,128)(2,1)S(1)} %bitcast.68, bf16[448,256]{1,0:T(8,128)(2,1)S(1)} %collective-permute-done.21.refs_1_, bf16[448,256]{1,0:T(8,128)(2,1)S(1)} %collective-permute-done.22.refs_2_, bf16[448,256]{1,0:T(8,128)(2,1)S(1)} %collective-permute-done.23.refs_3_), custom_call_target="tpu_custom_call" | custom-call | tf_op jit(solution)/shard_map/laid_out/pallas_call | solution.py:418
  103.3 0.2 collective-permute-done.19
  103.4 0.7 fusion.5
  (32 shorter events, 0.2 us)
Async XLA Ops:
  9.6 8.4 %collective-permute-start.1 = (bf16[2,128,256]{2,1,0:T(8,128)(2,1)S(1)}, bf16[2,128,256]{2,1,0:T(8,128)(2,1)S(1)}, u32[]{:S(2)}, u32[]{:S(2)}) collective-permute-start(bf16[2,128,256]{2,1,0:T(8,128)(2,1)S(1)} %get-tuple-element.95), channel_id=1, source_target_pairs={{4,8},{12,16},{20,24},{28,0},{8,4},{16,12},{24,20},{0,28},{5,9},{1... | collective-permute-start | bytes 393224 | tf_op jit(solution)/shard_map/ppermute | solution.py:33
  12.9 5.0 %collective-permute-start = (bf16[2,128,256]{2,1,0:T(8,128)(2,1)S(1)}, bf16[2,128,256]{2,1,0:T(8,128)(2,1)S(1)}, u32[]{:S(2)}, u32[]{:S(2)}) collective-permute-start(bf16[2,128,256]{2,1,0:T(8,128)(2,1)S(1)} %get-tuple-element.96), channel_id=1, source_target_pairs={{0,4},{4,0},{8,12},{12,8},{16,20},{20,16},{24,28},{28,24},{1,5},{5... | collective-permute-start | bytes 393224 | tf_op jit(solution)/shard_map/ppermute | solution.py:38
  12.9 15.7 %collective-permute-start.2 = (bf16[576,256]{1,0:T(8,128)(2,1)}, bf16[576,256]{1,0:T(8,128)(2,1)S(1)}, u32[]{:S(2)}, u32[]{:S(2)}) collective-permute-start(bf16[576,256]{1,0:T(8,128)(2,1)} %get-tuple-element.45), channel_id=1, source_target_pairs={{0,1},{1,0},{2,3},{3,2},{4,5},{5,4},{6,7},{7,6},{8,9},{9,8},{10,11... | collective-permute-start | bytes 884744 | tf_op jit(solution)/shard_map/ppermute | solution.py:38
  14.5 23.6 %collective-permute-start.3 = (bf16[576,256]{1,0:T(8,128)(2,1)}, bf16[576,256]{1,0:T(8,128)(2,1)S(1)}, u32[]{:S(2)}, u32[]{:S(2)}) collective-permute-start(bf16[576,256]{1,0:T(8,128)(2,1)} %get-tuple-element.46), channel_id=1, source_target_pairs={{0,2},{1,3},{2,0},{3,1},{4,6},{5,7},{6,4},{7,5},{8,10},{9,11},{10,... | collective-permute-start | bytes 884744 | tf_op jit(solution)/shard_map/ppermute | solution.py:38
  17.1 21.0 %collective-permute-start.4 = (bf16[576,256]{1,0:T(8,128)(2,1)}, bf16[576,256]{1,0:T(8,128)(2,1)S(1)}, u32[]{:S(2)}, u32[]{:S(2)}) collective-permute-start(bf16[576,256]{1,0:T(8,128)(2,1)} %get-tuple-element.47), channel_id=1, source_target_pairs={{0,3},{1,2},{2,1},{3,0},{4,7},{5,6},{6,5},{7,4},{8,11},{9,10},{10,... | collective-permute-start | bytes 884744 | tf_op jit(solution)/shard_map/ppermute | solution.py:38
  17.9 0.6 copy-start.4
  17.9 0.7 copy-start.5
  18.6 6.4 %copy-start.6 = (s32[112]{0:T(128)S(1)}, s32[112]{0:T(128)}, u32[]{:S(2)}) copy-start(s32[112]{0:T(128)} %shuffle.3) | copy-start | bytes 1348
  18.6 24.0 %copy-start = (bf16[14,128,256]{2,1,0:T(8,128)(2,1)S(1)}, bf16[14,128,256]{2,1,0:T(8,128)(2,1)}, u32[]{:S(2)}) copy-start(bf16[14,128,256]{2,1,0:T(8,128)(2,1)} %get-tuple-element.53.clean) | copy-start | bytes 2752516
  18.6 24.0 %copy-start.2 = (s32[2]{0:T(128)S(1)}, s32[2]{0:T(128)}, u32[]{:S(2)}) copy-start(s32[2]{0:T(128)} %pad_add_fusion.index) | copy-start | bytes 28
  21.3 4.3 %copy-start.3 = (bf16[2,2,128,256]{3,2,1,0:T(8,128)(2,1)S(1)}, bf16[2,2,128,256]{3,2,1,0:T(8,128)(2,1)}, u32[]{:S(2)}) copy-start(bf16[2,2,128,256]{3,2,1,0:T(8,128)(2,1)} %get-tuple-element.54) | copy-start | bytes 786436
  21.3 19.5 %all-to-all-start = ((bf16[16,128,256]{2,1,0:T(8,128)(2,1)}), bf16[16,128,256]{2,1,0:T(8,128)(2,1)S(1)}, u32[]{:S(2)}, u32[]{:S(2)}) async-start(bf16[16,128,256]{2,1,0:T(8,128)(2,1)} %patch.1), calls=%async_computation | async-start | bytes 2097152 | tf_op jit(solution)/shard_map/all_to_all | solution.py:42
  25.6 17.0 %collective-permute-start.6 = (bf16[2,128,256]{2,1,0:T(8,128)(2,1)S(1)}, bf16[2,128,256]{2,1,0:T(8,128)(2,1)S(1)}, u32[]{:S(2)}, u32[]{:S(2)}) collective-permute-start(bf16[2,128,256]{2,1,0:T(8,128)(2,1)S(1)} %get-tuple-element.93), channel_id=1, source_target_pairs={{4,8},{12,16},{20,24},{28,0},{8,4},{16,12},{24,20},{0,28},{5,9},{1... | collective-permute-start | bytes 393224 | tf_op jit(solution)/shard_map/ppermute | solution.py:33
  28.3 14.4 %collective-permute-start.5 = (bf16[2,128,256]{2,1,0:T(8,128)(2,1)S(1)}, bf16[2,128,256]{2,1,0:T(8,128)(2,1)S(1)}, u32[]{:S(2)}, u32[]{:S(2)}) collective-permute-start(bf16[2,128,256]{2,1,0:T(8,128)(2,1)S(1)} %get-tuple-element.94), channel_id=1, source_target_pairs={{0,4},{4,0},{8,12},{12,8},{16,20},{20,16},{24,28},{28,24},{1,5},{5... | collective-permute-start | bytes 393224 | tf_op jit(solution)/shard_map/ppermute | solution.py:38
  40.8 6.7 %copy-start.1 = (bf16[576,256]{1,0:T(8,128)(2,1)S(1)}, bf16[576,256]{1,0:T(8,128)(2,1)}, u32[]{:S(2)}) copy-start(bf16[576,256]{1,0:T(8,128)(2,1)} %get-tuple-element.48.refs_0_) | copy-start | bytes 884740
  43.8 10.4 %collective-permute-start.9 = (bf16[448,256]{1,0:T(8,128)(2,1)S(1)}, bf16[448,256]{1,0:T(8,128)(2,1)S(1)}, u32[]{:S(2)}, u32[]{:S(2)}) collective-permute-start(bf16[448,256]{1,0:T(8,128)(2,1)S(1)} %get-tuple-element.83), channel_id=1, source_target_pairs={{0,3},{1,2},{2,1},{3,0},{4,7},{5,6},{6,5},{7,4},{8,11},{9,10},{10,... | collective-permute-start | bytes 688136 | tf_op jit(solution)/shard_map/ppermute | solution.py:38
  47.6 20.0 %collective-permute-start.12 = (bf16[4,128,256]{2,1,0:T(8,128)(2,1)S(1)}, bf16[4,128,256]{2,1,0:T(8,128)(2,1)S(1)}, u32[]{:S(2)}, u32[]{:S(2)}) collective-permute-start(bf16[4,128,256]{2,1,0:T(8,128)(2,1)S(1)} %pad_maximum_fusion.1), channel_id=1, source_target_pairs={{0,24},{4,28},{8,16},{12,20},{16,8},{20,12},{24,0},{28,4},{1,25},{... | collective-permute-start | bytes 786440 | tf_op jit(solution)/shard_map/ppermute | solution.py:38
  48.2 19.3 %collective-permute-start.11 = (bf16[4,128,256]{2,1,0:T(8,128)(2,1)S(1)}, bf16[4,128,256]{2,1,0:T(8,128)(2,1)S(1)}, u32[]{:S(2)}, u32[]{:S(2)}) collective-permute-start(bf16[4,128,256]{2,1,0:T(8,128)(2,1)S(1)} %pad_maximum_fusion.1), channel_id=1, source_target_pairs={{0,16},{4,20},{8,24},{12,28},{16,0},{20,4},{24,8},{28,12},{1,17},{... | collective-permute-start | bytes 786440 | tf_op jit(solution)/shard_map/ppermute | solution.py:38
  48.8 18.7 %collective-permute-start.10 = (bf16[4,128,256]{2,1,0:T(8,128)(2,1)S(1)}, bf16[4,128,256]{2,1,0:T(8,128)(2,1)S(1)}, u32[]{:S(2)}, u32[]{:S(2)}) collective-permute-start(bf16[4,128,256]{2,1,0:T(8,128)(2,1)S(1)} %pad_maximum_fusion.1), channel_id=1, source_target_pairs={{0,8},{4,12},{8,0},{12,4},{16,24},{20,28},{24,16},{28,20},{1,9},{5... | collective-permute-start | bytes 786440 | tf_op jit(solution)/shard_map/ppermute | solution.py:38
  51.1 8.7 %collective-permute-start.8 = (bf16[448,256]{1,0:T(8,128)(2,1)S(1)}, bf16[448,256]{1,0:T(8,128)(2,1)S(1)}, u32[]{:S(2)}, u32[]{:S(2)}) collective-permute-start(bf16[448,256]{1,0:T(8,128)(2,1)S(1)} %get-tuple-element.84), channel_id=1, source_target_pairs={{0,1},{1,0},{2,3},{3,2},{4,5},{5,4},{6,7},{7,6},{8,9},{9,8},{10,11... | collective-permute-start | bytes 688136 | tf_op jit(solution)/shard_map/ppermute | solution.py:38
  54.2 13.4 %collective-permute-start.7 = (bf16[448,256]{1,0:T(8,128)(2,1)S(1)}, bf16[448,256]{1,0:T(8,128)(2,1)S(1)}, u32[]{:S(2)}, u32[]{:S(2)}) collective-permute-start(bf16[448,256]{1,0:T(8,128)(2,1)S(1)} %get-tuple-element.85), channel_id=1, source_target_pairs={{0,2},{1,3},{2,0},{3,1},{4,6},{5,7},{6,4},{7,5},{8,10},{9,11},{10,... | collective-permute-start | bytes 688136 | tf_op jit(solution)/shard_map/ppermute | solution.py:38
  67.7 2.7 %collective-permute-start.13 = (bf16[4,4,128,256]{3,2,1,0:T(8,128)(2,1)S(1)}, bf16[4,4,128,256]{3,2,1,0:T(8,128)(2,1)S(1)}, u32[]{:S(2)}, u32[]{:S(2)}) collective-permute-start(bf16[4,4,128,256]{3,2,1,0:T(8,128)(2,1)S(1)} %pad_maximum_fusion.refs_4_), channel_id=1, source_target_pairs={{0,4},{4,0},{8,12},{12,8},{16,20},{20,16},{24,28},{28,24},{1,5},{5... | collective-permute-start | bytes 3145736 | tf_op jit(solution)/shard_map/ppermute | solution.py:38
  70.4 2.9 %collective-permute-start.14 = (bf16[4,4,128,256]{3,2,1,0:T(8,128)(2,1)S(1)}, bf16[4,4,128,256]{3,2,1,0:T(8,128)(2,1)S(1)}, u32[]{:S(2)}, u32[]{:S(2)}) collective-permute-start(bf16[4,4,128,256]{3,2,1,0:T(8,128)(2,1)S(1)} %get-tuple-element.66), channel_id=1, source_target_pairs={{0,4},{4,0},{8,12},{12,8},{16,20},{20,16},{24,28},{28,24},{1,5},{5... | collective-permute-start | bytes 3145736 | tf_op jit(solution)/shard_map/ppermute | solution.py:38
  73.8 9.2 %collective-permute-start.15 = (bf16[4,128,256]{2,1,0:T(8,128)(2,1)S(1)}, bf16[4,128,256]{2,1,0:T(8,128)(2,1)S(1)}, u32[]{:S(2)}, u32[]{:S(2)}) collective-permute-start(bf16[4,128,256]{2,1,0:T(8,128)(2,1)S(1)} %get-tuple-element.80), channel_id=1, source_target_pairs={{0,8},{4,12},{8,0},{12,4},{16,24},{20,28},{24,16},{28,20},{1,9},{5... | collective-permute-start | bytes 786440 | tf_op jit(solution)/shard_map/ppermute | solution.py:38
  75.5 14.2 %collective-permute-start.17 = (bf16[4,128,256]{2,1,0:T(8,128)(2,1)S(1)}, bf16[4,128,256]{2,1,0:T(8,128)(2,1)S(1)}, u32[]{:S(2)}, u32[]{:S(2)}) collective-permute-start(bf16[4,128,256]{2,1,0:T(8,128)(2,1)S(1)} %get-tuple-element.81), channel_id=1, source_target_pairs={{0,24},{4,28},{8,16},{12,20},{16,8},{20,12},{24,0},{28,4},{1,25},{... | collective-permute-start | bytes 786440 | tf_op jit(solution)/shard_map/ppermute | solution.py:38
  77.5 13.6 %collective-permute-start.16 = (bf16[4,128,256]{2,1,0:T(8,128)(2,1)S(1)}, bf16[4,128,256]{2,1,0:T(8,128)(2,1)S(1)}, u32[]{:S(2)}, u32[]{:S(2)}) collective-permute-start(bf16[4,128,256]{2,1,0:T(8,128)(2,1)S(1)} %get-tuple-element.82), channel_id=1, source_target_pairs={{0,16},{4,20},{8,24},{12,28},{16,0},{20,4},{24,8},{28,12},{1,17},{... | collective-permute-start | bytes 786440 | tf_op jit(solution)/shard_map/ppermute | solution.py:38
  77.5 15.2 %collective-permute-start.23 = (bf16[448,256]{1,0:T(8,128)(2,1)S(1)}, bf16[448,256]{1,0:T(8,128)(2,1)S(1)}, u32[]{:S(2)}, u32[]{:S(2)}) collective-permute-start(bf16[448,256]{1,0:T(8,128)(2,1)S(1)} %get-tuple-element.87), channel_id=1, source_target_pairs={{0,3},{1,2},{2,1},{3,0},{4,7},{5,6},{6,5},{7,4},{8,11},{9,10},{10,... | collective-permute-start | bytes 688136 | tf_op jit(solution)/shard_map/ppermute | solution.py:38
  79.4 22.3 %collective-permute-start.22 = (bf16[448,256]{1,0:T(8,128)(2,1)S(1)}, bf16[448,256]{1,0:T(8,128)(2,1)S(1)}, u32[]{:S(2)}, u32[]{:S(2)}) collective-permute-start(bf16[448,256]{1,0:T(8,128)(2,1)S(1)} %get-tuple-element.88), channel_id=1, source_target_pairs={{0,2},{1,3},{2,0},{3,1},{4,6},{5,7},{6,4},{7,5},{8,10},{9,11},{10,... | collective-permute-start | bytes 688136 | tf_op jit(solution)/shard_map/ppermute | solution.py:38
  83.0 18.7 %collective-permute-start.21 = (bf16[448,256]{1,0:T(8,128)(2,1)S(1)}, bf16[448,256]{1,0:T(8,128)(2,1)S(1)}, u32[]{:S(2)}, u32[]{:S(2)}) collective-permute-start(bf16[448,256]{1,0:T(8,128)(2,1)S(1)} %get-tuple-element.89), channel_id=1, source_target_pairs={{0,1},{1,0},{2,3},{3,2},{4,5},{5,4},{6,7},{7,6},{8,9},{9,8},{10,11... | collective-permute-start | bytes 688136 | tf_op jit(solution)/shard_map/ppermute | solution.py:38
  91.2 12.0 %collective-permute-start.18 = (bf16[128,256]{1,0:T(8,128)(2,1)S(1)}, bf16[128,256]{1,0:T(8,128)(2,1)S(1)}, u32[]{:S(2)}, u32[]{:S(2)}) collective-permute-start(bf16[128,256]{1,0:T(8,128)(2,1)S(1)} %get-tuple-element.90), channel_id=1, source_target_pairs={{0,1},{1,0},{2,3},{3,2},{4,5},{5,4},{6,7},{7,6},{8,9},{9,8},{10,11... | collective-permute-start | bytes 196616 | tf_op jit(solution)/shard_map/ppermute | solution.py:38
  91.3 11.9 %collective-permute-start.20 = (bf16[128,256]{1,0:T(8,128)(2,1)S(1)}, bf16[128,256]{1,0:T(8,128)(2,1)S(1)}, u32[]{:S(2)}, u32[]{:S(2)}) collective-permute-start(bf16[128,256]{1,0:T(8,128)(2,1)S(1)} %get-tuple-element.91), channel_id=1, source_target_pairs={{0,3},{1,2},{2,1},{3,0},{4,7},{5,6},{6,5},{7,4},{8,11},{9,10},{10,... | collective-permute-start | bytes 196616 | tf_op jit(solution)/shard_map/ppermute | solution.py:38
  92.8 10.7 %collective-permute-start.19 = (bf16[128,256]{1,0:T(8,128)(2,1)S(1)}, bf16[128,256]{1,0:T(8,128)(2,1)S(1)}, u32[]{:S(2)}, u32[]{:S(2)}) collective-permute-start(bf16[128,256]{1,0:T(8,128)(2,1)S(1)} %get-tuple-element.92), channel_id=1, source_target_pairs={{0,2},{1,3},{2,0},{3,1},{4,6},{5,7},{6,4},{7,5},{8,10},{9,11},{10,... | collective-permute-start | bytes 196616 | tf_op jit(solution)/shard_map/ppermute | solution.py:38

commit v18 on v17

--- a/solution.py
+++ b/solution.py
@@ -29,7 +29,7 @@
 
 def swapped_beside(value, axis):
     size = lax.axis_size(axis)
-    pairs = [(i, (i + 1) % size) for i in range(1, size, 2)]
+    pairs = [(i, i + 1) for i in range(1, size - 1, 2)]
     return lax.ppermute(value, axis, pairs + [(j, i) for i, j in pairs])
 
 

time: 104 us -> 106 us (1.019)
  starting transfers between devices: 36.1 us -> 43.5 us
  waiting for transfers between devices: 43.2 us -> 37.5 us
    ppermute x22, starting transfers between devices: 26.3 us -> 38.5 us  [swapped(): return lax.ppermute(value, axis, [(i, i ^ by) for i in range(size)])]
    ppermute x2, starting transfers between devices: 6.05 us -> 1.34 us  [swapped_beside(): return lax.ppermute(value, axis, pairs + [(j, i) for i, j in pairs])]
    ppermute x22, waiting for transfers between devices: 38.7 us -> 35.4 us  [swapped(): return lax.ppermute(value, axis, [(i, i ^ by) for i in range(size)])]
    ppermute x2, waiting for transfers between devices: 1.86 us -> 0.01 us  [swapped_beside(): return lax.ppermute(value, axis, pairs + [(j, i) for i, j in pairs])]
  transfers between devices with their start and end apart: 25 -> 25, of which waited for: 11 -> 8; matrix products, arithmetic and copies ran while one was open for 2% -> 2% of each run, Pallas kernels for 10% -> 10%
where the time goes in v18:
time: 106 us
  starting transfers between devices  43.5 us (41%)
  waiting for transfers between devices  37.5 us (35%)
  Pallas kernels  19.1 us (18%)
  other arithmetic  2.5 us (2%)
  local copies, waits for them, and re-layouts  2.3 us (2%)
    ppermute x22, starting transfers between devices, swapped(): return lax.ppermute(value, axis, [(i, i ^ by) for i in range(size)])  38.5 us
    ppermute x22, waiting for transfers between devices, swapped(): return lax.ppermute(value, axis, [(i, i ^ by) for i in range(size)])  35.4 us
    pallas_call x1, Pallas kernels, aggregate(): pl.pallas_call(functools.partial(aggregate_kernel, reach, groups, send_sl...  7.91 us
    all_to_all x1, starting transfers between devices, exchanged(): return lax.all_to_all(value, axis, split_axis=0, concat_axis=0, tiled=True)  3.7 us
    pallas_call x2, Pallas kernels, feature_rows(): pl.pallas_call(functools.partial(feature_kernel, first), in_specs=[IN_SME...  3.33 us
    pallas_call x1, Pallas kernels, weight_partial(): pl.pallas_call(functools.partial(weight_kernel, devs), in_specs=[IN_SMEM]...  2.65 us
    pallas_call x1, Pallas kernels, patch(): pl.pallas_call(functools.partial(patch_kernel, reach, blocks, slots), in_...  2.62 us
    all_to_all x1, waiting for transfers between devices, exchanged(): return lax.all_to_all(value, axis, split_axis=0, concat_axis=0, tiled=True)  2.15 us
  transfers between devices with their start and end apart: 25, of which 8 were waited for; matrix products, arithmetic and copies ran while one was open for 2% of the time, Pallas kernels for 10%

profile of v18, /device:TPU:0, one launch (start us, length us, event | category | flops | bytes accessed | tf_op | source)
XLA Modules:
  0.0 105.9 jit_solution(16006956167633517112)
XLA Ops:
  0.6 7.9 %aggregate.1 = (bf16[14,128,256]{2,1,0:T(8,128)(2,1)}, bf16[16,128,256]{2,1,0:T(8,128)(2,1)}, bf16[2,2,128,256]{3,2,1,0:T(8,128)(2,1)}, bf16[2,2,128,256]{3,2,1,...) custom-call(s32[112]{0:T(128)} %shuffle.3, ...), custom_call_target="tpu_custom_call" | custom-call | flops 1174405120 | bytes 7798784 | tf_op jit(solution)/shard_map/aggregate/pallas_call | solution.py:186
  8.5 1.0 slice_bitcast_fusion.14
  9.5 0.7 collective-permute-start.1
  10.2 4.4 %collective-permute-start = (bf16[2,128,256]{2,1,0:T(8,128)(2,1)S(1)}, bf16[2,128,256]{2,1,0:T(8,128)(2,1)S(1)}, u32[]{:S(2)}, u32[]{:S(2)}) collective-permute-start(bf16[2,128,256]{2,1,0:T(8,128)(2,1)S(1)} %get-tuple-element.96), channel_id=1, source_target_pairs={{0,4},{4,0},{8,12},{12,8},{16,20},{20,16},{24,28},{28,24},{1,5},{5... | collective-permute-start | bytes 393224 | tf_op jit(solution)/shard_map/ppermute | solution.py:38
  14.6 1.6 %collective-permute-start.2 = (bf16[576,256]{1,0:T(8,128)(2,1)}, bf16[576,256]{1,0:T(8,128)(2,1)S(1)}, u32[]{:S(2)}, u32[]{:S(2)}) collective-permute-start(bf16[576,256]{1,0:T(8,128)(2,1)} %get-tuple-element.45), channel_id=1, source_target_pairs={{0,1},{1,0},{2,3},{3,2},{4,5},{5,4},{6,7},{7,6},{8,9},{9,8},{10,11... | collective-permute-start | bytes 884744 | tf_op jit(solution)/shard_map/ppermute | solution.py:38
  16.1 2.6 %collective-permute-start.3 = (bf16[576,256]{1,0:T(8,128)(2,1)}, bf16[576,256]{1,0:T(8,128)(2,1)S(1)}, u32[]{:S(2)}, u32[]{:S(2)}) collective-permute-start(bf16[576,256]{1,0:T(8,128)(2,1)} %get-tuple-element.46), channel_id=1, source_target_pairs={{0,2},{1,3},{2,0},{3,1},{4,6},{5,7},{6,4},{7,5},{8,10},{9,11},{10,... | collective-permute-start | bytes 884744 | tf_op jit(solution)/shard_map/ppermute | solution.py:38
  18.7 0.2 collective-permute-start.4
  19.0 0.6 pad_add_fusion.index
  19.6 0.0 collective-permute-done.1.beside
  19.6 0.0 copy-start.5
  19.6 0.6 copy-done.4
  20.2 0.1 copy-done.5
  20.3 2.6 %patch.1 = bf16[16,128,256]{2,1,0:T(8,128)(2,1)} custom-call(s32[2]{0:T(128)} %pad_add_fusion.index, s32[112]{0:T(128)} %shuffle.3, bf16[16,128,256]{2,1,0:T(8,128)(2,1)} %get-tuple-element.39.outgoing, bf16[2,128,256]{2,1,0:T(8,128)(2,1)} %copy-done.5, bf16[2,128,256]{2,1,0:T(8,128)(2,1)} %copy-done.4), custom_call_target="tpu_custom_call", output_to_operand_aliasing={{}: (2, {})} | custom-call | tf_op jit(solution)/shard_map/patch/pallas_call | solution.py:249
  22.9 3.7 %all-to-all-start = ((bf16[16,128,256]{2,1,0:T(8,128)(2,1)}), bf16[16,128,256]{2,1,0:T(8,128)(2,1)S(1)}, u32[]{:S(2)}, u32[]{:S(2)}) async-start(bf16[16,128,256]{2,1,0:T(8,128)(2,1)} %patch.1), calls=%async_computation | async-start | bytes 2097152 | tf_op jit(solution)/shard_map/all_to_all | solution.py:42
  26.6 0.1 eq.30
  26.7 0.1 add.45
  26.8 0.3 convert_reduce_fusion
  27.2 0.1 copy.14
  27.3 0.7 collective-permute-start.6
  27.9 3.3 %collective-permute-start.5 = (bf16[2,128,256]{2,1,0:T(8,128)(2,1)S(1)}, bf16[2,128,256]{2,1,0:T(8,128)(2,1)S(1)}, u32[]{:S(2)}, u32[]{:S(2)}) collective-permute-start(bf16[2,128,256]{2,1,0:T(8,128)(2,1)S(1)} %get-tuple-element.94), channel_id=1, source_target_pairs={{0,4},{4,0},{8,12},{12,8},{16,20},{20,16},{24,28},{28,24},{1,5},{5... | collective-permute-start | bytes 393224 | tf_op jit(solution)/shard_map/ppermute | solution.py:38
  31.3 0.1 select_reduce_fusion
  31.4 0.1 copy.15
  31.5 0.1 sub.13.landing
  31.6 0.0 collective-permute-done.2.refs_1_
  31.6 8.2 %collective-permute-done.3.refs_2_ = bf16[576,256]{1,0:T(8,128)(2,1)S(1)} collective-permute-done((bf16[576,256]{1,0:T(8,128)(2,1)}, bf16[576,256]{1,0:T(8,128)(2,1)S(1)}, u32[]{:S(2)}, u32[]{:S(2)}) %collective-permute-start.3) | collective-permute-done | bytes 294944 | tf_op jit(solution)/shard_map/ppermute | solution.py:38
  39.8 0.0 collective-permute-done.4.refs_3_
  39.8 2.1 %all-to-all-done.incoming = bf16[16,128,256]{2,1,0:T(8,128)(2,1)S(1)} async-done(((bf16[16,128,256]{2,1,0:T(8,128)(2,1)}), bf16[16,128,256]{2,1,0:T(8,128)(2,1)S(1)}, u32[]{:S(2)}, u32[]{:S(2)}) %all-to-all-start) | async-done | bytes 1048608 | tf_op jit(solution)/shard_map/all_to_all | solution.py:42
  42.0 1.1 %merge.1 = bf16[4,448,256]{2,1,0:T(8,128)(2,1)S(1)} custom-call(s32[2]{0:T(128)S(1)} %copy-done.2, s32[16]{0:T(128)S(1)} %sub.13.landing, bf16[14,128,256]{2,1,0:T(8,128)(2,1)S(1)} %copy-done, bf16[2,128,256]{2,1,0:T(8,128)(2,1)S(1)} %collective-permute-done.5.pair, bf16[2,128,256]{2,1,0:T(8,128)(2,1)S(1)} %collective-permute-done.6.beside, ...), custom_call_target="tpu_custom_call" | custom-call | tf_op jit(solution)/shard_map/merge/pallas_call | solution.py:297
  43.1 0.1 slice_bitcast_fusion.4
  43.1 3.7 %collective-permute-start.9 = (bf16[448,256]{1,0:T(8,128)(2,1)S(1)}, bf16[448,256]{1,0:T(8,128)(2,1)S(1)}, u32[]{:S(2)}, u32[]{:S(2)}) collective-permute-start(bf16[448,256]{1,0:T(8,128)(2,1)S(1)} %get-tuple-element.83), channel_id=1, source_target_pairs={{0,3},{1,2},{2,1},{3,0},{4,7},{5,6},{6,5},{7,4},{8,11},{9,10},{10,... | collective-permute-start | bytes 688136 | tf_op jit(solution)/shard_map/ppermute | solution.py:38
  46.9 3.0 %collective-permute-start.12 = (bf16[4,128,256]{2,1,0:T(8,128)(2,1)S(1)}, bf16[4,128,256]{2,1,0:T(8,128)(2,1)S(1)}, u32[]{:S(2)}, u32[]{:S(2)}) collective-permute-start(bf16[4,128,256]{2,1,0:T(8,128)(2,1)S(1)} %pad_maximum_fusion.1), channel_id=1, source_target_pairs={{0,24},{4,28},{8,16},{12,20},{16,8},{20,12},{24,0},{28,4},{1,25},{... | collective-permute-start | bytes 786440 | tf_op jit(solution)/shard_map/ppermute | solution.py:38
  49.8 0.0 collective-permute-start.11
  49.9 1.4 %collective-permute-start.10 = (bf16[4,128,256]{2,1,0:T(8,128)(2,1)S(1)}, bf16[4,128,256]{2,1,0:T(8,128)(2,1)S(1)}, u32[]{:S(2)}, u32[]{:S(2)}) collective-permute-start(bf16[4,128,256]{2,1,0:T(8,128)(2,1)S(1)} %pad_maximum_fusion.1), channel_id=1, source_target_pairs={{0,8},{4,12},{8,0},{12,4},{16,24},{20,28},{24,16},{28,20},{1,9},{5... | collective-permute-start | bytes 786440 | tf_op jit(solution)/shard_map/ppermute | solution.py:38
  51.3 0.7 collective-permute-start.8
  52.0 0.8 collective-permute-done.9.refs_7_.refs_3_
  52.8 6.7 %collective-permute-start.7 = (bf16[448,256]{1,0:T(8,128)(2,1)S(1)}, bf16[448,256]{1,0:T(8,128)(2,1)S(1)}, u32[]{:S(2)}, u32[]{:S(2)}) collective-permute-start(bf16[448,256]{1,0:T(8,128)(2,1)S(1)} %get-tuple-element.85), channel_id=1, source_target_pairs={{0,2},{1,3},{2,0},{3,1},{4,6},{5,7},{6,4},{7,5},{8,10},{9,11},{10,... | collective-permute-start | bytes 688136 | tf_op jit(solution)/shard_map/ppermute | solution.py:38
  59.5 0.0 collective-permute-done.8.refs_5_.refs_1_
  59.5 9.1 %collective-permute-done.7.refs_6_.refs_2_ = bf16[448,256]{1,0:T(8,128)(2,1)S(1)} collective-permute-done((bf16[448,256]{1,0:T(8,128)(2,1)S(1)}, bf16[448,256]{1,0:T(8,128)(2,1)S(1)}, u32[]{:S(2)}, u32[]{:S(2)}) %collective-permute-start.7) | collective-permute-done | bytes 229408 | tf_op jit(solution)/shard_map/ppermute | solution.py:38
  68.6 0.0 collective-permute-done.12
  68.6 0.0 collective-permute-done.11
  68.6 0.0 collective-permute-done.10
  68.6 0.1 pad_maximum_fusion.refs_4_
  68.7 0.1 collective-permute-start.13
  68.8 2.7 %weight_partial.1 = (bf16[4,4,128,256]{3,2,1,0:T(8,128)(2,1)S(1)}, bf16[4,4,128,256]{3,2,1,0:T(8,128)(2,1)S(1)}) custom-call(s32[2]{0:T(128)S(1)} %copy-done.2, bf16[576,256]{1,0:T(8,128)(2,1)S(1)} %copy-done.1, bf16[576,256]{1,0:T(8,128)(2,1)S(1)} %collective-permute-done.2.refs_1_, bf16[576,256]{1,0:T(8,128)(2,1)S(1)} %collective-permute-done.3.refs_2_, ...), custom_call_target="tpu_custom_call" | custom-call | flops 939524096 | bytes 3932160 | tf_op jit(solution)/shard_map/weight_partial/pallas_call | solution.py:338
  71.5 0.0 collective-permute-done.13.refs_5_
  71.5 0.5 collective-permute-start.14
  72.0 2.3 %feature_rows.2 = bf16[3,448,256]{2,1,0:T(8,128)(2,1)S(1)} custom-call(s32[2]{0:T(128)S(1)} %copy-done.2, bf16[448,256]{1,0:T(8,128)(2,1)S(1)} %get-tuple-element.69.refs_4_.refs_0_, bf16[448,256]{1,0:T(8,128)(2,1)S(1)} %collective-permute-done.8.refs_5_.refs_1_, bf16[448,256]{1,0:T(8,128)(2,1)S(1)} %collective-permute-done.7.refs_6_.refs_2_, ...), custom_call_target="tpu_custom_call" | custom-call | flops 704643072 | bytes 3178496 | tf_op jit(solution)/shard_map/feature_rows/pallas_call | solution.py:386
  74.4 0.4 convert_add_fusion
  74.8 0.1 slice_bitcast_fusion.3
  74.9 1.1 %collective-permute-start.15 = (bf16[4,128,256]{2,1,0:T(8,128)(2,1)S(1)}, bf16[4,128,256]{2,1,0:T(8,128)(2,1)S(1)}, u32[]{:S(2)}, u32[]{:S(2)}) collective-permute-start(bf16[4,128,256]{2,1,0:T(8,128)(2,1)S(1)} %get-tuple-element.80), channel_id=1, source_target_pairs={{0,8},{4,12},{8,0},{12,4},{16,24},{20,28},{24,16},{28,20},{1,9},{5... | collective-permute-start | bytes 786440 | tf_op jit(solution)/shard_map/ppermute | solution.py:38
  76.0 1.7 %collective-permute-start.17 = (bf16[4,128,256]{2,1,0:T(8,128)(2,1)S(1)}, bf16[4,128,256]{2,1,0:T(8,128)(2,1)S(1)}, u32[]{:S(2)}, u32[]{:S(2)}) collective-permute-start(bf16[4,128,256]{2,1,0:T(8,128)(2,1)S(1)} %get-tuple-element.81), channel_id=1, source_target_pairs={{0,24},{4,28},{8,16},{12,20},{16,8},{20,12},{24,0},{28,4},{1,25},{... | collective-permute-start | bytes 786440 | tf_op jit(solution)/shard_map/ppermute | solution.py:38
  77.6 0.8 collective-permute-start.16
  78.5 2.6 %collective-permute-start.23 = (bf16[448,256]{1,0:T(8,128)(2,1)S(1)}, bf16[448,256]{1,0:T(8,128)(2,1)S(1)}, u32[]{:S(2)}, u32[]{:S(2)}) collective-permute-start(bf16[448,256]{1,0:T(8,128)(2,1)S(1)} %get-tuple-element.87), channel_id=1, source_target_pairs={{0,3},{1,2},{2,1},{3,0},{4,7},{5,6},{6,5},{7,4},{8,11},{9,10},{10,... | collective-permute-start | bytes 688136 | tf_op jit(solution)/shard_map/ppermute | solution.py:38
  81.0 3.0 %collective-permute-done.15 = bf16[4,128,256]{2,1,0:T(8,128)(2,1)S(1)} collective-permute-done((bf16[4,128,256]{2,1,0:T(8,128)(2,1)S(1)}, bf16[4,128,256]{2,1,0:T(8,128)(2,1)S(1)}, u32[]{:S(2)}, u32[]{:S(2)}) %collective-permute-start.15) | collective-permute-done | bytes 262176 | tf_op jit(solution)/shard_map/ppermute | solution.py:38
  84.0 5.9 %collective-permute-done.17 = bf16[4,128,256]{2,1,0:T(8,128)(2,1)S(1)} collective-permute-done((bf16[4,128,256]{2,1,0:T(8,128)(2,1)S(1)}, bf16[4,128,256]{2,1,0:T(8,128)(2,1)S(1)}, u32[]{:S(2)}, u32[]{:S(2)}) %collective-permute-start.17) | collective-permute-done | bytes 262176 | tf_op jit(solution)/shard_map/ppermute | solution.py:38
  90.0 1.4 %collective-permute-done.16 = bf16[4,128,256]{2,1,0:T(8,128)(2,1)S(1)} collective-permute-done((bf16[4,128,256]{2,1,0:T(8,128)(2,1)S(1)}, bf16[4,128,256]{2,1,0:T(8,128)(2,1)S(1)}, u32[]{:S(2)}, u32[]{:S(2)}) %collective-permute-start.16) | collective-permute-done | bytes 262176 | tf_op jit(solution)/shard_map/ppermute | solution.py:38
  91.4 0.2 fusion.10
  91.6 0.1 collective-permute-start.18
  91.7 2.3 %collective-permute-start.20 = (bf16[128,256]{1,0:T(8,128)(2,1)S(1)}, bf16[128,256]{1,0:T(8,128)(2,1)S(1)}, u32[]{:S(2)}, u32[]{:S(2)}) collective-permute-start(bf16[128,256]{1,0:T(8,128)(2,1)S(1)} %get-tuple-element.91), channel_id=1, source_target_pairs={{0,3},{1,2},{2,1},{3,0},{4,7},{5,6},{6,5},{7,4},{8,11},{9,10},{10,... | collective-permute-start | bytes 196616 | tf_op jit(solution)/shard_map/ppermute | solution.py:38
  94.0 1.7 %collective-permute-start.19 = (bf16[128,256]{1,0:T(8,128)(2,1)S(1)}, bf16[128,256]{1,0:T(8,128)(2,1)S(1)}, u32[]{:S(2)}, u32[]{:S(2)}) collective-permute-start(bf16[128,256]{1,0:T(8,128)(2,1)S(1)} %get-tuple-element.92), channel_id=1, source_target_pairs={{0,2},{1,3},{2,0},{3,1},{4,6},{5,7},{6,4},{7,5},{8,10},{9,11},{10,... | collective-permute-start | bytes 196616 | tf_op jit(solution)/shard_map/ppermute | solution.py:38
  95.7 1.0 feature_rows.3
  96.7 6.9 %collective-permute-done.22.refs_2_ = bf16[448,256]{1,0:T(8,128)(2,1)S(1)} collective-permute-done((bf16[448,256]{1,0:T(8,128)(2,1)S(1)}, bf16[448,256]{1,0:T(8,128)(2,1)S(1)}, u32[]{:S(2)}, u32[]{:S(2)}) %collective-permute-start.22) | collective-permute-done | bytes 229408 | tf_op jit(solution)/shard_map/ppermute | solution.py:38
  103.6 1.5 %laid_out.1 = bf16[1792,256]{1,0:T(8,128)(2,1)} custom-call(s32[2]{0:T(128)S(1)} %copy-done.2, bf16[448,256]{1,0:T(8,128)(2,1)S(1)} %bitcast.68, bf16[448,256]{1,0:T(8,128)(2,1)S(1)} %collective-permute-done.21.refs_1_, bf16[448,256]{1,0:T(8,128)(2,1)S(1)} %collective-permute-done.22.refs_2_, bf16[448,256]{1,0:T(8,128)(2,1)S(1)} %collective-permute-done.23.refs_3_), custom_call_target="tpu_custom_call" | custom-call | tf_op jit(solution)/shard_map/laid_out/pallas_call | solution.py:418
  105.2 0.7 fusion.5
  (32 shorter events, 0.2 us)
Async XLA Ops:
  9.5 10.0 %collective-permute-start.1 = (bf16[2,128,256]{2,1,0:T(8,128)(2,1)S(1)}, bf16[2,128,256]{2,1,0:T(8,128)(2,1)S(1)}, u32[]{:S(2)}, u32[]{:S(2)}) collective-permute-start(bf16[2,128,256]{2,1,0:T(8,128)(2,1)S(1)} %get-tuple-element.95), channel_id=1, source_target_pairs={{4,8},{12,16},{20,24},{8,4},{16,12},{24,20},{5,9},{13,17},{21,25},... | collective-permute-start | bytes 393224 | tf_op jit(solution)/shard_map/ppermute | solution.py:33
  10.2 9.4 %collective-permute-start = (bf16[2,128,256]{2,1,0:T(8,128)(2,1)S(1)}, bf16[2,128,256]{2,1,0:T(8,128)(2,1)S(1)}, u32[]{:S(2)}, u32[]{:S(2)}) collective-permute-start(bf16[2,128,256]{2,1,0:T(8,128)(2,1)S(1)} %get-tuple-element.96), channel_id=1, source_target_pairs={{0,4},{4,0},{8,12},{12,8},{16,20},{20,16},{24,28},{28,24},{1,5},{5... | collective-permute-start | bytes 393224 | tf_op jit(solution)/shard_map/ppermute | solution.py:38
  14.6 17.0 %collective-permute-start.2 = (bf16[576,256]{1,0:T(8,128)(2,1)}, bf16[576,256]{1,0:T(8,128)(2,1)S(1)}, u32[]{:S(2)}, u32[]{:S(2)}) collective-permute-start(bf16[576,256]{1,0:T(8,128)(2,1)} %get-tuple-element.45), channel_id=1, source_target_pairs={{0,1},{1,0},{2,3},{3,2},{4,5},{5,4},{6,7},{7,6},{8,9},{9,8},{10,11... | collective-permute-start | bytes 884744 | tf_op jit(solution)/shard_map/ppermute | solution.py:38
  16.1 23.7 %collective-permute-start.3 = (bf16[576,256]{1,0:T(8,128)(2,1)}, bf16[576,256]{1,0:T(8,128)(2,1)S(1)}, u32[]{:S(2)}, u32[]{:S(2)}) collective-permute-start(bf16[576,256]{1,0:T(8,128)(2,1)} %get-tuple-element.46), channel_id=1, source_target_pairs={{0,2},{1,3},{2,0},{3,1},{4,6},{5,7},{6,4},{7,5},{8,10},{9,11},{10,... | collective-permute-start | bytes 884744 | tf_op jit(solution)/shard_map/ppermute | solution.py:38
  18.7 21.1 %collective-permute-start.4 = (bf16[576,256]{1,0:T(8,128)(2,1)}, bf16[576,256]{1,0:T(8,128)(2,1)S(1)}, u32[]{:S(2)}, u32[]{:S(2)}) collective-permute-start(bf16[576,256]{1,0:T(8,128)(2,1)} %get-tuple-element.47), channel_id=1, source_target_pairs={{0,3},{1,2},{2,1},{3,0},{4,7},{5,6},{6,5},{7,4},{8,11},{9,10},{10,... | collective-permute-start | bytes 884744 | tf_op jit(solution)/shard_map/ppermute | solution.py:38
  19.6 0.6 copy-start.4
  19.6 0.7 copy-start.5
  20.3 6.4 %copy-start.6 = (s32[112]{0:T(128)S(1)}, s32[112]{0:T(128)}, u32[]{:S(2)}) copy-start(s32[112]{0:T(128)} %shuffle.3) | copy-start | bytes 1348
  20.3 21.7 %copy-start = (bf16[14,128,256]{2,1,0:T(8,128)(2,1)S(1)}, bf16[14,128,256]{2,1,0:T(8,128)(2,1)}, u32[]{:S(2)}) copy-start(bf16[14,128,256]{2,1,0:T(8,128)(2,1)} %get-tuple-element.53.clean) | copy-start | bytes 2752516
  20.3 21.7 %copy-start.2 = (s32[2]{0:T(128)S(1)}, s32[2]{0:T(128)}, u32[]{:S(2)}) copy-start(s32[2]{0:T(128)} %pad_add_fusion.index) | copy-start | bytes 28
  22.9 4.3 %copy-start.3 = (bf16[2,2,128,256]{3,2,1,0:T(8,128)(2,1)S(1)}, bf16[2,2,128,256]{3,2,1,0:T(8,128)(2,1)}, u32[]{:S(2)}) copy-start(bf16[2,2,128,256]{3,2,1,0:T(8,128)(2,1)} %get-tuple-element.54) | copy-start | bytes 786436
  22.9 19.0 %all-to-all-start = ((bf16[16,128,256]{2,1,0:T(8,128)(2,1)}), bf16[16,128,256]{2,1,0:T(8,128)(2,1)S(1)}, u32[]{:S(2)}, u32[]{:S(2)}) async-start(bf16[16,128,256]{2,1,0:T(8,128)(2,1)} %patch.1), calls=%async_computation | async-start | bytes 2097152 | tf_op jit(solution)/shard_map/all_to_all | solution.py:42
  27.3 14.7 %collective-permute-start.6 = (bf16[2,128,256]{2,1,0:T(8,128)(2,1)S(1)}, bf16[2,128,256]{2,1,0:T(8,128)(2,1)S(1)}, u32[]{:S(2)}, u32[]{:S(2)}) collective-permute-start(bf16[2,128,256]{2,1,0:T(8,128)(2,1)S(1)} %get-tuple-element.93), channel_id=1, source_target_pairs={{4,8},{12,16},{20,24},{8,4},{16,12},{24,20},{5,9},{13,17},{21,25},... | collective-permute-start | bytes 393224 | tf_op jit(solution)/shard_map/ppermute | solution.py:33
  27.9 14.0 %collective-permute-start.5 = (bf16[2,128,256]{2,1,0:T(8,128)(2,1)S(1)}, bf16[2,128,256]{2,1,0:T(8,128)(2,1)S(1)}, u32[]{:S(2)}, u32[]{:S(2)}) collective-permute-start(bf16[2,128,256]{2,1,0:T(8,128)(2,1)S(1)} %get-tuple-element.94), channel_id=1, source_target_pairs={{0,4},{4,0},{8,12},{12,8},{16,20},{20,16},{24,28},{28,24},{1,5},{5... | collective-permute-start | bytes 393224 | tf_op jit(solution)/shard_map/ppermute | solution.py:38
  41.9 4.9 %copy-start.1 = (bf16[576,256]{1,0:T(8,128)(2,1)S(1)}, bf16[576,256]{1,0:T(8,128)(2,1)}, u32[]{:S(2)}) copy-start(bf16[576,256]{1,0:T(8,128)(2,1)} %get-tuple-element.48.refs_0_) | copy-start | bytes 884740
  43.1 9.7 %collective-permute-start.9 = (bf16[448,256]{1,0:T(8,128)(2,1)S(1)}, bf16[448,256]{1,0:T(8,128)(2,1)S(1)}, u32[]{:S(2)}, u32[]{:S(2)}) collective-permute-start(bf16[448,256]{1,0:T(8,128)(2,1)S(1)} %get-tuple-element.83), channel_id=1, source_target_pairs={{0,3},{1,2},{2,1},{3,0},{4,7},{5,6},{6,5},{7,4},{8,11},{9,10},{10,... | collective-permute-start | bytes 688136 | tf_op jit(solution)/shard_map/ppermute | solution.py:38
  46.9 21.7 %collective-permute-start.12 = (bf16[4,128,256]{2,1,0:T(8,128)(2,1)S(1)}, bf16[4,128,256]{2,1,0:T(8,128)(2,1)S(1)}, u32[]{:S(2)}, u32[]{:S(2)}) collective-permute-start(bf16[4,128,256]{2,1,0:T(8,128)(2,1)S(1)} %pad_maximum_fusion.1), channel_id=1, source_target_pairs={{0,24},{4,28},{8,16},{12,20},{16,8},{20,12},{24,0},{28,4},{1,25},{... | collective-permute-start | bytes 786440 | tf_op jit(solution)/shard_map/ppermute | solution.py:38
  49.8 18.7 %collective-permute-start.11 = (bf16[4,128,256]{2,1,0:T(8,128)(2,1)S(1)}, bf16[4,128,256]{2,1,0:T(8,128)(2,1)S(1)}, u32[]{:S(2)}, u32[]{:S(2)}) collective-permute-start(bf16[4,128,256]{2,1,0:T(8,128)(2,1)S(1)} %pad_maximum_fusion.1), channel_id=1, source_target_pairs={{0,16},{4,20},{8,24},{12,28},{16,0},{20,4},{24,8},{28,12},{1,17},{... | collective-permute-start | bytes 786440 | tf_op jit(solution)/shard_map/ppermute | solution.py:38
  49.9 18.7 %collective-permute-start.10 = (bf16[4,128,256]{2,1,0:T(8,128)(2,1)S(1)}, bf16[4,128,256]{2,1,0:T(8,128)(2,1)S(1)}, u32[]{:S(2)}, u32[]{:S(2)}) collective-permute-start(bf16[4,128,256]{2,1,0:T(8,128)(2,1)S(1)} %pad_maximum_fusion.1), channel_id=1, source_target_pairs={{0,8},{4,12},{8,0},{12,4},{16,24},{20,28},{24,16},{28,20},{1,9},{5... | collective-permute-start | bytes 786440 | tf_op jit(solution)/shard_map/ppermute | solution.py:38
  51.3 8.3 %collective-permute-start.8 = (bf16[448,256]{1,0:T(8,128)(2,1)S(1)}, bf16[448,256]{1,0:T(8,128)(2,1)S(1)}, u32[]{:S(2)}, u32[]{:S(2)}) collective-permute-start(bf16[448,256]{1,0:T(8,128)(2,1)S(1)} %get-tuple-element.84), channel_id=1, source_target_pairs={{0,1},{1,0},{2,3},{3,2},{4,5},{5,4},{6,7},{7,6},{8,9},{9,8},{10,11... | collective-permute-start | bytes 688136 | tf_op jit(solution)/shard_map/ppermute | solution.py:38
  52.8 15.8 %collective-permute-start.7 = (bf16[448,256]{1,0:T(8,128)(2,1)S(1)}, bf16[448,256]{1,0:T(8,128)(2,1)S(1)}, u32[]{:S(2)}, u32[]{:S(2)}) collective-permute-start(bf16[448,256]{1,0:T(8,128)(2,1)S(1)} %get-tuple-element.85), channel_id=1, source_target_pairs={{0,2},{1,3},{2,0},{3,1},{4,6},{5,7},{6,4},{7,5},{8,10},{9,11},{10,... | collective-permute-start | bytes 688136 | tf_op jit(solution)/shard_map/ppermute | solution.py:38
  68.7 2.7 %collective-permute-start.13 = (bf16[4,4,128,256]{3,2,1,0:T(8,128)(2,1)S(1)}, bf16[4,4,128,256]{3,2,1,0:T(8,128)(2,1)S(1)}, u32[]{:S(2)}, u32[]{:S(2)}) collective-permute-start(bf16[4,4,128,256]{3,2,1,0:T(8,128)(2,1)S(1)} %pad_maximum_fusion.refs_4_), channel_id=1, source_target_pairs={{0,4},{4,0},{8,12},{12,8},{16,20},{20,16},{24,28},{28,24},{1,5},{5... | collective-permute-start | bytes 3145736 | tf_op jit(solution)/shard_map/ppermute | solution.py:38
  71.5 2.9 %collective-permute-start.14 = (bf16[4,4,128,256]{3,2,1,0:T(8,128)(2,1)S(1)}, bf16[4,4,128,256]{3,2,1,0:T(8,128)(2,1)S(1)}, u32[]{:S(2)}, u32[]{:S(2)}) collective-permute-start(bf16[4,4,128,256]{3,2,1,0:T(8,128)(2,1)S(1)} %get-tuple-element.66), channel_id=1, source_target_pairs={{0,4},{4,0},{8,12},{12,8},{16,20},{20,16},{24,28},{28,24},{1,5},{5... | collective-permute-start | bytes 3145736 | tf_op jit(solution)/shard_map/ppermute | solution.py:38
  74.9 9.2 %collective-permute-start.15 = (bf16[4,128,256]{2,1,0:T(8,128)(2,1)S(1)}, bf16[4,128,256]{2,1,0:T(8,128)(2,1)S(1)}, u32[]{:S(2)}, u32[]{:S(2)}) collective-permute-start(bf16[4,128,256]{2,1,0:T(8,128)(2,1)S(1)} %get-tuple-element.80), channel_id=1, source_target_pairs={{0,8},{4,12},{8,0},{12,4},{16,24},{20,28},{24,16},{28,20},{1,9},{5... | collective-permute-start | bytes 786440 | tf_op jit(solution)/shard_map/ppermute | solution.py:38
  76.0 14.0 %collective-permute-start.17 = (bf16[4,128,256]{2,1,0:T(8,128)(2,1)S(1)}, bf16[4,128,256]{2,1,0:T(8,128)(2,1)S(1)}, u32[]{:S(2)}, u32[]{:S(2)}) collective-permute-start(bf16[4,128,256]{2,1,0:T(8,128)(2,1)S(1)} %get-tuple-element.81), channel_id=1, source_target_pairs={{0,24},{4,28},{8,16},{12,20},{16,8},{20,12},{24,0},{28,4},{1,25},{... | collective-permute-start | bytes 786440 | tf_op jit(solution)/shard_map/ppermute | solution.py:38
  77.6 13.8 %collective-permute-start.16 = (bf16[4,128,256]{2,1,0:T(8,128)(2,1)S(1)}, bf16[4,128,256]{2,1,0:T(8,128)(2,1)S(1)}, u32[]{:S(2)}, u32[]{:S(2)}) collective-permute-start(bf16[4,128,256]{2,1,0:T(8,128)(2,1)S(1)} %get-tuple-element.82), channel_id=1, source_target_pairs={{0,16},{4,20},{8,24},{12,28},{16,0},{20,4},{24,8},{28,12},{1,17},{... | collective-permute-start | bytes 786440 | tf_op jit(solution)/shard_map/ppermute | solution.py:38
  78.5 15.6 %collective-permute-start.23 = (bf16[448,256]{1,0:T(8,128)(2,1)S(1)}, bf16[448,256]{1,0:T(8,128)(2,1)S(1)}, u32[]{:S(2)}, u32[]{:S(2)}) collective-permute-start(bf16[448,256]{1,0:T(8,128)(2,1)S(1)} %get-tuple-element.87), channel_id=1, source_target_pairs={{0,3},{1,2},{2,1},{3,0},{4,7},{5,6},{6,5},{7,4},{8,11},{9,10},{10,... | collective-permute-start | bytes 688136 | tf_op jit(solution)/shard_map/ppermute | solution.py:38
  81.0 22.6 %collective-permute-start.22 = (bf16[448,256]{1,0:T(8,128)(2,1)S(1)}, bf16[448,256]{1,0:T(8,128)(2,1)S(1)}, u32[]{:S(2)}, u32[]{:S(2)}) collective-permute-start(bf16[448,256]{1,0:T(8,128)(2,1)S(1)} %get-tuple-element.88), channel_id=1, source_target_pairs={{0,2},{1,3},{2,0},{3,1},{4,6},{5,7},{6,4},{7,5},{8,10},{9,11},{10,... | collective-permute-start | bytes 688136 | tf_op jit(solution)/shard_map/ppermute | solution.py:38
  84.0 19.6 %collective-permute-start.21 = (bf16[448,256]{1,0:T(8,128)(2,1)S(1)}, bf16[448,256]{1,0:T(8,128)(2,1)S(1)}, u32[]{:S(2)}, u32[]{:S(2)}) collective-permute-start(bf16[448,256]{1,0:T(8,128)(2,1)S(1)} %get-tuple-element.89), channel_id=1, source_target_pairs={{0,1},{1,0},{2,3},{3,2},{4,5},{5,4},{6,7},{7,6},{8,9},{9,8},{10,11... | collective-permute-start | bytes 688136 | tf_op jit(solution)/shard_map/ppermute | solution.py:38
  91.6 13.5 %collective-permute-start.18 = (bf16[128,256]{1,0:T(8,128)(2,1)S(1)}, bf16[128,256]{1,0:T(8,128)(2,1)S(1)}, u32[]{:S(2)}, u32[]{:S(2)}) collective-permute-start(bf16[128,256]{1,0:T(8,128)(2,1)S(1)} %get-tuple-element.90), channel_id=1, source_target_pairs={{0,1},{1,0},{2,3},{3,2},{4,5},{5,4},{6,7},{7,6},{8,9},{9,8},{10,11... | collective-permute-start | bytes 196616 | tf_op jit(solution)/shard_map/ppermute | solution.py:38
  91.7 13.5 %collective-permute-start.20 = (bf16[128,256]{1,0:T(8,128)(2,1)S(1)}, bf16[128,256]{1,0:T(8,128)(2,1)S(1)}, u32[]{:S(2)}, u32[]{:S(2)}) collective-permute-start(bf16[128,256]{1,0:T(8,128)(2,1)S(1)} %get-tuple-element.91), channel_id=1, source_target_pairs={{0,3},{1,2},{2,1},{3,0},{4,7},{5,6},{6,5},{7,4},{8,11},{9,10},{10,... | collective-permute-start | bytes 196616 | tf_op jit(solution)/shard_map/ppermute | solution.py:38
  94.0 11.1 %collective-permute-start.19 = (bf16[128,256]{1,0:T(8,128)(2,1)S(1)}, bf16[128,256]{1,0:T(8,128)(2,1)S(1)}, u32[]{:S(2)}, u32[]{:S(2)}) collective-permute-start(bf16[128,256]{1,0:T(8,128)(2,1)S(1)} %get-tuple-element.92), channel_id=1, source_target_pairs={{0,2},{1,3},{2,0},{3,1},{4,6},{5,7},{6,4},{7,5},{8,10},{9,11},{10,... | collective-permute-start | bytes 196616 | tf_op jit(solution)/shard_map/ppermute | solution.py:38

commit v19 on v17

--- a/solution.py
+++ b/solution.py
@@ -60,12 +60,14 @@
     reach, groups, send_slots, shuffle, cols, count, gc, pc, gx, px, slopes, adj, features, weight, *refs
 ):
     clean, outgoing, *refs = refs
-    sides, packed, refs = refs[:2], refs[2 : 2 + groups], refs[2 + groups :]
-    data, tiles, rhs, stage, results, halos, packs, places, used, sems, pack_sems, out_sems = refs
+    sides, late, packed, refs = refs[:2], refs[2], refs[3 : 3 + groups], refs[3 + groups :]
+    moved = late.shape[1]
+    data, tiles, rhs, stage, results, halos, packs, held, places, used, sems, pack_sems, out_sems = refs
     blocks, slots, rows, _ = adj.shape
     width = gc.shape[1]
     me = (lax.axis_index("node"), lax.axis_index("chan"))
     quarter = features.shape[0] // groups
+    early = quarter - moved
     spare = blocks + 2 * reach
 
     def copies(step):
@@ -84,12 +86,14 @@
         copy.start()
     to_vmem, to_hbm = [], []
     for i in range(groups):
-        span = pl.ds(pl.multiple_of((me[1] ^ i) * quarter, quarter), quarter)
-        to_vmem.append(
-            pltpu.make_async_copy(features.at[span], packs.at[i, :quarter], pack_sems.at[0, i])
-        )
-        to_vmem.append(pltpu.make_async_copy(weight, packs.at[i, quarter:], pack_sems.at[1, i]))
-        to_hbm.append(pltpu.make_async_copy(packs.at[i], packed[i], pack_sems.at[2, i]))
+        start = pl.multiple_of((me[1] ^ i) * quarter, 16)
+        rest = pl.multiple_of((me[1] ^ i) * quarter + early, 16)
+        sources = (features.at[pl.ds(start, early)], weight, features.at[pl.ds(rest, moved)])
+        targets = (packs.at[i, :early], packs.at[i, early:], held.at[i])
+        for j, (source, target) in enumerate(zip(sources, targets)):
+            to_vmem.append(pltpu.make_async_copy(source, target, pack_sems.at[j, i]))
+        to_hbm.append(pltpu.make_async_copy(packs.at[i], packed[i], pack_sems.at[3, i]))
+        to_hbm.append(pltpu.make_async_copy(held.at[i], late.at[i], pack_sems.at[4, i]))
     stage[...] = jnp.zeros_like(stage)
     shape = (rows, rows)
     identity = (
@@ -177,18 +181,25 @@
         copy.wait()
 
 
+def moved_rows(quarter, weight_rows):
+    return min(weight_rows - quarter + 16, quarter // 64 * 16)
+
+
 def aggregate(shuffle, cols, count, gc, pc, gx, px, slopes, adj, features, weight, reach, devs, groups):
     blocks, slots, rows, _ = adj.shape
     width = gc.shape[1]
     send_slots = -(-blocks // devs)
     assert reach % 2 == 0 and blocks % 2 == 0
-    packed = features.shape[0] // groups + weight.shape[0]
+    quarter = features.shape[0] // groups
+    moved = moved_rows(quarter, groups * weight.shape[0])
+    packed = quarter - moved + weight.shape[0]
     return pl.pallas_call(
         functools.partial(aggregate_kernel, reach, groups, send_slots),
         in_specs=[IN_SMEM] * 3 + [IN_HBM] * 4 + [IN_VMEM] + [IN_HBM] * 3,
-        out_specs=[IN_HBM] * (4 + groups),
+        out_specs=[IN_HBM] * (5 + groups),
         out_shape=[bf16(blocks, rows, width), bf16(devs * send_slots, rows, width)]
         + [bf16(2, reach, rows, width)] * 2
+        + [bf16(groups, moved, width)]
         + [bf16(packed, width)] * groups,
         scratch_shapes=[
             pltpu.VMEM((4, blocks // 2, 2 * rows, width), jnp.bfloat16),
@@ -198,10 +209,11 @@
             pltpu.VMEM((2, blocks, rows, width), jnp.bfloat16),
             pltpu.VMEM((2, 2, reach, rows, width), jnp.bfloat16),
             pltpu.VMEM((groups, packed, width), jnp.bfloat16),
+            pltpu.VMEM((groups, moved, width), jnp.bfloat16),
             pltpu.SMEM((blocks,), jnp.int32),
             pltpu.SMEM((devs,), jnp.int32),
             pltpu.SemaphoreType.DMA((5, blocks // 2)),
-            pltpu.SemaphoreType.DMA((3, groups)),
+            pltpu.SemaphoreType.DMA((5, groups)),
             pltpu.SemaphoreType.DMA((4, blocks + 2 * reach)),
         ],
         compiler_params=params(VMEM_ALL),
@@ -265,7 +277,8 @@
     )(index, shuffle, outgoing, pair, beside)
 
 
-def merge_kernel(quarter, index, landing, clean, pair, beside, incoming, out, whole):
+def merge_kernel(quarter, index, landing, clean, pair, beside, incoming, late, out, whole):
+    out[:, quarter:] = late[...]
     blocks, rows, _ = clean.shape
     reach = pair.shape[0]
     group = index[1]
@@ -291,18 +304,19 @@
                 ]
 
 
-def merge(index, landing, clean, pair, beside, incoming, groups):
+def merge(index, landing, clean, pair, beside, incoming, late):
     blocks, rows, width = clean.shape
+    groups, moved, _ = late.shape
     quarter = blocks * rows // groups
     return pl.pallas_call(
         functools.partial(merge_kernel, quarter),
-        in_specs=[IN_SMEM] * 2 + [IN_VMEM] * 4,
+        in_specs=[IN_SMEM] * 2 + [IN_VMEM] * 5,
         out_specs=IN_VMEM,
-        out_shape=bf16(groups, quarter, width),
+        out_shape=bf16(groups, quarter + moved, width),
         scratch_shapes=[pltpu.VMEM((blocks, rows, width), jnp.float32)],
         compiler_params=params(),
         name="merge",
-    )(index, landing, clean, pair, beside, incoming)
+    )(index, landing, clean, pair, beside, incoming, late)
 
 
 def weight_kernel(devs, index, *refs):
@@ -311,10 +325,12 @@
     me, group = index[0], index[1]
     shares = devs // groups
     height, width = keep.shape[2:]
-    rhs = jnp.concatenate([piece[...] for piece in summed], axis=1)
+    early = packed[0].shape[0] - height
+    quarter = (summed[0].shape[0] + early) // 2
+    rhs = jnp.concatenate([piece[:quarter] for piece in summed], axis=1)
     for relative in range(groups):
         product = lax.dot_general(
-            packed[relative][: rhs.shape[0]],
+            jnp.concatenate([packed[relative][:early], summed[relative][quarter:]], axis=0),
             rhs,
             (((0,), (0,)), ((), ())),
             preferred_element_type=jnp.float32,
@@ -358,7 +374,7 @@
     shares = devs // groups
     height = even.shape[2]
     low = me & (shares - 1)
-    lhs = jnp.concatenate([piece[...] for piece in summed], axis=1)
+    lhs = jnp.concatenate([piece[: out.shape[1]] for piece in summed], axis=1)
     for relative in range(first, first + out.shape[0]):
         rows = []
         for i in range(shares):
@@ -380,9 +396,9 @@
             pl.when(low == flip)(functools.partial(store, flip))
 
 
-def feature_rows(index, summed, even, odd, first, count):
+def feature_rows(index, summed, even, odd, first, count, rows):
     groups = len(summed)
-    rows, width = summed[0].shape
+    width = summed[0].shape[1]
     return pl.pallas_call(
         functools.partial(feature_kernel, first),
         in_specs=[IN_SMEM] + [IN_VMEM] * (groups + 2),
@@ -466,7 +482,7 @@
     args = (shuffle_from, adj_cols.T, adj_count)
     args += (grad_clean, pre_clean, grad_corrupt, pre_corrupt, slopes[None, :], adj_vals)
     clean, outgoing, *sides = aggregate(*args, features, weight, reach, devs, groups)
-    (clean_side, side), packed = sides[:2], sides[2:]
+    (clean_side, side, late), packed = sides[:3], sides[3:]
     pair, beside = swapped(side[0], "node", 1), swapped_beside(side[1], "node")
     for i in exchange_order(groups):
         packed[i] = swapped(packed[i], "chan", i)
@@ -480,13 +496,14 @@
     landing = landing_blocks(shuffle_from, me, blocks, devs, slots)
     incoming = exchanged(outgoing, "node")
     incoming, packed = lax.optimization_barrier((incoming, packed))
-    merged = merge(index, landing, clean, clean_pair, clean_beside, incoming, groups)
+    merged = merge(index, landing, clean, clean_pair, clean_beside, incoming, late)
 
     quarter = row_count // groups
+    tiles = jnp.stack([piece[quarter - late.shape[1] :] for piece in packed])
+    merged, tiles = lax.optimization_barrier((merged, tiles))
     summed = [merged[0]] + [None] * (groups - 1)
     for i in exchange_order(groups):
         summed[i] = swapped(merged[i], "chan", i)
-    tiles = jnp.stack([piece[quarter:] for piece in packed])
     even = [tiles] + [swapped(tiles, "node", 2 * i) for i in range(1, devs // 2)]
     order = [0, *range(2, groups - 1), 1, groups - 1]
     listed, even = lax.optimization_barrier(([summed[i] for i in order], even))
@@ -497,9 +514,9 @@
     keep, send = weight_partial(index, packed, summed, devs)
     odd, send = lax.optimization_barrier((odd, send))
     arrived = swapped(send, "node", 1)
-    sent = feature_rows(index, summed, even, odd, 1, groups - 1)
+    sent = feature_rows(index, summed, even, odd, 1, groups - 1, quarter)
     arrived, sent, summed, even, odd = lax.optimization_barrier((arrived, sent, summed, even, odd))
-    pieces = [feature_rows(index, summed, even, odd, 0, 1)[0]] + [None] * (groups - 1)
+    pieces = [feature_rows(index, summed, even, odd, 0, 1, quarter)[0]] + [None] * (groups - 1)
     for i in exchange_order(groups):
         pieces[i] = swapped(sent[i - 1], "chan", i)
     total = wide(keep) + wide(arrived)

time: 104 us -> 109 us (1.048)
  waiting for transfers between devices: 43.2 us -> 51.3 us
  starting transfers between devices: 36.1 us -> 31.2 us
    ppermute x22, waiting for transfers between devices: 38.7 us -> 44.2 us  [swapped(): return lax.ppermute(value, axis, [(i, i ^ by) for i in range(size)])]
    ppermute x22, starting transfers between devices: 26.3 us -> 21.5 us  [swapped(): return lax.ppermute(value, axis, [(i, i ^ by) for i in range(size)])]
    all_to_all x1, waiting for transfers between devices: 2.63 us -> 5.34 us  [exchanged(): return lax.all_to_all(value, axis, split_axis=0, concat_axis=0, tiled=True)]
  transfers between devices with their start and end apart: 25 -> 25, of which waited for: 11 -> 12; matrix products, arithmetic and copies ran while one was open for 2% -> 2% of each run, Pallas kernels for 10% -> 9%
where the time goes in v19:
time: 109 us; the launch traced here: 108 us
  waiting for transfers between devices  51.3 us (47%)
  starting transfers between devices  31.2 us (29%)
  Pallas kernels  19.3 us (18%)
  local copies, waits for them, and re-layouts  3.03 us (3%)
  other arithmetic  2.53 us (2%)
    ppermute x22, waiting for transfers between devices, swapped(): return lax.ppermute(value, axis, [(i, i ^ by) for i in range(size)])  44.2 us
    ppermute x22, starting transfers between devices, swapped(): return lax.ppermute(value, axis, [(i, i ^ by) for i in range(size)])  21.5 us
    pallas_call x1, Pallas kernels, aggregate(): pl.pallas_call(functools.partial(aggregate_kernel, reach, groups, send_sl...  8.08 us
    ppermute x2, starting transfers between devices, swapped_beside(): return lax.ppermute(value, axis, pairs + [(j, i) for i, j in pairs])  5.98 us
    all_to_all x1, waiting for transfers between devices, exchanged(): return lax.all_to_all(value, axis, split_axis=0, concat_axis=0, tiled=True)  5.34 us
    all_to_all x1, starting transfers between devices, exchanged(): return lax.all_to_all(value, axis, split_axis=0, concat_axis=0, tiled=True)  3.7 us
    pallas_call x2, Pallas kernels, feature_rows(): pl.pallas_call(functools.partial(feature_kernel, first), in_specs=[IN_SME...  3.33 us
    pallas_call x1, Pallas kernels, weight_partial(): pl.pallas_call(functools.partial(weight_kernel, devs), in_specs=[IN_SMEM]...  2.65 us
  transfers between devices with their start and end apart: 25, of which 12 were waited for; matrix products, arithmetic and copies ran while one was open for 2% of the time, Pallas kernels for 9%

profile of v19, /device:TPU:0, one launch (start us, length us, event | category | flops | bytes accessed | tf_op | source)
XLA Modules:
  0.0 108.3 jit_solution(16290059523382660890)
XLA Ops:
  0.6 8.1 %aggregate.1 = (bf16[14,128,256]{2,1,0:T(8,128)(2,1)}, bf16[16,128,256]{2,1,0:T(8,128)(2,1)}, bf16[2,2,128,256]{3,2,1,0:T(8,128)(2,1)}, bf16[2,2,128,256]{3,2,1,...) custom-call(s32[112]{0:T(128)} %shuffle.3, ...), custom_call_target="tpu_custom_call" | custom-call | flops 1174405120 | bytes 7798784 | tf_op jit(solution)/shard_map/aggregate/pallas_call | solution.py:196
  8.7 1.0 slice_bitcast_fusion.14
  9.7 3.4 %collective-permute-start.1 = (bf16[2,128,256]{2,1,0:T(8,128)(2,1)S(1)}, bf16[2,128,256]{2,1,0:T(8,128)(2,1)S(1)}, u32[]{:S(2)}, u32[]{:S(2)}) collective-permute-start(bf16[2,128,256]{2,1,0:T(8,128)(2,1)S(1)} %get-tuple-element.101), channel_id=1, source_target_pairs={{4,8},{12,16},{20,24},{28,0},{8,4},{16,12},{24,20},{0,28},{5,9},{1... | collective-permute-start | bytes 393224 | tf_op jit(solution)/shard_map/ppermute | solution.py:33
  13.1 0.0 collective-permute-start
  13.1 1.6 %collective-permute-start.2 = (bf16[496,256]{1,0:T(8,128)(2,1)}, bf16[496,256]{1,0:T(8,128)(2,1)S(1)}, u32[]{:S(2)}, u32[]{:S(2)}) collective-permute-start(bf16[496,256]{1,0:T(8,128)(2,1)} %get-tuple-element.48), channel_id=1, source_target_pairs={{0,1},{1,0},{2,3},{3,2},{4,5},{5,4},{6,7},{7,6},{8,9},{9,8},{10,11... | collective-permute-start | bytes 761864 | tf_op jit(solution)/shard_map/ppermute | solution.py:38
  14.7 2.6 %collective-permute-start.3 = (bf16[496,256]{1,0:T(8,128)(2,1)}, bf16[496,256]{1,0:T(8,128)(2,1)S(1)}, u32[]{:S(2)}, u32[]{:S(2)}) collective-permute-start(bf16[496,256]{1,0:T(8,128)(2,1)} %get-tuple-element.49), channel_id=1, source_target_pairs={{0,2},{1,3},{2,0},{3,1},{4,6},{5,7},{6,4},{7,5},{8,10},{9,11},{10,... | collective-permute-start | bytes 761864 | tf_op jit(solution)/shard_map/ppermute | solution.py:38
  17.3 0.2 collective-permute-start.4
  17.5 0.6 pad_add_fusion.index
  18.1 0.0 collective-permute-done.1.beside
  18.1 0.0 copy-start.6
  18.2 0.6 copy-done.5
  18.8 0.0 copy-done.6
  18.8 2.6 %patch.1 = bf16[16,128,256]{2,1,0:T(8,128)(2,1)} custom-call(s32[2]{0:T(128)} %pad_add_fusion.index, s32[112]{0:T(128)} %shuffle.3, bf16[16,128,256]{2,1,0:T(8,128)(2,1)} %get-tuple-element.42.outgoing, bf16[2,128,256]{2,1,0:T(8,128)(2,1)} %copy-done.6, bf16[2,128,256]{2,1,0:T(8,128)(2,1)} %copy-done.5), custom_call_target="tpu_custom_call", output_to_operand_aliasing={{}: (2, {})} | custom-call | tf_op jit(solution)/shard_map/patch/pallas_call | solution.py:261
  21.5 0.0 copy-start
  21.5 3.7 %all-to-all-start = ((bf16[16,128,256]{2,1,0:T(8,128)(2,1)}), bf16[16,128,256]{2,1,0:T(8,128)(2,1)S(1)}, u32[]{:S(2)}, u32[]{:S(2)}) async-start(bf16[16,128,256]{2,1,0:T(8,128)(2,1)} %patch.1), calls=%async_computation | async-start | bytes 2097152 | tf_op jit(solution)/shard_map/all_to_all | solution.py:42
  25.2 0.1 eq.30
  25.3 0.1 add.45
  25.4 0.3 convert_reduce_fusion
  25.8 0.1 copy.14
  25.8 0.1 select_reduce_fusion
  26.0 0.1 copy.15
  26.1 0.1 sub.13.landing
  26.2 0.7 slice_bitcast_fusion.12
  26.9 2.6 %collective-permute-start.6 = (bf16[2,128,256]{2,1,0:T(8,128)(2,1)}, bf16[2,128,256]{2,1,0:T(8,128)(2,1)S(1)}, u32[]{:S(2)}, u32[]{:S(2)}) collective-permute-start(bf16[2,128,256]{2,1,0:T(8,128)(2,1)} %get-tuple-element.99), channel_id=1, source_target_pairs={{4,8},{12,16},{20,24},{28,0},{8,4},{16,12},{24,20},{0,28},{5,9},{1... | collective-permute-start | bytes 393224 | tf_op jit(solution)/shard_map/ppermute | solution.py:33
  29.5 0.0 collective-permute-start.5
  29.5 0.0 collective-permute-done.2.refs_1_
  29.5 6.2 %collective-permute-done.3.refs_2_ = bf16[496,256]{1,0:T(8,128)(2,1)S(1)} collective-permute-done((bf16[496,256]{1,0:T(8,128)(2,1)}, bf16[496,256]{1,0:T(8,128)(2,1)S(1)}, u32[]{:S(2)}, u32[]{:S(2)}) %collective-permute-start.3) | collective-permute-done | bytes 253984 | tf_op jit(solution)/shard_map/ppermute | solution.py:38
  35.7 5.3 %all-to-all-done.incoming = bf16[16,128,256]{2,1,0:T(8,128)(2,1)S(1)} async-done(((bf16[16,128,256]{2,1,0:T(8,128)(2,1)}), bf16[16,128,256]{2,1,0:T(8,128)(2,1)S(1)}, u32[]{:S(2)}, u32[]{:S(2)}) %all-to-all-start) | async-done | bytes 1048608 | tf_op jit(solution)/shard_map/all_to_all | solution.py:42
  41.1 1.8 %collective-permute-done.6.beside = bf16[2,128,256]{2,1,0:T(8,128)(2,1)S(1)} collective-permute-done((bf16[2,128,256]{2,1,0:T(8,128)(2,1)}, bf16[2,128,256]{2,1,0:T(8,128)(2,1)S(1)}, u32[]{:S(2)}, u32[]{:S(2)}) %collective-permute-start.6) | collective-permute-done | bytes 131104 | tf_op jit(solution)/shard_map/ppermute | solution.py:33
  42.9 1.1 %merge.1 = bf16[4,528,256]{2,1,0:T(8,128)(2,1)S(1)} custom-call(s32[2]{0:T(128)S(1)} %copy-done.3, s32[16]{0:T(128)S(1)} %sub.13.landing, bf16[14,128,256]{2,1,0:T(8,128)(2,1)S(1)} %copy-done, bf16[2,128,256]{2,1,0:T(8,128)(2,1)S(1)} %collective-permute-done.5.pair, bf16[2,128,256]{2,1,0:T(8,128)(2,1)S(1)} %collective-permute-done.6.beside, ...), custom_call_target="tpu_custom_call" | custom-call | tf_op jit(solution)/shard_map/merge/pallas_call | solution.py:311
  44.0 0.7 collective-permute-start.12
  44.6 0.1 slice_bitcast_fusion.1
  44.7 3.7 %collective-permute-start.9 = (bf16[528,256]{1,0:T(8,128)(2,1)S(1)}, bf16[528,256]{1,0:T(8,128)(2,1)S(1)}, u32[]{:S(2)}, u32[]{:S(2)}) collective-permute-start(bf16[528,256]{1,0:T(8,128)(2,1)S(1)} %get-tuple-element.86), channel_id=1, source_target_pairs={{0,3},{1,2},{2,1},{3,0},{4,7},{5,6},{6,5},{7,4},{8,11},{9,10},{10,... | collective-permute-start | bytes 811016 | tf_op jit(solution)/shard_map/ppermute | solution.py:38
  48.4 0.0 collective-permute-start.8
  48.4 0.8 collective-permute-start.7
  49.2 0.6 collective-permute-start.11
  49.8 3.2 %collective-permute-done.12 = bf16[4,128,256]{2,1,0:T(8,128)(2,1)S(1)} collective-permute-done((bf16[4,128,256]{2,1,0:T(8,128)(2,1)S(1)}, bf16[4,128,256]{2,1,0:T(8,128)(2,1)S(1)}, u32[]{:S(2)}, u32[]{:S(2)}) %collective-permute-start.12) | collective-permute-done | bytes 262176 | tf_op jit(solution)/shard_map/ppermute | solution.py:38
  52.9 0.8 collective-permute-start.10
  53.7 4.7 %collective-permute-done.11 = bf16[4,128,256]{2,1,0:T(8,128)(2,1)S(1)} collective-permute-done((bf16[4,128,256]{2,1,0:T(8,128)(2,1)S(1)}, bf16[4,128,256]{2,1,0:T(8,128)(2,1)S(1)}, u32[]{:S(2)}, u32[]{:S(2)}) %collective-permute-start.11) | collective-permute-done | bytes 262176 | tf_op jit(solution)/shard_map/ppermute | solution.py:38
  58.5 2.0 %collective-permute-done.10 = bf16[4,128,256]{2,1,0:T(8,128)(2,1)S(1)} collective-permute-done((bf16[4,128,256]{2,1,0:T(8,128)(2,1)S(1)}, bf16[4,128,256]{2,1,0:T(8,128)(2,1)S(1)}, u32[]{:S(2)}, u32[]{:S(2)}) %collective-permute-start.10) | collective-permute-done | bytes 262176 | tf_op jit(solution)/shard_map/ppermute | solution.py:38
  60.4 1.6 %collective-permute-done.8.refs_5_.refs_1_ = bf16[528,256]{1,0:T(8,128)(2,1)S(1)} collective-permute-done((bf16[528,256]{1,0:T(8,128)(2,1)S(1)}, bf16[528,256]{1,0:T(8,128)(2,1)S(1)}, u32[]{:S(2)}, u32[]{:S(2)}) %collective-permute-start.8) | collective-permute-done | bytes 270368 | tf_op jit(solution)/shard_map/ppermute | solution.py:38
  62.1 9.0 %collective-permute-done.7.refs_6_.refs_2_ = bf16[528,256]{1,0:T(8,128)(2,1)S(1)} collective-permute-done((bf16[528,256]{1,0:T(8,128)(2,1)S(1)}, bf16[528,256]{1,0:T(8,128)(2,1)S(1)}, u32[]{:S(2)}, u32[]{:S(2)}) %collective-permute-start.7) | collective-permute-done | bytes 270368 | tf_op jit(solution)/shard_map/ppermute | solution.py:38
  71.1 0.1 pad_maximum_fusion.refs_4_
  71.2 0.1 collective-permute-start.13
  71.3 2.7 %weight_partial.1 = (bf16[4,4,128,256]{3,2,1,0:T(8,128)(2,1)S(1)}, bf16[4,4,128,256]{3,2,1,0:T(8,128)(2,1)S(1)}) custom-call(s32[2]{0:T(128)S(1)} %copy-done.3, bf16[496,256]{1,0:T(8,128)(2,1)S(1)} %copy-done.2, bf16[496,256]{1,0:T(8,128)(2,1)S(1)} %collective-permute-done.2.refs_1_, bf16[496,256]{1,0:T(8,128)(2,1)S(1)} %collective-permute-done.3.refs_2_, ...), custom_call_target="tpu_custom_call" | custom-call | flops 1107296256 | bytes 4259840 | tf_op jit(solution)/shard_map/weight_partial/pallas_call | solution.py:354
  73.9 0.5 collective-permute-start.14
  74.5 2.3 %feature_rows.2 = bf16[3,448,256]{2,1,0:T(8,128)(2,1)S(1)} custom-call(s32[2]{0:T(128)S(1)} %copy-done.3, bf16[528,256]{1,0:T(8,128)(2,1)S(1)} %get-tuple-element.75.refs_4_.refs_0_, bf16[528,256]{1,0:T(8,128)(2,1)S(1)} %collective-permute-done.8.refs_5_.refs_1_, bf16[528,256]{1,0:T(8,128)(2,1)S(1)} %collective-permute-done.7.refs_6_.refs_2_, ...), custom_call_target="tpu_custom_call" | custom-call | flops 704643072 | bytes 3178496 | tf_op jit(solution)/shard_map/feature_rows/pallas_call | solution.py:402
  76.8 0.4 convert_add_fusion
  77.2 0.1 slice_bitcast_fusion.7
  77.3 1.7 %collective-permute-start.15 = (bf16[4,128,256]{2,1,0:T(8,128)(2,1)S(1)}, bf16[4,128,256]{2,1,0:T(8,128)(2,1)S(1)}, u32[]{:S(2)}, u32[]{:S(2)}) collective-permute-start(bf16[4,128,256]{2,1,0:T(8,128)(2,1)S(1)} %get-tuple-element.90), channel_id=1, source_target_pairs={{0,8},{4,12},{8,0},{12,4},{16,24},{20,28},{24,16},{28,20},{1,9},{5... | collective-permute-start | bytes 786440 | tf_op jit(solution)/shard_map/ppermute | solution.py:38
  79.0 1.5 %collective-permute-start.17 = (bf16[4,128,256]{2,1,0:T(8,128)(2,1)S(1)}, bf16[4,128,256]{2,1,0:T(8,128)(2,1)S(1)}, u32[]{:S(2)}, u32[]{:S(2)}) collective-permute-start(bf16[4,128,256]{2,1,0:T(8,128)(2,1)S(1)} %get-tuple-element.91), channel_id=1, source_target_pairs={{0,24},{4,28},{8,16},{12,20},{16,8},{20,12},{24,0},{28,4},{1,25},{... | collective-permute-start | bytes 786440 | tf_op jit(solution)/shard_map/ppermute | solution.py:38
  80.6 0.3 collective-permute-start.16
  80.9 2.5 %collective-permute-start.23 = (bf16[448,256]{1,0:T(8,128)(2,1)S(1)}, bf16[448,256]{1,0:T(8,128)(2,1)S(1)}, u32[]{:S(2)}, u32[]{:S(2)}) collective-permute-start(bf16[448,256]{1,0:T(8,128)(2,1)S(1)} %get-tuple-element.93), channel_id=1, source_target_pairs={{0,3},{1,2},{2,1},{3,0},{4,7},{5,6},{6,5},{7,4},{8,11},{9,10},{10,... | collective-permute-start | bytes 688136 | tf_op jit(solution)/shard_map/ppermute | solution.py:38
  83.4 3.0 %collective-permute-done.15 = bf16[4,128,256]{2,1,0:T(8,128)(2,1)S(1)} collective-permute-done((bf16[4,128,256]{2,1,0:T(8,128)(2,1)S(1)}, bf16[4,128,256]{2,1,0:T(8,128)(2,1)S(1)}, u32[]{:S(2)}, u32[]{:S(2)}) %collective-permute-start.15) | collective-permute-done | bytes 262176 | tf_op jit(solution)/shard_map/ppermute | solution.py:38
  86.5 6.3 %collective-permute-done.17 = bf16[4,128,256]{2,1,0:T(8,128)(2,1)S(1)} collective-permute-done((bf16[4,128,256]{2,1,0:T(8,128)(2,1)S(1)}, bf16[4,128,256]{2,1,0:T(8,128)(2,1)S(1)}, u32[]{:S(2)}, u32[]{:S(2)}) %collective-permute-start.17) | collective-permute-done | bytes 262176 | tf_op jit(solution)/shard_map/ppermute | solution.py:38
  92.8 1.4 %collective-permute-done.16 = bf16[4,128,256]{2,1,0:T(8,128)(2,1)S(1)} collective-permute-done((bf16[4,128,256]{2,1,0:T(8,128)(2,1)S(1)}, bf16[4,128,256]{2,1,0:T(8,128)(2,1)S(1)}, u32[]{:S(2)}, u32[]{:S(2)}) %collective-permute-start.16) | collective-permute-done | bytes 262176 | tf_op jit(solution)/shard_map/ppermute | solution.py:38
  94.1 0.2 fusion.10
  94.3 0.1 collective-permute-start.18
  94.4 2.5 %collective-permute-start.20 = (bf16[128,256]{1,0:T(8,128)(2,1)S(1)}, bf16[128,256]{1,0:T(8,128)(2,1)S(1)}, u32[]{:S(2)}, u32[]{:S(2)}) collective-permute-start(bf16[128,256]{1,0:T(8,128)(2,1)S(1)} %get-tuple-element.97), channel_id=1, source_target_pairs={{0,3},{1,2},{2,1},{3,0},{4,7},{5,6},{6,5},{7,4},{8,11},{9,10},{10,... | collective-permute-start | bytes 196616 | tf_op jit(solution)/shard_map/ppermute | solution.py:38
  96.9 1.3 %collective-permute-start.19 = (bf16[128,256]{1,0:T(8,128)(2,1)S(1)}, bf16[128,256]{1,0:T(8,128)(2,1)S(1)}, u32[]{:S(2)}, u32[]{:S(2)}) collective-permute-start(bf16[128,256]{1,0:T(8,128)(2,1)S(1)} %get-tuple-element.98), channel_id=1, source_target_pairs={{0,2},{1,3},{2,0},{3,1},{4,6},{5,7},{6,4},{7,5},{8,10},{9,11},{10,... | collective-permute-start | bytes 196616 | tf_op jit(solution)/shard_map/ppermute | solution.py:38
  98.2 1.0 feature_rows.3
  99.2 6.8 %collective-permute-done.22.refs_2_ = bf16[448,256]{1,0:T(8,128)(2,1)S(1)} collective-permute-done((bf16[448,256]{1,0:T(8,128)(2,1)S(1)}, bf16[448,256]{1,0:T(8,128)(2,1)S(1)}, u32[]{:S(2)}, u32[]{:S(2)}) %collective-permute-start.22) | collective-permute-done | bytes 229408 | tf_op jit(solution)/shard_map/ppermute | solution.py:38
  106.0 1.5 %laid_out.1 = bf16[1792,256]{1,0:T(8,128)(2,1)} custom-call(s32[2]{0:T(128)S(1)} %copy-done.3, bf16[448,256]{1,0:T(8,128)(2,1)S(1)} %bitcast.68, bf16[448,256]{1,0:T(8,128)(2,1)S(1)} %collective-permute-done.21.refs_1_, bf16[448,256]{1,0:T(8,128)(2,1)S(1)} %collective-permute-done.22.refs_2_, bf16[448,256]{1,0:T(8,128)(2,1)S(1)} %collective-permute-done.23.refs_3_), custom_call_target="tpu_custom_call" | custom-call | tf_op jit(solution)/shard_map/laid_out/pallas_call | solution.py:434
  107.6 0.7 fusion.5
  (34 shorter events, 0.2 us)
Async XLA Ops:
  9.7 8.4 %collective-permute-start.1 = (bf16[2,128,256]{2,1,0:T(8,128)(2,1)S(1)}, bf16[2,128,256]{2,1,0:T(8,128)(2,1)S(1)}, u32[]{:S(2)}, u32[]{:S(2)}) collective-permute-start(bf16[2,128,256]{2,1,0:T(8,128)(2,1)S(1)} %get-tuple-element.101), channel_id=1, source_target_pairs={{4,8},{12,16},{20,24},{28,0},{8,4},{16,12},{24,20},{0,28},{5,9},{1... | collective-permute-start | bytes 393224 | tf_op jit(solution)/shard_map/ppermute | solution.py:33
  13.1 5.0 %collective-permute-start = (bf16[2,128,256]{2,1,0:T(8,128)(2,1)S(1)}, bf16[2,128,256]{2,1,0:T(8,128)(2,1)S(1)}, u32[]{:S(2)}, u32[]{:S(2)}) collective-permute-start(bf16[2,128,256]{2,1,0:T(8,128)(2,1)S(1)} %get-tuple-element.102), channel_id=1, source_target_pairs={{0,4},{4,0},{8,12},{12,8},{16,20},{20,16},{24,28},{28,24},{1,5},{5... | collective-permute-start | bytes 393224 | tf_op jit(solution)/shard_map/ppermute | solution.py:38
  13.1 16.4 %collective-permute-start.2 = (bf16[496,256]{1,0:T(8,128)(2,1)}, bf16[496,256]{1,0:T(8,128)(2,1)S(1)}, u32[]{:S(2)}, u32[]{:S(2)}) collective-permute-start(bf16[496,256]{1,0:T(8,128)(2,1)} %get-tuple-element.48), channel_id=1, source_target_pairs={{0,1},{1,0},{2,3},{3,2},{4,5},{5,4},{6,7},{7,6},{8,9},{9,8},{10,11... | collective-permute-start | bytes 761864 | tf_op jit(solution)/shard_map/ppermute | solution.py:38
  14.7 21.0 %collective-permute-start.3 = (bf16[496,256]{1,0:T(8,128)(2,1)}, bf16[496,256]{1,0:T(8,128)(2,1)S(1)}, u32[]{:S(2)}, u32[]{:S(2)}) collective-permute-start(bf16[496,256]{1,0:T(8,128)(2,1)} %get-tuple-element.49), channel_id=1, source_target_pairs={{0,2},{1,3},{2,0},{3,1},{4,6},{5,7},{6,4},{7,5},{8,10},{9,11},{10,... | collective-permute-start | bytes 761864 | tf_op jit(solution)/shard_map/ppermute | solution.py:38
  17.3 18.4 %collective-permute-start.4 = (bf16[496,256]{1,0:T(8,128)(2,1)}, bf16[496,256]{1,0:T(8,128)(2,1)S(1)}, u32[]{:S(2)}, u32[]{:S(2)}) collective-permute-start(bf16[496,256]{1,0:T(8,128)(2,1)} %get-tuple-element.50), channel_id=1, source_target_pairs={{0,3},{1,2},{2,1},{3,0},{4,7},{5,6},{6,5},{7,4},{8,11},{9,10},{10,... | collective-permute-start | bytes 761864 | tf_op jit(solution)/shard_map/ppermute | solution.py:38
  18.1 0.7 copy-start.5
  18.1 0.7 copy-start.6
  18.8 6.4 %copy-start.7 = (s32[112]{0:T(128)S(1)}, s32[112]{0:T(128)}, u32[]{:S(2)}) copy-start(s32[112]{0:T(128)} %shuffle.3) | copy-start | bytes 1348
  18.8 22.2 %copy-start.2 = (bf16[496,256]{1,0:T(8,128)(2,1)S(1)}, bf16[496,256]{1,0:T(8,128)(2,1)}, u32[]{:S(2)}) copy-start(bf16[496,256]{1,0:T(8,128)(2,1)} %get-tuple-element.51.refs_0_) | copy-start | bytes 761860
  21.5 4.7 %copy-start.4 = (bf16[2,2,128,256]{3,2,1,0:T(8,128)(2,1)S(1)}, bf16[2,2,128,256]{3,2,1,0:T(8,128)(2,1)}, u32[]{:S(2)}) copy-start(bf16[2,2,128,256]{3,2,1,0:T(8,128)(2,1)} %get-tuple-element.57) | copy-start | bytes 786436
  21.5 21.4 %copy-start = (bf16[14,128,256]{2,1,0:T(8,128)(2,1)S(1)}, bf16[14,128,256]{2,1,0:T(8,128)(2,1)}, u32[]{:S(2)}) copy-start(bf16[14,128,256]{2,1,0:T(8,128)(2,1)} %get-tuple-element.56.clean) | copy-start | bytes 2752516
  21.5 21.4 %copy-start.1 = (bf16[4,80,256]{2,1,0:T(8,128)(2,1)S(1)}, bf16[4,80,256]{2,1,0:T(8,128)(2,1)}, u32[]{:S(2)}) copy-start(bf16[4,80,256]{2,1,0:T(8,128)(2,1)} %get-tuple-element.59.late) | copy-start | bytes 491524
  21.5 21.4 %copy-start.3 = (s32[2]{0:T(128)S(1)}, s32[2]{0:T(128)}, u32[]{:S(2)}) copy-start(s32[2]{0:T(128)} %pad_add_fusion.index) | copy-start | bytes 28
  21.5 19.5 %all-to-all-start = ((bf16[16,128,256]{2,1,0:T(8,128)(2,1)}), bf16[16,128,256]{2,1,0:T(8,128)(2,1)S(1)}, u32[]{:S(2)}, u32[]{:S(2)}) async-start(bf16[16,128,256]{2,1,0:T(8,128)(2,1)} %patch.1), calls=%async_computation | async-start | bytes 2097152 | tf_op jit(solution)/shard_map/all_to_all | solution.py:42
  26.9 16.0 %collective-permute-start.6 = (bf16[2,128,256]{2,1,0:T(8,128)(2,1)}, bf16[2,128,256]{2,1,0:T(8,128)(2,1)S(1)}, u32[]{:S(2)}, u32[]{:S(2)}) collective-permute-start(bf16[2,128,256]{2,1,0:T(8,128)(2,1)} %get-tuple-element.99), channel_id=1, source_target_pairs={{4,8},{12,16},{20,24},{28,0},{8,4},{16,12},{24,20},{0,28},{5,9},{1... | collective-permute-start | bytes 393224 | tf_op jit(solution)/shard_map/ppermute | solution.py:33
  29.5 13.4 %collective-permute-start.5 = (bf16[2,128,256]{2,1,0:T(8,128)(2,1)}, bf16[2,128,256]{2,1,0:T(8,128)(2,1)S(1)}, u32[]{:S(2)}, u32[]{:S(2)}) collective-permute-start(bf16[2,128,256]{2,1,0:T(8,128)(2,1)} %get-tuple-element.100), channel_id=1, source_target_pairs={{0,4},{4,0},{8,12},{12,8},{16,20},{20,16},{24,28},{28,24},{1,5},{5... | collective-permute-start | bytes 393224 | tf_op jit(solution)/shard_map/ppermute | solution.py:38
  44.0 8.9 %collective-permute-start.12 = (bf16[4,128,256]{2,1,0:T(8,128)(2,1)S(1)}, bf16[4,128,256]{2,1,0:T(8,128)(2,1)S(1)}, u32[]{:S(2)}, u32[]{:S(2)}) collective-permute-start(bf16[4,128,256]{2,1,0:T(8,128)(2,1)S(1)} %pad_maximum_fusion.1), channel_id=1, source_target_pairs={{0,24},{4,28},{8,16},{12,20},{16,8},{20,12},{24,0},{28,4},{1,25},{... | collective-permute-start | bytes 786440 | tf_op jit(solution)/shard_map/ppermute | solution.py:38
  44.7 15.7 %collective-permute-start.9 = (bf16[528,256]{1,0:T(8,128)(2,1)S(1)}, bf16[528,256]{1,0:T(8,128)(2,1)S(1)}, u32[]{:S(2)}, u32[]{:S(2)}) collective-permute-start(bf16[528,256]{1,0:T(8,128)(2,1)S(1)} %get-tuple-element.86), channel_id=1, source_target_pairs={{0,3},{1,2},{2,1},{3,0},{4,7},{5,6},{6,5},{7,4},{8,11},{9,10},{10,... | collective-permute-start | bytes 811016 | tf_op jit(solution)/shard_map/ppermute | solution.py:38
  48.4 13.7 %collective-permute-start.8 = (bf16[528,256]{1,0:T(8,128)(2,1)S(1)}, bf16[528,256]{1,0:T(8,128)(2,1)S(1)}, u32[]{:S(2)}, u32[]{:S(2)}) collective-permute-start(bf16[528,256]{1,0:T(8,128)(2,1)S(1)} %get-tuple-element.87), channel_id=1, source_target_pairs={{0,1},{1,0},{2,3},{3,2},{4,5},{5,4},{6,7},{7,6},{8,9},{9,8},{10,11... | collective-permute-start | bytes 811016 | tf_op jit(solution)/shard_map/ppermute | solution.py:38
  48.4 22.7 %collective-permute-start.7 = (bf16[528,256]{1,0:T(8,128)(2,1)S(1)}, bf16[528,256]{1,0:T(8,128)(2,1)S(1)}, u32[]{:S(2)}, u32[]{:S(2)}) collective-permute-start(bf16[528,256]{1,0:T(8,128)(2,1)S(1)} %get-tuple-element.88), channel_id=1, source_target_pairs={{0,2},{1,3},{2,0},{3,1},{4,6},{5,7},{6,4},{7,5},{8,10},{9,11},{10,... | collective-permute-start | bytes 811016 | tf_op jit(solution)/shard_map/ppermute | solution.py:38
  49.2 9.3 %collective-permute-start.11 = (bf16[4,128,256]{2,1,0:T(8,128)(2,1)S(1)}, bf16[4,128,256]{2,1,0:T(8,128)(2,1)S(1)}, u32[]{:S(2)}, u32[]{:S(2)}) collective-permute-start(bf16[4,128,256]{2,1,0:T(8,128)(2,1)S(1)} %pad_maximum_fusion.1), channel_id=1, source_target_pairs={{0,16},{4,20},{8,24},{12,28},{16,0},{20,4},{24,8},{28,12},{1,17},{... | collective-permute-start | bytes 786440 | tf_op jit(solution)/shard_map/ppermute | solution.py:38
  52.9 7.5 %collective-permute-start.10 = (bf16[4,128,256]{2,1,0:T(8,128)(2,1)S(1)}, bf16[4,128,256]{2,1,0:T(8,128)(2,1)S(1)}, u32[]{:S(2)}, u32[]{:S(2)}) collective-permute-start(bf16[4,128,256]{2,1,0:T(8,128)(2,1)S(1)} %pad_maximum_fusion.1), channel_id=1, source_target_pairs={{0,8},{4,12},{8,0},{12,4},{16,24},{20,28},{24,16},{28,20},{1,9},{5... | collective-permute-start | bytes 786440 | tf_op jit(solution)/shard_map/ppermute | solution.py:38
  71.2 2.7 %collective-permute-start.13 = (bf16[4,4,128,256]{3,2,1,0:T(8,128)(2,1)S(1)}, bf16[4,4,128,256]{3,2,1,0:T(8,128)(2,1)S(1)}, u32[]{:S(2)}, u32[]{:S(2)}) collective-permute-start(bf16[4,4,128,256]{3,2,1,0:T(8,128)(2,1)S(1)} %pad_maximum_fusion.refs_4_), channel_id=1, source_target_pairs={{0,4},{4,0},{8,12},{12,8},{16,20},{20,16},{24,28},{28,24},{1,5},{5... | collective-permute-start | bytes 3145736 | tf_op jit(solution)/shard_map/ppermute | solution.py:38
  73.9 2.9 %collective-permute-start.14 = (bf16[4,4,128,256]{3,2,1,0:T(8,128)(2,1)S(1)}, bf16[4,4,128,256]{3,2,1,0:T(8,128)(2,1)S(1)}, u32[]{:S(2)}, u32[]{:S(2)}) collective-permute-start(bf16[4,4,128,256]{3,2,1,0:T(8,128)(2,1)S(1)} %get-tuple-element.72), channel_id=1, source_target_pairs={{0,4},{4,0},{8,12},{12,8},{16,20},{20,16},{24,28},{28,24},{1,5},{5... | collective-permute-start | bytes 3145736 | tf_op jit(solution)/shard_map/ppermute | solution.py:38
  77.3 9.2 %collective-permute-start.15 = (bf16[4,128,256]{2,1,0:T(8,128)(2,1)S(1)}, bf16[4,128,256]{2,1,0:T(8,128)(2,1)S(1)}, u32[]{:S(2)}, u32[]{:S(2)}) collective-permute-start(bf16[4,128,256]{2,1,0:T(8,128)(2,1)S(1)} %get-tuple-element.90), channel_id=1, source_target_pairs={{0,8},{4,12},{8,0},{12,4},{16,24},{20,28},{24,16},{28,20},{1,9},{5... | collective-permute-start | bytes 786440 | tf_op jit(solution)/shard_map/ppermute | solution.py:38
  79.0 13.7 %collective-permute-start.17 = (bf16[4,128,256]{2,1,0:T(8,128)(2,1)S(1)}, bf16[4,128,256]{2,1,0:T(8,128)(2,1)S(1)}, u32[]{:S(2)}, u32[]{:S(2)}) collective-permute-start(bf16[4,128,256]{2,1,0:T(8,128)(2,1)S(1)} %get-tuple-element.91), channel_id=1, source_target_pairs={{0,24},{4,28},{8,16},{12,20},{16,8},{20,12},{24,0},{28,4},{1,25},{... | collective-permute-start | bytes 786440 | tf_op jit(solution)/shard_map/ppermute | solution.py:38
  80.6 13.6 %collective-permute-start.16 = (bf16[4,128,256]{2,1,0:T(8,128)(2,1)S(1)}, bf16[4,128,256]{2,1,0:T(8,128)(2,1)S(1)}, u32[]{:S(2)}, u32[]{:S(2)}) collective-permute-start(bf16[4,128,256]{2,1,0:T(8,128)(2,1)S(1)} %get-tuple-element.92), channel_id=1, source_target_pairs={{0,16},{4,20},{8,24},{12,28},{16,0},{20,4},{24,8},{28,12},{1,17},{... | collective-permute-start | bytes 786440 | tf_op jit(solution)/shard_map/ppermute | solution.py:38
  80.9 16.0 %collective-permute-start.23 = (bf16[448,256]{1,0:T(8,128)(2,1)S(1)}, bf16[448,256]{1,0:T(8,128)(2,1)S(1)}, u32[]{:S(2)}, u32[]{:S(2)}) collective-permute-start(bf16[448,256]{1,0:T(8,128)(2,1)S(1)} %get-tuple-element.93), channel_id=1, source_target_pairs={{0,3},{1,2},{2,1},{3,0},{4,7},{5,6},{6,5},{7,4},{8,11},{9,10},{10,... | collective-permute-start | bytes 688136 | tf_op jit(solution)/shard_map/ppermute | solution.py:38
  83.4 22.6 %collective-permute-start.22 = (bf16[448,256]{1,0:T(8,128)(2,1)S(1)}, bf16[448,256]{1,0:T(8,128)(2,1)S(1)}, u32[]{:S(2)}, u32[]{:S(2)}) collective-permute-start(bf16[448,256]{1,0:T(8,128)(2,1)S(1)} %get-tuple-element.94), channel_id=1, source_target_pairs={{0,2},{1,3},{2,0},{3,1},{4,6},{5,7},{6,4},{7,5},{8,10},{9,11},{10,... | collective-permute-start | bytes 688136 | tf_op jit(solution)/shard_map/ppermute | solution.py:38
  86.5 19.5 %collective-permute-start.21 = (bf16[448,256]{1,0:T(8,128)(2,1)S(1)}, bf16[448,256]{1,0:T(8,128)(2,1)S(1)}, u32[]{:S(2)}, u32[]{:S(2)}) collective-permute-start(bf16[448,256]{1,0:T(8,128)(2,1)S(1)} %get-tuple-element.95), channel_id=1, source_target_pairs={{0,1},{1,0},{2,3},{3,2},{4,5},{5,4},{6,7},{7,6},{8,9},{9,8},{10,11... | collective-permute-start | bytes 688136 | tf_op jit(solution)/shard_map/ppermute | solution.py:38
  94.3 13.2 %collective-permute-start.18 = (bf16[128,256]{1,0:T(8,128)(2,1)S(1)}, bf16[128,256]{1,0:T(8,128)(2,1)S(1)}, u32[]{:S(2)}, u32[]{:S(2)}) collective-permute-start(bf16[128,256]{1,0:T(8,128)(2,1)S(1)} %get-tuple-element.96), channel_id=1, source_target_pairs={{0,1},{1,0},{2,3},{3,2},{4,5},{5,4},{6,7},{7,6},{8,9},{9,8},{10,11... | collective-permute-start | bytes 196616 | tf_op jit(solution)/shard_map/ppermute | solution.py:38
  94.4 13.2 %collective-permute-start.20 = (bf16[128,256]{1,0:T(8,128)(2,1)S(1)}, bf16[128,256]{1,0:T(8,128)(2,1)S(1)}, u32[]{:S(2)}, u32[]{:S(2)}) collective-permute-start(bf16[128,256]{1,0:T(8,128)(2,1)S(1)} %get-tuple-element.97), channel_id=1, source_target_pairs={{0,3},{1,2},{2,1},{3,0},{4,7},{5,6},{6,5},{7,4},{8,11},{9,10},{10,... | collective-permute-start | bytes 196616 | tf_op jit(solution)/shard_map/ppermute | solution.py:38
  96.9 10.6 %collective-permute-start.19 = (bf16[128,256]{1,0:T(8,128)(2,1)S(1)}, bf16[128,256]{1,0:T(8,128)(2,1)S(1)}, u32[]{:S(2)}, u32[]{:S(2)}) collective-permute-start(bf16[128,256]{1,0:T(8,128)(2,1)S(1)} %get-tuple-element.98), channel_id=1, source_target_pairs={{0,2},{1,3},{2,0},{3,1},{4,6},{5,7},{6,4},{7,5},{8,10},{9,11},{10,... | collective-permute-start | bytes 196616 | tf_op jit(solution)/shard_map/ppermute | solution.py:38

commit v20 on v18

--- a/solution.py
+++ b/solution.py
@@ -27,9 +27,9 @@
     return value.astype(jnp.float32)
 
 
-def swapped_beside(value, axis):
+def swapped_beside(value, axis, round):
     size = lax.axis_size(axis)
-    pairs = [(i, i + 1) for i in range(1, size - 1, 2)]
+    pairs = [(i, (i + 1) % size) for i in range(1, size if round else size - 1, 2)]
     return lax.ppermute(value, axis, pairs + [(j, i) for i, j in pairs])
 
 
@@ -214,8 +214,9 @@
     )(shuffle, cols, count, gc, pc, gx, px, slopes, adj, features, weight)
 
 
-def patch_kernel(reach, blocks, slots, index, shuffle, outgoing, pair, beside, out, *scratch):
+def patch_kernel(reach, blocks, slots, shuffle, outgoing, pair, beside, out, *scratch):
     held, other, ready, places, used, sems = scratch
+    index = (lax.axis_index("node"),)
     odd = index[0] & 1
     arrivals = [
         pltpu.make_async_copy(pair, other.at[pl.ds((1 - odd) * reach, reach)], sems.at[2, 0]),
@@ -242,16 +243,16 @@
         copy.wait()
 
 
-def patch(index, shuffle, outgoing, pair, beside, blocks, slots):
+def patch(shuffle, outgoing, pair, beside, blocks, slots):
     sent, rows, width = outgoing.shape
     reach = pair.shape[0]
     border = pltpu.VMEM((2 * reach, rows, width), jnp.bfloat16)
     return pl.pallas_call(
         functools.partial(patch_kernel, reach, blocks, slots),
-        in_specs=[IN_SMEM] * 2 + [IN_HBM] * 3,
+        in_specs=[IN_SMEM] + [IN_HBM] * 3,
         out_specs=IN_HBM,
         out_shape=bf16(*outgoing.shape),
-        input_output_aliases={2: 0},
+        input_output_aliases={1: 0},
         scratch_shapes=[
             border,
             border,
@@ -262,7 +263,7 @@
         ],
         compiler_params=params(VMEM_ALL),
         name="patch",
-    )(index, shuffle, outgoing, pair, beside)
+    )(shuffle, outgoing, pair, beside)
 
 
 def merge_kernel(quarter, index, landing, clean, pair, beside, incoming, out, whole):
@@ -467,16 +468,16 @@
     args += (grad_clean, pre_clean, grad_corrupt, pre_corrupt, slopes[None, :], adj_vals)
     clean, outgoing, *sides = aggregate(*args, features, weight, reach, devs, groups)
     (clean_side, side), packed = sides[:2], sides[2:]
-    pair, beside = swapped(side[0], "node", 1), swapped_beside(side[1], "node")
+    pair, beside = swapped(side[0], "node", 1), swapped_beside(side[1], "node", True)
     for i in exchange_order(groups):
         packed[i] = swapped(packed[i], "chan", i)
 
-    outgoing = patch(index, shuffle_from, outgoing, pair, beside, blocks, slots)
+    outgoing = patch(shuffle_from, outgoing, pair, beside, blocks, slots)
     shuffle_from, outgoing, clean, clean_side = lax.optimization_barrier(
         (shuffle_from, outgoing, clean, clean_side)
     )
     clean_pair = swapped(clean_side[0], "node", 1)
-    clean_beside = swapped_beside(clean_side[1], "node")
+    clean_beside = swapped_beside(clean_side[1], "node", False)
     landing = landing_blocks(shuffle_from, me, blocks, devs, slots)
     incoming = exchanged(outgoing, "node")
     incoming, packed = lax.optimization_barrier((incoming, packed))

time: 106 us -> 105 us (level)
  waiting for transfers between devices: 37.5 us -> 35.5 us
  starting transfers between devices: 43.5 us -> 44.7 us
    ppermute x2, starting transfers between devices: 1.34 us -> 4.08 us  [swapped_beside(): return lax.ppermute(value, axis, pairs + [(j, i) for i, j in pairs])]
    ppermute x22, waiting for transfers between devices: 35.4 us -> 33.9 us  [swapped(): return lax.ppermute(value, axis, [(i, i ^ by) for i in range(size)])]
    ppermute x22, starting transfers between devices: 38.5 us -> 37 us  [swapped(): return lax.ppermute(value, axis, [(i, i ^ by) for i in range(size)])]
  transfers between devices with their start and end apart: 25 -> 25, of which waited for: 8 -> 8; matrix products, arithmetic and copies ran while one was open for 2% -> 1% of each run, Pallas kernels for 10% -> 10%
where the time goes in v20:
time: 105 us
  starting transfers between devices  44.7 us (43%)
  waiting for transfers between devices  35.5 us (34%)
  Pallas kernels  19.1 us (18%)
  local copies, waits for them, and re-layouts  2.3 us (2%)
  other arithmetic  1.98 us (2%)
    ppermute x22, starting transfers between devices, swapped(): return lax.ppermute(value, axis, [(i, i ^ by) for i in range(size)])  37 us
    ppermute x22, waiting for transfers between devices, swapped(): return lax.ppermute(value, axis, [(i, i ^ by) for i in range(size)])  33.9 us
    pallas_call x1, Pallas kernels, aggregate(): pl.pallas_call(functools.partial(aggregate_kernel, reach, groups, send_sl...  7.91 us
    ppermute x2, starting transfers between devices, swapped_beside(): return lax.ppermute(value, axis, pairs + [(j, i) for i, j in pairs])  4.08 us
    all_to_all x1, starting transfers between devices, exchanged(): return lax.all_to_all(value, axis, split_axis=0, concat_axis=0, tiled=True)  3.7 us
    pallas_call x2, Pallas kernels, feature_rows(): pl.pallas_call(functools.partial(feature_kernel, first), in_specs=[IN_SME...  3.33 us
    pallas_call x1, Pallas kernels, weight_partial(): pl.pallas_call(functools.partial(weight_kernel, devs), in_specs=[IN_SMEM]...  2.65 us
    pallas_call x1, Pallas kernels, patch(): pl.pallas_call(functools.partial(patch_kernel, reach, blocks, slots), in_...  2.63 us
  transfers between devices with their start and end apart: 25, of which 8 were waited for; matrix products, arithmetic and copies ran while one was open for 1% of the time, Pallas kernels for 10%

profile of v20, /device:TPU:0, one launch (start us, length us, event | category | flops | bytes accessed | tf_op | source)
XLA Modules:
  0.0 104.6 jit_solution(15209850630235517105)
XLA Ops:
  0.6 7.9 %aggregate.1 = (bf16[14,128,256]{2,1,0:T(8,128)(2,1)}, bf16[16,128,256]{2,1,0:T(8,128)(2,1)}, bf16[2,2,128,256]{3,2,1,0:T(8,128)(2,1)}, bf16[2,2,128,256]{3,2,1,...) custom-call(s32[112]{0:T(128)} %shuffle.3, ...), custom_call_target="tpu_custom_call" | custom-call | flops 1174405120 | bytes 7798784 | tf_op jit(solution)/shard_map/aggregate/pallas_call | solution.py:186
  8.6 1.0 slice_bitcast_fusion.14
  9.5 3.4 %collective-permute-start.1 = (bf16[2,128,256]{2,1,0:T(8,128)(2,1)S(1)}, bf16[2,128,256]{2,1,0:T(8,128)(2,1)S(1)}, u32[]{:S(2)}, u32[]{:S(2)}) collective-permute-start(bf16[2,128,256]{2,1,0:T(8,128)(2,1)S(1)} %get-tuple-element.95), channel_id=1, source_target_pairs={{4,8},{12,16},{20,24},{28,0},{8,4},{16,12},{24,20},{0,28},{5,9},{1... | collective-permute-start | bytes 393224 | tf_op jit(solution)/shard_map/ppermute | solution.py:33
  13.0 0.0 collective-permute-start
  13.0 1.6 %collective-permute-start.2 = (bf16[576,256]{1,0:T(8,128)(2,1)}, bf16[576,256]{1,0:T(8,128)(2,1)S(1)}, u32[]{:S(2)}, u32[]{:S(2)}) collective-permute-start(bf16[576,256]{1,0:T(8,128)(2,1)} %get-tuple-element.45), channel_id=1, source_target_pairs={{0,1},{1,0},{2,3},{3,2},{4,5},{5,4},{6,7},{7,6},{8,9},{9,8},{10,11... | collective-permute-start | bytes 884744 | tf_op jit(solution)/shard_map/ppermute | solution.py:38
  14.5 2.6 %collective-permute-start.3 = (bf16[576,256]{1,0:T(8,128)(2,1)}, bf16[576,256]{1,0:T(8,128)(2,1)S(1)}, u32[]{:S(2)}, u32[]{:S(2)}) collective-permute-start(bf16[576,256]{1,0:T(8,128)(2,1)} %get-tuple-element.46), channel_id=1, source_target_pairs={{0,2},{1,3},{2,0},{3,1},{4,6},{5,7},{6,4},{7,5},{8,10},{9,11},{10,... | collective-permute-start | bytes 884744 | tf_op jit(solution)/shard_map/ppermute | solution.py:38
  17.1 0.2 collective-permute-start.4
  17.3 0.1 pad_add_fusion.index
  17.5 0.0 copy-start.4
  17.5 0.6 copy-done.3
  18.1 0.0 copy-done.4
  18.1 2.6 %patch.1 = bf16[16,128,256]{2,1,0:T(8,128)(2,1)} custom-call(s32[112]{0:T(128)} %shuffle.3, bf16[16,128,256]{2,1,0:T(8,128)(2,1)} %get-tuple-element.39.outgoing, bf16[2,128,256]{2,1,0:T(8,128)(2,1)} %copy-done.4, bf16[2,128,256]{2,1,0:T(8,128)(2,1)} %copy-done.3), custom_call_target="tpu_custom_call", output_to_operand_aliasing={{}: (1, {})} | custom-call | tf_op jit(solution)/shard_map/patch/pallas_call | solution.py:250
  20.8 3.7 %all-to-all-start = ((bf16[16,128,256]{2,1,0:T(8,128)(2,1)}), bf16[16,128,256]{2,1,0:T(8,128)(2,1)S(1)}, u32[]{:S(2)}, u32[]{:S(2)}) async-start(bf16[16,128,256]{2,1,0:T(8,128)(2,1)} %patch.1), calls=%async_computation | async-start | bytes 2097152 | tf_op jit(solution)/shard_map/all_to_all | solution.py:42
  24.5 0.1 eq.30
  24.6 0.1 add.45
  24.7 0.3 convert_reduce_fusion
  25.0 0.1 copy.14
  25.1 0.7 collective-permute-start.6
  25.8 3.3 %collective-permute-start.5 = (bf16[2,128,256]{2,1,0:T(8,128)(2,1)S(1)}, bf16[2,128,256]{2,1,0:T(8,128)(2,1)S(1)}, u32[]{:S(2)}, u32[]{:S(2)}) collective-permute-start(bf16[2,128,256]{2,1,0:T(8,128)(2,1)S(1)} %get-tuple-element.94), channel_id=1, source_target_pairs={{0,4},{4,0},{8,12},{12,8},{16,20},{20,16},{24,28},{28,24},{1,5},{5... | collective-permute-start | bytes 393224 | tf_op jit(solution)/shard_map/ppermute | solution.py:38
  29.2 0.1 select_reduce_fusion
  29.3 0.1 copy.15
  29.4 0.1 sub.13.landing
  29.5 0.0 collective-permute-done.2.refs_1_
  29.5 8.7 %collective-permute-done.3.refs_2_ = bf16[576,256]{1,0:T(8,128)(2,1)S(1)} collective-permute-done((bf16[576,256]{1,0:T(8,128)(2,1)}, bf16[576,256]{1,0:T(8,128)(2,1)S(1)}, u32[]{:S(2)}, u32[]{:S(2)}) %collective-permute-start.3) | collective-permute-done | bytes 294944 | tf_op jit(solution)/shard_map/ppermute | solution.py:38
  38.2 0.0 collective-permute-done.4.refs_3_
  38.2 1.6 %all-to-all-done.incoming = bf16[16,128,256]{2,1,0:T(8,128)(2,1)S(1)} async-done(((bf16[16,128,256]{2,1,0:T(8,128)(2,1)}), bf16[16,128,256]{2,1,0:T(8,128)(2,1)S(1)}, u32[]{:S(2)}, u32[]{:S(2)}) %all-to-all-start) | async-done | bytes 1048608 | tf_op jit(solution)/shard_map/all_to_all | solution.py:42
  39.8 0.0 collective-permute-done.6.beside
  39.8 0.0 collective-permute-done.5.pair
  39.8 1.1 %merge.1 = bf16[4,448,256]{2,1,0:T(8,128)(2,1)S(1)} custom-call(s32[2]{0:T(128)S(1)} %pad_add_fusion.index, s32[16]{0:T(128)S(1)} %sub.13.landing, bf16[14,128,256]{2,1,0:T(8,128)(2,1)S(1)} %copy-done, bf16[2,128,256]{2,1,0:T(8,128)(2,1)S(1)} %collective-permute-done.5.pair, bf16[2,128,256]{2,1,0:T(8,128)(2,1)S(1)} %collective-permute-done.6.beside, ...), custom_call_target="tpu_custom_call" | custom-call | tf_op jit(solution)/shard_map/merge/pallas_call | solution.py:298
  40.9 0.1 slice_bitcast_fusion.4
  41.0 3.9 %collective-permute-start.9 = (bf16[448,256]{1,0:T(8,128)(2,1)S(1)}, bf16[448,256]{1,0:T(8,128)(2,1)S(1)}, u32[]{:S(2)}, u32[]{:S(2)}) collective-permute-start(bf16[448,256]{1,0:T(8,128)(2,1)S(1)} %get-tuple-element.83), channel_id=1, source_target_pairs={{0,3},{1,2},{2,1},{3,0},{4,7},{5,6},{6,5},{7,4},{8,11},{9,10},{10,... | collective-permute-start | bytes 688136 | tf_op jit(solution)/shard_map/ppermute | solution.py:38
  45.0 3.0 %collective-permute-start.12 = (bf16[4,128,256]{2,1,0:T(8,128)(2,1)S(1)}, bf16[4,128,256]{2,1,0:T(8,128)(2,1)S(1)}, u32[]{:S(2)}, u32[]{:S(2)}) collective-permute-start(bf16[4,128,256]{2,1,0:T(8,128)(2,1)S(1)} %pad_maximum_fusion.1), channel_id=1, source_target_pairs={{0,24},{4,28},{8,16},{12,20},{16,8},{20,12},{24,0},{28,4},{1,25},{... | collective-permute-start | bytes 786440 | tf_op jit(solution)/shard_map/ppermute | solution.py:38
  47.9 0.0 collective-permute-start.11
  48.0 1.4 %collective-permute-start.10 = (bf16[4,128,256]{2,1,0:T(8,128)(2,1)S(1)}, bf16[4,128,256]{2,1,0:T(8,128)(2,1)S(1)}, u32[]{:S(2)}, u32[]{:S(2)}) collective-permute-start(bf16[4,128,256]{2,1,0:T(8,128)(2,1)S(1)} %pad_maximum_fusion.1), channel_id=1, source_target_pairs={{0,8},{4,12},{8,0},{12,4},{16,24},{20,28},{24,16},{28,20},{1,9},{5... | collective-permute-start | bytes 786440 | tf_op jit(solution)/shard_map/ppermute | solution.py:38
  49.4 1.5 %collective-permute-start.8 = (bf16[448,256]{1,0:T(8,128)(2,1)S(1)}, bf16[448,256]{1,0:T(8,128)(2,1)S(1)}, u32[]{:S(2)}, u32[]{:S(2)}) collective-permute-start(bf16[448,256]{1,0:T(8,128)(2,1)S(1)} %get-tuple-element.84), channel_id=1, source_target_pairs={{0,1},{1,0},{2,3},{3,2},{4,5},{5,4},{6,7},{7,6},{8,9},{9,8},{10,11... | collective-permute-start | bytes 688136 | tf_op jit(solution)/shard_map/ppermute | solution.py:38
  50.8 7.6 %collective-permute-start.7 = (bf16[448,256]{1,0:T(8,128)(2,1)S(1)}, bf16[448,256]{1,0:T(8,128)(2,1)S(1)}, u32[]{:S(2)}, u32[]{:S(2)}) collective-permute-start(bf16[448,256]{1,0:T(8,128)(2,1)S(1)} %get-tuple-element.85), channel_id=1, source_target_pairs={{0,2},{1,3},{2,0},{3,1},{4,6},{5,7},{6,4},{7,5},{8,10},{9,11},{10,... | collective-permute-start | bytes 688136 | tf_op jit(solution)/shard_map/ppermute | solution.py:38
  58.5 9.9 %collective-permute-done.7.refs_6_.refs_2_ = bf16[448,256]{1,0:T(8,128)(2,1)S(1)} collective-permute-done((bf16[448,256]{1,0:T(8,128)(2,1)S(1)}, bf16[448,256]{1,0:T(8,128)(2,1)S(1)}, u32[]{:S(2)}, u32[]{:S(2)}) %collective-permute-start.7) | collective-permute-done | bytes 229408 | tf_op jit(solution)/shard_map/ppermute | solution.py:38
  68.3 0.0 collective-permute-done.11
  68.3 0.0 collective-permute-done.10
  68.3 0.1 pad_maximum_fusion.refs_4_
  68.5 0.1 collective-permute-start.13
  68.6 2.7 %weight_partial.1 = (bf16[4,4,128,256]{3,2,1,0:T(8,128)(2,1)S(1)}, bf16[4,4,128,256]{3,2,1,0:T(8,128)(2,1)S(1)}) custom-call(s32[2]{0:T(128)S(1)} %pad_add_fusion.index, bf16[576,256]{1,0:T(8,128)(2,1)S(1)} %copy-done.1, bf16[576,256]{1,0:T(8,128)(2,1)S(1)} %collective-permute-done.2.refs_1_, bf16[576,256]{1,0:T(8,128)(2,1)S(1)} %collective-permute-done.3.refs_2_, ...), custom_call_target="tpu_custom_call" | custom-call | flops 939524096 | bytes 3932160 | tf_op jit(solution)/shard_map/weight_partial/pallas_call | solution.py:339
  71.2 0.0 collective-permute-done.13.refs_5_
  71.2 0.5 collective-permute-start.14
  71.8 2.3 %feature_rows.2 = bf16[3,448,256]{2,1,0:T(8,128)(2,1)S(1)} custom-call(s32[2]{0:T(128)S(1)} %pad_add_fusion.index, bf16[448,256]{1,0:T(8,128)(2,1)S(1)} %get-tuple-element.69.refs_4_.refs_0_, bf16[448,256]{1,0:T(8,128)(2,1)S(1)} %collective-permute-done.8.refs_5_.refs_1_, bf16[448,256]{1,0:T(8,128)(2,1)S(1)} %collective-permute-done.7.refs_6_.refs_2_, ...), custom_call_target="tpu_custom_call" | custom-call | flops 704643072 | bytes 3178496 | tf_op jit(solution)/shard_map/feature_rows/pallas_call | solution.py:387
  74.1 0.0 collective-permute-done.14
  74.1 0.4 convert_add_fusion
  74.5 0.1 slice_bitcast_fusion.3
  74.6 0.9 collective-permute-start.15
  75.4 0.2 collective-permute-start.17
  75.6 2.5 %collective-permute-start.16 = (bf16[4,128,256]{2,1,0:T(8,128)(2,1)S(1)}, bf16[4,128,256]{2,1,0:T(8,128)(2,1)S(1)}, u32[]{:S(2)}, u32[]{:S(2)}) collective-permute-start(bf16[4,128,256]{2,1,0:T(8,128)(2,1)S(1)} %get-tuple-element.82), channel_id=1, source_target_pairs={{0,16},{4,20},{8,24},{12,28},{16,0},{20,4},{24,8},{28,12},{1,17},{... | collective-permute-start | bytes 786440 | tf_op jit(solution)/shard_map/ppermute | solution.py:38
  78.2 1.7 %collective-permute-start.23 = (bf16[448,256]{1,0:T(8,128)(2,1)S(1)}, bf16[448,256]{1,0:T(8,128)(2,1)S(1)}, u32[]{:S(2)}, u32[]{:S(2)}) collective-permute-start(bf16[448,256]{1,0:T(8,128)(2,1)S(1)} %get-tuple-element.87), channel_id=1, source_target_pairs={{0,3},{1,2},{2,1},{3,0},{4,7},{5,6},{6,5},{7,4},{8,11},{9,10},{10,... | collective-permute-start | bytes 688136 | tf_op jit(solution)/shard_map/ppermute | solution.py:38
  79.9 3.9 %collective-permute-done.15 = bf16[4,128,256]{2,1,0:T(8,128)(2,1)S(1)} collective-permute-done((bf16[4,128,256]{2,1,0:T(8,128)(2,1)S(1)}, bf16[4,128,256]{2,1,0:T(8,128)(2,1)S(1)}, u32[]{:S(2)}, u32[]{:S(2)}) %collective-permute-start.15) | collective-permute-done | bytes 262176 | tf_op jit(solution)/shard_map/ppermute | solution.py:38
  83.8 4.3 %collective-permute-done.17 = bf16[4,128,256]{2,1,0:T(8,128)(2,1)S(1)} collective-permute-done((bf16[4,128,256]{2,1,0:T(8,128)(2,1)S(1)}, bf16[4,128,256]{2,1,0:T(8,128)(2,1)S(1)}, u32[]{:S(2)}, u32[]{:S(2)}) %collective-permute-start.17) | collective-permute-done | bytes 262176 | tf_op jit(solution)/shard_map/ppermute | solution.py:38
  88.1 1.9 %collective-permute-done.16 = bf16[4,128,256]{2,1,0:T(8,128)(2,1)S(1)} collective-permute-done((bf16[4,128,256]{2,1,0:T(8,128)(2,1)S(1)}, bf16[4,128,256]{2,1,0:T(8,128)(2,1)S(1)}, u32[]{:S(2)}, u32[]{:S(2)}) %collective-permute-start.16) | collective-permute-done | bytes 262176 | tf_op jit(solution)/shard_map/ppermute | solution.py:38
  90.0 0.2 fusion.10
  90.2 0.1 collective-permute-start.18
  90.2 1.7 %collective-permute-start.20 = (bf16[128,256]{1,0:T(8,128)(2,1)S(1)}, bf16[128,256]{1,0:T(8,128)(2,1)S(1)}, u32[]{:S(2)}, u32[]{:S(2)}) collective-permute-start(bf16[128,256]{1,0:T(8,128)(2,1)S(1)} %get-tuple-element.91), channel_id=1, source_target_pairs={{0,3},{1,2},{2,1},{3,0},{4,7},{5,6},{6,5},{7,4},{8,11},{9,10},{10,... | collective-permute-start | bytes 196616 | tf_op jit(solution)/shard_map/ppermute | solution.py:38
  91.9 4.3 %collective-permute-start.19 = (bf16[128,256]{1,0:T(8,128)(2,1)S(1)}, bf16[128,256]{1,0:T(8,128)(2,1)S(1)}, u32[]{:S(2)}, u32[]{:S(2)}) collective-permute-start(bf16[128,256]{1,0:T(8,128)(2,1)S(1)} %get-tuple-element.92), channel_id=1, source_target_pairs={{0,2},{1,3},{2,0},{3,1},{4,6},{5,7},{6,4},{7,5},{8,10},{9,11},{10,... | collective-permute-start | bytes 196616 | tf_op jit(solution)/shard_map/ppermute | solution.py:38
  96.2 1.0 feature_rows.3
  97.2 5.0 %collective-permute-done.22.refs_2_ = bf16[448,256]{1,0:T(8,128)(2,1)S(1)} collective-permute-done((bf16[448,256]{1,0:T(8,128)(2,1)S(1)}, bf16[448,256]{1,0:T(8,128)(2,1)S(1)}, u32[]{:S(2)}, u32[]{:S(2)}) %collective-permute-start.22) | collective-permute-done | bytes 229408 | tf_op jit(solution)/shard_map/ppermute | solution.py:38
  102.2 1.5 %laid_out.1 = bf16[1792,256]{1,0:T(8,128)(2,1)} custom-call(s32[2]{0:T(128)S(1)} %pad_add_fusion.index, bf16[448,256]{1,0:T(8,128)(2,1)S(1)} %bitcast.68, bf16[448,256]{1,0:T(8,128)(2,1)S(1)} %collective-permute-done.21.refs_1_, bf16[448,256]{1,0:T(8,128)(2,1)S(1)} %collective-permute-done.22.refs_2_, bf16[448,256]{1,0:T(8,128)(2,1)S(1)} %collective-permute-done.23.refs_3_), custom_call_target="tpu_custom_call" | custom-call | tf_op jit(solution)/shard_map/laid_out/pallas_call | solution.py:419
  103.8 0.1 collective-permute-done.19
  103.9 0.7 fusion.5
  (30 shorter events, 0.2 us)
Async XLA Ops:
  9.5 7.9 %collective-permute-start.1 = (bf16[2,128,256]{2,1,0:T(8,128)(2,1)S(1)}, bf16[2,128,256]{2,1,0:T(8,128)(2,1)S(1)}, u32[]{:S(2)}, u32[]{:S(2)}) collective-permute-start(bf16[2,128,256]{2,1,0:T(8,128)(2,1)S(1)} %get-tuple-element.95), channel_id=1, source_target_pairs={{4,8},{12,16},{20,24},{28,0},{8,4},{16,12},{24,20},{0,28},{5,9},{1... | collective-permute-start | bytes 393224 | tf_op jit(solution)/shard_map/ppermute | solution.py:33
  13.0 4.5 %collective-permute-start = (bf16[2,128,256]{2,1,0:T(8,128)(2,1)S(1)}, bf16[2,128,256]{2,1,0:T(8,128)(2,1)S(1)}, u32[]{:S(2)}, u32[]{:S(2)}) collective-permute-start(bf16[2,128,256]{2,1,0:T(8,128)(2,1)S(1)} %get-tuple-element.96), channel_id=1, source_target_pairs={{0,4},{4,0},{8,12},{12,8},{16,20},{20,16},{24,28},{28,24},{1,5},{5... | collective-permute-start | bytes 393224 | tf_op jit(solution)/shard_map/ppermute | solution.py:38
  13.0 16.5 %collective-permute-start.2 = (bf16[576,256]{1,0:T(8,128)(2,1)}, bf16[576,256]{1,0:T(8,128)(2,1)S(1)}, u32[]{:S(2)}, u32[]{:S(2)}) collective-permute-start(bf16[576,256]{1,0:T(8,128)(2,1)} %get-tuple-element.45), channel_id=1, source_target_pairs={{0,1},{1,0},{2,3},{3,2},{4,5},{5,4},{6,7},{7,6},{8,9},{9,8},{10,11... | collective-permute-start | bytes 884744 | tf_op jit(solution)/shard_map/ppermute | solution.py:38
  14.5 23.6 %collective-permute-start.3 = (bf16[576,256]{1,0:T(8,128)(2,1)}, bf16[576,256]{1,0:T(8,128)(2,1)S(1)}, u32[]{:S(2)}, u32[]{:S(2)}) collective-permute-start(bf16[576,256]{1,0:T(8,128)(2,1)} %get-tuple-element.46), channel_id=1, source_target_pairs={{0,2},{1,3},{2,0},{3,1},{4,6},{5,7},{6,4},{7,5},{8,10},{9,11},{10,... | collective-permute-start | bytes 884744 | tf_op jit(solution)/shard_map/ppermute | solution.py:38
  17.1 21.0 %collective-permute-start.4 = (bf16[576,256]{1,0:T(8,128)(2,1)}, bf16[576,256]{1,0:T(8,128)(2,1)S(1)}, u32[]{:S(2)}, u32[]{:S(2)}) collective-permute-start(bf16[576,256]{1,0:T(8,128)(2,1)} %get-tuple-element.47), channel_id=1, source_target_pairs={{0,3},{1,2},{2,1},{3,0},{4,7},{5,6},{6,5},{7,4},{8,11},{9,10},{10,... | collective-permute-start | bytes 884744 | tf_op jit(solution)/shard_map/ppermute | solution.py:38
  17.4 0.7 copy-start.3
  17.5 0.7 copy-start.4
  18.1 6.4 %copy-start.5 = (s32[112]{0:T(128)S(1)}, s32[112]{0:T(128)}, u32[]{:S(2)}) copy-start(s32[112]{0:T(128)} %shuffle.3) | copy-start | bytes 1348
  18.1 21.7 %copy-start = (bf16[14,128,256]{2,1,0:T(8,128)(2,1)S(1)}, bf16[14,128,256]{2,1,0:T(8,128)(2,1)}, u32[]{:S(2)}) copy-start(bf16[14,128,256]{2,1,0:T(8,128)(2,1)} %get-tuple-element.53.clean) | copy-start | bytes 2752516
  20.8 4.3 %copy-start.2 = (bf16[2,2,128,256]{3,2,1,0:T(8,128)(2,1)S(1)}, bf16[2,2,128,256]{3,2,1,0:T(8,128)(2,1)}, u32[]{:S(2)}) copy-start(bf16[2,2,128,256]{3,2,1,0:T(8,128)(2,1)} %get-tuple-element.54) | copy-start | bytes 786436
  20.8 19.0 %all-to-all-start = ((bf16[16,128,256]{2,1,0:T(8,128)(2,1)}), bf16[16,128,256]{2,1,0:T(8,128)(2,1)S(1)}, u32[]{:S(2)}, u32[]{:S(2)}) async-start(bf16[16,128,256]{2,1,0:T(8,128)(2,1)} %patch.1), calls=%async_computation | async-start | bytes 2097152 | tf_op jit(solution)/shard_map/all_to_all | solution.py:42
  25.1 14.7 %collective-permute-start.6 = (bf16[2,128,256]{2,1,0:T(8,128)(2,1)S(1)}, bf16[2,128,256]{2,1,0:T(8,128)(2,1)S(1)}, u32[]{:S(2)}, u32[]{:S(2)}) collective-permute-start(bf16[2,128,256]{2,1,0:T(8,128)(2,1)S(1)} %get-tuple-element.93), channel_id=1, source_target_pairs={{4,8},{12,16},{20,24},{8,4},{16,12},{24,20},{5,9},{13,17},{21,25},... | collective-permute-start | bytes 393224 | tf_op jit(solution)/shard_map/ppermute | solution.py:33
  25.8 14.0 %collective-permute-start.5 = (bf16[2,128,256]{2,1,0:T(8,128)(2,1)S(1)}, bf16[2,128,256]{2,1,0:T(8,128)(2,1)S(1)}, u32[]{:S(2)}, u32[]{:S(2)}) collective-permute-start(bf16[2,128,256]{2,1,0:T(8,128)(2,1)S(1)} %get-tuple-element.94), channel_id=1, source_target_pairs={{0,4},{4,0},{8,12},{12,8},{16,20},{20,16},{24,28},{28,24},{1,5},{5... | collective-permute-start | bytes 393224 | tf_op jit(solution)/shard_map/ppermute | solution.py:38
  39.8 5.1 %copy-start.1 = (bf16[576,256]{1,0:T(8,128)(2,1)S(1)}, bf16[576,256]{1,0:T(8,128)(2,1)}, u32[]{:S(2)}) copy-start(bf16[576,256]{1,0:T(8,128)(2,1)} %get-tuple-element.48.refs_0_) | copy-start | bytes 884740
  41.0 9.8 %collective-permute-start.9 = (bf16[448,256]{1,0:T(8,128)(2,1)S(1)}, bf16[448,256]{1,0:T(8,128)(2,1)S(1)}, u32[]{:S(2)}, u32[]{:S(2)}) collective-permute-start(bf16[448,256]{1,0:T(8,128)(2,1)S(1)} %get-tuple-element.83), channel_id=1, source_target_pairs={{0,3},{1,2},{2,1},{3,0},{4,7},{5,6},{6,5},{7,4},{8,11},{9,10},{10,... | collective-permute-start | bytes 688136 | tf_op jit(solution)/shard_map/ppermute | solution.py:38
  45.0 23.4 %collective-permute-start.12 = (bf16[4,128,256]{2,1,0:T(8,128)(2,1)S(1)}, bf16[4,128,256]{2,1,0:T(8,128)(2,1)S(1)}, u32[]{:S(2)}, u32[]{:S(2)}) collective-permute-start(bf16[4,128,256]{2,1,0:T(8,128)(2,1)S(1)} %pad_maximum_fusion.1), channel_id=1, source_target_pairs={{0,24},{4,28},{8,16},{12,20},{16,8},{20,12},{24,0},{28,4},{1,25},{... | collective-permute-start | bytes 786440 | tf_op jit(solution)/shard_map/ppermute | solution.py:38
  47.9 20.4 %collective-permute-start.11 = (bf16[4,128,256]{2,1,0:T(8,128)(2,1)S(1)}, bf16[4,128,256]{2,1,0:T(8,128)(2,1)S(1)}, u32[]{:S(2)}, u32[]{:S(2)}) collective-permute-start(bf16[4,128,256]{2,1,0:T(8,128)(2,1)S(1)} %pad_maximum_fusion.1), channel_id=1, source_target_pairs={{0,16},{4,20},{8,24},{12,28},{16,0},{20,4},{24,8},{28,12},{1,17},{... | collective-permute-start | bytes 786440 | tf_op jit(solution)/shard_map/ppermute | solution.py:38
  48.0 20.4 %collective-permute-start.10 = (bf16[4,128,256]{2,1,0:T(8,128)(2,1)S(1)}, bf16[4,128,256]{2,1,0:T(8,128)(2,1)S(1)}, u32[]{:S(2)}, u32[]{:S(2)}) collective-permute-start(bf16[4,128,256]{2,1,0:T(8,128)(2,1)S(1)} %pad_maximum_fusion.1), channel_id=1, source_target_pairs={{0,8},{4,12},{8,0},{12,4},{16,24},{20,28},{24,16},{28,20},{1,9},{5... | collective-permute-start | bytes 786440 | tf_op jit(solution)/shard_map/ppermute | solution.py:38
  49.4 9.1 %collective-permute-start.8 = (bf16[448,256]{1,0:T(8,128)(2,1)S(1)}, bf16[448,256]{1,0:T(8,128)(2,1)S(1)}, u32[]{:S(2)}, u32[]{:S(2)}) collective-permute-start(bf16[448,256]{1,0:T(8,128)(2,1)S(1)} %get-tuple-element.84), channel_id=1, source_target_pairs={{0,1},{1,0},{2,3},{3,2},{4,5},{5,4},{6,7},{7,6},{8,9},{9,8},{10,11... | collective-permute-start | bytes 688136 | tf_op jit(solution)/shard_map/ppermute | solution.py:38
  50.8 17.5 %collective-permute-start.7 = (bf16[448,256]{1,0:T(8,128)(2,1)S(1)}, bf16[448,256]{1,0:T(8,128)(2,1)S(1)}, u32[]{:S(2)}, u32[]{:S(2)}) collective-permute-start(bf16[448,256]{1,0:T(8,128)(2,1)S(1)} %get-tuple-element.85), channel_id=1, source_target_pairs={{0,2},{1,3},{2,0},{3,1},{4,6},{5,7},{6,4},{7,5},{8,10},{9,11},{10,... | collective-permute-start | bytes 688136 | tf_op jit(solution)/shard_map/ppermute | solution.py:38
  68.5 2.7 %collective-permute-start.13 = (bf16[4,4,128,256]{3,2,1,0:T(8,128)(2,1)S(1)}, bf16[4,4,128,256]{3,2,1,0:T(8,128)(2,1)S(1)}, u32[]{:S(2)}, u32[]{:S(2)}) collective-permute-start(bf16[4,4,128,256]{3,2,1,0:T(8,128)(2,1)S(1)} %pad_maximum_fusion.refs_4_), channel_id=1, source_target_pairs={{0,4},{4,0},{8,12},{12,8},{16,20},{20,16},{24,28},{28,24},{1,5},{5... | collective-permute-start | bytes 3145736 | tf_op jit(solution)/shard_map/ppermute | solution.py:38
  71.2 2.9 %collective-permute-start.14 = (bf16[4,4,128,256]{3,2,1,0:T(8,128)(2,1)S(1)}, bf16[4,4,128,256]{3,2,1,0:T(8,128)(2,1)S(1)}, u32[]{:S(2)}, u32[]{:S(2)}) collective-permute-start(bf16[4,4,128,256]{3,2,1,0:T(8,128)(2,1)S(1)} %get-tuple-element.66), channel_id=1, source_target_pairs={{0,4},{4,0},{8,12},{12,8},{16,20},{20,16},{24,28},{28,24},{1,5},{5... | collective-permute-start | bytes 3145736 | tf_op jit(solution)/shard_map/ppermute | solution.py:38
  74.6 9.2 %collective-permute-start.15 = (bf16[4,128,256]{2,1,0:T(8,128)(2,1)S(1)}, bf16[4,128,256]{2,1,0:T(8,128)(2,1)S(1)}, u32[]{:S(2)}, u32[]{:S(2)}) collective-permute-start(bf16[4,128,256]{2,1,0:T(8,128)(2,1)S(1)} %get-tuple-element.80), channel_id=1, source_target_pairs={{0,8},{4,12},{8,0},{12,4},{16,24},{20,28},{24,16},{28,20},{1,9},{5... | collective-permute-start | bytes 786440 | tf_op jit(solution)/shard_map/ppermute | solution.py:38
  75.4 12.6 %collective-permute-start.17 = (bf16[4,128,256]{2,1,0:T(8,128)(2,1)S(1)}, bf16[4,128,256]{2,1,0:T(8,128)(2,1)S(1)}, u32[]{:S(2)}, u32[]{:S(2)}) collective-permute-start(bf16[4,128,256]{2,1,0:T(8,128)(2,1)S(1)} %get-tuple-element.81), channel_id=1, source_target_pairs={{0,24},{4,28},{8,16},{12,20},{16,8},{20,12},{24,0},{28,4},{1,25},{... | collective-permute-start | bytes 786440 | tf_op jit(solution)/shard_map/ppermute | solution.py:38
  75.6 14.3 %collective-permute-start.16 = (bf16[4,128,256]{2,1,0:T(8,128)(2,1)S(1)}, bf16[4,128,256]{2,1,0:T(8,128)(2,1)S(1)}, u32[]{:S(2)}, u32[]{:S(2)}) collective-permute-start(bf16[4,128,256]{2,1,0:T(8,128)(2,1)S(1)} %get-tuple-element.82), channel_id=1, source_target_pairs={{0,16},{4,20},{8,24},{12,28},{16,0},{20,4},{24,8},{28,12},{1,17},{... | collective-permute-start | bytes 786440 | tf_op jit(solution)/shard_map/ppermute | solution.py:38
  78.2 13.7 %collective-permute-start.23 = (bf16[448,256]{1,0:T(8,128)(2,1)S(1)}, bf16[448,256]{1,0:T(8,128)(2,1)S(1)}, u32[]{:S(2)}, u32[]{:S(2)}) collective-permute-start(bf16[448,256]{1,0:T(8,128)(2,1)S(1)} %get-tuple-element.87), channel_id=1, source_target_pairs={{0,3},{1,2},{2,1},{3,0},{4,7},{5,6},{6,5},{7,4},{8,11},{9,10},{10,... | collective-permute-start | bytes 688136 | tf_op jit(solution)/shard_map/ppermute | solution.py:38
  79.9 22.4 %collective-permute-start.22 = (bf16[448,256]{1,0:T(8,128)(2,1)S(1)}, bf16[448,256]{1,0:T(8,128)(2,1)S(1)}, u32[]{:S(2)}, u32[]{:S(2)}) collective-permute-start(bf16[448,256]{1,0:T(8,128)(2,1)S(1)} %get-tuple-element.88), channel_id=1, source_target_pairs={{0,2},{1,3},{2,0},{3,1},{4,6},{5,7},{6,4},{7,5},{8,10},{9,11},{10,... | collective-permute-start | bytes 688136 | tf_op jit(solution)/shard_map/ppermute | solution.py:38
  83.8 18.5 %collective-permute-start.21 = (bf16[448,256]{1,0:T(8,128)(2,1)S(1)}, bf16[448,256]{1,0:T(8,128)(2,1)S(1)}, u32[]{:S(2)}, u32[]{:S(2)}) collective-permute-start(bf16[448,256]{1,0:T(8,128)(2,1)S(1)} %get-tuple-element.89), channel_id=1, source_target_pairs={{0,1},{1,0},{2,3},{3,2},{4,5},{5,4},{6,7},{7,6},{8,9},{9,8},{10,11... | collective-permute-start | bytes 688136 | tf_op jit(solution)/shard_map/ppermute | solution.py:38
  90.2 13.6 %collective-permute-start.18 = (bf16[128,256]{1,0:T(8,128)(2,1)S(1)}, bf16[128,256]{1,0:T(8,128)(2,1)S(1)}, u32[]{:S(2)}, u32[]{:S(2)}) collective-permute-start(bf16[128,256]{1,0:T(8,128)(2,1)S(1)} %get-tuple-element.90), channel_id=1, source_target_pairs={{0,1},{1,0},{2,3},{3,2},{4,5},{5,4},{6,7},{7,6},{8,9},{9,8},{10,11... | collective-permute-start | bytes 196616 | tf_op jit(solution)/shard_map/ppermute | solution.py:38
  90.2 13.5 %collective-permute-start.20 = (bf16[128,256]{1,0:T(8,128)(2,1)S(1)}, bf16[128,256]{1,0:T(8,128)(2,1)S(1)}, u32[]{:S(2)}, u32[]{:S(2)}) collective-permute-start(bf16[128,256]{1,0:T(8,128)(2,1)S(1)} %get-tuple-element.91), channel_id=1, source_target_pairs={{0,3},{1,2},{2,1},{3,0},{4,7},{5,6},{6,5},{7,4},{8,11},{9,10},{10,... | collective-permute-start | bytes 196616 | tf_op jit(solution)/shard_map/ppermute | solution.py:38
  91.9 12.0 %collective-permute-start.19 = (bf16[128,256]{1,0:T(8,128)(2,1)S(1)}, bf16[128,256]{1,0:T(8,128)(2,1)S(1)}, u32[]{:S(2)}, u32[]{:S(2)}) collective-permute-start(bf16[128,256]{1,0:T(8,128)(2,1)S(1)} %get-tuple-element.92), channel_id=1, source_target_pairs={{0,2},{1,3},{2,0},{3,1},{4,6},{5,7},{6,4},{7,5},{8,10},{9,11},{10,... | collective-permute-start | bytes 196616 | tf_op jit(solution)/shard_map/ppermute | solution.py:38

commit v21 on v20

--- a/solution.py
+++ b/solution.py
@@ -477,7 +477,7 @@
         (shuffle_from, outgoing, clean, clean_side)
     )
     clean_pair = swapped(clean_side[0], "node", 1)
-    clean_beside = swapped_beside(clean_side[1], "node", False)
+    clean_beside = swapped_beside(clean_side[1], "node", True)
     landing = landing_blocks(shuffle_from, me, blocks, devs, slots)
     incoming = exchanged(outgoing, "node")
     incoming, packed = lax.optimization_barrier((incoming, packed))

time: 105 us -> 105 us (level)
  starting transfers between devices: 44.7 us -> 37 us
  waiting for transfers between devices: 35.5 us -> 43.2 us
    ppermute x22, starting transfers between devices: 37 us -> 27.3 us  [swapped(): return lax.ppermute(value, axis, [(i, i ^ by) for i in range(size)])]
    ppermute x22, waiting for transfers between devices: 33.9 us -> 39.2 us  [swapped(): return lax.ppermute(value, axis, [(i, i ^ by) for i in range(size)])]
    ppermute x2, starting transfers between devices: 4.08 us -> 6.07 us  [swapped_beside(): return lax.ppermute(value, axis, pairs + [(j, i) for i, j in pairs])]
    ppermute x2, waiting for transfers between devices: 0.01 us -> 1.86 us  [swapped_beside(): return lax.ppermute(value, axis, pairs + [(j, i) for i, j in pairs])]
  transfers between devices with their start and end apart: 25 -> 25, of which waited for: 8 -> 10; matrix products, arithmetic and copies ran while one was open for 1% -> 1% of each run, Pallas kernels for 10% -> 10%
where the time goes in v21:
time: 105 us
  waiting for transfers between devices  43.2 us (41%)
  starting transfers between devices  37 us (35%)
  Pallas kernels  19.1 us (18%)
  local copies, waits for them, and re-layouts  2.3 us (2%)
  other arithmetic  1.99 us (2%)
    ppermute x22, waiting for transfers between devices, swapped(): return lax.ppermute(value, axis, [(i, i ^ by) for i in range(size)])  39.2 us
    ppermute x22, starting transfers between devices, swapped(): return lax.ppermute(value, axis, [(i, i ^ by) for i in range(size)])  27.3 us
    pallas_call x1, Pallas kernels, aggregate(): pl.pallas_call(functools.partial(aggregate_kernel, reach, groups, send_sl...  7.9 us
    ppermute x2, starting transfers between devices, swapped_beside(): return lax.ppermute(value, axis, pairs + [(j, i) for i, j in pairs])  6.07 us
    all_to_all x1, starting transfers between devices, exchanged(): return lax.all_to_all(value, axis, split_axis=0, concat_axis=0, tiled=True)  3.7 us
    pallas_call x2, Pallas kernels, feature_rows(): pl.pallas_call(functools.partial(feature_kernel, first), in_specs=[IN_SME...  3.34 us
    pallas_call x1, Pallas kernels, weight_partial(): pl.pallas_call(functools.partial(weight_kernel, devs), in_specs=[IN_SMEM]...  2.65 us
    pallas_call x1, Pallas kernels, patch(): pl.pallas_call(functools.partial(patch_kernel, reach, blocks, slots), in_...  2.64 us
  transfers between devices with their start and end apart: 25, of which 10 were waited for; matrix products, arithmetic and copies ran while one was open for 1% of the time, Pallas kernels for 10%

profile of v21, /device:TPU:0, one launch (start us, length us, event | category | flops | bytes accessed | tf_op | source)
XLA Modules:
  0.0 104.5 jit_solution(1244315237184141118)
XLA Ops:
  0.6 7.9 %aggregate.1 = (bf16[14,128,256]{2,1,0:T(8,128)(2,1)}, bf16[16,128,256]{2,1,0:T(8,128)(2,1)}, bf16[2,2,128,256]{3,2,1,0:T(8,128)(2,1)}, bf16[2,2,128,256]{3,2,1,...) custom-call(s32[112]{0:T(128)} %shuffle.3, ...), custom_call_target="tpu_custom_call" | custom-call | flops 1174405120 | bytes 7798784 | tf_op jit(solution)/shard_map/aggregate/pallas_call | solution.py:186
  8.5 1.0 slice_bitcast_fusion.14
  9.5 3.4 %collective-permute-start.1 = (bf16[2,128,256]{2,1,0:T(8,128)(2,1)S(1)}, bf16[2,128,256]{2,1,0:T(8,128)(2,1)S(1)}, u32[]{:S(2)}, u32[]{:S(2)}) collective-permute-start(bf16[2,128,256]{2,1,0:T(8,128)(2,1)S(1)} %get-tuple-element.95), channel_id=1, source_target_pairs={{4,8},{12,16},{20,24},{28,0},{8,4},{16,12},{24,20},{0,28},{5,9},{1... | collective-permute-start | bytes 393224 | tf_op jit(solution)/shard_map/ppermute | solution.py:33
  13.0 1.6 %collective-permute-start.2 = (bf16[576,256]{1,0:T(8,128)(2,1)}, bf16[576,256]{1,0:T(8,128)(2,1)S(1)}, u32[]{:S(2)}, u32[]{:S(2)}) collective-permute-start(bf16[576,256]{1,0:T(8,128)(2,1)} %get-tuple-element.45), channel_id=1, source_target_pairs={{0,1},{1,0},{2,3},{3,2},{4,5},{5,4},{6,7},{7,6},{8,9},{9,8},{10,11... | collective-permute-start | bytes 884744 | tf_op jit(solution)/shard_map/ppermute | solution.py:38
  14.5 2.6 %collective-permute-start.3 = (bf16[576,256]{1,0:T(8,128)(2,1)}, bf16[576,256]{1,0:T(8,128)(2,1)S(1)}, u32[]{:S(2)}, u32[]{:S(2)}) collective-permute-start(bf16[576,256]{1,0:T(8,128)(2,1)} %get-tuple-element.46), channel_id=1, source_target_pairs={{0,2},{1,3},{2,0},{3,1},{4,6},{5,7},{6,4},{7,5},{8,10},{9,11},{10,... | collective-permute-start | bytes 884744 | tf_op jit(solution)/shard_map/ppermute | solution.py:38
  17.1 0.2 collective-permute-start.4
  17.3 0.1 pad_add_fusion.index
  17.4 0.0 copy-start.4
  17.5 0.6 copy-done.3
  18.1 0.0 copy-done.4
  18.1 2.6 %patch.1 = bf16[16,128,256]{2,1,0:T(8,128)(2,1)} custom-call(s32[112]{0:T(128)} %shuffle.3, bf16[16,128,256]{2,1,0:T(8,128)(2,1)} %get-tuple-element.39.outgoing, bf16[2,128,256]{2,1,0:T(8,128)(2,1)} %copy-done.4, bf16[2,128,256]{2,1,0:T(8,128)(2,1)} %copy-done.3), custom_call_target="tpu_custom_call", output_to_operand_aliasing={{}: (1, {})} | custom-call | tf_op jit(solution)/shard_map/patch/pallas_call | solution.py:250
  20.8 3.7 %all-to-all-start = ((bf16[16,128,256]{2,1,0:T(8,128)(2,1)}), bf16[16,128,256]{2,1,0:T(8,128)(2,1)S(1)}, u32[]{:S(2)}, u32[]{:S(2)}) async-start(bf16[16,128,256]{2,1,0:T(8,128)(2,1)} %patch.1), calls=%async_computation | async-start | bytes 2097152 | tf_op jit(solution)/shard_map/all_to_all | solution.py:42
  24.5 0.1 eq.30
  24.6 0.1 add.45
  24.7 0.3 convert_reduce_fusion
  25.0 0.1 copy.14
  25.2 2.7 %collective-permute-start.6 = (bf16[2,128,256]{2,1,0:T(8,128)(2,1)S(1)}, bf16[2,128,256]{2,1,0:T(8,128)(2,1)S(1)}, u32[]{:S(2)}, u32[]{:S(2)}) collective-permute-start(bf16[2,128,256]{2,1,0:T(8,128)(2,1)S(1)} %get-tuple-element.93), channel_id=1, source_target_pairs={{4,8},{12,16},{20,24},{28,0},{8,4},{16,12},{24,20},{0,28},{5,9},{1... | collective-permute-start | bytes 393224 | tf_op jit(solution)/shard_map/ppermute | solution.py:33
  27.8 0.1 select_reduce_fusion
  28.0 0.1 copy.15
  28.1 0.1 sub.13.landing
  28.1 0.4 collective-permute-done.2.refs_1_
  28.5 9.7 %collective-permute-done.3.refs_2_ = bf16[576,256]{1,0:T(8,128)(2,1)S(1)} collective-permute-done((bf16[576,256]{1,0:T(8,128)(2,1)}, bf16[576,256]{1,0:T(8,128)(2,1)S(1)}, u32[]{:S(2)}, u32[]{:S(2)}) %collective-permute-start.3) | collective-permute-done | bytes 294944 | tf_op jit(solution)/shard_map/ppermute | solution.py:38
  38.2 2.1 %all-to-all-done.incoming = bf16[16,128,256]{2,1,0:T(8,128)(2,1)S(1)} async-done(((bf16[16,128,256]{2,1,0:T(8,128)(2,1)}), bf16[16,128,256]{2,1,0:T(8,128)(2,1)S(1)}, u32[]{:S(2)}, u32[]{:S(2)}) %all-to-all-start) | async-done | bytes 1048608 | tf_op jit(solution)/shard_map/all_to_all | solution.py:42
  40.3 1.9 %collective-permute-done.6.beside = bf16[2,128,256]{2,1,0:T(8,128)(2,1)S(1)} collective-permute-done((bf16[2,128,256]{2,1,0:T(8,128)(2,1)S(1)}, bf16[2,128,256]{2,1,0:T(8,128)(2,1)S(1)}, u32[]{:S(2)}, u32[]{:S(2)}) %collective-permute-start.6) | collective-permute-done | bytes 131104 | tf_op jit(solution)/shard_map/ppermute | solution.py:33
  42.2 0.0 collective-permute-done.5.pair
  42.2 1.1 %merge.1 = bf16[4,448,256]{2,1,0:T(8,128)(2,1)S(1)} custom-call(s32[2]{0:T(128)S(1)} %pad_add_fusion.index, s32[16]{0:T(128)S(1)} %sub.13.landing, bf16[14,128,256]{2,1,0:T(8,128)(2,1)S(1)} %copy-done, bf16[2,128,256]{2,1,0:T(8,128)(2,1)S(1)} %collective-permute-done.5.pair, bf16[2,128,256]{2,1,0:T(8,128)(2,1)S(1)} %collective-permute-done.6.beside, ...), custom_call_target="tpu_custom_call" | custom-call | tf_op jit(solution)/shard_map/merge/pallas_call | solution.py:298
  43.3 0.1 slice_bitcast_fusion.4
  43.3 3.9 %collective-permute-start.9 = (bf16[448,256]{1,0:T(8,128)(2,1)S(1)}, bf16[448,256]{1,0:T(8,128)(2,1)S(1)}, u32[]{:S(2)}, u32[]{:S(2)}) collective-permute-start(bf16[448,256]{1,0:T(8,128)(2,1)S(1)} %get-tuple-element.83), channel_id=1, source_target_pairs={{0,3},{1,2},{2,1},{3,0},{4,7},{5,6},{6,5},{7,4},{8,11},{9,10},{10,... | collective-permute-start | bytes 688136 | tf_op jit(solution)/shard_map/ppermute | solution.py:38
  47.3 0.7 collective-permute-start.12
  47.9 0.6 collective-permute-start.11
  48.5 2.3 %collective-permute-start.10 = (bf16[4,128,256]{2,1,0:T(8,128)(2,1)S(1)}, bf16[4,128,256]{2,1,0:T(8,128)(2,1)S(1)}, u32[]{:S(2)}, u32[]{:S(2)}) collective-permute-start(bf16[4,128,256]{2,1,0:T(8,128)(2,1)S(1)} %pad_maximum_fusion.1), channel_id=1, source_target_pairs={{0,8},{4,12},{8,0},{12,4},{16,24},{20,28},{24,16},{28,20},{1,9},{5... | collective-permute-start | bytes 786440 | tf_op jit(solution)/shard_map/ppermute | solution.py:38
  50.8 0.0 collective-permute-start.8
  50.8 2.8 %collective-permute-done.9.refs_7_.refs_3_ = bf16[448,256]{1,0:T(8,128)(2,1)S(1)} collective-permute-done((bf16[448,256]{1,0:T(8,128)(2,1)S(1)}, bf16[448,256]{1,0:T(8,128)(2,1)S(1)}, u32[]{:S(2)}, u32[]{:S(2)}) %collective-permute-start.9) | collective-permute-done | bytes 229408 | tf_op jit(solution)/shard_map/ppermute | solution.py:38
  53.7 4.8 %collective-permute-start.7 = (bf16[448,256]{1,0:T(8,128)(2,1)S(1)}, bf16[448,256]{1,0:T(8,128)(2,1)S(1)}, u32[]{:S(2)}, u32[]{:S(2)}) collective-permute-start(bf16[448,256]{1,0:T(8,128)(2,1)S(1)} %get-tuple-element.85), channel_id=1, source_target_pairs={{0,2},{1,3},{2,0},{3,1},{4,6},{5,7},{6,4},{7,5},{8,10},{9,11},{10,... | collective-permute-start | bytes 688136 | tf_op jit(solution)/shard_map/ppermute | solution.py:38
  58.4 9.2 %collective-permute-done.7.refs_6_.refs_2_ = bf16[448,256]{1,0:T(8,128)(2,1)S(1)} collective-permute-done((bf16[448,256]{1,0:T(8,128)(2,1)S(1)}, bf16[448,256]{1,0:T(8,128)(2,1)S(1)}, u32[]{:S(2)}, u32[]{:S(2)}) %collective-permute-start.7) | collective-permute-done | bytes 229408 | tf_op jit(solution)/shard_map/ppermute | solution.py:38
  67.6 0.0 collective-permute-done.12
  67.6 0.0 collective-permute-done.11
  67.6 0.0 collective-permute-done.10
  67.6 0.1 pad_maximum_fusion.refs_4_
  67.8 0.1 collective-permute-start.13
  67.8 2.7 %weight_partial.1 = (bf16[4,4,128,256]{3,2,1,0:T(8,128)(2,1)S(1)}, bf16[4,4,128,256]{3,2,1,0:T(8,128)(2,1)S(1)}) custom-call(s32[2]{0:T(128)S(1)} %pad_add_fusion.index, bf16[576,256]{1,0:T(8,128)(2,1)S(1)} %copy-done.1, bf16[576,256]{1,0:T(8,128)(2,1)S(1)} %collective-permute-done.2.refs_1_, bf16[576,256]{1,0:T(8,128)(2,1)S(1)} %collective-permute-done.3.refs_2_, ...), custom_call_target="tpu_custom_call" | custom-call | flops 939524096 | bytes 3932160 | tf_op jit(solution)/shard_map/weight_partial/pallas_call | solution.py:339
  70.5 0.5 collective-permute-start.14
  71.1 2.3 %feature_rows.2 = bf16[3,448,256]{2,1,0:T(8,128)(2,1)S(1)} custom-call(s32[2]{0:T(128)S(1)} %pad_add_fusion.index, bf16[448,256]{1,0:T(8,128)(2,1)S(1)} %get-tuple-element.69.refs_4_.refs_0_, bf16[448,256]{1,0:T(8,128)(2,1)S(1)} %collective-permute-done.8.refs_5_.refs_1_, bf16[448,256]{1,0:T(8,128)(2,1)S(1)} %collective-permute-done.7.refs_6_.refs_2_, ...), custom_call_target="tpu_custom_call" | custom-call | flops 704643072 | bytes 3178496 | tf_op jit(solution)/shard_map/feature_rows/pallas_call | solution.py:387
  73.4 0.0 collective-permute-done.14
  73.4 0.4 convert_add_fusion
  73.8 0.1 slice_bitcast_fusion.3
  73.9 1.5 %collective-permute-start.15 = (bf16[4,128,256]{2,1,0:T(8,128)(2,1)S(1)}, bf16[4,128,256]{2,1,0:T(8,128)(2,1)S(1)}, u32[]{:S(2)}, u32[]{:S(2)}) collective-permute-start(bf16[4,128,256]{2,1,0:T(8,128)(2,1)S(1)} %get-tuple-element.80), channel_id=1, source_target_pairs={{0,8},{4,12},{8,0},{12,4},{16,24},{20,28},{24,16},{28,20},{1,9},{5... | collective-permute-start | bytes 786440 | tf_op jit(solution)/shard_map/ppermute | solution.py:38
  75.4 2.0 %collective-permute-start.17 = (bf16[4,128,256]{2,1,0:T(8,128)(2,1)S(1)}, bf16[4,128,256]{2,1,0:T(8,128)(2,1)S(1)}, u32[]{:S(2)}, u32[]{:S(2)}) collective-permute-start(bf16[4,128,256]{2,1,0:T(8,128)(2,1)S(1)} %get-tuple-element.81), channel_id=1, source_target_pairs={{0,24},{4,28},{8,16},{12,20},{16,8},{20,12},{24,0},{28,4},{1,25},{... | collective-permute-start | bytes 786440 | tf_op jit(solution)/shard_map/ppermute | solution.py:38
  77.4 0.0 collective-permute-start.16
  77.5 2.2 %collective-permute-start.23 = (bf16[448,256]{1,0:T(8,128)(2,1)S(1)}, bf16[448,256]{1,0:T(8,128)(2,1)S(1)}, u32[]{:S(2)}, u32[]{:S(2)}) collective-permute-start(bf16[448,256]{1,0:T(8,128)(2,1)S(1)} %get-tuple-element.87), channel_id=1, source_target_pairs={{0,3},{1,2},{2,1},{3,0},{4,7},{5,6},{6,5},{7,4},{8,11},{9,10},{10,... | collective-permute-start | bytes 688136 | tf_op jit(solution)/shard_map/ppermute | solution.py:38
  79.7 3.4 %collective-permute-done.15 = bf16[4,128,256]{2,1,0:T(8,128)(2,1)S(1)} collective-permute-done((bf16[4,128,256]{2,1,0:T(8,128)(2,1)S(1)}, bf16[4,128,256]{2,1,0:T(8,128)(2,1)S(1)}, u32[]{:S(2)}, u32[]{:S(2)}) %collective-permute-start.15) | collective-permute-done | bytes 262176 | tf_op jit(solution)/shard_map/ppermute | solution.py:38
  83.1 0.0 collective-permute-start.21
  83.1 6.6 %collective-permute-done.17 = bf16[4,128,256]{2,1,0:T(8,128)(2,1)S(1)} collective-permute-done((bf16[4,128,256]{2,1,0:T(8,128)(2,1)S(1)}, bf16[4,128,256]{2,1,0:T(8,128)(2,1)S(1)}, u32[]{:S(2)}, u32[]{:S(2)}) %collective-permute-start.17) | collective-permute-done | bytes 262176 | tf_op jit(solution)/shard_map/ppermute | solution.py:38
  89.6 1.4 %collective-permute-done.16 = bf16[4,128,256]{2,1,0:T(8,128)(2,1)S(1)} collective-permute-done((bf16[4,128,256]{2,1,0:T(8,128)(2,1)S(1)}, bf16[4,128,256]{2,1,0:T(8,128)(2,1)S(1)}, u32[]{:S(2)}, u32[]{:S(2)}) %collective-permute-start.16) | collective-permute-done | bytes 262176 | tf_op jit(solution)/shard_map/ppermute | solution.py:38
  91.0 0.2 fusion.10
  91.2 0.1 collective-permute-start.18
  91.3 1.7 %collective-permute-start.20 = (bf16[128,256]{1,0:T(8,128)(2,1)S(1)}, bf16[128,256]{1,0:T(8,128)(2,1)S(1)}, u32[]{:S(2)}, u32[]{:S(2)}) collective-permute-start(bf16[128,256]{1,0:T(8,128)(2,1)S(1)} %get-tuple-element.91), channel_id=1, source_target_pairs={{0,3},{1,2},{2,1},{3,0},{4,7},{5,6},{6,5},{7,4},{8,11},{9,10},{10,... | collective-permute-start | bytes 196616 | tf_op jit(solution)/shard_map/ppermute | solution.py:38
  93.0 0.0 collective-permute-done.23.refs_3_
  93.0 2.4 %collective-permute-start.19 = (bf16[128,256]{1,0:T(8,128)(2,1)S(1)}, bf16[128,256]{1,0:T(8,128)(2,1)S(1)}, u32[]{:S(2)}, u32[]{:S(2)}) collective-permute-start(bf16[128,256]{1,0:T(8,128)(2,1)S(1)} %get-tuple-element.92), channel_id=1, source_target_pairs={{0,2},{1,3},{2,0},{3,1},{4,6},{5,7},{6,4},{7,5},{8,10},{9,11},{10,... | collective-permute-start | bytes 196616 | tf_op jit(solution)/shard_map/ppermute | solution.py:38
  95.4 1.0 feature_rows.3
  96.4 5.9 %collective-permute-done.22.refs_2_ = bf16[448,256]{1,0:T(8,128)(2,1)S(1)} collective-permute-done((bf16[448,256]{1,0:T(8,128)(2,1)S(1)}, bf16[448,256]{1,0:T(8,128)(2,1)S(1)}, u32[]{:S(2)}, u32[]{:S(2)}) %collective-permute-start.22) | collective-permute-done | bytes 229408 | tf_op jit(solution)/shard_map/ppermute | solution.py:38
  102.3 0.0 collective-permute-done.21.refs_1_
  102.3 1.5 %laid_out.1 = bf16[1792,256]{1,0:T(8,128)(2,1)} custom-call(s32[2]{0:T(128)S(1)} %pad_add_fusion.index, bf16[448,256]{1,0:T(8,128)(2,1)S(1)} %bitcast.68, bf16[448,256]{1,0:T(8,128)(2,1)S(1)} %collective-permute-done.21.refs_1_, bf16[448,256]{1,0:T(8,128)(2,1)S(1)} %collective-permute-done.22.refs_2_, bf16[448,256]{1,0:T(8,128)(2,1)S(1)} %collective-permute-done.23.refs_3_), custom_call_target="tpu_custom_call" | custom-call | tf_op jit(solution)/shard_map/laid_out/pallas_call | solution.py:419
  103.8 0.7 fusion.5
  (30 shorter events, 0.2 us)
Async XLA Ops:
  9.5 7.9 %collective-permute-start.1 = (bf16[2,128,256]{2,1,0:T(8,128)(2,1)S(1)}, bf16[2,128,256]{2,1,0:T(8,128)(2,1)S(1)}, u32[]{:S(2)}, u32[]{:S(2)}) collective-permute-start(bf16[2,128,256]{2,1,0:T(8,128)(2,1)S(1)} %get-tuple-element.95), channel_id=1, source_target_pairs={{4,8},{12,16},{20,24},{28,0},{8,4},{16,12},{24,20},{0,28},{5,9},{1... | collective-permute-start | bytes 393224 | tf_op jit(solution)/shard_map/ppermute | solution.py:33
  12.9 4.5 %collective-permute-start = (bf16[2,128,256]{2,1,0:T(8,128)(2,1)S(1)}, bf16[2,128,256]{2,1,0:T(8,128)(2,1)S(1)}, u32[]{:S(2)}, u32[]{:S(2)}) collective-permute-start(bf16[2,128,256]{2,1,0:T(8,128)(2,1)S(1)} %get-tuple-element.96), channel_id=1, source_target_pairs={{0,4},{4,0},{8,12},{12,8},{16,20},{20,16},{24,28},{28,24},{1,5},{5... | collective-permute-start | bytes 393224 | tf_op jit(solution)/shard_map/ppermute | solution.py:38
  13.0 15.5 %collective-permute-start.2 = (bf16[576,256]{1,0:T(8,128)(2,1)}, bf16[576,256]{1,0:T(8,128)(2,1)S(1)}, u32[]{:S(2)}, u32[]{:S(2)}) collective-permute-start(bf16[576,256]{1,0:T(8,128)(2,1)} %get-tuple-element.45), channel_id=1, source_target_pairs={{0,1},{1,0},{2,3},{3,2},{4,5},{5,4},{6,7},{7,6},{8,9},{9,8},{10,11... | collective-permute-start | bytes 884744 | tf_op jit(solution)/shard_map/ppermute | solution.py:38
  14.5 23.6 %collective-permute-start.3 = (bf16[576,256]{1,0:T(8,128)(2,1)}, bf16[576,256]{1,0:T(8,128)(2,1)S(1)}, u32[]{:S(2)}, u32[]{:S(2)}) collective-permute-start(bf16[576,256]{1,0:T(8,128)(2,1)} %get-tuple-element.46), channel_id=1, source_target_pairs={{0,2},{1,3},{2,0},{3,1},{4,6},{5,7},{6,4},{7,5},{8,10},{9,11},{10,... | collective-permute-start | bytes 884744 | tf_op jit(solution)/shard_map/ppermute | solution.py:38
  17.1 21.0 %collective-permute-start.4 = (bf16[576,256]{1,0:T(8,128)(2,1)}, bf16[576,256]{1,0:T(8,128)(2,1)S(1)}, u32[]{:S(2)}, u32[]{:S(2)}) collective-permute-start(bf16[576,256]{1,0:T(8,128)(2,1)} %get-tuple-element.47), channel_id=1, source_target_pairs={{0,3},{1,2},{2,1},{3,0},{4,7},{5,6},{6,5},{7,4},{8,11},{9,10},{10,... | collective-permute-start | bytes 884744 | tf_op jit(solution)/shard_map/ppermute | solution.py:38
  17.4 0.7 copy-start.3
  17.4 0.7 copy-start.4
  18.1 6.4 %copy-start.5 = (s32[112]{0:T(128)S(1)}, s32[112]{0:T(128)}, u32[]{:S(2)}) copy-start(s32[112]{0:T(128)} %shuffle.3) | copy-start | bytes 1348
  18.1 24.0 %copy-start = (bf16[14,128,256]{2,1,0:T(8,128)(2,1)S(1)}, bf16[14,128,256]{2,1,0:T(8,128)(2,1)}, u32[]{:S(2)}) copy-start(bf16[14,128,256]{2,1,0:T(8,128)(2,1)} %get-tuple-element.53.clean) | copy-start | bytes 2752516
  20.8 4.3 %copy-start.2 = (bf16[2,2,128,256]{3,2,1,0:T(8,128)(2,1)S(1)}, bf16[2,2,128,256]{3,2,1,0:T(8,128)(2,1)}, u32[]{:S(2)}) copy-start(bf16[2,2,128,256]{3,2,1,0:T(8,128)(2,1)} %get-tuple-element.54) | copy-start | bytes 786436
  20.8 19.5 %all-to-all-start = ((bf16[16,128,256]{2,1,0:T(8,128)(2,1)}), bf16[16,128,256]{2,1,0:T(8,128)(2,1)S(1)}, u32[]{:S(2)}, u32[]{:S(2)}) async-start(bf16[16,128,256]{2,1,0:T(8,128)(2,1)} %patch.1), calls=%async_computation | async-start | bytes 2097152 | tf_op jit(solution)/shard_map/all_to_all | solution.py:42
  25.2 17.0 %collective-permute-start.6 = (bf16[2,128,256]{2,1,0:T(8,128)(2,1)S(1)}, bf16[2,128,256]{2,1,0:T(8,128)(2,1)S(1)}, u32[]{:S(2)}, u32[]{:S(2)}) collective-permute-start(bf16[2,128,256]{2,1,0:T(8,128)(2,1)S(1)} %get-tuple-element.93), channel_id=1, source_target_pairs={{4,8},{12,16},{20,24},{28,0},{8,4},{16,12},{24,20},{0,28},{5,9},{1... | collective-permute-start | bytes 393224 | tf_op jit(solution)/shard_map/ppermute | solution.py:33
  27.8 14.4 %collective-permute-start.5 = (bf16[2,128,256]{2,1,0:T(8,128)(2,1)S(1)}, bf16[2,128,256]{2,1,0:T(8,128)(2,1)S(1)}, u32[]{:S(2)}, u32[]{:S(2)}) collective-permute-start(bf16[2,128,256]{2,1,0:T(8,128)(2,1)S(1)} %get-tuple-element.94), channel_id=1, source_target_pairs={{0,4},{4,0},{8,12},{12,8},{16,20},{20,16},{24,28},{28,24},{1,5},{5... | collective-permute-start | bytes 393224 | tf_op jit(solution)/shard_map/ppermute | solution.py:38
  40.3 6.9 %copy-start.1 = (bf16[576,256]{1,0:T(8,128)(2,1)S(1)}, bf16[576,256]{1,0:T(8,128)(2,1)}, u32[]{:S(2)}) copy-start(bf16[576,256]{1,0:T(8,128)(2,1)} %get-tuple-element.48.refs_0_) | copy-start | bytes 884740
  43.3 10.3 %collective-permute-start.9 = (bf16[448,256]{1,0:T(8,128)(2,1)S(1)}, bf16[448,256]{1,0:T(8,128)(2,1)S(1)}, u32[]{:S(2)}, u32[]{:S(2)}) collective-permute-start(bf16[448,256]{1,0:T(8,128)(2,1)S(1)} %get-tuple-element.83), channel_id=1, source_target_pairs={{0,3},{1,2},{2,1},{3,0},{4,7},{5,6},{6,5},{7,4},{8,11},{9,10},{10,... | collective-permute-start | bytes 688136 | tf_op jit(solution)/shard_map/ppermute | solution.py:38
  47.3 20.3 %collective-permute-start.12 = (bf16[4,128,256]{2,1,0:T(8,128)(2,1)S(1)}, bf16[4,128,256]{2,1,0:T(8,128)(2,1)S(1)}, u32[]{:S(2)}, u32[]{:S(2)}) collective-permute-start(bf16[4,128,256]{2,1,0:T(8,128)(2,1)S(1)} %pad_maximum_fusion.1), channel_id=1, source_target_pairs={{0,24},{4,28},{8,16},{12,20},{16,8},{20,12},{24,0},{28,4},{1,25},{... | collective-permute-start | bytes 786440 | tf_op jit(solution)/shard_map/ppermute | solution.py:38
  47.9 19.7 %collective-permute-start.11 = (bf16[4,128,256]{2,1,0:T(8,128)(2,1)S(1)}, bf16[4,128,256]{2,1,0:T(8,128)(2,1)S(1)}, u32[]{:S(2)}, u32[]{:S(2)}) collective-permute-start(bf16[4,128,256]{2,1,0:T(8,128)(2,1)S(1)} %pad_maximum_fusion.1), channel_id=1, source_target_pairs={{0,16},{4,20},{8,24},{12,28},{16,0},{20,4},{24,8},{28,12},{1,17},{... | collective-permute-start | bytes 786440 | tf_op jit(solution)/shard_map/ppermute | solution.py:38
  48.5 19.1 %collective-permute-start.10 = (bf16[4,128,256]{2,1,0:T(8,128)(2,1)S(1)}, bf16[4,128,256]{2,1,0:T(8,128)(2,1)S(1)}, u32[]{:S(2)}, u32[]{:S(2)}) collective-permute-start(bf16[4,128,256]{2,1,0:T(8,128)(2,1)S(1)} %pad_maximum_fusion.1), channel_id=1, source_target_pairs={{0,8},{4,12},{8,0},{12,4},{16,24},{20,28},{24,16},{28,20},{1,9},{5... | collective-permute-start | bytes 786440 | tf_op jit(solution)/shard_map/ppermute | solution.py:38
  50.8 7.6 %collective-permute-start.8 = (bf16[448,256]{1,0:T(8,128)(2,1)S(1)}, bf16[448,256]{1,0:T(8,128)(2,1)S(1)}, u32[]{:S(2)}, u32[]{:S(2)}) collective-permute-start(bf16[448,256]{1,0:T(8,128)(2,1)S(1)} %get-tuple-element.84), channel_id=1, source_target_pairs={{0,1},{1,0},{2,3},{3,2},{4,5},{5,4},{6,7},{7,6},{8,9},{9,8},{10,11... | collective-permute-start | bytes 688136 | tf_op jit(solution)/shard_map/ppermute | solution.py:38
  53.7 13.9 %collective-permute-start.7 = (bf16[448,256]{1,0:T(8,128)(2,1)S(1)}, bf16[448,256]{1,0:T(8,128)(2,1)S(1)}, u32[]{:S(2)}, u32[]{:S(2)}) collective-permute-start(bf16[448,256]{1,0:T(8,128)(2,1)S(1)} %get-tuple-element.85), channel_id=1, source_target_pairs={{0,2},{1,3},{2,0},{3,1},{4,6},{5,7},{6,4},{7,5},{8,10},{9,11},{10,... | collective-permute-start | bytes 688136 | tf_op jit(solution)/shard_map/ppermute | solution.py:38
  67.8 2.7 %collective-permute-start.13 = (bf16[4,4,128,256]{3,2,1,0:T(8,128)(2,1)S(1)}, bf16[4,4,128,256]{3,2,1,0:T(8,128)(2,1)S(1)}, u32[]{:S(2)}, u32[]{:S(2)}) collective-permute-start(bf16[4,4,128,256]{3,2,1,0:T(8,128)(2,1)S(1)} %pad_maximum_fusion.refs_4_), channel_id=1, source_target_pairs={{0,4},{4,0},{8,12},{12,8},{16,20},{20,16},{24,28},{28,24},{1,5},{5... | collective-permute-start | bytes 3145736 | tf_op jit(solution)/shard_map/ppermute | solution.py:38
  70.5 2.9 %collective-permute-start.14 = (bf16[4,4,128,256]{3,2,1,0:T(8,128)(2,1)S(1)}, bf16[4,4,128,256]{3,2,1,0:T(8,128)(2,1)S(1)}, u32[]{:S(2)}, u32[]{:S(2)}) collective-permute-start(bf16[4,4,128,256]{3,2,1,0:T(8,128)(2,1)S(1)} %get-tuple-element.66), channel_id=1, source_target_pairs={{0,4},{4,0},{8,12},{12,8},{16,20},{20,16},{24,28},{28,24},{1,5},{5... | collective-permute-start | bytes 3145736 | tf_op jit(solution)/shard_map/ppermute | solution.py:38
  73.9 9.2 %collective-permute-start.15 = (bf16[4,128,256]{2,1,0:T(8,128)(2,1)S(1)}, bf16[4,128,256]{2,1,0:T(8,128)(2,1)S(1)}, u32[]{:S(2)}, u32[]{:S(2)}) collective-permute-start(bf16[4,128,256]{2,1,0:T(8,128)(2,1)S(1)} %get-tuple-element.80), channel_id=1, source_target_pairs={{0,8},{4,12},{8,0},{12,4},{16,24},{20,28},{24,16},{28,20},{1,9},{5... | collective-permute-start | bytes 786440 | tf_op jit(solution)/shard_map/ppermute | solution.py:38
  75.4 14.2 %collective-permute-start.17 = (bf16[4,128,256]{2,1,0:T(8,128)(2,1)S(1)}, bf16[4,128,256]{2,1,0:T(8,128)(2,1)S(1)}, u32[]{:S(2)}, u32[]{:S(2)}) collective-permute-start(bf16[4,128,256]{2,1,0:T(8,128)(2,1)S(1)} %get-tuple-element.81), channel_id=1, source_target_pairs={{0,24},{4,28},{8,16},{12,20},{16,8},{20,12},{24,0},{28,4},{1,25},{... | collective-permute-start | bytes 786440 | tf_op jit(solution)/shard_map/ppermute | solution.py:38
  77.4 13.6 %collective-permute-start.16 = (bf16[4,128,256]{2,1,0:T(8,128)(2,1)S(1)}, bf16[4,128,256]{2,1,0:T(8,128)(2,1)S(1)}, u32[]{:S(2)}, u32[]{:S(2)}) collective-permute-start(bf16[4,128,256]{2,1,0:T(8,128)(2,1)S(1)} %get-tuple-element.82), channel_id=1, source_target_pairs={{0,16},{4,20},{8,24},{12,28},{16,0},{20,4},{24,8},{28,12},{1,17},{... | collective-permute-start | bytes 786440 | tf_op jit(solution)/shard_map/ppermute | solution.py:38
  77.5 15.5 %collective-permute-start.23 = (bf16[448,256]{1,0:T(8,128)(2,1)S(1)}, bf16[448,256]{1,0:T(8,128)(2,1)S(1)}, u32[]{:S(2)}, u32[]{:S(2)}) collective-permute-start(bf16[448,256]{1,0:T(8,128)(2,1)S(1)} %get-tuple-element.87), channel_id=1, source_target_pairs={{0,3},{1,2},{2,1},{3,0},{4,7},{5,6},{6,5},{7,4},{8,11},{9,10},{10,... | collective-permute-start | bytes 688136 | tf_op jit(solution)/shard_map/ppermute | solution.py:38
  79.7 22.6 %collective-permute-start.22 = (bf16[448,256]{1,0:T(8,128)(2,1)S(1)}, bf16[448,256]{1,0:T(8,128)(2,1)S(1)}, u32[]{:S(2)}, u32[]{:S(2)}) collective-permute-start(bf16[448,256]{1,0:T(8,128)(2,1)S(1)} %get-tuple-element.88), channel_id=1, source_target_pairs={{0,2},{1,3},{2,0},{3,1},{4,6},{5,7},{6,4},{7,5},{8,10},{9,11},{10,... | collective-permute-start | bytes 688136 | tf_op jit(solution)/shard_map/ppermute | solution.py:38
  83.1 19.2 %collective-permute-start.21 = (bf16[448,256]{1,0:T(8,128)(2,1)S(1)}, bf16[448,256]{1,0:T(8,128)(2,1)S(1)}, u32[]{:S(2)}, u32[]{:S(2)}) collective-permute-start(bf16[448,256]{1,0:T(8,128)(2,1)S(1)} %get-tuple-element.89), channel_id=1, source_target_pairs={{0,1},{1,0},{2,3},{3,2},{4,5},{5,4},{6,7},{7,6},{8,9},{9,8},{10,11... | collective-permute-start | bytes 688136 | tf_op jit(solution)/shard_map/ppermute | solution.py:38
  91.2 12.6 %collective-permute-start.18 = (bf16[128,256]{1,0:T(8,128)(2,1)S(1)}, bf16[128,256]{1,0:T(8,128)(2,1)S(1)}, u32[]{:S(2)}, u32[]{:S(2)}) collective-permute-start(bf16[128,256]{1,0:T(8,128)(2,1)S(1)} %get-tuple-element.90), channel_id=1, source_target_pairs={{0,1},{1,0},{2,3},{3,2},{4,5},{5,4},{6,7},{7,6},{8,9},{9,8},{10,11... | collective-permute-start | bytes 196616 | tf_op jit(solution)/shard_map/ppermute | solution.py:38
  91.3 12.6 %collective-permute-start.20 = (bf16[128,256]{1,0:T(8,128)(2,1)S(1)}, bf16[128,256]{1,0:T(8,128)(2,1)S(1)}, u32[]{:S(2)}, u32[]{:S(2)}) collective-permute-start(bf16[128,256]{1,0:T(8,128)(2,1)S(1)} %get-tuple-element.91), channel_id=1, source_target_pairs={{0,3},{1,2},{2,1},{3,0},{4,7},{5,6},{6,5},{7,4},{8,11},{9,10},{10,... | collective-permute-start | bytes 196616 | tf_op jit(solution)/shard_map/ppermute | solution.py:38
  93.0 10.8 %collective-permute-start.19 = (bf16[128,256]{1,0:T(8,128)(2,1)S(1)}, bf16[128,256]{1,0:T(8,128)(2,1)S(1)}, u32[]{:S(2)}, u32[]{:S(2)}) collective-permute-start(bf16[128,256]{1,0:T(8,128)(2,1)S(1)} %get-tuple-element.92), channel_id=1, source_target_pairs={{0,2},{1,3},{2,0},{3,1},{4,6},{5,7},{6,4},{7,5},{8,10},{9,11},{10,... | collective-permute-start | bytes 196616 | tf_op jit(solution)/shard_map/ppermute | solution.py:38
